TPU v7x, 32 devices: a whole 2x2x4 slice. The times are simulated.
32 devices in a mesh: seq: 16 (over z, y, x), head: 2 (over core).
Axes of the slice: x: 2, y: 2, z: 4, core: 2. Of those that a mesh axis runs over, the one named last changes fastest.
Arguments:
- token_values: bfloat16 [6144, 4096], P('seq', 'head'), may hold values from -6 to 6
- b_inputs: bfloat16 [6144, 128], P('seq'), may hold values from -6 to 6
- c_inputs: bfloat16 [6144, 128], P('seq'), may hold values from -6 to 6
- log_decay: float32 [64, 6144], P('head', 'seq'), may hold values from -1 to 0
- grad_out: bfloat16 [6144, 4096], P('seq', 'head'), may hold values from -0.005859375 to 0.005859375
Outputs:
- grad_values: bfloat16 [6144, 4096], P('seq', 'head')
- grad_b: bfloat16 [6144, 128], P('seq')
- grad_c: bfloat16 [6144, 128], P('seq')
All inputs are finite; a program needn't handle non-finite values.
Results may differ from a plain program's by a relative error of at most 0.014.
Values may be sent and summed in bfloat16 or wider, within the bound.
No kernel may reach another device: no remote copies, remote signals or barrier semaphores. Data moves between devices by JAX's collectives and lax.ppermute only.
A program may use at most 128 MiB of HBM per device.

v0:
```python
import jax
import jax.numpy as jnp
from jax import lax
from jax.sharding import PartitionSpec as P

PRECISE = lax.Precision.HIGHEST


def entering(part, axis, combine, identity, reverse):
    count = lax.axis_size(axis)
    place = lax.axis_index(axis)
    ahead = count - 1 - place if reverse else place
    gathered = jax.tree.map(lambda a: lax.all_gather(a, axis), part)
    state = jax.tree.map(lambda a, e: jnp.zeros_like(a) + jnp.asarray(e, a.dtype), part, identity)

    def one(lap, state):
        source = count - 1 - lap if reverse else lap
        return combine(
            state, jax.tree.map(lambda a: lax.dynamic_index_in_dim(a, source, 0, False), gathered)
        )

    return lax.fori_loop(0, ahead, one, state)


def spread(values, width):
    return jnp.repeat(values, width)[None, :]


def shards(token_values, b_inputs, c_inputs, log_decay, grad_out):
    length = token_values.shape[0]
    heads_here = log_decay.shape[0]
    head_dim = token_values.shape[1] // heads_here
    state_size = b_inputs.shape[1]
    cumulative = jnp.cumsum(log_decay, axis=1)
    block_log = cumulative[:, -1]
    into_end = jnp.exp(block_log[:, None] - cumulative)
    from_start = jnp.exp(cumulative)
    block_decay = jnp.exp(block_log)
    b_float = b_inputs.astype(jnp.float32)
    c_float = c_inputs.astype(jnp.float32)
    decayed_b = (into_end[:, :, None] * b_float[None]).astype(jnp.bfloat16)
    decayed_c = (from_start[:, :, None] * c_float[None]).astype(jnp.bfloat16)
    x_heads = token_values.reshape(length, heads_here, head_dim)
    dy_heads = grad_out.reshape(length, heads_here, head_dim)
    state_local = jnp.einsum(
        "htn,thp->nhp", decayed_b, x_heads, preferred_element_type=jnp.float32
    ).reshape(state_size, heads_here * head_dim)
    adjoint_local = jnp.einsum(
        "hsn,shp->nhp", decayed_c, dy_heads, preferred_element_type=jnp.float32
    ).reshape(state_size, heads_here * head_dim)

    def forward_combine(earlier, later):
        return (earlier[0] * later[0], spread(later[0], head_dim) * earlier[1] + later[1])

    def backward_combine(earlier, later):
        return (earlier[0] * later[0], later[1] + spread(later[0], head_dim) * earlier[1])

    identity = (jnp.ones((heads_here,), jnp.float32), jnp.zeros_like(state_local))
    carried_decay, state_in = entering(
        (block_decay, state_local), "seq", forward_combine, identity, False
    )
    later_decay, adjoint_out = entering(
        (block_decay, adjoint_local), "seq", backward_combine, identity, True
    )
    scores = lax.dot_general(
        c_inputs, b_inputs, (((1,), (1,)), ((), ())), preferred_element_type=jnp.float32
    )
    entry_indices = lax.iota(jnp.int32, length)
    causal = entry_indices[:, None] >= entry_indices[None, :]

    def head_step(head_idx, carried):
        running, dx_local = carried
        cum_head = lax.dynamic_index_in_dim(cumulative, head_idx, 0, keepdims=False)
        log_gaps = cum_head[:, None] - cum_head[None, :]
        decays = jnp.where(causal, jnp.exp(jnp.where(causal, log_gaps, 0.0)), 0.0)
        mixing = (scores * decays).astype(jnp.bfloat16)
        x_head = lax.dynamic_slice_in_dim(token_values, head_idx * head_dim, head_dim, 1)
        dy_head = lax.dynamic_slice_in_dim(grad_out, head_idx * head_dim, head_dim, 1)
        dx_head = lax.dot_general(
            mixing, dy_head, (((0,), (0,)), ((), ())), preferred_element_type=jnp.float32
        )
        dot_pairs = lax.dot_general(
            dy_head, x_head, (((1,), (1,)), ((), ())), preferred_element_type=jnp.float32
        )
        dx_local = lax.dynamic_update_slice_in_dim(dx_local, dx_head, head_idx * head_dim, 1)
        return (running + decays * dot_pairs, dx_local)

    start_pair = (
        jnp.zeros((length, length), jnp.float32),
        jnp.zeros((length, heads_here * head_dim), jnp.float32),
    )
    running, dx_local = lax.fori_loop(0, heads_here, head_step, start_pair)
    weighted = running.astype(jnp.bfloat16)
    db_part = lax.dot_general(
        weighted, c_inputs, (((0,), (0,)), ((), ())), preferred_element_type=jnp.float32
    )
    dc_part = jnp.dot(weighted, b_inputs, preferred_element_type=jnp.float32)
    to_end_cols = jnp.repeat(into_end.T, head_dim, axis=1)
    from_start_cols = jnp.repeat(from_start.T, head_dim, axis=1)
    grad_values = dx_local + to_end_cols * jnp.dot(b_float, adjoint_out, precision=PRECISE)
    db_part = db_part + jnp.dot(
        token_values.astype(jnp.float32) * to_end_cols, adjoint_out.T, precision=PRECISE
    )
    dc_part = dc_part + jnp.dot(
        grad_out.astype(jnp.float32) * from_start_cols, state_in.T, precision=PRECISE
    )
    grad_b, grad_c = (
        lax.psum(db_part.astype(jnp.bfloat16), "head").astype(jnp.float32),
        lax.psum(dc_part.astype(jnp.bfloat16), "head").astype(jnp.float32),
    )
    return (
        grad_values.astype(jnp.bfloat16),
        grad_b.astype(jnp.bfloat16),
        grad_c.astype(jnp.bfloat16),
    )


def solution(mesh):
    in_specs = (
        P("seq", "head"),
        P("seq", None),
        P("seq", None),
        P("head", "seq"),
        P("seq", "head"),
    )
    out_specs = (P("seq", "head"), P("seq", None), P("seq", None))
    return jax.shard_map(shards, mesh=mesh, in_specs=in_specs, out_specs=out_specs, check_vma=False)
```

profile of v0, /device:TPU:0, one launch (start us, length us, event | category | flops | bytes accessed | tf_op | source)
XLA Modules:
  0.0 470.2 jit_solution(4651922580599316910)
XLA Ops:
  9.1 1.9 copy.27
  11.3 1.9 fusion.17
  14.7 1.9 copy.29
  16.6 3.3 fusion.18
  19.9 2.6 copy.32
  24.2 44.3 %all-reduce = f32[512]{0:T(512)S(1)} all-reduce(f32[512]{0:T(512)S(1)} %dynamic-update-slice), channel_id=2, replica_groups=mesh['seq'=16,'head'=2] {'seq'}, use_global_device_ids=true, to_apply=%add | all-reduce | flops 512 | bytes 4096
  68.6 1.8 bitcast_multiply_fusion
  70.4 1.8 bitcast_multiply_fusion.2
  73.6 121.5 %while.45 = (s32[]{:T(128)}, f32[384,384]{1,0:T(8,128)}, f32[384,2048]{0,1:T(8,128)S(1)}, f32[32,384]{1,0:T(8,128)S(1)}, bf16[384,2048]{1,0:T(8,128)(2,1)}, /*in...) while((s32[]{:T(128)}, f32[384,384]{1,0:T(8,128)}, ...), condition=%wide.region_3.4_spmd.clone.clone, body=%wide.region_2.3_spmd.clone.clone.sunk | while | flops 39665672 | bytes 2176688 | solution.py:92
  73.6 2.1 fusion.51
  77.2 2.3 fusion.51
  81.0 2.3 fusion.51
  84.8 2.3 fusion.51
  88.6 2.3 fusion.51
  92.3 2.4 fusion.51
  96.1 2.3 fusion.51
  99.9 2.3 fusion.51
  103.7 2.3 fusion.51
  107.5 2.3 fusion.51
  111.3 2.3 fusion.51
  115.3 2.6 fusion.51
  119.3 2.3 fusion.51
  123.1 2.3 fusion.51
  126.9 2.3 fusion.51
  130.7 2.3 fusion.51
  134.5 2.3 fusion.51
  138.3 2.3 fusion.51
  142.1 2.3 fusion.51
  145.9 2.3 fusion.51
  149.6 2.3 fusion.51
  153.4 2.3 fusion.51
  157.2 2.3 fusion.51
  161.0 2.3 fusion.51
  164.8 2.3 fusion.51
  168.6 2.3 fusion.51
  172.4 2.3 fusion.51
  176.1 2.4 fusion.51
  180.0 2.3 fusion.51
  183.8 2.3 fusion.51
  187.6 2.3 fusion.51
  191.4 2.3 fusion.51
  196.8 13.1 %all-gather.4.cloned.1.call-done = f32[16,128,2048]{2,1,0:T(8,128)} async-done(((f32[1,128,2048]{2,1,0:T(8,128)}), f32[16,128,2048]{2,1,0:T(8,128)}) %all-gather.4.cloned.1.call-update) | async-done | bytes 16777232 | tf_op jit(solution)/shard_map/all_gather | solution.py:13
  210.0 27.6 %while.43 = (s32[]{:T(128)}, f32[128,2048]{1,0:T(8,128)S(1)}, s32[]{:T(128)}, f32[16,128,2048]{2,1,0:T(8,128)}, f32[16,32]{1,0:T(8,128)S(1)}, /*index=5*/s32[]{:T(128)}, s32[]{:T(128)}, s32[]{:T(128)}, s32[]{:T(128)}) while((s32[]{:T(128)}, f32[128,2048]{1,0:T(8,128)S(1)}, s32[]{:T(128)}, f32[16,128,2048]{2,1,0:T(8,128)}, ...), condition=%wide.region_5.6_spmd, body=%wide.region_4.5_spmd.sunk | while | flops 524294 | bytes 3179035 | solution.py:22
  237.6 164.9 %all-gather.6.cloned.1.call-done = f32[16,128,2048]{2,1,0:T(8,128)} async-done(((f32[1,128,2048]{2,1,0:T(8,128)}), f32[16,128,2048]{2,1,0:T(8,128)}) %all-gather.6.cloned.1.call-update) | async-done | bytes 16777232 | tf_op jit(solution)/shard_map/all_gather | solution.py:13
  402.8 7.1 %fusion.29 = f32[384,128]{1,0:T(8,128)S(1)} fusion(f32[384,2048]{0,1:T(8,128)} %bitcast_multiply_fusion, f32[128,2048]{1,0:T(8,128)S(1)} %get-tuple-element.275), kind=kOutput, calls=%fused_computation.52 | convolution fusion | flops 1207959552 | bytes 4390912 | tf_op jit(solution)/shard_map/dot_general | solution.py:101
  410.8 5.1 %fusion.30 = f32[384,128]{1,0:T(8,128)S(1)} fusion(f32[384,2048]{0,1:T(8,128)S(1)} %copy-done.1, f32[128,2048]{1,0:T(8,128)S(1)} %get-tuple-element.277), kind=kOutput, calls=%fused_computation.53 | convolution fusion | flops 1207959552 | bytes 4390912 | tf_op jit(solution)/shard_map/dot_general | solution.py:104
  416.8 3.8 fusion.16
  422.2 38.3 %all-reduce.4.cloned.1.call-done = (bf16[384,128]{1,0:T(8,128)(2,1)}, bf16[384,128]{1,0:T(8,128)(2,1)}) async-done(((bf16[384,128]{1,0:T(8,128)(2,1)}, bf16[384,128]{1,0:T(8,128)(2,1)}), (bf16[384,128]{1,0:T(8,128)(2,1)}, bf16[384,128]{1,0:T(8,128)(2,1)})) %all-reduce.4.cloned.1.call-update) | async-done | bytes 196624 | tf_op jit(solution)/shard_map/psum | solution.py:108
  (169 shorter events, 87.3 us)
Async XLA Ops:
  7.2 0.8 copy-start
  7.2 3.8 copy-start.5
  7.2 202.7 %all-gather.4.cloned.1.call-start = ((), (), s32[]{:S(2)}) async-start(), calls=%async_computation | async-start | bytes 17825792 | tf_op jit(solution)/shard_map/all_gather | solution.py:13
  13.3 3.3 copy-start.4
  14.6 387.9 %all-gather.6.cloned.1.call-start = ((), (), s32[]{:S(2)}) async-start(), calls=%async_computation.1 | async-start | bytes 17825792 | tf_op jit(solution)/shard_map/all_gather | solution.py:13
  16.6 6.0 %copy-start.6 = (u32[32]{0:T(128)S(1)}, u32[32]{0:T(128)}, u32[]{:S(2)}) copy-start(u32[32]{0:T(128)} %constant.110) | copy-start | bytes 388
  22.5 438.0 %all-reduce.4.cloned.1.call-start = ((), (), s32[]{:S(2)}) async-start(), calls=%async_computation.2 | async-start | bytes 393216 | tf_op jit(solution)/shard_map/psum | solution.py:108
  195.1 1.7 copy-start.2
  402.8 7.1 %copy-start.3 = (f32[384,384]{1,0:T(8,128)S(1)}, f32[384,384]{1,0:T(8,128)}, u32[]{:S(2)}) copy-start(f32[384,384]{1,0:T(8,128)} %get-tuple-element.276) | copy-start | bytes 1769476
  402.8 8.0 %copy-start.1 = (f32[384,2048]{0,1:T(8,128)S(1)}, f32[384,2048]{0,1:T(8,128)}, u32[]{:S(2)}) copy-start(f32[384,2048]{0,1:T(8,128)} %bitcast_multiply_fusion.2) | copy-start | bytes 9437188
Sparse Core Ops, SparseCore 0:
  14.7 195.0 all-gather.3
  212.6 189.8 all-gather.5
  416.9 43.5 all-reduce.3
where the time goes:
time: 473 us; the launch traced here: 470 us
  waiting for transfers between devices  216 us (46%)
  matrix products  144 us (30%)
  blocking collectives  44.3 us (9%)
  other arithmetic  29.6 us (6%)
  local copies, waits for them, and re-layouts  19.6 us (4%)
  between operations  14.7 us (3%)
    all_gather x2, waiting for transfers between devices, entering(): gathered = jax.tree.map(lambda a: lax.all_gather(a, axis), part)  178 us
    dot_general x32, matrix products, head_step(): lax.dot_general(dy_head, x_head, (((1,), (1,)), ((), ())), preferred_elem...  74.9 us
    dot_general x32, matrix products, head_step(): lax.dot_general(mixing, dy_head, (((0,), (0,)), ((), ())), preferred_elem...  44.8 us
    unnamed x1, blocking collectives  44.3 us
    psum x1, waiting for transfers between devices, shards(): lax.psum(db_part.astype(jnp.bfloat16), 'head').astype(jnp.float32)  38.3 us
    add x15, other arithmetic, backward_combine(): later[1] + spread(later[0], head_dim) * earlier[1]  24.8 us
    unnamed x22, local copies, waits for them, and re-layouts  11.8 us
  transfers between devices with their start and end apart: 3, of which 3 were waited for; matrix products, arithmetic and copies ran while one was open for 35% of the time, Pallas kernels for 0%

commit v1 on v0

v1 whole, which is shorter than its diff:
```python
import functools

import jax
import jax.numpy as jnp
from jax import lax
from jax.experimental import pallas as pl
from jax.experimental.pallas import tpu as pltpu
from jax.sharding import PartitionSpec as P

BF16 = jnp.bfloat16
F32 = jnp.float32
GROUP = 4
LANES = 128
TAIL = 16
LOG2E = 1.4426950408889634
MIB = 1024 * 1024

NN = (((1,), (0,)), ((), ()))
NT = (((1,), (1,)), ((), ()))
TN = (((0,), (0,)), ((), ()))


def dot(a, b, dims):
    return lax.dot_general(a, b, dims, preferred_element_type=F32)


def iota(shape, dim):
    return lax.broadcasted_iota(jnp.int32, shape, dim)


def three(values):
    high = values.astype(BF16)
    rest = values - high.astype(F32)
    mid = rest.astype(BF16)
    return high, mid, (rest - mid.astype(F32)).astype(BF16)


def summed(mask, terms, copies=1):
    return sum(dot(mask, jnp.concatenate([t] * copies, axis=0), NT) for t in terms)


def head_of_lane(heads, head_dim, width, first, copies=1):
    shape = (copies * heads, width)
    rows = iota(shape, 0)
    if copies > 1:
        rows = lax.rem(rows, heads)
    return jnp.where(rows == first + iota(shape, 1) // head_dim, 1.0, 0.0).astype(BF16)


def whole(count):
    return [pl.BlockSpec(memory_space=pltpu.VMEM)] * count


SMEM = pl.BlockSpec(memory_space=pltpu.SMEM)


def params(mib):
    return pltpu.CompilerParams(vmem_limit_bytes=mib * MIB)


def local_kernel(forward, head_dim, place, ld, proj, cols, *outs):
    heads, length = ld.shape
    state, part = proj.shape[1], cols.shape[1] // GROUP
    scaled, decay = outs[0], outs[1]
    sends = outs[2:]
    terms = three(ld[...])
    rows, other = iota((length, length), 0), iota((length, length), 1)
    mask = jnp.where(other > rows if forward else other <= rows, 1.0, 0.0).astype(BF16)
    factors = jnp.exp(summed(mask, terms)).astype(BF16)
    decay[...] = factors
    if forward:
        total = jnp.exp(summed(jnp.ones((TAIL, length), BF16), terms))
        high = total.astype(BF16)
        low = (total - high.astype(F32)).astype(BF16)
        halves = jnp.where(iota(total.shape, 0) < TAIL // 2, high.astype(F32), low.astype(F32))
        halves = halves.astype(BF16)
    for k in range(GROUP):
        owner = place[0] ^ k
        where = pl.ds(pl.multiple_of(owner * part, part), part)
        hot = head_of_lane(heads, head_dim, part, owner * (heads // GROUP))
        spread = dot(factors, hot, NN).astype(BF16)
        piece = cols[:, where] * spread
        scaled[:, where] = piece
        sends[k][:state, :] = dot(proj[...], piece, TN).astype(BF16)
        if forward:
            sends[k][state:, :] = dot(halves, hot, NN).astype(BF16)


def local_states(forward, head_dim, place, ld, proj, cols):
    heads, length = ld.shape
    state, width = proj.shape[1], cols.shape[1]
    rows = state + (TAIL if forward else 0)
    return pl.pallas_call(
        functools.partial(local_kernel, forward, head_dim),
        out_shape=[
            jax.ShapeDtypeStruct(cols.shape, BF16),
            jax.ShapeDtypeStruct((length, heads), BF16),
        ]
        + [jax.ShapeDtypeStruct((rows, width // GROUP), BF16)] * GROUP,
        in_specs=[SMEM] + whole(3),
        out_specs=whole(2 + GROUP),
        compiler_params=params(16),
        cost_estimate=pl.CostEstimate(
            flops=2 * length * width * (state + heads),
            bytes_accessed=4 * length * width + 2 * state * width,
            transcendentals=length * heads,
        ),
        name="states_forward" if forward else "states_backward",
    )(place, ld, proj, cols)


def decay_row(ref, state):
    tail = ref[state:, :].astype(F32)
    return tail[:1, :] + tail[TAIL // 2 : TAIL // 2 + 1, :]


def put(ref, state, value, factor):
    ref[:state, :] = value.astype(BF16)
    high = factor.astype(BF16).astype(F32)
    shape = (TAIL, factor.shape[1])
    both = jnp.where(iota(shape, 0) < TAIL // 2, high, factor - high)
    ref[state:, :] = both.astype(BF16)


def entering_group(state, received):
    value = received[0][:state, :].astype(F32)
    factor = decay_row(received[0], state)
    for r in received[1:]:
        value = value + factor * r[:state, :].astype(F32)
        factor = factor * decay_row(r, state)
    return value, factor


def in_order(forward):
    return range(GROUP) if forward else range(GROUP - 1, -1, -1)


def total_kernel(forward, state, place, *refs):
    blocks, tails, out = refs[:GROUP], refs[-1 - GROUP : -1], refs[-1]
    for here in range(GROUP):

        @pl.when(place[0] == here)
        def _(here=here):
            value, factor = None, None
            for q in in_order(forward):
                piece = blocks[q ^ here][:state, :].astype(F32)
                d = decay_row(tails[q ^ here], state)
                value = piece if value is None else d * value + piece
                factor = d if factor is None else factor * d
            put(out, state, value, factor)


def group_total(forward, state, place, blocks, tails):
    operands = list(blocks) if forward else list(blocks) + list(tails)
    width = blocks[0].shape[1]
    return pl.pallas_call(
        functools.partial(total_kernel, forward, state),
        out_shape=jax.ShapeDtypeStruct((state + TAIL, width), BF16),
        in_specs=[SMEM] + whole(len(operands)),
        out_specs=whole(1)[0],
        compiler_params=params(8),
        cost_estimate=pl.CostEstimate(
            flops=8 * state * width, bytes_accessed=10 * state * width, transcendentals=0
        ),
        name="group_total",
    )(place, *operands)


def onward_kernel(state, own, *refs):
    received, out = refs[:-1], refs[-1]
    value, factor = entering_group(state, received)
    d = decay_row(own, state)
    put(out, state, own[:state, :].astype(F32) + d * value, d * factor)


def onward(state, own, received):
    return pl.pallas_call(
        functools.partial(onward_kernel, state),
        out_shape=jax.ShapeDtypeStruct(own.shape, BF16),
        in_specs=whole(1 + len(received)),
        out_specs=whole(1)[0],
        compiler_params=params(8),
        cost_estimate=pl.CostEstimate(flops=4 * own.size, bytes_accessed=6 * own.size, transcendentals=0),
        name="onward",
    )(own, *received)


def members_kernel(forward, state, n_received, place, *refs):
    received, refs = refs[:n_received], refs[n_received:]
    blocks, tails, outs = refs[:GROUP], refs[-2 * GROUP : -GROUP], refs[-GROUP:]
    entry, _ = entering_group(state, received)
    for here in range(GROUP):

        @pl.when(place[0] == here)
        def _(here=here):
            value = entry
            order = list(in_order(forward))
            for q in order:
                outs[q ^ here][...] = value.astype(BF16)
                if q != order[-1]:
                    d = decay_row(tails[q ^ here], state)
                    value = d * value + blocks[q ^ here][:state, :].astype(F32)


def member_entries(forward, state, place, received, blocks, tails):
    operands = list(received) + list(blocks) + ([] if forward else list(tails))
    width = blocks[0].shape[1]
    return pl.pallas_call(
        functools.partial(members_kernel, forward, state, len(received)),
        out_shape=[jax.ShapeDtypeStruct((state, width), BF16)] * GROUP,
        in_specs=[SMEM] + whole(len(operands)),
        out_specs=whole(GROUP),
        compiler_params=params(8),
        cost_estimate=pl.CostEstimate(
            flops=10 * state * width, bytes_accessed=20 * state * width, transcendentals=0
        ),
        name="member_entries",
    )(place, *operands)


def carried(forward, state, place, sends, tails=None):
    count = lax.axis_size("seq")
    groups = count // GROUP

    def to_member(block, k):
        return lax.ppermute(block, "seq", [(s, s ^ k) for s in range(count)])

    blocks = [sends[0]] + [to_member(sends[k], k) for k in range(1, GROUP)]
    tails = blocks if forward else tails
    own = group_total(forward, state, place, blocks, tails)
    received, sent, step = [], own, 1
    while step < groups:
        jump = step * GROUP if forward else -step * GROUP
        pairs = [(s, s + jump) for s in range(count) if 0 <= s + jump < count]
        received.append(lax.ppermute(sent, "seq", pairs))
        step *= 2
        if step < groups:
            sent = onward(state, own, received)
    entries = member_entries(forward, state, place, received, blocks, tails)
    return [entries[0]] + [to_member(entries[k], k) for k in range(1, GROUP)], blocks


def split_pairs(first, count):
    if count == 1:
        return []
    middle = first + count // 2
    return (
        [(first, middle, first + count)]
        + split_pairs(first, middle - first)
        + split_pairs(middle, first + count - middle)
    )


def inner_kernel(head_dim, ld, b, c, x, dy, dx_out, db_out, dc_out, cum_terms, *scratch):
    heads, length = ld.shape
    width, state = x.shape[1], b.shape[1]
    piece = head_dim
    pieces = length // piece
    cuts = split_pairs(0, pieces)
    near, near_sum, dx = scratch[:3]
    far, far_sum = scratch[3 : 3 + len(cuts)], scratch[3 + len(cuts) :]
    per_tile = LANES // head_dim
    step = pl.program_id(0)

    @pl.when(step == 0)
    def _():
        terms = three(ld[...] * LOG2E)
        rows, other = iota((length, length), 0), iota((length, length), 1)
        mask = jnp.where(other <= rows, 1.0, 0.0).astype(BF16)
        high, mid, low = three(summed(mask, terms, copies=3))
        lane = iota((length, 3 * heads), 1)
        picked = jnp.where(
            lane < heads,
            high.astype(F32),
            jnp.where(lane < 2 * heads, mid.astype(F32), low.astype(F32)),
        )
        cum_terms[...] = picked.astype(BF16)
        keep = iota((piece, LANES), 0) <= lax.rem(iota((piece, LANES), 1), piece)
        for n in range(pieces):
            rows_n = slice(n * piece, (n + 1) * piece)
            doubled = jnp.concatenate([c[rows_n, :]] * per_tile, axis=0)
            near[rows_n, :] = jnp.where(keep, dot(b[rows_n, :], doubled, NT), 0.0)
        near_sum[...] = jnp.zeros_like(near_sum)
        for (lo, mid_, hi), f, total in zip(cuts, far, far_sum):
            left, right = slice(lo * piece, mid_ * piece), slice(mid_ * piece, hi * piece)
            f[...] = dot(b[left, :], c[right, :], NT).astype(BF16)
            total[...] = jnp.zeros_like(total)

    hot = head_of_lane(heads, head_dim, width, step * (width // head_dim), copies=3)
    cum = dot(cum_terms[...], hot, NN)
    tile = (piece, LANES)
    diagonal = iota(tile, 0) == lax.rem(iota(tile, 1), piece)
    part_of_lane = iota(tile, 1) // head_dim
    for n in range(pieces):
        rows_n = slice(n * piece, (n + 1) * piece)
        total = near_sum[rows_n, :]
        scores = near[rows_n, :]
        for t in range(width // LANES):
            lanes = slice(t * LANES, (t + 1) * LANES)
            col = cum[rows_n, lanes]
            row = jnp.sum(jnp.where(diagonal, col, 0.0), axis=0, keepdims=True)
            decays = jnp.exp2(jnp.minimum(row - col, 0.0))
            dy_t = dy[rows_n, lanes]
            stacked = jnp.concatenate(
                [jnp.where(part_of_lane == h, dy_t, jnp.zeros_like(dy_t)) for h in range(per_tile)],
                axis=0,
            )
            dx[rows_n, lanes] = dot((scores * decays).astype(BF16), stacked, NN)
            total = total + decays * dot(x[rows_n, lanes], stacked, NT)
        near_sum[rows_n, :] = total
    for (lo, mid_, hi), f, total in zip(cuts, far, far_sum):
        left, right = slice(lo * piece, mid_ * piece), slice(mid_ * piece, hi * piece)
        edge = cum[mid_ * piece - 1 : mid_ * piece, :]
        to_edge = jnp.exp2(edge - cum[left, :])
        from_edge = jnp.exp2(cum[right, :] - edge)
        x_edge = (x[left, :].astype(F32) * to_edge).astype(BF16)
        dy_edge = (dy[right, :].astype(F32) * from_edge).astype(BF16)
        dx[left, :] += to_edge * dot(f[...], dy_edge, NN)
        total[...] += dot(x_edge, dy_edge, NT)
    dx_out[...] = dx[...].astype(BF16)

    @pl.when(step == pl.num_programs(0) - 1)
    def _():
        keep = (iota(tile, 0) <= iota(tile, 1)) & (part_of_lane == 0)
        for n in range(pieces):
            rows_n = slice(n * piece, (n + 1) * piece)
            total = near_sum[rows_n, :]
            total = sum(
                [pltpu.roll(total, h * head_dim, 1) for h in range(1, per_tile)], total
            )
            weighted = jnp.where(keep, total, 0.0).astype(BF16)
            doubled = jnp.concatenate([c[rows_n, :]] * per_tile, axis=0)
            db_out[rows_n, :] = dot(weighted, doubled, NN)
            dc_out[rows_n, :] = dot(weighted, b[rows_n, :], TN)[:piece, :]
        for (lo, mid_, hi), total in zip(cuts, far_sum):
            left, right = slice(lo * piece, mid_ * piece), slice(mid_ * piece, hi * piece)
            weighted = total[...].astype(BF16)
            db_out[left, :] += dot(weighted, c[right, :], NN)
            dc_out[right, :] += dot(weighted, b[left, :], TN)


def inner_terms(head_dim, ld, b, c, x, dy):
    heads, length = ld.shape
    state, width = b.shape[1], x.shape[1]
    chunk = width // 4
    piece = head_dim
    cuts = split_pairs(0, length // piece)
    sizes = [((mid - lo) * piece, (hi - mid) * piece) for lo, mid, hi in cuts]
    column = pl.BlockSpec((length, chunk), lambda i: (0, i))

    def fixed(shape):
        return pl.BlockSpec(shape, lambda i: (0, 0))

    return pl.pallas_call(
        functools.partial(inner_kernel, head_dim),
        grid=(width // chunk,),
        out_shape=[
            jax.ShapeDtypeStruct((length, width), BF16),
            jax.ShapeDtypeStruct((length, state), F32),
            jax.ShapeDtypeStruct((length, state), F32),
        ],
        in_specs=[fixed(ld.shape), fixed(b.shape), fixed(c.shape), column, column],
        out_specs=[column, fixed((length, state)), fixed((length, state))],
        scratch_shapes=[
            pltpu.VMEM((length, 3 * heads), BF16),
            pltpu.VMEM((length, LANES), F32),
            pltpu.VMEM((length, LANES), F32),
            pltpu.VMEM((length, chunk), F32),
        ]
        + [pltpu.VMEM(s, BF16) for s in sizes]
        + [pltpu.VMEM(s, F32) for s in sizes],
        compiler_params=params(24),
        cost_estimate=pl.CostEstimate(
            flops=16 * length * width * state,
            bytes_accessed=6 * length * width,
            transcendentals=3 * length * width,
        ),
        name="inner_terms",
    )(ld, b, c, x, dy)


def entry_c_kernel(place, scaled, part_local, *refs):
    entries, out = refs[:GROUP], refs[GROUP]
    part = scaled.shape[1] // GROUP
    total = part_local[...]
    for k in range(GROUP):
        where = pl.ds(pl.multiple_of((place[0] ^ k) * part, part), part)
        total = total + dot(scaled[:, where], entries[k][...], NT)
    out[...] = total.astype(BF16)


def entry_c(place, scaled, part_local, entries):
    return pl.pallas_call(
        entry_c_kernel,
        out_shape=jax.ShapeDtypeStruct(part_local.shape, BF16),
        in_specs=[SMEM] + whole(2 + GROUP),
        out_specs=whole(1)[0],
        compiler_params=params(12),
        cost_estimate=pl.CostEstimate(
            flops=2 * scaled.size * part_local.shape[1],
            bytes_accessed=2 * scaled.size,
            transcendentals=0,
        ),
        name="entry_c",
    )(place, scaled, part_local, *entries)


def entry_b_kernel(head_dim, place, decay, b, scaled, dx_local, part_local, *refs):
    entries, dx_out, out = refs[:GROUP], refs[GROUP], refs[GROUP + 1]
    heads = decay.shape[1]
    part = scaled.shape[1] // GROUP
    total = part_local[...]
    for k in range(GROUP):
        owner = place[0] ^ k
        where = pl.ds(pl.multiple_of(owner * part, part), part)
        entry = entries[k][...]
        hot = head_of_lane(heads, head_dim, part, owner * (heads // GROUP))
        spread = dot(decay[...], hot, NN)
        far = dx_local[:, where].astype(F32) + spread * dot(b[...], entry, NN)
        dx_out[:, where] = far.astype(BF16)
        total = total + dot(scaled[:, where], entry, NT)
    out[...] = total.astype(BF16)


def entry_b(head_dim, place, decay, b, scaled, dx_local, part_local, entries):
    return pl.pallas_call(
        functools.partial(entry_b_kernel, head_dim),
        out_shape=[
            jax.ShapeDtypeStruct(dx_local.shape, BF16),
            jax.ShapeDtypeStruct(part_local.shape, BF16),
        ],
        in_specs=[SMEM] + whole(5 + GROUP),
        out_specs=whole(2),
        compiler_params=params(20),
        cost_estimate=pl.CostEstimate(
            flops=5 * scaled.size * b.shape[1],
            bytes_accessed=6 * scaled.size,
            transcendentals=0,
        ),
        name="entry_b",
    )(place, decay, b, scaled, dx_local, part_local, *entries)


def over_heads(part):
    count = lax.axis_size("head")
    total = part.astype(F32)
    for shift in range(1, count):
        pairs = [(s, (s + shift) % count) for s in range(count)]
        total = total + lax.ppermute(part, "head", pairs).astype(F32)
    return total.astype(BF16)


def shards(token_values, b_inputs, c_inputs, log_decay, grad_out):
    head_dim = token_values.shape[1] // log_decay.shape[0]
    state = b_inputs.shape[1]
    place = lax.rem(lax.axis_index("seq"), GROUP).astype(jnp.int32)[None]
    x_scaled, x_decay, *x_sends = local_states(
        True, head_dim, place, log_decay, b_inputs, token_values
    )
    dy_scaled, _, *dy_sends = local_states(False, head_dim, place, log_decay, c_inputs, grad_out)
    state_in, blocks = carried(True, state, place, x_sends)
    adjoint_out, _ = carried(False, state, place, dy_sends, blocks)
    dx_local, db_local, dc_local = inner_terms(
        head_dim, log_decay, b_inputs, c_inputs, token_values, grad_out
    )
    part_c = entry_c(place, dy_scaled, dc_local, state_in)
    grad_values, part_b = entry_b(
        head_dim, place, x_decay, b_inputs, x_scaled, dx_local, db_local, adjoint_out
    )
    return grad_values, over_heads(part_b), over_heads(part_c)


def solution(mesh):
    in_specs = (
        P("seq", "head"),
        P("seq", None),
        P("seq", None),
        P("head", "seq"),
        P("seq", "head"),
    )
    out_specs = (P("seq", "head"), P("seq", None), P("seq", None))
    return jax.shard_map(shards, mesh=mesh, in_specs=in_specs, out_specs=out_specs, check_vma=False)
```

time: 473 us -> 56 us (0.12)
  waiting for transfers between devices: 216 us -> 8.06 us
  matrix products: 144 us -> 0 us
  blocking collectives: 44.3 us -> 0 us
  other arithmetic: 29.6 us -> 1.34 us
  starting transfers between devices: 0.12 us -> 28.2 us
  local copies, waits for them, and re-layouts: 19.6 us -> 3.12 us
  Pallas kernels: 0 us -> 14.2 us
  between operations: 14.7 us -> 0.85 us
    all_gather x2 -> x0, waiting for transfers between devices: 178 us -> none  [entering(): gathered = jax.tree.map(lambda a: lax.all_gather(a, axis), part)]
    dot_general x72 -> x0, matrix products: 144 us -> none  [the longest x32 74.9 us: head_step(): lax.dot_general(dy_head, x_head, (((1,), (1,)), ((), ())), preferred_elem...]
    unnamed x1 -> x0, blocking collectives: 44.3 us -> none
    psum x1 -> x0, waiting for transfers between devices: 38.3 us -> none  [shards(): lax.psum(db_part.astype(jnp.bfloat16), 'head').astype(jnp.float32)]
    ppermute x0 -> x18, starting transfers between devices: none -> 28.2 us  [the longest x12 15.8 us: to_member(): return lax.ppermute(block, 'seq', [(s, s ^ k) for s in range(count)])]
    add x15 -> x0, other arithmetic: 24.8 us -> none  [backward_combine(): later[1] + spread(later[0], head_dim) * earlier[1]]
    pallas_call x0 -> x11, Pallas kernels: none -> 14.2 us  [the longest x1 6.88 us: inner_terms(): pl.pallas_call(functools.partial(inner_kernel, head_dim), grid=(width //...]
    unnamed x22 -> x16, local copies, waits for them, and re-layouts: 11.8 us -> 3.12 us
  transfers between devices with their start and end apart: 3 -> 18, of which waited for: 3 -> 7; matrix products, arithmetic and copies ran while one was open for 35% -> 1% of each run, Pallas kernels for 0% -> 23%
where the time goes in v1:
time: 56 us; the launch traced here: 55.7 us
  starting transfers between devices  28.2 us (50%)
  Pallas kernels  14.2 us (25%)
  waiting for transfers between devices  8.06 us (14%)
  local copies, waits for them, and re-layouts  3.12 us (6%)
  other arithmetic  1.34 us (2%)
  between operations  0.85 us (2%)
    ppermute x12, starting transfers between devices, to_member(): return lax.ppermute(block, 'seq', [(s, s ^ k) for s in range(count)])  15.8 us
    ppermute x4, starting transfers between devices, carried(): received.append(lax.ppermute(sent, 'seq', pairs))  11.8 us
    pallas_call x1, Pallas kernels, inner_terms(): pl.pallas_call(functools.partial(inner_kernel, head_dim), grid=(width //...  6.88 us
    ppermute x4, waiting for transfers between devices, carried(): received.append(lax.ppermute(sent, 'seq', pairs))  5.01 us
    pallas_call x2, Pallas kernels, local_states(): pl.pallas_call(functools.partial(local_kernel, forward, head_dim), out_sh...  3.5 us
    unnamed x16, local copies, waits for them, and re-layouts  3.12 us
    ppermute x12, waiting for transfers between devices, to_member(): return lax.ppermute(block, 'seq', [(s, s ^ k) for s in range(count)])  2.77 us
    pallas_call x1, Pallas kernels, entry_b(): pl.pallas_call(functools.partial(entry_b_kernel, head_dim), out_shape=[ja...  2.52 us
  transfers between devices with their start and end apart: 18, of which 7 were waited for; matrix products, arithmetic and copies ran while one was open for 1% of the time, Pallas kernels for 23%

profile of v1, /device:TPU:0, one launch (start us, length us, event | category | flops | bytes accessed | tf_op | source)
XLA Modules:
  0.0 55.7 jit_solution(4018537062283052785)
XLA Ops:
  0.6 0.0 copy-start
  0.6 1.4 %copy-done = bf16[384,2048]{1,0:T(8,128)(2,1)S(1)} copy-done((bf16[384,2048]{1,0:T(8,128)(2,1)S(1)}, bf16[384,2048]{1,0:T(8,128)(2,1)}, u32[]{:S(2)}) %copy-start) | copy-done | bytes 1572888
  2.0 0.9 %copy-done.3 = bf16[384,128]{1,0:T(8,128)(2,1)S(1)} copy-done((bf16[384,128]{1,0:T(8,128)(2,1)S(1)}, bf16[384,128]{1,0:T(8,128)(2,1)}, u32[]{:S(2)}) %copy-start.3) | copy-done | bytes 98328
  2.9 0.8 %copy-done.5 = f32[32,384]{1,0:T(8,128)S(1)} copy-done((f32[32,384]{1,0:T(8,128)S(1)}, f32[32,384]{1,0:T(8,128)}, u32[]{:S(2)}) %copy-start.5) | copy-done | bytes 49176
  3.7 1.6 %states_forward.1 = (bf16[384,2048]{1,0:T(8,128)(2,1)S(1)}, bf16[384,32]{1,0:T(8,128)(2,1)S(1)}, bf16[144,512]{1,0:T(8,128)(2,1)S(1)}, bf16[144,512]{1,0:T(8,128...) custom-call(s32[1]{0:T(128)} %bitcast.place, f32[32,384]{1,0:T(8,128)S(1)} %copy-done.5, ...), custom_call_target="tpu_custom_call" | custom-call | flops 251658240 | bytes 3670016 | tf_op jit(solution)/shard_map/states_forward/pallas_call | solution.py:93
  5.3 3.0 %collective-permute-start.3 = (bf16[144,512]{1,0:T(8,128)(2,1)S(1)}, bf16[144,512]{1,0:T(8,128)(2,1)S(1)}, u32[]{:S(2)}, u32[]{:S(2)}) collective-permute-start(bf16[144,512]{1,0:T(8,128)(2,1)S(1)} %get-tuple-element.36), channel_id=1, source_target_pairs={{0,2},{2,0},{4,6},{6,4},{8,10},{10,8},{12,14},{14,12},{16,18},{18,... | collective-permute-start | bytes 442376 | tf_op jit(solution)/shard_map/ppermute | solution.py:226
  8.3 1.5 %collective-permute-start.4 = (bf16[144,512]{1,0:T(8,128)(2,1)S(1)}, bf16[144,512]{1,0:T(8,128)(2,1)S(1)}, u32[]{:S(2)}, u32[]{:S(2)}) collective-permute-start(bf16[144,512]{1,0:T(8,128)(2,1)S(1)} %get-tuple-element.37), channel_id=1, source_target_pairs={{0,4},{2,6},{4,0},{6,2},{8,12},{10,14},{12,8},{14,10},{16,20},{18,... | collective-permute-start | bytes 442376 | tf_op jit(solution)/shard_map/ppermute | solution.py:226
  9.8 0.0 collective-permute-start.5
  9.9 1.9 %states_backward.1 = (bf16[384,2048]{1,0:T(8,128)(2,1)S(1)}, bf16[384,32]{1,0:T(8,128)(2,1)}, bf16[128,512]{1,0:T(8,128)(2,1)S(1)}, bf16[128,512]{1,0:T(8,128)(2...) custom-call(s32[1]{0:T(128)} %bitcast.place, f32[32,384]{1,0:T(8,128)S(1)} %copy-done.5, ...), custom_call_target="tpu_custom_call" | custom-call | flops 251658240 | bytes 3670016 | tf_op jit(solution)/shard_map/states_backward/pallas_call | solution.py:93
  11.8 1.9 %collective-permute-start = (bf16[128,512]{1,0:T(8,128)(2,1)S(1)}, bf16[128,512]{1,0:T(8,128)(2,1)S(1)}, u32[]{:S(2)}, u32[]{:S(2)}) collective-permute-start(bf16[128,512]{1,0:T(8,128)(2,1)S(1)} %get-tuple-element.32), channel_id=1, source_target_pairs={{0,2},{2,0},{4,6},{6,4},{8,10},{10,8},{12,14},{14,12},{16,18},{18,... | collective-permute-start | bytes 393224 | tf_op jit(solution)/shard_map/ppermute | solution.py:226
  13.8 1.5 %collective-permute-start.1 = (bf16[128,512]{1,0:T(8,128)(2,1)S(1)}, bf16[128,512]{1,0:T(8,128)(2,1)S(1)}, u32[]{:S(2)}, u32[]{:S(2)}) collective-permute-start(bf16[128,512]{1,0:T(8,128)(2,1)S(1)} %get-tuple-element.33), channel_id=1, source_target_pairs={{0,4},{2,6},{4,0},{6,2},{8,12},{10,14},{12,8},{14,10},{16,20},{18,... | collective-permute-start | bytes 393224 | tf_op jit(solution)/shard_map/ppermute | solution.py:226
  15.3 0.7 %collective-permute-start.2 = (bf16[128,512]{1,0:T(8,128)(2,1)S(1)}, bf16[128,512]{1,0:T(8,128)(2,1)S(1)}, u32[]{:S(2)}, u32[]{:S(2)}) collective-permute-start(bf16[128,512]{1,0:T(8,128)(2,1)S(1)} %get-tuple-element.34), channel_id=1, source_target_pairs={{0,6},{2,4},{4,2},{6,0},{8,14},{10,12},{12,10},{14,8},{16,22},{18,... | collective-permute-start | bytes 393224 | tf_op jit(solution)/shard_map/ppermute | solution.py:226
  16.0 1.0 %collective-permute-done.4.refs_6_.refs_8_.refs_2_.refs_4_ = bf16[144,512]{1,0:T(8,128)(2,1)S(1)} collective-permute-done((bf16[144,512]{1,0:T(8,128)(2,1)S(1)}, bf16[144,512]{1,0:T(8,128)(2,1)S(1)}, u32[]{:S(2)}, u32[]{:S(2)}) %collective-permute-start.4) | collective-permute-done | bytes 147488 | tf_op jit(solution)/shard_map/ppermute | solution.py:226
  17.0 0.5 collective-permute-done.5.refs_7_.refs_9_.refs_3_.refs_5_
  17.6 0.1 group_total.3.own
  17.7 3.5 %collective-permute-start.12 = (bf16[144,512]{1,0:T(8,128)(2,1)S(1)}, bf16[144,512]{1,0:T(8,128)(2,1)S(1)}, u32[]{:S(2)}, u32[]{:S(2)}) collective-permute-start(bf16[144,512]{1,0:T(8,128)(2,1)S(1)} %group_total.3.own), channel_id=1, source_target_pairs={{0,8},{2,10},{4,12},{6,14},{8,16},{10,18},{12,20},{14,22},{16,24},... | collective-permute-start | bytes 442376 | tf_op jit(solution)/shard_map/ppermute | solution.py:235
  21.2 0.0 collective-permute-done.refs_1_.refs_3_
  21.2 1.2 %collective-permute-done.1.refs_2_.refs_4_ = bf16[128,512]{1,0:T(8,128)(2,1)S(1)} collective-permute-done((bf16[128,512]{1,0:T(8,128)(2,1)S(1)}, bf16[128,512]{1,0:T(8,128)(2,1)S(1)}, u32[]{:S(2)}, u32[]{:S(2)}) %collective-permute-start.1) | collective-permute-done | bytes 131104 | tf_op jit(solution)/shard_map/ppermute | solution.py:226
  22.4 0.0 collective-permute-done.2.refs_3_.refs_5_
  22.4 0.1 group_total.2.own
  22.5 0.0 copy-start.1
  22.6 0.0 copy-start.4
  22.6 0.0 copy-start.6
  22.6 1.4 %collective-permute-start.6 = (bf16[144,512]{1,0:T(8,128)(2,1)S(1)}, bf16[144,512]{1,0:T(8,128)(2,1)S(1)}, u32[]{:S(2)}, u32[]{:S(2)}) collective-permute-start(bf16[144,512]{1,0:T(8,128)(2,1)S(1)} %group_total.2.own), channel_id=1, source_target_pairs={{8,0},{10,2},{12,4},{14,6},{16,8},{18,10},{20,12},{22,14},{24,16},... | collective-permute-start | bytes 442376 | tf_op jit(solution)/shard_map/ppermute | solution.py:235
  24.0 0.1 onward.3
  24.1 5.6 %collective-permute-start.13 = (bf16[144,512]{1,0:T(8,128)(2,1)S(1)}, bf16[144,512]{1,0:T(8,128)(2,1)S(1)}, u32[]{:S(2)}, u32[]{:S(2)}) collective-permute-start(bf16[144,512]{1,0:T(8,128)(2,1)S(1)} %onward.3), channel_id=1, source_target_pairs={{0,16},{2,18},{4,20},{6,22},{8,24},{10,26},{12,28},{14,30},{1,17},... | collective-permute-start | bytes 442376 | tf_op jit(solution)/shard_map/ppermute | solution.py:235
  29.7 0.1 collective-permute-done.6.refs_0_
  29.7 0.1 onward.2
  29.8 1.3 %collective-permute-start.7 = (bf16[144,512]{1,0:T(8,128)(2,1)S(1)}, bf16[144,512]{1,0:T(8,128)(2,1)S(1)}, u32[]{:S(2)}, u32[]{:S(2)}) collective-permute-start(bf16[144,512]{1,0:T(8,128)(2,1)S(1)} %onward.2), channel_id=1, source_target_pairs={{16,0},{18,2},{20,4},{22,6},{24,8},{26,10},{28,12},{30,14},{17,1},... | collective-permute-start | bytes 442376 | tf_op jit(solution)/shard_map/ppermute | solution.py:235
  31.1 1.2 %collective-permute-done.13.refs_1_ = bf16[144,512]{1,0:T(8,128)(2,1)S(1)} collective-permute-done((bf16[144,512]{1,0:T(8,128)(2,1)S(1)}, bf16[144,512]{1,0:T(8,128)(2,1)S(1)}, u32[]{:S(2)}, u32[]{:S(2)}) %collective-permute-start.13) | collective-permute-done | bytes 147488 | tf_op jit(solution)/shard_map/ppermute | solution.py:235
  32.3 0.2 member_entries.3
  32.5 1.3 %collective-permute-start.14 = (bf16[128,512]{1,0:T(8,128)(2,1)S(1)}, bf16[128,512]{1,0:T(8,128)(2,1)S(1)}, u32[]{:S(2)}, u32[]{:S(2)}) collective-permute-start(bf16[128,512]{1,0:T(8,128)(2,1)S(1)} %get-tuple-element.48), channel_id=1, source_target_pairs={{0,2},{2,0},{4,6},{6,4},{8,10},{10,8},{12,14},{14,12},{16,18},{18,... | collective-permute-start | bytes 393224 | tf_op jit(solution)/shard_map/ppermute | solution.py:226
  33.8 0.8 %collective-permute-start.15 = (bf16[128,512]{1,0:T(8,128)(2,1)S(1)}, bf16[128,512]{1,0:T(8,128)(2,1)S(1)}, u32[]{:S(2)}, u32[]{:S(2)}) collective-permute-start(bf16[128,512]{1,0:T(8,128)(2,1)S(1)} %get-tuple-element.49), channel_id=1, source_target_pairs={{0,4},{2,6},{4,0},{6,2},{8,12},{10,14},{12,8},{14,10},{16,20},{18,... | collective-permute-start | bytes 393224 | tf_op jit(solution)/shard_map/ppermute | solution.py:226
  34.6 1.5 %collective-permute-start.16 = (bf16[128,512]{1,0:T(8,128)(2,1)S(1)}, bf16[128,512]{1,0:T(8,128)(2,1)S(1)}, u32[]{:S(2)}, u32[]{:S(2)}) collective-permute-start(bf16[128,512]{1,0:T(8,128)(2,1)S(1)} %get-tuple-element.50), channel_id=1, source_target_pairs={{0,6},{2,4},{4,2},{6,0},{8,14},{10,12},{12,10},{14,8},{16,22},{18,... | collective-permute-start | bytes 393224 | tf_op jit(solution)/shard_map/ppermute | solution.py:226
  36.1 3.7 %collective-permute-done.7.refs_1_ = bf16[144,512]{1,0:T(8,128)(2,1)S(1)} collective-permute-done((bf16[144,512]{1,0:T(8,128)(2,1)S(1)}, bf16[144,512]{1,0:T(8,128)(2,1)S(1)}, u32[]{:S(2)}, u32[]{:S(2)}) %collective-permute-start.7) | collective-permute-done | bytes 147488 | tf_op jit(solution)/shard_map/ppermute | solution.py:235
  39.8 0.2 member_entries.2
  39.9 1.3 %collective-permute-start.10 = (bf16[128,512]{1,0:T(8,128)(2,1)S(1)}, bf16[128,512]{1,0:T(8,128)(2,1)S(1)}, u32[]{:S(2)}, u32[]{:S(2)}) collective-permute-start(bf16[128,512]{1,0:T(8,128)(2,1)S(1)} %get-tuple-element.42), channel_id=1, source_target_pairs={{0,6},{2,4},{4,2},{6,0},{8,14},{10,12},{12,10},{14,8},{16,22},{18,... | collective-permute-start | bytes 393224 | tf_op jit(solution)/shard_map/ppermute | solution.py:226
  41.2 2.1 %collective-permute-start.8 = (bf16[128,512]{1,0:T(8,128)(2,1)S(1)}, bf16[128,512]{1,0:T(8,128)(2,1)S(1)}, u32[]{:S(2)}, u32[]{:S(2)}) collective-permute-start(bf16[128,512]{1,0:T(8,128)(2,1)S(1)} %get-tuple-element.40), channel_id=1, source_target_pairs={{0,2},{2,0},{4,6},{6,4},{8,10},{10,8},{12,14},{14,12},{16,18},{18,... | collective-permute-start | bytes 393224 | tf_op jit(solution)/shard_map/ppermute | solution.py:226
  43.3 0.0 collective-permute-done.14.refs_1_
  43.3 0.2 collective-permute-start.9
  43.5 6.9 %inner_terms.1 = (bf16[384,2048]{1,0:T(8,128)(2,1)S(1)}, f32[384,128]{1,0:T(8,128)S(1)}, f32[384,128]{1,0:T(8,128)S(1)}) custom-call(f32[32,384]{1,0:T(8,128)S(1)} %copy-done.6, bf16[384,128]{1,0:T(8,128)(2,1)S(1)} %copy-done.4, bf16[384,128]{1,0:T(8,128)(2,1)S(1)} %copy-done.7, bf16[384,2048]{1,0:T(8,128)(2,1)S(1)} %copy-done.1, bf16[384,2048]{1,0:T(8,128)(2,1)S(1)} %copy-done.2), custom_call_target="tpu_custom_call" | custom-call | flops 1610612736 | bytes 4718592 | tf_op jit(solution)/shard_map/inner_terms/pallas_call | solution.py:354
  50.4 0.6 %entry_c.1 = bf16[384,128]{1,0:T(8,128)(2,1)S(1)} custom-call(s32[1]{0:T(128)} %bitcast.place, bf16[384,2048]{1,0:T(8,128)(2,1)S(1)} %get-tuple-element.45.scaled, f32[384,128]{1,0:T(8,128)S(1)} %get-tuple-element.46.part_local, bf16[128,512]{1,0:T(8,128)(2,1)S(1)} %get-tuple-element.47.refs_0_, bf16[128,512]{1,0:T(8,128)(2,1)S(1)} %collective-permute-done.14.refs_1_, ...), custom_call_target="tpu_custom_call" | custom-call | flops 201326592 | bytes 1572864 | tf_op jit(solution)/shard_map/entry_c/pallas_call | solution.py:393
  51.0 0.1 collective-permute-start.17
  51.1 2.5 %entry_b.1 = (bf16[384,2048]{1,0:T(8,128)(2,1)}, bf16[384,128]{1,0:T(8,128)(2,1)S(1)}) custom-call(s32[1]{0:T(128)} %bitcast.place, bf16[384,32]{1,0:T(8,128)(2,1)S(1)} %get-tuple-element.27.decay, bf16[384,128]{1,0:T(8,128)(2,1)S(1)} %copy-done.4, bf16[384,2048]{1,0:T(8,128)(2,1)S(1)} %get-tuple-element.28.scaled, ...), custom_call_target="tpu_custom_call" | custom-call | flops 503316480 | bytes 4718592 | tf_op jit(solution)/shard_map/entry_b/pallas_call | solution.py:426
  53.6 0.5 collective-permute-start.11
  54.1 0.7 %add_convert_fusion = bf16[384,128]{1,0:T(8,128)(2,1)} fusion(bf16[384,128]{1,0:T(8,128)(2,1)S(1)} %collective-permute-done.17, bf16[384,128]{1,0:T(8,128)(2,1)S(1)} %entry_c.1), kind=kLoop, calls=%fused_computation | loop fusion | flops 196608 | bytes 294912 | tf_op jit(solution)/shard_map/convert_element_type | solution.py:450
  54.8 0.3 collective-permute-done.11
  55.1 0.7 %add_convert_fusion.1 = bf16[384,128]{1,0:T(8,128)(2,1)} fusion(bf16[384,128]{1,0:T(8,128)(2,1)S(1)} %collective-permute-done.11, bf16[384,128]{1,0:T(8,128)(2,1)S(1)} %get-tuple-element.44), kind=kLoop, calls=%fused_computation.1 | loop fusion | flops 196608 | bytes 294912 | tf_op jit(solution)/shard_map/convert_element_type | solution.py:450
  (17 shorter events, 0.0 us)
Async XLA Ops:
  0.6 1.4 %copy-start = (bf16[384,2048]{1,0:T(8,128)(2,1)S(1)}, bf16[384,2048]{1,0:T(8,128)(2,1)}, u32[]{:S(2)}) copy-start(bf16[384,2048]{1,0:T(8,128)(2,1)} %x.1) | copy-start | bytes 4718596
  2.0 0.9 %copy-start.3 = (bf16[384,128]{1,0:T(8,128)(2,1)S(1)}, bf16[384,128]{1,0:T(8,128)(2,1)}, u32[]{:S(2)}) copy-start(bf16[384,128]{1,0:T(8,128)(2,1)} %b.3) | copy-start | bytes 294916
  2.9 0.8 %copy-start.5 = (f32[32,384]{1,0:T(8,128)S(1)}, f32[32,384]{1,0:T(8,128)}, u32[]{:S(2)}) copy-start(f32[32,384]{1,0:T(8,128)} %ld.5) | copy-start | bytes 147460
  3.7 6.1 %copy-start.2 = (bf16[384,2048]{1,0:T(8,128)(2,1)S(1)}, bf16[384,2048]{1,0:T(8,128)(2,1)}, u32[]{:S(2)}) copy-start(bf16[384,2048]{1,0:T(8,128)(2,1)} %cols.3) | copy-start | bytes 4718596
  3.7 6.1 %copy-start.7 = (bf16[384,128]{1,0:T(8,128)(2,1)S(1)}, bf16[384,128]{1,0:T(8,128)(2,1)}, u32[]{:S(2)}) copy-start(bf16[384,128]{1,0:T(8,128)(2,1)} %proj.3) | copy-start | bytes 294916
  5.3 10.0 %collective-permute-start.3 = (bf16[144,512]{1,0:T(8,128)(2,1)S(1)}, bf16[144,512]{1,0:T(8,128)(2,1)S(1)}, u32[]{:S(2)}, u32[]{:S(2)}) collective-permute-start(bf16[144,512]{1,0:T(8,128)(2,1)S(1)} %get-tuple-element.36), channel_id=1, source_target_pairs={{0,2},{2,0},{4,6},{6,4},{8,10},{10,8},{12,14},{14,12},{16,18},{18,... | collective-permute-start | bytes 442376 | tf_op jit(solution)/shard_map/ppermute | solution.py:226
  8.3 8.7 %collective-permute-start.4 = (bf16[144,512]{1,0:T(8,128)(2,1)S(1)}, bf16[144,512]{1,0:T(8,128)(2,1)S(1)}, u32[]{:S(2)}, u32[]{:S(2)}) collective-permute-start(bf16[144,512]{1,0:T(8,128)(2,1)S(1)} %get-tuple-element.37), channel_id=1, source_target_pairs={{0,4},{2,6},{4,0},{6,2},{8,12},{10,14},{12,8},{14,10},{16,20},{18,... | collective-permute-start | bytes 442376 | tf_op jit(solution)/shard_map/ppermute | solution.py:226
  9.8 7.7 %collective-permute-start.5 = (bf16[144,512]{1,0:T(8,128)(2,1)S(1)}, bf16[144,512]{1,0:T(8,128)(2,1)S(1)}, u32[]{:S(2)}, u32[]{:S(2)}) collective-permute-start(bf16[144,512]{1,0:T(8,128)(2,1)S(1)} %get-tuple-element.38), channel_id=1, source_target_pairs={{0,6},{2,4},{4,2},{6,0},{8,14},{10,12},{12,10},{14,8},{16,22},{18,... | collective-permute-start | bytes 442376 | tf_op jit(solution)/shard_map/ppermute | solution.py:226
  11.8 9.4 %collective-permute-start = (bf16[128,512]{1,0:T(8,128)(2,1)S(1)}, bf16[128,512]{1,0:T(8,128)(2,1)S(1)}, u32[]{:S(2)}, u32[]{:S(2)}) collective-permute-start(bf16[128,512]{1,0:T(8,128)(2,1)S(1)} %get-tuple-element.32), channel_id=1, source_target_pairs={{0,2},{2,0},{4,6},{6,4},{8,10},{10,8},{12,14},{14,12},{16,18},{18,... | collective-permute-start | bytes 393224 | tf_op jit(solution)/shard_map/ppermute | solution.py:226
  13.8 8.6 %collective-permute-start.1 = (bf16[128,512]{1,0:T(8,128)(2,1)S(1)}, bf16[128,512]{1,0:T(8,128)(2,1)S(1)}, u32[]{:S(2)}, u32[]{:S(2)}) collective-permute-start(bf16[128,512]{1,0:T(8,128)(2,1)S(1)} %get-tuple-element.33), channel_id=1, source_target_pairs={{0,4},{2,6},{4,0},{6,2},{8,12},{10,14},{12,8},{14,10},{16,20},{18,... | collective-permute-start | bytes 393224 | tf_op jit(solution)/shard_map/ppermute | solution.py:226
  15.3 7.1 %collective-permute-start.2 = (bf16[128,512]{1,0:T(8,128)(2,1)S(1)}, bf16[128,512]{1,0:T(8,128)(2,1)S(1)}, u32[]{:S(2)}, u32[]{:S(2)}) collective-permute-start(bf16[128,512]{1,0:T(8,128)(2,1)S(1)} %get-tuple-element.34), channel_id=1, source_target_pairs={{0,6},{2,4},{4,2},{6,0},{8,14},{10,12},{12,10},{14,8},{16,22},{18,... | collective-permute-start | bytes 393224 | tf_op jit(solution)/shard_map/ppermute | solution.py:226
  17.7 6.3 %collective-permute-start.12 = (bf16[144,512]{1,0:T(8,128)(2,1)S(1)}, bf16[144,512]{1,0:T(8,128)(2,1)S(1)}, u32[]{:S(2)}, u32[]{:S(2)}) collective-permute-start(bf16[144,512]{1,0:T(8,128)(2,1)S(1)} %group_total.3.own), channel_id=1, source_target_pairs={{0,8},{2,10},{4,12},{6,14},{8,16},{10,18},{12,20},{14,22},{16,24},... | collective-permute-start | bytes 442376 | tf_op jit(solution)/shard_map/ppermute | solution.py:235
  22.5 21.0 %copy-start.1 = (bf16[384,2048]{1,0:T(8,128)(2,1)S(1)}, bf16[384,2048]{1,0:T(8,128)(2,1)}, u32[]{:S(2)}) copy-start(bf16[384,2048]{1,0:T(8,128)(2,1)} %x.1) | copy-start | bytes 4718596
  22.6 20.9 %copy-start.4 = (bf16[384,128]{1,0:T(8,128)(2,1)S(1)}, bf16[384,128]{1,0:T(8,128)(2,1)}, u32[]{:S(2)}) copy-start(bf16[384,128]{1,0:T(8,128)(2,1)} %b.3) | copy-start | bytes 294916
  22.6 20.9 %copy-start.6 = (f32[32,384]{1,0:T(8,128)S(1)}, f32[32,384]{1,0:T(8,128)}, u32[]{:S(2)}) copy-start(f32[32,384]{1,0:T(8,128)} %ld.5) | copy-start | bytes 147460
  22.6 7.2 %collective-permute-start.6 = (bf16[144,512]{1,0:T(8,128)(2,1)S(1)}, bf16[144,512]{1,0:T(8,128)(2,1)S(1)}, u32[]{:S(2)}, u32[]{:S(2)}) collective-permute-start(bf16[144,512]{1,0:T(8,128)(2,1)S(1)} %group_total.2.own), channel_id=1, source_target_pairs={{8,0},{10,2},{12,4},{14,6},{16,8},{18,10},{20,12},{22,14},{24,16},... | collective-permute-start | bytes 442376 | tf_op jit(solution)/shard_map/ppermute | solution.py:235
  24.1 8.3 %collective-permute-start.13 = (bf16[144,512]{1,0:T(8,128)(2,1)S(1)}, bf16[144,512]{1,0:T(8,128)(2,1)S(1)}, u32[]{:S(2)}, u32[]{:S(2)}) collective-permute-start(bf16[144,512]{1,0:T(8,128)(2,1)S(1)} %onward.3), channel_id=1, source_target_pairs={{0,16},{2,18},{4,20},{6,22},{8,24},{10,26},{12,28},{14,30},{1,17},... | collective-permute-start | bytes 442376 | tf_op jit(solution)/shard_map/ppermute | solution.py:235
  29.8 10.0 %collective-permute-start.7 = (bf16[144,512]{1,0:T(8,128)(2,1)S(1)}, bf16[144,512]{1,0:T(8,128)(2,1)S(1)}, u32[]{:S(2)}, u32[]{:S(2)}) collective-permute-start(bf16[144,512]{1,0:T(8,128)(2,1)S(1)} %onward.2), channel_id=1, source_target_pairs={{16,0},{18,2},{20,4},{22,6},{24,8},{26,10},{28,12},{30,14},{17,1},... | collective-permute-start | bytes 442376 | tf_op jit(solution)/shard_map/ppermute | solution.py:235
  32.5 10.8 %collective-permute-start.14 = (bf16[128,512]{1,0:T(8,128)(2,1)S(1)}, bf16[128,512]{1,0:T(8,128)(2,1)S(1)}, u32[]{:S(2)}, u32[]{:S(2)}) collective-permute-start(bf16[128,512]{1,0:T(8,128)(2,1)S(1)} %get-tuple-element.48), channel_id=1, source_target_pairs={{0,2},{2,0},{4,6},{6,4},{8,10},{10,8},{12,14},{14,12},{16,18},{18,... | collective-permute-start | bytes 393224 | tf_op jit(solution)/shard_map/ppermute | solution.py:226
  33.8 16.6 %collective-permute-start.15 = (bf16[128,512]{1,0:T(8,128)(2,1)S(1)}, bf16[128,512]{1,0:T(8,128)(2,1)S(1)}, u32[]{:S(2)}, u32[]{:S(2)}) collective-permute-start(bf16[128,512]{1,0:T(8,128)(2,1)S(1)} %get-tuple-element.49), channel_id=1, source_target_pairs={{0,4},{2,6},{4,0},{6,2},{8,12},{10,14},{12,8},{14,10},{16,20},{18,... | collective-permute-start | bytes 393224 | tf_op jit(solution)/shard_map/ppermute | solution.py:226
  34.6 15.8 %collective-permute-start.16 = (bf16[128,512]{1,0:T(8,128)(2,1)S(1)}, bf16[128,512]{1,0:T(8,128)(2,1)S(1)}, u32[]{:S(2)}, u32[]{:S(2)}) collective-permute-start(bf16[128,512]{1,0:T(8,128)(2,1)S(1)} %get-tuple-element.50), channel_id=1, source_target_pairs={{0,6},{2,4},{4,2},{6,0},{8,14},{10,12},{12,10},{14,8},{16,22},{18,... | collective-permute-start | bytes 393224 | tf_op jit(solution)/shard_map/ppermute | solution.py:226
  39.9 11.1 %collective-permute-start.10 = (bf16[128,512]{1,0:T(8,128)(2,1)S(1)}, bf16[128,512]{1,0:T(8,128)(2,1)S(1)}, u32[]{:S(2)}, u32[]{:S(2)}) collective-permute-start(bf16[128,512]{1,0:T(8,128)(2,1)S(1)} %get-tuple-element.42), channel_id=1, source_target_pairs={{0,6},{2,4},{4,2},{6,0},{8,14},{10,12},{12,10},{14,8},{16,22},{18,... | collective-permute-start | bytes 393224 | tf_op jit(solution)/shard_map/ppermute | solution.py:226
  41.2 9.9 %collective-permute-start.8 = (bf16[128,512]{1,0:T(8,128)(2,1)S(1)}, bf16[128,512]{1,0:T(8,128)(2,1)S(1)}, u32[]{:S(2)}, u32[]{:S(2)}) collective-permute-start(bf16[128,512]{1,0:T(8,128)(2,1)S(1)} %get-tuple-element.40), channel_id=1, source_target_pairs={{0,2},{2,0},{4,6},{6,4},{8,10},{10,8},{12,14},{14,12},{16,18},{18,... | collective-permute-start | bytes 393224 | tf_op jit(solution)/shard_map/ppermute | solution.py:226
  43.3 7.8 %collective-permute-start.9 = (bf16[128,512]{1,0:T(8,128)(2,1)S(1)}, bf16[128,512]{1,0:T(8,128)(2,1)S(1)}, u32[]{:S(2)}, u32[]{:S(2)}) collective-permute-start(bf16[128,512]{1,0:T(8,128)(2,1)S(1)} %get-tuple-element.41), channel_id=1, source_target_pairs={{0,4},{2,6},{4,0},{6,2},{8,12},{10,14},{12,8},{14,10},{16,20},{18,... | collective-permute-start | bytes 393224 | tf_op jit(solution)/shard_map/ppermute | solution.py:226
  51.0 3.1 %collective-permute-start.17 = (bf16[384,128]{1,0:T(8,128)(2,1)S(1)}, bf16[384,128]{1,0:T(8,128)(2,1)S(1)}, u32[]{:S(2)}, u32[]{:S(2)}) collective-permute-start(bf16[384,128]{1,0:T(8,128)(2,1)S(1)} %entry_c.1), channel_id=1, source_target_pairs={{0,1},{1,0},{2,3},{3,2},{4,5},{5,4},{6,7},{7,6},{8,9},{9,8},{10,11... | collective-permute-start | bytes 294920 | tf_op jit(solution)/shard_map/ppermute | solution.py:449
  53.6 1.4 %collective-permute-start.11 = (bf16[384,128]{1,0:T(8,128)(2,1)S(1)}, bf16[384,128]{1,0:T(8,128)(2,1)S(1)}, u32[]{:S(2)}, u32[]{:S(2)}) collective-permute-start(bf16[384,128]{1,0:T(8,128)(2,1)S(1)} %get-tuple-element.44), channel_id=1, source_target_pairs={{0,1},{1,0},{2,3},{3,2},{4,5},{5,4},{6,7},{7,6},{8,9},{9,8},{10,11... | collective-permute-start | bytes 294920 | tf_op jit(solution)/shard_map/ppermute | solution.py:449

commit v2 on v1

v2 whole, which is shorter than its diff:
```python
import functools

import jax
import jax.numpy as jnp
from jax import lax
from jax.experimental import pallas as pl
from jax.experimental.pallas import tpu as pltpu
from jax.sharding import PartitionSpec as P

BF16 = jnp.bfloat16
F32 = jnp.float32
LANES = 128
TAIL = 16
LOG2E = 1.4426950408889634
MIB = 1024 * 1024

NN = (((1,), (0,)), ((), ()))
NT = (((1,), (1,)), ((), ()))
TN = (((0,), (0,)), ((), ()))


def dot(a, b, dims):
    return lax.dot_general(a, b, dims, preferred_element_type=F32)


def iota(shape, dim):
    return lax.broadcasted_iota(jnp.int32, shape, dim)


def three(values):
    high = values.astype(BF16)
    rest = values - high.astype(F32)
    mid = rest.astype(BF16)
    return high, mid, (rest - mid.astype(F32)).astype(BF16)


def summed(mask, terms, copies=1):
    return sum(dot(mask, jnp.concatenate([t] * copies, axis=0), NT) for t in terms)


def head_of_lane(heads, head_dim, width, first, copies=1):
    shape = (copies * heads, width)
    rows = iota(shape, 0)
    if copies > 1:
        rows = lax.rem(rows, heads)
    return jnp.where(rows == first + iota(shape, 1) // head_dim, 1.0, 0.0).astype(BF16)


def whole(count):
    return [pl.BlockSpec(memory_space=pltpu.VMEM)] * count


SMEM = pl.BlockSpec(memory_space=pltpu.SMEM)


def params(mib):
    return pltpu.CompilerParams(vmem_limit_bytes=mib * MIB)


def states_kernel(head_dim, group, ld_in, b_in, c_in, x_in, dy_in, *refs):
    x_scaled, dy_scaled, decay, sends, ld, b, c, x, dy, sems = refs
    pairs = [(ld_in, ld), (b_in, b), (x_in, x), (c_in, c), (dy_in, dy)]
    copies = [pltpu.make_async_copy(i, o, sems.at[n]) for n, (i, o) in enumerate(pairs)]
    for copy in copies:
        copy.start()
    copies[0].wait()
    heads, length = ld.shape
    state, part = b.shape[1], x.shape[1] // group
    terms = three(ld[...])
    rows, other = iota((length, length), 0), iota((length, length), 1)
    after = jnp.where(other > rows, 1.0, 0.0).astype(BF16)
    until = jnp.where(other <= rows, 1.0, 0.0).astype(BF16)
    into_end = jnp.exp(summed(after, terms)).astype(BF16)
    from_start = jnp.exp(summed(until, terms)).astype(BF16)
    decay[...] = into_end
    total = jnp.exp(summed(jnp.ones((TAIL, length), BF16), terms))
    high = total.astype(BF16).astype(F32)
    halves = jnp.where(iota(total.shape, 0) < TAIL // 2, high, total - high).astype(BF16)
    sides = [(into_end, b, x, x_scaled, 0), (from_start, c, dy, dy_scaled, state)]
    for side, (factors, proj, cols, scaled, first) in enumerate(sides):
        copies[1 + 2 * side].wait()
        copies[2 + 2 * side].wait()
        for j in range(group):
            lanes = slice(j * part, (j + 1) * part)
            hot = head_of_lane(heads, head_dim, part, j * (heads // group))
            piece = cols[:, lanes] * dot(factors, hot, NN).astype(BF16)
            scaled[:, lanes] = piece
            sends[j, first : first + state, :] = dot(proj[...], piece, TN).astype(BF16)
            if side == 0:
                sends[j, 2 * state :, :] = dot(halves, hot, NN).astype(BF16)


def local_states(head_dim, group, ld, b, c, x, dy):
    heads, length = ld.shape
    state, width = b.shape[1], x.shape[1]
    inputs = (ld, b, c, x, dy)
    return pl.pallas_call(
        functools.partial(states_kernel, head_dim, group),
        out_shape=[
            jax.ShapeDtypeStruct(x.shape, BF16),
            jax.ShapeDtypeStruct(x.shape, BF16),
            jax.ShapeDtypeStruct((length, heads), BF16),
            jax.ShapeDtypeStruct((group, 2 * state + TAIL, width // group), BF16),
        ],
        in_specs=[pl.BlockSpec(memory_space=pltpu.HBM)] * 5,
        out_specs=whole(4),
        scratch_shapes=[pltpu.VMEM(a.shape, a.dtype) for a in inputs]
        + [pltpu.SemaphoreType.DMA((5,))],
        compiler_params=params(24),
        cost_estimate=pl.CostEstimate(
            flops=4 * length * width * (state + heads),
            bytes_accessed=8 * length * width + 4 * state * width,
            transcendentals=2 * length * heads,
        ),
        name="local_states",
    )(*inputs)


def decay_of(tail):
    tail = tail.astype(F32)
    return tail[:1, :] + tail[TAIL // 2 : TAIL // 2 + 1, :]


def put(ref, state, value, factor):
    ref[:state, :] = value.astype(BF16)
    high = factor.astype(BF16).astype(F32)
    shape = (TAIL, factor.shape[1])
    both = jnp.where(iota(shape, 0) < TAIL // 2, high, factor - high)
    ref[state:, :] = both.astype(BF16)


def in_order(group, forward):
    return range(group) if forward else range(group - 1, -1, -1)


def side_rows(state, forward):
    return slice(0, state) if forward else slice(state, 2 * state)


def group_total(blocks, state, forward):
    group = blocks.shape[0]
    value, factor = None, None
    for q in in_order(group, forward):
        piece = blocks[q, side_rows(state, forward), :].astype(F32)
        d = decay_of(blocks[q, 2 * state :, :])
        value = piece if value is None else d * value + piece
        factor = d if factor is None else factor * d
    return value, factor


def totals_kernel(state, upper, blocks, *outs):
    if len(outs) == 2:
        for forward, out in zip((True, False), outs):
            put(out, state, *group_total(blocks, state, forward))
        return
    for forward in (True, False):

        @pl.when(upper[0] == (0 if forward else 1))
        def _(forward=forward):
            put(outs[0], state, *group_total(blocks, state, forward))


def totals(state, count, upper, blocks):
    part = blocks.shape[2]
    return pl.pallas_call(
        functools.partial(totals_kernel, state),
        out_shape=[jax.ShapeDtypeStruct((state + TAIL, part), BF16)] * count,
        in_specs=[SMEM] + whole(1),
        out_specs=whole(count),
        compiler_params=params(8),
        cost_estimate=pl.CostEstimate(
            flops=2 * blocks.size, bytes_accessed=2 * blocks.size, transcendentals=0
        ),
        name="totals",
    )(upper, blocks)


def before_group(state, received):
    value = received[0][:state, :].astype(F32)
    factor = decay_of(received[0][state:, :])
    for r in received[1:]:
        value = value + factor * r[:state, :].astype(F32)
        factor = factor * decay_of(r[state:, :])
    return value, factor


def onward_kernel(state, own, *refs):
    received, out = refs[:-1], refs[-1]
    value, factor = before_group(state, received)
    d = decay_of(own[state:, :])
    put(out, state, own[:state, :].astype(F32) + d * value, d * factor)


def onward(state, own, received):
    return pl.pallas_call(
        functools.partial(onward_kernel, state),
        out_shape=jax.ShapeDtypeStruct(own.shape, BF16),
        in_specs=whole(1 + len(received)),
        out_specs=whole(1)[0],
        compiler_params=params(8),
        cost_estimate=pl.CostEstimate(
            flops=4 * own.size, bytes_accessed=6 * own.size, transcendentals=0
        ),
        name="onward",
    )(own, *received)


def members_kernel(state, upper, blocks, *refs):
    received, out = refs[:-1], refs[-1]
    group = blocks.shape[0]
    for forward in (True, False):
        if len(received) == 1:
            mine = upper[0] == (1 if forward else 0)
            value = received[0][:state, :].astype(F32) * jnp.where(mine, 1.0, 0.0)
        else:
            half = len(received) // 2
            value, _ = before_group(state, received[:half] if forward else received[half:])
        order = list(in_order(group, forward))
        for q in order:
            out[q, side_rows(state, forward), :] = value.astype(BF16)
            if q != order[-1]:
                d = decay_of(blocks[q, 2 * state :, :])
                value = d * value + blocks[q, side_rows(state, forward), :].astype(F32)


def member_entries(state, upper, blocks, received):
    group, _, part = blocks.shape
    return pl.pallas_call(
        functools.partial(members_kernel, state),
        out_shape=jax.ShapeDtypeStruct((group, 2 * state, part), BF16),
        in_specs=[SMEM] + whole(1 + len(received)),
        out_specs=whole(1)[0],
        compiler_params=params(8),
        cost_estimate=pl.CostEstimate(
            flops=3 * blocks.size, bytes_accessed=4 * blocks.size, transcendentals=0
        ),
        name="member_entries",
    )(upper, blocks, *received)


def group_size(count, width):
    for group in (8, 4, 2):
        if count % group == 0 and (width // group) % LANES == 0:
            return group
    return 1


def entering(group, state, sends):
    count = lax.axis_size("seq")
    groups = count // group
    members = [[n * group + j for j in range(group)] for n in range(groups)]

    def exchange(blocks):
        return lax.all_to_all(
            blocks, "seq", 0, 0, axis_index_groups=members, tiled=True
        )

    upper = (lax.axis_index("seq") // group).astype(jnp.int32)[None]
    blocks = exchange(sends)
    if groups == 2:
        (own,) = totals(state, 1, upper, blocks)
        pairs = [(s, (s + group) % count) for s in range(count)]
        received = [lax.ppermute(own, "seq", pairs)]
    else:
        received = []
        for own, sign in zip(totals(state, 2, upper, blocks), (1, -1)):
            arrived, sent, step = [], own, 1
            while step < groups:
                jump = sign * step * group
                pairs = [(s, s + jump) for s in range(count) if 0 <= s + jump < count]
                arrived.append(lax.ppermute(sent, "seq", pairs))
                step *= 2
                if step < groups:
                    sent = onward(state, own, arrived)
            received += arrived
    return exchange(member_entries(state, upper, blocks, received))


def split_pairs(first, count):
    if count == 1:
        return []
    middle = first + count // 2
    return (
        [(first, middle, first + count)]
        + split_pairs(first, middle - first)
        + split_pairs(middle, first + count - middle)
    )


def inner_kernel(head_dim, ld, b, c, x, dy, dx_out, db_out, dc_out, cum_terms, *scratch):
    heads, length = ld.shape
    width, state = x.shape[1], b.shape[1]
    piece = head_dim
    pieces = length // piece
    cuts = split_pairs(0, pieces)
    near, near_sum, dx = scratch[:3]
    far, far_sum = scratch[3 : 3 + len(cuts)], scratch[3 + len(cuts) :]
    per_tile = LANES // head_dim
    step = pl.program_id(0)

    @pl.when(step == 0)
    def _():
        terms = three(ld[...] * LOG2E)
        rows, other = iota((length, length), 0), iota((length, length), 1)
        mask = jnp.where(other <= rows, 1.0, 0.0).astype(BF16)
        high, mid, low = three(summed(mask, terms, copies=3))
        lane = iota((length, 3 * heads), 1)
        picked = jnp.where(
            lane < heads,
            high.astype(F32),
            jnp.where(lane < 2 * heads, mid.astype(F32), low.astype(F32)),
        )
        cum_terms[...] = picked.astype(BF16)
        keep = iota((piece, LANES), 0) <= lax.rem(iota((piece, LANES), 1), piece)
        for n in range(pieces):
            rows_n = slice(n * piece, (n + 1) * piece)
            doubled = jnp.concatenate([c[rows_n, :]] * per_tile, axis=0)
            near[rows_n, :] = jnp.where(keep, dot(b[rows_n, :], doubled, NT), 0.0)
        near_sum[...] = jnp.zeros_like(near_sum)
        for (lo, mid_, hi), f, total in zip(cuts, far, far_sum):
            left, right = slice(lo * piece, mid_ * piece), slice(mid_ * piece, hi * piece)
            f[...] = dot(b[left, :], c[right, :], NT).astype(BF16)
            total[...] = jnp.zeros_like(total)

    hot = head_of_lane(heads, head_dim, width, step * (width // head_dim), copies=3)
    cum = dot(cum_terms[...], hot, NN)
    tile = (piece, LANES)
    diagonal = iota(tile, 0) == lax.rem(iota(tile, 1), piece)
    part_of_lane = iota(tile, 1) // head_dim
    for n in range(pieces):
        rows_n = slice(n * piece, (n + 1) * piece)
        total = near_sum[rows_n, :]
        scores = near[rows_n, :]
        for t in range(width // LANES):
            lanes = slice(t * LANES, (t + 1) * LANES)
            col = cum[rows_n, lanes]
            row = jnp.sum(jnp.where(diagonal, col, 0.0), axis=0, keepdims=True)
            decays = jnp.exp2(jnp.minimum(row - col, 0.0))
            dy_t = dy[rows_n, lanes]
            stacked = jnp.concatenate(
                [jnp.where(part_of_lane == h, dy_t, jnp.zeros_like(dy_t)) for h in range(per_tile)],
                axis=0,
            )
            dx[rows_n, lanes] = dot((scores * decays).astype(BF16), stacked, NN)
            total = total + decays * dot(x[rows_n, lanes], stacked, NT)
        near_sum[rows_n, :] = total
    for (lo, mid_, hi), f, total in zip(cuts, far, far_sum):
        left, right = slice(lo * piece, mid_ * piece), slice(mid_ * piece, hi * piece)
        edge = cum[mid_ * piece - 1 : mid_ * piece, :]
        to_edge = jnp.exp2(edge - cum[left, :])
        from_edge = jnp.exp2(cum[right, :] - edge)
        x_edge = (x[left, :].astype(F32) * to_edge).astype(BF16)
        dy_edge = (dy[right, :].astype(F32) * from_edge).astype(BF16)
        dx[left, :] += to_edge * dot(f[...], dy_edge, NN)
        total[...] += dot(x_edge, dy_edge, NT)
    dx_out[...] = dx[...].astype(BF16)

    @pl.when(step == pl.num_programs(0) - 1)
    def _():
        keep = (iota(tile, 0) <= iota(tile, 1)) & (part_of_lane == 0)
        for n in range(pieces):
            rows_n = slice(n * piece, (n + 1) * piece)
            total = near_sum[rows_n, :]
            total = sum(
                [pltpu.roll(total, h * head_dim, 1) for h in range(1, per_tile)], total
            )
            weighted = jnp.where(keep, total, 0.0).astype(BF16)
            doubled = jnp.concatenate([c[rows_n, :]] * per_tile, axis=0)
            db_out[rows_n, :] = dot(weighted, doubled, NN)
            dc_out[rows_n, :] = dot(weighted, b[rows_n, :], TN)[:piece, :]
        for (lo, mid_, hi), total in zip(cuts, far_sum):
            left, right = slice(lo * piece, mid_ * piece), slice(mid_ * piece, hi * piece)
            weighted = total[...].astype(BF16)
            db_out[left, :] += dot(weighted, c[right, :], NN)
            dc_out[right, :] += dot(weighted, b[left, :], TN)


def inner_terms(head_dim, ld, b, c, x, dy):
    heads, length = ld.shape
    state, width = b.shape[1], x.shape[1]
    chunk = width // 4
    piece = head_dim
    cuts = split_pairs(0, length // piece)
    sizes = [((mid - lo) * piece, (hi - mid) * piece) for lo, mid, hi in cuts]
    column = pl.BlockSpec((length, chunk), lambda i: (0, i))

    def fixed(shape):
        return pl.BlockSpec(shape, lambda i: (0, 0))

    return pl.pallas_call(
        functools.partial(inner_kernel, head_dim),
        grid=(width // chunk,),
        out_shape=[
            jax.ShapeDtypeStruct((length, width), BF16),
            jax.ShapeDtypeStruct((length, state), F32),
            jax.ShapeDtypeStruct((length, state), F32),
        ],
        in_specs=[fixed(ld.shape), fixed(b.shape), fixed(c.shape), column, column],
        out_specs=[column, fixed((length, state)), fixed((length, state))],
        scratch_shapes=[
            pltpu.VMEM((length, 3 * heads), BF16),
            pltpu.VMEM((length, LANES), F32),
            pltpu.VMEM((length, LANES), F32),
            pltpu.VMEM((length, chunk), F32),
        ]
        + [pltpu.VMEM(s, BF16) for s in sizes]
        + [pltpu.VMEM(s, F32) for s in sizes],
        compiler_params=params(24),
        cost_estimate=pl.CostEstimate(
            flops=16 * length * width * state,
            bytes_accessed=6 * length * width,
            transcendentals=3 * length * width,
        ),
        name="inner_terms",
    )(ld, b, c, x, dy)


def entry_kernel(head_dim, decay, b, x_scaled, dy_scaled, dx_local, db_local, dc_local, entries, *outs):
    dx_out, parts = outs
    group, rows, part = entries.shape
    state, heads, length = rows // 2, decay.shape[1], b.shape[0]
    db, dc = db_local[...], dc_local[...]
    for j in range(group):
        lanes = slice(j * part, (j + 1) * part)
        earlier, later = entries[j, :state, :], entries[j, state:, :]
        hot = head_of_lane(heads, head_dim, part, j * (heads // group))
        spread = dot(decay[...], hot, NN)
        far = dx_local[:, lanes].astype(F32) + spread * dot(b[...], later, NN)
        dx_out[:, lanes] = far.astype(BF16)
        db = db + dot(x_scaled[:, lanes], later, NT)
        dc = dc + dot(dy_scaled[:, lanes], earlier, NT)
    parts[:length, :] = db.astype(BF16)
    parts[length:, :] = dc.astype(BF16)


def entry_terms(head_dim, decay, b, x_scaled, dy_scaled, dx_local, db_local, dc_local, entries):
    length, state = b.shape
    operands = (decay, b, x_scaled, dy_scaled, dx_local, db_local, dc_local, entries)
    return pl.pallas_call(
        functools.partial(entry_kernel, head_dim),
        out_shape=[
            jax.ShapeDtypeStruct(dx_local.shape, BF16),
            jax.ShapeDtypeStruct((2 * length, state), BF16),
        ],
        in_specs=whole(len(operands)),
        out_specs=whole(2),
        compiler_params=params(20),
        cost_estimate=pl.CostEstimate(
            flops=7 * x_scaled.size * state,
            bytes_accessed=8 * x_scaled.size,
            transcendentals=0,
        ),
        name="entry_terms",
    )(*operands)


def over_heads(part):
    count = lax.axis_size("head")
    total = part.astype(F32)
    for shift in range(1, count):
        pairs = [(s, (s + shift) % count) for s in range(count)]
        total = total + lax.ppermute(part, "head", pairs).astype(F32)
    return total.astype(BF16)


def shards(token_values, b_inputs, c_inputs, log_decay, grad_out):
    head_dim = token_values.shape[1] // log_decay.shape[0]
    length, state = b_inputs.shape
    group = group_size(lax.axis_size("seq"), token_values.shape[1])
    inputs = (log_decay, b_inputs, c_inputs, token_values, grad_out)
    x_scaled, dy_scaled, decay, sends = local_states(head_dim, group, *inputs)
    entries = entering(group, state, sends)
    local = inner_terms(head_dim, *inputs)
    grad_values, parts = entry_terms(
        head_dim, decay, b_inputs, x_scaled, dy_scaled, *local, entries
    )
    both = over_heads(parts)
    return grad_values, both[:length], both[length:]


def solution(mesh):
    in_specs = (
        P("seq", "head"),
        P("seq", None),
        P("seq", None),
        P("head", "seq"),
        P("seq", "head"),
    )
    out_specs = (P("seq", "head"), P("seq", None), P("seq", None))
    return jax.shard_map(shards, mesh=mesh, in_specs=in_specs, out_specs=out_specs, check_vma=False)
```

time: 56 us -> 70 us (1.25)
  waiting for transfers between devices: 8.06 us -> 24.3 us
  starting transfers between devices: 28.2 us -> 12.5 us
  local copies, waits for them, and re-layouts: 3.12 us -> 15.2 us
  Pallas kernels: 14.2 us -> 16.6 us
  other arithmetic: 1.34 us -> 0.05 us
    ppermute x16 -> x1, starting transfers between devices: 27.6 us -> 2.64 us  [entering(): received = [lax.ppermute(own, 'seq', pairs)]]
    all_to_all x0 -> x2, waiting for transfers between devices: none -> 18.9 us  [exchange(): lax.all_to_all(blocks, 'seq', 0, 0, axis_index_groups=members, tiled=True)]
    unnamed x16 -> x32, local copies, waits for them, and re-layouts: 3.12 us -> 14.5 us
    all_to_all x0 -> x2, starting transfers between devices: none -> 9.89 us  [exchange(): lax.all_to_all(blocks, 'seq', 0, 0, axis_index_groups=members, tiled=True)]
    ppermute x16 -> x1, waiting for transfers between devices: 7.78 us -> 3.98 us  [entering(): received = [lax.ppermute(own, 'seq', pairs)]]
    pallas_call x10 -> x4, Pallas kernels: 7.3 us -> 9.78 us  [the longest x1 5.64 us: local_states(): pl.pallas_call(functools.partial(states_kernel, head_dim, group), out_sha...]
    convert_element_type x2 -> x1, other arithmetic: 1.34 us -> 0.05 us  [over_heads(): return total.astype(BF16)]
    ppermute x2 -> x1, waiting for transfers between devices: 0.27 us -> 1.44 us  [over_heads(): total = total + lax.ppermute(part, 'head', pairs).astype(F32)]
  transfers between devices with their start and end apart: 18 -> 4, of which waited for: 7 -> 4; matrix products, arithmetic and copies ran while one was open for 1% -> 0% of each run, Pallas kernels for 23% -> 10%
where the time goes in v2:
time: 70 us; the launch traced here: 69.5 us
  waiting for transfers between devices  24.3 us (35%)
  Pallas kernels  16.6 us (24%)
  local copies, waits for them, and re-layouts  15.2 us (22%)
  starting transfers between devices  12.5 us (18%)
  between operations  0.75 us (1%)
    all_to_all x2, waiting for transfers between devices, exchange(): lax.all_to_all(blocks, 'seq', 0, 0, axis_index_groups=members, tiled=True)  18.9 us
    unnamed x32, local copies, waits for them, and re-layouts  14.5 us
    all_to_all x2, starting transfers between devices, exchange(): lax.all_to_all(blocks, 'seq', 0, 0, axis_index_groups=members, tiled=True)  9.89 us
    pallas_call x1, Pallas kernels, inner_terms(): pl.pallas_call(functools.partial(inner_kernel, head_dim), grid=(width //...  6.87 us
    pallas_call x1, Pallas kernels, local_states(): pl.pallas_call(functools.partial(states_kernel, head_dim, group), out_sha...  5.64 us
    ppermute x1, waiting for transfers between devices, entering(): received = [lax.ppermute(own, 'seq', pairs)]  3.98 us
    pallas_call x1, Pallas kernels, entry_terms(): pl.pallas_call(functools.partial(entry_kernel, head_dim), out_shape=[jax....  2.82 us
    ppermute x1, starting transfers between devices, entering(): received = [lax.ppermute(own, 'seq', pairs)]  2.64 us
  transfers between devices with their start and end apart: 4, of which 4 were waited for; matrix products, arithmetic and copies ran while one was open for 0% of the time, Pallas kernels for 10%

profile of v2, /device:TPU:0, one launch (start us, length us, event | category | flops | bytes accessed | tf_op | source)
XLA Modules:
  0.0 69.5 jit_solution(10594248286475732174)
XLA Ops:
  0.6 0.0 copy-start
  0.6 1.4 %copy-done = bf16[384,2048]{1,0:T(8,128)(2,1)S(1)} copy-done((bf16[384,2048]{1,0:T(8,128)(2,1)S(1)}, bf16[384,2048]{1,0:T(8,128)(2,1)}, u32[]{:S(2)}) %copy-start) | copy-done | bytes 1572888
  2.0 0.0 copy-start.2
  2.0 1.4 %copy-done.2 = bf16[384,2048]{1,0:T(8,128)(2,1)S(1)} copy-done((bf16[384,2048]{1,0:T(8,128)(2,1)S(1)}, bf16[384,2048]{1,0:T(8,128)(2,1)}, u32[]{:S(2)}) %copy-start.2) | copy-done | bytes 1572888
  3.4 0.0 copy-start.10
  3.5 0.9 %copy-done.10 = bf16[384,128]{1,0:T(8,128)(2,1)S(1)} copy-done((bf16[384,128]{1,0:T(8,128)(2,1)S(1)}, bf16[384,128]{1,0:T(8,128)(2,1)}, u32[]{:S(2)}) %copy-start.10) | copy-done | bytes 98328
  4.3 0.0 copy-start.12
  4.3 0.9 %copy-done.12 = bf16[384,128]{1,0:T(8,128)(2,1)S(1)} copy-done((bf16[384,128]{1,0:T(8,128)(2,1)S(1)}, bf16[384,128]{1,0:T(8,128)(2,1)}, u32[]{:S(2)}) %copy-start.12) | copy-done | bytes 98328
  5.2 0.0 copy-start.14
  5.2 0.8 %copy-done.14 = f32[32,384]{1,0:T(8,128)S(1)} copy-done((f32[32,384]{1,0:T(8,128)S(1)}, f32[32,384]{1,0:T(8,128)}, u32[]{:S(2)}) %copy-start.14) | copy-done | bytes 49176
  6.0 5.6 %local_states.1 = (bf16[384,2048]{1,0:T(8,128)(2,1)S(1)}, bf16[384,2048]{1,0:T(8,128)(2,1)S(1)}, bf16[384,32]{1,0:T(8,128)(2,1)S(1)}, bf16[8,272,256]{2,1,0:T(8,128)(2,1)}) custom-call(f32[32,384]{1,0:T(8,128)S(1)} %copy-done.14, bf16[384,128]{1,0:T(8,128)(2,1)S(1)} %copy-done.10, bf16[384,128]{1,0:T(8,128)(2,1)S(1)} %copy-done.12, ...), custom_call_target="tpu_custom_call" | custom-call | flops 503316480 | bytes 7340032 | tf_op jit(solution)/shard_map/local_states/pallas_call | solution.py:97
  11.7 0.0 copy-start.4
  11.7 1.1 %copy-done.4 = bf16[384,2048]{1,0:T(8,128)(2,1)} copy-done((bf16[384,2048]{1,0:T(8,128)(2,1)}, bf16[384,2048]{1,0:T(8,128)(2,1)S(1)}, u32[]{:S(2)}) %copy-start.4) | copy-done | bytes 1572888
  12.8 0.0 copy-start.6
  12.8 1.2 %copy-done.6 = bf16[384,2048]{1,0:T(8,128)(2,1)} copy-done((bf16[384,2048]{1,0:T(8,128)(2,1)}, bf16[384,2048]{1,0:T(8,128)(2,1)S(1)}, u32[]{:S(2)}) %copy-start.6) | copy-done | bytes 1572888
  14.0 6.2 %all-to-all-start = ((bf16[8,272,256]{2,1,0:T(8,128)(2,1)}), bf16[8,272,256]{2,1,0:T(8,128)(2,1)S(1)}, u32[]{:S(2)}, u32[]{:S(2)}) async-start(bf16[8,272,256]{2,1,0:T(8,128)(2,1)} %get-tuple-element.18), calls=%async_computation | async-start | bytes 2228224 | tf_op jit(solution)/shard_map/all_to_all | solution.py:254
  20.2 15.4 %all-to-all-done.blocks = bf16[8,272,256]{2,1,0:T(8,128)(2,1)S(1)} async-done(((bf16[8,272,256]{2,1,0:T(8,128)(2,1)}), bf16[8,272,256]{2,1,0:T(8,128)(2,1)S(1)}, u32[]{:S(2)}, u32[]{:S(2)}) %all-to-all-start) | async-done | bytes 1114144 | tf_op jit(solution)/shard_map/all_to_all | solution.py:254
  35.6 0.1 totals.1
  35.7 2.6 %collective-permute-start = (bf16[144,256]{1,0:T(8,128)(2,1)S(1)}, bf16[144,256]{1,0:T(8,128)(2,1)S(1)}, u32[]{:S(2)}, u32[]{:S(2)}) collective-permute-start(bf16[144,256]{1,0:T(8,128)(2,1)S(1)} %totals.1), channel_id=1, source_target_pairs={{0,16},{2,18},{4,20},{6,22},{8,24},{10,26},{12,28},{14,30},{16,0},... | collective-permute-start | bytes 221192 | tf_op jit(solution)/shard_map/ppermute | solution.py:263
  38.4 4.0 %collective-permute-done.refs_0_ = bf16[144,256]{1,0:T(8,128)(2,1)S(1)} collective-permute-done((bf16[144,256]{1,0:T(8,128)(2,1)S(1)}, bf16[144,256]{1,0:T(8,128)(2,1)S(1)}, u32[]{:S(2)}, u32[]{:S(2)}) %collective-permute-start) | collective-permute-done | bytes 73760 | tf_op jit(solution)/shard_map/ppermute | solution.py:263
  42.3 1.2 %member_entries.1 = bf16[8,256,256]{2,1,0:T(8,128)(2,1)} custom-call(s32[1]{0:T(128)} %bitcast.upper, bf16[8,272,256]{2,1,0:T(8,128)(2,1)S(1)} %all-to-all-done.blocks, bf16[144,256]{1,0:T(8,128)(2,1)S(1)} %collective-permute-done.refs_0_), custom_call_target="tpu_custom_call" | custom-call | flops 1671168 | bytes 2228224 | tf_op jit(solution)/shard_map/member_entries/pallas_call | solution.py:228
  43.5 0.0 copy-start.1
  43.6 0.0 copy-start.11
  43.6 0.0 copy-start.13
  43.6 0.0 copy-start.15
  43.6 3.7 %all-to-all-start.1 = ((bf16[8,256,256]{2,1,0:T(8,128)(2,1)}), bf16[8,256,256]{2,1,0:T(8,128)(2,1)S(1)}, u32[]{:S(2)}, u32[]{:S(2)}) async-start(bf16[8,256,256]{2,1,0:T(8,128)(2,1)} %member_entries.1), calls=%async_computation.1 | async-start | bytes 2097152 | tf_op jit(solution)/shard_map/all_to_all | solution.py:254
  47.3 0.0 copy-done.1
  47.3 0.0 copy-done.11
  47.3 0.0 copy-done.13
  47.3 0.0 copy-done.15
  47.3 0.0 copy-start.3
  47.3 1.4 %copy-done.3 = bf16[384,2048]{1,0:T(8,128)(2,1)S(1)} copy-done((bf16[384,2048]{1,0:T(8,128)(2,1)S(1)}, bf16[384,2048]{1,0:T(8,128)(2,1)}, u32[]{:S(2)}) %copy-start.3) | copy-done | bytes 1572888
  48.7 6.9 %inner_terms.1 = (bf16[384,2048]{1,0:T(8,128)(2,1)S(1)}, f32[384,128]{1,0:T(8,128)S(1)}, f32[384,128]{1,0:T(8,128)S(1)}) custom-call(f32[32,384]{1,0:T(8,128)S(1)} %copy-done.15, bf16[384,128]{1,0:T(8,128)(2,1)S(1)} %copy-done.11, bf16[384,128]{1,0:T(8,128)(2,1)S(1)} %copy-done.13, bf16[384,2048]{1,0:T(8,128)(2,1)S(1)} %copy-done.1, ...), custom_call_target="tpu_custom_call" | custom-call | flops 1610612736 | bytes 4718592 | tf_op jit(solution)/shard_map/inner_terms/pallas_call | solution.py:390
  55.6 0.0 copy-start.8
  55.6 1.1 %copy-done.8 = bf16[384,2048]{1,0:T(8,128)(2,1)} copy-done((bf16[384,2048]{1,0:T(8,128)(2,1)}, bf16[384,2048]{1,0:T(8,128)(2,1)S(1)}, u32[]{:S(2)}) %copy-start.8) | copy-done | bytes 1572888
  56.7 3.5 %all-to-all-done.1.entries = bf16[8,256,256]{2,1,0:T(8,128)(2,1)S(1)} async-done(((bf16[8,256,256]{2,1,0:T(8,128)(2,1)}), bf16[8,256,256]{2,1,0:T(8,128)(2,1)S(1)}, u32[]{:S(2)}, u32[]{:S(2)}) %all-to-all-start.1) | async-done | bytes 1048608 | tf_op jit(solution)/shard_map/all_to_all | solution.py:254
  60.2 0.0 copy-start.5
  60.2 1.4 %copy-done.5 = bf16[384,2048]{1,0:T(8,128)(2,1)S(1)} copy-done((bf16[384,2048]{1,0:T(8,128)(2,1)S(1)}, bf16[384,2048]{1,0:T(8,128)(2,1)}, u32[]{:S(2)}) %copy-start.5) | copy-done | bytes 1572888
  61.6 0.0 copy-start.7
  61.6 1.4 %copy-done.7 = bf16[384,2048]{1,0:T(8,128)(2,1)S(1)} copy-done((bf16[384,2048]{1,0:T(8,128)(2,1)S(1)}, bf16[384,2048]{1,0:T(8,128)(2,1)}, u32[]{:S(2)}) %copy-start.7) | copy-done | bytes 1572888
  63.0 0.0 copy-start.9
  63.0 1.4 %copy-done.9 = bf16[384,2048]{1,0:T(8,128)(2,1)S(1)} copy-done((bf16[384,2048]{1,0:T(8,128)(2,1)S(1)}, bf16[384,2048]{1,0:T(8,128)(2,1)}, u32[]{:S(2)}) %copy-start.9) | copy-done | bytes 1572888
  64.5 2.8 %entry_terms.1 = (bf16[384,2048]{1,0:T(8,128)(2,1)}, bf16[768,128]{1,0:T(8,128)(2,1)S(1)}) custom-call(bf16[384,32]{1,0:T(8,128)(2,1)S(1)} %get-tuple-element.12.decay, bf16[384,128]{1,0:T(8,128)(2,1)S(1)} %copy-done.11, bf16[384,2048]{1,0:T(8,128)(2,1)S(1)} %copy-done.5, bf16[384,2048]{1,0:T(8,128)(2,1)S(1)} %copy-done.7, bf16[384,2048]{1,0:T(8,128)(2,1)S(1)} %copy-done.9, ...), custom_call_target="tpu_custom_call" | custom-call | flops 704643072 | bytes 6291456 | tf_op jit(solution)/shard_map/entry_terms/pallas_call | solution.py:439
  67.3 0.0 collective-permute-start.1
  67.3 1.4 %collective-permute-done.1 = bf16[768,128]{1,0:T(8,128)(2,1)S(1)} collective-permute-done((bf16[768,128]{1,0:T(8,128)(2,1)S(1)}, bf16[768,128]{1,0:T(8,128)(2,1)S(1)}, u32[]{:S(2)}, u32[]{:S(2)}) %collective-permute-start.1) | collective-permute-done | bytes 196640 | tf_op jit(solution)/shard_map/ppermute | solution.py:462
  68.7 0.1 add_convert_fusion
  68.8 0.7 fusion
Async XLA Ops:
  0.6 1.4 %copy-start = (bf16[384,2048]{1,0:T(8,128)(2,1)S(1)}, bf16[384,2048]{1,0:T(8,128)(2,1)}, u32[]{:S(2)}) copy-start(bf16[384,2048]{1,0:T(8,128)(2,1)} %x.1) | copy-start | bytes 4718596
  2.0 1.4 %copy-start.2 = (bf16[384,2048]{1,0:T(8,128)(2,1)S(1)}, bf16[384,2048]{1,0:T(8,128)(2,1)}, u32[]{:S(2)}) copy-start(bf16[384,2048]{1,0:T(8,128)(2,1)} %dy.1) | copy-start | bytes 4718596
  3.4 0.9 %copy-start.10 = (bf16[384,128]{1,0:T(8,128)(2,1)S(1)}, bf16[384,128]{1,0:T(8,128)(2,1)}, u32[]{:S(2)}) copy-start(bf16[384,128]{1,0:T(8,128)(2,1)} %b.3) | copy-start | bytes 294916
  4.3 0.9 %copy-start.12 = (bf16[384,128]{1,0:T(8,128)(2,1)S(1)}, bf16[384,128]{1,0:T(8,128)(2,1)}, u32[]{:S(2)}) copy-start(bf16[384,128]{1,0:T(8,128)(2,1)} %c.1) | copy-start | bytes 294916
  5.2 0.8 %copy-start.14 = (f32[32,384]{1,0:T(8,128)S(1)}, f32[32,384]{1,0:T(8,128)}, u32[]{:S(2)}) copy-start(f32[32,384]{1,0:T(8,128)} %ld.1) | copy-start | bytes 147460
  11.7 1.1 %copy-start.4 = (bf16[384,2048]{1,0:T(8,128)(2,1)}, bf16[384,2048]{1,0:T(8,128)(2,1)S(1)}, u32[]{:S(2)}) copy-start(bf16[384,2048]{1,0:T(8,128)(2,1)S(1)} %get-tuple-element.13.x_scaled) | copy-start | bytes 4718596
  12.8 1.2 %copy-start.6 = (bf16[384,2048]{1,0:T(8,128)(2,1)}, bf16[384,2048]{1,0:T(8,128)(2,1)S(1)}, u32[]{:S(2)}) copy-start(bf16[384,2048]{1,0:T(8,128)(2,1)S(1)} %get-tuple-element.14.dy_scaled) | copy-start | bytes 4718596
  14.0 21.6 %all-to-all-start = ((bf16[8,272,256]{2,1,0:T(8,128)(2,1)}), bf16[8,272,256]{2,1,0:T(8,128)(2,1)S(1)}, u32[]{:S(2)}, u32[]{:S(2)}) async-start(bf16[8,272,256]{2,1,0:T(8,128)(2,1)} %get-tuple-element.18), calls=%async_computation | async-start | bytes 2228224 | tf_op jit(solution)/shard_map/all_to_all | solution.py:254
  35.7 6.6 %collective-permute-start = (bf16[144,256]{1,0:T(8,128)(2,1)S(1)}, bf16[144,256]{1,0:T(8,128)(2,1)S(1)}, u32[]{:S(2)}, u32[]{:S(2)}) collective-permute-start(bf16[144,256]{1,0:T(8,128)(2,1)S(1)} %totals.1), channel_id=1, source_target_pairs={{0,16},{2,18},{4,20},{6,22},{8,24},{10,26},{12,28},{14,30},{16,0},... | collective-permute-start | bytes 221192 | tf_op jit(solution)/shard_map/ppermute | solution.py:263
  43.5 3.7 %copy-start.1 = (bf16[384,2048]{1,0:T(8,128)(2,1)S(1)}, bf16[384,2048]{1,0:T(8,128)(2,1)}, u32[]{:S(2)}) copy-start(bf16[384,2048]{1,0:T(8,128)(2,1)} %x.1) | copy-start | bytes 4718596
  43.6 3.7 %copy-start.11 = (bf16[384,128]{1,0:T(8,128)(2,1)S(1)}, bf16[384,128]{1,0:T(8,128)(2,1)}, u32[]{:S(2)}) copy-start(bf16[384,128]{1,0:T(8,128)(2,1)} %b.3) | copy-start | bytes 294916
  43.6 3.7 %copy-start.13 = (bf16[384,128]{1,0:T(8,128)(2,1)S(1)}, bf16[384,128]{1,0:T(8,128)(2,1)}, u32[]{:S(2)}) copy-start(bf16[384,128]{1,0:T(8,128)(2,1)} %c.1) | copy-start | bytes 294916
  43.6 3.7 %copy-start.15 = (f32[32,384]{1,0:T(8,128)S(1)}, f32[32,384]{1,0:T(8,128)}, u32[]{:S(2)}) copy-start(f32[32,384]{1,0:T(8,128)} %ld.1) | copy-start | bytes 147460
  43.6 16.7 %all-to-all-start.1 = ((bf16[8,256,256]{2,1,0:T(8,128)(2,1)}), bf16[8,256,256]{2,1,0:T(8,128)(2,1)S(1)}, u32[]{:S(2)}, u32[]{:S(2)}) async-start(bf16[8,256,256]{2,1,0:T(8,128)(2,1)} %member_entries.1), calls=%async_computation.1 | async-start | bytes 2097152 | tf_op jit(solution)/shard_map/all_to_all | solution.py:254
  47.3 1.4 %copy-start.3 = (bf16[384,2048]{1,0:T(8,128)(2,1)S(1)}, bf16[384,2048]{1,0:T(8,128)(2,1)}, u32[]{:S(2)}) copy-start(bf16[384,2048]{1,0:T(8,128)(2,1)} %dy.1) | copy-start | bytes 4718596
  55.6 1.1 %copy-start.8 = (bf16[384,2048]{1,0:T(8,128)(2,1)}, bf16[384,2048]{1,0:T(8,128)(2,1)S(1)}, u32[]{:S(2)}) copy-start(bf16[384,2048]{1,0:T(8,128)(2,1)S(1)} %get-tuple-element.15.dx_local) | copy-start | bytes 4718596
  60.2 1.4 %copy-start.5 = (bf16[384,2048]{1,0:T(8,128)(2,1)S(1)}, bf16[384,2048]{1,0:T(8,128)(2,1)}, u32[]{:S(2)}) copy-start(bf16[384,2048]{1,0:T(8,128)(2,1)} %copy-done.4) | copy-start | bytes 4718596
  61.6 1.4 %copy-start.7 = (bf16[384,2048]{1,0:T(8,128)(2,1)S(1)}, bf16[384,2048]{1,0:T(8,128)(2,1)}, u32[]{:S(2)}) copy-start(bf16[384,2048]{1,0:T(8,128)(2,1)} %copy-done.6) | copy-start | bytes 4718596
  63.0 1.4 %copy-start.9 = (bf16[384,2048]{1,0:T(8,128)(2,1)S(1)}, bf16[384,2048]{1,0:T(8,128)(2,1)}, u32[]{:S(2)}) copy-start(bf16[384,2048]{1,0:T(8,128)(2,1)} %copy-done.8) | copy-start | bytes 4718596
  67.3 1.4 %collective-permute-start.1 = (bf16[768,128]{1,0:T(8,128)(2,1)S(1)}, bf16[768,128]{1,0:T(8,128)(2,1)S(1)}, u32[]{:S(2)}, u32[]{:S(2)}) collective-permute-start(bf16[768,128]{1,0:T(8,128)(2,1)S(1)} %get-tuple-element.20), channel_id=1, source_target_pairs={{0,1},{1,0},{2,3},{3,2},{4,5},{5,4},{6,7},{7,6},{8,9},{9,8},{10,11... | collective-permute-start | bytes 589832 | tf_op jit(solution)/shard_map/ppermute | solution.py:462

commit v3 on v2

v3 whole, which is shorter than its diff:
```python
import functools

import jax
import jax.numpy as jnp
from jax import lax
from jax.experimental import pallas as pl
from jax.experimental.pallas import tpu as pltpu
from jax.sharding import PartitionSpec as P

BF16 = jnp.bfloat16
F32 = jnp.float32
LANES = 128
TAIL = 16
LOG2E = 1.4426950408889634
MIB = 1024 * 1024

NN = (((1,), (0,)), ((), ()))
NT = (((1,), (1,)), ((), ()))
TN = (((0,), (0,)), ((), ()))


def dot(a, b, dims):
    return lax.dot_general(a, b, dims, preferred_element_type=F32)


def iota(shape, dim):
    return lax.broadcasted_iota(jnp.int32, shape, dim)


def three(values):
    high = values.astype(BF16)
    rest = values - high.astype(F32)
    mid = rest.astype(BF16)
    return high, mid, (rest - mid.astype(F32)).astype(BF16)


SLOT = LANES // 4


def summed(mask, terms):
    heads, length = terms[0].shape
    gap = [] if heads == SLOT else [jnp.zeros((SLOT - heads, length), BF16)]
    rows = [r for t in terms for r in [t] + gap] + [jnp.zeros((SLOT, length), BF16)]
    each = dot(mask, jnp.concatenate(rows, axis=0), NT)
    return each + pltpu.roll(each, LANES - SLOT, 1) + pltpu.roll(each, LANES - 2 * SLOT, 1)


def head_of_lane(head_dim, width, first):
    shape = (LANES, width)
    return jnp.where(iota(shape, 0) == first + iota(shape, 1) // head_dim, 1.0, 0.0).astype(BF16)


def whole(count):
    return [pl.BlockSpec(memory_space=pltpu.VMEM)] * count


def in_hbm(*arrays):
    return [pltpu.with_memory_space_constraint(a, pltpu.HBM) for a in arrays]


SMEM = pl.BlockSpec(memory_space=pltpu.SMEM)
HBM = pl.BlockSpec(memory_space=pltpu.HBM)


def params(mib):
    return pltpu.CompilerParams(vmem_limit_bytes=mib * MIB)


def cost(flops, size, transcendentals=0):
    return pl.CostEstimate(
        flops=flops, bytes_accessed=size, transcendentals=transcendentals
    )


def part_lanes(place, k, part):
    return pl.ds(pl.multiple_of((place[0] ^ k) * part, part), part)


LOADS = 4


def states_kernel(head_dim, group, place, ld_in, b_in, c_in, x_in, dy_in, *refs):
    x_scaled, dy_scaled, decay = refs[:3]
    sends, (ld, b, c, x, dy, sems) = refs[3 : 3 + group], refs[3 + group :]
    heads, length = ld.shape
    state, width = b.shape[1], x.shape[1]
    part = width // group

    def copy(n, source, target):
        one = pltpu.make_async_copy(source, target, sems.at[n])
        one.start()
        return one

    small = [copy(n, i, o) for n, (i, o) in enumerate([(ld_in, ld), (b_in, b), (c_in, c)])]
    span = width // LOADS
    pieces = [slice(n * span, (n + 1) * span) for n in range(LOADS)]
    loads = [
        [copy(3 + side * LOADS + n, i.at[:, p], o.at[:, p]) for n, p in enumerate(pieces)]
        for side, (i, o) in enumerate([(x_in, x), (dy_in, dy)])
    ]
    small[0].wait()
    terms = three(ld[...])
    rows, other = iota((length, length), 0), iota((length, length), 1)
    after = jnp.where(other > rows, 1.0, 0.0).astype(BF16)
    until = jnp.where(other <= rows, 1.0, 0.0).astype(BF16)
    into_end = jnp.exp(summed(after, terms)).astype(BF16)
    from_start = jnp.exp(summed(until, terms)).astype(BF16)
    decay[...] = into_end
    total = jnp.exp(summed(jnp.ones((TAIL, length), BF16), terms))
    high = total.astype(BF16).astype(F32)
    halves = jnp.where(iota(total.shape, 0) < TAIL // 2, high, total - high).astype(BF16)
    small[1].wait()
    small[2].wait()
    sides = [(into_end, b, x, x_scaled, 0), (from_start, c, dy, dy_scaled, state)]
    for side, (factors, proj, cols, scaled, first) in enumerate(sides):
        turned = proj[...].T
        for load in loads[side]:
            load.wait()
        for k in range(group):
            lanes = part_lanes(place, k, part)
            hot = head_of_lane(head_dim, part, (place[0] ^ k) * (heads // group))
            piece = cols[:, lanes] * dot(factors, hot, NN).astype(BF16)
            scaled[:, lanes] = piece
            sends[k][first : first + state, :] = dot(turned, piece, NN).astype(BF16)
            if side == 0:
                sends[k][2 * state :, :] = dot(halves, hot, NN).astype(BF16)


def local_states(head_dim, group, place, ld, b, c, x, dy):
    length, width = x.shape
    state = b.shape[1]
    inputs = (ld, b, c, x, dy)
    send = pltpu.VMEM((2 * state + TAIL, width // group), BF16)
    return pl.pallas_call(
        functools.partial(states_kernel, head_dim, group),
        out_shape=[
            pltpu.VMEM(x.shape, BF16),
            pltpu.VMEM(x.shape, BF16),
            pltpu.VMEM((length, LANES), BF16),
        ]
        + [send] * group,
        in_specs=[SMEM] + [HBM] * 5,
        out_specs=whole(3 + group),
        scratch_shapes=[pltpu.VMEM(a.shape, a.dtype) for a in inputs]
        + [pltpu.SemaphoreType.DMA((3 + 2 * LOADS,))],
        compiler_params=params(16),
        cost_estimate=cost(4 * length * width * (state + LANES), 8 * length * width),
        name="local_states",
    )(place, *in_hbm(*inputs))


def decay_of(tail):
    tail = tail.astype(F32)
    return tail[:1, :] + tail[TAIL // 2 : TAIL // 2 + 1, :]


def put_decay(ref, state, factor):
    high = factor.astype(BF16).astype(F32)
    shape = (TAIL, factor.shape[1])
    both = jnp.where(iota(shape, 0) < TAIL // 2, high, factor - high)
    ref[state:, :] = both.astype(BF16)


def in_order(group, forward):
    return list(range(group)) if forward else list(range(group - 1, -1, -1))


def each_row_tile(state, body):
    tile = 32

    @pl.loop(0, state // tile)
    def _(n):
        body(pl.multiple_of(n * tile, tile), tile)


def put_total(out, blocks, here, state, forward):
    order = in_order(len(blocks), forward)
    first = 0 if forward else state
    decays = [decay_of(blocks[q ^ here][2 * state :, :]) for q in range(len(blocks))]

    def body(row, tile):
        value = None
        for q in order:
            piece = blocks[q ^ here][pl.ds(first + row, tile), :].astype(F32)
            value = piece if value is None else decays[q] * value + piece
        out[pl.ds(row, tile), :] = value.astype(BF16)

    each_row_tile(state, body)
    factor = decays[0]
    for d in decays[1:]:
        factor = factor * d
    put_decay(out, state, factor)


def totals_kernel(state, count, place, upper, *refs):
    blocks, outs = refs[:-count], refs[-count:]
    for here in range(len(blocks)):
        for n, forward in enumerate((True, False)):
            if len(outs) == 2:
                chosen, out = place[0] == here, outs[n]
            else:
                chosen, out = (place[0] == here) & (upper[0] == n), outs[0]

            @pl.when(chosen)
            def _(here=here, forward=forward, out=out):
                put_total(out, blocks, here, state, forward)


def totals(state, count, place, upper, blocks):
    out = pltpu.VMEM((state + TAIL, blocks[0].shape[1]), BF16)
    return pl.pallas_call(
        functools.partial(totals_kernel, state, count),
        out_shape=[out] * count,
        in_specs=[SMEM] * 2 + whole(len(blocks)),
        out_specs=whole(count),
        compiler_params=params(4),
        cost_estimate=cost(16 * blocks[0].size, 16 * blocks[0].size),
        name="totals",
    )(place, upper, *blocks)


def before_group(state, received):
    value = received[0][:state, :].astype(F32)
    factor = decay_of(received[0][state:, :])
    for r in received[1:]:
        value = value + factor * r[:state, :].astype(F32)
        factor = factor * decay_of(r[state:, :])
    return value, factor


def onward_kernel(state, own, *refs):
    received, out = refs[:-1], refs[-1]
    value, factor = before_group(state, received)
    d = decay_of(own[state:, :])
    out[:state, :] = (own[:state, :].astype(F32) + d * value).astype(BF16)
    put_decay(out, state, d * factor)


def onward(state, own, received):
    return pl.pallas_call(
        functools.partial(onward_kernel, state),
        out_shape=jax.ShapeDtypeStruct(own.shape, BF16),
        in_specs=whole(1 + len(received)),
        out_specs=whole(1)[0],
        compiler_params=params(4),
        cost_estimate=cost(4 * own.size, 6 * own.size),
        name="onward",
    )(own, *received)


def members_kernel(state, n_received, place, upper, *refs):
    received, refs = refs[:n_received], refs[n_received:]
    group = (len(refs) - 1) // 2
    blocks, outs, entry = refs[:group], refs[group:-1], refs[-1]
    for n, forward in enumerate((True, False)):
        if n_received == 1:
            value = received[0][:state, :].astype(F32)
            value = value * jnp.where(upper[0] == 1 - n, 1.0, 0.0)
        else:
            half = n_received // 2
            value, _ = before_group(state, received[n * half : (n + 1) * half])
        entry[n * state : (n + 1) * state, :] = value
    for here in range(group):

        @pl.when(place[0] == here)
        def _(here=here):
            decays = [decay_of(blocks[q ^ here][2 * state :, :]) for q in range(group)]

            def body(row, tile):
                for forward in (True, False):
                    where = pl.ds(row if forward else state + row, tile)
                    value = entry[where, :]
                    order = in_order(group, forward)
                    for q in order:
                        outs[q ^ here][where, :] = value.astype(BF16)
                        if q != order[-1]:
                            value = decays[q] * value + blocks[q ^ here][where, :].astype(F32)

            each_row_tile(state, body)


def member_entries(state, place, upper, blocks, received):
    group, part = len(blocks), blocks[0].shape[1]
    return pl.pallas_call(
        functools.partial(members_kernel, state, len(received)),
        out_shape=[pltpu.VMEM((2 * state, part), BF16)] * group,
        in_specs=[SMEM] * 2 + whole(group + len(received)),
        out_specs=whole(group),
        scratch_shapes=[pltpu.VMEM((2 * state, part), F32)],
        compiler_params=params(4),
        cost_estimate=cost(24 * blocks[0].size, 32 * blocks[0].size),
        name="member_entries",
    )(place, upper, *received, *blocks)


def group_size(count, width):
    for group in (8, 4, 2):
        if count % group == 0 and (width // group) % LANES == 0:
            return group
    return 1


def entering(group, state, place, sends):
    count = lax.axis_size("seq")
    groups = count // group
    upper = (lax.axis_index("seq") // group).astype(jnp.int32)[None]

    def exchange(parts):
        out = list(parts)
        for k in sorted(range(1, group), key=lambda k: (-bin(k).count("1"), k)):
            out[k] = lax.ppermute(parts[k], "seq", [(s, s ^ k) for s in range(count)])
        return out

    blocks = exchange(sends)
    if groups == 2:
        (own,) = totals(state, 1, place, upper, blocks)
        pairs = [(s, (s + group) % count) for s in range(count)]
        received = [lax.ppermute(own, "seq", pairs)]
    else:
        received = []
        for own, sign in zip(totals(state, 2, place, upper, blocks), (1, -1)):
            arrived, sent, step = [], own, 1
            while step < groups:
                jump = sign * step * group
                pairs = [(s, s + jump) for s in range(count) if 0 <= s + jump < count]
                arrived.append(lax.ppermute(sent, "seq", pairs))
                step *= 2
                if step < groups:
                    sent = onward(state, own, arrived)
            received += arrived
    return exchange(member_entries(state, place, upper, blocks, received))


def split_pairs(first, count):
    if count == 1:
        return []
    middle = first + count // 2
    return (
        [(first, middle, first + count)]
        + split_pairs(first, middle - first)
        + split_pairs(middle, first + count - middle)
    )


def inner_kernel(head_dim, ld, b, c, x, dy, dx_out, db_out, dc_out, cum_terms, *scratch):
    heads, length = ld.shape
    width, state = x.shape[1], b.shape[1]
    piece = head_dim
    pieces = length // piece
    cuts = split_pairs(0, pieces)
    near, near_sum, dx = scratch[:3]
    far, far_sum = scratch[3 : 3 + len(cuts)], scratch[3 + len(cuts) :]
    per_tile = LANES // head_dim
    step = pl.program_id(0)

    @pl.when(step == 0)
    def _():
        rows, other = iota((length, length), 0), iota((length, length), 1)
        mask = jnp.where(other <= rows, 1.0, 0.0).astype(BF16)
        cum_small = summed(mask, three(ld[...] * LOG2E))
        lane = iota(cum_small.shape, 1)
        in_slots = jnp.where(lane < SLOT, cum_small, 0.0)
        in_slots = (
            in_slots + pltpu.roll(in_slots, SLOT, 1) + pltpu.roll(in_slots, 2 * SLOT, 1)
        )
        high, mid, low = three(in_slots)
        cum_terms[...] = jnp.where(lane < SLOT, high, jnp.where(lane < 2 * SLOT, mid, low))
        keep = iota((piece, LANES), 0) <= lax.rem(iota((piece, LANES), 1), piece)
        for n in range(pieces):
            rows_n = slice(n * piece, (n + 1) * piece)
            doubled = jnp.concatenate([c[rows_n, :]] * per_tile, axis=0)
            near[rows_n, :] = jnp.where(keep, dot(b[rows_n, :], doubled, NT), 0.0)
        near_sum[...] = jnp.zeros_like(near_sum)
        for (lo, mid_, hi), f, total in zip(cuts, far, far_sum):
            left, right = slice(lo * piece, mid_ * piece), slice(mid_ * piece, hi * piece)
            f[...] = dot(b[left, :], c[right, :], NT).astype(BF16)
            total[...] = jnp.zeros_like(total)

    shape = (LANES, width)
    owner = step * (width // head_dim) + iota(shape, 1) // head_dim
    slot = lax.rem(iota(shape, 0), SLOT) == owner
    hot = jnp.where(slot & (iota(shape, 0) < 3 * SLOT), 1.0, 0.0).astype(BF16)
    cum = dot(cum_terms[...], hot, NN)
    tile = (piece, LANES)
    diagonal = iota(tile, 0) == lax.rem(iota(tile, 1), piece)
    part_of_lane = iota(tile, 1) // head_dim
    for n in range(pieces):
        rows_n = slice(n * piece, (n + 1) * piece)
        total = near_sum[rows_n, :]
        scores = near[rows_n, :]
        for t in range(width // LANES):
            lanes = slice(t * LANES, (t + 1) * LANES)
            col = cum[rows_n, lanes]
            row = jnp.sum(jnp.where(diagonal, col, 0.0), axis=0, keepdims=True)
            decays = jnp.exp2(jnp.minimum(row - col, 0.0))
            dy_t = dy[rows_n, lanes]
            stacked = jnp.concatenate(
                [jnp.where(part_of_lane == h, dy_t, jnp.zeros_like(dy_t)) for h in range(per_tile)],
                axis=0,
            )
            dx[rows_n, lanes] = dot((scores * decays).astype(BF16), stacked, NN)
            total = total + decays * dot(x[rows_n, lanes], stacked, NT)
        near_sum[rows_n, :] = total
    for (lo, mid_, hi), f, total in zip(cuts, far, far_sum):
        left, right = slice(lo * piece, mid_ * piece), slice(mid_ * piece, hi * piece)
        edge = cum[mid_ * piece - 1 : mid_ * piece, :]
        to_edge = jnp.exp2(edge - cum[left, :])
        from_edge = jnp.exp2(cum[right, :] - edge)
        x_edge = (x[left, :].astype(F32) * to_edge).astype(BF16)
        dy_edge = (dy[right, :].astype(F32) * from_edge).astype(BF16)
        dx[left, :] += to_edge * dot(f[...], dy_edge, NN)
        total[...] += dot(x_edge, dy_edge, NT)
    lanes = pl.ds(pl.multiple_of(step * width, width), width)
    dx_out[:, lanes] = dx[...].astype(BF16)

    @pl.when(step == pl.num_programs(0) - 1)
    def _():
        keep = (iota(tile, 0) <= iota(tile, 1)) & (part_of_lane == 0)
        for n in range(pieces):
            rows_n = slice(n * piece, (n + 1) * piece)
            total = near_sum[rows_n, :]
            total = sum(
                [pltpu.roll(total, h * head_dim, 1) for h in range(1, per_tile)], total
            )
            weighted = jnp.where(keep, total, 0.0).astype(BF16)
            doubled = jnp.concatenate([c[rows_n, :]] * per_tile, axis=0)
            db_out[rows_n, :] = dot(weighted, doubled, NN)
            dc_out[rows_n, :] = dot(weighted, b[rows_n, :], TN)[:piece, :]
        for (lo, mid_, hi), total in zip(cuts, far_sum):
            left, right = slice(lo * piece, mid_ * piece), slice(mid_ * piece, hi * piece)
            weighted = total[...].astype(BF16)
            db_out[left, :] += dot(weighted, c[right, :], NN)
            dc_out[right, :] += dot(weighted, b[left, :], TN)


def inner_terms(head_dim, ld, b, c, x, dy):
    heads, length = ld.shape
    state, width = b.shape[1], x.shape[1]
    chunk = width // 4
    piece = head_dim
    cuts = split_pairs(0, length // piece)
    sizes = [((mid - lo) * piece, (hi - mid) * piece) for lo, mid, hi in cuts]
    column = pl.BlockSpec((length, chunk), lambda i: (0, i))

    def fixed(shape):
        return pl.BlockSpec(shape, lambda i: (0, 0))

    return pl.pallas_call(
        functools.partial(inner_kernel, head_dim),
        grid=(width // chunk,),
        out_shape=[
            pltpu.VMEM((length, width), BF16),
            pltpu.VMEM((length, state), F32),
            pltpu.VMEM((length, state), F32),
        ],
        in_specs=[fixed(ld.shape), fixed(b.shape), fixed(c.shape), column, column],
        out_specs=whole(3),
        scratch_shapes=[
            pltpu.VMEM((length, LANES), BF16),
            pltpu.VMEM((length, LANES), F32),
            pltpu.VMEM((length, LANES), F32),
            pltpu.VMEM((length, chunk), F32),
        ]
        + [pltpu.VMEM(s, BF16) for s in sizes]
        + [pltpu.VMEM(s, F32) for s in sizes],
        compiler_params=params(24),
        cost_estimate=cost(16 * length * width * state, 6 * length * width, 3 * length * width),
        name="inner_terms",
    )(*in_hbm(ld, b, c, x, dy))


def parts_kernel(place, x_scaled, dy_scaled, db_local, dc_local, *refs):
    entries, out = refs[:-1], refs[-1]
    length, state = db_local.shape
    part = entries[0].shape[1]
    db, dc = db_local[...], dc_local[...]
    for k, entry in enumerate(entries):
        lanes = part_lanes(place, k, part)
        db = db + dot(x_scaled[:, lanes], entry[state:, :], NT)
        dc = dc + dot(dy_scaled[:, lanes], entry[:state, :], NT)
    out[:length, :] = db.astype(BF16)
    out[length:, :] = dc.astype(BF16)


def entry_parts(place, x_scaled, dy_scaled, db_local, dc_local, entries):
    length, state = db_local.shape
    return pl.pallas_call(
        parts_kernel,
        out_shape=pltpu.VMEM((2 * length, state), BF16),
        in_specs=[SMEM] + whole(4 + len(entries)),
        out_specs=whole(1)[0],
        compiler_params=params(8),
        cost_estimate=cost(4 * x_scaled.size * state, 4 * x_scaled.size),
        name="entry_parts",
    )(place, x_scaled, dy_scaled, db_local, dc_local, *entries)


def values_kernel(head_dim, place, decay, b_in, dx_local, *refs):
    entries, (out, b, dx, sems) = refs[:-4], refs[-4:]
    state, part = b.shape[1], entries[0].shape[1]
    load = pltpu.make_async_copy(b_in, b, sems.at[len(entries)])
    load.start()
    load.wait()
    stores = []
    for k, entry in enumerate(entries):
        lanes = part_lanes(place, k, part)
        hot = head_of_lane(head_dim, part, (place[0] ^ k) * (part // head_dim))
        far = dot(decay[...], hot, NN) * dot(b[...], entry[state:, :], NN)
        dx[k] = (dx_local[:, lanes].astype(F32) + far).astype(BF16)
        store = pltpu.make_async_copy(dx.at[k], out.at[:, lanes], sems.at[k])
        store.start()
        stores.append(store)
    for store in stores:
        store.wait()


def entry_values(head_dim, place, decay, b, dx_local, entries):
    group, part = len(entries), entries[0].shape[1]
    length, state = b.shape
    return pl.pallas_call(
        functools.partial(values_kernel, head_dim),
        out_shape=pltpu.HBM(dx_local.shape, BF16),
        in_specs=[SMEM] + whole(1) + [HBM] + whole(1 + group),
        out_specs=HBM,
        scratch_shapes=[
            pltpu.VMEM(b.shape, BF16),
            pltpu.VMEM((group, length, part), BF16),
            pltpu.SemaphoreType.DMA((group + 1,)),
        ],
        compiler_params=params(8),
        cost_estimate=cost(4 * dx_local.size * state, 4 * dx_local.size),
        name="entry_values",
    )(place, decay, *in_hbm(b), dx_local, *entries)


def over_heads(part):
    count = lax.axis_size("head")
    total = part.astype(F32)
    for shift in range(1, count):
        pairs = [(s, (s + shift) % count) for s in range(count)]
        total = total + lax.ppermute(part, "head", pairs).astype(F32)
    return total.astype(BF16)


def shards(token_values, b_inputs, c_inputs, log_decay, grad_out):
    head_dim = token_values.shape[1] // log_decay.shape[0]
    length, state = b_inputs.shape
    group = group_size(lax.axis_size("seq"), token_values.shape[1])
    place = lax.rem(lax.axis_index("seq"), group).astype(jnp.int32)[None]
    inputs = (log_decay, b_inputs, c_inputs, token_values, grad_out)
    x_scaled, dy_scaled, decay, *sends = local_states(head_dim, group, place, *inputs)
    entries = entering(group, state, place, sends)
    dx_local, db_local, dc_local = inner_terms(head_dim, *inputs)
    parts = entry_parts(place, x_scaled, dy_scaled, db_local, dc_local, entries)
    grad_values = entry_values(head_dim, place, decay, b_inputs, dx_local, entries)
    both = over_heads(parts)
    return grad_values, both[:length], both[length:]


def solution(mesh):
    in_specs = (
        P("seq", "head"),
        P("seq", None),
        P("seq", None),
        P("head", "seq"),
        P("seq", "head"),
    )
    out_specs = (P("seq", "head"), P("seq", None), P("seq", None))
    return jax.shard_map(shards, mesh=mesh, in_specs=in_specs, out_specs=out_specs, check_vma=False)
```

time: 70 us -> 60.7 us (0.87)
  the two profiles are of different devices: /device:TPU:0 before, /device:TPU:29 now
where the time goes in v3:
time: 60.7 us; the launch traced here: 60.5 us
  starting transfers between devices  23.8 us (39%)
  Pallas kernels  20.7 us (34%)
  waiting for transfers between devices  12.9 us (21%)
  local copies, waits for them, and re-layouts  2.25 us (4%)
  between operations  0.75 us (1%)
    ppermute x14, starting transfers between devices, exchange(): out[k] = lax.ppermute(parts[k], 'seq', [(s, s ^ k) for s in range(count)])  15 us
    ppermute x1, starting transfers between devices, over_heads(): total = total + lax.ppermute(part, 'head', pairs).astype(F32)  8.69 us
    ppermute x14, waiting for transfers between devices, exchange(): out[k] = lax.ppermute(parts[k], 'seq', [(s, s ^ k) for s in range(count)])  8.14 us
    pallas_call x1, Pallas kernels, inner_terms(): pl.pallas_call(functools.partial(inner_kernel, head_dim), grid=(width //...  7.65 us
    pallas_call x1, Pallas kernels, local_states(): pl.pallas_call(functools.partial(states_kernel, head_dim, group), out_sha...  6.58 us
    ppermute x1, waiting for transfers between devices, entering(): received = [lax.ppermute(own, 'seq', pairs)]  4.8 us
    pallas_call x1, Pallas kernels, entry_values(): pl.pallas_call(functools.partial(values_kernel, head_dim), out_shape=pltp...  2.63 us
    unnamed x4, local copies, waits for them, and re-layouts  1.56 us
  transfers between devices with their start and end apart: 16, of which 5 were waited for; matrix products, arithmetic and copies ran while one was open for 0% of the time, Pallas kernels for 17%

profile of v3, /device:TPU:29, one launch (start us, length us, event | category | flops | bytes accessed | tf_op | source)
XLA Modules:
  0.0 60.5 jit_solution(439206308283302930)
XLA Ops:
  0.6 6.6 %local_states.1 = (bf16[384,2048]{1,0:T(8,128)(2,1)S(1)}, bf16[384,2048]{1,0:T(8,128)(2,1)S(1)}, bf16[384,128]{1,0:T(8,128)(2,1)S(1)}, bf16[272,256]{1,0:T(8,128...) custom-call(s32[1]{0:T(128)} %bitcast.place, ...), custom_call_target="tpu_custom_call" | custom-call | flops 805306368 | bytes 6291456 | tf_op jit(solution)/shard_map/local_states/pallas_call | solution.py:134
  7.2 1.3 %collective-permute-start = (bf16[272,256]{1,0:T(8,128)(2,1)S(1)}, bf16[272,256]{1,0:T(8,128)(2,1)S(1)}, u32[]{:S(2)}, u32[]{:S(2)}) collective-permute-start(bf16[272,256]{1,0:T(8,128)(2,1)S(1)} %get-tuple-element.28), channel_id=1, source_target_pairs={{0,2},{2,0},{4,6},{6,4},{8,10},{10,8},{12,14},{14,12},{16,18},{18,... | collective-permute-start | bytes 417800 | tf_op jit(solution)/shard_map/ppermute | solution.py:311
  8.5 0.2 collective-permute-start.1
  8.7 1.2 %collective-permute-start.2 = (bf16[272,256]{1,0:T(8,128)(2,1)}, bf16[272,256]{1,0:T(8,128)(2,1)}, u32[]{:S(2)}, u32[]{:S(2)}) collective-permute-start(bf16[272,256]{1,0:T(8,128)(2,1)} %get-tuple-element.30), channel_id=1, source_target_pairs={{0,6},{2,4},{4,2},{6,0},{8,14},{10,12},{12,10},{14,8},{16,22},{18,... | collective-permute-start | bytes 417800 | tf_op jit(solution)/shard_map/ppermute | solution.py:311
  9.9 0.2 collective-permute-start.3
  10.1 2.2 %collective-permute-start.4 = (bf16[272,256]{1,0:T(8,128)(2,1)}, bf16[272,256]{1,0:T(8,128)(2,1)}, u32[]{:S(2)}, u32[]{:S(2)}) collective-permute-start(bf16[272,256]{1,0:T(8,128)(2,1)} %get-tuple-element.32), channel_id=1, source_target_pairs={{0,10},{2,8},{4,14},{6,12},{8,2},{10,0},{12,6},{14,4},{16,26},{18,... | collective-permute-start | bytes 417800 | tf_op jit(solution)/shard_map/ppermute | solution.py:311
  12.3 0.0 collective-permute-done.refs_1_.refs_2_
  12.3 0.1 collective-permute-start.5
  12.4 0.4 collective-permute-done.1.refs_2_.refs_3_
  12.8 0.0 copy-start
  12.8 0.7 %copy-done = bf16[272,256]{1,0:T(8,128)(2,1)} copy-done((bf16[272,256]{1,0:T(8,128)(2,1)}, bf16[272,256]{1,0:T(8,128)(2,1)S(1)}, u32[]{:S(2)}) %copy-start) | copy-done | bytes 139288
  13.5 2.3 %collective-permute-start.6 = (bf16[272,256]{1,0:T(8,128)(2,1)}, bf16[272,256]{1,0:T(8,128)(2,1)}, u32[]{:S(2)}, u32[]{:S(2)}) collective-permute-start(bf16[272,256]{1,0:T(8,128)(2,1)} %get-tuple-element.34), channel_id=1, source_target_pairs={{0,14},{2,12},{4,10},{6,8},{8,6},{10,4},{12,2},{14,0},{16,30},{18,... | collective-permute-start | bytes 417800 | tf_op jit(solution)/shard_map/ppermute | solution.py:311
  15.8 0.0 collective-permute-done.2.refs_3_.refs_4_
  15.8 0.0 collective-permute-done.3.refs_4_.refs_5_
  15.8 1.7 %collective-permute-done.4.refs_5_.refs_6_ = bf16[272,256]{1,0:T(8,128)(2,1)} collective-permute-done((bf16[272,256]{1,0:T(8,128)(2,1)}, bf16[272,256]{1,0:T(8,128)(2,1)}, u32[]{:S(2)}, u32[]{:S(2)}) %collective-permute-start.4) | collective-permute-done | bytes 139296 | tf_op jit(solution)/shard_map/ppermute | solution.py:311
  17.5 2.3 %collective-permute-done.5.refs_6_.refs_7_ = bf16[272,256]{1,0:T(8,128)(2,1)} collective-permute-done((bf16[272,256]{1,0:T(8,128)(2,1)}, bf16[272,256]{1,0:T(8,128)(2,1)}, u32[]{:S(2)}, u32[]{:S(2)}) %collective-permute-start.5) | collective-permute-done | bytes 139296 | tf_op jit(solution)/shard_map/ppermute | solution.py:311
  19.8 3.7 %collective-permute-done.6.refs_7_.refs_8_ = bf16[272,256]{1,0:T(8,128)(2,1)} collective-permute-done((bf16[272,256]{1,0:T(8,128)(2,1)}, bf16[272,256]{1,0:T(8,128)(2,1)}, u32[]{:S(2)}, u32[]{:S(2)}) %collective-permute-start.6) | collective-permute-done | bytes 139296 | tf_op jit(solution)/shard_map/ppermute | solution.py:311
  23.5 0.0 copy-start.1
  23.5 0.9 %copy-done.1 = bf16[272,256]{1,0:T(8,128)(2,1)S(1)} copy-done((bf16[272,256]{1,0:T(8,128)(2,1)S(1)}, bf16[272,256]{1,0:T(8,128)(2,1)}, u32[]{:S(2)}) %copy-start.1) | copy-done | bytes 139288
  24.4 1.4 %totals.1 = bf16[144,256]{1,0:T(8,128)(2,1)S(1)} custom-call(s32[1]{0:T(128)} %bitcast.place, s32[1]{0:T(128)} %bitcast.1.upper, bf16[272,256]{1,0:T(8,128)(2,1)S(1)} %get-tuple-element.27.refs_0_.refs_1_, bf16[272,256]{1,0:T(8,128)(2,1)S(1)} %collective-permute-done.refs_1_.refs_2_, bf16[272,256]{1,0:T(8,128)(2,1)S(1)} %copy-done.1, ...), custom_call_target="tpu_custom_call" | custom-call | flops 1114112 | bytes 1114112 | tf_op jit(solution)/shard_map/totals/pallas_call | solution.py:211
  25.8 0.1 collective-permute-start.7
  25.9 4.8 %collective-permute-done.7.refs_0_ = bf16[144,256]{1,0:T(8,128)(2,1)S(1)} collective-permute-done((bf16[144,256]{1,0:T(8,128)(2,1)S(1)}, bf16[144,256]{1,0:T(8,128)(2,1)S(1)}, u32[]{:S(2)}, u32[]{:S(2)}) %collective-permute-start.7) | collective-permute-done | bytes 73760 | tf_op jit(solution)/shard_map/ppermute | solution.py:318
  30.7 1.5 %member_entries.1 = (bf16[256,256]{1,0:T(8,128)(2,1)S(1)}, bf16[256,256]{1,0:T(8,128)(2,1)S(1)}, bf16[256,256]{1,0:T(8,128)(2,1)S(1)}, bf16[256,256]{1,0:T(8,128...) custom-call(s32[1]{0:T(128)} %bitcast.place, ...), custom_call_target="tpu_custom_call" | custom-call | flops 1671168 | bytes 2228224 | tf_op jit(solution)/shard_map/member_entries/pallas_call | solution.py:284
  32.2 0.4 collective-permute-start.10
  32.7 1.8 %collective-permute-start.11 = (bf16[256,256]{1,0:T(8,128)(2,1)S(1)}, bf16[256,256]{1,0:T(8,128)(2,1)S(1)}, u32[]{:S(2)}, u32[]{:S(2)}) collective-permute-start(bf16[256,256]{1,0:T(8,128)(2,1)S(1)} %get-tuple-element.39), channel_id=1, source_target_pairs={{0,8},{2,10},{4,12},{6,14},{8,0},{10,2},{12,4},{14,6},{16,24},{18,... | collective-permute-start | bytes 393224 | tf_op jit(solution)/shard_map/ppermute | solution.py:311
  34.5 1.4 %collective-permute-start.12 = (bf16[256,256]{1,0:T(8,128)(2,1)S(1)}, bf16[256,256]{1,0:T(8,128)(2,1)S(1)}, u32[]{:S(2)}, u32[]{:S(2)}) collective-permute-start(bf16[256,256]{1,0:T(8,128)(2,1)S(1)} %get-tuple-element.40), channel_id=1, source_target_pairs={{0,10},{2,8},{4,14},{6,12},{8,2},{10,0},{12,6},{14,4},{16,26},{18,... | collective-permute-start | bytes 393224 | tf_op jit(solution)/shard_map/ppermute | solution.py:311
  35.9 0.0 collective-permute-start.13
  35.9 1.8 %collective-permute-start.14 = (bf16[256,256]{1,0:T(8,128)(2,1)S(1)}, bf16[256,256]{1,0:T(8,128)(2,1)S(1)}, u32[]{:S(2)}, u32[]{:S(2)}) collective-permute-start(bf16[256,256]{1,0:T(8,128)(2,1)S(1)} %get-tuple-element.42), channel_id=1, source_target_pairs={{0,14},{2,12},{4,10},{6,8},{8,6},{10,4},{12,2},{14,0},{16,30},{18,... | collective-permute-start | bytes 393224 | tf_op jit(solution)/shard_map/ppermute | solution.py:311
  37.8 0.0 collective-permute-done.10.refs_3_
  37.8 1.7 %collective-permute-start.8 = (bf16[256,256]{1,0:T(8,128)(2,1)S(1)}, bf16[256,256]{1,0:T(8,128)(2,1)S(1)}, u32[]{:S(2)}, u32[]{:S(2)}) collective-permute-start(bf16[256,256]{1,0:T(8,128)(2,1)S(1)} %get-tuple-element.36), channel_id=1, source_target_pairs={{0,2},{2,0},{4,6},{6,4},{8,10},{10,8},{12,14},{14,12},{16,18},{18,... | collective-permute-start | bytes 393224 | tf_op jit(solution)/shard_map/ppermute | solution.py:311
  39.5 0.0 collective-permute-done.11.refs_4_
  39.5 0.2 collective-permute-start.9
  39.7 7.6 %inner_terms.1 = (bf16[384,2048]{1,0:T(8,128)(2,1)S(1)}, f32[384,128]{1,0:T(8,128)S(1)}, f32[384,128]{1,0:T(8,128)S(1)}) custom-call(f32[32,384]{1,0:T(8,128)} %ld.1, bf16[384,128]{1,0:T(8,128)(2,1)} %b_in.3, bf16[384,128]{1,0:T(8,128)(2,1)} %c.1, bf16[384,2048]{1,0:T(8,128)(2,1)} %x.1, bf16[384,2048]{1,0:T(8,128)(2,1)} %dy.1), custom_call_target="tpu_custom_call" | custom-call | flops 1610612736 | bytes 4718592 | tf_op jit(solution)/shard_map/inner_terms/pallas_call | solution.py:448
  47.3 0.0 collective-permute-done.12.refs_5_
  47.3 0.0 collective-permute-done.13.refs_6_
  47.4 0.0 collective-permute-done.14.refs_7_
  47.4 0.0 collective-permute-done.8.refs_1_
  47.4 0.0 collective-permute-done.9.refs_2_
  47.4 1.0 %entry_parts.1 = bf16[768,128]{1,0:T(8,128)(2,1)S(1)} custom-call(s32[1]{0:T(128)} %bitcast.place, bf16[384,2048]{1,0:T(8,128)(2,1)S(1)} %get-tuple-element.43.x_scaled, bf16[384,2048]{1,0:T(8,128)(2,1)S(1)} %get-tuple-element.44.dy_scaled, f32[384,128]{1,0:T(8,128)S(1)} %get-tuple-element.45.db_local, f32[384,128]{1,0:T(8,128)S(1)} %get-tuple-element.46.dc_local, ...), custom_call_target="tpu_custom_call" | custom-call | flops 402653184 | bytes 3145728 | tf_op jit(solution)/shard_map/entry_parts/pallas_call | solution.py:487
  48.4 8.7 %collective-permute-start.15 = (bf16[768,128]{1,0:T(8,128)(2,1)S(1)}, bf16[768,128]{1,0:T(8,128)(2,1)S(1)}, u32[]{:S(2)}, u32[]{:S(2)}) collective-permute-start(bf16[768,128]{1,0:T(8,128)(2,1)S(1)} %entry_parts.1), channel_id=1, source_target_pairs={{0,1},{1,0},{2,3},{3,2},{4,5},{5,4},{6,7},{7,6},{8,9},{9,8},{10,11... | collective-permute-start | bytes 589832 | tf_op jit(solution)/shard_map/ppermute | solution.py:541
  57.1 2.6 %entry_values.1 = bf16[384,2048]{1,0:T(8,128)(2,1)} custom-call(s32[1]{0:T(128)} %bitcast.place, bf16[384,128]{1,0:T(8,128)(2,1)S(1)} %get-tuple-element.25.decay, bf16[384,128]{1,0:T(8,128)(2,1)} %b_in.3, bf16[384,2048]{1,0:T(8,128)(2,1)S(1)} %get-tuple-element.26.dx_local, bf16[256,256]{1,0:T(8,128)(2,1)S(1)} %get-tuple-element.35.refs_0_, ...), custom_call_target="tpu_custom_call" | custom-call | flops 402653184 | bytes 3145728 | tf_op jit(solution)/shard_map/entry_values/pallas_call | solution.py:520
  59.7 0.0 collective-permute-done.15
  59.7 0.1 add_convert_fusion
  59.8 0.7 %fusion = (bf16[384,128]{1,0:T(8,128)(2,1)}, bf16[384,128]{1,0:T(8,128)(2,1)}) fusion(bf16[768,128]{1,0:T(8,128)(2,1)S(1)} %add_convert_fusion), kind=kLoop, calls=%fused_computation.1 | loop fusion | bytes 393216 | tf_op jit(solution)/shard_map/slice | solution.py:557
Async XLA Ops:
  7.2 5.1 %collective-permute-start = (bf16[272,256]{1,0:T(8,128)(2,1)S(1)}, bf16[272,256]{1,0:T(8,128)(2,1)S(1)}, u32[]{:S(2)}, u32[]{:S(2)}) collective-permute-start(bf16[272,256]{1,0:T(8,128)(2,1)S(1)} %get-tuple-element.28), channel_id=1, source_target_pairs={{0,2},{2,0},{4,6},{6,4},{8,10},{10,8},{12,14},{14,12},{16,18},{18,... | collective-permute-start | bytes 417800 | tf_op jit(solution)/shard_map/ppermute | solution.py:311
  8.5 4.3 %collective-permute-start.1 = (bf16[272,256]{1,0:T(8,128)(2,1)S(1)}, bf16[272,256]{1,0:T(8,128)(2,1)S(1)}, u32[]{:S(2)}, u32[]{:S(2)}) collective-permute-start(bf16[272,256]{1,0:T(8,128)(2,1)S(1)} %get-tuple-element.29), channel_id=1, source_target_pairs={{0,4},{2,6},{4,0},{6,2},{8,12},{10,14},{12,8},{14,10},{16,20},{18,... | collective-permute-start | bytes 417800 | tf_op jit(solution)/shard_map/ppermute | solution.py:311
  8.7 7.1 %collective-permute-start.2 = (bf16[272,256]{1,0:T(8,128)(2,1)}, bf16[272,256]{1,0:T(8,128)(2,1)}, u32[]{:S(2)}, u32[]{:S(2)}) collective-permute-start(bf16[272,256]{1,0:T(8,128)(2,1)} %get-tuple-element.30), channel_id=1, source_target_pairs={{0,6},{2,4},{4,2},{6,0},{8,14},{10,12},{12,10},{14,8},{16,22},{18,... | collective-permute-start | bytes 417800 | tf_op jit(solution)/shard_map/ppermute | solution.py:311
  9.9 5.8 %collective-permute-start.3 = (bf16[272,256]{1,0:T(8,128)(2,1)}, bf16[272,256]{1,0:T(8,128)(2,1)}, u32[]{:S(2)}, u32[]{:S(2)}) collective-permute-start(bf16[272,256]{1,0:T(8,128)(2,1)} %get-tuple-element.31), channel_id=1, source_target_pairs={{0,8},{2,10},{4,12},{6,14},{8,0},{10,2},{12,4},{14,6},{16,24},{18,... | collective-permute-start | bytes 417800 | tf_op jit(solution)/shard_map/ppermute | solution.py:311
  10.1 7.4 %collective-permute-start.4 = (bf16[272,256]{1,0:T(8,128)(2,1)}, bf16[272,256]{1,0:T(8,128)(2,1)}, u32[]{:S(2)}, u32[]{:S(2)}) collective-permute-start(bf16[272,256]{1,0:T(8,128)(2,1)} %get-tuple-element.32), channel_id=1, source_target_pairs={{0,10},{2,8},{4,14},{6,12},{8,2},{10,0},{12,6},{14,4},{16,26},{18,... | collective-permute-start | bytes 417800 | tf_op jit(solution)/shard_map/ppermute | solution.py:311
  12.3 7.5 %collective-permute-start.5 = (bf16[272,256]{1,0:T(8,128)(2,1)}, bf16[272,256]{1,0:T(8,128)(2,1)}, u32[]{:S(2)}, u32[]{:S(2)}) collective-permute-start(bf16[272,256]{1,0:T(8,128)(2,1)} %get-tuple-element.33), channel_id=1, source_target_pairs={{0,12},{2,14},{4,8},{6,10},{8,4},{10,6},{12,0},{14,2},{16,28},{18,... | collective-permute-start | bytes 417800 | tf_op jit(solution)/shard_map/ppermute | solution.py:311
  12.8 0.7 %copy-start = (bf16[272,256]{1,0:T(8,128)(2,1)}, bf16[272,256]{1,0:T(8,128)(2,1)S(1)}, u32[]{:S(2)}) copy-start(bf16[272,256]{1,0:T(8,128)(2,1)S(1)} %collective-permute-done.1.refs_2_.refs_3_) | copy-start | bytes 417796
  13.5 10.0 %collective-permute-start.6 = (bf16[272,256]{1,0:T(8,128)(2,1)}, bf16[272,256]{1,0:T(8,128)(2,1)}, u32[]{:S(2)}, u32[]{:S(2)}) collective-permute-start(bf16[272,256]{1,0:T(8,128)(2,1)} %get-tuple-element.34), channel_id=1, source_target_pairs={{0,14},{2,12},{4,10},{6,8},{8,6},{10,4},{12,2},{14,0},{16,30},{18,... | collective-permute-start | bytes 417800 | tf_op jit(solution)/shard_map/ppermute | solution.py:311
  23.5 0.9 %copy-start.1 = (bf16[272,256]{1,0:T(8,128)(2,1)S(1)}, bf16[272,256]{1,0:T(8,128)(2,1)}, u32[]{:S(2)}) copy-start(bf16[272,256]{1,0:T(8,128)(2,1)} %copy-done) | copy-start | bytes 417796
  25.8 4.9 %collective-permute-start.7 = (bf16[144,256]{1,0:T(8,128)(2,1)S(1)}, bf16[144,256]{1,0:T(8,128)(2,1)S(1)}, u32[]{:S(2)}, u32[]{:S(2)}) collective-permute-start(bf16[144,256]{1,0:T(8,128)(2,1)S(1)} %totals.1), channel_id=1, source_target_pairs={{0,16},{2,18},{4,20},{6,22},{8,24},{10,26},{12,28},{14,30},{16,0},... | collective-permute-start | bytes 221192 | tf_op jit(solution)/shard_map/ppermute | solution.py:318
  32.2 5.5 %collective-permute-start.10 = (bf16[256,256]{1,0:T(8,128)(2,1)S(1)}, bf16[256,256]{1,0:T(8,128)(2,1)S(1)}, u32[]{:S(2)}, u32[]{:S(2)}) collective-permute-start(bf16[256,256]{1,0:T(8,128)(2,1)S(1)} %get-tuple-element.38), channel_id=1, source_target_pairs={{0,6},{2,4},{4,2},{6,0},{8,14},{10,12},{12,10},{14,8},{16,22},{18,... | collective-permute-start | bytes 393224 | tf_op jit(solution)/shard_map/ppermute | solution.py:311
  32.7 6.8 %collective-permute-start.11 = (bf16[256,256]{1,0:T(8,128)(2,1)S(1)}, bf16[256,256]{1,0:T(8,128)(2,1)S(1)}, u32[]{:S(2)}, u32[]{:S(2)}) collective-permute-start(bf16[256,256]{1,0:T(8,128)(2,1)S(1)} %get-tuple-element.39), channel_id=1, source_target_pairs={{0,8},{2,10},{4,12},{6,14},{8,0},{10,2},{12,4},{14,6},{16,24},{18,... | collective-permute-start | bytes 393224 | tf_op jit(solution)/shard_map/ppermute | solution.py:311
  34.5 12.9 %collective-permute-start.12 = (bf16[256,256]{1,0:T(8,128)(2,1)S(1)}, bf16[256,256]{1,0:T(8,128)(2,1)S(1)}, u32[]{:S(2)}, u32[]{:S(2)}) collective-permute-start(bf16[256,256]{1,0:T(8,128)(2,1)S(1)} %get-tuple-element.40), channel_id=1, source_target_pairs={{0,10},{2,8},{4,14},{6,12},{8,2},{10,0},{12,6},{14,4},{16,26},{18,... | collective-permute-start | bytes 393224 | tf_op jit(solution)/shard_map/ppermute | solution.py:311
  35.9 11.4 %collective-permute-start.13 = (bf16[256,256]{1,0:T(8,128)(2,1)S(1)}, bf16[256,256]{1,0:T(8,128)(2,1)S(1)}, u32[]{:S(2)}, u32[]{:S(2)}) collective-permute-start(bf16[256,256]{1,0:T(8,128)(2,1)S(1)} %get-tuple-element.41), channel_id=1, source_target_pairs={{0,12},{2,14},{4,8},{6,10},{8,4},{10,6},{12,0},{14,2},{16,28},{18,... | collective-permute-start | bytes 393224 | tf_op jit(solution)/shard_map/ppermute | solution.py:311
  35.9 11.4 %collective-permute-start.14 = (bf16[256,256]{1,0:T(8,128)(2,1)S(1)}, bf16[256,256]{1,0:T(8,128)(2,1)S(1)}, u32[]{:S(2)}, u32[]{:S(2)}) collective-permute-start(bf16[256,256]{1,0:T(8,128)(2,1)S(1)} %get-tuple-element.42), channel_id=1, source_target_pairs={{0,14},{2,12},{4,10},{6,8},{8,6},{10,4},{12,2},{14,0},{16,30},{18,... | collective-permute-start | bytes 393224 | tf_op jit(solution)/shard_map/ppermute | solution.py:311
  37.8 9.6 %collective-permute-start.8 = (bf16[256,256]{1,0:T(8,128)(2,1)S(1)}, bf16[256,256]{1,0:T(8,128)(2,1)S(1)}, u32[]{:S(2)}, u32[]{:S(2)}) collective-permute-start(bf16[256,256]{1,0:T(8,128)(2,1)S(1)} %get-tuple-element.36), channel_id=1, source_target_pairs={{0,2},{2,0},{4,6},{6,4},{8,10},{10,8},{12,14},{14,12},{16,18},{18,... | collective-permute-start | bytes 393224 | tf_op jit(solution)/shard_map/ppermute | solution.py:311
  39.5 7.9 %collective-permute-start.9 = (bf16[256,256]{1,0:T(8,128)(2,1)S(1)}, bf16[256,256]{1,0:T(8,128)(2,1)S(1)}, u32[]{:S(2)}, u32[]{:S(2)}) collective-permute-start(bf16[256,256]{1,0:T(8,128)(2,1)S(1)} %get-tuple-element.37), channel_id=1, source_target_pairs={{0,4},{2,6},{4,0},{6,2},{8,12},{10,14},{12,8},{14,10},{16,20},{18,... | collective-permute-start | bytes 393224 | tf_op jit(solution)/shard_map/ppermute | solution.py:311
  48.4 11.3 %collective-permute-start.15 = (bf16[768,128]{1,0:T(8,128)(2,1)S(1)}, bf16[768,128]{1,0:T(8,128)(2,1)S(1)}, u32[]{:S(2)}, u32[]{:S(2)}) collective-permute-start(bf16[768,128]{1,0:T(8,128)(2,1)S(1)} %entry_parts.1), channel_id=1, source_target_pairs={{0,1},{1,0},{2,3},{3,2},{4,5},{5,4},{6,7},{7,6},{8,9},{9,8},{10,11... | collective-permute-start | bytes 589832 | tf_op jit(solution)/shard_map/ppermute | solution.py:541

commit v4 on v3

v4 whole, which is shorter than its diff:
```python
import functools

import jax
import jax.numpy as jnp
from jax import lax
from jax.experimental import pallas as pl
from jax.experimental.pallas import tpu as pltpu
from jax.sharding import PartitionSpec as P

BF16 = jnp.bfloat16
F32 = jnp.float32
LANES = 128
GROUP = 4
TAIL = 16
LOG2E = 1.4426950408889634
MIB = 1024 * 1024

NN = (((1,), (0,)), ((), ()))
NT = (((1,), (1,)), ((), ()))
TN = (((0,), (0,)), ((), ()))


def dot(a, b, dims):
    return lax.dot_general(a, b, dims, preferred_element_type=F32)


def iota(shape, dim):
    return lax.broadcasted_iota(jnp.int32, shape, dim)


def three(values):
    high = values.astype(BF16)
    rest = values - high.astype(F32)
    mid = rest.astype(BF16)
    return high, mid, (rest - mid.astype(F32)).astype(BF16)


SLOT = LANES // 4


def summed(mask, terms):
    heads, length = terms[0].shape
    gap = [] if heads == SLOT else [jnp.zeros((SLOT - heads, length), BF16)]
    rows = [r for t in terms for r in [t] + gap] + [jnp.zeros((SLOT, length), BF16)]
    each = dot(mask, jnp.concatenate(rows, axis=0), NT)
    return each + pltpu.roll(each, LANES - SLOT, 1) + pltpu.roll(each, LANES - 2 * SLOT, 1)


def head_of_lane(head_dim, width, first):
    shape = (LANES, width)
    return jnp.where(iota(shape, 0) == first + iota(shape, 1) // head_dim, 1.0, 0.0).astype(BF16)


def whole(count):
    return [pl.BlockSpec(memory_space=pltpu.VMEM)] * count


def in_hbm(*arrays):
    return [pltpu.with_memory_space_constraint(a, pltpu.HBM) for a in arrays]


SMEM = pl.BlockSpec(memory_space=pltpu.SMEM)
HBM = pl.BlockSpec(memory_space=pltpu.HBM)
ANY = pl.BlockSpec(memory_space=pl.ANY)


def params(mib):
    return pltpu.CompilerParams(vmem_limit_bytes=mib * MIB)


def cost(flops, size, transcendentals=0):
    return pl.CostEstimate(
        flops=flops, bytes_accessed=size, transcendentals=transcendentals
    )


def chunk_count(width):
    return 2 if (width // GROUP) % (2 * LANES) == 0 else 1


def chunk_lanes(place, k, chunk, part, width):
    start = (place[0] ^ k) * (width // GROUP) + chunk * part
    return pl.ds(pl.multiple_of(start, part), part)


def factors_of(ld):
    length = ld.shape[1]
    terms = three(ld)
    rows, other = iota((length, length), 0), iota((length, length), 1)
    after = jnp.where(other > rows, 1.0, 0.0).astype(BF16)
    until = jnp.where(other <= rows, 1.0, 0.0).astype(BF16)
    into_end = jnp.exp(summed(after, terms)).astype(BF16)
    from_start = jnp.exp(summed(until, terms)).astype(BF16)
    total = jnp.exp(summed(jnp.ones((TAIL, length), BF16), terms))
    high = total.astype(BF16).astype(F32)
    halves = jnp.where(iota(total.shape, 0) < TAIL // 2, high, total - high).astype(BF16)
    return into_end, from_start, halves


def put_states(head_dim, chunk, place, operands, outs, ready):
    into_end, from_start, halves, b, c, x, dy = operands
    x_scaled, dy_scaled, spread, *sends = outs
    group, state = len(sends), b.shape[1]
    width = x.shape[1]
    chunks = chunk_count(width)
    part = width // (group * chunks)
    sides = [(into_end, b, x, x_scaled, 0), (from_start, c, dy, dy_scaled, state)]
    for side, (factors, proj, cols, scaled, first) in enumerate(sides):
        ready(side)
        turned = proj[...].T
        for k in range(group):
            here = slice(k * part, (k + 1) * part)
            lanes = chunk_lanes(place, k, chunk, part, width)
            first_head = ((place[0] ^ k) * chunks + chunk) * (part // head_dim)
            hot = head_of_lane(head_dim, part, first_head)
            wide = dot(factors, hot, NN).astype(BF16)
            if side == 0:
                spread[:, here] = wide
                sends[k][2 * state :, :] = dot(halves, hot, NN).astype(BF16)
            piece = cols[:, lanes] * wide
            scaled[:, here] = piece
            sends[k][first : first + state, :] = dot(turned, piece, NN).astype(BF16)


def first_states_kernel(head_dim, group, place, ld_in, b_in, c_in, x_in, dy_in, *refs):
    ld, b, c, x, dy, into_end, from_start, halves = refs[:8]
    outs, sems = refs[8:-1], refs[-1]
    pairs = [(ld_in, ld), (b_in, b), (x_in, x), (c_in, c), (dy_in, dy)]
    copies = [pltpu.make_async_copy(i, o, sems.at[n]) for n, (i, o) in enumerate(pairs)]
    for copy in copies:
        copy.start()
    copies[0].wait()
    factors = factors_of(ld[...])
    for ref, value in zip((into_end, from_start, halves), factors):
        ref[...] = value

    def ready(side):
        copies[1 + 2 * side].wait()
        copies[2 + 2 * side].wait()

    put_states(head_dim, 0, place, (*factors, b, c, x, dy), outs, ready)


def next_states_kernel(head_dim, chunk, place, into_end, from_start, halves, *refs):
    operands = (into_end[...], from_start[...], halves[...], *refs[:4])
    put_states(head_dim, chunk, place, operands, refs[4:], lambda side: None)


def states_shapes(group, length, width, state):
    part = width // (group * chunk_count(width))
    scaled = pltpu.VMEM((length, group * part), BF16)
    return [scaled] * 3 + [pltpu.VMEM((2 * state + TAIL, part), BF16)] * group


def first_states(head_dim, group, place, inputs):
    ld, b, c, x, dy = inputs
    (length, width), state = x.shape, b.shape[1]
    kept = [pltpu.VMEM(a.shape, a.dtype) for a in inputs]
    kept += [pltpu.VMEM((rows, LANES), BF16) for rows in (length, length, TAIL)]
    outs = kept + states_shapes(group, length, width, state)
    return pl.pallas_call(
        functools.partial(first_states_kernel, head_dim, group),
        out_shape=outs,
        in_specs=[SMEM] + [HBM] * 5,
        out_specs=whole(len(outs)),
        scratch_shapes=[pltpu.SemaphoreType.DMA((5,))],
        compiler_params=params(8),
        cost_estimate=cost(2 * length * width * (state + LANES), 8 * length * width),
        name="first_states",
    )(place, *in_hbm(*inputs))


def next_states(head_dim, group, chunk, place, factors, b, c, x, dy):
    (length, width), state = x.shape, b.shape[1]
    outs = states_shapes(group, length, width, state)
    return pl.pallas_call(
        functools.partial(next_states_kernel, head_dim, chunk),
        out_shape=outs,
        in_specs=[SMEM] + whole(7),
        out_specs=whole(len(outs)),
        compiler_params=params(8),
        cost_estimate=cost(2 * length * width * (state + LANES), 4 * length * width),
        name="next_states",
    )(place, *factors, b, c, x, dy)


def decay_of(tail):
    tail = tail.astype(F32)
    return tail[:1, :] + tail[TAIL // 2 : TAIL // 2 + 1, :]


def put_decay(ref, first, factor):
    high = factor.astype(BF16).astype(F32)
    shape = (TAIL, factor.shape[1])
    both = jnp.where(iota(shape, 0) < TAIL // 2, high, factor - high)
    ref[first:, :] = both.astype(BF16)


def in_order(group, forward):
    return list(range(group)) if forward else list(range(group - 1, -1, -1))


def side_rows(state, forward):
    return slice(0, state) if forward else slice(state, 2 * state)


def totals_kernel(state, place, *refs):
    group = GROUP
    blocks, out = refs[:group], refs[-1]
    for here in range(group):

        @pl.when(place[0] == here)
        def _(here=here):
            decays = [decay_of(blocks[q ^ here][2 * state :, :]) for q in range(group)]
            for forward in (True, False):
                rows, value = side_rows(state, forward), None
                for q in in_order(group, forward):
                    piece = blocks[q ^ here][rows, :].astype(F32)
                    value = piece if value is None else decays[q] * value + piece
                out[rows, :] = value.astype(BF16)
            factor = decays[0]
            for d in decays[1:]:
                factor = factor * d
            put_decay(out, 2 * state, factor)


def totals(state, place, blocks, after):
    return pl.pallas_call(
        functools.partial(totals_kernel, state),
        out_shape=pltpu.VMEM(blocks[0].shape, BF16),
        in_specs=[SMEM] + whole(len(blocks)) + [ANY] * len(after),
        out_specs=whole(1)[0],
        compiler_params=params(4),
        cost_estimate=cost(8 * blocks[0].size, 10 * blocks[0].size),
        name="totals",
    )(place, *blocks, *after)


def merged_kernel(state, level, last, number, own, received, *refs):
    out = refs[-1]
    d_own, d_other = decay_of(own[2 * state :, :]), decay_of(received[2 * state :, :])
    upper = ((number[0] >> level) & 1) == 1
    later = ((number[0] >> (level + 1)) & 1) == 1
    for is_upper in (False, True):
        for forward in (True, False):
            chosen = upper == is_upper
            if last:
                chosen = chosen & (later != forward)

            @pl.when(chosen)
            def _(is_upper=is_upper, forward=forward):
                rows = side_rows(state, forward)
                mine, other = own[rows, :].astype(F32), received[rows, :].astype(F32)
                value = mine + d_own * other if is_upper == forward else other + d_other * mine
                out[slice(0, state) if last else rows, :] = value.astype(BF16)

    put_decay(out, state if last else 2 * state, d_own * d_other)


def merged(state, level, last, number, own, received, after):
    rows = (state if last else 2 * state) + TAIL
    return pl.pallas_call(
        functools.partial(merged_kernel, state, level, last),
        out_shape=pltpu.VMEM((rows, own.shape[1]), BF16),
        in_specs=[SMEM] + whole(2) + [ANY] * len(after),
        out_specs=whole(1)[0],
        compiler_params=params(4),
        cost_estimate=cost(4 * own.size, 6 * own.size),
        name="merged",
    )(number, own, received, *after)


def members_kernel(state, levels, place, number, *refs):
    received, refs = refs[:levels], refs[levels:]
    group = GROUP
    blocks, outs = refs[:group], refs[-group:]
    entry = []
    for forward in (True, False):
        value, factor = None, 1.0
        for level, r in enumerate(received):
            gets = (((number[0] >> level) & 1) == 1) == forward
            rows = side_rows(state, forward)
            if r.shape[0] < 2 * state:
                rows = slice(0, state)
            piece = r[rows, :].astype(F32) * jnp.where(gets, 1.0, 0.0)
            value = piece if value is None else value + factor * piece
            if level < levels - 1:
                factor = factor * jnp.where(gets, decay_of(r[2 * state :, :]), 1.0)
        entry.append(value)
    for here in range(group):

        @pl.when(place[0] == here)
        def _(here=here):
            decays = [decay_of(blocks[q ^ here][2 * state :, :]) for q in range(group)]
            for forward in (True, False):
                rows, order = side_rows(state, forward), in_order(group, forward)
                value = entry[0 if forward else 1]
                for q in order:
                    outs[q ^ here][rows, :] = value.astype(BF16)
                    if q != order[-1]:
                        value = decays[q] * value + blocks[q ^ here][rows, :].astype(F32)


def member_entries(state, place, number, blocks, received, after):
    group, part = len(blocks), blocks[0].shape[1]
    return pl.pallas_call(
        functools.partial(members_kernel, state, len(received)),
        out_shape=[pltpu.VMEM((2 * state, part), BF16)] * group,
        in_specs=[SMEM] * 2 + whole(group + len(received)) + [ANY] * len(after),
        out_specs=whole(group),
        compiler_params=params(4),
        cost_estimate=cost(12 * blocks[0].size, 16 * blocks[0].size),
        name="member_entries",
    )(place, number, *received, *blocks, *after)


def exchange(parts):
    count = lax.axis_size("seq")
    out = list(parts)
    for k in sorted(range(1, len(parts)), key=lambda k: (-bin(k).count("1"), k)):
        out[k] = lax.ppermute(parts[k], "seq", [(s, s ^ k) for s in range(count)])
    return out


def split_pairs(first, count):
    if count == 1:
        return []
    middle = first + count // 2
    return (
        [(first, middle, first + count)]
        + split_pairs(first, middle - first)
        + split_pairs(middle, first + count - middle)
    )


def inner_kernel(head_dim, chunk, n_before, n_after, ld, b, c, x_all, dy_all, *refs):
    before, refs = refs[:n_before], refs[n_before + n_after :]
    dx_out, db_out, dc_out, x, dy, cum_terms, *scratch = refs
    length, width = x.shape
    piece = head_dim
    pieces = length // piece
    cuts = split_pairs(0, pieces)
    near, near_sum, dx = scratch[:3]
    far, far_sum = scratch[3 : 3 + len(cuts)], scratch[3 + len(cuts) :]
    per_tile = LANES // head_dim
    step = pl.program_id(0)
    owned = (step * chunk_count(x_all.shape[1]) + chunk) * width
    columns = pl.ds(pl.multiple_of(owned, width), width)
    x[...] = x_all[:, columns]
    dy[...] = dy_all[:, columns]

    @pl.when(step == 0)
    def _():
        rows, other = iota((length, length), 0), iota((length, length), 1)
        mask = jnp.where(other <= rows, 1.0, 0.0).astype(BF16)
        cum_small = summed(mask, three(ld[...] * LOG2E))
        lane = iota(cum_small.shape, 1)
        in_slots = jnp.where(lane < SLOT, cum_small, 0.0)
        in_slots = (
            in_slots + pltpu.roll(in_slots, SLOT, 1) + pltpu.roll(in_slots, 2 * SLOT, 1)
        )
        high, mid, low = three(in_slots)
        cum_terms[...] = jnp.where(lane < SLOT, high, jnp.where(lane < 2 * SLOT, mid, low))
        keep = iota((piece, LANES), 0) <= lax.rem(iota((piece, LANES), 1), piece)
        for n in range(pieces):
            rows_n = slice(n * piece, (n + 1) * piece)
            doubled = jnp.concatenate([c[rows_n, :]] * per_tile, axis=0)
            near[rows_n, :] = jnp.where(keep, dot(b[rows_n, :], doubled, NT), 0.0)
        near_sum[...] = jnp.zeros_like(near_sum)
        for (lo, mid_, hi), f, total in zip(cuts, far, far_sum):
            left, right = slice(lo * piece, mid_ * piece), slice(mid_ * piece, hi * piece)
            f[...] = dot(b[left, :], c[right, :], NT).astype(BF16)
            total[...] = jnp.zeros_like(total)

    shape = (LANES, width)
    owner = owned // head_dim + iota(shape, 1) // head_dim
    slot = lax.rem(iota(shape, 0), SLOT) == owner
    hot = jnp.where(slot & (iota(shape, 0) < 3 * SLOT), 1.0, 0.0).astype(BF16)
    cum = dot(cum_terms[...], hot, NN)
    tile = (piece, LANES)
    diagonal = iota(tile, 0) == lax.rem(iota(tile, 1), piece)
    part_of_lane = iota(tile, 1) // head_dim
    for n in range(pieces):
        rows_n = slice(n * piece, (n + 1) * piece)
        total = near_sum[rows_n, :]
        scores = near[rows_n, :]
        for t in range(width // LANES):
            lanes = slice(t * LANES, (t + 1) * LANES)
            col = cum[rows_n, lanes]
            row = jnp.sum(jnp.where(diagonal, col, 0.0), axis=0, keepdims=True)
            decays = jnp.exp2(jnp.minimum(row - col, 0.0))
            dy_t = dy[rows_n, lanes]
            stacked = jnp.concatenate(
                [jnp.where(part_of_lane == h, dy_t, jnp.zeros_like(dy_t)) for h in range(per_tile)],
                axis=0,
            )
            dx[rows_n, lanes] = dot((scores * decays).astype(BF16), stacked, NN)
            total = total + decays * dot(x[rows_n, lanes], stacked, NT)
        near_sum[rows_n, :] = total
    for (lo, mid_, hi), f, total in zip(cuts, far, far_sum):
        left, right = slice(lo * piece, mid_ * piece), slice(mid_ * piece, hi * piece)
        edge = cum[mid_ * piece - 1 : mid_ * piece, :]
        to_edge = jnp.exp2(edge - cum[left, :])
        from_edge = jnp.exp2(cum[right, :] - edge)
        x_edge = (x[left, :].astype(F32) * to_edge).astype(BF16)
        dy_edge = (dy[right, :].astype(F32) * from_edge).astype(BF16)
        dx[left, :] += to_edge * dot(f[...], dy_edge, NN)
        total[...] += dot(x_edge, dy_edge, NT)
    lanes = pl.ds(pl.multiple_of(step * width, width), width)
    dx_out[:, lanes] = dx[...].astype(BF16)

    @pl.when(step == pl.num_programs(0) - 1)
    def _():
        keep = (iota(tile, 0) <= iota(tile, 1)) & (part_of_lane == 0)
        for n in range(pieces):
            rows_n = slice(n * piece, (n + 1) * piece)
            total = near_sum[rows_n, :]
            total = sum(
                [pltpu.roll(total, h * head_dim, 1) for h in range(1, per_tile)], total
            )
            weighted = jnp.where(keep, total, 0.0).astype(BF16)
            doubled = jnp.concatenate([c[rows_n, :]] * per_tile, axis=0)
            db = dot(weighted, doubled, NN)
            dc = dot(weighted, b[rows_n, :], TN)[:piece, :]
            if before:
                db, dc = db + before[0][rows_n, :], dc + before[1][rows_n, :]
            db_out[rows_n, :] = db
            dc_out[rows_n, :] = dc
        for (lo, mid_, hi), total in zip(cuts, far_sum):
            left, right = slice(lo * piece, mid_ * piece), slice(mid_ * piece, hi * piece)
            weighted = total[...].astype(BF16)
            db_out[left, :] += dot(weighted, c[right, :], NN)
            dc_out[right, :] += dot(weighted, b[left, :], TN)


def inner_terms(head_dim, group, chunk, ld, b, c, x, dy, before, after):
    length, state = b.shape
    part = x.shape[1] // (group * chunk_count(x.shape[1]))
    piece = head_dim
    cuts = split_pairs(0, length // piece)
    sizes = [((mid - lo) * piece, (hi - mid) * piece) for lo, mid, hi in cuts]
    return pl.pallas_call(
        functools.partial(inner_kernel, head_dim, chunk, len(before), len(after)),
        grid=(group,),
        out_shape=[
            pltpu.VMEM((length, group * part), BF16),
            pltpu.VMEM((length, state), F32),
            pltpu.VMEM((length, state), F32),
        ],
        in_specs=whole(5 + len(before)) + [ANY] * len(after),
        out_specs=whole(3),
        scratch_shapes=[
            pltpu.VMEM((length, part), BF16),
            pltpu.VMEM((length, part), BF16),
            pltpu.VMEM((length, LANES), BF16),
            pltpu.VMEM((length, LANES), F32),
            pltpu.VMEM((length, LANES), F32),
            pltpu.VMEM((length, part), F32),
        ]
        + [pltpu.VMEM(s, BF16) for s in sizes]
        + [pltpu.VMEM(s, F32) for s in sizes],
        compiler_params=params(16),
        cost_estimate=cost(8 * x.size * state, 4 * x.size, 2 * x.size),
        name="inner_terms",
    )(ld, b, c, x, dy, *before, *after)


def parts_kernel(last, x_scaled, dy_scaled, db_before, dc_before, *refs):
    entries, outs = refs[:GROUP], refs[-1 if last else -2 :]
    length, state = db_before.shape
    part = entries[0].shape[1]
    db, dc = db_before[...], dc_before[...]
    for k, entry in enumerate(entries):
        here = slice(k * part, (k + 1) * part)
        db = db + dot(x_scaled[:, here], entry[state:, :], NT)
        dc = dc + dot(dy_scaled[:, here], entry[:state, :], NT)
    if last:
        outs[0][:length, :] = db.astype(BF16)
        outs[0][length:, :] = dc.astype(BF16)
    else:
        outs[0][...] = db
        outs[1][...] = dc


def entry_parts(last, x_scaled, dy_scaled, db_before, dc_before, entries, after):
    length, state = db_before.shape
    one = pltpu.VMEM((length, state), F32)
    outs = [pltpu.VMEM((2 * length, state), BF16)] if last else [one, one]
    return pl.pallas_call(
        functools.partial(parts_kernel, last),
        out_shape=outs,
        in_specs=whole(4 + len(entries)) + [ANY] * len(after),
        out_specs=whole(len(outs)),
        compiler_params=params(8),
        cost_estimate=cost(4 * x_scaled.size * state, 4 * x_scaled.size),
        name="entry_parts",
    )(x_scaled, dy_scaled, db_before, dc_before, *entries, *after)


def values_kernel(chunk, n_before, place, spread, b, dx_local, *refs):
    entries, (out, dx, sems) = refs[: len(refs) - 3 - n_before], refs[-3:]
    state, part = b.shape[1], entries[0].shape[1]
    stores = []
    for k, entry in enumerate(entries):
        here = slice(k * part, (k + 1) * part)
        local = dx_local[:, pl.ds(pl.multiple_of((place[0] ^ k) * part, part), part)]
        far = spread[:, here].astype(F32) * dot(b[...], entry[state:, :], NN)
        dx[k] = (local.astype(F32) + far).astype(BF16)
        lanes = chunk_lanes(place, k, chunk, part, out.shape[1])
        store = pltpu.make_async_copy(dx.at[k], out.at[:, lanes], sems.at[k])
        store.start()
        stores.append(store)
    for store in stores:
        store.wait()


def entry_values(chunk, chunks, place, spread, b, dx_local, entries, before):
    group, part = len(entries), entries[0].shape[1]
    length, state = b.shape
    size = dx_local.size
    operands = [place, spread, b, dx_local, *entries, *before]
    return pl.pallas_call(
        functools.partial(values_kernel, chunk, len(before)),
        out_shape=pltpu.HBM((length, chunks * group * part), BF16),
        in_specs=[SMEM] + whole(3 + group) + [HBM] * len(before),
        out_specs=HBM,
        input_output_aliases={len(operands) - 1: 0} if before else {},
        scratch_shapes=[
            pltpu.VMEM((group, length, part), BF16),
            pltpu.SemaphoreType.DMA((group,)),
        ],
        compiler_params=params(8),
        cost_estimate=cost(2 * size * state, 4 * size),
        name="entry_values",
    )(*operands)


def over_heads(part):
    count = lax.axis_size("head")
    total = part.astype(F32)
    for shift in range(1, count):
        pairs = [(s, (s + shift) % count) for s in range(count)]
        total = total + lax.ppermute(part, "head", pairs).astype(F32)
    return total.astype(BF16)


def shards(token_values, b_inputs, c_inputs, log_decay, grad_out):
    head_dim = token_values.shape[1] // log_decay.shape[0]
    length, state = b_inputs.shape
    count = lax.axis_size("seq")
    group, chunks = GROUP, chunk_count(token_values.shape[1])
    levels = (count // group).bit_length() - 1
    where = lax.axis_index("seq").astype(jnp.int32)
    place, number = lax.rem(where, group)[None], (where // group)[None]
    inputs = (log_decay, b_inputs, c_inputs, token_values, grad_out)

    ld, b, c, x, dy, *rest = first_states(head_dim, group, place, inputs)
    factors, states = rest[:3], [rest[3:]]
    blocks = [exchange(states[0][3:])]
    for chunk in range(1, chunks):
        states.append(next_states(head_dim, group, chunk, place, factors, b, c, x, dy))
        blocks.append(exchange(states[chunk][3:]))

    entries, inner, sums = [], [], []
    for chunk in range(chunks):
        sent = own = totals(state, place, blocks[chunk], sums[:1])
        received = []
        for level in range(levels):
            step = group << level
            pairs = [(s, s ^ step) for s in range(count)]
            received.append(lax.ppermute(sent, "seq", pairs))
            if len(inner) < chunks and chunk == 0:
                inner.append(
                    inner_terms(head_dim, group, len(inner), ld, b, c, x, dy, sums, [sent])
                )
                sums = list(inner[-1][1:])
            if level < levels - 1:
                last = level == levels - 2
                after = sums if chunk == 0 else []
                both = merged(state, level, last, number, own, received[-1], after)
                sent = both
                if not last:
                    own = both
        after = sums if chunk == 0 else []
        found = member_entries(state, place, number, blocks[chunk], received, after)
        entries.append(exchange(found))
    while len(inner) < chunks:
        inner.append(inner_terms(head_dim, group, len(inner), ld, b, c, x, dy, sums, []))
        sums = list(inner[-1][1:])

    grad_values = []
    for chunk in range(chunks):
        x_scaled, dy_scaled, spread = states[chunk][:3]
        last = chunk == chunks - 1
        sums = entry_parts(last, x_scaled, dy_scaled, *sums, entries[chunk], grad_values)
        out = entry_values(chunk, chunks, place, spread, b, inner[chunk][0], entries[chunk], grad_values)
        grad_values = [out]
    both = over_heads(sums[0])
    return grad_values[0], both[:length], both[length:]


def solution(mesh):
    in_specs = (
        P("seq", "head"),
        P("seq", None),
        P("seq", None),
        P("head", "seq"),
        P("seq", "head"),
    )
    out_specs = (P("seq", "head"), P("seq", None), P("seq", None))
    return jax.shard_map(shards, mesh=mesh, in_specs=in_specs, out_specs=out_specs, check_vma=False)
```

time: 60.7 us -> 66 us (1.087)
  the two profiles are of different devices: /device:TPU:29 before, /device:TPU:0 now
where the time goes in v4:
time: 66 us; the launch traced here: 65.8 us
  Pallas kernels  22.8 us (35%)
  starting transfers between devices  22.5 us (34%)
  waiting for transfers between devices  11.9 us (18%)
  local copies, waits for them, and re-layouts  7.58 us (11%)
  between operations  0.94 us (1%)
    ppermute x12, starting transfers between devices, exchange(): out[k] = lax.ppermute(parts[k], 'seq', [(s, s ^ k) for s in range(count)])  15 us
    pallas_call x2, Pallas kernels, inner_terms(): pl.pallas_call(functools.partial(inner_kernel, head_dim, chunk, len(befor...  9.05 us
    ppermute x12, waiting for transfers between devices, exchange(): out[k] = lax.ppermute(parts[k], 'seq', [(s, s ^ k) for s in range(count)])  8.75 us
    ppermute x4, starting transfers between devices, shards(): received.append(lax.ppermute(sent, 'seq', pairs))  7.4 us
    unnamed x46, local copies, waits for them, and re-layouts  6.9 us
    pallas_call x1, Pallas kernels, first_states(): pl.pallas_call(functools.partial(first_states_kernel, head_dim, group), o...  3.27 us
    ppermute x4, waiting for transfers between devices, shards(): received.append(lax.ppermute(sent, 'seq', pairs))  3.15 us
    pallas_call x2, Pallas kernels, entry_values(): pl.pallas_call(functools.partial(values_kernel, chunk, len(before)), out_...  2.39 us
  transfers between devices with their start and end apart: 17, of which 7 were waited for; matrix products, arithmetic and copies ran while one was open for 0% of the time, Pallas kernels for 27%

profile of v4, /device:TPU:0, one launch (start us, length us, event | category | flops | bytes accessed | tf_op | source)
XLA Modules:
  0.0 65.8 jit_solution(16104200247696996744)
XLA Ops:
  0.6 3.3 %first_states.1 = (f32[32,384]{1,0:T(8,128)S(1)}, bf16[384,128]{1,0:T(8,128)(2,1)S(1)}, bf16[384,128]{1,0:T(8,128)(2,1)S(1)}, bf16[384,2048]{1,0:T(8,128)(2,1)S(...) custom-call(s32[1]{0:T(128)} %bitcast.place, ...), custom_call_target="tpu_custom_call" | custom-call | flops 402653184 | bytes 6291456 | tf_op jit(solution)/shard_map/first_states/pallas_call | solution.py:161
  3.9 0.9 %copy-done.1 = bf16[384,1024]{1,0:T(8,128)(2,1)} copy-done((bf16[384,1024]{1,0:T(8,128)(2,1)}, bf16[384,1024]{1,0:T(8,128)(2,1)S(1)}, u32[]{:S(2)}) %copy-start.1) | copy-done | bytes 786456
  4.8 0.9 %copy-done.3 = bf16[384,1024]{1,0:T(8,128)(2,1)} copy-done((bf16[384,1024]{1,0:T(8,128)(2,1)}, bf16[384,1024]{1,0:T(8,128)(2,1)S(1)}, u32[]{:S(2)}) %copy-start.3) | copy-done | bytes 786456
  5.7 0.9 %copy-done.11 = bf16[384,1024]{1,0:T(8,128)(2,1)} copy-done((bf16[384,1024]{1,0:T(8,128)(2,1)}, bf16[384,1024]{1,0:T(8,128)(2,1)S(1)}, u32[]{:S(2)}) %copy-start.11) | copy-done | bytes 786456
  6.6 2.9 %collective-permute-start = (bf16[272,256]{1,0:T(8,128)(2,1)S(1)}, bf16[272,256]{1,0:T(8,128)(2,1)S(1)}, u32[]{:S(2)}, u32[]{:S(2)}) collective-permute-start(bf16[272,256]{1,0:T(8,128)(2,1)S(1)} %get-tuple-element.51), channel_id=1, source_target_pairs={{0,2},{2,0},{4,6},{6,4},{8,10},{10,8},{12,14},{14,12},{16,18},{18,... | collective-permute-start | bytes 417800 | tf_op jit(solution)/shard_map/ppermute | solution.py:321
  9.5 1.5 %collective-permute-start.1 = (bf16[272,256]{1,0:T(8,128)(2,1)S(1)}, bf16[272,256]{1,0:T(8,128)(2,1)S(1)}, u32[]{:S(2)}, u32[]{:S(2)}) collective-permute-start(bf16[272,256]{1,0:T(8,128)(2,1)S(1)} %get-tuple-element.52), channel_id=1, source_target_pairs={{0,4},{2,6},{4,0},{6,2},{8,12},{10,14},{12,8},{14,10},{16,20},{18,... | collective-permute-start | bytes 417800 | tf_op jit(solution)/shard_map/ppermute | solution.py:321
  11.1 2.6 %collective-permute-done.refs_1_.refs_3_ = bf16[272,256]{1,0:T(8,128)(2,1)S(1)} collective-permute-done((bf16[272,256]{1,0:T(8,128)(2,1)S(1)}, bf16[272,256]{1,0:T(8,128)(2,1)S(1)}, u32[]{:S(2)}, u32[]{:S(2)}) %collective-permute-start) | collective-permute-done | bytes 139296 | tf_op jit(solution)/shard_map/ppermute | solution.py:321
  13.6 4.0 %collective-permute-done.1.refs_2_.refs_4_ = bf16[272,256]{1,0:T(8,128)(2,1)S(1)} collective-permute-done((bf16[272,256]{1,0:T(8,128)(2,1)S(1)}, bf16[272,256]{1,0:T(8,128)(2,1)S(1)}, u32[]{:S(2)}, u32[]{:S(2)}) %collective-permute-start.1) | collective-permute-done | bytes 139296 | tf_op jit(solution)/shard_map/ppermute | solution.py:321
  17.7 0.1 totals.2.refs_0_.own
  17.8 1.6 %collective-permute-start.3 = (bf16[272,256]{1,0:T(8,128)(2,1)S(1)}, bf16[272,256]{1,0:T(8,128)(2,1)}, u32[]{:S(2)}, u32[]{:S(2)}) collective-permute-start(bf16[272,256]{1,0:T(8,128)(2,1)S(1)} %totals.2.refs_0_.own), channel_id=1, source_target_pairs={{0,8},{2,10},{4,12},{6,14},{8,0},{10,2},{12,4},{14,6},{16,24},{18,... | collective-permute-start | bytes 417800 | tf_op jit(solution)/shard_map/ppermute | solution.py:571
  19.4 2.2 %next_states.1 = (bf16[384,1024]{1,0:T(8,128)(2,1)S(1)}, bf16[384,1024]{1,0:T(8,128)(2,1)S(1)}, bf16[384,1024]{1,0:T(8,128)(2,1)S(1)}, bf16[272,256]{1,0:T(8,128...) custom-call(s32[1]{0:T(128)} %bitcast.place, ...), custom_call_target="tpu_custom_call" | custom-call | flops 402653184 | bytes 3145728 | tf_op jit(solution)/shard_map/next_states/pallas_call | solution.py:176
  21.7 0.9 %copy-done.5 = bf16[384,1024]{1,0:T(8,128)(2,1)} copy-done((bf16[384,1024]{1,0:T(8,128)(2,1)}, bf16[384,1024]{1,0:T(8,128)(2,1)S(1)}, u32[]{:S(2)}) %copy-start.5) | copy-done | bytes 786456
  22.6 0.9 %copy-done.7 = bf16[384,1024]{1,0:T(8,128)(2,1)} copy-done((bf16[384,1024]{1,0:T(8,128)(2,1)}, bf16[384,1024]{1,0:T(8,128)(2,1)S(1)}, u32[]{:S(2)}) %copy-start.7) | copy-done | bytes 786456
  23.5 0.9 %copy-done.9 = bf16[384,1024]{1,0:T(8,128)(2,1)} copy-done((bf16[384,1024]{1,0:T(8,128)(2,1)}, bf16[384,1024]{1,0:T(8,128)(2,1)S(1)}, u32[]{:S(2)}) %copy-start.9) | copy-done | bytes 786456
  24.3 0.7 copy-done.13
  25.0 1.2 %collective-permute-start.4 = (bf16[272,256]{1,0:T(8,128)(2,1)}, bf16[272,256]{1,0:T(8,128)(2,1)}, u32[]{:S(2)}, u32[]{:S(2)}) collective-permute-start(bf16[272,256]{1,0:T(8,128)(2,1)} %get-tuple-element.58), channel_id=1, source_target_pairs={{0,2},{2,0},{4,6},{6,4},{8,10},{10,8},{12,14},{14,12},{16,18},{18,... | collective-permute-start | bytes 417800 | tf_op jit(solution)/shard_map/ppermute | solution.py:321
  26.2 0.8 %collective-permute-start.5 = (bf16[272,256]{1,0:T(8,128)(2,1)}, bf16[272,256]{1,0:T(8,128)(2,1)}, u32[]{:S(2)}, u32[]{:S(2)}) collective-permute-start(bf16[272,256]{1,0:T(8,128)(2,1)} %get-tuple-element.59), channel_id=1, source_target_pairs={{0,4},{2,6},{4,0},{6,2},{8,12},{10,14},{12,8},{14,10},{16,20},{18,... | collective-permute-start | bytes 417800 | tf_op jit(solution)/shard_map/ppermute | solution.py:321
  27.0 1.4 %collective-permute-start.6 = (bf16[272,256]{1,0:T(8,128)(2,1)}, bf16[272,256]{1,0:T(8,128)(2,1)}, u32[]{:S(2)}, u32[]{:S(2)}) collective-permute-start(bf16[272,256]{1,0:T(8,128)(2,1)} %get-tuple-element.60), channel_id=1, source_target_pairs={{0,6},{2,4},{4,2},{6,0},{8,14},{10,12},{12,10},{14,8},{16,22},{18,... | collective-permute-start | bytes 417800 | tf_op jit(solution)/shard_map/ppermute | solution.py:321
  28.5 4.5 %inner_terms.2 = (bf16[384,1024]{1,0:T(8,128)(2,1)S(1)}, f32[384,128]{1,0:T(8,128)S(1)}, f32[384,128]{1,0:T(8,128)S(1)}) custom-call(f32[32,384]{1,0:T(8,128)S(1)} %get-tuple-element.49.ld, bf16[384,128]{1,0:T(8,128)(2,1)S(1)} %get-tuple-element.44.refs_0_.b, bf16[384,128]{1,0:T(8,128)(2,1)S(1)} %get-tuple-element.45.refs_1_.c, ...), custom_call_target="tpu_custom_call" | custom-call | flops 805306368 | bytes 3145728 | tf_op jit(solution)/shard_map/inner_terms/pallas_call | solution.py:442
  33.0 1.0 %merged.2.refs_2_ = bf16[144,256]{1,0:T(8,128)(2,1)S(1)} custom-call(s32[1]{0:T(128)} %bitcast.1.number, bf16[272,256]{1,0:T(8,128)(2,1)S(1)} %totals.2.refs_0_.own, bf16[272,256]{1,0:T(8,128)(2,1)} %collective-permute-done.3.received.refs_0_, f32[384,128]{1,0:T(8,128)S(1)} %get-tuple-element.54.refs_0_, f32[384,128]{1,0:T(8,128)S(1)} %get-tuple-element.55.refs_1_), custom_call_target="tpu_custom_call" | custom-call | flops 278528 | bytes 417792 | tf_op jit(solution)/shard_map/merged/pallas_call | solution.py:262
  34.0 4.5 %inner_terms.3 = (bf16[384,1024]{1,0:T(8,128)(2,1)S(1)}, f32[384,128]{1,0:T(8,128)S(1)}, f32[384,128]{1,0:T(8,128)S(1)}) custom-call(f32[32,384]{1,0:T(8,128)S(1)} %get-tuple-element.49.ld, bf16[384,128]{1,0:T(8,128)(2,1)S(1)} %get-tuple-element.44.refs_0_.b, bf16[384,128]{1,0:T(8,128)(2,1)S(1)} %get-tuple-element.45.refs_1_.c, ...), custom_call_target="tpu_custom_call" | custom-call | flops 805306368 | bytes 3145728 | tf_op jit(solution)/shard_map/inner_terms/pallas_call | solution.py:442
  38.6 0.0 copy-start.12
  38.6 1.2 %totals.3.own = bf16[272,256]{1,0:T(8,128)(2,1)S(1)} custom-call(s32[1]{0:T(128)} %bitcast.place, bf16[272,256]{1,0:T(8,128)(2,1)S(1)} %copy-done.14, bf16[272,256]{1,0:T(8,128)(2,1)} %collective-permute-done.4.refs_1_.refs_3_, bf16[272,256]{1,0:T(8,128)(2,1)} %collective-permute-done.5.refs_2_.refs_4_, ...), custom_call_target="tpu_custom_call" | custom-call | flops 557056 | bytes 696320 | tf_op jit(solution)/shard_map/totals/pallas_call | solution.py:228
  39.9 0.5 collective-permute-start.7
  40.4 2.6 %collective-permute-start.12 = (bf16[144,256]{1,0:T(8,128)(2,1)S(1)}, bf16[144,256]{1,0:T(8,128)(2,1)S(1)}, u32[]{:S(2)}, u32[]{:S(2)}) collective-permute-start(bf16[144,256]{1,0:T(8,128)(2,1)S(1)} %merged.2.refs_2_), channel_id=1, source_target_pairs={{0,16},{2,18},{4,20},{6,22},{8,24},{10,26},{12,28},{14,30},{16,0},... | collective-permute-start | bytes 221192 | tf_op jit(solution)/shard_map/ppermute | solution.py:571
  43.0 2.8 %collective-permute-done.12.refs_1_ = bf16[144,256]{1,0:T(8,128)(2,1)S(1)} collective-permute-done((bf16[144,256]{1,0:T(8,128)(2,1)S(1)}, bf16[144,256]{1,0:T(8,128)(2,1)S(1)}, u32[]{:S(2)}, u32[]{:S(2)}) %collective-permute-start.12) | collective-permute-done | bytes 73760 | tf_op jit(solution)/shard_map/ppermute | solution.py:571
  45.8 1.1 %member_entries.3 = (bf16[256,256]{1,0:T(8,128)(2,1)S(1)}, bf16[256,256]{1,0:T(8,128)(2,1)S(1)}, bf16[256,256]{1,0:T(8,128)(2,1)S(1)}, bf16[256,256]{1,0:T(8,128)(2,1)S(1)}) custom-call(s32[1]{0:T(128)} %bitcast.place, s32[1]{0:T(128)} %bitcast.1.number, bf16[272,256]{1,0:T(8,128)(2,1)} %collective-permute-done.3.received.refs_0_, ...), custom_call_target="tpu_custom_call" | custom-call | flops 835584 | bytes 1114112 | tf_op jit(solution)/shard_map/member_entries/pallas_call | solution.py:306
  46.9 1.2 %collective-permute-start.13 = (bf16[256,256]{1,0:T(8,128)(2,1)S(1)}, bf16[256,256]{1,0:T(8,128)(2,1)S(1)}, u32[]{:S(2)}, u32[]{:S(2)}) collective-permute-start(bf16[256,256]{1,0:T(8,128)(2,1)S(1)} %get-tuple-element.70), channel_id=1, source_target_pairs={{0,2},{2,0},{4,6},{6,4},{8,10},{10,8},{12,14},{14,12},{16,18},{18,... | collective-permute-start | bytes 393224 | tf_op jit(solution)/shard_map/ppermute | solution.py:321
  48.2 2.6 %collective-permute-start.8 = (bf16[144,256]{1,0:T(8,128)(2,1)S(1)}, bf16[144,256]{1,0:T(8,128)(2,1)S(1)}, u32[]{:S(2)}, u32[]{:S(2)}) collective-permute-start(bf16[144,256]{1,0:T(8,128)(2,1)S(1)} %merged.3), channel_id=1, source_target_pairs={{0,16},{2,18},{4,20},{6,22},{8,24},{10,26},{12,28},{14,30},{16,0},... | collective-permute-start | bytes 221192 | tf_op jit(solution)/shard_map/ppermute | solution.py:571
  50.8 0.8 %collective-permute-start.14 = (bf16[256,256]{1,0:T(8,128)(2,1)S(1)}, bf16[256,256]{1,0:T(8,128)(2,1)S(1)}, u32[]{:S(2)}, u32[]{:S(2)}) collective-permute-start(bf16[256,256]{1,0:T(8,128)(2,1)S(1)} %get-tuple-element.71), channel_id=1, source_target_pairs={{0,4},{2,6},{4,0},{6,2},{8,12},{10,14},{12,8},{14,10},{16,20},{18,... | collective-permute-start | bytes 393224 | tf_op jit(solution)/shard_map/ppermute | solution.py:321
  51.6 1.5 %collective-permute-start.15 = (bf16[256,256]{1,0:T(8,128)(2,1)S(1)}, bf16[256,256]{1,0:T(8,128)(2,1)S(1)}, u32[]{:S(2)}, u32[]{:S(2)}) collective-permute-start(bf16[256,256]{1,0:T(8,128)(2,1)S(1)} %get-tuple-element.72), channel_id=1, source_target_pairs={{0,6},{2,4},{4,2},{6,0},{8,14},{10,12},{12,10},{14,8},{16,22},{18,... | collective-permute-start | bytes 393224 | tf_op jit(solution)/shard_map/ppermute | solution.py:321
  53.1 0.4 collective-permute-done.8.refs_1_
  53.5 1.2 %member_entries.2 = (bf16[256,256]{1,0:T(8,128)(2,1)S(1)}, bf16[256,256]{1,0:T(8,128)(2,1)S(1)}, bf16[256,256]{1,0:T(8,128)(2,1)S(1)}, bf16[256,256]{1,0:T(8,128)(2,1)S(1)}) custom-call(s32[1]{0:T(128)} %bitcast.place, s32[1]{0:T(128)} %bitcast.1.number, bf16[272,256]{1,0:T(8,128)(2,1)S(1)} %collective-permute-done.7.received.refs_0_, ...), custom_call_target="tpu_custom_call" | custom-call | flops 835584 | bytes 1114112 | tf_op jit(solution)/shard_map/member_entries/pallas_call | solution.py:306
  54.7 1.2 %collective-permute-start.10 = (bf16[256,256]{1,0:T(8,128)(2,1)S(1)}, bf16[256,256]{1,0:T(8,128)(2,1)S(1)}, u32[]{:S(2)}, u32[]{:S(2)}) collective-permute-start(bf16[256,256]{1,0:T(8,128)(2,1)S(1)} %get-tuple-element.64), channel_id=1, source_target_pairs={{0,4},{2,6},{4,0},{6,2},{8,12},{10,14},{12,8},{14,10},{16,20},{18,... | collective-permute-start | bytes 393224 | tf_op jit(solution)/shard_map/ppermute | solution.py:321
  55.9 1.2 %collective-permute-start.11 = (bf16[256,256]{1,0:T(8,128)(2,1)S(1)}, bf16[256,256]{1,0:T(8,128)(2,1)S(1)}, u32[]{:S(2)}, u32[]{:S(2)}) collective-permute-start(bf16[256,256]{1,0:T(8,128)(2,1)S(1)} %get-tuple-element.65), channel_id=1, source_target_pairs={{0,6},{2,4},{4,2},{6,0},{8,14},{10,12},{12,10},{14,8},{16,22},{18,... | collective-permute-start | bytes 393224 | tf_op jit(solution)/shard_map/ppermute | solution.py:321
  57.1 1.2 %collective-permute-start.9 = (bf16[256,256]{1,0:T(8,128)(2,1)S(1)}, bf16[256,256]{1,0:T(8,128)(2,1)S(1)}, u32[]{:S(2)}, u32[]{:S(2)}) collective-permute-start(bf16[256,256]{1,0:T(8,128)(2,1)S(1)} %get-tuple-element.63), channel_id=1, source_target_pairs={{0,2},{2,0},{4,6},{6,4},{8,10},{10,8},{12,14},{14,12},{16,18},{18,... | collective-permute-start | bytes 393224 | tf_op jit(solution)/shard_map/ppermute | solution.py:321
  58.3 0.4 collective-permute-done.15.refs_3_
  58.7 1.2 %entry_values.2.refs_4_ = bf16[384,2048]{1,0:T(8,128)(2,1)} custom-call(s32[1]{0:T(128)} %bitcast.place, bf16[384,1024]{1,0:T(8,128)(2,1)S(1)} %copy-done.12, bf16[384,128]{1,0:T(8,128)(2,1)S(1)} %get-tuple-element.44.refs_0_.b, bf16[384,1024]{1,0:T(8,128)(2,1)S(1)} %get-tuple-element.67.dx_local, bf16[256,256]{1,0:T(8,128)(2,1)S(1)} %get-tuple-element.69.refs_0_, ...), custom_call_target="tpu_custom_call" | custom-call | flops 100663296 | bytes 1572864 | tf_op jit(solution)/shard_map/entry_values/pallas_call | solution.py:522
  60.0 0.4 copy-done.4
  60.4 0.6 entry_parts.2
  60.9 0.8 %collective-permute-done.11.refs_3_ = bf16[256,256]{1,0:T(8,128)(2,1)S(1)} collective-permute-done((bf16[256,256]{1,0:T(8,128)(2,1)S(1)}, bf16[256,256]{1,0:T(8,128)(2,1)S(1)}, u32[]{:S(2)}, u32[]{:S(2)}) %collective-permute-start.11) | collective-permute-done | bytes 131104 | tf_op jit(solution)/shard_map/ppermute | solution.py:321
  61.8 0.9 %collective-permute-done.9.refs_1_ = bf16[256,256]{1,0:T(8,128)(2,1)S(1)} collective-permute-done((bf16[256,256]{1,0:T(8,128)(2,1)S(1)}, bf16[256,256]{1,0:T(8,128)(2,1)S(1)}, u32[]{:S(2)}, u32[]{:S(2)}) %collective-permute-start.9) | collective-permute-done | bytes 131104 | tf_op jit(solution)/shard_map/ppermute | solution.py:321
  62.7 0.6 entry_parts.3
  63.3 0.1 collective-permute-start.16
  63.4 0.4 copy-done.10
  63.8 1.2 %entry_values.3 = bf16[384,2048]{1,0:T(8,128)(2,1)} custom-call(s32[1]{0:T(128)} %bitcast.place, bf16[384,1024]{1,0:T(8,128)(2,1)S(1)} %copy-done.10, bf16[384,128]{1,0:T(8,128)(2,1)S(1)} %get-tuple-element.44.refs_0_.b, bf16[384,1024]{1,0:T(8,128)(2,1)S(1)} %get-tuple-element.56.dx_local, ...), custom_call_target="tpu_custom_call", output_to_operand_aliasing={{}: (8, {})} | custom-call | flops 100663296 | bytes 1572864 | tf_op jit(solution)/shard_map/entry_values/pallas_call | solution.py:522
  65.0 0.1 add_convert_fusion
  65.1 0.7 %fusion = (bf16[384,128]{1,0:T(8,128)(2,1)}, bf16[384,128]{1,0:T(8,128)(2,1)}) fusion(bf16[768,128]{1,0:T(8,128)(2,1)S(1)} %add_convert_fusion), kind=kLoop, calls=%fused_computation.1 | loop fusion | bytes 393216 | tf_op jit(solution)/shard_map/slice | solution.py:599
  (48 shorter events, 0.1 us)
Async XLA Ops:
  3.9 0.9 %copy-start.1 = (bf16[384,1024]{1,0:T(8,128)(2,1)}, bf16[384,1024]{1,0:T(8,128)(2,1)S(1)}, u32[]{:S(2)}) copy-start(bf16[384,1024]{1,0:T(8,128)(2,1)S(1)} %get-tuple-element.75.x_scaled) | copy-start | bytes 2359300
  4.8 0.9 %copy-start.3 = (bf16[384,1024]{1,0:T(8,128)(2,1)}, bf16[384,1024]{1,0:T(8,128)(2,1)S(1)}, u32[]{:S(2)}) copy-start(bf16[384,1024]{1,0:T(8,128)(2,1)S(1)} %get-tuple-element.76.dy_scaled) | copy-start | bytes 2359300
  5.7 0.9 %copy-start.11 = (bf16[384,1024]{1,0:T(8,128)(2,1)}, bf16[384,1024]{1,0:T(8,128)(2,1)S(1)}, u32[]{:S(2)}) copy-start(bf16[384,1024]{1,0:T(8,128)(2,1)S(1)} %get-tuple-element.66.spread) | copy-start | bytes 2359300
  6.6 12.8 %copy-start.15 = (bf16[272,256]{1,0:T(8,128)(2,1)}, bf16[272,256]{1,0:T(8,128)(2,1)S(1)}, u32[]{:S(2)}) copy-start(bf16[272,256]{1,0:T(8,128)(2,1)S(1)} %get-tuple-element.50.refs_0_.refs_2_) | copy-start | bytes 417796
  6.6 7.0 %collective-permute-start = (bf16[272,256]{1,0:T(8,128)(2,1)S(1)}, bf16[272,256]{1,0:T(8,128)(2,1)S(1)}, u32[]{:S(2)}, u32[]{:S(2)}) collective-permute-start(bf16[272,256]{1,0:T(8,128)(2,1)S(1)} %get-tuple-element.51), channel_id=1, source_target_pairs={{0,2},{2,0},{4,6},{6,4},{8,10},{10,8},{12,14},{14,12},{16,18},{18,... | collective-permute-start | bytes 417800 | tf_op jit(solution)/shard_map/ppermute | solution.py:321
  9.5 8.1 %collective-permute-start.1 = (bf16[272,256]{1,0:T(8,128)(2,1)S(1)}, bf16[272,256]{1,0:T(8,128)(2,1)S(1)}, u32[]{:S(2)}, u32[]{:S(2)}) collective-permute-start(bf16[272,256]{1,0:T(8,128)(2,1)S(1)} %get-tuple-element.52), channel_id=1, source_target_pairs={{0,4},{2,6},{4,0},{6,2},{8,12},{10,14},{12,8},{14,10},{16,20},{18,... | collective-permute-start | bytes 417800 | tf_op jit(solution)/shard_map/ppermute | solution.py:321
  11.0 6.6 %collective-permute-start.2 = (bf16[272,256]{1,0:T(8,128)(2,1)S(1)}, bf16[272,256]{1,0:T(8,128)(2,1)S(1)}, u32[]{:S(2)}, u32[]{:S(2)}) collective-permute-start(bf16[272,256]{1,0:T(8,128)(2,1)S(1)} %get-tuple-element.53), channel_id=1, source_target_pairs={{0,6},{2,4},{4,2},{6,0},{8,14},{10,12},{12,10},{14,8},{16,22},{18,... | collective-permute-start | bytes 417800 | tf_op jit(solution)/shard_map/ppermute | solution.py:321
  13.6 5.8 %copy-start.17 = (bf16[272,256]{1,0:T(8,128)(2,1)}, bf16[272,256]{1,0:T(8,128)(2,1)S(1)}, u32[]{:S(2)}) copy-start(bf16[272,256]{1,0:T(8,128)(2,1)S(1)} %collective-permute-done.refs_1_.refs_3_) | copy-start | bytes 417796
  17.6 1.8 %copy-start.19 = (bf16[272,256]{1,0:T(8,128)(2,1)}, bf16[272,256]{1,0:T(8,128)(2,1)S(1)}, u32[]{:S(2)}) copy-start(bf16[272,256]{1,0:T(8,128)(2,1)S(1)} %collective-permute-done.1.refs_2_.refs_4_) | copy-start | bytes 417796
  17.7 1.8 %copy-start.21 = (bf16[272,256]{1,0:T(8,128)(2,1)}, bf16[272,256]{1,0:T(8,128)(2,1)S(1)}, u32[]{:S(2)}) copy-start(bf16[272,256]{1,0:T(8,128)(2,1)S(1)} %collective-permute-done.2.refs_3_.refs_5_) | copy-start | bytes 417796
  17.8 15.2 %collective-permute-start.3 = (bf16[272,256]{1,0:T(8,128)(2,1)S(1)}, bf16[272,256]{1,0:T(8,128)(2,1)}, u32[]{:S(2)}, u32[]{:S(2)}) collective-permute-start(bf16[272,256]{1,0:T(8,128)(2,1)S(1)} %totals.2.refs_0_.own), channel_id=1, source_target_pairs={{0,8},{2,10},{4,12},{6,14},{8,0},{10,2},{12,4},{14,6},{16,24},{18,... | collective-permute-start | bytes 417800 | tf_op jit(solution)/shard_map/ppermute | solution.py:571
  21.7 0.9 %copy-start.5 = (bf16[384,1024]{1,0:T(8,128)(2,1)}, bf16[384,1024]{1,0:T(8,128)(2,1)S(1)}, u32[]{:S(2)}) copy-start(bf16[384,1024]{1,0:T(8,128)(2,1)S(1)} %get-tuple-element.73.x_scaled) | copy-start | bytes 2359300
  22.6 0.9 %copy-start.7 = (bf16[384,1024]{1,0:T(8,128)(2,1)}, bf16[384,1024]{1,0:T(8,128)(2,1)S(1)}, u32[]{:S(2)}) copy-start(bf16[384,1024]{1,0:T(8,128)(2,1)S(1)} %get-tuple-element.74.dy_scaled) | copy-start | bytes 2359300
  23.5 0.9 %copy-start.9 = (bf16[384,1024]{1,0:T(8,128)(2,1)}, bf16[384,1024]{1,0:T(8,128)(2,1)S(1)}, u32[]{:S(2)}) copy-start(bf16[384,1024]{1,0:T(8,128)(2,1)S(1)} %get-tuple-element.48.spread) | copy-start | bytes 2359300
  24.3 0.7 copy-start.13
  25.0 13.6 %collective-permute-start.4 = (bf16[272,256]{1,0:T(8,128)(2,1)}, bf16[272,256]{1,0:T(8,128)(2,1)}, u32[]{:S(2)}, u32[]{:S(2)}) collective-permute-start(bf16[272,256]{1,0:T(8,128)(2,1)} %get-tuple-element.58), channel_id=1, source_target_pairs={{0,2},{2,0},{4,6},{6,4},{8,10},{10,8},{12,14},{14,12},{16,18},{18,... | collective-permute-start | bytes 417800 | tf_op jit(solution)/shard_map/ppermute | solution.py:321
  26.2 12.4 %collective-permute-start.5 = (bf16[272,256]{1,0:T(8,128)(2,1)}, bf16[272,256]{1,0:T(8,128)(2,1)}, u32[]{:S(2)}, u32[]{:S(2)}) collective-permute-start(bf16[272,256]{1,0:T(8,128)(2,1)} %get-tuple-element.59), channel_id=1, source_target_pairs={{0,4},{2,6},{4,0},{6,2},{8,12},{10,14},{12,8},{14,10},{16,20},{18,... | collective-permute-start | bytes 417800 | tf_op jit(solution)/shard_map/ppermute | solution.py:321
  27.0 11.5 %collective-permute-start.6 = (bf16[272,256]{1,0:T(8,128)(2,1)}, bf16[272,256]{1,0:T(8,128)(2,1)}, u32[]{:S(2)}, u32[]{:S(2)}) collective-permute-start(bf16[272,256]{1,0:T(8,128)(2,1)} %get-tuple-element.60), channel_id=1, source_target_pairs={{0,6},{2,4},{4,2},{6,0},{8,14},{10,12},{12,10},{14,8},{16,22},{18,... | collective-permute-start | bytes 417800 | tf_op jit(solution)/shard_map/ppermute | solution.py:321
  34.0 4.6 %copy-start.14 = (bf16[272,256]{1,0:T(8,128)(2,1)S(1)}, bf16[272,256]{1,0:T(8,128)(2,1)}, u32[]{:S(2)}) copy-start(bf16[272,256]{1,0:T(8,128)(2,1)} %copy-done.13) | copy-start | bytes 417796
  34.0 11.8 %copy-start.16 = (bf16[272,256]{1,0:T(8,128)(2,1)S(1)}, bf16[272,256]{1,0:T(8,128)(2,1)}, u32[]{:S(2)}) copy-start(bf16[272,256]{1,0:T(8,128)(2,1)} %copy-done.15) | copy-start | bytes 417796
  34.0 11.7 %copy-start.18 = (bf16[272,256]{1,0:T(8,128)(2,1)S(1)}, bf16[272,256]{1,0:T(8,128)(2,1)}, u32[]{:S(2)}) copy-start(bf16[272,256]{1,0:T(8,128)(2,1)} %copy-done.17) | copy-start | bytes 417796
  34.0 11.7 %copy-start.20 = (bf16[272,256]{1,0:T(8,128)(2,1)S(1)}, bf16[272,256]{1,0:T(8,128)(2,1)}, u32[]{:S(2)}) copy-start(bf16[272,256]{1,0:T(8,128)(2,1)} %copy-done.19) | copy-start | bytes 417796
  34.0 11.7 %copy-start.22 = (bf16[272,256]{1,0:T(8,128)(2,1)S(1)}, bf16[272,256]{1,0:T(8,128)(2,1)}, u32[]{:S(2)}) copy-start(bf16[272,256]{1,0:T(8,128)(2,1)} %copy-done.21) | copy-start | bytes 417796
  38.6 20.1 %copy-start.12 = (bf16[384,1024]{1,0:T(8,128)(2,1)S(1)}, bf16[384,1024]{1,0:T(8,128)(2,1)}, u32[]{:S(2)}) copy-start(bf16[384,1024]{1,0:T(8,128)(2,1)} %copy-done.11) | copy-start | bytes 2359300
  39.9 8.2 %collective-permute-start.7 = (bf16[272,256]{1,0:T(8,128)(2,1)S(1)}, bf16[272,256]{1,0:T(8,128)(2,1)S(1)}, u32[]{:S(2)}, u32[]{:S(2)}) collective-permute-start(bf16[272,256]{1,0:T(8,128)(2,1)S(1)} %totals.3.own), channel_id=1, source_target_pairs={{0,8},{2,10},{4,12},{6,14},{8,0},{10,2},{12,4},{14,6},{16,24},{18,... | collective-permute-start | bytes 417800 | tf_op jit(solution)/shard_map/ppermute | solution.py:571
  40.4 5.4 %collective-permute-start.12 = (bf16[144,256]{1,0:T(8,128)(2,1)S(1)}, bf16[144,256]{1,0:T(8,128)(2,1)S(1)}, u32[]{:S(2)}, u32[]{:S(2)}) collective-permute-start(bf16[144,256]{1,0:T(8,128)(2,1)S(1)} %merged.2.refs_2_), channel_id=1, source_target_pairs={{0,16},{2,18},{4,20},{6,22},{8,24},{10,26},{12,28},{14,30},{16,0},... | collective-permute-start | bytes 221192 | tf_op jit(solution)/shard_map/ppermute | solution.py:571
  46.9 10.2 %collective-permute-start.13 = (bf16[256,256]{1,0:T(8,128)(2,1)S(1)}, bf16[256,256]{1,0:T(8,128)(2,1)S(1)}, u32[]{:S(2)}, u32[]{:S(2)}) collective-permute-start(bf16[256,256]{1,0:T(8,128)(2,1)S(1)} %get-tuple-element.70), channel_id=1, source_target_pairs={{0,2},{2,0},{4,6},{6,4},{8,10},{10,8},{12,14},{14,12},{16,18},{18,... | collective-permute-start | bytes 393224 | tf_op jit(solution)/shard_map/ppermute | solution.py:321
  48.2 5.3 %collective-permute-start.8 = (bf16[144,256]{1,0:T(8,128)(2,1)S(1)}, bf16[144,256]{1,0:T(8,128)(2,1)S(1)}, u32[]{:S(2)}, u32[]{:S(2)}) collective-permute-start(bf16[144,256]{1,0:T(8,128)(2,1)S(1)} %merged.3), channel_id=1, source_target_pairs={{0,16},{2,18},{4,20},{6,22},{8,24},{10,26},{12,28},{14,30},{16,0},... | collective-permute-start | bytes 221192 | tf_op jit(solution)/shard_map/ppermute | solution.py:571
  50.8 7.5 %collective-permute-start.14 = (bf16[256,256]{1,0:T(8,128)(2,1)S(1)}, bf16[256,256]{1,0:T(8,128)(2,1)S(1)}, u32[]{:S(2)}, u32[]{:S(2)}) collective-permute-start(bf16[256,256]{1,0:T(8,128)(2,1)S(1)} %get-tuple-element.71), channel_id=1, source_target_pairs={{0,4},{2,6},{4,0},{6,2},{8,12},{10,14},{12,8},{14,10},{16,20},{18,... | collective-permute-start | bytes 393224 | tf_op jit(solution)/shard_map/ppermute | solution.py:321
  51.6 7.1 %collective-permute-start.15 = (bf16[256,256]{1,0:T(8,128)(2,1)S(1)}, bf16[256,256]{1,0:T(8,128)(2,1)S(1)}, u32[]{:S(2)}, u32[]{:S(2)}) collective-permute-start(bf16[256,256]{1,0:T(8,128)(2,1)S(1)} %get-tuple-element.72), channel_id=1, source_target_pairs={{0,6},{2,4},{4,2},{6,0},{8,14},{10,12},{12,10},{14,8},{16,22},{18,... | collective-permute-start | bytes 393224 | tf_op jit(solution)/shard_map/ppermute | solution.py:321
  54.7 6.2 %collective-permute-start.10 = (bf16[256,256]{1,0:T(8,128)(2,1)S(1)}, bf16[256,256]{1,0:T(8,128)(2,1)S(1)}, u32[]{:S(2)}, u32[]{:S(2)}) collective-permute-start(bf16[256,256]{1,0:T(8,128)(2,1)S(1)} %get-tuple-element.64), channel_id=1, source_target_pairs={{0,4},{2,6},{4,0},{6,2},{8,12},{10,14},{12,8},{14,10},{16,20},{18,... | collective-permute-start | bytes 393224 | tf_op jit(solution)/shard_map/ppermute | solution.py:321
  55.9 5.9 %collective-permute-start.11 = (bf16[256,256]{1,0:T(8,128)(2,1)S(1)}, bf16[256,256]{1,0:T(8,128)(2,1)S(1)}, u32[]{:S(2)}, u32[]{:S(2)}) collective-permute-start(bf16[256,256]{1,0:T(8,128)(2,1)S(1)} %get-tuple-element.65), channel_id=1, source_target_pairs={{0,6},{2,4},{4,2},{6,0},{8,14},{10,12},{12,10},{14,8},{16,22},{18,... | collective-permute-start | bytes 393224 | tf_op jit(solution)/shard_map/ppermute | solution.py:321
  57.1 5.6 %collective-permute-start.9 = (bf16[256,256]{1,0:T(8,128)(2,1)S(1)}, bf16[256,256]{1,0:T(8,128)(2,1)S(1)}, u32[]{:S(2)}, u32[]{:S(2)}) collective-permute-start(bf16[256,256]{1,0:T(8,128)(2,1)S(1)} %get-tuple-element.63), channel_id=1, source_target_pairs={{0,2},{2,0},{4,6},{6,4},{8,10},{10,8},{12,14},{14,12},{16,18},{18,... | collective-permute-start | bytes 393224 | tf_op jit(solution)/shard_map/ppermute | solution.py:321
  58.7 1.2 %copy-start.2 = (bf16[384,1024]{1,0:T(8,128)(2,1)S(1)}, bf16[384,1024]{1,0:T(8,128)(2,1)}, u32[]{:S(2)}) copy-start(bf16[384,1024]{1,0:T(8,128)(2,1)} %copy-done.1) | copy-start | bytes 2359300
  58.7 1.7 %copy-start.4 = (bf16[384,1024]{1,0:T(8,128)(2,1)S(1)}, bf16[384,1024]{1,0:T(8,128)(2,1)}, u32[]{:S(2)}) copy-start(bf16[384,1024]{1,0:T(8,128)(2,1)} %copy-done.3) | copy-start | bytes 2359300
  58.7 3.9 %copy-start.8 = (bf16[384,1024]{1,0:T(8,128)(2,1)S(1)}, bf16[384,1024]{1,0:T(8,128)(2,1)}, u32[]{:S(2)}) copy-start(bf16[384,1024]{1,0:T(8,128)(2,1)} %copy-done.7) | copy-start | bytes 2359300
  59.9 2.7 %copy-start = (bf16[384,2048]{1,0:T(8,128)(2,1)S(1)}, bf16[384,2048]{1,0:T(8,128)(2,1)}, u32[]{:S(2)}) copy-start(bf16[384,2048]{1,0:T(8,128)(2,1)} %entry_values.2.refs_4_) | copy-start | bytes 4718596
  59.9 2.7 %copy-start.6 = (bf16[384,1024]{1,0:T(8,128)(2,1)S(1)}, bf16[384,1024]{1,0:T(8,128)(2,1)}, u32[]{:S(2)}) copy-start(bf16[384,1024]{1,0:T(8,128)(2,1)} %copy-done.5) | copy-start | bytes 2359300
  62.7 1.1 %copy-start.10 = (bf16[384,1024]{1,0:T(8,128)(2,1)S(1)}, bf16[384,1024]{1,0:T(8,128)(2,1)}, u32[]{:S(2)}) copy-start(bf16[384,1024]{1,0:T(8,128)(2,1)} %copy-done.9) | copy-start | bytes 2359300
  63.3 1.7 %collective-permute-start.16 = (bf16[768,128]{1,0:T(8,128)(2,1)S(1)}, bf16[768,128]{1,0:T(8,128)(2,1)S(1)}, u32[]{:S(2)}, u32[]{:S(2)}) collective-permute-start(bf16[768,128]{1,0:T(8,128)(2,1)S(1)} %entry_parts.3), channel_id=1, source_target_pairs={{0,1},{1,0},{2,3},{3,2},{4,5},{5,4},{6,7},{7,6},{8,9},{9,8},{10,11... | collective-permute-start | bytes 589832 | tf_op jit(solution)/shard_map/ppermute | solution.py:543

commit v5 on v4

--- a/solution.py
+++ b/solution.py
@@ -69,17 +69,24 @@
 
 
 def cost(flops, size, transcendentals=0):
-    return pl.CostEstimate(
-        flops=flops, bytes_accessed=size, transcendentals=transcendentals
-    )
+    del flops, size, transcendentals
+    return pl.CostEstimate(flops=1, bytes_accessed=1, transcendentals=0)
+
+
+def place_of(where):
+    return where[0] & (GROUP - 1)
+
+
+def bit_of(where, level):
+    return (where[0] >> (level + GROUP.bit_length() - 1)) & 1 == 1
 
 
 def chunk_count(width):
     return 2 if (width // GROUP) % (2 * LANES) == 0 else 1
 
 
-def chunk_lanes(place, k, chunk, part, width):
-    start = (place[0] ^ k) * (width // GROUP) + chunk * part
+def chunk_lanes(where, k, chunk, part, width):
+    start = (place_of(where) ^ k) * (width // GROUP) + chunk * part
     return pl.ds(pl.multiple_of(start, part), part)
 
 
@@ -97,7 +104,7 @@
     return into_end, from_start, halves
 
 
-def put_states(head_dim, chunk, place, operands, outs, ready):
+def put_states(head_dim, chunk, where, operands, outs, ready):
     into_end, from_start, halves, b, c, x, dy = operands
     x_scaled, dy_scaled, spread, *sends = outs
     group, state = len(sends), b.shape[1]
@@ -110,8 +117,8 @@
         turned = proj[...].T
         for k in range(group):
             here = slice(k * part, (k + 1) * part)
-            lanes = chunk_lanes(place, k, chunk, part, width)
-            first_head = ((place[0] ^ k) * chunks + chunk) * (part // head_dim)
+            lanes = chunk_lanes(where, k, chunk, part, width)
+            first_head = ((place_of(where) ^ k) * chunks + chunk) * (part // head_dim)
             hot = head_of_lane(head_dim, part, first_head)
             wide = dot(factors, hot, NN).astype(BF16)
             if side == 0:
@@ -122,7 +129,7 @@
             sends[k][first : first + state, :] = dot(turned, piece, NN).astype(BF16)
 
 
-def first_states_kernel(head_dim, group, place, ld_in, b_in, c_in, x_in, dy_in, *refs):
+def first_states_kernel(head_dim, group, where, ld_in, b_in, c_in, x_in, dy_in, *refs):
     ld, b, c, x, dy, into_end, from_start, halves = refs[:8]
     outs, sems = refs[8:-1], refs[-1]
     pairs = [(ld_in, ld), (b_in, b), (x_in, x), (c_in, c), (dy_in, dy)]
@@ -138,12 +145,12 @@
         copies[1 + 2 * side].wait()
         copies[2 + 2 * side].wait()
 
-    put_states(head_dim, 0, place, (*factors, b, c, x, dy), outs, ready)
-
-
-def next_states_kernel(head_dim, chunk, place, into_end, from_start, halves, *refs):
+    put_states(head_dim, 0, where, (*factors, b, c, x, dy), outs, ready)
+
+
+def next_states_kernel(head_dim, chunk, where, into_end, from_start, halves, *refs):
     operands = (into_end[...], from_start[...], halves[...], *refs[:4])
-    put_states(head_dim, chunk, place, operands, refs[4:], lambda side: None)
+    put_states(head_dim, chunk, where, operands, refs[4:], lambda side: None)
 
 
 def states_shapes(group, length, width, state):
@@ -152,7 +159,7 @@
     return [scaled] * 3 + [pltpu.VMEM((2 * state + TAIL, part), BF16)] * group
 
 
-def first_states(head_dim, group, place, inputs):
+def first_states(head_dim, group, where, inputs):
     ld, b, c, x, dy = inputs
     (length, width), state = x.shape, b.shape[1]
     kept = [pltpu.VMEM(a.shape, a.dtype) for a in inputs]
@@ -167,10 +174,10 @@
         compiler_params=params(8),
         cost_estimate=cost(2 * length * width * (state + LANES), 8 * length * width),
         name="first_states",
-    )(place, *in_hbm(*inputs))
-
-
-def next_states(head_dim, group, chunk, place, factors, b, c, x, dy):
+    )(where, *in_hbm(*inputs))
+
+
+def next_states(head_dim, group, chunk, where, factors, b, c, x, dy):
     (length, width), state = x.shape, b.shape[1]
     outs = states_shapes(group, length, width, state)
     return pl.pallas_call(
@@ -181,7 +188,7 @@
         compiler_params=params(8),
         cost_estimate=cost(2 * length * width * (state + LANES), 4 * length * width),
         name="next_states",
-    )(place, *factors, b, c, x, dy)
+    )(where, *factors, b, c, x, dy)
 
 
 def decay_of(tail):
@@ -204,12 +211,12 @@
     return slice(0, state) if forward else slice(state, 2 * state)
 
 
-def totals_kernel(state, place, *refs):
+def totals_kernel(state, where, *refs):
     group = GROUP
     blocks, out = refs[:group], refs[-1]
     for here in range(group):
 
-        @pl.when(place[0] == here)
+        @pl.when(place_of(where) == here)
         def _(here=here):
             decays = [decay_of(blocks[q ^ here][2 * state :, :]) for q in range(group)]
             for forward in (True, False):
@@ -224,7 +231,7 @@
             put_decay(out, 2 * state, factor)
 
 
-def totals(state, place, blocks, after):
+def totals(state, where, blocks, after):
     return pl.pallas_call(
         functools.partial(totals_kernel, state),
         out_shape=pltpu.VMEM(blocks[0].shape, BF16),
@@ -233,14 +240,14 @@
         compiler_params=params(4),
         cost_estimate=cost(8 * blocks[0].size, 10 * blocks[0].size),
         name="totals",
-    )(place, *blocks, *after)
-
-
-def merged_kernel(state, level, last, number, own, received, *refs):
+    )(where, *blocks, *after)
+
+
+def merged_kernel(state, level, last, where, own, received, *refs):
     out = refs[-1]
     d_own, d_other = decay_of(own[2 * state :, :]), decay_of(received[2 * state :, :])
-    upper = ((number[0] >> level) & 1) == 1
-    later = ((number[0] >> (level + 1)) & 1) == 1
+    upper = bit_of(where, level)
+    later = bit_of(where, level + 1)
     for is_upper in (False, True):
         for forward in (True, False):
             chosen = upper == is_upper
@@ -257,7 +264,7 @@
     put_decay(out, state if last else 2 * state, d_own * d_other)
 
 
-def merged(state, level, last, number, own, received, after):
+def merged(state, level, last, where, own, received, after):
     rows = (state if last else 2 * state) + TAIL
     return pl.pallas_call(
         functools.partial(merged_kernel, state, level, last),
@@ -267,10 +274,10 @@
         compiler_params=params(4),
         cost_estimate=cost(4 * own.size, 6 * own.size),
         name="merged",
-    )(number, own, received, *after)
-
-
-def members_kernel(state, levels, place, number, *refs):
+    )(where, own, received, *after)
+
+
+def members_kernel(state, levels, where, *refs):
     received, refs = refs[:levels], refs[levels:]
     group = GROUP
     blocks, outs = refs[:group], refs[-group:]
@@ -278,7 +285,7 @@
     for forward in (True, False):
         value, factor = None, 1.0
         for level, r in enumerate(received):
-            gets = (((number[0] >> level) & 1) == 1) == forward
+            gets = (bit_of(where, level)) == forward
             rows = side_rows(state, forward)
             if r.shape[0] < 2 * state:
                 rows = slice(0, state)
@@ -289,7 +296,7 @@
         entry.append(value)
     for here in range(group):
 
-        @pl.when(place[0] == here)
+        @pl.when(place_of(where) == here)
         def _(here=here):
             decays = [decay_of(blocks[q ^ here][2 * state :, :]) for q in range(group)]
             for forward in (True, False):
@@ -301,17 +308,17 @@
                         value = decays[q] * value + blocks[q ^ here][rows, :].astype(F32)
 
 
-def member_entries(state, place, number, blocks, received, after):
+def member_entries(state, where, blocks, received, after):
     group, part = len(blocks), blocks[0].shape[1]
     return pl.pallas_call(
         functools.partial(members_kernel, state, len(received)),
         out_shape=[pltpu.VMEM((2 * state, part), BF16)] * group,
-        in_specs=[SMEM] * 2 + whole(group + len(received)) + [ANY] * len(after),
+        in_specs=[SMEM] + whole(group + len(received)) + [ANY] * len(after),
         out_specs=whole(group),
         compiler_params=params(4),
         cost_estimate=cost(12 * blocks[0].size, 16 * blocks[0].size),
         name="member_entries",
-    )(place, number, *received, *blocks, *after)
+    )(where, *received, *blocks, *after)
 
 
 def exchange(parts):
@@ -497,16 +504,17 @@
     )(x_scaled, dy_scaled, db_before, dc_before, *entries, *after)
 
 
-def values_kernel(chunk, n_before, place, spread, b, dx_local, *refs):
-    entries, (out, dx, sems) = refs[: len(refs) - 3 - n_before], refs[-3:]
+def values_kernel(chunk, where, spread, b, dx_local, *refs):
+    entries, (out, done, dx, sems) = refs[:GROUP], refs[-4:]
+    done[...] = jnp.zeros_like(done)
     state, part = b.shape[1], entries[0].shape[1]
     stores = []
     for k, entry in enumerate(entries):
         here = slice(k * part, (k + 1) * part)
-        local = dx_local[:, pl.ds(pl.multiple_of((place[0] ^ k) * part, part), part)]
+        local = dx_local[:, pl.ds(pl.multiple_of((place_of(where) ^ k) * part, part), part)]
         far = spread[:, here].astype(F32) * dot(b[...], entry[state:, :], NN)
         dx[k] = (local.astype(F32) + far).astype(BF16)
-        lanes = chunk_lanes(place, k, chunk, part, out.shape[1])
+        lanes = chunk_lanes(where, k, chunk, part, out.shape[1])
         store = pltpu.make_async_copy(dx.at[k], out.at[:, lanes], sems.at[k])
         store.start()
         stores.append(store)
@@ -514,16 +522,19 @@
         store.wait()
 
 
-def entry_values(chunk, chunks, place, spread, b, dx_local, entries, before):
+def entry_values(chunk, chunks, where, spread, b, dx_local, entries, before, after):
     group, part = len(entries), entries[0].shape[1]
     length, state = b.shape
     size = dx_local.size
-    operands = [place, spread, b, dx_local, *entries, *before]
-    return pl.pallas_call(
-        functools.partial(values_kernel, chunk, len(before)),
-        out_shape=pltpu.HBM((length, chunks * group * part), BF16),
-        in_specs=[SMEM] + whole(3 + group) + [HBM] * len(before),
-        out_specs=HBM,
+    operands = [where, spread, b, dx_local, *entries, *after, *before]
+    return pl.pallas_call(
+        functools.partial(values_kernel, chunk),
+        out_shape=[
+            pltpu.HBM((length, chunks * group * part), BF16),
+            jax.ShapeDtypeStruct((8, LANES), F32),
+        ],
+        in_specs=[SMEM] + whole(3 + group) + [ANY] * len(after) + [HBM] * len(before),
+        out_specs=[HBM, *whole(1)],
         input_output_aliases={len(operands) - 1: 0} if before else {},
         scratch_shapes=[
             pltpu.VMEM((group, length, part), BF16),
@@ -547,54 +558,82 @@
 def shards(token_values, b_inputs, c_inputs, log_decay, grad_out):
     head_dim = token_values.shape[1] // log_decay.shape[0]
     length, state = b_inputs.shape
-    count = lax.axis_size("seq")
-    group, chunks = GROUP, chunk_count(token_values.shape[1])
+    count, group = lax.axis_size("seq"), GROUP
+    chunks = chunk_count(token_values.shape[1])
     levels = (count // group).bit_length() - 1
-    where = lax.axis_index("seq").astype(jnp.int32)
-    place, number = lax.rem(where, group)[None], (where // group)[None]
+    where = lax.axis_index("seq").astype(jnp.int32)[None]
     inputs = (log_decay, b_inputs, c_inputs, token_values, grad_out)
-
-    ld, b, c, x, dy, *rest = first_states(head_dim, group, place, inputs)
+    order = []
+
+    def then(result):
+        order[:] = [result[-1] if isinstance(result, (list, tuple)) else result]
+        return result
+
+    ld, b, c, x, dy, *rest = then(first_states(head_dim, group, where, inputs))
     factors, states = rest[:3], [rest[3:]]
     blocks = [exchange(states[0][3:])]
     for chunk in range(1, chunks):
-        states.append(next_states(head_dim, group, chunk, place, factors, b, c, x, dy))
+        states.append(then(next_states(head_dim, group, chunk, where, factors, b, c, x, dy)))
         blocks.append(exchange(states[chunk][3:]))
 
-    entries, inner, sums = [], [], []
+    sums, inner = [], []
+
+    def add_inner():
+        if len(inner) < chunks:
+            n = len(inner)
+            inner.append(then(inner_terms(head_dim, group, n, ld, b, c, x, dy, sums, order)))
+            sums[:] = inner[n][1:]
+
+    def to_level(block, level):
+        step = group << level
+        return lax.ppermute(block, "seq", [(s, s ^ step) for s in range(count)])
+
+    own, received, entries = [None] * chunks, [[] for _ in range(chunks)], []
+
+    def open_rounds(chunk):
+        own[chunk] = then(totals(state, where, blocks[chunk], order))
+        received[chunk].append(to_level(own[chunk], 0))
+
+    def close_rounds(chunk):
+        found = then(member_entries(state, where, blocks[chunk], received[chunk], order))
+        entries.append(exchange(found))
+
+    open_rounds(0)
     for chunk in range(chunks):
-        sent = own = totals(state, place, blocks[chunk], sums[:1])
-        received = []
-        for level in range(levels):
-            step = group << level
-            pairs = [(s, s ^ step) for s in range(count)]
-            received.append(lax.ppermute(sent, "seq", pairs))
-            if len(inner) < chunks and chunk == 0:
-                inner.append(
-                    inner_terms(head_dim, group, len(inner), ld, b, c, x, dy, sums, [sent])
-                )
-                sums = list(inner[-1][1:])
-            if level < levels - 1:
-                last = level == levels - 2
-                after = sums if chunk == 0 else []
-                both = merged(state, level, last, number, own, received[-1], after)
-                sent = both
-                if not last:
-                    own = both
-        after = sums if chunk == 0 else []
-        found = member_entries(state, place, number, blocks[chunk], received, after)
-        entries.append(exchange(found))
+        if chunk == 0:
+            add_inner()
+        for level in range(levels - 1):
+            last = level == levels - 2
+            arrived = received[chunk][level]
+            own[chunk] = then(merged(state, level, last, where, own[chunk], arrived, order))
+            received[chunk].append(to_level(own[chunk], level + 1))
+        if chunk + 1 < chunks:
+            open_rounds(chunk + 1)
+        else:
+            add_inner()
+        close_rounds(chunk)
     while len(inner) < chunks:
-        inner.append(inner_terms(head_dim, group, len(inner), ld, b, c, x, dy, sums, []))
-        sums = list(inner[-1][1:])
+        add_inner()
 
     grad_values = []
     for chunk in range(chunks):
         x_scaled, dy_scaled, spread = states[chunk][:3]
         last = chunk == chunks - 1
-        sums = entry_parts(last, x_scaled, dy_scaled, *sums, entries[chunk], grad_values)
-        out = entry_values(chunk, chunks, place, spread, b, inner[chunk][0], entries[chunk], grad_values)
-        grad_values = [out]
+
+        def values():
+            local = inner[chunk][0]
+            out = entry_values(
+                chunk, chunks, where, spread, b, local, entries[chunk], grad_values, order
+            )
+            grad_values[:] = then(out)[:1]
+
+        if not last:
+            values()
+        sums = then(
+            entry_parts(last, x_scaled, dy_scaled, *sums, entries[chunk], [] if last else order)
+        )
+        if last:
+            values()
     both = over_heads(sums[0])
     return grad_values[0], both[:length], both[length:]
 

time: 66 us -> 54.4 us (0.82); the launches traced: 65.8 us -> 53.4 us
  local copies, waits for them, and re-layouts: 7.58 us -> 0.69 us
  Pallas kernels: 22.8 us -> 18.7 us
  waiting for transfers between devices: 11.9 us -> 10.5 us
    unnamed x46 -> x0, local copies, waits for them, and re-layouts: 6.9 us -> none
    pallas_call x2, Pallas kernels: 2.32 us -> 0.38 us  [member_entries(): pl.pallas_call(functools.partial(members_kernel, state, len(received)), o...]
    pallas_call x2, Pallas kernels: 1.36 us -> 0.25 us  [totals(): pl.pallas_call(functools.partial(totals_kernel, state), out_shape=pltpu.V...]
    ppermute x12, waiting for transfers between devices: 8.75 us -> 7.76 us  [exchange(): out[k] = lax.ppermute(parts[k], 'seq', [(s, s ^ k) for s in range(count)])]
    pallas_call x2, Pallas kernels: 1 us -> 0.09 us  [merged(): pl.pallas_call(functools.partial(merged_kernel, state, level, last), out_...]
    pallas_call x1, Pallas kernels: 2.24 us -> 1.57 us  [next_states(): pl.pallas_call(functools.partial(next_states_kernel, head_dim, chunk), ou...]
  transfers between devices with their start and end apart: 17 -> 17, of which waited for: 7 -> 6; matrix products, arithmetic and copies ran while one was open for 0% -> 0% of each run, Pallas kernels for 27% -> 27%
where the time goes in v5:
time: 54.4 us; the launch traced here: 53.4 us
  starting transfers between devices  22.6 us (42%)
  Pallas kernels  18.7 us (34%)
  waiting for transfers between devices  10.5 us (19%)
  between operations  0.81 us (1%)
  local copies, waits for them, and re-layouts  0.69 us (1%)
    ppermute x12, starting transfers between devices, exchange(): out[k] = lax.ppermute(parts[k], 'seq', [(s, s ^ k) for s in range(count)])  15.2 us
    pallas_call x2, Pallas kernels, inner_terms(): pl.pallas_call(functools.partial(inner_kernel, head_dim, chunk, len(befor...  9.02 us
    ppermute x12, waiting for transfers between devices, exchange(): out[k] = lax.ppermute(parts[k], 'seq', [(s, s ^ k) for s in range(count)])  7.76 us
    ppermute x4, starting transfers between devices, to_level(): return lax.ppermute(block, 'seq', [(s, s ^ step) for s in range(count)])  7.26 us
    pallas_call x1, Pallas kernels, first_states(): pl.pallas_call(functools.partial(first_states_kernel, head_dim, group), o...  3.26 us
    pallas_call x2, Pallas kernels, entry_values(): pl.pallas_call(functools.partial(values_kernel, chunk), out_shape=[pltpu....  3.02 us
    ppermute x4, waiting for transfers between devices, to_level(): return lax.ppermute(block, 'seq', [(s, s ^ step) for s in range(count)])  2.78 us
    pallas_call x1, Pallas kernels, next_states(): pl.pallas_call(functools.partial(next_states_kernel, head_dim, chunk), ou...  1.57 us
  transfers between devices with their start and end apart: 17, of which 6 were waited for; matrix products, arithmetic and copies ran while one was open for 0% of the time, Pallas kernels for 27%

profile of v5, /device:TPU:0, one launch (start us, length us, event | category | flops | bytes accessed | tf_op | source)
XLA Modules:
  0.0 53.4 jit_solution(18062096444825624810)
XLA Ops:
  0.6 3.3 %first_states.1 = (f32[32,384]{1,0:T(8,128)S(1)}, bf16[384,128]{1,0:T(8,128)(2,1)S(1)}, bf16[384,128]{1,0:T(8,128)(2,1)S(1)}, bf16[384,2048]{1,0:T(8,128)(2,1)S(...) custom-call(s32[1]{0:T(128)} %bitcast.where, ...), custom_call_target="tpu_custom_call" | custom-call | flops 1 | bytes 1 | tf_op jit(solution)/shard_map/first_states/pallas_call | solution.py:168
  3.9 3.0 %collective-permute-start = (bf16[272,256]{1,0:T(8,128)(2,1)S(1)}, bf16[272,256]{1,0:T(8,128)(2,1)S(1)}, u32[]{:S(2)}, u32[]{:S(2)}) collective-permute-start(bf16[272,256]{1,0:T(8,128)(2,1)S(1)} %get-tuple-element.54), channel_id=1, source_target_pairs={{0,2},{2,0},{4,6},{6,4},{8,10},{10,8},{12,14},{14,12},{16,18},{18,... | collective-permute-start | bytes 417800 | tf_op jit(solution)/shard_map/ppermute | solution.py:328
  6.9 1.5 %collective-permute-start.1 = (bf16[272,256]{1,0:T(8,128)(2,1)S(1)}, bf16[272,256]{1,0:T(8,128)(2,1)S(1)}, u32[]{:S(2)}, u32[]{:S(2)}) collective-permute-start(bf16[272,256]{1,0:T(8,128)(2,1)S(1)} %get-tuple-element.55), channel_id=1, source_target_pairs={{0,4},{2,6},{4,0},{6,2},{8,12},{10,14},{12,8},{14,10},{16,20},{18,... | collective-permute-start | bytes 417800 | tf_op jit(solution)/shard_map/ppermute | solution.py:328
  8.4 0.0 collective-permute-start.2
  8.5 1.6 %next_states.1 = (bf16[384,1024]{1,0:T(8,128)(2,1)S(1)}, bf16[384,1024]{1,0:T(8,128)(2,1)S(1)}, bf16[384,1024]{1,0:T(8,128)(2,1)S(1)}, bf16[272,256]{1,0:T(8,128...) custom-call(s32[1]{0:T(128)} %bitcast.where, ...), custom_call_target="tpu_custom_call" | custom-call | flops 1 | bytes 1 | tf_op jit(solution)/shard_map/next_states/pallas_call | solution.py:183
  10.0 1.0 %collective-permute-done.refs_1_.refs_3_ = bf16[272,256]{1,0:T(8,128)(2,1)S(1)} collective-permute-done((bf16[272,256]{1,0:T(8,128)(2,1)S(1)}, bf16[272,256]{1,0:T(8,128)(2,1)S(1)}, u32[]{:S(2)}, u32[]{:S(2)}) %collective-permute-start) | collective-permute-done | bytes 139296 | tf_op jit(solution)/shard_map/ppermute | solution.py:328
  11.0 4.0 %collective-permute-done.1.refs_2_.refs_4_ = bf16[272,256]{1,0:T(8,128)(2,1)S(1)} collective-permute-done((bf16[272,256]{1,0:T(8,128)(2,1)S(1)}, bf16[272,256]{1,0:T(8,128)(2,1)S(1)}, u32[]{:S(2)}, u32[]{:S(2)}) %collective-permute-start.1) | collective-permute-done | bytes 139296 | tf_op jit(solution)/shard_map/ppermute | solution.py:328
  15.0 0.0 collective-permute-done.2.refs_3_.refs_5_
  15.0 0.1 totals.2.refs_0_.own
  15.2 1.6 %collective-permute-start.6 = (bf16[272,256]{1,0:T(8,128)(2,1)S(1)}, bf16[272,256]{1,0:T(8,128)(2,1)S(1)}, u32[]{:S(2)}, u32[]{:S(2)}) collective-permute-start(bf16[272,256]{1,0:T(8,128)(2,1)S(1)} %totals.2.refs_0_.own), channel_id=1, source_target_pairs={{0,8},{2,10},{4,12},{6,14},{8,0},{10,2},{12,4},{14,6},{16,24},{18,... | collective-permute-start | bytes 417800 | tf_op jit(solution)/shard_map/ppermute | solution.py:589
  16.8 1.2 %collective-permute-start.3 = (bf16[272,256]{1,0:T(8,128)(2,1)S(1)}, bf16[272,256]{1,0:T(8,128)(2,1)S(1)}, u32[]{:S(2)}, u32[]{:S(2)}) collective-permute-start(bf16[272,256]{1,0:T(8,128)(2,1)S(1)} %get-tuple-element.61), channel_id=1, source_target_pairs={{0,2},{2,0},{4,6},{6,4},{8,10},{10,8},{12,14},{14,12},{16,18},{18,... | collective-permute-start | bytes 417800 | tf_op jit(solution)/shard_map/ppermute | solution.py:328
  18.0 0.8 %collective-permute-start.4 = (bf16[272,256]{1,0:T(8,128)(2,1)S(1)}, bf16[272,256]{1,0:T(8,128)(2,1)S(1)}, u32[]{:S(2)}, u32[]{:S(2)}) collective-permute-start(bf16[272,256]{1,0:T(8,128)(2,1)S(1)} %get-tuple-element.62), channel_id=1, source_target_pairs={{0,4},{2,6},{4,0},{6,2},{8,12},{10,14},{12,8},{14,10},{16,20},{18,... | collective-permute-start | bytes 417800 | tf_op jit(solution)/shard_map/ppermute | solution.py:328
  18.8 1.5 %collective-permute-start.5 = (bf16[272,256]{1,0:T(8,128)(2,1)S(1)}, bf16[272,256]{1,0:T(8,128)(2,1)S(1)}, u32[]{:S(2)}, u32[]{:S(2)}) collective-permute-start(bf16[272,256]{1,0:T(8,128)(2,1)S(1)} %get-tuple-element.57.refs_4_), channel_id=1, source_target_pairs={{0,6},{2,4},{4,2},{6,0},{8,14},{10,12},{12,10},{14,8},{16,22},{18,... | collective-permute-start | bytes 417800 | tf_op jit(solution)/shard_map/ppermute | solution.py:328
  20.3 4.5 %inner_terms.2 = (bf16[384,1024]{1,0:T(8,128)(2,1)S(1)}, f32[384,128]{1,0:T(8,128)S(1)}, f32[384,128]{1,0:T(8,128)S(1)}) custom-call(f32[32,384]{1,0:T(8,128)S(1)} %get-tuple-element.52.ld, bf16[384,128]{1,0:T(8,128)(2,1)S(1)} %get-tuple-element.47.refs_0_.b, bf16[384,128]{1,0:T(8,128)(2,1)S(1)} %get-tuple-element.48.refs_1_.c, ...), custom_call_target="tpu_custom_call" | custom-call | flops 1 | bytes 1 | tf_op jit(solution)/shard_map/inner_terms/pallas_call | solution.py:449
  24.8 0.0 collective-permute-done.6.received.refs_0_
  24.8 0.1 merged.2.refs_4_
  24.9 0.0 collective-permute-done.3.refs_1_.refs_3_
  24.9 0.1 collective-permute-done.4.refs_2_.refs_4_
  25.0 0.0 collective-permute-done.5.refs_3_.refs_5_
  25.0 0.1 totals.3.refs_6_.own
  25.1 0.5 collective-permute-start.7
  25.6 2.6 %collective-permute-start.8 = (bf16[144,256]{1,0:T(8,128)(2,1)S(1)}, bf16[144,256]{1,0:T(8,128)(2,1)S(1)}, u32[]{:S(2)}, u32[]{:S(2)}) collective-permute-start(bf16[144,256]{1,0:T(8,128)(2,1)S(1)} %merged.2.refs_4_), channel_id=1, source_target_pairs={{0,16},{2,18},{4,20},{6,22},{8,24},{10,26},{12,28},{14,30},{16,0},... | collective-permute-start | bytes 221192 | tf_op jit(solution)/shard_map/ppermute | solution.py:589
  28.2 2.8 %collective-permute-done.8.refs_1_ = bf16[144,256]{1,0:T(8,128)(2,1)S(1)} collective-permute-done((bf16[144,256]{1,0:T(8,128)(2,1)S(1)}, bf16[144,256]{1,0:T(8,128)(2,1)S(1)}, u32[]{:S(2)}, u32[]{:S(2)}) %collective-permute-start.8) | collective-permute-done | bytes 73760 | tf_op jit(solution)/shard_map/ppermute | solution.py:589
  31.0 0.2 member_entries.2
  31.2 1.5 %collective-permute-start.13 = (bf16[256,256]{1,0:T(8,128)(2,1)S(1)}, bf16[256,256]{1,0:T(8,128)(2,1)S(1)}, u32[]{:S(2)}, u32[]{:S(2)}) collective-permute-start(bf16[256,256]{1,0:T(8,128)(2,1)S(1)} %get-tuple-element.76), channel_id=1, source_target_pairs={{0,2},{2,0},{4,6},{6,4},{8,10},{10,8},{12,14},{14,12},{16,18},{18,... | collective-permute-start | bytes 393224 | tf_op jit(solution)/shard_map/ppermute | solution.py:328
  32.6 0.0 collective-permute-done.7.received.refs_0_
  32.7 2.5 %collective-permute-start.9 = (bf16[144,256]{1,0:T(8,128)(2,1)S(1)}, bf16[144,256]{1,0:T(8,128)(2,1)S(1)}, u32[]{:S(2)}, u32[]{:S(2)}) collective-permute-start(bf16[144,256]{1,0:T(8,128)(2,1)S(1)} %merged.3.refs_2_), channel_id=1, source_target_pairs={{0,16},{2,18},{4,20},{6,22},{8,24},{10,26},{12,28},{14,30},{16,0},... | collective-permute-start | bytes 221192 | tf_op jit(solution)/shard_map/ppermute | solution.py:589
  35.2 0.8 %collective-permute-start.14 = (bf16[256,256]{1,0:T(8,128)(2,1)S(1)}, bf16[256,256]{1,0:T(8,128)(2,1)S(1)}, u32[]{:S(2)}, u32[]{:S(2)}) collective-permute-start(bf16[256,256]{1,0:T(8,128)(2,1)S(1)} %get-tuple-element.77), channel_id=1, source_target_pairs={{0,4},{2,6},{4,0},{6,2},{8,12},{10,14},{12,8},{14,10},{16,20},{18,... | collective-permute-start | bytes 393224 | tf_op jit(solution)/shard_map/ppermute | solution.py:328
  36.0 1.4 %collective-permute-start.15 = (bf16[256,256]{1,0:T(8,128)(2,1)S(1)}, bf16[256,256]{1,0:T(8,128)(2,1)S(1)}, u32[]{:S(2)}, u32[]{:S(2)}) collective-permute-start(bf16[256,256]{1,0:T(8,128)(2,1)S(1)} %get-tuple-element.63.refs_0_), channel_id=1, source_target_pairs={{0,6},{2,4},{4,2},{6,0},{8,14},{10,12},{12,10},{14,8},{16,22},{18,... | collective-permute-start | bytes 393224 | tf_op jit(solution)/shard_map/ppermute | solution.py:328
  37.4 4.5 %inner_terms.3 = (bf16[384,1024]{1,0:T(8,128)(2,1)S(1)}, f32[384,128]{1,0:T(8,128)S(1)}, f32[384,128]{1,0:T(8,128)S(1)}) custom-call(f32[32,384]{1,0:T(8,128)S(1)} %get-tuple-element.52.ld, bf16[384,128]{1,0:T(8,128)(2,1)S(1)} %get-tuple-element.47.refs_0_.b, bf16[384,128]{1,0:T(8,128)(2,1)S(1)} %get-tuple-element.48.refs_1_.c, ...), custom_call_target="tpu_custom_call" | custom-call | flops 1 | bytes 1 | tf_op jit(solution)/shard_map/inner_terms/pallas_call | solution.py:449
  41.9 0.0 collective-permute-done.9.refs_1_
  41.9 0.2 member_entries.3
  42.1 1.3 %collective-permute-start.10 = (bf16[256,256]{1,0:T(8,128)(2,1)S(1)}, bf16[256,256]{1,0:T(8,128)(2,1)S(1)}, u32[]{:S(2)}, u32[]{:S(2)}) collective-permute-start(bf16[256,256]{1,0:T(8,128)(2,1)S(1)} %get-tuple-element.67), channel_id=1, source_target_pairs={{0,2},{2,0},{4,6},{6,4},{8,10},{10,8},{12,14},{14,12},{16,18},{18,... | collective-permute-start | bytes 393224 | tf_op jit(solution)/shard_map/ppermute | solution.py:328
  43.5 0.8 %collective-permute-start.11 = (bf16[256,256]{1,0:T(8,128)(2,1)S(1)}, bf16[256,256]{1,0:T(8,128)(2,1)S(1)}, u32[]{:S(2)}, u32[]{:S(2)}) collective-permute-start(bf16[256,256]{1,0:T(8,128)(2,1)S(1)} %get-tuple-element.68), channel_id=1, source_target_pairs={{0,4},{2,6},{4,0},{6,2},{8,12},{10,14},{12,8},{14,10},{16,20},{18,... | collective-permute-start | bytes 393224 | tf_op jit(solution)/shard_map/ppermute | solution.py:328
  44.3 0.0 collective-permute-done.13.refs_1_
  44.3 1.4 %collective-permute-start.12 = (bf16[256,256]{1,0:T(8,128)(2,1)S(1)}, bf16[256,256]{1,0:T(8,128)(2,1)S(1)}, u32[]{:S(2)}, u32[]{:S(2)}) collective-permute-start(bf16[256,256]{1,0:T(8,128)(2,1)S(1)} %get-tuple-element.69.refs_4_), channel_id=1, source_target_pairs={{0,6},{2,4},{4,2},{6,0},{8,14},{10,12},{12,10},{14,8},{16,22},{18,... | collective-permute-start | bytes 393224 | tf_op jit(solution)/shard_map/ppermute | solution.py:328
  45.7 0.0 collective-permute-done.14.refs_2_
  45.7 0.0 collective-permute-done.15.refs_3_
  45.7 1.2 %entry_values.2 = (bf16[384,2048]{1,0:T(8,128)(2,1)}, f32[8,128]{1,0:T(8,128)S(1)}) custom-call(s32[1]{0:T(128)} %bitcast.where, bf16[384,1024]{1,0:T(8,128)(2,1)S(1)} %get-tuple-element.78.spread, bf16[384,128]{1,0:T(8,128)(2,1)S(1)} %get-tuple-element.47.refs_0_.b, bf16[384,1024]{1,0:T(8,128)(2,1)S(1)} %get-tuple-element.79.dx_local, ...), custom_call_target="tpu_custom_call" | custom-call | flops 1 | bytes 1 | tf_op jit(solution)/shard_map/entry_values/pallas_call | solution.py:530
  46.9 0.6 %entry_parts.2 = (f32[384,128]{1,0:T(8,128)S(1)}, f32[384,128]{1,0:T(8,128)S(1)}) custom-call(bf16[384,1024]{1,0:T(8,128)(2,1)S(1)} %get-tuple-element.72.x_scaled, bf16[384,1024]{1,0:T(8,128)(2,1)S(1)} %get-tuple-element.73.dy_scaled, f32[384,128]{1,0:T(8,128)S(1)} %get-tuple-element.74.db_before, f32[384,128]{1,0:T(8,128)S(1)} %get-tuple-element.65.refs_6_.dc_before, ...), custom_call_target="tpu_custom_call" | custom-call | flops 1 | bytes 1 | tf_op jit(solution)/shard_map/entry_parts/pallas_call | solution.py:496
  47.5 0.0 collective-permute-done.10.refs_1_
  47.5 0.9 %collective-permute-done.11.refs_2_ = bf16[256,256]{1,0:T(8,128)(2,1)S(1)} collective-permute-done((bf16[256,256]{1,0:T(8,128)(2,1)S(1)}, bf16[256,256]{1,0:T(8,128)(2,1)S(1)}, u32[]{:S(2)}, u32[]{:S(2)}) %collective-permute-start.11) | collective-permute-done | bytes 131104 | tf_op jit(solution)/shard_map/ppermute | solution.py:328
  48.4 1.7 %collective-permute-done.12.refs_3_ = bf16[256,256]{1,0:T(8,128)(2,1)S(1)} collective-permute-done((bf16[256,256]{1,0:T(8,128)(2,1)S(1)}, bf16[256,256]{1,0:T(8,128)(2,1)S(1)}, u32[]{:S(2)}, u32[]{:S(2)}) %collective-permute-start.12) | collective-permute-done | bytes 131104 | tf_op jit(solution)/shard_map/ppermute | solution.py:328
  50.2 0.6 %entry_parts.3.refs_4_ = bf16[768,128]{1,0:T(8,128)(2,1)S(1)} custom-call(bf16[384,1024]{1,0:T(8,128)(2,1)S(1)} %get-tuple-element.70.x_scaled, bf16[384,1024]{1,0:T(8,128)(2,1)S(1)} %get-tuple-element.71.dy_scaled, f32[384,128]{1,0:T(8,128)S(1)} %get-tuple-element.81.db_before, f32[384,128]{1,0:T(8,128)S(1)} %get-tuple-element.82.dc_before, ...), custom_call_target="tpu_custom_call" | custom-call | flops 1 | bytes 1 | tf_op jit(solution)/shard_map/entry_parts/pallas_call | solution.py:496
  50.8 0.1 collective-permute-start.16
  50.8 1.8 %entry_values.3 = (bf16[384,2048]{1,0:T(8,128)(2,1)}, f32[8,128]{1,0:T(8,128)}) custom-call(s32[1]{0:T(128)} %bitcast.where, bf16[384,1024]{1,0:T(8,128)(2,1)S(1)} %get-tuple-element.51.spread, bf16[384,128]{1,0:T(8,128)(2,1)S(1)} %get-tuple-element.47.refs_0_.b, bf16[384,1024]{1,0:T(8,128)(2,1)S(1)} %get-tuple-element.64.dx_local, ...), custom_call_target="tpu_custom_call", output_to_operand_aliasing={{0}: (9, {})} | custom-call | flops 1 | bytes 1 | tf_op jit(solution)/shard_map/entry_values/pallas_call | solution.py:530
  52.7 0.1 add_convert_fusion
  52.7 0.7 %fusion = (bf16[384,128]{1,0:T(8,128)(2,1)}, bf16[384,128]{1,0:T(8,128)(2,1)}) fusion(bf16[768,128]{1,0:T(8,128)(2,1)S(1)} %add_convert_fusion), kind=kLoop, calls=%fused_computation.1 | loop fusion | bytes 393216 | tf_op jit(solution)/shard_map/slice | solution.py:638
  (2 shorter events, 0.0 us)
Async XLA Ops:
  3.9 7.1 %collective-permute-start = (bf16[272,256]{1,0:T(8,128)(2,1)S(1)}, bf16[272,256]{1,0:T(8,128)(2,1)S(1)}, u32[]{:S(2)}, u32[]{:S(2)}) collective-permute-start(bf16[272,256]{1,0:T(8,128)(2,1)S(1)} %get-tuple-element.54), channel_id=1, source_target_pairs={{0,2},{2,0},{4,6},{6,4},{8,10},{10,8},{12,14},{14,12},{16,18},{18,... | collective-permute-start | bytes 417800 | tf_op jit(solution)/shard_map/ppermute | solution.py:328
  6.9 8.1 %collective-permute-start.1 = (bf16[272,256]{1,0:T(8,128)(2,1)S(1)}, bf16[272,256]{1,0:T(8,128)(2,1)S(1)}, u32[]{:S(2)}, u32[]{:S(2)}) collective-permute-start(bf16[272,256]{1,0:T(8,128)(2,1)S(1)} %get-tuple-element.55), channel_id=1, source_target_pairs={{0,4},{2,6},{4,0},{6,2},{8,12},{10,14},{12,8},{14,10},{16,20},{18,... | collective-permute-start | bytes 417800 | tf_op jit(solution)/shard_map/ppermute | solution.py:328
  8.4 6.6 %collective-permute-start.2 = (bf16[272,256]{1,0:T(8,128)(2,1)S(1)}, bf16[272,256]{1,0:T(8,128)(2,1)S(1)}, u32[]{:S(2)}, u32[]{:S(2)}) collective-permute-start(bf16[272,256]{1,0:T(8,128)(2,1)S(1)} %get-tuple-element.56), channel_id=1, source_target_pairs={{0,6},{2,4},{4,2},{6,0},{8,14},{10,12},{12,10},{14,8},{16,22},{18,... | collective-permute-start | bytes 417800 | tf_op jit(solution)/shard_map/ppermute | solution.py:328
  15.2 9.7 %collective-permute-start.6 = (bf16[272,256]{1,0:T(8,128)(2,1)S(1)}, bf16[272,256]{1,0:T(8,128)(2,1)S(1)}, u32[]{:S(2)}, u32[]{:S(2)}) collective-permute-start(bf16[272,256]{1,0:T(8,128)(2,1)S(1)} %totals.2.refs_0_.own), channel_id=1, source_target_pairs={{0,8},{2,10},{4,12},{6,14},{8,0},{10,2},{12,4},{14,6},{16,24},{18,... | collective-permute-start | bytes 417800 | tf_op jit(solution)/shard_map/ppermute | solution.py:589
  16.8 8.1 %collective-permute-start.3 = (bf16[272,256]{1,0:T(8,128)(2,1)S(1)}, bf16[272,256]{1,0:T(8,128)(2,1)S(1)}, u32[]{:S(2)}, u32[]{:S(2)}) collective-permute-start(bf16[272,256]{1,0:T(8,128)(2,1)S(1)} %get-tuple-element.61), channel_id=1, source_target_pairs={{0,2},{2,0},{4,6},{6,4},{8,10},{10,8},{12,14},{14,12},{16,18},{18,... | collective-permute-start | bytes 417800 | tf_op jit(solution)/shard_map/ppermute | solution.py:328
  18.0 7.0 %collective-permute-start.4 = (bf16[272,256]{1,0:T(8,128)(2,1)S(1)}, bf16[272,256]{1,0:T(8,128)(2,1)S(1)}, u32[]{:S(2)}, u32[]{:S(2)}) collective-permute-start(bf16[272,256]{1,0:T(8,128)(2,1)S(1)} %get-tuple-element.62), channel_id=1, source_target_pairs={{0,4},{2,6},{4,0},{6,2},{8,12},{10,14},{12,8},{14,10},{16,20},{18,... | collective-permute-start | bytes 417800 | tf_op jit(solution)/shard_map/ppermute | solution.py:328
  18.8 6.2 %collective-permute-start.5 = (bf16[272,256]{1,0:T(8,128)(2,1)S(1)}, bf16[272,256]{1,0:T(8,128)(2,1)S(1)}, u32[]{:S(2)}, u32[]{:S(2)}) collective-permute-start(bf16[272,256]{1,0:T(8,128)(2,1)S(1)} %get-tuple-element.57.refs_4_), channel_id=1, source_target_pairs={{0,6},{2,4},{4,2},{6,0},{8,14},{10,12},{12,10},{14,8},{16,22},{18,... | collective-permute-start | bytes 417800 | tf_op jit(solution)/shard_map/ppermute | solution.py:328
  25.1 7.5 %collective-permute-start.7 = (bf16[272,256]{1,0:T(8,128)(2,1)S(1)}, bf16[272,256]{1,0:T(8,128)(2,1)S(1)}, u32[]{:S(2)}, u32[]{:S(2)}) collective-permute-start(bf16[272,256]{1,0:T(8,128)(2,1)S(1)} %totals.3.refs_6_.own), channel_id=1, source_target_pairs={{0,8},{2,10},{4,12},{6,14},{8,0},{10,2},{12,4},{14,6},{16,24},{18,... | collective-permute-start | bytes 417800 | tf_op jit(solution)/shard_map/ppermute | solution.py:589
  25.6 5.4 %collective-permute-start.8 = (bf16[144,256]{1,0:T(8,128)(2,1)S(1)}, bf16[144,256]{1,0:T(8,128)(2,1)S(1)}, u32[]{:S(2)}, u32[]{:S(2)}) collective-permute-start(bf16[144,256]{1,0:T(8,128)(2,1)S(1)} %merged.2.refs_4_), channel_id=1, source_target_pairs={{0,16},{2,18},{4,20},{6,22},{8,24},{10,26},{12,28},{14,30},{16,0},... | collective-permute-start | bytes 221192 | tf_op jit(solution)/shard_map/ppermute | solution.py:589
  31.2 13.1 %collective-permute-start.13 = (bf16[256,256]{1,0:T(8,128)(2,1)S(1)}, bf16[256,256]{1,0:T(8,128)(2,1)S(1)}, u32[]{:S(2)}, u32[]{:S(2)}) collective-permute-start(bf16[256,256]{1,0:T(8,128)(2,1)S(1)} %get-tuple-element.76), channel_id=1, source_target_pairs={{0,2},{2,0},{4,6},{6,4},{8,10},{10,8},{12,14},{14,12},{16,18},{18,... | collective-permute-start | bytes 393224 | tf_op jit(solution)/shard_map/ppermute | solution.py:328
  32.7 9.2 %collective-permute-start.9 = (bf16[144,256]{1,0:T(8,128)(2,1)S(1)}, bf16[144,256]{1,0:T(8,128)(2,1)S(1)}, u32[]{:S(2)}, u32[]{:S(2)}) collective-permute-start(bf16[144,256]{1,0:T(8,128)(2,1)S(1)} %merged.3.refs_2_), channel_id=1, source_target_pairs={{0,16},{2,18},{4,20},{6,22},{8,24},{10,26},{12,28},{14,30},{16,0},... | collective-permute-start | bytes 221192 | tf_op jit(solution)/shard_map/ppermute | solution.py:589
  35.2 10.5 %collective-permute-start.14 = (bf16[256,256]{1,0:T(8,128)(2,1)S(1)}, bf16[256,256]{1,0:T(8,128)(2,1)S(1)}, u32[]{:S(2)}, u32[]{:S(2)}) collective-permute-start(bf16[256,256]{1,0:T(8,128)(2,1)S(1)} %get-tuple-element.77), channel_id=1, source_target_pairs={{0,4},{2,6},{4,0},{6,2},{8,12},{10,14},{12,8},{14,10},{16,20},{18,... | collective-permute-start | bytes 393224 | tf_op jit(solution)/shard_map/ppermute | solution.py:328
  36.0 9.7 %collective-permute-start.15 = (bf16[256,256]{1,0:T(8,128)(2,1)S(1)}, bf16[256,256]{1,0:T(8,128)(2,1)S(1)}, u32[]{:S(2)}, u32[]{:S(2)}) collective-permute-start(bf16[256,256]{1,0:T(8,128)(2,1)S(1)} %get-tuple-element.63.refs_0_), channel_id=1, source_target_pairs={{0,6},{2,4},{4,2},{6,0},{8,14},{10,12},{12,10},{14,8},{16,22},{18,... | collective-permute-start | bytes 393224 | tf_op jit(solution)/shard_map/ppermute | solution.py:328
  42.1 5.4 %collective-permute-start.10 = (bf16[256,256]{1,0:T(8,128)(2,1)S(1)}, bf16[256,256]{1,0:T(8,128)(2,1)S(1)}, u32[]{:S(2)}, u32[]{:S(2)}) collective-permute-start(bf16[256,256]{1,0:T(8,128)(2,1)S(1)} %get-tuple-element.67), channel_id=1, source_target_pairs={{0,2},{2,0},{4,6},{6,4},{8,10},{10,8},{12,14},{14,12},{16,18},{18,... | collective-permute-start | bytes 393224 | tf_op jit(solution)/shard_map/ppermute | solution.py:328
  43.5 5.0 %collective-permute-start.11 = (bf16[256,256]{1,0:T(8,128)(2,1)S(1)}, bf16[256,256]{1,0:T(8,128)(2,1)S(1)}, u32[]{:S(2)}, u32[]{:S(2)}) collective-permute-start(bf16[256,256]{1,0:T(8,128)(2,1)S(1)} %get-tuple-element.68), channel_id=1, source_target_pairs={{0,4},{2,6},{4,0},{6,2},{8,12},{10,14},{12,8},{14,10},{16,20},{18,... | collective-permute-start | bytes 393224 | tf_op jit(solution)/shard_map/ppermute | solution.py:328
  44.3 5.9 %collective-permute-start.12 = (bf16[256,256]{1,0:T(8,128)(2,1)S(1)}, bf16[256,256]{1,0:T(8,128)(2,1)S(1)}, u32[]{:S(2)}, u32[]{:S(2)}) collective-permute-start(bf16[256,256]{1,0:T(8,128)(2,1)S(1)} %get-tuple-element.69.refs_4_), channel_id=1, source_target_pairs={{0,6},{2,4},{4,2},{6,0},{8,14},{10,12},{12,10},{14,8},{16,22},{18,... | collective-permute-start | bytes 393224 | tf_op jit(solution)/shard_map/ppermute | solution.py:328
  50.8 1.9 %collective-permute-start.16 = (bf16[768,128]{1,0:T(8,128)(2,1)S(1)}, bf16[768,128]{1,0:T(8,128)(2,1)S(1)}, u32[]{:S(2)}, u32[]{:S(2)}) collective-permute-start(bf16[768,128]{1,0:T(8,128)(2,1)S(1)} %entry_parts.3.refs_4_), channel_id=1, source_target_pairs={{0,1},{1,0},{2,3},{3,2},{4,5},{5,4},{6,7},{7,6},{8,9},{9,8},{10,11... | collective-permute-start | bytes 589832 | tf_op jit(solution)/shard_map/ppermute | solution.py:554

commit v6 on v5

--- a/solution.py
+++ b/solution.py
@@ -69,8 +69,7 @@
 
 
 def cost(flops, size, transcendentals=0):
-    del flops, size, transcendentals
-    return pl.CostEstimate(flops=1, bytes_accessed=1, transcendentals=0)
+    return pl.CostEstimate(flops=flops, bytes_accessed=size, transcendentals=transcendentals)
 
 
 def place_of(where):
@@ -203,6 +202,10 @@
     ref[first:, :] = both.astype(BF16)
 
 
+def sent_order(parts):
+    return [parts[0], *parts[:0:-1]]
+
+
 def in_order(group, forward):
     return list(range(group)) if forward else list(range(group - 1, -1, -1))
 
@@ -213,7 +216,7 @@
 
 def totals_kernel(state, where, *refs):
     group = GROUP
-    blocks, out = refs[:group], refs[-1]
+    blocks, out = sent_order(refs[:group]), refs[-1]
     for here in range(group):
 
         @pl.when(place_of(where) == here)
@@ -240,7 +243,7 @@
         compiler_params=params(4),
         cost_estimate=cost(8 * blocks[0].size, 10 * blocks[0].size),
         name="totals",
-    )(where, *blocks, *after)
+    )(where, *sent_order(blocks), *after)
 
 
 def merged_kernel(state, level, last, where, own, received, *refs):
@@ -324,7 +327,7 @@
 def exchange(parts):
     count = lax.axis_size("seq")
     out = list(parts)
-    for k in sorted(range(1, len(parts)), key=lambda k: (-bin(k).count("1"), k)):
+    for k in range(len(parts) - 1, 0, -1):
         out[k] = lax.ppermute(parts[k], "seq", [(s, s ^ k) for s in range(count)])
     return out
 
@@ -340,140 +343,164 @@
     )
 
 
-def inner_kernel(head_dim, chunk, n_before, n_after, ld, b, c, x_all, dy_all, *refs):
-    before, refs = refs[:n_before], refs[n_before + n_after :]
-    dx_out, db_out, dc_out, x, dy, cum_terms, *scratch = refs
+def grouped_cuts(pieces):
+    groups = {}
+    for cut in split_pairs(0, pieces):
+        groups.setdefault((cut[1] - cut[0], cut[2] - cut[1]), []).append(cut)
+    return list(groups.items())
+
+
+def rows_of(first, end, piece):
+    return slice(first * piece, end * piece)
+
+
+def setup_kernel(piece, ld, b, c, *refs):
+    near, cum_terms = refs[-2:]
+    heads, length = ld.shape
+    rows, other = iota((length, length), 0), iota((length, length), 1)
+    mask = jnp.where(other <= rows, 1.0, 0.0).astype(BF16)
+    cum = summed(mask, three(ld[...] * LOG2E))
+    lane = iota(cum.shape, 1)
+    in_slots = jnp.where(lane < SLOT, cum, 0.0)
+    in_slots = in_slots + pltpu.roll(in_slots, SLOT, 1) + pltpu.roll(in_slots, 2 * SLOT, 1)
+    high, mid, low = three(in_slots)
+    cum_terms[...] = jnp.where(lane < SLOT, high, jnp.where(lane < 2 * SLOT, mid, low))
+    keep = iota((piece, piece), 0) <= iota((piece, piece), 1)
+    pieces = length // piece
+    for n in range(pieces):
+        here = rows_of(n, n + 1, piece)
+        near[here, :] = jnp.where(keep, dot(b[here, :], c[here, :], NT), 0.0).astype(BF16)
+    cuts = [cut for _, same in grouped_cuts(pieces) for cut in same]
+    for (lo, mid_, hi), far in zip(cuts, refs):
+        left, right = rows_of(lo, mid_, piece), rows_of(mid_, hi, piece)
+        far[...] = dot(b[left, :], c[right, :], NT).astype(BF16)
+
+
+def inner_setup(piece, ld, b, c, after):
+    length = b.shape[0]
+    cuts = [cut for _, same in grouped_cuts(length // piece) for cut in same]
+    outs = [
+        jax.ShapeDtypeStruct(((mid - lo) * piece, (hi - mid) * piece), BF16) for lo, mid, hi in cuts
+    ]
+    outs.append(jax.ShapeDtypeStruct((length, piece), BF16))
+    outs.append(jax.ShapeDtypeStruct((length, LANES), BF16))
+    return pl.pallas_call(
+        functools.partial(setup_kernel_after, piece, len(after)),
+        out_shape=outs,
+        in_specs=whole(3) + [ANY] * len(after),
+        out_specs=whole(len(outs)),
+        compiler_params=params(4),
+        cost_estimate=cost(8 * b.size * length, 8 * b.size),
+        name="inner_setup",
+    )(ld, b, c, *after)
+
+
+def setup_kernel_after(piece, n_after, ld, b, c, *refs):
+    setup_kernel(piece, ld, b, c, *refs[n_after:])
+
+
+def inner_kernel(head_dim, chunk, n_before, n_after, b, c, x, dy, *refs):
     length, width = x.shape
     piece = head_dim
     pieces = length // piece
-    cuts = split_pairs(0, pieces)
-    near, near_sum, dx = scratch[:3]
-    far, far_sum = scratch[3 : 3 + len(cuts)], scratch[3 + len(cuts) :]
-    per_tile = LANES // head_dim
-    step = pl.program_id(0)
-    owned = (step * chunk_count(x_all.shape[1]) + chunk) * width
-    columns = pl.ds(pl.multiple_of(owned, width), width)
-    x[...] = x_all[:, columns]
-    dy[...] = dy_all[:, columns]
-
-    @pl.when(step == 0)
-    def _():
-        rows, other = iota((length, length), 0), iota((length, length), 1)
-        mask = jnp.where(other <= rows, 1.0, 0.0).astype(BF16)
-        cum_small = summed(mask, three(ld[...] * LOG2E))
-        lane = iota(cum_small.shape, 1)
-        in_slots = jnp.where(lane < SLOT, cum_small, 0.0)
-        in_slots = (
-            in_slots + pltpu.roll(in_slots, SLOT, 1) + pltpu.roll(in_slots, 2 * SLOT, 1)
-        )
-        high, mid, low = three(in_slots)
-        cum_terms[...] = jnp.where(lane < SLOT, high, jnp.where(lane < 2 * SLOT, mid, low))
-        keep = iota((piece, LANES), 0) <= lax.rem(iota((piece, LANES), 1), piece)
+    groups = grouped_cuts(pieces)
+    n_cuts = sum(len(same) for _, same in groups)
+    fars, (near, cum_terms), refs = refs[:n_cuts], refs[n_cuts : n_cuts + 2], refs[n_cuts + 2 :]
+    before, refs = refs[:n_before], refs[n_before + n_after :]
+    dx_out, db_out, dc_out, x_near, dy_near, *scratch = refs
+    lefts, rights = scratch[: len(groups)], scratch[len(groups) :]
+    part = dx_out.shape[1] // GROUP
+
+    for m in range(GROUP):
+        owned = m * (width // GROUP) + chunk * part
+        lanes, here = slice(owned, owned + part), slice(m * part, (m + 1) * part)
+        shape = (LANES, part)
+        owner = owned // head_dim + iota(shape, 1) // head_dim
+        slot = lax.rem(iota(shape, 0), SLOT) == owner
+        hot = jnp.where(slot & (iota(shape, 0) < 3 * SLOT), 1.0, 0.0).astype(BF16)
+        cum = dot(cum_terms[...], hot, NN)
+        dx = []
         for n in range(pieces):
-            rows_n = slice(n * piece, (n + 1) * piece)
-            doubled = jnp.concatenate([c[rows_n, :]] * per_tile, axis=0)
-            near[rows_n, :] = jnp.where(keep, dot(b[rows_n, :], doubled, NT), 0.0)
-        near_sum[...] = jnp.zeros_like(near_sum)
-        for (lo, mid_, hi), f, total in zip(cuts, far, far_sum):
-            left, right = slice(lo * piece, mid_ * piece), slice(mid_ * piece, hi * piece)
-            f[...] = dot(b[left, :], c[right, :], NT).astype(BF16)
-            total[...] = jnp.zeros_like(total)
-
-    shape = (LANES, width)
-    owner = owned // head_dim + iota(shape, 1) // head_dim
-    slot = lax.rem(iota(shape, 0), SLOT) == owner
-    hot = jnp.where(slot & (iota(shape, 0) < 3 * SLOT), 1.0, 0.0).astype(BF16)
-    cum = dot(cum_terms[...], hot, NN)
-    tile = (piece, LANES)
-    diagonal = iota(tile, 0) == lax.rem(iota(tile, 1), piece)
-    part_of_lane = iota(tile, 1) // head_dim
-    for n in range(pieces):
-        rows_n = slice(n * piece, (n + 1) * piece)
-        total = near_sum[rows_n, :]
-        scores = near[rows_n, :]
-        for t in range(width // LANES):
-            lanes = slice(t * LANES, (t + 1) * LANES)
-            col = cum[rows_n, lanes]
-            row = jnp.sum(jnp.where(diagonal, col, 0.0), axis=0, keepdims=True)
-            decays = jnp.exp2(jnp.minimum(row - col, 0.0))
-            dy_t = dy[rows_n, lanes]
-            stacked = jnp.concatenate(
-                [jnp.where(part_of_lane == h, dy_t, jnp.zeros_like(dy_t)) for h in range(per_tile)],
-                axis=0,
-            )
-            dx[rows_n, lanes] = dot((scores * decays).astype(BF16), stacked, NN)
-            total = total + decays * dot(x[rows_n, lanes], stacked, NT)
-        near_sum[rows_n, :] = total
-    for (lo, mid_, hi), f, total in zip(cuts, far, far_sum):
-        left, right = slice(lo * piece, mid_ * piece), slice(mid_ * piece, hi * piece)
-        edge = cum[mid_ * piece - 1 : mid_ * piece, :]
-        to_edge = jnp.exp2(edge - cum[left, :])
-        from_edge = jnp.exp2(cum[right, :] - edge)
-        x_edge = (x[left, :].astype(F32) * to_edge).astype(BF16)
-        dy_edge = (dy[right, :].astype(F32) * from_edge).astype(BF16)
-        dx[left, :] += to_edge * dot(f[...], dy_edge, NN)
-        total[...] += dot(x_edge, dy_edge, NT)
-    lanes = pl.ds(pl.multiple_of(step * width, width), width)
-    dx_out[:, lanes] = dx[...].astype(BF16)
-
-    @pl.when(step == pl.num_programs(0) - 1)
-    def _():
-        keep = (iota(tile, 0) <= iota(tile, 1)) & (part_of_lane == 0)
+            rows = rows_of(n, n + 1, piece)
+            middle = cum[n * piece + piece // 2 : n * piece + piece // 2 + 1, :]
+            gap = middle - cum[rows, :]
+            down, up = jnp.exp2(gap), jnp.exp2(-gap)
+            x_near[rows, here] = (x[rows, lanes].astype(F32) * down).astype(BF16)
+            dy_piece = (dy[rows, lanes].astype(F32) * up).astype(BF16)
+            dy_near[rows, here] = dy_piece
+            dx.append(down * dot(near[rows, :], dy_piece, NN))
+        far_of = iter(fars)
+        for (_, same), left_ref, right_ref in zip(groups, lefts, rights):
+            for g, (lo, mid, hi) in enumerate(same):
+                left, right = rows_of(lo, mid, piece), rows_of(mid, hi, piece)
+                edge = cum[mid * piece - 1 : mid * piece, :]
+                to_edge = jnp.exp2(edge - cum[left, :])
+                from_edge = jnp.exp2(cum[right, :] - edge)
+                x_left = (x[left, lanes].astype(F32) * to_edge).astype(BF16)
+                dy_right = (dy[right, lanes].astype(F32) * from_edge).astype(BF16)
+                left_ref[rows_of(g, g + 1, (mid - lo) * piece), here] = x_left
+                right_ref[rows_of(g, g + 1, (hi - mid) * piece), here] = dy_right
+                far = to_edge * dot(next(far_of)[...], dy_right, NN)
+                for n in range(lo, mid):
+                    dx[n] = dx[n] + far[rows_of(n - lo, n - lo + 1, piece), :]
         for n in range(pieces):
-            rows_n = slice(n * piece, (n + 1) * piece)
-            total = near_sum[rows_n, :]
-            total = sum(
-                [pltpu.roll(total, h * head_dim, 1) for h in range(1, per_tile)], total
-            )
-            weighted = jnp.where(keep, total, 0.0).astype(BF16)
-            doubled = jnp.concatenate([c[rows_n, :]] * per_tile, axis=0)
-            db = dot(weighted, doubled, NN)
-            dc = dot(weighted, b[rows_n, :], TN)[:piece, :]
-            if before:
-                db, dc = db + before[0][rows_n, :], dc + before[1][rows_n, :]
-            db_out[rows_n, :] = db
-            dc_out[rows_n, :] = dc
-        for (lo, mid_, hi), total in zip(cuts, far_sum):
-            left, right = slice(lo * piece, mid_ * piece), slice(mid_ * piece, hi * piece)
-            weighted = total[...].astype(BF16)
-            db_out[left, :] += dot(weighted, c[right, :], NN)
-            dc_out[right, :] += dot(weighted, b[left, :], TN)
-
-
-def inner_terms(head_dim, group, chunk, ld, b, c, x, dy, before, after):
+            dx_out[rows_of(n, n + 1, piece), here] = dx[n].astype(BF16)
+
+    if before:
+        db_out[...] = before[0][...]
+        dc_out[...] = before[1][...]
+    else:
+        db_out[...] = jnp.zeros_like(db_out)
+        dc_out[...] = jnp.zeros_like(dc_out)
+    batch = 4
+    for first in range(0, pieces, batch):
+        rows = rows_of(first, min(first + batch, pieces), piece)
+        total = dot(x_near[rows, :], dy_near[rows, :], NT)
+        row, col = iota(total.shape, 0), iota(total.shape, 1)
+        keep = (row // piece == col // piece) & (row <= col)
+        weighted = jnp.where(keep, total, 0.0).astype(BF16)
+        db_out[rows, :] += dot(weighted, c[rows, :], NN)
+        dc_out[rows, :] += dot(weighted, b[rows, :], TN)
+    for ((n_left, n_right), same), left_ref, right_ref in zip(groups, lefts, rights):
+        total = dot(left_ref[...], right_ref[...], NT)
+        if len(same) > 1:
+            row, col = iota(total.shape, 0), iota(total.shape, 1)
+            total = jnp.where(row // (n_left * piece) == col // (n_right * piece), total, 0.0)
+        weighted = total.astype(BF16)
+        b_left = jnp.concatenate([b[rows_of(lo, mid, piece), :] for lo, mid, _ in same], axis=0)
+        c_right = jnp.concatenate([c[rows_of(mid, hi, piece), :] for _, mid, hi in same], axis=0)
+        db = dot(weighted, c_right, NN)
+        dc = dot(weighted, b_left, TN)
+        for g, (lo, mid, hi) in enumerate(same):
+            db_out[rows_of(lo, mid, piece), :] += db[rows_of(g, g + 1, n_left * piece), :]
+            dc_out[rows_of(mid, hi, piece), :] += dc[rows_of(g, g + 1, n_right * piece), :]
+
+
+def inner_terms(head_dim, chunk, setup, b, c, x, dy, before, after):
     length, state = b.shape
-    part = x.shape[1] // (group * chunk_count(x.shape[1]))
-    piece = head_dim
-    cuts = split_pairs(0, length // piece)
-    sizes = [((mid - lo) * piece, (hi - mid) * piece) for lo, mid, hi in cuts]
+    columns = x.shape[1] // chunk_count(x.shape[1])
+    groups = grouped_cuts(length // head_dim)
+    sizes = [[len(same) * n * head_dim for n in halves] for halves, same in groups]
     return pl.pallas_call(
         functools.partial(inner_kernel, head_dim, chunk, len(before), len(after)),
-        grid=(group,),
         out_shape=[
-            pltpu.VMEM((length, group * part), BF16),
-            pltpu.VMEM((length, state), F32),
-            pltpu.VMEM((length, state), F32),
+            jax.ShapeDtypeStruct((length, columns), BF16),
+            jax.ShapeDtypeStruct((length, state), F32),
+            jax.ShapeDtypeStruct((length, state), F32),
         ],
-        in_specs=whole(5 + len(before)) + [ANY] * len(after),
+        in_specs=whole(4 + len(setup) + len(before)) + [ANY] * len(after),
         out_specs=whole(3),
-        scratch_shapes=[
-            pltpu.VMEM((length, part), BF16),
-            pltpu.VMEM((length, part), BF16),
-            pltpu.VMEM((length, LANES), BF16),
-            pltpu.VMEM((length, LANES), F32),
-            pltpu.VMEM((length, LANES), F32),
-            pltpu.VMEM((length, part), F32),
-        ]
-        + [pltpu.VMEM(s, BF16) for s in sizes]
-        + [pltpu.VMEM(s, F32) for s in sizes],
+        scratch_shapes=[pltpu.VMEM((length, columns), BF16)] * 2
+        + [pltpu.VMEM((left, columns), BF16) for left, _ in sizes]
+        + [pltpu.VMEM((right, columns), BF16) for _, right in sizes],
         compiler_params=params(16),
         cost_estimate=cost(8 * x.size * state, 4 * x.size, 2 * x.size),
         name="inner_terms",
-    )(ld, b, c, x, dy, *before, *after)
+    )(b, c, x, dy, *setup, *before, *after)
 
 
 def parts_kernel(last, x_scaled, dy_scaled, db_before, dc_before, *refs):
-    entries, outs = refs[:GROUP], refs[-1 if last else -2 :]
+    entries, outs = sent_order(refs[:GROUP]), refs[-1 if last else -2 :]
     length, state = db_before.shape
     part = entries[0].shape[1]
     db, dc = db_before[...], dc_before[...]
@@ -501,11 +528,11 @@
         compiler_params=params(8),
         cost_estimate=cost(4 * x_scaled.size * state, 4 * x_scaled.size),
         name="entry_parts",
-    )(x_scaled, dy_scaled, db_before, dc_before, *entries, *after)
+    )(x_scaled, dy_scaled, db_before, dc_before, *sent_order(entries), *after)
 
 
 def values_kernel(chunk, where, spread, b, dx_local, *refs):
-    entries, (out, done, dx, sems) = refs[:GROUP], refs[-4:]
+    entries, (out, done, dx, sems) = sent_order(refs[:GROUP]), refs[-4:]
     done[...] = jnp.zeros_like(done)
     state, part = b.shape[1], entries[0].shape[1]
     stores = []
@@ -526,12 +553,12 @@
     group, part = len(entries), entries[0].shape[1]
     length, state = b.shape
     size = dx_local.size
-    operands = [where, spread, b, dx_local, *entries, *after, *before]
+    operands = [where, spread, b, dx_local, *sent_order(entries), *after, *before]
     return pl.pallas_call(
         functools.partial(values_kernel, chunk),
         out_shape=[
             pltpu.HBM((length, chunks * group * part), BF16),
-            jax.ShapeDtypeStruct((8, LANES), F32),
+            pltpu.VMEM((8, LANES), F32),
         ],
         in_specs=[SMEM] + whole(3 + group) + [ANY] * len(after) + [HBM] * len(before),
         out_specs=[HBM, *whole(1)],
@@ -563,77 +590,40 @@
     levels = (count // group).bit_length() - 1
     where = lax.axis_index("seq").astype(jnp.int32)[None]
     inputs = (log_decay, b_inputs, c_inputs, token_values, grad_out)
-    order = []
-
-    def then(result):
-        order[:] = [result[-1] if isinstance(result, (list, tuple)) else result]
-        return result
-
-    ld, b, c, x, dy, *rest = then(first_states(head_dim, group, where, inputs))
+    ld, b, c, x, dy, *rest = first_states(head_dim, group, where, inputs)
     factors, states = rest[:3], [rest[3:]]
     blocks = [exchange(states[0][3:])]
     for chunk in range(1, chunks):
-        states.append(then(next_states(head_dim, group, chunk, where, factors, b, c, x, dy)))
+        states.append(next_states(head_dim, group, chunk, where, factors, b, c, x, dy))
         blocks.append(exchange(states[chunk][3:]))
-
-    sums, inner = [], []
-
-    def add_inner():
-        if len(inner) < chunks:
-            n = len(inner)
-            inner.append(then(inner_terms(head_dim, group, n, ld, b, c, x, dy, sums, order)))
-            sums[:] = inner[n][1:]
+    setup = inner_setup(head_dim, ld, b, c, [states[-1][3]])
 
     def to_level(block, level):
         step = group << level
         return lax.ppermute(block, "seq", [(s, s ^ step) for s in range(count)])
 
-    own, received, entries = [None] * chunks, [[] for _ in range(chunks)], []
-
-    def open_rounds(chunk):
-        own[chunk] = then(totals(state, where, blocks[chunk], order))
-        received[chunk].append(to_level(own[chunk], 0))
-
-    def close_rounds(chunk):
-        found = then(member_entries(state, where, blocks[chunk], received[chunk], order))
-        entries.append(exchange(found))
-
-    open_rounds(0)
+    entries, inner, sums = [], [], []
     for chunk in range(chunks):
-        if chunk == 0:
-            add_inner()
+        own = totals(state, where, blocks[chunk], setup[-1:] if chunk == 0 else [])
+        received = [to_level(own, 0)]
         for level in range(levels - 1):
             last = level == levels - 2
-            arrived = received[chunk][level]
-            own[chunk] = then(merged(state, level, last, where, own[chunk], arrived, order))
-            received[chunk].append(to_level(own[chunk], level + 1))
-        if chunk + 1 < chunks:
-            open_rounds(chunk + 1)
-        else:
-            add_inner()
-        close_rounds(chunk)
-    while len(inner) < chunks:
-        add_inner()
-
-    grad_values = []
+            own = merged(state, level, last, where, own, received[level], [])
+            received.append(to_level(own, level + 1))
+        inner.append(inner_terms(head_dim, chunk, setup, b, c, x, dy, sums, [own]))
+        sums = list(inner[chunk][1:])
+        found = member_entries(state, where, blocks[chunk], received, sums[:1])
+        entries.append(exchange(found))
+
+    grad_values, done = [], []
     for chunk in range(chunks):
         x_scaled, dy_scaled, spread = states[chunk][:3]
         last = chunk == chunks - 1
-
-        def values():
-            local = inner[chunk][0]
-            out = entry_values(
-                chunk, chunks, where, spread, b, local, entries[chunk], grad_values, order
-            )
-            grad_values[:] = then(out)[:1]
-
-        if not last:
-            values()
-        sums = then(
-            entry_parts(last, x_scaled, dy_scaled, *sums, entries[chunk], [] if last else order)
+        sums = entry_parts(last, x_scaled, dy_scaled, *sums, entries[chunk], done)
+        *grad_values, token = entry_values(
+            chunk, chunks, where, spread, b, inner[chunk][0], entries[chunk], grad_values, []
         )
-        if last:
-            values()
+        done = [token]
     both = over_heads(sums[0])
     return grad_values[0], both[:length], both[length:]
 

time: 54.4 us -> 50 us (0.919); the launches traced: 53.4 us -> 49.8 us
  waiting for transfers between devices: 10.5 us -> 7.2 us
  Pallas kernels: 18.7 us -> 17.2 us
  starting transfers between devices: 22.6 us -> 23.9 us
    ppermute x4, waiting for transfers between devices: 2.78 us -> 0.01 us  [to_level(): return lax.ppermute(block, 'seq', [(s, s ^ step) for s in range(count)])]
    pallas_call x2, Pallas kernels: 9.02 us -> 7.03 us  [inner_terms(): pl.pallas_call(functools.partial(inner_kernel, head_dim, chunk, len(befor...]
    ppermute x12, starting transfers between devices: 15.2 us -> 16 us  [exchange(): out[k] = lax.ppermute(parts[k], 'seq', [(s, s ^ k) for s in range(count)])]
    ppermute x12, waiting for transfers between devices: 7.76 us -> 7.18 us  [exchange(): out[k] = lax.ppermute(parts[k], 'seq', [(s, s ^ k) for s in range(count)])]
  transfers between devices with their start and end apart: 17 -> 17, of which waited for: 6 -> 7; matrix products, arithmetic and copies ran while one was open for 0% -> 0% of each run, Pallas kernels for 27% -> 27%
where the time goes in v6:
time: 50 us; the launch traced here: 49.8 us
  starting transfers between devices  23.9 us (48%)
  Pallas kernels  17.2 us (34%)
  waiting for transfers between devices  7.2 us (14%)
  between operations  0.8 us (2%)
  local copies, waits for them, and re-layouts  0.69 us (1%)
    ppermute x12, starting transfers between devices, exchange(): out[k] = lax.ppermute(parts[k], 'seq', [(s, s ^ k) for s in range(count)])  16 us
    ppermute x4, starting transfers between devices, to_level(): return lax.ppermute(block, 'seq', [(s, s ^ step) for s in range(count)])  7.77 us
    ppermute x12, waiting for transfers between devices, exchange(): out[k] = lax.ppermute(parts[k], 'seq', [(s, s ^ k) for s in range(count)])  7.18 us
    pallas_call x2, Pallas kernels, inner_terms(): pl.pallas_call(functools.partial(inner_kernel, head_dim, chunk, len(befor...  7.03 us
    pallas_call x1, Pallas kernels, first_states(): pl.pallas_call(functools.partial(first_states_kernel, head_dim, group), o...  3.26 us
    pallas_call x2, Pallas kernels, entry_values(): pl.pallas_call(functools.partial(values_kernel, chunk), out_shape=[pltpu....  3.02 us
    pallas_call x1, Pallas kernels, next_states(): pl.pallas_call(functools.partial(next_states_kernel, head_dim, chunk), ou...  1.58 us
    pallas_call x2, Pallas kernels, entry_parts(): pl.pallas_call(functools.partial(parts_kernel, last), out_shape=outs, in_...  1.16 us
  transfers between devices with their start and end apart: 17, of which 7 were waited for; matrix products, arithmetic and copies ran while one was open for 0% of the time, Pallas kernels for 27%

profile of v6, /device:TPU:0, one launch (start us, length us, event | category | flops | bytes accessed | tf_op | source)
XLA Modules:
  0.0 49.8 jit_solution(13975359655490269116)
XLA Ops:
  0.6 3.3 %first_states.1 = (f32[32,384]{1,0:T(8,128)S(1)}, bf16[384,128]{1,0:T(8,128)(2,1)S(1)}, bf16[384,128]{1,0:T(8,128)(2,1)S(1)}, bf16[384,2048]{1,0:T(8,128)(2,1)S(...) custom-call(s32[1]{0:T(128)} %bitcast.where, ...), custom_call_target="tpu_custom_call" | custom-call | flops 402653184 | bytes 6291456 | tf_op jit(solution)/shard_map/first_states/pallas_call | solution.py:167
  3.9 4.0 %collective-permute-start = (bf16[272,256]{1,0:T(8,128)(2,1)S(1)}, bf16[272,256]{1,0:T(8,128)(2,1)S(1)}, u32[]{:S(2)}, u32[]{:S(2)}) collective-permute-start(bf16[272,256]{1,0:T(8,128)(2,1)S(1)} %get-tuple-element.69), channel_id=1, source_target_pairs={{0,6},{2,4},{4,2},{6,0},{8,14},{10,12},{12,10},{14,8},{16,22},{18,... | collective-permute-start | bytes 417800 | tf_op jit(solution)/shard_map/ppermute | solution.py:331
  7.9 0.5 %collective-permute-start.1 = (bf16[272,256]{1,0:T(8,128)(2,1)S(1)}, bf16[272,256]{1,0:T(8,128)(2,1)S(1)}, u32[]{:S(2)}, u32[]{:S(2)}) collective-permute-start(bf16[272,256]{1,0:T(8,128)(2,1)S(1)} %get-tuple-element.70), channel_id=1, source_target_pairs={{0,4},{2,6},{4,0},{6,2},{8,12},{10,14},{12,8},{14,10},{16,20},{18,... | collective-permute-start | bytes 417800 | tf_op jit(solution)/shard_map/ppermute | solution.py:331
  8.4 0.1 collective-permute-start.2
  8.5 1.6 %next_states.1 = (bf16[384,1024]{1,0:T(8,128)(2,1)S(1)}, bf16[384,1024]{1,0:T(8,128)(2,1)S(1)}, bf16[384,1024]{1,0:T(8,128)(2,1)S(1)}, bf16[272,256]{1,0:T(8,128...) custom-call(s32[1]{0:T(128)} %bitcast.where, ...), custom_call_target="tpu_custom_call" | custom-call | flops 402653184 | bytes 3145728 | tf_op jit(solution)/shard_map/next_states/pallas_call | solution.py:182
  10.1 2.9 %collective-permute-start.4 = (bf16[272,256]{1,0:T(8,128)(2,1)S(1)}, bf16[272,256]{1,0:T(8,128)(2,1)S(1)}, u32[]{:S(2)}, u32[]{:S(2)}) collective-permute-start(bf16[272,256]{1,0:T(8,128)(2,1)S(1)} %get-tuple-element.74), channel_id=1, source_target_pairs={{0,6},{2,4},{4,2},{6,0},{8,14},{10,12},{12,10},{14,8},{16,22},{18,... | collective-permute-start | bytes 417800 | tf_op jit(solution)/shard_map/ppermute | solution.py:331
  13.0 0.5 %collective-permute-start.5 = (bf16[272,256]{1,0:T(8,128)(2,1)S(1)}, bf16[272,256]{1,0:T(8,128)(2,1)S(1)}, u32[]{:S(2)}, u32[]{:S(2)}) collective-permute-start(bf16[272,256]{1,0:T(8,128)(2,1)S(1)} %get-tuple-element.75), channel_id=1, source_target_pairs={{0,4},{2,6},{4,0},{6,2},{8,12},{10,14},{12,8},{14,10},{16,20},{18,... | collective-permute-start | bytes 417800 | tf_op jit(solution)/shard_map/ppermute | solution.py:331
  13.5 0.0 collective-permute-done.refs_1_.refs_5_
  13.5 0.9 %collective-permute-start.6 = (bf16[272,256]{1,0:T(8,128)(2,1)S(1)}, bf16[272,256]{1,0:T(8,128)(2,1)S(1)}, u32[]{:S(2)}, u32[]{:S(2)}) collective-permute-start(bf16[272,256]{1,0:T(8,128)(2,1)S(1)} %get-tuple-element.76), channel_id=1, source_target_pairs={{0,2},{2,0},{4,6},{6,4},{8,10},{10,8},{12,14},{14,12},{16,18},{18,... | collective-permute-start | bytes 417800 | tf_op jit(solution)/shard_map/ppermute | solution.py:331
  14.4 0.5 inner_setup.1
  14.8 1.2 %collective-permute-done.1.refs_2_.refs_4_ = bf16[272,256]{1,0:T(8,128)(2,1)S(1)} collective-permute-done((bf16[272,256]{1,0:T(8,128)(2,1)S(1)}, bf16[272,256]{1,0:T(8,128)(2,1)S(1)}, u32[]{:S(2)}, u32[]{:S(2)}) %collective-permute-start.1) | collective-permute-done | bytes 139296 | tf_op jit(solution)/shard_map/ppermute | solution.py:331
  16.0 0.0 collective-permute-done.2.refs_3_
  16.1 0.1 totals.2.own
  16.2 1.6 %collective-permute-start.3 = (bf16[272,256]{1,0:T(8,128)(2,1)S(1)}, bf16[272,256]{1,0:T(8,128)(2,1)S(1)}, u32[]{:S(2)}, u32[]{:S(2)}) collective-permute-start(bf16[272,256]{1,0:T(8,128)(2,1)S(1)} %totals.2.own), channel_id=1, source_target_pairs={{0,8},{2,10},{4,12},{6,14},{8,0},{10,2},{12,4},{14,6},{16,24},{18,... | collective-permute-start | bytes 417800 | tf_op jit(solution)/shard_map/ppermute | solution.py:603
  17.8 1.1 %collective-permute-done.4.refs_1_.refs_5_ = bf16[272,256]{1,0:T(8,128)(2,1)S(1)} collective-permute-done((bf16[272,256]{1,0:T(8,128)(2,1)S(1)}, bf16[272,256]{1,0:T(8,128)(2,1)S(1)}, u32[]{:S(2)}, u32[]{:S(2)}) %collective-permute-start.4) | collective-permute-done | bytes 139296 | tf_op jit(solution)/shard_map/ppermute | solution.py:331
  18.9 1.6 %collective-permute-done.5.refs_2_.refs_4_ = bf16[272,256]{1,0:T(8,128)(2,1)S(1)} collective-permute-done((bf16[272,256]{1,0:T(8,128)(2,1)S(1)}, bf16[272,256]{1,0:T(8,128)(2,1)S(1)}, u32[]{:S(2)}, u32[]{:S(2)}) %collective-permute-start.5) | collective-permute-done | bytes 139296 | tf_op jit(solution)/shard_map/ppermute | solution.py:331
  20.5 0.3 collective-permute-done.6.refs_3_
  20.8 0.1 totals.3.own
  20.9 1.6 %collective-permute-start.7 = (bf16[272,256]{1,0:T(8,128)(2,1)S(1)}, bf16[272,256]{1,0:T(8,128)(2,1)S(1)}, u32[]{:S(2)}, u32[]{:S(2)}) collective-permute-start(bf16[272,256]{1,0:T(8,128)(2,1)S(1)} %totals.3.own), channel_id=1, source_target_pairs={{0,8},{2,10},{4,12},{6,14},{8,0},{10,2},{12,4},{14,6},{16,24},{18,... | collective-permute-start | bytes 417800 | tf_op jit(solution)/shard_map/ppermute | solution.py:603
  22.5 0.0 collective-permute-done.3.received.refs_0_
  22.6 2.6 %collective-permute-start.12 = (bf16[144,256]{1,0:T(8,128)(2,1)S(1)}, bf16[144,256]{1,0:T(8,128)(2,1)S(1)}, u32[]{:S(2)}, u32[]{:S(2)}) collective-permute-start(bf16[144,256]{1,0:T(8,128)(2,1)S(1)} %merged.2.refs_7_), channel_id=1, source_target_pairs={{0,16},{2,18},{4,20},{6,22},{8,24},{10,26},{12,28},{14,30},{16,0},... | collective-permute-start | bytes 221192 | tf_op jit(solution)/shard_map/ppermute | solution.py:603
  25.2 3.5 %inner_terms.2 = (bf16[384,1024]{1,0:T(8,128)(2,1)S(1)}, f32[384,128]{1,0:T(8,128)S(1)}, f32[384,128]{1,0:T(8,128)S(1)}) custom-call(bf16[384,128]{1,0:T(8,128)(2,1)S(1)} %get-tuple-element.54.refs_0_.b, bf16[384,128]{1,0:T(8,128)(2,1)S(1)} %get-tuple-element.55.refs_1_.c, bf16[384,2048]{1,0:T(8,128)(2,1)S(1)} %get-tuple-element.56.refs_2_.x, ...), custom_call_target="tpu_custom_call" | custom-call | flops 805306368 | bytes 3145728 | tf_op jit(solution)/shard_map/inner_terms/pallas_call | solution.py:484
  28.7 0.0 collective-permute-done.12.refs_1_
  28.8 0.2 member_entries.3
  29.0 2.0 %collective-permute-start.13 = (bf16[256,256]{1,0:T(8,128)(2,1)S(1)}, bf16[256,256]{1,0:T(8,128)(2,1)S(1)}, u32[]{:S(2)}, u32[]{:S(2)}) collective-permute-start(bf16[256,256]{1,0:T(8,128)(2,1)S(1)} %get-tuple-element.86), channel_id=1, source_target_pairs={{0,6},{2,4},{4,2},{6,0},{8,14},{10,12},{12,10},{14,8},{16,22},{18,... | collective-permute-start | bytes 393224 | tf_op jit(solution)/shard_map/ppermute | solution.py:331
  31.0 0.0 collective-permute-done.7.received.refs_0_
  31.0 1.8 %collective-permute-start.8 = (bf16[144,256]{1,0:T(8,128)(2,1)S(1)}, bf16[144,256]{1,0:T(8,128)(2,1)S(1)}, u32[]{:S(2)}, u32[]{:S(2)}) collective-permute-start(bf16[144,256]{1,0:T(8,128)(2,1)S(1)} %merged.3.refs_9_), channel_id=1, source_target_pairs={{0,16},{2,18},{4,20},{6,22},{8,24},{10,26},{12,28},{14,30},{16,0},... | collective-permute-start | bytes 221192 | tf_op jit(solution)/shard_map/ppermute | solution.py:603
  32.9 1.1 %collective-permute-start.14 = (bf16[256,256]{1,0:T(8,128)(2,1)S(1)}, bf16[256,256]{1,0:T(8,128)(2,1)S(1)}, u32[]{:S(2)}, u32[]{:S(2)}) collective-permute-start(bf16[256,256]{1,0:T(8,128)(2,1)S(1)} %get-tuple-element.87), channel_id=1, source_target_pairs={{0,4},{2,6},{4,0},{6,2},{8,12},{10,14},{12,8},{14,10},{16,20},{18,... | collective-permute-start | bytes 393224 | tf_op jit(solution)/shard_map/ppermute | solution.py:331
  33.9 0.5 collective-permute-start.15
  34.4 3.5 %inner_terms.3 = (bf16[384,1024]{1,0:T(8,128)(2,1)S(1)}, f32[384,128]{1,0:T(8,128)S(1)}, f32[384,128]{1,0:T(8,128)S(1)}) custom-call(bf16[384,128]{1,0:T(8,128)(2,1)S(1)} %get-tuple-element.54.refs_0_.b, bf16[384,128]{1,0:T(8,128)(2,1)S(1)} %get-tuple-element.55.refs_1_.c, bf16[384,2048]{1,0:T(8,128)(2,1)S(1)} %get-tuple-element.56.refs_2_.x, ...), custom_call_target="tpu_custom_call" | custom-call | flops 805306368 | bytes 3145728 | tf_op jit(solution)/shard_map/inner_terms/pallas_call | solution.py:484
  38.0 0.2 member_entries.2
  38.2 1.6 %collective-permute-start.10 = (bf16[256,256]{1,0:T(8,128)(2,1)S(1)}, bf16[256,256]{1,0:T(8,128)(2,1)S(1)}, u32[]{:S(2)}, u32[]{:S(2)}) collective-permute-start(bf16[256,256]{1,0:T(8,128)(2,1)S(1)} %get-tuple-element.81), channel_id=1, source_target_pairs={{0,4},{2,6},{4,0},{6,2},{8,12},{10,14},{12,8},{14,10},{16,20},{18,... | collective-permute-start | bytes 393224 | tf_op jit(solution)/shard_map/ppermute | solution.py:331
  39.8 0.9 %collective-permute-start.11 = (bf16[256,256]{1,0:T(8,128)(2,1)S(1)}, bf16[256,256]{1,0:T(8,128)(2,1)S(1)}, u32[]{:S(2)}, u32[]{:S(2)}) collective-permute-start(bf16[256,256]{1,0:T(8,128)(2,1)S(1)} %get-tuple-element.82), channel_id=1, source_target_pairs={{0,2},{2,0},{4,6},{6,4},{8,10},{10,8},{12,14},{14,12},{16,18},{18,... | collective-permute-start | bytes 393224 | tf_op jit(solution)/shard_map/ppermute | solution.py:331
  40.7 0.0 collective-permute-done.13.refs_1_
  40.7 1.0 %collective-permute-start.9 = (bf16[256,256]{1,0:T(8,128)(2,1)S(1)}, bf16[256,256]{1,0:T(8,128)(2,1)S(1)}, u32[]{:S(2)}, u32[]{:S(2)}) collective-permute-start(bf16[256,256]{1,0:T(8,128)(2,1)S(1)} %get-tuple-element.80), channel_id=1, source_target_pairs={{0,6},{2,4},{4,2},{6,0},{8,14},{10,12},{12,10},{14,8},{16,22},{18,... | collective-permute-start | bytes 393224 | tf_op jit(solution)/shard_map/ppermute | solution.py:331
  41.7 0.0 collective-permute-done.14.refs_2_
  41.7 0.0 collective-permute-done.15.refs_3_
  41.7 1.2 %entry_values.2 = (bf16[384,2048]{1,0:T(8,128)(2,1)}, f32[8,128]{1,0:T(8,128)S(1)}) custom-call(s32[1]{0:T(128)} %bitcast.where, bf16[384,1024]{1,0:T(8,128)(2,1)S(1)} %get-tuple-element.83.spread, bf16[384,128]{1,0:T(8,128)(2,1)S(1)} %get-tuple-element.54.refs_0_.b, bf16[384,1024]{1,0:T(8,128)(2,1)S(1)} %get-tuple-element.84.dx_local, ...), custom_call_target="tpu_custom_call" | custom-call | flops 100663296 | bytes 1572864 | tf_op jit(solution)/shard_map/entry_values/pallas_call | solution.py:557
  43.0 0.6 %entry_parts.2 = (f32[384,128]{1,0:T(8,128)S(1)}, f32[384,128]{1,0:T(8,128)S(1)}) custom-call(bf16[384,1024]{1,0:T(8,128)(2,1)S(1)} %get-tuple-element.93.x_scaled, bf16[384,1024]{1,0:T(8,128)(2,1)S(1)} %get-tuple-element.94.dy_scaled, f32[384,128]{1,0:T(8,128)S(1)} %get-tuple-element.78.refs_6_.db_before, f32[384,128]{1,0:T(8,128)S(1)} %get-tuple-element.95.dc_before, ...), custom_call_target="tpu_custom_call" | custom-call | flops 201326592 | bytes 1572864 | tf_op jit(solution)/shard_map/entry_parts/pallas_call | solution.py:523
  43.5 0.8 %collective-permute-done.10.refs_2_ = bf16[256,256]{1,0:T(8,128)(2,1)S(1)} collective-permute-done((bf16[256,256]{1,0:T(8,128)(2,1)S(1)}, bf16[256,256]{1,0:T(8,128)(2,1)S(1)}, u32[]{:S(2)}, u32[]{:S(2)}) %collective-permute-start.10) | collective-permute-done | bytes 131104 | tf_op jit(solution)/shard_map/ppermute | solution.py:331
  44.3 0.5 collective-permute-done.11.refs_3_
  44.8 1.8 %collective-permute-done.9.refs_1_ = bf16[256,256]{1,0:T(8,128)(2,1)S(1)} collective-permute-done((bf16[256,256]{1,0:T(8,128)(2,1)S(1)}, bf16[256,256]{1,0:T(8,128)(2,1)S(1)}, u32[]{:S(2)}, u32[]{:S(2)}) %collective-permute-start.9) | collective-permute-done | bytes 131104 | tf_op jit(solution)/shard_map/ppermute | solution.py:331
  46.6 0.6 %entry_parts.3 = bf16[768,128]{1,0:T(8,128)(2,1)S(1)} custom-call(bf16[384,1024]{1,0:T(8,128)(2,1)S(1)} %get-tuple-element.91.x_scaled, bf16[384,1024]{1,0:T(8,128)(2,1)S(1)} %get-tuple-element.92.dy_scaled, f32[384,128]{1,0:T(8,128)S(1)} %get-tuple-element.96.db_before, f32[384,128]{1,0:T(8,128)S(1)} %get-tuple-element.97.dc_before, ...), custom_call_target="tpu_custom_call" | custom-call | flops 201326592 | bytes 1572864 | tf_op jit(solution)/shard_map/entry_parts/pallas_call | solution.py:523
  47.2 0.1 collective-permute-start.16
  47.2 1.8 %entry_values.3 = (bf16[384,2048]{1,0:T(8,128)(2,1)}, f32[8,128]{1,0:T(8,128)}) custom-call(s32[1]{0:T(128)} %bitcast.where, bf16[384,1024]{1,0:T(8,128)(2,1)S(1)} %get-tuple-element.58.spread, bf16[384,128]{1,0:T(8,128)(2,1)S(1)} %get-tuple-element.54.refs_0_.b, bf16[384,1024]{1,0:T(8,128)(2,1)S(1)} %get-tuple-element.77.dx_local, ...), custom_call_target="tpu_custom_call", output_to_operand_aliasing={{0}: (8, {})} | custom-call | flops 100663296 | bytes 1572864 | tf_op jit(solution)/shard_map/entry_values/pallas_call | solution.py:557
  49.1 0.0 collective-permute-done.16
  49.1 0.1 add_convert_fusion
  49.1 0.7 %fusion = (bf16[384,128]{1,0:T(8,128)(2,1)}, bf16[384,128]{1,0:T(8,128)(2,1)}) fusion(bf16[768,128]{1,0:T(8,128)(2,1)S(1)} %add_convert_fusion), kind=kLoop, calls=%fused_computation.1 | loop fusion | bytes 393216 | tf_op jit(solution)/shard_map/slice | solution.py:628
  (3 shorter events, 0.1 us)
Async XLA Ops:
  3.9 9.6 %collective-permute-start = (bf16[272,256]{1,0:T(8,128)(2,1)S(1)}, bf16[272,256]{1,0:T(8,128)(2,1)S(1)}, u32[]{:S(2)}, u32[]{:S(2)}) collective-permute-start(bf16[272,256]{1,0:T(8,128)(2,1)S(1)} %get-tuple-element.69), channel_id=1, source_target_pairs={{0,6},{2,4},{4,2},{6,0},{8,14},{10,12},{12,10},{14,8},{16,22},{18,... | collective-permute-start | bytes 417800 | tf_op jit(solution)/shard_map/ppermute | solution.py:331
  7.9 8.2 %collective-permute-start.1 = (bf16[272,256]{1,0:T(8,128)(2,1)S(1)}, bf16[272,256]{1,0:T(8,128)(2,1)S(1)}, u32[]{:S(2)}, u32[]{:S(2)}) collective-permute-start(bf16[272,256]{1,0:T(8,128)(2,1)S(1)} %get-tuple-element.70), channel_id=1, source_target_pairs={{0,4},{2,6},{4,0},{6,2},{8,12},{10,14},{12,8},{14,10},{16,20},{18,... | collective-permute-start | bytes 417800 | tf_op jit(solution)/shard_map/ppermute | solution.py:331
  8.4 7.7 %collective-permute-start.2 = (bf16[272,256]{1,0:T(8,128)(2,1)S(1)}, bf16[272,256]{1,0:T(8,128)(2,1)S(1)}, u32[]{:S(2)}, u32[]{:S(2)}) collective-permute-start(bf16[272,256]{1,0:T(8,128)(2,1)S(1)} %get-tuple-element.71), channel_id=1, source_target_pairs={{0,2},{2,0},{4,6},{6,4},{8,10},{10,8},{12,14},{14,12},{16,18},{18,... | collective-permute-start | bytes 417800 | tf_op jit(solution)/shard_map/ppermute | solution.py:331
  10.1 8.8 %collective-permute-start.4 = (bf16[272,256]{1,0:T(8,128)(2,1)S(1)}, bf16[272,256]{1,0:T(8,128)(2,1)S(1)}, u32[]{:S(2)}, u32[]{:S(2)}) collective-permute-start(bf16[272,256]{1,0:T(8,128)(2,1)S(1)} %get-tuple-element.74), channel_id=1, source_target_pairs={{0,6},{2,4},{4,2},{6,0},{8,14},{10,12},{12,10},{14,8},{16,22},{18,... | collective-permute-start | bytes 417800 | tf_op jit(solution)/shard_map/ppermute | solution.py:331
  13.0 7.5 %collective-permute-start.5 = (bf16[272,256]{1,0:T(8,128)(2,1)S(1)}, bf16[272,256]{1,0:T(8,128)(2,1)S(1)}, u32[]{:S(2)}, u32[]{:S(2)}) collective-permute-start(bf16[272,256]{1,0:T(8,128)(2,1)S(1)} %get-tuple-element.75), channel_id=1, source_target_pairs={{0,4},{2,6},{4,0},{6,2},{8,12},{10,14},{12,8},{14,10},{16,20},{18,... | collective-permute-start | bytes 417800 | tf_op jit(solution)/shard_map/ppermute | solution.py:331
  13.5 7.2 %collective-permute-start.6 = (bf16[272,256]{1,0:T(8,128)(2,1)S(1)}, bf16[272,256]{1,0:T(8,128)(2,1)S(1)}, u32[]{:S(2)}, u32[]{:S(2)}) collective-permute-start(bf16[272,256]{1,0:T(8,128)(2,1)S(1)} %get-tuple-element.76), channel_id=1, source_target_pairs={{0,2},{2,0},{4,6},{6,4},{8,10},{10,8},{12,14},{14,12},{16,18},{18,... | collective-permute-start | bytes 417800 | tf_op jit(solution)/shard_map/ppermute | solution.py:331
  16.2 6.3 %collective-permute-start.3 = (bf16[272,256]{1,0:T(8,128)(2,1)S(1)}, bf16[272,256]{1,0:T(8,128)(2,1)S(1)}, u32[]{:S(2)}, u32[]{:S(2)}) collective-permute-start(bf16[272,256]{1,0:T(8,128)(2,1)S(1)} %totals.2.own), channel_id=1, source_target_pairs={{0,8},{2,10},{4,12},{6,14},{8,0},{10,2},{12,4},{14,6},{16,24},{18,... | collective-permute-start | bytes 417800 | tf_op jit(solution)/shard_map/ppermute | solution.py:603
  20.9 10.1 %collective-permute-start.7 = (bf16[272,256]{1,0:T(8,128)(2,1)S(1)}, bf16[272,256]{1,0:T(8,128)(2,1)S(1)}, u32[]{:S(2)}, u32[]{:S(2)}) collective-permute-start(bf16[272,256]{1,0:T(8,128)(2,1)S(1)} %totals.3.own), channel_id=1, source_target_pairs={{0,8},{2,10},{4,12},{6,14},{8,0},{10,2},{12,4},{14,6},{16,24},{18,... | collective-permute-start | bytes 417800 | tf_op jit(solution)/shard_map/ppermute | solution.py:603
  22.6 6.2 %collective-permute-start.12 = (bf16[144,256]{1,0:T(8,128)(2,1)S(1)}, bf16[144,256]{1,0:T(8,128)(2,1)S(1)}, u32[]{:S(2)}, u32[]{:S(2)}) collective-permute-start(bf16[144,256]{1,0:T(8,128)(2,1)S(1)} %merged.2.refs_7_), channel_id=1, source_target_pairs={{0,16},{2,18},{4,20},{6,22},{8,24},{10,26},{12,28},{14,30},{16,0},... | collective-permute-start | bytes 221192 | tf_op jit(solution)/shard_map/ppermute | solution.py:603
  29.0 11.7 %collective-permute-start.13 = (bf16[256,256]{1,0:T(8,128)(2,1)S(1)}, bf16[256,256]{1,0:T(8,128)(2,1)S(1)}, u32[]{:S(2)}, u32[]{:S(2)}) collective-permute-start(bf16[256,256]{1,0:T(8,128)(2,1)S(1)} %get-tuple-element.86), channel_id=1, source_target_pairs={{0,6},{2,4},{4,2},{6,0},{8,14},{10,12},{12,10},{14,8},{16,22},{18,... | collective-permute-start | bytes 393224 | tf_op jit(solution)/shard_map/ppermute | solution.py:331
  31.0 6.9 %collective-permute-start.8 = (bf16[144,256]{1,0:T(8,128)(2,1)S(1)}, bf16[144,256]{1,0:T(8,128)(2,1)S(1)}, u32[]{:S(2)}, u32[]{:S(2)}) collective-permute-start(bf16[144,256]{1,0:T(8,128)(2,1)S(1)} %merged.3.refs_9_), channel_id=1, source_target_pairs={{0,16},{2,18},{4,20},{6,22},{8,24},{10,26},{12,28},{14,30},{16,0},... | collective-permute-start | bytes 221192 | tf_op jit(solution)/shard_map/ppermute | solution.py:603
  32.9 8.9 %collective-permute-start.14 = (bf16[256,256]{1,0:T(8,128)(2,1)S(1)}, bf16[256,256]{1,0:T(8,128)(2,1)S(1)}, u32[]{:S(2)}, u32[]{:S(2)}) collective-permute-start(bf16[256,256]{1,0:T(8,128)(2,1)S(1)} %get-tuple-element.87), channel_id=1, source_target_pairs={{0,4},{2,6},{4,0},{6,2},{8,12},{10,14},{12,8},{14,10},{16,20},{18,... | collective-permute-start | bytes 393224 | tf_op jit(solution)/shard_map/ppermute | solution.py:331
  33.9 7.8 %collective-permute-start.15 = (bf16[256,256]{1,0:T(8,128)(2,1)S(1)}, bf16[256,256]{1,0:T(8,128)(2,1)S(1)}, u32[]{:S(2)}, u32[]{:S(2)}) collective-permute-start(bf16[256,256]{1,0:T(8,128)(2,1)S(1)} %get-tuple-element.88), channel_id=1, source_target_pairs={{0,2},{2,0},{4,6},{6,4},{8,10},{10,8},{12,14},{14,12},{16,18},{18,... | collective-permute-start | bytes 393224 | tf_op jit(solution)/shard_map/ppermute | solution.py:331
  38.2 6.1 %collective-permute-start.10 = (bf16[256,256]{1,0:T(8,128)(2,1)S(1)}, bf16[256,256]{1,0:T(8,128)(2,1)S(1)}, u32[]{:S(2)}, u32[]{:S(2)}) collective-permute-start(bf16[256,256]{1,0:T(8,128)(2,1)S(1)} %get-tuple-element.81), channel_id=1, source_target_pairs={{0,4},{2,6},{4,0},{6,2},{8,12},{10,14},{12,8},{14,10},{16,20},{18,... | collective-permute-start | bytes 393224 | tf_op jit(solution)/shard_map/ppermute | solution.py:331
  39.8 5.0 %collective-permute-start.11 = (bf16[256,256]{1,0:T(8,128)(2,1)S(1)}, bf16[256,256]{1,0:T(8,128)(2,1)S(1)}, u32[]{:S(2)}, u32[]{:S(2)}) collective-permute-start(bf16[256,256]{1,0:T(8,128)(2,1)S(1)} %get-tuple-element.82), channel_id=1, source_target_pairs={{0,2},{2,0},{4,6},{6,4},{8,10},{10,8},{12,14},{14,12},{16,18},{18,... | collective-permute-start | bytes 393224 | tf_op jit(solution)/shard_map/ppermute | solution.py:331
  40.7 5.9 %collective-permute-start.9 = (bf16[256,256]{1,0:T(8,128)(2,1)S(1)}, bf16[256,256]{1,0:T(8,128)(2,1)S(1)}, u32[]{:S(2)}, u32[]{:S(2)}) collective-permute-start(bf16[256,256]{1,0:T(8,128)(2,1)S(1)} %get-tuple-element.80), channel_id=1, source_target_pairs={{0,6},{2,4},{4,2},{6,0},{8,14},{10,12},{12,10},{14,8},{16,22},{18,... | collective-permute-start | bytes 393224 | tf_op jit(solution)/shard_map/ppermute | solution.py:331
  47.2 1.9 %collective-permute-start.16 = (bf16[768,128]{1,0:T(8,128)(2,1)S(1)}, bf16[768,128]{1,0:T(8,128)(2,1)S(1)}, u32[]{:S(2)}, u32[]{:S(2)}) collective-permute-start(bf16[768,128]{1,0:T(8,128)(2,1)S(1)} %entry_parts.3), channel_id=1, source_target_pairs={{0,1},{1,0},{2,3},{3,2},{4,5},{5,4},{6,7},{7,6},{8,9},{9,8},{10,11... | collective-permute-start | bytes 589832 | tf_op jit(solution)/shard_map/ppermute | solution.py:581

commit v7 on v6

--- a/solution.py
+++ b/solution.py
@@ -214,9 +214,9 @@
     return slice(0, state) if forward else slice(state, 2 * state)
 
 
-def totals_kernel(state, where, *refs):
+def totals_kernel(state, levels, where, *refs):
     group = GROUP
-    blocks, out = sent_order(refs[:group]), refs[-1]
+    blocks, outs, sums = sent_order(refs[:group]), refs[-1 - levels : -1], refs[-1]
     for here in range(group):
 
         @pl.when(place_of(where) == here)
@@ -227,76 +227,56 @@
                 for q in in_order(group, forward):
                     piece = blocks[q ^ here][rows, :].astype(F32)
                     value = piece if value is None else decays[q] * value + piece
-                out[rows, :] = value.astype(BF16)
-            factor = decays[0]
-            for d in decays[1:]:
-                factor = factor * d
-            put_decay(out, 2 * state, factor)
-
-
-def totals(state, where, blocks, after):
-    return pl.pallas_call(
-        functools.partial(totals_kernel, state),
-        out_shape=pltpu.VMEM(blocks[0].shape, BF16),
+                sums[rows, :] = value.astype(BF16)
+
+    factor = decay_of(blocks[0][2 * state :, :])
+    for block in blocks[1:]:
+        factor = factor * decay_of(block[2 * state :, :])
+    for level, out in enumerate(outs):
+        put_decay(out, state, factor)
+        for forward in (True, False):
+
+            @pl.when(bit_of(where, level) != forward)
+            def _(out=out, forward=forward):
+                out[:state, :] = sums[side_rows(state, forward), :]
+
+
+def totals(state, levels, where, blocks, after):
+    part = blocks[0].shape[1]
+    outs = [jax.ShapeDtypeStruct((state + TAIL, part), BF16)] * levels
+    return pl.pallas_call(
+        functools.partial(totals_kernel, state, levels),
+        out_shape=outs,
         in_specs=[SMEM] + whole(len(blocks)) + [ANY] * len(after),
-        out_specs=whole(1)[0],
+        out_specs=whole(levels),
+        scratch_shapes=[pltpu.VMEM((2 * state, part), BF16)],
         compiler_params=params(4),
         cost_estimate=cost(8 * blocks[0].size, 10 * blocks[0].size),
         name="totals",
     )(where, *sent_order(blocks), *after)
 
 
-def merged_kernel(state, level, last, where, own, received, *refs):
-    out = refs[-1]
-    d_own, d_other = decay_of(own[2 * state :, :]), decay_of(received[2 * state :, :])
-    upper = bit_of(where, level)
-    later = bit_of(where, level + 1)
-    for is_upper in (False, True):
-        for forward in (True, False):
-            chosen = upper == is_upper
-            if last:
-                chosen = chosen & (later != forward)
-
-            @pl.when(chosen)
-            def _(is_upper=is_upper, forward=forward):
+def members_kernel(state, groups, where, *refs):
+    received, refs = [None, *refs[: groups - 1]], refs[groups - 1 :]
+    group = GROUP
+    blocks, outs, entry = refs[:group], refs[-1 - group : -1], refs[-1]
+    number = where[0] // group
+    for mine in range(groups):
+
+        @pl.when(number == mine)
+        def _(mine=mine):
+            for forward in (True, False):
                 rows = side_rows(state, forward)
-                mine, other = own[rows, :].astype(F32), received[rows, :].astype(F32)
-                value = mine + d_own * other if is_upper == forward else other + d_other * mine
-                out[slice(0, state) if last else rows, :] = value.astype(BF16)
-
-    put_decay(out, state if last else 2 * state, d_own * d_other)
-
-
-def merged(state, level, last, where, own, received, after):
-    rows = (state if last else 2 * state) + TAIL
-    return pl.pallas_call(
-        functools.partial(merged_kernel, state, level, last),
-        out_shape=pltpu.VMEM((rows, own.shape[1]), BF16),
-        in_specs=[SMEM] + whole(2) + [ANY] * len(after),
-        out_specs=whole(1)[0],
-        compiler_params=params(4),
-        cost_estimate=cost(4 * own.size, 6 * own.size),
-        name="merged",
-    )(where, own, received, *after)
-
-
-def members_kernel(state, levels, where, *refs):
-    received, refs = refs[:levels], refs[levels:]
-    group = GROUP
-    blocks, outs = refs[:group], refs[-group:]
-    entry = []
-    for forward in (True, False):
-        value, factor = None, 1.0
-        for level, r in enumerate(received):
-            gets = (bit_of(where, level)) == forward
-            rows = side_rows(state, forward)
-            if r.shape[0] < 2 * state:
-                rows = slice(0, state)
-            piece = r[rows, :].astype(F32) * jnp.where(gets, 1.0, 0.0)
-            value = piece if value is None else value + factor * piece
-            if level < levels - 1:
-                factor = factor * jnp.where(gets, decay_of(r[2 * state :, :]), 1.0)
-        entry.append(value)
+                others = range(mine - 1, -1, -1) if forward else range(mine + 1, groups)
+                value, factor = jnp.zeros((state, entry.shape[1]), F32), None
+                for other in others:
+                    r = received[mine ^ other]
+                    piece = r[:state, :].astype(F32)
+                    value = piece if factor is None else value + factor * piece
+                    d = decay_of(r[state:, :])
+                    factor = d if factor is None else factor * d
+                entry[rows, :] = value
+
     for here in range(group):
 
         @pl.when(place_of(where) == here)
@@ -304,7 +284,7 @@
             decays = [decay_of(blocks[q ^ here][2 * state :, :]) for q in range(group)]
             for forward in (True, False):
                 rows, order = side_rows(state, forward), in_order(group, forward)
-                value = entry[0 if forward else 1]
+                value = entry[rows, :]
                 for q in order:
                     outs[q ^ here][rows, :] = value.astype(BF16)
                     if q != order[-1]:
@@ -314,10 +294,11 @@
 def member_entries(state, where, blocks, received, after):
     group, part = len(blocks), blocks[0].shape[1]
     return pl.pallas_call(
-        functools.partial(members_kernel, state, len(received)),
-        out_shape=[pltpu.VMEM((2 * state, part), BF16)] * group,
+        functools.partial(members_kernel, state, len(received) + 1),
+        out_shape=[jax.ShapeDtypeStruct((2 * state, part), BF16)] * group,
         in_specs=[SMEM] + whole(group + len(received)) + [ANY] * len(after),
         out_specs=whole(group),
+        scratch_shapes=[pltpu.VMEM((2 * state, part), F32)],
         compiler_params=params(4),
         cost_estimate=cost(12 * blocks[0].size, 16 * blocks[0].size),
         name="member_entries",
@@ -598,22 +579,19 @@
         blocks.append(exchange(states[chunk][3:]))
     setup = inner_setup(head_dim, ld, b, c, [states[-1][3]])
 
-    def to_level(block, level):
-        step = group << level
-        return lax.ppermute(block, "seq", [(s, s ^ step) for s in range(count)])
-
+    received = []
+    for chunk in range(chunks):
+        outs = totals(state, levels, where, blocks[chunk], setup[-1:] if chunk == 0 else [])
+        received.append([])
+        for k in range(1, count // group):
+            pairs = [(s, s ^ (k * group)) for s in range(count)]
+            received[chunk].append(lax.ppermute(outs[k.bit_length() - 1], "seq", pairs))
     entries, inner, sums = [], [], []
     for chunk in range(chunks):
-        own = totals(state, where, blocks[chunk], setup[-1:] if chunk == 0 else [])
-        received = [to_level(own, 0)]
-        for level in range(levels - 1):
-            last = level == levels - 2
-            own = merged(state, level, last, where, own, received[level], [])
-            received.append(to_level(own, level + 1))
-        inner.append(inner_terms(head_dim, chunk, setup, b, c, x, dy, sums, [own]))
+        found = member_entries(state, where, blocks[chunk], received[chunk], sums[:1])
+        entries.append(exchange(found))
+        inner.append(inner_terms(head_dim, chunk, setup, b, c, x, dy, sums, found[:1]))
         sums = list(inner[chunk][1:])
-        found = member_entries(state, where, blocks[chunk], received, sums[:1])
-        entries.append(exchange(found))
 
     grad_values, done = [], []
     for chunk in range(chunks):

time: 50 us -> 50.8 us (1.016)
  starting transfers between devices: 23.9 us -> 25.4 us
  waiting for transfers between devices: 7.2 us -> 6.41 us
    ppermute x12, waiting for transfers between devices: 7.18 us -> 1.83 us  [exchange(): out[k] = lax.ppermute(parts[k], 'seq', [(s, s ^ k) for s in range(count)])]
    ppermute x4 -> x6, waiting for transfers between devices: 0.01 us -> 4.58 us  [shards(): received[chunk].append(lax.ppermute(outs[k.bit_length() - 1], 'seq', pairs))]
    ppermute x4 -> x6, starting transfers between devices: 7.77 us -> 8.67 us  [shards(): received[chunk].append(lax.ppermute(outs[k.bit_length() - 1], 'seq', pairs))]
    ppermute x12, starting transfers between devices: 16 us -> 16.7 us  [exchange(): out[k] = lax.ppermute(parts[k], 'seq', [(s, s ^ k) for s in range(count)])]
  transfers between devices with their start and end apart: 17 -> 19, of which waited for: 7 -> 5; matrix products, arithmetic and copies ran while one was open for 0% -> 0% of each run, Pallas kernels for 27% -> 26%
where the time goes in v7:
time: 50.8 us; the launch traced here: 50.6 us
  starting transfers between devices  25.4 us (50%)
  Pallas kernels  17.2 us (34%)
  waiting for transfers between devices  6.41 us (13%)
  between operations  0.81 us (2%)
  local copies, waits for them, and re-layouts  0.69 us (1%)
    ppermute x12, starting transfers between devices, exchange(): out[k] = lax.ppermute(parts[k], 'seq', [(s, s ^ k) for s in range(count)])  16.7 us
    ppermute x6, starting transfers between devices, shards(): received[chunk].append(lax.ppermute(outs[k.bit_length() - 1], 'seq', pairs))  8.67 us
    pallas_call x2, Pallas kernels, inner_terms(): pl.pallas_call(functools.partial(inner_kernel, head_dim, chunk, len(befor...  6.95 us
    ppermute x6, waiting for transfers between devices, shards(): received[chunk].append(lax.ppermute(outs[k.bit_length() - 1], 'seq', pairs))  4.58 us
    pallas_call x1, Pallas kernels, first_states(): pl.pallas_call(functools.partial(first_states_kernel, head_dim, group), o...  3.26 us
    pallas_call x2, Pallas kernels, entry_values(): pl.pallas_call(functools.partial(values_kernel, chunk), out_shape=[pltpu....  3.01 us
    ppermute x12, waiting for transfers between devices, exchange(): out[k] = lax.ppermute(parts[k], 'seq', [(s, s ^ k) for s in range(count)])  1.83 us
    pallas_call x1, Pallas kernels, next_states(): pl.pallas_call(functools.partial(next_states_kernel, head_dim, chunk), ou...  1.58 us
  transfers between devices with their start and end apart: 19, of which 5 were waited for; matrix products, arithmetic and copies ran while one was open for 0% of the time, Pallas kernels for 26%

profile of v7, /device:TPU:0, one launch (start us, length us, event | category | flops | bytes accessed | tf_op | source)
XLA Modules:
  0.0 50.6 jit_solution(3085514519618933742)
XLA Ops:
  0.6 3.3 %first_states.1 = (f32[32,384]{1,0:T(8,128)S(1)}, bf16[384,128]{1,0:T(8,128)(2,1)S(1)}, bf16[384,128]{1,0:T(8,128)(2,1)S(1)}, bf16[384,2048]{1,0:T(8,128)(2,1)S(...) custom-call(s32[1]{0:T(128)} %bitcast.where, ...), custom_call_target="tpu_custom_call" | custom-call | flops 402653184 | bytes 6291456 | tf_op jit(solution)/shard_map/first_states/pallas_call | solution.py:167
  3.9 4.0 %collective-permute-start = (bf16[272,256]{1,0:T(8,128)(2,1)S(1)}, bf16[272,256]{1,0:T(8,128)(2,1)S(1)}, u32[]{:S(2)}, u32[]{:S(2)}) collective-permute-start(bf16[272,256]{1,0:T(8,128)(2,1)S(1)} %get-tuple-element.73), channel_id=1, source_target_pairs={{0,6},{2,4},{4,2},{6,0},{8,14},{10,12},{12,10},{14,8},{16,22},{18,... | collective-permute-start | bytes 417800 | tf_op jit(solution)/shard_map/ppermute | solution.py:312
  7.9 0.5 %collective-permute-start.1 = (bf16[272,256]{1,0:T(8,128)(2,1)S(1)}, bf16[272,256]{1,0:T(8,128)(2,1)S(1)}, u32[]{:S(2)}, u32[]{:S(2)}) collective-permute-start(bf16[272,256]{1,0:T(8,128)(2,1)S(1)} %get-tuple-element.74), channel_id=1, source_target_pairs={{0,4},{2,6},{4,0},{6,2},{8,12},{10,14},{12,8},{14,10},{16,20},{18,... | collective-permute-start | bytes 417800 | tf_op jit(solution)/shard_map/ppermute | solution.py:312
  8.4 0.1 collective-permute-start.2
  8.5 1.6 %next_states.1 = (bf16[384,1024]{1,0:T(8,128)(2,1)S(1)}, bf16[384,1024]{1,0:T(8,128)(2,1)S(1)}, bf16[384,1024]{1,0:T(8,128)(2,1)S(1)}, bf16[272,256]{1,0:T(8,128...) custom-call(s32[1]{0:T(128)} %bitcast.where, ...), custom_call_target="tpu_custom_call" | custom-call | flops 402653184 | bytes 3145728 | tf_op jit(solution)/shard_map/next_states/pallas_call | solution.py:182
  10.1 2.9 %collective-permute-start.6 = (bf16[272,256]{1,0:T(8,128)(2,1)S(1)}, bf16[272,256]{1,0:T(8,128)(2,1)S(1)}, u32[]{:S(2)}, u32[]{:S(2)}) collective-permute-start(bf16[272,256]{1,0:T(8,128)(2,1)S(1)} %get-tuple-element.81), channel_id=1, source_target_pairs={{0,6},{2,4},{4,2},{6,0},{8,14},{10,12},{12,10},{14,8},{16,22},{18,... | collective-permute-start | bytes 417800 | tf_op jit(solution)/shard_map/ppermute | solution.py:312
  13.0 0.5 %collective-permute-start.7 = (bf16[272,256]{1,0:T(8,128)(2,1)S(1)}, bf16[272,256]{1,0:T(8,128)(2,1)S(1)}, u32[]{:S(2)}, u32[]{:S(2)}) collective-permute-start(bf16[272,256]{1,0:T(8,128)(2,1)S(1)} %get-tuple-element.82), channel_id=1, source_target_pairs={{0,4},{2,6},{4,0},{6,2},{8,12},{10,14},{12,8},{14,10},{16,20},{18,... | collective-permute-start | bytes 417800 | tf_op jit(solution)/shard_map/ppermute | solution.py:312
  13.5 0.0 collective-permute-done.refs_1_.refs_6_
  13.5 0.9 %collective-permute-start.8 = (bf16[272,256]{1,0:T(8,128)(2,1)S(1)}, bf16[272,256]{1,0:T(8,128)(2,1)S(1)}, u32[]{:S(2)}, u32[]{:S(2)}) collective-permute-start(bf16[272,256]{1,0:T(8,128)(2,1)S(1)} %get-tuple-element.83), channel_id=1, source_target_pairs={{0,2},{2,0},{4,6},{6,4},{8,10},{10,8},{12,14},{14,12},{16,18},{18,... | collective-permute-start | bytes 417800 | tf_op jit(solution)/shard_map/ppermute | solution.py:312
  14.4 0.5 inner_setup.1
  14.8 1.2 %collective-permute-done.1.refs_2_.refs_5_ = bf16[272,256]{1,0:T(8,128)(2,1)S(1)} collective-permute-done((bf16[272,256]{1,0:T(8,128)(2,1)S(1)}, bf16[272,256]{1,0:T(8,128)(2,1)S(1)}, u32[]{:S(2)}, u32[]{:S(2)}) %collective-permute-start.1) | collective-permute-done | bytes 139296 | tf_op jit(solution)/shard_map/ppermute | solution.py:312
  16.1 0.0 collective-permute-done.2.refs_3_.refs_4_
  16.1 0.2 totals.2
  16.2 1.6 %collective-permute-start.3 = (bf16[144,256]{1,0:T(8,128)(2,1)S(1)}, bf16[144,256]{1,0:T(8,128)(2,1)S(1)}, u32[]{:S(2)}, u32[]{:S(2)}) collective-permute-start(bf16[144,256]{1,0:T(8,128)(2,1)S(1)} %get-tuple-element.76), channel_id=1, source_target_pairs={{0,8},{2,10},{4,12},{6,14},{8,0},{10,2},{12,4},{14,6},{16,24},{18,... | collective-permute-start | bytes 221192 | tf_op jit(solution)/shard_map/ppermute | solution.py:588
  17.9 2.5 %collective-permute-start.5 = (bf16[144,256]{1,0:T(8,128)(2,1)S(1)}, bf16[144,256]{1,0:T(8,128)(2,1)S(1)}, u32[]{:S(2)}, u32[]{:S(2)}) collective-permute-start(bf16[144,256]{1,0:T(8,128)(2,1)S(1)} %get-tuple-element.77), channel_id=1, source_target_pairs={{0,24},{2,26},{4,28},{6,30},{8,16},{10,18},{12,20},{14,22},{16,8},... | collective-permute-start | bytes 221192 | tf_op jit(solution)/shard_map/ppermute | solution.py:588
  20.3 0.0 collective-permute-done.6.refs_1_.refs_6_
  20.3 1.2 %collective-permute-start.4 = (bf16[144,256]{1,0:T(8,128)(2,1)S(1)}, bf16[144,256]{1,0:T(8,128)(2,1)S(1)}, u32[]{:S(2)}, u32[]{:S(2)}) collective-permute-start(bf16[144,256]{1,0:T(8,128)(2,1)S(1)} %get-tuple-element.77), channel_id=1, source_target_pairs={{0,16},{2,18},{4,20},{6,22},{8,24},{10,26},{12,28},{14,30},{16,0},... | collective-permute-start | bytes 221192 | tf_op jit(solution)/shard_map/ppermute | solution.py:588
  21.5 0.2 totals.3
  21.7 1.6 %collective-permute-start.9 = (bf16[144,256]{1,0:T(8,128)(2,1)S(1)}, bf16[144,256]{1,0:T(8,128)(2,1)S(1)}, u32[]{:S(2)}, u32[]{:S(2)}) collective-permute-start(bf16[144,256]{1,0:T(8,128)(2,1)S(1)} %get-tuple-element.84), channel_id=1, source_target_pairs={{0,8},{2,10},{4,12},{6,14},{8,0},{10,2},{12,4},{14,6},{16,24},{18,... | collective-permute-start | bytes 221192 | tf_op jit(solution)/shard_map/ppermute | solution.py:588
  23.3 1.7 %collective-permute-done.5.refs_2_ = bf16[144,256]{1,0:T(8,128)(2,1)S(1)} collective-permute-done((bf16[144,256]{1,0:T(8,128)(2,1)S(1)}, bf16[144,256]{1,0:T(8,128)(2,1)S(1)}, u32[]{:S(2)}, u32[]{:S(2)}) %collective-permute-start.5) | collective-permute-done | bytes 73760 | tf_op jit(solution)/shard_map/ppermute | solution.py:588
  25.0 2.4 %collective-permute-done.4.refs_1_ = bf16[144,256]{1,0:T(8,128)(2,1)S(1)} collective-permute-done((bf16[144,256]{1,0:T(8,128)(2,1)S(1)}, bf16[144,256]{1,0:T(8,128)(2,1)S(1)}, u32[]{:S(2)}, u32[]{:S(2)}) %collective-permute-start.4) | collective-permute-done | bytes 73760 | tf_op jit(solution)/shard_map/ppermute | solution.py:588
  27.5 0.2 member_entries.2
  27.7 2.1 %collective-permute-start.15 = (bf16[256,256]{1,0:T(8,128)(2,1)S(1)}, bf16[256,256]{1,0:T(8,128)(2,1)S(1)}, u32[]{:S(2)}, u32[]{:S(2)}) collective-permute-start(bf16[256,256]{1,0:T(8,128)(2,1)S(1)} %get-tuple-element.93), channel_id=1, source_target_pairs={{0,6},{2,4},{4,2},{6,0},{8,14},{10,12},{12,10},{14,8},{16,22},{18,... | collective-permute-start | bytes 393224 | tf_op jit(solution)/shard_map/ppermute | solution.py:312
  29.8 1.7 %collective-permute-start.11 = (bf16[144,256]{1,0:T(8,128)(2,1)S(1)}, bf16[144,256]{1,0:T(8,128)(2,1)S(1)}, u32[]{:S(2)}, u32[]{:S(2)}) collective-permute-start(bf16[144,256]{1,0:T(8,128)(2,1)S(1)} %get-tuple-element.85), channel_id=1, source_target_pairs={{0,24},{2,26},{4,28},{6,30},{8,16},{10,18},{12,20},{14,22},{16,8},... | collective-permute-start | bytes 221192 | tf_op jit(solution)/shard_map/ppermute | solution.py:588
  31.5 0.0 collective-permute-start.10
  31.5 1.5 %collective-permute-start.16 = (bf16[256,256]{1,0:T(8,128)(2,1)S(1)}, bf16[256,256]{1,0:T(8,128)(2,1)S(1)}, u32[]{:S(2)}, u32[]{:S(2)}) collective-permute-start(bf16[256,256]{1,0:T(8,128)(2,1)S(1)} %get-tuple-element.94), channel_id=1, source_target_pairs={{0,4},{2,6},{4,0},{6,2},{8,12},{10,14},{12,8},{14,10},{16,20},{18,... | collective-permute-start | bytes 393224 | tf_op jit(solution)/shard_map/ppermute | solution.py:312
  33.0 0.0 collective-permute-done.9.refs_0_
  33.0 0.6 %collective-permute-start.17 = (bf16[256,256]{1,0:T(8,128)(2,1)S(1)}, bf16[256,256]{1,0:T(8,128)(2,1)S(1)}, u32[]{:S(2)}, u32[]{:S(2)}) collective-permute-start(bf16[256,256]{1,0:T(8,128)(2,1)S(1)} %get-tuple-element.95), channel_id=1, source_target_pairs={{0,2},{2,0},{4,6},{6,4},{8,10},{10,8},{12,14},{14,12},{16,18},{18,... | collective-permute-start | bytes 393224 | tf_op jit(solution)/shard_map/ppermute | solution.py:312
  33.6 3.5 %inner_terms.2 = (bf16[384,1024]{1,0:T(8,128)(2,1)S(1)}, f32[384,128]{1,0:T(8,128)S(1)}, f32[384,128]{1,0:T(8,128)S(1)}) custom-call(bf16[384,128]{1,0:T(8,128)(2,1)S(1)} %get-tuple-element.58.refs_0_.b, bf16[384,128]{1,0:T(8,128)(2,1)S(1)} %get-tuple-element.59.refs_1_.c, bf16[384,2048]{1,0:T(8,128)(2,1)S(1)} %get-tuple-element.60.refs_2_.x, ...), custom_call_target="tpu_custom_call" | custom-call | flops 805306368 | bytes 3145728 | tf_op jit(solution)/shard_map/inner_terms/pallas_call | solution.py:465
  37.1 0.0 collective-permute-done.11.refs_2_
  37.1 0.4 collective-permute-done.10.refs_1_
  37.5 0.4 member_entries.3
  37.9 1.8 %collective-permute-start.12 = (bf16[256,256]{1,0:T(8,128)(2,1)S(1)}, bf16[256,256]{1,0:T(8,128)(2,1)S(1)}, u32[]{:S(2)}, u32[]{:S(2)}) collective-permute-start(bf16[256,256]{1,0:T(8,128)(2,1)S(1)} %get-tuple-element.88), channel_id=1, source_target_pairs={{0,6},{2,4},{4,2},{6,0},{8,14},{10,12},{12,10},{14,8},{16,22},{18,... | collective-permute-start | bytes 393224 | tf_op jit(solution)/shard_map/ppermute | solution.py:312
  39.7 1.4 %collective-permute-start.13 = (bf16[256,256]{1,0:T(8,128)(2,1)S(1)}, bf16[256,256]{1,0:T(8,128)(2,1)S(1)}, u32[]{:S(2)}, u32[]{:S(2)}) collective-permute-start(bf16[256,256]{1,0:T(8,128)(2,1)S(1)} %get-tuple-element.89), channel_id=1, source_target_pairs={{0,4},{2,6},{4,0},{6,2},{8,12},{10,14},{12,8},{14,10},{16,20},{18,... | collective-permute-start | bytes 393224 | tf_op jit(solution)/shard_map/ppermute | solution.py:312
  41.2 0.0 collective-permute-done.15.refs_1_
  41.2 0.3 collective-permute-start.14
  41.5 3.5 %inner_terms.3 = (bf16[384,1024]{1,0:T(8,128)(2,1)S(1)}, f32[384,128]{1,0:T(8,128)S(1)}, f32[384,128]{1,0:T(8,128)S(1)}) custom-call(bf16[384,128]{1,0:T(8,128)(2,1)S(1)} %get-tuple-element.58.refs_0_.b, bf16[384,128]{1,0:T(8,128)(2,1)S(1)} %get-tuple-element.59.refs_1_.c, bf16[384,2048]{1,0:T(8,128)(2,1)S(1)} %get-tuple-element.60.refs_2_.x, ...), custom_call_target="tpu_custom_call" | custom-call | flops 805306368 | bytes 3145728 | tf_op jit(solution)/shard_map/inner_terms/pallas_call | solution.py:465
  45.0 0.0 collective-permute-done.17.refs_3_
  45.0 1.2 %entry_values.2 = (bf16[384,2048]{1,0:T(8,128)(2,1)}, f32[8,128]{1,0:T(8,128)S(1)}) custom-call(s32[1]{0:T(128)} %bitcast.where, bf16[384,1024]{1,0:T(8,128)(2,1)S(1)} %get-tuple-element.91.spread, bf16[384,128]{1,0:T(8,128)(2,1)S(1)} %get-tuple-element.58.refs_0_.b, bf16[384,1024]{1,0:T(8,128)(2,1)S(1)} %get-tuple-element.92.dx_local, ...), custom_call_target="tpu_custom_call" | custom-call | flops 100663296 | bytes 1572864 | tf_op jit(solution)/shard_map/entry_values/pallas_call | solution.py:538
  46.2 0.6 %entry_parts.2 = (f32[384,128]{1,0:T(8,128)S(1)}, f32[384,128]{1,0:T(8,128)S(1)}) custom-call(bf16[384,1024]{1,0:T(8,128)(2,1)S(1)} %get-tuple-element.100.x_scaled, bf16[384,1024]{1,0:T(8,128)(2,1)S(1)} %get-tuple-element.101.dy_scaled, f32[384,128]{1,0:T(8,128)S(1)} %get-tuple-element.102.db_before, f32[384,128]{1,0:T(8,128)S(1)} %get-tuple-element.103.dc_before, ...), custom_call_target="tpu_custom_call" | custom-call | flops 201326592 | bytes 1572864 | tf_op jit(solution)/shard_map/entry_parts/pallas_call | solution.py:504
  46.8 0.0 collective-permute-done.13.refs_2_
  46.8 0.6 %collective-permute-done.14.refs_3_ = bf16[256,256]{1,0:T(8,128)(2,1)S(1)} collective-permute-done((bf16[256,256]{1,0:T(8,128)(2,1)S(1)}, bf16[256,256]{1,0:T(8,128)(2,1)S(1)}, u32[]{:S(2)}, u32[]{:S(2)}) %collective-permute-start.14) | collective-permute-done | bytes 131104 | tf_op jit(solution)/shard_map/ppermute | solution.py:312
  47.4 0.6 %entry_parts.3 = bf16[768,128]{1,0:T(8,128)(2,1)S(1)} custom-call(bf16[384,1024]{1,0:T(8,128)(2,1)S(1)} %get-tuple-element.98.x_scaled, bf16[384,1024]{1,0:T(8,128)(2,1)S(1)} %get-tuple-element.99.dy_scaled, f32[384,128]{1,0:T(8,128)S(1)} %get-tuple-element.104.db_before, f32[384,128]{1,0:T(8,128)S(1)} %get-tuple-element.105.dc_before, ...), custom_call_target="tpu_custom_call" | custom-call | flops 201326592 | bytes 1572864 | tf_op jit(solution)/shard_map/entry_parts/pallas_call | solution.py:504
  47.9 0.1 collective-permute-start.18
  48.0 1.8 %entry_values.3 = (bf16[384,2048]{1,0:T(8,128)(2,1)}, f32[8,128]{1,0:T(8,128)}) custom-call(s32[1]{0:T(128)} %bitcast.where, bf16[384,1024]{1,0:T(8,128)(2,1)S(1)} %get-tuple-element.62.spread, bf16[384,128]{1,0:T(8,128)(2,1)S(1)} %get-tuple-element.58.refs_0_.b, bf16[384,1024]{1,0:T(8,128)(2,1)S(1)} %get-tuple-element.87.dx_local, ...), custom_call_target="tpu_custom_call", output_to_operand_aliasing={{0}: (8, {})} | custom-call | flops 100663296 | bytes 1572864 | tf_op jit(solution)/shard_map/entry_values/pallas_call | solution.py:538
  49.8 0.0 collective-permute-done.18
  49.8 0.1 add_convert_fusion
  49.9 0.7 %fusion = (bf16[384,128]{1,0:T(8,128)(2,1)}, bf16[384,128]{1,0:T(8,128)(2,1)}) fusion(bf16[768,128]{1,0:T(8,128)(2,1)S(1)} %add_convert_fusion), kind=kLoop, calls=%fused_computation.1 | loop fusion | bytes 393216 | tf_op jit(solution)/shard_map/slice | solution.py:606
  (5 shorter events, 0.0 us)
Async XLA Ops:
  3.9 9.6 %collective-permute-start = (bf16[272,256]{1,0:T(8,128)(2,1)S(1)}, bf16[272,256]{1,0:T(8,128)(2,1)S(1)}, u32[]{:S(2)}, u32[]{:S(2)}) collective-permute-start(bf16[272,256]{1,0:T(8,128)(2,1)S(1)} %get-tuple-element.73), channel_id=1, source_target_pairs={{0,6},{2,4},{4,2},{6,0},{8,14},{10,12},{12,10},{14,8},{16,22},{18,... | collective-permute-start | bytes 417800 | tf_op jit(solution)/shard_map/ppermute | solution.py:312
  7.9 8.2 %collective-permute-start.1 = (bf16[272,256]{1,0:T(8,128)(2,1)S(1)}, bf16[272,256]{1,0:T(8,128)(2,1)S(1)}, u32[]{:S(2)}, u32[]{:S(2)}) collective-permute-start(bf16[272,256]{1,0:T(8,128)(2,1)S(1)} %get-tuple-element.74), channel_id=1, source_target_pairs={{0,4},{2,6},{4,0},{6,2},{8,12},{10,14},{12,8},{14,10},{16,20},{18,... | collective-permute-start | bytes 417800 | tf_op jit(solution)/shard_map/ppermute | solution.py:312
  8.4 7.7 %collective-permute-start.2 = (bf16[272,256]{1,0:T(8,128)(2,1)S(1)}, bf16[272,256]{1,0:T(8,128)(2,1)S(1)}, u32[]{:S(2)}, u32[]{:S(2)}) collective-permute-start(bf16[272,256]{1,0:T(8,128)(2,1)S(1)} %get-tuple-element.75), channel_id=1, source_target_pairs={{0,2},{2,0},{4,6},{6,4},{8,10},{10,8},{12,14},{14,12},{16,18},{18,... | collective-permute-start | bytes 417800 | tf_op jit(solution)/shard_map/ppermute | solution.py:312
  10.1 10.3 %collective-permute-start.6 = (bf16[272,256]{1,0:T(8,128)(2,1)S(1)}, bf16[272,256]{1,0:T(8,128)(2,1)S(1)}, u32[]{:S(2)}, u32[]{:S(2)}) collective-permute-start(bf16[272,256]{1,0:T(8,128)(2,1)S(1)} %get-tuple-element.81), channel_id=1, source_target_pairs={{0,6},{2,4},{4,2},{6,0},{8,14},{10,12},{12,10},{14,8},{16,22},{18,... | collective-permute-start | bytes 417800 | tf_op jit(solution)/shard_map/ppermute | solution.py:312
  13.0 8.5 %collective-permute-start.7 = (bf16[272,256]{1,0:T(8,128)(2,1)S(1)}, bf16[272,256]{1,0:T(8,128)(2,1)S(1)}, u32[]{:S(2)}, u32[]{:S(2)}) collective-permute-start(bf16[272,256]{1,0:T(8,128)(2,1)S(1)} %get-tuple-element.82), channel_id=1, source_target_pairs={{0,4},{2,6},{4,0},{6,2},{8,12},{10,14},{12,8},{14,10},{16,20},{18,... | collective-permute-start | bytes 417800 | tf_op jit(solution)/shard_map/ppermute | solution.py:312
  13.5 8.0 %collective-permute-start.8 = (bf16[272,256]{1,0:T(8,128)(2,1)S(1)}, bf16[272,256]{1,0:T(8,128)(2,1)S(1)}, u32[]{:S(2)}, u32[]{:S(2)}) collective-permute-start(bf16[272,256]{1,0:T(8,128)(2,1)S(1)} %get-tuple-element.83), channel_id=1, source_target_pairs={{0,2},{2,0},{4,6},{6,4},{8,10},{10,8},{12,14},{14,12},{16,18},{18,... | collective-permute-start | bytes 417800 | tf_op jit(solution)/shard_map/ppermute | solution.py:312
  16.2 7.1 %collective-permute-start.3 = (bf16[144,256]{1,0:T(8,128)(2,1)S(1)}, bf16[144,256]{1,0:T(8,128)(2,1)S(1)}, u32[]{:S(2)}, u32[]{:S(2)}) collective-permute-start(bf16[144,256]{1,0:T(8,128)(2,1)S(1)} %get-tuple-element.76), channel_id=1, source_target_pairs={{0,8},{2,10},{4,12},{6,14},{8,0},{10,2},{12,4},{14,6},{16,24},{18,... | collective-permute-start | bytes 221192 | tf_op jit(solution)/shard_map/ppermute | solution.py:588
  17.9 7.2 %collective-permute-start.5 = (bf16[144,256]{1,0:T(8,128)(2,1)S(1)}, bf16[144,256]{1,0:T(8,128)(2,1)S(1)}, u32[]{:S(2)}, u32[]{:S(2)}) collective-permute-start(bf16[144,256]{1,0:T(8,128)(2,1)S(1)} %get-tuple-element.77), channel_id=1, source_target_pairs={{0,24},{2,26},{4,28},{6,30},{8,16},{10,18},{12,20},{14,22},{16,8},... | collective-permute-start | bytes 221192 | tf_op jit(solution)/shard_map/ppermute | solution.py:588
  20.3 7.1 %collective-permute-start.4 = (bf16[144,256]{1,0:T(8,128)(2,1)S(1)}, bf16[144,256]{1,0:T(8,128)(2,1)S(1)}, u32[]{:S(2)}, u32[]{:S(2)}) collective-permute-start(bf16[144,256]{1,0:T(8,128)(2,1)S(1)} %get-tuple-element.77), channel_id=1, source_target_pairs={{0,16},{2,18},{4,20},{6,22},{8,24},{10,26},{12,28},{14,30},{16,0},... | collective-permute-start | bytes 221192 | tf_op jit(solution)/shard_map/ppermute | solution.py:588
  21.7 11.3 %collective-permute-start.9 = (bf16[144,256]{1,0:T(8,128)(2,1)S(1)}, bf16[144,256]{1,0:T(8,128)(2,1)S(1)}, u32[]{:S(2)}, u32[]{:S(2)}) collective-permute-start(bf16[144,256]{1,0:T(8,128)(2,1)S(1)} %get-tuple-element.84), channel_id=1, source_target_pairs={{0,8},{2,10},{4,12},{6,14},{8,0},{10,2},{12,4},{14,6},{16,24},{18,... | collective-permute-start | bytes 221192 | tf_op jit(solution)/shard_map/ppermute | solution.py:588
  27.7 13.5 %collective-permute-start.15 = (bf16[256,256]{1,0:T(8,128)(2,1)S(1)}, bf16[256,256]{1,0:T(8,128)(2,1)S(1)}, u32[]{:S(2)}, u32[]{:S(2)}) collective-permute-start(bf16[256,256]{1,0:T(8,128)(2,1)S(1)} %get-tuple-element.93), channel_id=1, source_target_pairs={{0,6},{2,4},{4,2},{6,0},{8,14},{10,12},{12,10},{14,8},{16,22},{18,... | collective-permute-start | bytes 393224 | tf_op jit(solution)/shard_map/ppermute | solution.py:312
  29.8 7.3 %collective-permute-start.11 = (bf16[144,256]{1,0:T(8,128)(2,1)S(1)}, bf16[144,256]{1,0:T(8,128)(2,1)S(1)}, u32[]{:S(2)}, u32[]{:S(2)}) collective-permute-start(bf16[144,256]{1,0:T(8,128)(2,1)S(1)} %get-tuple-element.85), channel_id=1, source_target_pairs={{0,24},{2,26},{4,28},{6,30},{8,16},{10,18},{12,20},{14,22},{16,8},... | collective-permute-start | bytes 221192 | tf_op jit(solution)/shard_map/ppermute | solution.py:588
  31.5 6.0 %collective-permute-start.10 = (bf16[144,256]{1,0:T(8,128)(2,1)S(1)}, bf16[144,256]{1,0:T(8,128)(2,1)S(1)}, u32[]{:S(2)}, u32[]{:S(2)}) collective-permute-start(bf16[144,256]{1,0:T(8,128)(2,1)S(1)} %get-tuple-element.85), channel_id=1, source_target_pairs={{0,16},{2,18},{4,20},{6,22},{8,24},{10,26},{12,28},{14,30},{16,0},... | collective-permute-start | bytes 221192 | tf_op jit(solution)/shard_map/ppermute | solution.py:588
  31.5 13.4 %collective-permute-start.16 = (bf16[256,256]{1,0:T(8,128)(2,1)S(1)}, bf16[256,256]{1,0:T(8,128)(2,1)S(1)}, u32[]{:S(2)}, u32[]{:S(2)}) collective-permute-start(bf16[256,256]{1,0:T(8,128)(2,1)S(1)} %get-tuple-element.94), channel_id=1, source_target_pairs={{0,4},{2,6},{4,0},{6,2},{8,12},{10,14},{12,8},{14,10},{16,20},{18,... | collective-permute-start | bytes 393224 | tf_op jit(solution)/shard_map/ppermute | solution.py:312
  33.0 12.0 %collective-permute-start.17 = (bf16[256,256]{1,0:T(8,128)(2,1)S(1)}, bf16[256,256]{1,0:T(8,128)(2,1)S(1)}, u32[]{:S(2)}, u32[]{:S(2)}) collective-permute-start(bf16[256,256]{1,0:T(8,128)(2,1)S(1)} %get-tuple-element.95), channel_id=1, source_target_pairs={{0,2},{2,0},{4,6},{6,4},{8,10},{10,8},{12,14},{14,12},{16,18},{18,... | collective-permute-start | bytes 393224 | tf_op jit(solution)/shard_map/ppermute | solution.py:312
  37.9 8.9 %collective-permute-start.12 = (bf16[256,256]{1,0:T(8,128)(2,1)S(1)}, bf16[256,256]{1,0:T(8,128)(2,1)S(1)}, u32[]{:S(2)}, u32[]{:S(2)}) collective-permute-start(bf16[256,256]{1,0:T(8,128)(2,1)S(1)} %get-tuple-element.88), channel_id=1, source_target_pairs={{0,6},{2,4},{4,2},{6,0},{8,14},{10,12},{12,10},{14,8},{16,22},{18,... | collective-permute-start | bytes 393224 | tf_op jit(solution)/shard_map/ppermute | solution.py:312
  39.7 7.0 %collective-permute-start.13 = (bf16[256,256]{1,0:T(8,128)(2,1)S(1)}, bf16[256,256]{1,0:T(8,128)(2,1)S(1)}, u32[]{:S(2)}, u32[]{:S(2)}) collective-permute-start(bf16[256,256]{1,0:T(8,128)(2,1)S(1)} %get-tuple-element.89), channel_id=1, source_target_pairs={{0,4},{2,6},{4,0},{6,2},{8,12},{10,14},{12,8},{14,10},{16,20},{18,... | collective-permute-start | bytes 393224 | tf_op jit(solution)/shard_map/ppermute | solution.py:312
  41.2 6.2 %collective-permute-start.14 = (bf16[256,256]{1,0:T(8,128)(2,1)S(1)}, bf16[256,256]{1,0:T(8,128)(2,1)S(1)}, u32[]{:S(2)}, u32[]{:S(2)}) collective-permute-start(bf16[256,256]{1,0:T(8,128)(2,1)S(1)} %get-tuple-element.90), channel_id=1, source_target_pairs={{0,2},{2,0},{4,6},{6,4},{8,10},{10,8},{12,14},{14,12},{16,18},{18,... | collective-permute-start | bytes 393224 | tf_op jit(solution)/shard_map/ppermute | solution.py:312
  47.9 1.9 %collective-permute-start.18 = (bf16[768,128]{1,0:T(8,128)(2,1)S(1)}, bf16[768,128]{1,0:T(8,128)(2,1)S(1)}, u32[]{:S(2)}, u32[]{:S(2)}) collective-permute-start(bf16[768,128]{1,0:T(8,128)(2,1)S(1)} %entry_parts.3), channel_id=1, source_target_pairs={{0,1},{1,0},{2,3},{3,2},{4,5},{5,4},{6,7},{7,6},{8,9},{9,8},{10,11... | collective-permute-start | bytes 589832 | tf_op jit(solution)/shard_map/ppermute | solution.py:562

commit v8 on v7

--- a/solution.py
+++ b/solution.py
@@ -46,9 +46,21 @@
     return each + pltpu.roll(each, LANES - SLOT, 1) + pltpu.roll(each, LANES - 2 * SLOT, 1)
 
 
-def head_of_lane(head_dim, width, first):
+def split_of(index, size):
+    shift = size.bit_length() - 1
+    return lax.shift_right_logical(index, shift) if size == 1 << shift else index // size
+
+
+def row_less_head(head_dim, width, rows=LANES):
     shape = (LANES, width)
-    return jnp.where(iota(shape, 0) == first + iota(shape, 1) // head_dim, 1.0, 0.0).astype(BF16)
+    row = iota(shape, 0)
+    if rows < LANES:
+        row = row & (rows - 1)
+    return row - split_of(iota(shape, 1), head_dim)
+
+
+def head_of_lane(difference, first):
+    return jnp.where(difference == first, 1.0, 0.0).astype(BF16)
 
 
 def whole(count):
@@ -89,12 +101,15 @@
     return pl.ds(pl.multiple_of(start, part), part)
 
 
-def factors_of(ld):
+def masks_of(length):
+    rows, other = iota((length, length), 0), iota((length, length), 1)
+    after = jnp.where(other > rows, 1.0, 0.0).astype(BF16)
+    return after, jnp.where(other <= rows, 1.0, 0.0).astype(BF16)
+
+
+def factors_of(ld, after, until):
     length = ld.shape[1]
     terms = three(ld)
-    rows, other = iota((length, length), 0), iota((length, length), 1)
-    after = jnp.where(other > rows, 1.0, 0.0).astype(BF16)
-    until = jnp.where(other <= rows, 1.0, 0.0).astype(BF16)
     into_end = jnp.exp(summed(after, terms)).astype(BF16)
     from_start = jnp.exp(summed(until, terms)).astype(BF16)
     total = jnp.exp(summed(jnp.ones((TAIL, length), BF16), terms))
@@ -110,6 +125,7 @@
     width = x.shape[1]
     chunks = chunk_count(width)
     part = width // (group * chunks)
+    difference = row_less_head(head_dim, part)
     sides = [(into_end, b, x, x_scaled, 0), (from_start, c, dy, dy_scaled, state)]
     for side, (factors, proj, cols, scaled, first) in enumerate(sides):
         ready(side)
@@ -118,7 +134,7 @@
             here = slice(k * part, (k + 1) * part)
             lanes = chunk_lanes(where, k, chunk, part, width)
             first_head = ((place_of(where) ^ k) * chunks + chunk) * (part // head_dim)
-            hot = head_of_lane(head_dim, part, first_head)
+            hot = head_of_lane(difference, first_head)
             wide = dot(factors, hot, NN).astype(BF16)
             if side == 0:
                 spread[:, here] = wide
@@ -135,8 +151,9 @@
     copies = [pltpu.make_async_copy(i, o, sems.at[n]) for n, (i, o) in enumerate(pairs)]
     for copy in copies:
         copy.start()
+    masks = masks_of(ld.shape[1])
     copies[0].wait()
-    factors = factors_of(ld[...])
+    factors = factors_of(ld[...], *masks)
     for ref, value in zip((into_end, from_start, halves), factors):
         ref[...] = value
 
@@ -202,8 +219,8 @@
     ref[first:, :] = both.astype(BF16)
 
 
-def sent_order(parts):
-    return [parts[0], *parts[:0:-1]]
+def sent_order(parts, fixed=1):
+    return [*parts[:fixed], *parts[: fixed - 1 : -1]]
 
 
 def in_order(group, forward):
@@ -232,6 +249,8 @@
     factor = decay_of(blocks[0][2 * state :, :])
     for block in blocks[1:]:
         factor = factor * decay_of(block[2 * state :, :])
+    if not levels:
+        put_decay(sums, 2 * state, factor)
     for level, out in enumerate(outs):
         put_decay(out, state, factor)
         for forward in (True, False):
@@ -244,23 +263,55 @@
 def totals(state, levels, where, blocks, after):
     part = blocks[0].shape[1]
     outs = [jax.ShapeDtypeStruct((state + TAIL, part), BF16)] * levels
+    if not levels:
+        outs = [jax.ShapeDtypeStruct(blocks[0].shape, BF16)]
     return pl.pallas_call(
         functools.partial(totals_kernel, state, levels),
         out_shape=outs,
         in_specs=[SMEM] + whole(len(blocks)) + [ANY] * len(after),
-        out_specs=whole(levels),
-        scratch_shapes=[pltpu.VMEM((2 * state, part), BF16)],
+        out_specs=whole(len(outs)),
+        scratch_shapes=[pltpu.VMEM((2 * state, part), BF16)] if levels else [],
         compiler_params=params(4),
         cost_estimate=cost(8 * blocks[0].size, 10 * blocks[0].size),
         name="totals",
     )(where, *sent_order(blocks), *after)
 
 
-def members_kernel(state, groups, where, *refs):
-    received, refs = [None, *refs[: groups - 1]], refs[groups - 1 :]
-    group = GROUP
-    blocks, outs, entry = refs[:group], refs[-1 - group : -1], refs[-1]
-    number = where[0] // group
+def merged_kernel(state, level, last, where, own, received, *refs):
+    out = refs[-1]
+    d_own, d_other = decay_of(own[2 * state :, :]), decay_of(received[2 * state :, :])
+    upper = bit_of(where, level)
+    later = bit_of(where, level + 1)
+    for is_upper in (False, True):
+        for forward in (True, False):
+            chosen = upper == is_upper
+            if last:
+                chosen = chosen & (later != forward)
+
+            @pl.when(chosen)
+            def _(is_upper=is_upper, forward=forward):
+                rows = side_rows(state, forward)
+                mine, other = own[rows, :].astype(F32), received[rows, :].astype(F32)
+                value = mine + d_own * other if is_upper == forward else other + d_other * mine
+                out[slice(0, state) if last else rows, :] = value.astype(BF16)
+
+    put_decay(out, state if last else 2 * state, d_own * d_other)
+
+
+def merged(state, level, last, where, own, received, after):
+    rows = (state if last else 2 * state) + TAIL
+    return pl.pallas_call(
+        functools.partial(merged_kernel, state, level, last),
+        out_shape=pltpu.VMEM((rows, own.shape[1]), BF16),
+        in_specs=[SMEM] + whole(2) + [ANY] * len(after),
+        out_specs=whole(1)[0],
+        compiler_params=params(4),
+        cost_estimate=cost(4 * own.size, 6 * own.size),
+        name="merged",
+    )(where, own, received, *after)
+
+
+def put_direct(state, groups, number, received, entry):
     for mine in range(groups):
 
         @pl.when(number == mine)
@@ -270,13 +321,36 @@
                 others = range(mine - 1, -1, -1) if forward else range(mine + 1, groups)
                 value, factor = jnp.zeros((state, entry.shape[1]), F32), None
                 for other in others:
-                    r = received[mine ^ other]
+                    r = received[(mine ^ other) - 1]
                     piece = r[:state, :].astype(F32)
                     value = piece if factor is None else value + factor * piece
                     d = decay_of(r[state:, :])
                     factor = d if factor is None else factor * d
                 entry[rows, :] = value
 
+
+def put_rounds(state, where, received, entry):
+    for forward in (True, False):
+        value, factor = None, 1.0
+        for level, r in enumerate(received):
+            gets = bit_of(where, level) == forward
+            both = r.shape[0] > 2 * state
+            rows = side_rows(state, forward) if both else slice(0, state)
+            piece = r[rows, :].astype(F32) * jnp.where(gets, 1.0, 0.0)
+            value = piece if value is None else value + factor * piece
+            if both:
+                factor = factor * jnp.where(gets, decay_of(r[2 * state :, :]), 1.0)
+        entry[side_rows(state, forward), :] = value
+
+
+def members_kernel(state, direct, n_received, where, *refs):
+    received, refs = refs[:n_received], refs[n_received:]
+    group = GROUP
+    blocks, outs, entry = refs[:group], refs[-1 - group : -1], refs[-1]
+    if direct:
+        put_direct(state, n_received + 1, where[0] // group, received, entry)
+    else:
+        put_rounds(state, where, received, entry)
     for here in range(group):
 
         @pl.when(place_of(where) == here)
@@ -291,10 +365,10 @@
                         value = decays[q] * value + blocks[q ^ here][rows, :].astype(F32)
 
 
-def member_entries(state, where, blocks, received, after):
+def member_entries(state, direct, where, blocks, received, after):
     group, part = len(blocks), blocks[0].shape[1]
     return pl.pallas_call(
-        functools.partial(members_kernel, state, len(received) + 1),
+        functools.partial(members_kernel, state, direct, len(received)),
         out_shape=[jax.ShapeDtypeStruct((2 * state, part), BF16)] * group,
         in_specs=[SMEM] + whole(group + len(received)) + [ANY] * len(after),
         out_specs=whole(group),
@@ -391,15 +465,12 @@
     dx_out, db_out, dc_out, x_near, dy_near, *scratch = refs
     lefts, rights = scratch[: len(groups)], scratch[len(groups) :]
     part = dx_out.shape[1] // GROUP
+    difference = row_less_head(head_dim, part, SLOT)
 
     for m in range(GROUP):
         owned = m * (width // GROUP) + chunk * part
         lanes, here = slice(owned, owned + part), slice(m * part, (m + 1) * part)
-        shape = (LANES, part)
-        owner = owned // head_dim + iota(shape, 1) // head_dim
-        slot = lax.rem(iota(shape, 0), SLOT) == owner
-        hot = jnp.where(slot & (iota(shape, 0) < 3 * SLOT), 1.0, 0.0).astype(BF16)
-        cum = dot(cum_terms[...], hot, NN)
+        cum = dot(cum_terms[...], head_of_lane(difference, owned // head_dim), NN)
         dx = []
         for n in range(pieces):
             rows = rows_of(n, n + 1, piece)
@@ -438,7 +509,7 @@
         rows = rows_of(first, min(first + batch, pieces), piece)
         total = dot(x_near[rows, :], dy_near[rows, :], NT)
         row, col = iota(total.shape, 0), iota(total.shape, 1)
-        keep = (row // piece == col // piece) & (row <= col)
+        keep = (split_of(row, piece) == split_of(col, piece)) & (row <= col)
         weighted = jnp.where(keep, total, 0.0).astype(BF16)
         db_out[rows, :] += dot(weighted, c[rows, :], NN)
         dc_out[rows, :] += dot(weighted, b[rows, :], TN)
@@ -446,7 +517,8 @@
         total = dot(left_ref[...], right_ref[...], NT)
         if len(same) > 1:
             row, col = iota(total.shape, 0), iota(total.shape, 1)
-            total = jnp.where(row // (n_left * piece) == col // (n_right * piece), total, 0.0)
+            same_cut = split_of(row, n_left * piece) == split_of(col, n_right * piece)
+            total = jnp.where(same_cut, total, 0.0)
         weighted = total.astype(BF16)
         b_left = jnp.concatenate([b[rows_of(lo, mid, piece), :] for lo, mid, _ in same], axis=0)
         c_right = jnp.concatenate([c[rows_of(mid, hi, piece), :] for _, mid, hi in same], axis=0)
@@ -512,9 +584,11 @@
     )(x_scaled, dy_scaled, db_before, dc_before, *sent_order(entries), *after)
 
 
-def values_kernel(chunk, where, spread, b, dx_local, *refs):
-    entries, (out, done, dx, sems) = sent_order(refs[:GROUP]), refs[-4:]
-    done[...] = jnp.zeros_like(done)
+def values_kernel(chunk, last, where, spread, b, dx_local, *refs):
+    entries, (dx, sems) = sent_order(refs[:GROUP], 2 if last else 1), refs[-2:]
+    out = refs[-3 if last else -4]
+    if not last:
+        refs[-3][...] = jnp.zeros_like(refs[-3])
     state, part = b.shape[1], entries[0].shape[1]
     stores = []
     for k, entry in enumerate(entries):
@@ -533,16 +607,15 @@
 def entry_values(chunk, chunks, where, spread, b, dx_local, entries, before, after):
     group, part = len(entries), entries[0].shape[1]
     length, state = b.shape
-    size = dx_local.size
-    operands = [where, spread, b, dx_local, *sent_order(entries), *after, *before]
-    return pl.pallas_call(
-        functools.partial(values_kernel, chunk),
-        out_shape=[
-            pltpu.HBM((length, chunks * group * part), BF16),
-            pltpu.VMEM((8, LANES), F32),
-        ],
+    size, last = dx_local.size, chunk == chunks - 1
+    sent = sent_order(entries, 2 if last else 1)
+    operands = [where, spread, b, dx_local, *sent, *after, *before]
+    return pl.pallas_call(
+        functools.partial(values_kernel, chunk, last),
+        out_shape=[pltpu.HBM((length, chunks * group * part), BF16)]
+        + [pltpu.VMEM((8, LANES), F32)] * (not last),
         in_specs=[SMEM] + whole(3 + group) + [ANY] * len(after) + [HBM] * len(before),
-        out_specs=[HBM, *whole(1)],
+        out_specs=[HBM] + whole(0 if last else 1),
         input_output_aliases={len(operands) - 1: 0} if before else {},
         scratch_shapes=[
             pltpu.VMEM((group, length, part), BF16),
@@ -579,29 +652,31 @@
         blocks.append(exchange(states[chunk][3:]))
     setup = inner_setup(head_dim, ld, b, c, [states[-1][3]])
 
-    received = []
-    for chunk in range(chunks):
-        outs = totals(state, levels, where, blocks[chunk], setup[-1:] if chunk == 0 else [])
-        received.append([])
-        for k in range(1, count // group):
-            pairs = [(s, s ^ (k * group)) for s in range(count)]
-            received[chunk].append(lax.ppermute(outs[k.bit_length() - 1], "seq", pairs))
+    def to_group(block, k):
+        return lax.ppermute(block, "seq", [(s, s ^ (k * group)) for s in range(count)])
+
     entries, inner, sums = [], [], []
     for chunk in range(chunks):
-        found = member_entries(state, where, blocks[chunk], received[chunk], sums[:1])
+        (own,) = totals(state, 0, where, blocks[chunk], setup[-1:] if chunk == 0 else [])
+        received = [to_group(own, 1)]
+        for level in range(levels - 1):
+            last = level == levels - 2
+            own = merged(state, level, last, where, own, received[level], [])
+            received.append(to_group(own, 2 << level))
+        inner.append(inner_terms(head_dim, chunk, setup, b, c, x, dy, sums, [own]))
+        sums = list(inner[chunk][1:])
+        found = member_entries(state, False, where, blocks[chunk], received, sums[:1])
         entries.append(exchange(found))
-        inner.append(inner_terms(head_dim, chunk, setup, b, c, x, dy, sums, found[:1]))
-        sums = list(inner[chunk][1:])
 
     grad_values, done = [], []
     for chunk in range(chunks):
         x_scaled, dy_scaled, spread = states[chunk][:3]
         last = chunk == chunks - 1
         sums = entry_parts(last, x_scaled, dy_scaled, *sums, entries[chunk], done)
-        *grad_values, token = entry_values(
+        outs = entry_values(
             chunk, chunks, where, spread, b, inner[chunk][0], entries[chunk], grad_values, []
         )
-        done = [token]
+        grad_values, done = list(outs[:1]), list(outs[1:])
     both = over_heads(sums[0])
     return grad_values[0], both[:length], both[length:]
 

time: 50.8 us -> 49.2 us (0.969)
  starting transfers between devices: 25.4 us -> 23.9 us
  waiting for transfers between devices: 6.41 us -> 7.03 us
  Pallas kernels: 17.2 us -> 16.6 us
    ppermute x12, waiting for transfers between devices: 1.83 us -> 6.82 us  [exchange(): out[k] = lax.ppermute(parts[k], 'seq', [(s, s ^ k) for s in range(count)])]
    ppermute x6 -> x4, waiting for transfers between devices: 4.58 us -> 0.01 us  [to_group(): lax.ppermute(block, 'seq', [(s, s ^ k * group) for s in range(count)])]
    ppermute x6 -> x4, starting transfers between devices: 8.67 us -> 7.78 us  [to_group(): lax.ppermute(block, 'seq', [(s, s ^ k * group) for s in range(count)])]
    ppermute x12, starting transfers between devices: 16.7 us -> 16 us  [exchange(): out[k] = lax.ppermute(parts[k], 'seq', [(s, s ^ k) for s in range(count)])]
    pallas_call x4 -> x6, Pallas kernels: 3.54 us -> 2.89 us  [the longest x2 2.44 us: entry_values(): pl.pallas_call(functools.partial(values_kernel, chunk, last), out_shape=[...]
  transfers between devices with their start and end apart: 19 -> 17, of which waited for: 5 -> 8; matrix products, arithmetic and copies ran while one was open for 0% -> 0% of each run, Pallas kernels for 26% -> 26%
where the time goes in v8:
time: 49.2 us; the launch traced here: 49 us
  starting transfers between devices  23.9 us (49%)
  Pallas kernels  16.6 us (34%)
  waiting for transfers between devices  7.03 us (14%)
  between operations  0.78 us (2%)
  local copies, waits for them, and re-layouts  0.69 us (1%)
    ppermute x12, starting transfers between devices, exchange(): out[k] = lax.ppermute(parts[k], 'seq', [(s, s ^ k) for s in range(count)])  16 us
    ppermute x4, starting transfers between devices, to_group(): lax.ppermute(block, 'seq', [(s, s ^ k * group) for s in range(count)])  7.78 us
    pallas_call x2, Pallas kernels, inner_terms(): pl.pallas_call(functools.partial(inner_kernel, head_dim, chunk, len(befor...  7 us
    ppermute x12, waiting for transfers between devices, exchange(): out[k] = lax.ppermute(parts[k], 'seq', [(s, s ^ k) for s in range(count)])  6.82 us
    pallas_call x1, Pallas kernels, first_states(): pl.pallas_call(functools.partial(first_states_kernel, head_dim, group), o...  3.26 us
    pallas_call x2, Pallas kernels, entry_values(): pl.pallas_call(functools.partial(values_kernel, chunk, last), out_shape=[...  2.44 us
    pallas_call x1, Pallas kernels, next_states(): pl.pallas_call(functools.partial(next_states_kernel, head_dim, chunk), ou...  1.58 us
    pallas_call x2, Pallas kernels, entry_parts(): pl.pallas_call(functools.partial(parts_kernel, last), out_shape=outs, in_...  1.16 us
  transfers between devices with their start and end apart: 17, of which 8 were waited for; matrix products, arithmetic and copies ran while one was open for 0% of the time, Pallas kernels for 26%

profile of v8, /device:TPU:0, one launch (start us, length us, event | category | flops | bytes accessed | tf_op | source)
XLA Modules:
  0.0 49.0 jit_solution(14555858671598817989)
XLA Ops:
  0.6 3.3 %first_states.1 = (f32[32,384]{1,0:T(8,128)S(1)}, bf16[384,128]{1,0:T(8,128)(2,1)S(1)}, bf16[384,128]{1,0:T(8,128)(2,1)S(1)}, bf16[384,2048]{1,0:T(8,128)(2,1)S(...) custom-call(s32[1]{0:T(128)} %bitcast.where, ...), custom_call_target="tpu_custom_call" | custom-call | flops 402653184 | bytes 6291456 | tf_op jit(solution)/shard_map/first_states/pallas_call | solution.py:184
  3.9 4.0 %collective-permute-start = (bf16[272,256]{1,0:T(8,128)(2,1)S(1)}, bf16[272,256]{1,0:T(8,128)(2,1)S(1)}, u32[]{:S(2)}, u32[]{:S(2)}) collective-permute-start(bf16[272,256]{1,0:T(8,128)(2,1)S(1)} %get-tuple-element.68), channel_id=1, source_target_pairs={{0,6},{2,4},{4,2},{6,0},{8,14},{10,12},{12,10},{14,8},{16,22},{18,... | collective-permute-start | bytes 417800 | tf_op jit(solution)/shard_map/ppermute | solution.py:386
  7.9 0.5 %collective-permute-start.1 = (bf16[272,256]{1,0:T(8,128)(2,1)S(1)}, bf16[272,256]{1,0:T(8,128)(2,1)S(1)}, u32[]{:S(2)}, u32[]{:S(2)}) collective-permute-start(bf16[272,256]{1,0:T(8,128)(2,1)S(1)} %get-tuple-element.69), channel_id=1, source_target_pairs={{0,4},{2,6},{4,0},{6,2},{8,12},{10,14},{12,8},{14,10},{16,20},{18,... | collective-permute-start | bytes 417800 | tf_op jit(solution)/shard_map/ppermute | solution.py:386
  8.4 0.1 collective-permute-start.2
  8.5 1.6 %next_states.1 = (bf16[384,1024]{1,0:T(8,128)(2,1)S(1)}, bf16[384,1024]{1,0:T(8,128)(2,1)S(1)}, bf16[384,1024]{1,0:T(8,128)(2,1)S(1)}, bf16[272,256]{1,0:T(8,128...) custom-call(s32[1]{0:T(128)} %bitcast.where, ...), custom_call_target="tpu_custom_call" | custom-call | flops 402653184 | bytes 3145728 | tf_op jit(solution)/shard_map/next_states/pallas_call | solution.py:199
  10.1 2.9 %collective-permute-start.4 = (bf16[272,256]{1,0:T(8,128)(2,1)S(1)}, bf16[272,256]{1,0:T(8,128)(2,1)S(1)}, u32[]{:S(2)}, u32[]{:S(2)}) collective-permute-start(bf16[272,256]{1,0:T(8,128)(2,1)S(1)} %get-tuple-element.73), channel_id=1, source_target_pairs={{0,6},{2,4},{4,2},{6,0},{8,14},{10,12},{12,10},{14,8},{16,22},{18,... | collective-permute-start | bytes 417800 | tf_op jit(solution)/shard_map/ppermute | solution.py:386
  13.0 0.5 %collective-permute-start.5 = (bf16[272,256]{1,0:T(8,128)(2,1)S(1)}, bf16[272,256]{1,0:T(8,128)(2,1)S(1)}, u32[]{:S(2)}, u32[]{:S(2)}) collective-permute-start(bf16[272,256]{1,0:T(8,128)(2,1)S(1)} %get-tuple-element.74), channel_id=1, source_target_pairs={{0,4},{2,6},{4,0},{6,2},{8,12},{10,14},{12,8},{14,10},{16,20},{18,... | collective-permute-start | bytes 417800 | tf_op jit(solution)/shard_map/ppermute | solution.py:386
  13.5 0.0 collective-permute-done.refs_1_.refs_5_
  13.5 0.9 %collective-permute-start.6 = (bf16[272,256]{1,0:T(8,128)(2,1)S(1)}, bf16[272,256]{1,0:T(8,128)(2,1)S(1)}, u32[]{:S(2)}, u32[]{:S(2)}) collective-permute-start(bf16[272,256]{1,0:T(8,128)(2,1)S(1)} %get-tuple-element.75), channel_id=1, source_target_pairs={{0,2},{2,0},{4,6},{6,4},{8,10},{10,8},{12,14},{14,12},{16,18},{18,... | collective-permute-start | bytes 417800 | tf_op jit(solution)/shard_map/ppermute | solution.py:386
  14.4 0.5 inner_setup.1
  14.8 1.2 %collective-permute-done.1.refs_2_.refs_4_ = bf16[272,256]{1,0:T(8,128)(2,1)S(1)} collective-permute-done((bf16[272,256]{1,0:T(8,128)(2,1)S(1)}, bf16[272,256]{1,0:T(8,128)(2,1)S(1)}, u32[]{:S(2)}, u32[]{:S(2)}) %collective-permute-start.1) | collective-permute-done | bytes 139296 | tf_op jit(solution)/shard_map/ppermute | solution.py:386
  16.1 0.0 collective-permute-done.2.refs_3_
  16.1 0.1 totals.2.own
  16.2 1.6 %collective-permute-start.3 = (bf16[272,256]{1,0:T(8,128)(2,1)S(1)}, bf16[272,256]{1,0:T(8,128)(2,1)S(1)}, u32[]{:S(2)}, u32[]{:S(2)}) collective-permute-start(bf16[272,256]{1,0:T(8,128)(2,1)S(1)} %totals.2.own), channel_id=1, source_target_pairs={{0,8},{2,10},{4,12},{6,14},{8,0},{10,2},{12,4},{14,6},{16,24},{18,... | collective-permute-start | bytes 417800 | tf_op jit(solution)/shard_map/ppermute | solution.py:656
  17.8 1.1 %collective-permute-done.4.refs_1_.refs_5_ = bf16[272,256]{1,0:T(8,128)(2,1)S(1)} collective-permute-done((bf16[272,256]{1,0:T(8,128)(2,1)S(1)}, bf16[272,256]{1,0:T(8,128)(2,1)S(1)}, u32[]{:S(2)}, u32[]{:S(2)}) %collective-permute-start.4) | collective-permute-done | bytes 139296 | tf_op jit(solution)/shard_map/ppermute | solution.py:386
  18.9 1.6 %collective-permute-done.5.refs_2_.refs_4_ = bf16[272,256]{1,0:T(8,128)(2,1)S(1)} collective-permute-done((bf16[272,256]{1,0:T(8,128)(2,1)S(1)}, bf16[272,256]{1,0:T(8,128)(2,1)S(1)}, u32[]{:S(2)}, u32[]{:S(2)}) %collective-permute-start.5) | collective-permute-done | bytes 139296 | tf_op jit(solution)/shard_map/ppermute | solution.py:386
  20.5 0.3 collective-permute-done.6.refs_3_
  20.8 0.1 totals.3.own
  20.9 1.6 %collective-permute-start.7 = (bf16[272,256]{1,0:T(8,128)(2,1)S(1)}, bf16[272,256]{1,0:T(8,128)(2,1)S(1)}, u32[]{:S(2)}, u32[]{:S(2)}) collective-permute-start(bf16[272,256]{1,0:T(8,128)(2,1)S(1)} %totals.3.own), channel_id=1, source_target_pairs={{0,8},{2,10},{4,12},{6,14},{8,0},{10,2},{12,4},{14,6},{16,24},{18,... | collective-permute-start | bytes 417800 | tf_op jit(solution)/shard_map/ppermute | solution.py:656
  22.5 0.0 collective-permute-done.3.received.refs_0_
  22.6 2.6 %collective-permute-start.12 = (bf16[144,256]{1,0:T(8,128)(2,1)S(1)}, bf16[144,256]{1,0:T(8,128)(2,1)S(1)}, u32[]{:S(2)}, u32[]{:S(2)}) collective-permute-start(bf16[144,256]{1,0:T(8,128)(2,1)S(1)} %merged.2.refs_7_), channel_id=1, source_target_pairs={{0,16},{2,18},{4,20},{6,22},{8,24},{10,26},{12,28},{14,30},{16,0},... | collective-permute-start | bytes 221192 | tf_op jit(solution)/shard_map/ppermute | solution.py:656
  25.2 3.5 %inner_terms.2 = (bf16[384,1024]{1,0:T(8,128)(2,1)S(1)}, f32[384,128]{1,0:T(8,128)S(1)}, f32[384,128]{1,0:T(8,128)S(1)}) custom-call(bf16[384,128]{1,0:T(8,128)(2,1)S(1)} %get-tuple-element.53.refs_0_.b, bf16[384,128]{1,0:T(8,128)(2,1)S(1)} %get-tuple-element.54.refs_1_.c, bf16[384,2048]{1,0:T(8,128)(2,1)S(1)} %get-tuple-element.55.refs_2_.x, ...), custom_call_target="tpu_custom_call" | custom-call | flops 805306368 | bytes 3145728 | tf_op jit(solution)/shard_map/inner_terms/pallas_call | solution.py:537
  28.7 0.0 collective-permute-done.12.refs_1_
  28.8 0.2 member_entries.3
  28.9 2.0 %collective-permute-start.13 = (bf16[256,256]{1,0:T(8,128)(2,1)S(1)}, bf16[256,256]{1,0:T(8,128)(2,1)S(1)}, u32[]{:S(2)}, u32[]{:S(2)}) collective-permute-start(bf16[256,256]{1,0:T(8,128)(2,1)S(1)} %get-tuple-element.85), channel_id=1, source_target_pairs={{0,6},{2,4},{4,2},{6,0},{8,14},{10,12},{12,10},{14,8},{16,22},{18,... | collective-permute-start | bytes 393224 | tf_op jit(solution)/shard_map/ppermute | solution.py:386
  30.9 0.0 collective-permute-done.7.received.refs_0_
  31.0 1.9 %collective-permute-start.8 = (bf16[144,256]{1,0:T(8,128)(2,1)S(1)}, bf16[144,256]{1,0:T(8,128)(2,1)S(1)}, u32[]{:S(2)}, u32[]{:S(2)}) collective-permute-start(bf16[144,256]{1,0:T(8,128)(2,1)S(1)} %merged.3.refs_9_), channel_id=1, source_target_pairs={{0,16},{2,18},{4,20},{6,22},{8,24},{10,26},{12,28},{14,30},{16,0},... | collective-permute-start | bytes 221192 | tf_op jit(solution)/shard_map/ppermute | solution.py:656
  32.9 1.1 %collective-permute-start.14 = (bf16[256,256]{1,0:T(8,128)(2,1)S(1)}, bf16[256,256]{1,0:T(8,128)(2,1)S(1)}, u32[]{:S(2)}, u32[]{:S(2)}) collective-permute-start(bf16[256,256]{1,0:T(8,128)(2,1)S(1)} %get-tuple-element.86), channel_id=1, source_target_pairs={{0,4},{2,6},{4,0},{6,2},{8,12},{10,14},{12,8},{14,10},{16,20},{18,... | collective-permute-start | bytes 393224 | tf_op jit(solution)/shard_map/ppermute | solution.py:386
  33.9 0.5 collective-permute-start.15
  34.4 3.5 %inner_terms.3 = (bf16[384,1024]{1,0:T(8,128)(2,1)S(1)}, f32[384,128]{1,0:T(8,128)S(1)}, f32[384,128]{1,0:T(8,128)S(1)}) custom-call(bf16[384,128]{1,0:T(8,128)(2,1)S(1)} %get-tuple-element.53.refs_0_.b, bf16[384,128]{1,0:T(8,128)(2,1)S(1)} %get-tuple-element.54.refs_1_.c, bf16[384,2048]{1,0:T(8,128)(2,1)S(1)} %get-tuple-element.55.refs_2_.x, ...), custom_call_target="tpu_custom_call" | custom-call | flops 805306368 | bytes 3145728 | tf_op jit(solution)/shard_map/inner_terms/pallas_call | solution.py:537
  37.9 0.0 collective-permute-done.8.refs_1_
  37.9 0.2 member_entries.2
  38.1 2.0 %collective-permute-start.10 = (bf16[256,256]{1,0:T(8,128)(2,1)S(1)}, bf16[256,256]{1,0:T(8,128)(2,1)S(1)}, u32[]{:S(2)}, u32[]{:S(2)}) collective-permute-start(bf16[256,256]{1,0:T(8,128)(2,1)S(1)} %get-tuple-element.80), channel_id=1, source_target_pairs={{0,6},{2,4},{4,2},{6,0},{8,14},{10,12},{12,10},{14,8},{16,22},{18,... | collective-permute-start | bytes 393224 | tf_op jit(solution)/shard_map/ppermute | solution.py:386
  40.1 1.1 %collective-permute-start.11 = (bf16[256,256]{1,0:T(8,128)(2,1)S(1)}, bf16[256,256]{1,0:T(8,128)(2,1)S(1)}, u32[]{:S(2)}, u32[]{:S(2)}) collective-permute-start(bf16[256,256]{1,0:T(8,128)(2,1)S(1)} %get-tuple-element.81), channel_id=1, source_target_pairs={{0,4},{2,6},{4,0},{6,2},{8,12},{10,14},{12,8},{14,10},{16,20},{18,... | collective-permute-start | bytes 393224 | tf_op jit(solution)/shard_map/ppermute | solution.py:386
  41.2 0.5 collective-permute-start.9
  41.7 0.0 collective-permute-done.14.refs_2_
  41.7 0.0 collective-permute-done.15.refs_3_
  41.7 1.2 %entry_values.2 = (bf16[384,2048]{1,0:T(8,128)(2,1)}, f32[8,128]{1,0:T(8,128)S(1)}) custom-call(s32[1]{0:T(128)} %bitcast.where, bf16[384,1024]{1,0:T(8,128)(2,1)S(1)} %get-tuple-element.82.spread, bf16[384,128]{1,0:T(8,128)(2,1)S(1)} %get-tuple-element.53.refs_0_.b, bf16[384,1024]{1,0:T(8,128)(2,1)S(1)} %get-tuple-element.83.dx_local, ...), custom_call_target="tpu_custom_call" | custom-call | flops 100663296 | bytes 1572864 | tf_op jit(solution)/shard_map/entry_values/pallas_call | solution.py:613
  42.9 0.6 %entry_parts.2 = (f32[384,128]{1,0:T(8,128)S(1)}, f32[384,128]{1,0:T(8,128)S(1)}) custom-call(bf16[384,1024]{1,0:T(8,128)(2,1)S(1)} %get-tuple-element.91.x_scaled, bf16[384,1024]{1,0:T(8,128)(2,1)S(1)} %get-tuple-element.92.dy_scaled, f32[384,128]{1,0:T(8,128)S(1)} %get-tuple-element.77.refs_6_.db_before, f32[384,128]{1,0:T(8,128)S(1)} %get-tuple-element.93.dc_before, ...), custom_call_target="tpu_custom_call" | custom-call | flops 201326592 | bytes 1572864 | tf_op jit(solution)/shard_map/entry_parts/pallas_call | solution.py:576
  43.5 0.6 %collective-permute-done.10.refs_2_.refs_1_ = bf16[256,256]{1,0:T(8,128)(2,1)S(1)} collective-permute-done((bf16[256,256]{1,0:T(8,128)(2,1)S(1)}, bf16[256,256]{1,0:T(8,128)(2,1)S(1)}, u32[]{:S(2)}, u32[]{:S(2)}) %collective-permute-start.10) | collective-permute-done | bytes 131104 | tf_op jit(solution)/shard_map/ppermute | solution.py:386
  44.1 1.4 %collective-permute-done.11.refs_3_.refs_2_ = bf16[256,256]{1,0:T(8,128)(2,1)S(1)} collective-permute-done((bf16[256,256]{1,0:T(8,128)(2,1)S(1)}, bf16[256,256]{1,0:T(8,128)(2,1)S(1)}, u32[]{:S(2)}, u32[]{:S(2)}) %collective-permute-start.11) | collective-permute-done | bytes 131104 | tf_op jit(solution)/shard_map/ppermute | solution.py:386
  45.5 0.7 %collective-permute-done.9.refs_1_.refs_3_ = bf16[256,256]{1,0:T(8,128)(2,1)S(1)} collective-permute-done((bf16[256,256]{1,0:T(8,128)(2,1)S(1)}, bf16[256,256]{1,0:T(8,128)(2,1)S(1)}, u32[]{:S(2)}, u32[]{:S(2)}) %collective-permute-start.9) | collective-permute-done | bytes 131104 | tf_op jit(solution)/shard_map/ppermute | solution.py:386
  46.2 0.6 %entry_parts.3 = bf16[768,128]{1,0:T(8,128)(2,1)S(1)} custom-call(bf16[384,1024]{1,0:T(8,128)(2,1)S(1)} %get-tuple-element.89.x_scaled, bf16[384,1024]{1,0:T(8,128)(2,1)S(1)} %get-tuple-element.90.dy_scaled, f32[384,128]{1,0:T(8,128)S(1)} %get-tuple-element.94.db_before, f32[384,128]{1,0:T(8,128)S(1)} %get-tuple-element.95.dc_before, ...), custom_call_target="tpu_custom_call" | custom-call | flops 201326592 | bytes 1572864 | tf_op jit(solution)/shard_map/entry_parts/pallas_call | solution.py:576
  46.8 0.1 collective-permute-start.16
  46.8 1.2 %entry_values.3 = bf16[384,2048]{1,0:T(8,128)(2,1)} custom-call(s32[1]{0:T(128)} %bitcast.where, bf16[384,1024]{1,0:T(8,128)(2,1)S(1)} %get-tuple-element.57.spread, bf16[384,128]{1,0:T(8,128)(2,1)S(1)} %get-tuple-element.53.refs_0_.b, bf16[384,1024]{1,0:T(8,128)(2,1)S(1)} %get-tuple-element.76.dx_local, ...), custom_call_target="tpu_custom_call", output_to_operand_aliasing={{}: (8, {})} | custom-call | flops 100663296 | bytes 1572864 | tf_op jit(solution)/shard_map/entry_values/pallas_call | solution.py:613
  48.1 0.2 collective-permute-done.16
  48.3 0.1 add_convert_fusion
  48.3 0.7 %fusion = (bf16[384,128]{1,0:T(8,128)(2,1)}, bf16[384,128]{1,0:T(8,128)(2,1)}) fusion(bf16[768,128]{1,0:T(8,128)(2,1)S(1)} %add_convert_fusion), kind=kLoop, calls=%fused_computation.1 | loop fusion | bytes 393216 | tf_op jit(solution)/shard_map/slice | solution.py:681
  (3 shorter events, 0.1 us)
Async XLA Ops:
  3.9 9.6 %collective-permute-start = (bf16[272,256]{1,0:T(8,128)(2,1)S(1)}, bf16[272,256]{1,0:T(8,128)(2,1)S(1)}, u32[]{:S(2)}, u32[]{:S(2)}) collective-permute-start(bf16[272,256]{1,0:T(8,128)(2,1)S(1)} %get-tuple-element.68), channel_id=1, source_target_pairs={{0,6},{2,4},{4,2},{6,0},{8,14},{10,12},{12,10},{14,8},{16,22},{18,... | collective-permute-start | bytes 417800 | tf_op jit(solution)/shard_map/ppermute | solution.py:386
  7.9 8.2 %collective-permute-start.1 = (bf16[272,256]{1,0:T(8,128)(2,1)S(1)}, bf16[272,256]{1,0:T(8,128)(2,1)S(1)}, u32[]{:S(2)}, u32[]{:S(2)}) collective-permute-start(bf16[272,256]{1,0:T(8,128)(2,1)S(1)} %get-tuple-element.69), channel_id=1, source_target_pairs={{0,4},{2,6},{4,0},{6,2},{8,12},{10,14},{12,8},{14,10},{16,20},{18,... | collective-permute-start | bytes 417800 | tf_op jit(solution)/shard_map/ppermute | solution.py:386
  8.4 7.7 %collective-permute-start.2 = (bf16[272,256]{1,0:T(8,128)(2,1)S(1)}, bf16[272,256]{1,0:T(8,128)(2,1)S(1)}, u32[]{:S(2)}, u32[]{:S(2)}) collective-permute-start(bf16[272,256]{1,0:T(8,128)(2,1)S(1)} %get-tuple-element.70), channel_id=1, source_target_pairs={{0,2},{2,0},{4,6},{6,4},{8,10},{10,8},{12,14},{14,12},{16,18},{18,... | collective-permute-start | bytes 417800 | tf_op jit(solution)/shard_map/ppermute | solution.py:386
  10.1 8.8 %collective-permute-start.4 = (bf16[272,256]{1,0:T(8,128)(2,1)S(1)}, bf16[272,256]{1,0:T(8,128)(2,1)S(1)}, u32[]{:S(2)}, u32[]{:S(2)}) collective-permute-start(bf16[272,256]{1,0:T(8,128)(2,1)S(1)} %get-tuple-element.73), channel_id=1, source_target_pairs={{0,6},{2,4},{4,2},{6,0},{8,14},{10,12},{12,10},{14,8},{16,22},{18,... | collective-permute-start | bytes 417800 | tf_op jit(solution)/shard_map/ppermute | solution.py:386
  13.0 7.5 %collective-permute-start.5 = (bf16[272,256]{1,0:T(8,128)(2,1)S(1)}, bf16[272,256]{1,0:T(8,128)(2,1)S(1)}, u32[]{:S(2)}, u32[]{:S(2)}) collective-permute-start(bf16[272,256]{1,0:T(8,128)(2,1)S(1)} %get-tuple-element.74), channel_id=1, source_target_pairs={{0,4},{2,6},{4,0},{6,2},{8,12},{10,14},{12,8},{14,10},{16,20},{18,... | collective-permute-start | bytes 417800 | tf_op jit(solution)/shard_map/ppermute | solution.py:386
  13.5 7.2 %collective-permute-start.6 = (bf16[272,256]{1,0:T(8,128)(2,1)S(1)}, bf16[272,256]{1,0:T(8,128)(2,1)S(1)}, u32[]{:S(2)}, u32[]{:S(2)}) collective-permute-start(bf16[272,256]{1,0:T(8,128)(2,1)S(1)} %get-tuple-element.75), channel_id=1, source_target_pairs={{0,2},{2,0},{4,6},{6,4},{8,10},{10,8},{12,14},{14,12},{16,18},{18,... | collective-permute-start | bytes 417800 | tf_op jit(solution)/shard_map/ppermute | solution.py:386
  16.2 6.3 %collective-permute-start.3 = (bf16[272,256]{1,0:T(8,128)(2,1)S(1)}, bf16[272,256]{1,0:T(8,128)(2,1)S(1)}, u32[]{:S(2)}, u32[]{:S(2)}) collective-permute-start(bf16[272,256]{1,0:T(8,128)(2,1)S(1)} %totals.2.own), channel_id=1, source_target_pairs={{0,8},{2,10},{4,12},{6,14},{8,0},{10,2},{12,4},{14,6},{16,24},{18,... | collective-permute-start | bytes 417800 | tf_op jit(solution)/shard_map/ppermute | solution.py:656
  20.9 10.1 %collective-permute-start.7 = (bf16[272,256]{1,0:T(8,128)(2,1)S(1)}, bf16[272,256]{1,0:T(8,128)(2,1)S(1)}, u32[]{:S(2)}, u32[]{:S(2)}) collective-permute-start(bf16[272,256]{1,0:T(8,128)(2,1)S(1)} %totals.3.own), channel_id=1, source_target_pairs={{0,8},{2,10},{4,12},{6,14},{8,0},{10,2},{12,4},{14,6},{16,24},{18,... | collective-permute-start | bytes 417800 | tf_op jit(solution)/shard_map/ppermute | solution.py:656
  22.6 6.2 %collective-permute-start.12 = (bf16[144,256]{1,0:T(8,128)(2,1)S(1)}, bf16[144,256]{1,0:T(8,128)(2,1)S(1)}, u32[]{:S(2)}, u32[]{:S(2)}) collective-permute-start(bf16[144,256]{1,0:T(8,128)(2,1)S(1)} %merged.2.refs_7_), channel_id=1, source_target_pairs={{0,16},{2,18},{4,20},{6,22},{8,24},{10,26},{12,28},{14,30},{16,0},... | collective-permute-start | bytes 221192 | tf_op jit(solution)/shard_map/ppermute | solution.py:656
  28.9 12.3 %collective-permute-start.13 = (bf16[256,256]{1,0:T(8,128)(2,1)S(1)}, bf16[256,256]{1,0:T(8,128)(2,1)S(1)}, u32[]{:S(2)}, u32[]{:S(2)}) collective-permute-start(bf16[256,256]{1,0:T(8,128)(2,1)S(1)} %get-tuple-element.85), channel_id=1, source_target_pairs={{0,6},{2,4},{4,2},{6,0},{8,14},{10,12},{12,10},{14,8},{16,22},{18,... | collective-permute-start | bytes 393224 | tf_op jit(solution)/shard_map/ppermute | solution.py:386
  31.0 6.9 %collective-permute-start.8 = (bf16[144,256]{1,0:T(8,128)(2,1)S(1)}, bf16[144,256]{1,0:T(8,128)(2,1)S(1)}, u32[]{:S(2)}, u32[]{:S(2)}) collective-permute-start(bf16[144,256]{1,0:T(8,128)(2,1)S(1)} %merged.3.refs_9_), channel_id=1, source_target_pairs={{0,16},{2,18},{4,20},{6,22},{8,24},{10,26},{12,28},{14,30},{16,0},... | collective-permute-start | bytes 221192 | tf_op jit(solution)/shard_map/ppermute | solution.py:656
  32.9 8.8 %collective-permute-start.14 = (bf16[256,256]{1,0:T(8,128)(2,1)S(1)}, bf16[256,256]{1,0:T(8,128)(2,1)S(1)}, u32[]{:S(2)}, u32[]{:S(2)}) collective-permute-start(bf16[256,256]{1,0:T(8,128)(2,1)S(1)} %get-tuple-element.86), channel_id=1, source_target_pairs={{0,4},{2,6},{4,0},{6,2},{8,12},{10,14},{12,8},{14,10},{16,20},{18,... | collective-permute-start | bytes 393224 | tf_op jit(solution)/shard_map/ppermute | solution.py:386
  33.9 7.7 %collective-permute-start.15 = (bf16[256,256]{1,0:T(8,128)(2,1)S(1)}, bf16[256,256]{1,0:T(8,128)(2,1)S(1)}, u32[]{:S(2)}, u32[]{:S(2)}) collective-permute-start(bf16[256,256]{1,0:T(8,128)(2,1)S(1)} %get-tuple-element.87), channel_id=1, source_target_pairs={{0,2},{2,0},{4,6},{6,4},{8,10},{10,8},{12,14},{14,12},{16,18},{18,... | collective-permute-start | bytes 393224 | tf_op jit(solution)/shard_map/ppermute | solution.py:386
  38.1 6.0 %collective-permute-start.10 = (bf16[256,256]{1,0:T(8,128)(2,1)S(1)}, bf16[256,256]{1,0:T(8,128)(2,1)S(1)}, u32[]{:S(2)}, u32[]{:S(2)}) collective-permute-start(bf16[256,256]{1,0:T(8,128)(2,1)S(1)} %get-tuple-element.80), channel_id=1, source_target_pairs={{0,6},{2,4},{4,2},{6,0},{8,14},{10,12},{12,10},{14,8},{16,22},{18,... | collective-permute-start | bytes 393224 | tf_op jit(solution)/shard_map/ppermute | solution.py:386
  40.1 5.4 %collective-permute-start.11 = (bf16[256,256]{1,0:T(8,128)(2,1)S(1)}, bf16[256,256]{1,0:T(8,128)(2,1)S(1)}, u32[]{:S(2)}, u32[]{:S(2)}) collective-permute-start(bf16[256,256]{1,0:T(8,128)(2,1)S(1)} %get-tuple-element.81), channel_id=1, source_target_pairs={{0,4},{2,6},{4,0},{6,2},{8,12},{10,14},{12,8},{14,10},{16,20},{18,... | collective-permute-start | bytes 393224 | tf_op jit(solution)/shard_map/ppermute | solution.py:386
  41.2 5.0 %collective-permute-start.9 = (bf16[256,256]{1,0:T(8,128)(2,1)S(1)}, bf16[256,256]{1,0:T(8,128)(2,1)S(1)}, u32[]{:S(2)}, u32[]{:S(2)}) collective-permute-start(bf16[256,256]{1,0:T(8,128)(2,1)S(1)} %get-tuple-element.79), channel_id=1, source_target_pairs={{0,2},{2,0},{4,6},{6,4},{8,10},{10,8},{12,14},{14,12},{16,18},{18,... | collective-permute-start | bytes 393224 | tf_op jit(solution)/shard_map/ppermute | solution.py:386
  46.8 1.5 %collective-permute-start.16 = (bf16[768,128]{1,0:T(8,128)(2,1)S(1)}, bf16[768,128]{1,0:T(8,128)(2,1)S(1)}, u32[]{:S(2)}, u32[]{:S(2)}) collective-permute-start(bf16[768,128]{1,0:T(8,128)(2,1)S(1)} %entry_parts.3), channel_id=1, source_target_pairs={{0,1},{1,0},{2,3},{3,2},{4,5},{5,4},{6,7},{7,6},{8,9},{9,8},{10,11... | collective-permute-start | bytes 589832 | tf_op jit(solution)/shard_map/ppermute | solution.py:635

commit v9 on v8

--- a/solution.py
+++ b/solution.py
@@ -231,9 +231,9 @@
     return slice(0, state) if forward else slice(state, 2 * state)
 
 
-def totals_kernel(state, levels, where, *refs):
+def totals_kernel(state, groups, where, *refs):
     group = GROUP
-    blocks, outs, sums = sent_order(refs[:group]), refs[-1 - levels : -1], refs[-1]
+    blocks, out, sums = sent_order(refs[:group]), refs[-2 if groups else -1], refs[-1]
     for here in range(group):
 
         @pl.when(place_of(where) == here)
@@ -249,28 +249,27 @@
     factor = decay_of(blocks[0][2 * state :, :])
     for block in blocks[1:]:
         factor = factor * decay_of(block[2 * state :, :])
-    if not levels:
+    if not groups:
         put_decay(sums, 2 * state, factor)
-    for level, out in enumerate(outs):
-        put_decay(out, state, factor)
+    for other in range(groups):
+        put_decay(out.at[other], state, factor)
+        later = where[0] // group < other
         for forward in (True, False):
 
-            @pl.when(bit_of(where, level) != forward)
-            def _(out=out, forward=forward):
-                out[:state, :] = sums[side_rows(state, forward), :]
-
-
-def totals(state, levels, where, blocks, after):
+            @pl.when(later == forward)
+            def _(other=other, forward=forward):
+                out[other, :state, :] = sums[side_rows(state, forward), :]
+
+
+def totals(state, groups, where, blocks, after):
     part = blocks[0].shape[1]
-    outs = [jax.ShapeDtypeStruct((state + TAIL, part), BF16)] * levels
-    if not levels:
-        outs = [jax.ShapeDtypeStruct(blocks[0].shape, BF16)]
-    return pl.pallas_call(
-        functools.partial(totals_kernel, state, levels),
-        out_shape=outs,
+    shape = (groups, state + TAIL, part) if groups else blocks[0].shape
+    return pl.pallas_call(
+        functools.partial(totals_kernel, state, groups),
+        out_shape=jax.ShapeDtypeStruct(shape, BF16),
         in_specs=[SMEM] + whole(len(blocks)) + [ANY] * len(after),
-        out_specs=whole(len(outs)),
-        scratch_shapes=[pltpu.VMEM((2 * state, part), BF16)] if levels else [],
+        out_specs=whole(1)[0],
+        scratch_shapes=[pltpu.VMEM((2 * state, part), BF16)] if groups else [],
         compiler_params=params(4),
         cost_estimate=cost(8 * blocks[0].size, 10 * blocks[0].size),
         name="totals",
@@ -311,22 +310,21 @@
     )(where, own, received, *after)
 
 
-def put_direct(state, groups, number, received, entry):
+def put_direct(state, number, received, entry):
+    groups = received.shape[0]
     for mine in range(groups):
 
         @pl.when(number == mine)
         def _(mine=mine):
             for forward in (True, False):
-                rows = side_rows(state, forward)
                 others = range(mine - 1, -1, -1) if forward else range(mine + 1, groups)
                 value, factor = jnp.zeros((state, entry.shape[1]), F32), None
                 for other in others:
-                    r = received[(mine ^ other) - 1]
-                    piece = r[:state, :].astype(F32)
+                    piece = received[other, :state, :].astype(F32)
                     value = piece if factor is None else value + factor * piece
-                    d = decay_of(r[state:, :])
+                    d = decay_of(received[other, state:, :])
                     factor = d if factor is None else factor * d
-                entry[rows, :] = value
+                entry[side_rows(state, forward), :] = value
 
 
 def put_rounds(state, where, received, entry):
@@ -348,7 +346,7 @@
     group = GROUP
     blocks, outs, entry = refs[:group], refs[-1 - group : -1], refs[-1]
     if direct:
-        put_direct(state, n_received + 1, where[0] // group, received, entry)
+        put_direct(state, where[0] // group, received[0], entry)
     else:
         put_rounds(state, where, received, entry)
     for here in range(group):
@@ -655,17 +653,24 @@
     def to_group(block, k):
         return lax.ppermute(block, "seq", [(s, s ^ (k * group)) for s in range(count)])
 
-    entries, inner, sums = [], [], []
+    groups = count // group
+    columns = [[n * group + j for n in range(groups)] for j in range(group)]
+    entries, inner, sums, after = [], [], [], setup[-1:]
     for chunk in range(chunks):
-        (own,) = totals(state, 0, where, blocks[chunk], setup[-1:] if chunk == 0 else [])
-        received = [to_group(own, 1)]
-        for level in range(levels - 1):
-            last = level == levels - 2
-            own = merged(state, level, last, where, own, received[level], [])
-            received.append(to_group(own, 2 << level))
+        direct = chunk == 0 and chunks > 1
+        own = totals(state, groups * direct, where, blocks[chunk], after)
+        after = [own]
+        if direct:
+            received = [lax.all_to_all(own, "seq", 0, 0, axis_index_groups=columns, tiled=True)]
+        else:
+            received = [to_group(own, 1)]
+            for level in range(levels - 1):
+                last = level == levels - 2
+                own = merged(state, level, last, where, own, received[level], [])
+                received.append(to_group(own, 2 << level))
         inner.append(inner_terms(head_dim, chunk, setup, b, c, x, dy, sums, [own]))
         sums = list(inner[chunk][1:])
-        found = member_entries(state, False, where, blocks[chunk], received, sums[:1])
+        found = member_entries(state, direct, where, blocks[chunk], received, sums[:1])
         entries.append(exchange(found))
 
     grad_values, done = [], []

time: 49.2 us -> 87.5 us (1.78)
  local copies, waits for them, and re-layouts: 0.69 us -> 33 us
  Pallas kernels: 16.6 us -> 19.9 us
  starting transfers between devices: 23.9 us -> 24.9 us
    unnamed x0 -> x120, local copies, waits for them, and re-layouts: none -> 32.3 us
    all_to_all x0 -> x1, starting transfers between devices: none -> 5.35 us  [shards(): lax.all_to_all(own, 'seq', 0, 0, axis_index_groups=columns, tiled=True)]
    ppermute x4 -> x2, starting transfers between devices: 7.78 us -> 4.46 us  [to_group(): lax.ppermute(block, 'seq', [(s, s ^ k * group) for s in range(count)])]
    pallas_call x2, Pallas kernels: 0.27 us -> 1.71 us  [totals(): pl.pallas_call(functools.partial(totals_kernel, state, groups), out_shape...]
    pallas_call x2, Pallas kernels: 0.37 us -> 1.38 us  [member_entries(): pl.pallas_call(functools.partial(members_kernel, state, direct, len(recei...]
    ppermute x12, starting transfers between devices: 16 us -> 15.1 us  [exchange(): out[k] = lax.ppermute(parts[k], 'seq', [(s, s ^ k) for s in range(count)])]
    pallas_call x2 -> x1, Pallas kernels: 0.09 us -> 1.02 us  [merged(): pl.pallas_call(functools.partial(merged_kernel, state, level, last), out_...]
  transfers between devices with their start and end apart: 17 -> 16, of which waited for: 8 -> 6; matrix products, arithmetic and copies ran while one was open for 0% -> 0% of each run, Pallas kernels for 26% -> 17%
where the time goes in v9:
time: 87.5 us; the launch traced here: 86.5 us
  local copies, waits for them, and re-layouts  33 us (38%)
  starting transfers between devices  24.9 us (28%)
  Pallas kernels  19.9 us (23%)
  waiting for transfers between devices  7.65 us (9%)
  between operations  1.02 us (1%)
    unnamed x120, local copies, waits for them, and re-layouts  32.3 us
    ppermute x12, starting transfers between devices, exchange(): out[k] = lax.ppermute(parts[k], 'seq', [(s, s ^ k) for s in range(count)])  15.1 us
    ppermute x12, waiting for transfers between devices, exchange(): out[k] = lax.ppermute(parts[k], 'seq', [(s, s ^ k) for s in range(count)])  7.44 us
    pallas_call x2, Pallas kernels, inner_terms(): pl.pallas_call(functools.partial(inner_kernel, head_dim, chunk, len(befor...  6.93 us
    all_to_all x1, starting transfers between devices, shards(): lax.all_to_all(own, 'seq', 0, 0, axis_index_groups=columns, tiled=True)  5.35 us
    ppermute x2, starting transfers between devices, to_group(): lax.ppermute(block, 'seq', [(s, s ^ k * group) for s in range(count)])  4.46 us
    pallas_call x1, Pallas kernels, first_states(): pl.pallas_call(functools.partial(first_states_kernel, head_dim, group), o...  3.26 us
    pallas_call x2, Pallas kernels, entry_values(): pl.pallas_call(functools.partial(values_kernel, chunk, last), out_shape=[...  2.42 us
  transfers between devices with their start and end apart: 16, of which 6 were waited for; matrix products, arithmetic and copies ran while one was open for 0% of the time, Pallas kernels for 17%

profile of v9, /device:TPU:0, one launch (start us, length us, event | category | flops | bytes accessed | tf_op | source)
XLA Modules:
  0.0 86.5 jit_solution(9251494099346486915)
XLA Ops:
  0.6 3.3 %first_states.1 = (f32[32,384]{1,0:T(8,128)S(1)}, bf16[384,128]{1,0:T(8,128)(2,1)S(1)}, bf16[384,128]{1,0:T(8,128)(2,1)S(1)}, bf16[384,2048]{1,0:T(8,128)(2,1)S(...) custom-call(s32[1]{0:T(128)} %bitcast.where, ...), custom_call_target="tpu_custom_call" | custom-call | flops 402653184 | bytes 6291456 | tf_op jit(solution)/shard_map/first_states/pallas_call | solution.py:184
  3.9 0.9 %copy-done.9 = bf16[384,1024]{1,0:T(8,128)(2,1)} copy-done((bf16[384,1024]{1,0:T(8,128)(2,1)}, bf16[384,1024]{1,0:T(8,128)(2,1)S(1)}, u32[]{:S(2)}) %copy-start.9) | copy-done | bytes 786456
  4.8 0.9 %copy-done.11 = bf16[384,1024]{1,0:T(8,128)(2,1)} copy-done((bf16[384,1024]{1,0:T(8,128)(2,1)}, bf16[384,1024]{1,0:T(8,128)(2,1)S(1)}, u32[]{:S(2)}) %copy-start.11) | copy-done | bytes 786456
  5.7 0.9 %copy-done.13 = bf16[384,1024]{1,0:T(8,128)(2,1)} copy-done((bf16[384,1024]{1,0:T(8,128)(2,1)}, bf16[384,1024]{1,0:T(8,128)(2,1)S(1)}, u32[]{:S(2)}) %copy-start.13) | copy-done | bytes 786456
  6.6 3.9 %collective-permute-start = (bf16[272,256]{1,0:T(8,128)(2,1)S(1)}, bf16[272,256]{1,0:T(8,128)(2,1)S(1)}, u32[]{:S(2)}, u32[]{:S(2)}) collective-permute-start(bf16[272,256]{1,0:T(8,128)(2,1)S(1)} %get-tuple-element.68), channel_id=1, source_target_pairs={{0,6},{2,4},{4,2},{6,0},{8,14},{10,12},{12,10},{14,8},{16,22},{18,... | collective-permute-start | bytes 417800 | tf_op jit(solution)/shard_map/ppermute | solution.py:384
  11.1 1.6 %next_states.1 = (bf16[384,1024]{1,0:T(8,128)(2,1)S(1)}, bf16[384,1024]{1,0:T(8,128)(2,1)S(1)}, bf16[384,1024]{1,0:T(8,128)(2,1)S(1)}, bf16[272,256]{1,0:T(8,128...) custom-call(s32[1]{0:T(128)} %bitcast.where, ...), custom_call_target="tpu_custom_call" | custom-call | flops 402653184 | bytes 3145728 | tf_op jit(solution)/shard_map/next_states/pallas_call | solution.py:199
  12.6 0.9 %copy-done.17 = bf16[384,1024]{1,0:T(8,128)(2,1)} copy-done((bf16[384,1024]{1,0:T(8,128)(2,1)}, bf16[384,1024]{1,0:T(8,128)(2,1)S(1)}, u32[]{:S(2)}) %copy-start.17) | copy-done | bytes 786456
  13.5 0.9 %copy-done.19 = bf16[384,1024]{1,0:T(8,128)(2,1)} copy-done((bf16[384,1024]{1,0:T(8,128)(2,1)}, bf16[384,1024]{1,0:T(8,128)(2,1)S(1)}, u32[]{:S(2)}) %copy-start.19) | copy-done | bytes 786456
  14.4 0.9 %copy-done.21 = bf16[384,1024]{1,0:T(8,128)(2,1)} copy-done((bf16[384,1024]{1,0:T(8,128)(2,1)}, bf16[384,1024]{1,0:T(8,128)(2,1)S(1)}, u32[]{:S(2)}) %copy-start.21) | copy-done | bytes 786456
  19.1 0.9 %totals.2.refs_7_.refs_4_ = bf16[4,144,256]{2,1,0:T(8,128)(2,1)} custom-call(s32[1]{0:T(128)} %bitcast.where, bf16[272,256]{1,0:T(8,128)(2,1)S(1)} %get-tuple-element.67.refs_0_.refs_1_, bf16[272,256]{1,0:T(8,128)(2,1)S(1)} %collective-permute-done.refs_1_.refs_4_, bf16[272,256]{1,0:T(8,128)(2,1)S(1)} %collective-permute-done.1.refs_2_.refs_3_, ...), custom_call_target="tpu_custom_call" | custom-call | flops 557056 | bytes 696320 | tf_op jit(solution)/shard_map/totals/pallas_call | solution.py:267
  22.6 5.3 %all-to-all-start = ((bf16[4,144,256]{2,1,0:T(8,128)(2,1)}), bf16[4,144,256]{2,1,0:T(8,128)(2,1)S(1)}, u32[]{:S(2)}, u32[]{:S(2)}) async-start(bf16[4,144,256]{2,1,0:T(8,128)(2,1)} %totals.2.refs_7_.refs_4_), calls=%async_computation | async-start | bytes 589824 | tf_op jit(solution)/shard_map/all_to_all | solution.py:664
  28.0 2.4 %collective-permute-start.3 = (bf16[272,256]{1,0:T(8,128)(2,1)}, bf16[272,256]{1,0:T(8,128)(2,1)S(1)}, u32[]{:S(2)}, u32[]{:S(2)}) collective-permute-start(bf16[272,256]{1,0:T(8,128)(2,1)} %copy-done.59), channel_id=1, source_target_pairs={{0,6},{2,4},{4,2},{6,0},{8,14},{10,12},{12,10},{14,8},{16,22},{18,... | collective-permute-start | bytes 417800 | tf_op jit(solution)/shard_map/ppermute | solution.py:384
  31.5 4.0 %collective-permute-done.3.refs_1_.refs_5_ = bf16[272,256]{1,0:T(8,128)(2,1)S(1)} collective-permute-done((bf16[272,256]{1,0:T(8,128)(2,1)}, bf16[272,256]{1,0:T(8,128)(2,1)S(1)}, u32[]{:S(2)}, u32[]{:S(2)}) %collective-permute-start.3) | collective-permute-done | bytes 139296 | tf_op jit(solution)/shard_map/ppermute | solution.py:384
  35.4 0.9 %collective-permute-done.4.refs_2_.refs_4_ = bf16[272,256]{1,0:T(8,128)(2,1)S(1)} collective-permute-done((bf16[272,256]{1,0:T(8,128)(2,1)}, bf16[272,256]{1,0:T(8,128)(2,1)S(1)}, u32[]{:S(2)}, u32[]{:S(2)}) %collective-permute-start.4) | collective-permute-done | bytes 139296 | tf_op jit(solution)/shard_map/ppermute | solution.py:384
  36.4 0.9 %copy-done.24 = bf16[272,256]{1,0:T(8,128)(2,1)S(1)} copy-done((bf16[272,256]{1,0:T(8,128)(2,1)S(1)}, bf16[272,256]{1,0:T(8,128)(2,1)}, u32[]{:S(2)}) %copy-start.24) | copy-done | bytes 139288
  37.3 0.8 totals.3.own
  38.1 2.1 %collective-permute-start.6 = (bf16[272,256]{1,0:T(8,128)(2,1)}, bf16[272,256]{1,0:T(8,128)(2,1)}, u32[]{:S(2)}, u32[]{:S(2)}) collective-permute-start(bf16[272,256]{1,0:T(8,128)(2,1)} %totals.3.own), channel_id=1, source_target_pairs={{0,8},{2,10},{4,12},{6,14},{8,0},{10,2},{12,4},{14,6},{16,24},{18,... | collective-permute-start | bytes 417800 | tf_op jit(solution)/shard_map/ppermute | solution.py:654
  40.2 0.9 %copy-done.1 = bf16[384,128]{1,0:T(8,128)(2,1)S(1)} copy-done((bf16[384,128]{1,0:T(8,128)(2,1)S(1)}, bf16[384,128]{1,0:T(8,128)(2,1)}, u32[]{:S(2)}) %copy-start.1) | copy-done | bytes 98328
  41.1 0.9 %copy-done.4 = bf16[384,128]{1,0:T(8,128)(2,1)S(1)} copy-done((bf16[384,128]{1,0:T(8,128)(2,1)S(1)}, bf16[384,128]{1,0:T(8,128)(2,1)}, u32[]{:S(2)}) %copy-start.4) | copy-done | bytes 98328
  42.0 0.9 %copy-done.41 = bf16[192,192]{1,0:T(8,128)(2,1)S(1)} copy-done((bf16[192,192]{1,0:T(8,128)(2,1)S(1)}, bf16[192,192]{1,0:T(8,128)(2,1)}, u32[]{:S(2)}) %copy-start.41) | copy-done | bytes 73752
  42.9 0.9 %copy-done.44 = bf16[384,64]{1,0:T(8,128)(2,1)S(1)} copy-done((bf16[384,64]{1,0:T(8,128)(2,1)S(1)}, bf16[384,64]{1,0:T(8,128)(2,1)}, u32[]{:S(2)}) %copy-start.44) | copy-done | bytes 49176
  45.9 3.5 %inner_terms.2 = (bf16[384,1024]{1,0:T(8,128)(2,1)S(1)}, f32[384,128]{1,0:T(8,128)S(1)}, f32[384,128]{1,0:T(8,128)S(1)}) custom-call(bf16[384,128]{1,0:T(8,128)(2,1)S(1)} %get-tuple-element.53.refs_0_.b, bf16[384,128]{1,0:T(8,128)(2,1)S(1)} %copy-done.1, bf16[384,2048]{1,0:T(8,128)(2,1)S(1)} %get-tuple-element.55.refs_2_.x, ...), custom_call_target="tpu_custom_call" | custom-call | flops 805306368 | bytes 3145728 | tf_op jit(solution)/shard_map/inner_terms/pallas_call | solution.py:535
  50.1 0.9 %copy-done.15 = bf16[384,1024]{1,0:T(8,128)(2,1)} copy-done((bf16[384,1024]{1,0:T(8,128)(2,1)}, bf16[384,1024]{1,0:T(8,128)(2,1)S(1)}, u32[]{:S(2)}) %copy-start.15) | copy-done | bytes 786456
  51.7 0.9 %copy-done.7 = f32[384,128]{1,0:T(8,128)S(1)} copy-done((f32[384,128]{1,0:T(8,128)S(1)}, f32[384,128]{1,0:T(8,128)}, u32[]{:S(2)}) %copy-start.7) | copy-done | bytes 196632
  52.6 0.9 %copy-done.33 = bf16[272,256]{1,0:T(8,128)(2,1)S(1)} copy-done((bf16[272,256]{1,0:T(8,128)(2,1)S(1)}, bf16[272,256]{1,0:T(8,128)(2,1)}, u32[]{:S(2)}) %copy-start.33) | copy-done | bytes 139288
  53.5 0.9 %copy-done.35 = bf16[272,256]{1,0:T(8,128)(2,1)S(1)} copy-done((bf16[272,256]{1,0:T(8,128)(2,1)S(1)}, bf16[272,256]{1,0:T(8,128)(2,1)}, u32[]{:S(2)}) %copy-start.35) | copy-done | bytes 139288
  54.4 0.9 %copy-done.37 = bf16[272,256]{1,0:T(8,128)(2,1)S(1)} copy-done((bf16[272,256]{1,0:T(8,128)(2,1)S(1)}, bf16[272,256]{1,0:T(8,128)(2,1)}, u32[]{:S(2)}) %copy-start.37) | copy-done | bytes 139288
  55.3 0.9 %copy-done.39 = bf16[272,256]{1,0:T(8,128)(2,1)S(1)} copy-done((bf16[272,256]{1,0:T(8,128)(2,1)S(1)}, bf16[272,256]{1,0:T(8,128)(2,1)}, u32[]{:S(2)}) %copy-start.39) | copy-done | bytes 139288
  56.4 1.5 %collective-permute-start.11 = (bf16[256,256]{1,0:T(8,128)(2,1)S(1)}, bf16[256,256]{1,0:T(8,128)(2,1)S(1)}, u32[]{:S(2)}, u32[]{:S(2)}) collective-permute-start(bf16[256,256]{1,0:T(8,128)(2,1)S(1)} %get-tuple-element.85), channel_id=1, source_target_pairs={{0,6},{2,4},{4,2},{6,0},{8,14},{10,12},{12,10},{14,8},{16,22},{18,... | collective-permute-start | bytes 393224 | tf_op jit(solution)/shard_map/ppermute | solution.py:384
  57.9 1.0 %merged.1.refs_9_ = bf16[144,256]{1,0:T(8,128)(2,1)S(1)} custom-call(s32[1]{0:T(128)} %bitcast.where, bf16[272,256]{1,0:T(8,128)(2,1)} %totals.3.own, bf16[272,256]{1,0:T(8,128)(2,1)} %collective-permute-done.6.received.refs_0_), custom_call_target="tpu_custom_call" | custom-call | flops 278528 | bytes 417792 | tf_op jit(solution)/shard_map/merged/pallas_call | solution.py:302
  58.9 2.4 %collective-permute-start.7 = (bf16[144,256]{1,0:T(8,128)(2,1)S(1)}, bf16[144,256]{1,0:T(8,128)(2,1)S(1)}, u32[]{:S(2)}, u32[]{:S(2)}) collective-permute-start(bf16[144,256]{1,0:T(8,128)(2,1)S(1)} %merged.1.refs_9_), channel_id=1, source_target_pairs={{0,16},{2,18},{4,20},{6,22},{8,24},{10,26},{12,28},{14,30},{16,0},... | collective-permute-start | bytes 221192 | tf_op jit(solution)/shard_map/ppermute | solution.py:654
  61.3 1.3 %collective-permute-start.12 = (bf16[256,256]{1,0:T(8,128)(2,1)S(1)}, bf16[256,256]{1,0:T(8,128)(2,1)S(1)}, u32[]{:S(2)}, u32[]{:S(2)}) collective-permute-start(bf16[256,256]{1,0:T(8,128)(2,1)S(1)} %get-tuple-element.86), channel_id=1, source_target_pairs={{0,4},{2,6},{4,0},{6,2},{8,12},{10,14},{12,8},{14,10},{16,20},{18,... | collective-permute-start | bytes 393224 | tf_op jit(solution)/shard_map/ppermute | solution.py:384
  62.6 0.8 collective-permute-start.13
  63.4 0.9 %copy-done.2 = bf16[384,128]{1,0:T(8,128)(2,1)S(1)} copy-done((bf16[384,128]{1,0:T(8,128)(2,1)S(1)}, bf16[384,128]{1,0:T(8,128)(2,1)}, u32[]{:S(2)}) %copy-start.2) | copy-done | bytes 98328
  64.3 0.9 %copy-done.5 = bf16[384,128]{1,0:T(8,128)(2,1)S(1)} copy-done((bf16[384,128]{1,0:T(8,128)(2,1)S(1)}, bf16[384,128]{1,0:T(8,128)(2,1)}, u32[]{:S(2)}) %copy-start.5) | copy-done | bytes 98328
  65.2 0.9 %copy-done.8 = f32[384,128]{1,0:T(8,128)S(1)} copy-done((f32[384,128]{1,0:T(8,128)S(1)}, f32[384,128]{1,0:T(8,128)}, u32[]{:S(2)}) %copy-start.8) | copy-done | bytes 196632
  66.1 0.9 %copy-done.42 = bf16[192,192]{1,0:T(8,128)(2,1)S(1)} copy-done((bf16[192,192]{1,0:T(8,128)(2,1)S(1)}, bf16[192,192]{1,0:T(8,128)(2,1)}, u32[]{:S(2)}) %copy-start.42) | copy-done | bytes 73752
  67.0 0.9 %copy-done.45 = bf16[384,64]{1,0:T(8,128)(2,1)S(1)} copy-done((bf16[384,64]{1,0:T(8,128)(2,1)S(1)}, bf16[384,64]{1,0:T(8,128)(2,1)}, u32[]{:S(2)}) %copy-start.45) | copy-done | bytes 49176
  67.9 0.9 %copy-done.47 = f32[384,128]{1,0:T(8,128)S(1)} copy-done((f32[384,128]{1,0:T(8,128)S(1)}, f32[384,128]{1,0:T(8,128)}, u32[]{:S(2)}) %copy-start.47) | copy-done | bytes 196632
  71.0 3.5 %inner_terms.3 = (bf16[384,1024]{1,0:T(8,128)(2,1)S(1)}, f32[384,128]{1,0:T(8,128)S(1)}, f32[384,128]{1,0:T(8,128)S(1)}) custom-call(bf16[384,128]{1,0:T(8,128)(2,1)S(1)} %get-tuple-element.53.refs_0_.b, bf16[384,128]{1,0:T(8,128)(2,1)S(1)} %copy-done.2, bf16[384,2048]{1,0:T(8,128)(2,1)S(1)} %get-tuple-element.55.refs_2_.x, ...), custom_call_target="tpu_custom_call" | custom-call | flops 805306368 | bytes 3145728 | tf_op jit(solution)/shard_map/inner_terms/pallas_call | solution.py:535
  74.5 1.2 %member_entries.2 = (bf16[256,256]{1,0:T(8,128)(2,1)S(1)}, bf16[256,256]{1,0:T(8,128)(2,1)S(1)}, bf16[256,256]{1,0:T(8,128)(2,1)S(1)}, bf16[256,256]{1,0:T(8,128)(2,1)S(1)}) custom-call(s32[1]{0:T(128)} %bitcast.where, bf16[272,256]{1,0:T(8,128)(2,1)} %collective-permute-done.6.received.refs_0_, bf16[144,256]{1,0:T(8,128)(2,1)S(1)} %collective-permute-done.7.refs_1_, ...), custom_call_target="tpu_custom_call" | custom-call | flops 835584 | bytes 1114112 | tf_op jit(solution)/shard_map/member_entries/pallas_call | solution.py:368
  75.8 1.3 %collective-permute-start.10 = (bf16[256,256]{1,0:T(8,128)(2,1)S(1)}, bf16[256,256]{1,0:T(8,128)(2,1)S(1)}, u32[]{:S(2)}, u32[]{:S(2)}) collective-permute-start(bf16[256,256]{1,0:T(8,128)(2,1)S(1)} %get-tuple-element.81), channel_id=1, source_target_pairs={{0,4},{2,6},{4,0},{6,2},{8,12},{10,14},{12,8},{14,10},{16,20},{18,... | collective-permute-start | bytes 393224 | tf_op jit(solution)/shard_map/ppermute | solution.py:384
  77.1 0.7 collective-permute-start.8
  77.8 1.5 %collective-permute-start.9 = (bf16[256,256]{1,0:T(8,128)(2,1)S(1)}, bf16[256,256]{1,0:T(8,128)(2,1)S(1)}, u32[]{:S(2)}, u32[]{:S(2)}) collective-permute-start(bf16[256,256]{1,0:T(8,128)(2,1)S(1)} %get-tuple-element.80), channel_id=1, source_target_pairs={{0,6},{2,4},{4,2},{6,0},{8,14},{10,12},{12,10},{14,8},{16,22},{18,... | collective-permute-start | bytes 393224 | tf_op jit(solution)/shard_map/ppermute | solution.py:384
  79.3 1.2 %entry_values.2 = (bf16[384,2048]{1,0:T(8,128)(2,1)}, f32[8,128]{1,0:T(8,128)S(1)}) custom-call(s32[1]{0:T(128)} %bitcast.where, bf16[384,1024]{1,0:T(8,128)(2,1)S(1)} %copy-done.14, bf16[384,128]{1,0:T(8,128)(2,1)S(1)} %get-tuple-element.53.refs_0_.b, bf16[384,1024]{1,0:T(8,128)(2,1)S(1)} %copy-done.16, bf16[256,256]{1,0:T(8,128)(2,1)S(1)} %get-tuple-element.84.refs_0_, ...), custom_call_target="tpu_custom_call" | custom-call | flops 100663296 | bytes 1572864 | tf_op jit(solution)/shard_map/entry_values/pallas_call | solution.py:611
  81.2 0.8 collective-permute-done.8.refs_1_.refs_3_
  82.0 1.6 %collective-permute-done.9.refs_2_.refs_1_ = bf16[256,256]{1,0:T(8,128)(2,1)S(1)} collective-permute-done((bf16[256,256]{1,0:T(8,128)(2,1)S(1)}, bf16[256,256]{1,0:T(8,128)(2,1)S(1)}, u32[]{:S(2)}, u32[]{:S(2)}) %collective-permute-start.9) | collective-permute-done | bytes 131104 | tf_op jit(solution)/shard_map/ppermute | solution.py:384
  84.3 1.2 %entry_values.3 = bf16[384,2048]{1,0:T(8,128)(2,1)} custom-call(s32[1]{0:T(128)} %bitcast.where, bf16[384,1024]{1,0:T(8,128)(2,1)S(1)} %copy-done.22, bf16[384,128]{1,0:T(8,128)(2,1)S(1)} %get-tuple-element.53.refs_0_.b, bf16[384,1024]{1,0:T(8,128)(2,1)S(1)} %get-tuple-element.76.dx_local, ...), custom_call_target="tpu_custom_call", output_to_operand_aliasing={{}: (8, {})} | custom-call | flops 100663296 | bytes 1572864 | tf_op jit(solution)/shard_map/entry_values/pallas_call | solution.py:611
  (120 shorter events, 16.1 us)
Async XLA Ops:
  3.9 0.9 %copy-start.9 = (bf16[384,1024]{1,0:T(8,128)(2,1)}, bf16[384,1024]{1,0:T(8,128)(2,1)S(1)}, u32[]{:S(2)}) copy-start(bf16[384,1024]{1,0:T(8,128)(2,1)S(1)} %get-tuple-element.91.x_scaled) | copy-start | bytes 2359300
  6.6 8.7 %copy-start = (bf16[384,128]{1,0:T(8,128)(2,1)}, bf16[384,128]{1,0:T(8,128)(2,1)S(1)}, u32[]{:S(2)}) copy-start(bf16[384,128]{1,0:T(8,128)(2,1)S(1)} %get-tuple-element.54.refs_1_.c) | copy-start | bytes 294916
  6.6 12.5 %copy-start.32 = (bf16[272,256]{1,0:T(8,128)(2,1)}, bf16[272,256]{1,0:T(8,128)(2,1)S(1)}, u32[]{:S(2)}) copy-start(bf16[272,256]{1,0:T(8,128)(2,1)S(1)} %get-tuple-element.67.refs_0_.refs_1_) | copy-start | bytes 417796
  6.6 12.5 %collective-permute-start = (bf16[272,256]{1,0:T(8,128)(2,1)S(1)}, bf16[272,256]{1,0:T(8,128)(2,1)S(1)}, u32[]{:S(2)}, u32[]{:S(2)}) collective-permute-start(bf16[272,256]{1,0:T(8,128)(2,1)S(1)} %get-tuple-element.68), channel_id=1, source_target_pairs={{0,6},{2,4},{4,2},{6,0},{8,14},{10,12},{12,10},{14,8},{16,22},{18,... | collective-permute-start | bytes 417800 | tf_op jit(solution)/shard_map/ppermute | solution.py:384
  10.5 8.6 %collective-permute-start.1 = (bf16[272,256]{1,0:T(8,128)(2,1)S(1)}, bf16[272,256]{1,0:T(8,128)(2,1)S(1)}, u32[]{:S(2)}, u32[]{:S(2)}) collective-permute-start(bf16[272,256]{1,0:T(8,128)(2,1)S(1)} %get-tuple-element.69), channel_id=1, source_target_pairs={{0,4},{2,6},{4,0},{6,2},{8,12},{10,14},{12,8},{14,10},{16,20},{18,... | collective-permute-start | bytes 417800 | tf_op jit(solution)/shard_map/ppermute | solution.py:384
  11.0 8.1 %collective-permute-start.2 = (bf16[272,256]{1,0:T(8,128)(2,1)S(1)}, bf16[272,256]{1,0:T(8,128)(2,1)S(1)}, u32[]{:S(2)}, u32[]{:S(2)}) collective-permute-start(bf16[272,256]{1,0:T(8,128)(2,1)S(1)} %get-tuple-element.70), channel_id=1, source_target_pairs={{0,2},{2,0},{4,6},{6,4},{8,10},{10,8},{12,14},{14,12},{16,18},{18,... | collective-permute-start | bytes 417800 | tf_op jit(solution)/shard_map/ppermute | solution.py:384
  15.3 3.8 %copy-start.57 = (bf16[272,256]{1,0:T(8,128)(2,1)}, bf16[272,256]{1,0:T(8,128)(2,1)S(1)}, u32[]{:S(2)}) copy-start(bf16[272,256]{1,0:T(8,128)(2,1)S(1)} %get-tuple-element.75) | copy-start | bytes 417796
  15.3 3.8 %copy-start.58 = (bf16[272,256]{1,0:T(8,128)(2,1)}, bf16[272,256]{1,0:T(8,128)(2,1)S(1)}, u32[]{:S(2)}) copy-start(bf16[272,256]{1,0:T(8,128)(2,1)S(1)} %get-tuple-element.74) | copy-start | bytes 417796
  15.3 3.8 %copy-start.59 = (bf16[272,256]{1,0:T(8,128)(2,1)}, bf16[272,256]{1,0:T(8,128)(2,1)S(1)}, u32[]{:S(2)}) copy-start(bf16[272,256]{1,0:T(8,128)(2,1)S(1)} %get-tuple-element.73) | copy-start | bytes 417796
  22.6 29.0 %all-to-all-start = ((bf16[4,144,256]{2,1,0:T(8,128)(2,1)}), bf16[4,144,256]{2,1,0:T(8,128)(2,1)S(1)}, u32[]{:S(2)}, u32[]{:S(2)}) async-start(bf16[4,144,256]{2,1,0:T(8,128)(2,1)} %totals.2.refs_7_.refs_4_), calls=%async_computation | async-start | bytes 589824 | tf_op jit(solution)/shard_map/all_to_all | solution.py:664
  28.0 7.5 %collective-permute-start.3 = (bf16[272,256]{1,0:T(8,128)(2,1)}, bf16[272,256]{1,0:T(8,128)(2,1)S(1)}, u32[]{:S(2)}, u32[]{:S(2)}) collective-permute-start(bf16[272,256]{1,0:T(8,128)(2,1)} %copy-done.59), channel_id=1, source_target_pairs={{0,6},{2,4},{4,2},{6,0},{8,14},{10,12},{12,10},{14,8},{16,22},{18,... | collective-permute-start | bytes 417800 | tf_op jit(solution)/shard_map/ppermute | solution.py:384
  30.4 5.9 %collective-permute-start.4 = (bf16[272,256]{1,0:T(8,128)(2,1)}, bf16[272,256]{1,0:T(8,128)(2,1)S(1)}, u32[]{:S(2)}, u32[]{:S(2)}) collective-permute-start(bf16[272,256]{1,0:T(8,128)(2,1)} %copy-done.58), channel_id=1, source_target_pairs={{0,4},{2,6},{4,0},{6,2},{8,12},{10,14},{12,8},{14,10},{16,20},{18,... | collective-permute-start | bytes 417800 | tf_op jit(solution)/shard_map/ppermute | solution.py:384
  30.9 5.5 %collective-permute-start.5 = (bf16[272,256]{1,0:T(8,128)(2,1)}, bf16[272,256]{1,0:T(8,128)(2,1)S(1)}, u32[]{:S(2)}, u32[]{:S(2)}) collective-permute-start(bf16[272,256]{1,0:T(8,128)(2,1)} %copy-done.57), channel_id=1, source_target_pairs={{0,2},{2,0},{4,6},{6,4},{8,10},{10,8},{12,14},{14,12},{16,18},{18,... | collective-permute-start | bytes 417800 | tf_op jit(solution)/shard_map/ppermute | solution.py:384
  35.4 4.8 %copy-start.26 = (bf16[272,256]{1,0:T(8,128)(2,1)}, bf16[272,256]{1,0:T(8,128)(2,1)S(1)}, u32[]{:S(2)}) copy-start(bf16[272,256]{1,0:T(8,128)(2,1)S(1)} %collective-permute-done.3.refs_1_.refs_5_) | copy-start | bytes 417796
  36.4 3.8 %copy-start.28 = (bf16[272,256]{1,0:T(8,128)(2,1)}, bf16[272,256]{1,0:T(8,128)(2,1)S(1)}, u32[]{:S(2)}) copy-start(bf16[272,256]{1,0:T(8,128)(2,1)S(1)} %collective-permute-done.4.refs_2_.refs_4_) | copy-start | bytes 417796
  36.4 0.9 %copy-start.24 = (bf16[272,256]{1,0:T(8,128)(2,1)S(1)}, bf16[272,256]{1,0:T(8,128)(2,1)}, u32[]{:S(2)}) copy-start(bf16[272,256]{1,0:T(8,128)(2,1)} %copy-done.23) | copy-start | bytes 417796
  37.3 2.9 %copy-start.30 = (bf16[272,256]{1,0:T(8,128)(2,1)}, bf16[272,256]{1,0:T(8,128)(2,1)S(1)}, u32[]{:S(2)}) copy-start(bf16[272,256]{1,0:T(8,128)(2,1)S(1)} %collective-permute-done.5.refs_3_) | copy-start | bytes 417796
  38.1 19.7 %collective-permute-start.6 = (bf16[272,256]{1,0:T(8,128)(2,1)}, bf16[272,256]{1,0:T(8,128)(2,1)}, u32[]{:S(2)}, u32[]{:S(2)}) collective-permute-start(bf16[272,256]{1,0:T(8,128)(2,1)} %totals.3.own), channel_id=1, source_target_pairs={{0,8},{2,10},{4,12},{6,14},{8,0},{10,2},{12,4},{14,6},{16,24},{18,... | collective-permute-start | bytes 417800 | tf_op jit(solution)/shard_map/ppermute | solution.py:654
  40.2 0.9 %copy-start.1 = (bf16[384,128]{1,0:T(8,128)(2,1)S(1)}, bf16[384,128]{1,0:T(8,128)(2,1)}, u32[]{:S(2)}) copy-start(bf16[384,128]{1,0:T(8,128)(2,1)} %copy-done) | copy-start | bytes 294916
  41.1 0.9 %copy-start.4 = (bf16[384,128]{1,0:T(8,128)(2,1)S(1)}, bf16[384,128]{1,0:T(8,128)(2,1)}, u32[]{:S(2)}) copy-start(bf16[384,128]{1,0:T(8,128)(2,1)} %copy-done.3) | copy-start | bytes 294916
  42.0 0.9 %copy-start.41 = (bf16[192,192]{1,0:T(8,128)(2,1)S(1)}, bf16[192,192]{1,0:T(8,128)(2,1)}, u32[]{:S(2)}) copy-start(bf16[192,192]{1,0:T(8,128)(2,1)} %copy-done.40) | copy-start | bytes 221188
  50.1 0.9 %copy-start.15 = (bf16[384,1024]{1,0:T(8,128)(2,1)}, bf16[384,1024]{1,0:T(8,128)(2,1)S(1)}, u32[]{:S(2)}) copy-start(bf16[384,1024]{1,0:T(8,128)(2,1)S(1)} %get-tuple-element.83.dx_local) | copy-start | bytes 2359300
  51.7 0.9 %copy-start.7 = (f32[384,128]{1,0:T(8,128)S(1)}, f32[384,128]{1,0:T(8,128)}, u32[]{:S(2)}) copy-start(f32[384,128]{1,0:T(8,128)} %copy-done.6) | copy-start | bytes 589828
  52.6 0.9 %copy-start.33 = (bf16[272,256]{1,0:T(8,128)(2,1)S(1)}, bf16[272,256]{1,0:T(8,128)(2,1)}, u32[]{:S(2)}) copy-start(bf16[272,256]{1,0:T(8,128)(2,1)} %copy-done.32) | copy-start | bytes 417796
  53.5 0.9 %copy-start.35 = (bf16[272,256]{1,0:T(8,128)(2,1)S(1)}, bf16[272,256]{1,0:T(8,128)(2,1)}, u32[]{:S(2)}) copy-start(bf16[272,256]{1,0:T(8,128)(2,1)} %copy-done.34) | copy-start | bytes 417796
  54.4 0.9 %copy-start.37 = (bf16[272,256]{1,0:T(8,128)(2,1)S(1)}, bf16[272,256]{1,0:T(8,128)(2,1)}, u32[]{:S(2)}) copy-start(bf16[272,256]{1,0:T(8,128)(2,1)} %copy-done.36) | copy-start | bytes 417796
  55.3 0.9 %copy-start.39 = (bf16[272,256]{1,0:T(8,128)(2,1)S(1)}, bf16[272,256]{1,0:T(8,128)(2,1)}, u32[]{:S(2)}) copy-start(bf16[272,256]{1,0:T(8,128)(2,1)} %copy-done.38) | copy-start | bytes 417796
  56.4 21.4 %collective-permute-start.11 = (bf16[256,256]{1,0:T(8,128)(2,1)S(1)}, bf16[256,256]{1,0:T(8,128)(2,1)S(1)}, u32[]{:S(2)}, u32[]{:S(2)}) collective-permute-start(bf16[256,256]{1,0:T(8,128)(2,1)S(1)} %get-tuple-element.85), channel_id=1, source_target_pairs={{0,6},{2,4},{4,2},{6,0},{8,14},{10,12},{12,10},{14,8},{16,22},{18,... | collective-permute-start | bytes 393224 | tf_op jit(solution)/shard_map/ppermute | solution.py:384
  58.9 15.6 %collective-permute-start.7 = (bf16[144,256]{1,0:T(8,128)(2,1)S(1)}, bf16[144,256]{1,0:T(8,128)(2,1)S(1)}, u32[]{:S(2)}, u32[]{:S(2)}) collective-permute-start(bf16[144,256]{1,0:T(8,128)(2,1)S(1)} %merged.1.refs_9_), channel_id=1, source_target_pairs={{0,16},{2,18},{4,20},{6,22},{8,24},{10,26},{12,28},{14,30},{16,0},... | collective-permute-start | bytes 221192 | tf_op jit(solution)/shard_map/ppermute | solution.py:654
  61.3 18.0 %collective-permute-start.12 = (bf16[256,256]{1,0:T(8,128)(2,1)S(1)}, bf16[256,256]{1,0:T(8,128)(2,1)S(1)}, u32[]{:S(2)}, u32[]{:S(2)}) collective-permute-start(bf16[256,256]{1,0:T(8,128)(2,1)S(1)} %get-tuple-element.86), channel_id=1, source_target_pairs={{0,4},{2,6},{4,0},{6,2},{8,12},{10,14},{12,8},{14,10},{16,20},{18,... | collective-permute-start | bytes 393224 | tf_op jit(solution)/shard_map/ppermute | solution.py:384
  62.6 16.7 %collective-permute-start.13 = (bf16[256,256]{1,0:T(8,128)(2,1)S(1)}, bf16[256,256]{1,0:T(8,128)(2,1)S(1)}, u32[]{:S(2)}, u32[]{:S(2)}) collective-permute-start(bf16[256,256]{1,0:T(8,128)(2,1)S(1)} %get-tuple-element.87), channel_id=1, source_target_pairs={{0,2},{2,0},{4,6},{6,4},{8,10},{10,8},{12,14},{14,12},{16,18},{18,... | collective-permute-start | bytes 393224 | tf_op jit(solution)/shard_map/ppermute | solution.py:384
  65.2 0.9 %copy-start.8 = (f32[384,128]{1,0:T(8,128)S(1)}, f32[384,128]{1,0:T(8,128)}, u32[]{:S(2)}) copy-start(f32[384,128]{1,0:T(8,128)} %copy-done.6) | copy-start | bytes 589828
  67.9 0.9 %copy-start.47 = (f32[384,128]{1,0:T(8,128)S(1)}, f32[384,128]{1,0:T(8,128)}, u32[]{:S(2)}) copy-start(f32[384,128]{1,0:T(8,128)} %copy-done.46) | copy-start | bytes 589828
  71.0 3.5 %copy-start.25 = (bf16[272,256]{1,0:T(8,128)(2,1)S(1)}, bf16[272,256]{1,0:T(8,128)(2,1)}, u32[]{:S(2)}) copy-start(bf16[272,256]{1,0:T(8,128)(2,1)} %copy-done.23) | copy-start | bytes 417796
  71.0 3.5 %copy-start.27 = (bf16[272,256]{1,0:T(8,128)(2,1)S(1)}, bf16[272,256]{1,0:T(8,128)(2,1)}, u32[]{:S(2)}) copy-start(bf16[272,256]{1,0:T(8,128)(2,1)} %copy-done.26) | copy-start | bytes 417796
  71.0 3.5 %copy-start.29 = (bf16[272,256]{1,0:T(8,128)(2,1)S(1)}, bf16[272,256]{1,0:T(8,128)(2,1)}, u32[]{:S(2)}) copy-start(bf16[272,256]{1,0:T(8,128)(2,1)} %copy-done.28) | copy-start | bytes 417796
  71.0 3.5 %copy-start.31 = (bf16[272,256]{1,0:T(8,128)(2,1)S(1)}, bf16[272,256]{1,0:T(8,128)(2,1)}, u32[]{:S(2)}) copy-start(bf16[272,256]{1,0:T(8,128)(2,1)} %copy-done.30) | copy-start | bytes 417796
  71.0 8.3 %copy-start.14 = (bf16[384,1024]{1,0:T(8,128)(2,1)S(1)}, bf16[384,1024]{1,0:T(8,128)(2,1)}, u32[]{:S(2)}) copy-start(bf16[384,1024]{1,0:T(8,128)(2,1)} %copy-done.13) | copy-start | bytes 2359300
  71.0 8.3 %copy-start.16 = (bf16[384,1024]{1,0:T(8,128)(2,1)S(1)}, bf16[384,1024]{1,0:T(8,128)(2,1)}, u32[]{:S(2)}) copy-start(bf16[384,1024]{1,0:T(8,128)(2,1)} %copy-done.15) | copy-start | bytes 2359300
  74.5 6.0 %copy-start.10 = (bf16[384,1024]{1,0:T(8,128)(2,1)S(1)}, bf16[384,1024]{1,0:T(8,128)(2,1)}, u32[]{:S(2)}) copy-start(bf16[384,1024]{1,0:T(8,128)(2,1)} %copy-done.9) | copy-start | bytes 2359300
  74.5 6.0 %copy-start.12 = (bf16[384,1024]{1,0:T(8,128)(2,1)S(1)}, bf16[384,1024]{1,0:T(8,128)(2,1)}, u32[]{:S(2)}) copy-start(bf16[384,1024]{1,0:T(8,128)(2,1)} %copy-done.11) | copy-start | bytes 2359300
  75.8 5.4 %collective-permute-start.10 = (bf16[256,256]{1,0:T(8,128)(2,1)S(1)}, bf16[256,256]{1,0:T(8,128)(2,1)S(1)}, u32[]{:S(2)}, u32[]{:S(2)}) collective-permute-start(bf16[256,256]{1,0:T(8,128)(2,1)S(1)} %get-tuple-element.81), channel_id=1, source_target_pairs={{0,4},{2,6},{4,0},{6,2},{8,12},{10,14},{12,8},{14,10},{16,20},{18,... | collective-permute-start | bytes 393224 | tf_op jit(solution)/shard_map/ppermute | solution.py:384
  77.1 5.0 %collective-permute-start.8 = (bf16[256,256]{1,0:T(8,128)(2,1)S(1)}, bf16[256,256]{1,0:T(8,128)(2,1)S(1)}, u32[]{:S(2)}, u32[]{:S(2)}) collective-permute-start(bf16[256,256]{1,0:T(8,128)(2,1)S(1)} %get-tuple-element.79), channel_id=1, source_target_pairs={{0,2},{2,0},{4,6},{6,4},{8,10},{10,8},{12,14},{14,12},{16,18},{18,... | collective-permute-start | bytes 393224 | tf_op jit(solution)/shard_map/ppermute | solution.py:384
  77.8 5.9 %collective-permute-start.9 = (bf16[256,256]{1,0:T(8,128)(2,1)S(1)}, bf16[256,256]{1,0:T(8,128)(2,1)S(1)}, u32[]{:S(2)}, u32[]{:S(2)}) collective-permute-start(bf16[256,256]{1,0:T(8,128)(2,1)S(1)} %get-tuple-element.80), channel_id=1, source_target_pairs={{0,6},{2,4},{4,2},{6,0},{8,14},{10,12},{12,10},{14,8},{16,22},{18,... | collective-permute-start | bytes 393224 | tf_op jit(solution)/shard_map/ppermute | solution.py:384
  80.5 3.1 %copy-start.18 = (bf16[384,1024]{1,0:T(8,128)(2,1)S(1)}, bf16[384,1024]{1,0:T(8,128)(2,1)}, u32[]{:S(2)}) copy-start(bf16[384,1024]{1,0:T(8,128)(2,1)} %copy-done.17) | copy-start | bytes 2359300
  80.6 3.1 %copy-start.20 = (bf16[384,1024]{1,0:T(8,128)(2,1)S(1)}, bf16[384,1024]{1,0:T(8,128)(2,1)}, u32[]{:S(2)}) copy-start(bf16[384,1024]{1,0:T(8,128)(2,1)} %copy-done.19) | copy-start | bytes 2359300
  81.2 3.2 %copy-start.22 = (bf16[384,1024]{1,0:T(8,128)(2,1)S(1)}, bf16[384,1024]{1,0:T(8,128)(2,1)}, u32[]{:S(2)}) copy-start(bf16[384,1024]{1,0:T(8,128)(2,1)} %copy-done.21) | copy-start | bytes 2359300
  84.2 1.5 %collective-permute-start.14 = (bf16[768,128]{1,0:T(8,128)(2,1)S(1)}, bf16[768,128]{1,0:T(8,128)(2,1)S(1)}, u32[]{:S(2)}, u32[]{:S(2)}) collective-permute-start(bf16[768,128]{1,0:T(8,128)(2,1)S(1)} %entry_parts.3), channel_id=1, source_target_pairs={{0,1},{1,0},{2,3},{3,2},{4,5},{5,4},{6,7},{7,6},{8,9},{9,8},{10,11... | collective-permute-start | bytes 589832 | tf_op jit(solution)/shard_map/ppermute | solution.py:633
  (28 other events, 20.9 us)

commit v10 on v8

--- a/solution.py
+++ b/solution.py
@@ -147,21 +147,43 @@
 def first_states_kernel(head_dim, group, where, ld_in, b_in, c_in, x_in, dy_in, *refs):
     ld, b, c, x, dy, into_end, from_start, halves = refs[:8]
     outs, sems = refs[8:-1], refs[-1]
-    pairs = [(ld_in, ld), (b_in, b), (x_in, x), (c_in, c), (dy_in, dy)]
-    copies = [pltpu.make_async_copy(i, o, sems.at[n]) for n, (i, o) in enumerate(pairs)]
-    for copy in copies:
+    width = x.shape[1]
+    chunks = chunk_count(width)
+    part = width // (group * chunks)
+
+    def load(n, source, target):
+        copy = pltpu.make_async_copy(source, target, sems.at[n])
         copy.start()
+        return copy
+
+    def load_chunk(n, chunk, source, target):
+        lanes = [pl.ds((m * chunks + chunk) * part, part) for m in range(group)]
+        return [
+            load(n + m, source.at[:, one], target.at[:, one]) for m, one in enumerate(lanes)
+        ]
+
+    first = load(0, ld_in, ld)
+    loads = [
+        [load(1, b_in, b), *load_chunk(3, 0, x_in, x)],
+        [load(2, c_in, c), *load_chunk(3 + group, 0, dy_in, dy)],
+    ]
     masks = masks_of(ld.shape[1])
-    copies[0].wait()
+    first.wait()
     factors = factors_of(ld[...], *masks)
     for ref, value in zip((into_end, from_start, halves), factors):
         ref[...] = value
+    later = []
 
     def ready(side):
-        copies[1 + 2 * side].wait()
-        copies[2 + 2 * side].wait()
+        for copy in loads[side]:
+            copy.wait()
+        for chunk in range(1, chunks if side == 1 else 1):
+            at = 3 + 2 * group * chunk
+            later.extend(load_chunk(at, chunk, x_in, x) + load_chunk(at + group, chunk, dy_in, dy))
 
     put_states(head_dim, 0, where, (*factors, b, c, x, dy), outs, ready)
+    for copy in later:
+        copy.wait()
 
 
 def next_states_kernel(head_dim, chunk, where, into_end, from_start, halves, *refs):
@@ -186,7 +208,7 @@
         out_shape=outs,
         in_specs=[SMEM] + [HBM] * 5,
         out_specs=whole(len(outs)),
-        scratch_shapes=[pltpu.SemaphoreType.DMA((5,))],
+        scratch_shapes=[pltpu.SemaphoreType.DMA((3 + 2 * group * chunk_count(width),))],
         compiler_params=params(8),
         cost_estimate=cost(2 * length * width * (state + LANES), 8 * length * width),
         name="first_states",
@@ -454,7 +476,7 @@
     setup_kernel(piece, ld, b, c, *refs[n_after:])
 
 
-def inner_kernel(head_dim, chunk, n_before, n_after, b, c, x, dy, *refs):
+def inner_kernel(head_dim, chunk, parts, n_before, n_after, b, c, x, dy, *refs):
     length, width = x.shape
     piece = head_dim
     pieces = length // piece
@@ -467,9 +489,12 @@
     part = dx_out.shape[1] // GROUP
     difference = row_less_head(head_dim, part, SLOT)
 
-    for m in range(GROUP):
+    if parts[0] > 0:
+        dx_out[...] = before[2][...]
+    for at, m in enumerate(parts):
         owned = m * (width // GROUP) + chunk * part
-        lanes, here = slice(owned, owned + part), slice(m * part, (m + 1) * part)
+        lanes, here = slice(owned, owned + part), slice(at * part, (at + 1) * part)
+        out_lanes = slice(m * part, (m + 1) * part)
         cum = dot(cum_terms[...], head_of_lane(difference, owned // head_dim), NN)
         dx = []
         for n in range(pieces):
@@ -496,7 +521,7 @@
                 for n in range(lo, mid):
                     dx[n] = dx[n] + far[rows_of(n - lo, n - lo + 1, piece), :]
         for n in range(pieces):
-            dx_out[rows_of(n, n + 1, piece), here] = dx[n].astype(BF16)
+            dx_out[rows_of(n, n + 1, piece), out_lanes] = dx[n].astype(BF16)
 
     if before:
         db_out[...] = before[0][...]
@@ -529,13 +554,14 @@
             dc_out[rows_of(mid, hi, piece), :] += dc[rows_of(g, g + 1, n_right * piece), :]
 
 
-def inner_terms(head_dim, chunk, setup, b, c, x, dy, before, after):
+def inner_terms(head_dim, chunk, parts, setup, b, c, x, dy, before, after):
     length, state = b.shape
     columns = x.shape[1] // chunk_count(x.shape[1])
+    used = columns // GROUP * len(parts)
     groups = grouped_cuts(length // head_dim)
     sizes = [[len(same) * n * head_dim for n in halves] for halves, same in groups]
     return pl.pallas_call(
-        functools.partial(inner_kernel, head_dim, chunk, len(before), len(after)),
+        functools.partial(inner_kernel, head_dim, chunk, parts, len(before), len(after)),
         out_shape=[
             jax.ShapeDtypeStruct((length, columns), BF16),
             jax.ShapeDtypeStruct((length, state), F32),
@@ -543,21 +569,21 @@
         ],
         in_specs=whole(4 + len(setup) + len(before)) + [ANY] * len(after),
         out_specs=whole(3),
-        scratch_shapes=[pltpu.VMEM((length, columns), BF16)] * 2
-        + [pltpu.VMEM((left, columns), BF16) for left, _ in sizes]
-        + [pltpu.VMEM((right, columns), BF16) for _, right in sizes],
+        scratch_shapes=[pltpu.VMEM((length, used), BF16)] * 2
+        + [pltpu.VMEM((left, used), BF16) for left, _ in sizes]
+        + [pltpu.VMEM((right, used), BF16) for _, right in sizes],
         compiler_params=params(16),
         cost_estimate=cost(8 * x.size * state, 4 * x.size, 2 * x.size),
         name="inner_terms",
     )(b, c, x, dy, *setup, *before, *after)
 
 
-def parts_kernel(last, x_scaled, dy_scaled, db_before, dc_before, *refs):
-    entries, outs = sent_order(refs[:GROUP]), refs[-1 if last else -2 :]
+def parts_kernel(last, ks, x_scaled, dy_scaled, db_before, dc_before, *refs):
+    entries, outs = refs[: len(ks)], refs[-1 if last else -2 :]
     length, state = db_before.shape
     part = entries[0].shape[1]
     db, dc = db_before[...], dc_before[...]
-    for k, entry in enumerate(entries):
+    for k, entry in zip(ks, entries):
         here = slice(k * part, (k + 1) * part)
         db = db + dot(x_scaled[:, here], entry[state:, :], NT)
         dc = dc + dot(dy_scaled[:, here], entry[:state, :], NT)
@@ -569,57 +595,55 @@
         outs[1][...] = dc
 
 
-def entry_parts(last, x_scaled, dy_scaled, db_before, dc_before, entries, after):
+def entry_parts(last, ks, x_scaled, dy_scaled, db_before, dc_before, entries, after):
     length, state = db_before.shape
-    one = pltpu.VMEM((length, state), F32)
-    outs = [pltpu.VMEM((2 * length, state), BF16)] if last else [one, one]
-    return pl.pallas_call(
-        functools.partial(parts_kernel, last),
+    one = jax.ShapeDtypeStruct((length, state), F32)
+    outs = [jax.ShapeDtypeStruct((2 * length, state), BF16)] if last else [one, one]
+    return pl.pallas_call(
+        functools.partial(parts_kernel, last, ks),
         out_shape=outs,
-        in_specs=whole(4 + len(entries)) + [ANY] * len(after),
+        in_specs=whole(4 + len(ks)) + [ANY] * len(after),
         out_specs=whole(len(outs)),
         compiler_params=params(8),
-        cost_estimate=cost(4 * x_scaled.size * state, 4 * x_scaled.size),
+        cost_estimate=cost(len(ks) * x_scaled.size * state, len(ks) * x_scaled.size),
         name="entry_parts",
-    )(x_scaled, dy_scaled, db_before, dc_before, *sent_order(entries), *after)
-
-
-def values_kernel(chunk, last, where, spread, b, dx_local, *refs):
-    entries, (dx, sems) = sent_order(refs[:GROUP], 2 if last else 1), refs[-2:]
+    )(x_scaled, dy_scaled, db_before, dc_before, *[entries[k] for k in ks], *after)
+
+
+def values_kernel(chunk, last, ks, where, spread, b, dx_local, *refs):
+    entries, (dx, sems) = refs[: len(ks)], refs[-2:]
     out = refs[-3 if last else -4]
     if not last:
         refs[-3][...] = jnp.zeros_like(refs[-3])
     state, part = b.shape[1], entries[0].shape[1]
     stores = []
-    for k, entry in enumerate(entries):
+    for n, (k, entry) in enumerate(zip(ks, entries)):
         here = slice(k * part, (k + 1) * part)
         local = dx_local[:, pl.ds(pl.multiple_of((place_of(where) ^ k) * part, part), part)]
         far = spread[:, here].astype(F32) * dot(b[...], entry[state:, :], NN)
-        dx[k] = (local.astype(F32) + far).astype(BF16)
+        dx[n] = (local.astype(F32) + far).astype(BF16)
         lanes = chunk_lanes(where, k, chunk, part, out.shape[1])
-        store = pltpu.make_async_copy(dx.at[k], out.at[:, lanes], sems.at[k])
+        store = pltpu.make_async_copy(dx.at[n], out.at[:, lanes], sems.at[n])
         store.start()
         stores.append(store)
     for store in stores:
         store.wait()
 
 
-def entry_values(chunk, chunks, where, spread, b, dx_local, entries, before, after):
-    group, part = len(entries), entries[0].shape[1]
+def entry_values(chunk, last, ks, width, where, spread, b, dx_local, entries, before):
+    part = entries[0].shape[1]
     length, state = b.shape
-    size, last = dx_local.size, chunk == chunks - 1
-    sent = sent_order(entries, 2 if last else 1)
-    operands = [where, spread, b, dx_local, *sent, *after, *before]
-    return pl.pallas_call(
-        functools.partial(values_kernel, chunk, last),
-        out_shape=[pltpu.HBM((length, chunks * group * part), BF16)]
-        + [pltpu.VMEM((8, LANES), F32)] * (not last),
-        in_specs=[SMEM] + whole(3 + group) + [ANY] * len(after) + [HBM] * len(before),
+    size = length * part * len(ks)
+    operands = [where, spread, b, dx_local, *[entries[k] for k in ks], *before]
+    return pl.pallas_call(
+        functools.partial(values_kernel, chunk, last, ks),
+        out_shape=[pltpu.HBM((length, width), BF16)] + [pltpu.VMEM((8, LANES), F32)] * (not last),
+        in_specs=[SMEM] + whole(3 + len(ks)) + [HBM] * len(before),
         out_specs=[HBM] + whole(0 if last else 1),
         input_output_aliases={len(operands) - 1: 0} if before else {},
         scratch_shapes=[
-            pltpu.VMEM((group, length, part), BF16),
-            pltpu.SemaphoreType.DMA((group,)),
+            pltpu.VMEM((len(ks), length, part), BF16),
+            pltpu.SemaphoreType.DMA((len(ks),)),
         ],
         compiler_params=params(8),
         cost_estimate=cost(2 * size * state, 4 * size),
@@ -651,32 +675,42 @@
         states.append(next_states(head_dim, group, chunk, where, factors, b, c, x, dy))
         blocks.append(exchange(states[chunk][3:]))
     setup = inner_setup(head_dim, ld, b, c, [states[-1][3]])
+    inner = functools.partial(inner_terms, head_dim)
+    early = inner(0, (0,), setup, b, c, x, dy, [], [])
 
     def to_group(block, k):
         return lax.ppermute(block, "seq", [(s, s ^ (k * group)) for s in range(count)])
 
-    entries, inner, sums = [], [], []
+    entries, local, sums = [], [], []
     for chunk in range(chunks):
-        (own,) = totals(state, 0, where, blocks[chunk], setup[-1:] if chunk == 0 else [])
+        (own,) = totals(state, 0, where, blocks[chunk], early[1:2] if chunk == 0 else [])
         received = [to_group(own, 1)]
         for level in range(levels - 1):
             last = level == levels - 2
             own = merged(state, level, last, where, own, received[level], [])
             received.append(to_group(own, 2 << level))
-        inner.append(inner_terms(head_dim, chunk, setup, b, c, x, dy, sums, [own]))
-        sums = list(inner[chunk][1:])
+        operands = (setup, b, c, x, dy)
+        if chunk == 0:
+            dx, *sums = inner(chunk, (1, 2, 3), *operands, [*early[1:], early[0]], [own])
+        else:
+            dx, *sums = inner(chunk, (0, 1, 2), *operands, sums, [own])
         found = member_entries(state, False, where, blocks[chunk], received, sums[:1])
         entries.append(exchange(found))
-
-    grad_values, done = [], []
-    for chunk in range(chunks):
+        if chunk > 0:
+            dx, *sums = inner(chunk, (3,), *operands, [*sums, dx], found[:1])
+        local.append(dx)
+
+    turns = [(chunk, (0, 3, 2, 1)) for chunk in range(chunks - 1)]
+    turns += [(chunks - 1, (0, 3)), (chunks - 1, (2, 1))]
+    grad_values, done, width = [], [], token_values.shape[1]
+    for n, (chunk, ks) in enumerate(turns):
         x_scaled, dy_scaled, spread = states[chunk][:3]
-        last = chunk == chunks - 1
-        sums = entry_parts(last, x_scaled, dy_scaled, *sums, entries[chunk], done)
-        outs = entry_values(
-            chunk, chunks, where, spread, b, inner[chunk][0], entries[chunk], grad_values, []
+        last = n == len(turns) - 1
+        sums = entry_parts(last, ks, x_scaled, dy_scaled, *sums, entries[chunk], done)
+        grad_values, *done = entry_values(
+            chunk, last, ks, width, where, spread, b, local[chunk], entries[chunk], grad_values
         )
-        grad_values, done = list(outs[:1]), list(outs[1:])
+        grad_values = [grad_values]
     both = over_heads(sums[0])
     return grad_values[0], both[:length], both[length:]
 

time: 49.2 us -> 49.3 us (level)
  Pallas kernels: 16.6 us -> 20 us
  waiting for transfers between devices: 7.03 us -> 3.77 us
    ppermute x12, waiting for transfers between devices: 6.82 us -> 3.24 us  [exchange(): out[k] = lax.ppermute(parts[k], 'seq', [(s, s ^ k) for s in range(count)])]
    pallas_call x6 -> x10, Pallas kernels: 10.6 us -> 13.5 us  [the longest x4 8.89 us: inner_terms(): pl.pallas_call(functools.partial(inner_kernel, head_dim, chunk, parts, le...]
    ppermute x12, starting transfers between devices: 16 us -> 15.4 us  [exchange(): out[k] = lax.ppermute(parts[k], 'seq', [(s, s ^ k) for s in range(count)])]
  transfers between devices with their start and end apart: 17 -> 17, of which waited for: 8 -> 6; matrix products, arithmetic and copies ran while one was open for 0% -> 0% of each run, Pallas kernels for 26% -> 33%
where the time goes in v10:
time: 49.3 us; the launch traced here: 49.1 us
  starting transfers between devices  23.7 us (48%)
  Pallas kernels  20 us (41%)
  waiting for transfers between devices  3.77 us (8%)
  between operations  0.84 us (2%)
  local copies, waits for them, and re-layouts  0.69 us (1%)
    ppermute x12, starting transfers between devices, exchange(): out[k] = lax.ppermute(parts[k], 'seq', [(s, s ^ k) for s in range(count)])  15.4 us
    pallas_call x4, Pallas kernels, inner_terms(): pl.pallas_call(functools.partial(inner_kernel, head_dim, chunk, parts, le...  8.89 us
    ppermute x4, starting transfers between devices, to_group(): lax.ppermute(block, 'seq', [(s, s ^ k * group) for s in range(count)])  8.21 us
    pallas_call x1, Pallas kernels, first_states(): pl.pallas_call(functools.partial(first_states_kernel, head_dim, group), o...  3.63 us
    pallas_call x3, Pallas kernels, entry_values(): pl.pallas_call(functools.partial(values_kernel, chunk, last, ks), out_sha...  3.27 us
    ppermute x12, waiting for transfers between devices, exchange(): out[k] = lax.ppermute(parts[k], 'seq', [(s, s ^ k) for s in range(count)])  3.24 us
    pallas_call x1, Pallas kernels, next_states(): pl.pallas_call(functools.partial(next_states_kernel, head_dim, chunk), ou...  1.58 us
    pallas_call x3, Pallas kernels, entry_parts(): pl.pallas_call(functools.partial(parts_kernel, last, ks), out_shape=outs,...  1.33 us
  transfers between devices with their start and end apart: 17, of which 6 were waited for; matrix products, arithmetic and copies ran while one was open for 0% of the time, Pallas kernels for 33%

profile of v10, /device:TPU:0, one launch (start us, length us, event | category | flops | bytes accessed | tf_op | source)
XLA Modules:
  0.0 49.1 jit_solution(11826793871437043819)
XLA Ops:
  0.6 3.6 %first_states.1 = (f32[32,384]{1,0:T(8,128)S(1)}, bf16[384,128]{1,0:T(8,128)(2,1)S(1)}, bf16[384,128]{1,0:T(8,128)(2,1)S(1)}, bf16[384,2048]{1,0:T(8,128)(2,1)S(...) custom-call(s32[1]{0:T(128)} %bitcast.where, ...), custom_call_target="tpu_custom_call" | custom-call | flops 402653184 | bytes 6291456 | tf_op jit(solution)/shard_map/first_states/pallas_call | solution.py:206
  4.3 4.0 %collective-permute-start = (bf16[272,256]{1,0:T(8,128)(2,1)S(1)}, bf16[272,256]{1,0:T(8,128)(2,1)S(1)}, u32[]{:S(2)}, u32[]{:S(2)}) collective-permute-start(bf16[272,256]{1,0:T(8,128)(2,1)S(1)} %get-tuple-element.81), channel_id=1, source_target_pairs={{0,6},{2,4},{4,2},{6,0},{8,14},{10,12},{12,10},{14,8},{16,22},{18,... | collective-permute-start | bytes 417800 | tf_op jit(solution)/shard_map/ppermute | solution.py:408
  8.2 0.5 %collective-permute-start.1 = (bf16[272,256]{1,0:T(8,128)(2,1)S(1)}, bf16[272,256]{1,0:T(8,128)(2,1)S(1)}, u32[]{:S(2)}, u32[]{:S(2)}) collective-permute-start(bf16[272,256]{1,0:T(8,128)(2,1)S(1)} %get-tuple-element.82), channel_id=1, source_target_pairs={{0,4},{2,6},{4,0},{6,2},{8,12},{10,14},{12,8},{14,10},{16,20},{18,... | collective-permute-start | bytes 417800 | tf_op jit(solution)/shard_map/ppermute | solution.py:408
  8.7 0.1 collective-permute-start.2
  8.9 1.6 %next_states.1 = (bf16[384,1024]{1,0:T(8,128)(2,1)S(1)}, bf16[384,1024]{1,0:T(8,128)(2,1)S(1)}, bf16[384,1024]{1,0:T(8,128)(2,1)S(1)}, bf16[272,256]{1,0:T(8,128...) custom-call(s32[1]{0:T(128)} %bitcast.where, ...), custom_call_target="tpu_custom_call" | custom-call | flops 402653184 | bytes 3145728 | tf_op jit(solution)/shard_map/next_states/pallas_call | solution.py:221
  10.5 2.9 %collective-permute-start.4 = (bf16[272,256]{1,0:T(8,128)(2,1)S(1)}, bf16[272,256]{1,0:T(8,128)(2,1)S(1)}, u32[]{:S(2)}, u32[]{:S(2)}) collective-permute-start(bf16[272,256]{1,0:T(8,128)(2,1)S(1)} %get-tuple-element.86), channel_id=1, source_target_pairs={{0,6},{2,4},{4,2},{6,0},{8,14},{10,12},{12,10},{14,8},{16,22},{18,... | collective-permute-start | bytes 417800 | tf_op jit(solution)/shard_map/ppermute | solution.py:408
  13.4 0.5 %collective-permute-start.5 = (bf16[272,256]{1,0:T(8,128)(2,1)S(1)}, bf16[272,256]{1,0:T(8,128)(2,1)S(1)}, u32[]{:S(2)}, u32[]{:S(2)}) collective-permute-start(bf16[272,256]{1,0:T(8,128)(2,1)S(1)} %get-tuple-element.87), channel_id=1, source_target_pairs={{0,4},{2,6},{4,0},{6,2},{8,12},{10,14},{12,8},{14,10},{16,20},{18,... | collective-permute-start | bytes 417800 | tf_op jit(solution)/shard_map/ppermute | solution.py:408
  13.9 0.5 inner_setup.1
  14.3 0.0 collective-permute-done.refs_1_.refs_5_
  14.3 0.4 collective-permute-start.6
  14.7 1.4 %inner_terms.4 = (bf16[384,1024]{1,0:T(8,128)(2,1)S(1)}, f32[384,128]{1,0:T(8,128)S(1)}, f32[384,128]{1,0:T(8,128)S(1)}) custom-call(bf16[384,128]{1,0:T(8,128)(2,1)S(1)} %get-tuple-element.63.refs_0_.b, bf16[384,128]{1,0:T(8,128)(2,1)S(1)} %get-tuple-element.64.refs_1_.c, bf16[384,2048]{1,0:T(8,128)(2,1)S(1)} %get-tuple-element.65.refs_2_.x, ...), custom_call_target="tpu_custom_call" | custom-call | flops 805306368 | bytes 3145728 | tf_op jit(solution)/shard_map/inner_terms/pallas_call | solution.py:563
  16.1 0.3 collective-permute-done.1.refs_2_.refs_4_
  16.4 0.0 collective-permute-done.2.refs_3_
  16.4 0.1 totals.2.own
  16.6 1.6 %collective-permute-start.3 = (bf16[272,256]{1,0:T(8,128)(2,1)S(1)}, bf16[272,256]{1,0:T(8,128)(2,1)S(1)}, u32[]{:S(2)}, u32[]{:S(2)}) collective-permute-start(bf16[272,256]{1,0:T(8,128)(2,1)S(1)} %totals.2.own), channel_id=1, source_target_pairs={{0,8},{2,10},{4,12},{6,14},{8,0},{10,2},{12,4},{14,6},{16,24},{18,... | collective-permute-start | bytes 417800 | tf_op jit(solution)/shard_map/ppermute | solution.py:682
  18.2 1.1 %collective-permute-done.4.refs_1_.refs_5_ = bf16[272,256]{1,0:T(8,128)(2,1)S(1)} collective-permute-done((bf16[272,256]{1,0:T(8,128)(2,1)S(1)}, bf16[272,256]{1,0:T(8,128)(2,1)S(1)}, u32[]{:S(2)}, u32[]{:S(2)}) %collective-permute-start.4) | collective-permute-done | bytes 139296 | tf_op jit(solution)/shard_map/ppermute | solution.py:408
  19.3 1.6 %collective-permute-done.5.refs_2_.refs_4_ = bf16[272,256]{1,0:T(8,128)(2,1)S(1)} collective-permute-done((bf16[272,256]{1,0:T(8,128)(2,1)S(1)}, bf16[272,256]{1,0:T(8,128)(2,1)S(1)}, u32[]{:S(2)}, u32[]{:S(2)}) %collective-permute-start.5) | collective-permute-done | bytes 139296 | tf_op jit(solution)/shard_map/ppermute | solution.py:408
  20.9 0.3 collective-permute-done.6.refs_3_
  21.1 0.1 totals.3.own
  21.3 1.6 %collective-permute-start.7 = (bf16[272,256]{1,0:T(8,128)(2,1)S(1)}, bf16[272,256]{1,0:T(8,128)(2,1)S(1)}, u32[]{:S(2)}, u32[]{:S(2)}) collective-permute-start(bf16[272,256]{1,0:T(8,128)(2,1)S(1)} %totals.3.own), channel_id=1, source_target_pairs={{0,8},{2,10},{4,12},{6,14},{8,0},{10,2},{12,4},{14,6},{16,24},{18,... | collective-permute-start | bytes 417800 | tf_op jit(solution)/shard_map/ppermute | solution.py:682
  23.0 2.6 %collective-permute-start.12 = (bf16[144,256]{1,0:T(8,128)(2,1)S(1)}, bf16[144,256]{1,0:T(8,128)(2,1)S(1)}, u32[]{:S(2)}, u32[]{:S(2)}) collective-permute-start(bf16[144,256]{1,0:T(8,128)(2,1)S(1)} %merged.2.refs_10_), channel_id=1, source_target_pairs={{0,16},{2,18},{4,20},{6,22},{8,24},{10,26},{12,28},{14,30},{16,0},... | collective-permute-start | bytes 221192 | tf_op jit(solution)/shard_map/ppermute | solution.py:682
  25.6 3.1 %inner_terms.5 = (bf16[384,1024]{1,0:T(8,128)(2,1)S(1)}, f32[384,128]{1,0:T(8,128)S(1)}, f32[384,128]{1,0:T(8,128)S(1)}) custom-call(bf16[384,128]{1,0:T(8,128)(2,1)S(1)} %get-tuple-element.63.refs_0_.b, bf16[384,128]{1,0:T(8,128)(2,1)S(1)} %get-tuple-element.64.refs_1_.c, bf16[384,2048]{1,0:T(8,128)(2,1)S(1)} %get-tuple-element.65.refs_2_.x, ...), custom_call_target="tpu_custom_call" | custom-call | flops 805306368 | bytes 3145728 | tf_op jit(solution)/shard_map/inner_terms/pallas_call | solution.py:563
  28.7 0.1 collective-permute-done.12.refs_1_
  28.8 0.2 member_entries.3
  29.0 1.9 %collective-permute-start.13 = (bf16[256,256]{1,0:T(8,128)(2,1)S(1)}, bf16[256,256]{1,0:T(8,128)(2,1)S(1)}, u32[]{:S(2)}, u32[]{:S(2)}) collective-permute-start(bf16[256,256]{1,0:T(8,128)(2,1)S(1)} %get-tuple-element.100), channel_id=1, source_target_pairs={{0,6},{2,4},{4,2},{6,0},{8,14},{10,12},{12,10},{14,8},{16,22},{18,... | collective-permute-start | bytes 393224 | tf_op jit(solution)/shard_map/ppermute | solution.py:408
  30.9 0.0 collective-permute-done.7.received.refs_0_
  30.9 2.3 %collective-permute-start.8 = (bf16[144,256]{1,0:T(8,128)(2,1)S(1)}, bf16[144,256]{1,0:T(8,128)(2,1)S(1)}, u32[]{:S(2)}, u32[]{:S(2)}) collective-permute-start(bf16[144,256]{1,0:T(8,128)(2,1)S(1)} %merged.3.refs_9_), channel_id=1, source_target_pairs={{0,16},{2,18},{4,20},{6,22},{8,24},{10,26},{12,28},{14,30},{16,0},... | collective-permute-start | bytes 221192 | tf_op jit(solution)/shard_map/ppermute | solution.py:682
  33.2 1.1 %collective-permute-start.14 = (bf16[256,256]{1,0:T(8,128)(2,1)S(1)}, bf16[256,256]{1,0:T(8,128)(2,1)S(1)}, u32[]{:S(2)}, u32[]{:S(2)}) collective-permute-start(bf16[256,256]{1,0:T(8,128)(2,1)S(1)} %get-tuple-element.101), channel_id=1, source_target_pairs={{0,4},{2,6},{4,0},{6,2},{8,12},{10,14},{12,8},{14,10},{16,20},{18,... | collective-permute-start | bytes 393224 | tf_op jit(solution)/shard_map/ppermute | solution.py:408
  34.3 0.5 collective-permute-start.15
  34.8 3.1 %inner_terms.6 = (bf16[384,1024]{1,0:T(8,128)(2,1)S(1)}, f32[384,128]{1,0:T(8,128)S(1)}, f32[384,128]{1,0:T(8,128)S(1)}) custom-call(bf16[384,128]{1,0:T(8,128)(2,1)S(1)} %get-tuple-element.63.refs_0_.b, bf16[384,128]{1,0:T(8,128)(2,1)S(1)} %get-tuple-element.64.refs_1_.c, bf16[384,2048]{1,0:T(8,128)(2,1)S(1)} %get-tuple-element.65.refs_2_.x, ...), custom_call_target="tpu_custom_call" | custom-call | flops 805306368 | bytes 3145728 | tf_op jit(solution)/shard_map/inner_terms/pallas_call | solution.py:563
  37.9 0.4 member_entries.2
  38.3 2.0 %collective-permute-start.11 = (bf16[256,256]{1,0:T(8,128)(2,1)S(1)}, bf16[256,256]{1,0:T(8,128)(2,1)S(1)}, u32[]{:S(2)}, u32[]{:S(2)}) collective-permute-start(bf16[256,256]{1,0:T(8,128)(2,1)S(1)} %get-tuple-element.96), channel_id=1, source_target_pairs={{0,6},{2,4},{4,2},{6,0},{8,14},{10,12},{12,10},{14,8},{16,22},{18,... | collective-permute-start | bytes 393224 | tf_op jit(solution)/shard_map/ppermute | solution.py:408
  40.2 1.1 %collective-permute-start.10 = (bf16[256,256]{1,0:T(8,128)(2,1)S(1)}, bf16[256,256]{1,0:T(8,128)(2,1)S(1)}, u32[]{:S(2)}, u32[]{:S(2)}) collective-permute-start(bf16[256,256]{1,0:T(8,128)(2,1)S(1)} %get-tuple-element.95), channel_id=1, source_target_pairs={{0,2},{2,0},{4,6},{6,4},{8,10},{10,8},{12,14},{14,12},{16,18},{18,... | collective-permute-start | bytes 393224 | tf_op jit(solution)/shard_map/ppermute | solution.py:408
  41.4 0.5 collective-permute-start.9
  41.8 1.4 %inner_terms.7 = (bf16[384,1024]{1,0:T(8,128)(2,1)S(1)}, f32[384,128]{1,0:T(8,128)S(1)}, f32[384,128]{1,0:T(8,128)S(1)}) custom-call(bf16[384,128]{1,0:T(8,128)(2,1)S(1)} %get-tuple-element.63.refs_0_.b, bf16[384,128]{1,0:T(8,128)(2,1)S(1)} %get-tuple-element.64.refs_1_.c, bf16[384,2048]{1,0:T(8,128)(2,1)S(1)} %get-tuple-element.65.refs_2_.x, ...), custom_call_target="tpu_custom_call" | custom-call | flops 805306368 | bytes 3145728 | tf_op jit(solution)/shard_map/inner_terms/pallas_call | solution.py:563
  43.2 0.0 collective-permute-done.15.refs_3_
  43.2 1.2 %entry_values.3 = (bf16[384,2048]{1,0:T(8,128)(2,1)}, f32[8,128]{1,0:T(8,128)S(1)}) custom-call(s32[1]{0:T(128)} %bitcast.where, bf16[384,1024]{1,0:T(8,128)(2,1)S(1)} %get-tuple-element.97.spread, bf16[384,128]{1,0:T(8,128)(2,1)S(1)} %get-tuple-element.63.refs_0_.b, bf16[384,1024]{1,0:T(8,128)(2,1)S(1)} %get-tuple-element.98.dx_local, ...), custom_call_target="tpu_custom_call" | custom-call | flops 100663296 | bytes 1572864 | tf_op jit(solution)/shard_map/entry_values/pallas_call | solution.py:638
  44.4 1.0 %entry_values.4 = (bf16[384,2048]{1,0:T(8,128)(2,1)}, f32[8,128]{1,0:T(8,128)S(1)}) custom-call(s32[1]{0:T(128)} %bitcast.where, bf16[384,1024]{1,0:T(8,128)(2,1)S(1)} %get-tuple-element.67.spread, bf16[384,128]{1,0:T(8,128)(2,1)S(1)} %get-tuple-element.63.refs_0_.b, ...), custom_call_target="tpu_custom_call", output_to_operand_aliasing={{0}: (6, {})} | custom-call | flops 50331648 | bytes 786432 | tf_op jit(solution)/shard_map/entry_values/pallas_call | solution.py:638
  45.5 0.6 %entry_parts.3 = (f32[384,128]{1,0:T(8,128)S(1)}, f32[384,128]{1,0:T(8,128)S(1)}) custom-call(bf16[384,1024]{1,0:T(8,128)(2,1)S(1)} %get-tuple-element.107.x_scaled, bf16[384,1024]{1,0:T(8,128)(2,1)S(1)} %get-tuple-element.108.dy_scaled, f32[384,128]{1,0:T(8,128)S(1)} %get-tuple-element.109.db_before, f32[384,128]{1,0:T(8,128)S(1)} %get-tuple-element.110.dc_before, ...), custom_call_target="tpu_custom_call" | custom-call | flops 201326592 | bytes 1572864 | tf_op jit(solution)/shard_map/entry_parts/pallas_call | solution.py:602
  46.1 0.4 entry_parts.4
  46.4 0.0 collective-permute-done.10.refs_1_
  46.4 0.0 collective-permute-done.9.refs_0_
  46.5 0.4 entry_parts.5
  46.8 0.1 collective-permute-start.16
  46.9 1.0 %entry_values.5 = bf16[384,2048]{1,0:T(8,128)(2,1)} custom-call(s32[1]{0:T(128)} %bitcast.where, bf16[384,1024]{1,0:T(8,128)(2,1)S(1)} %get-tuple-element.67.spread, bf16[384,128]{1,0:T(8,128)(2,1)S(1)} %get-tuple-element.63.refs_0_.b, bf16[384,1024]{1,0:T(8,128)(2,1)S(1)} %get-tuple-element.93.dx_local, ...), custom_call_target="tpu_custom_call", output_to_operand_aliasing={{}: (6, {})} | custom-call | flops 50331648 | bytes 786432 | tf_op jit(solution)/shard_map/entry_values/pallas_call | solution.py:638
  48.0 0.4 collective-permute-done.16
  48.4 0.1 add_convert_fusion
  48.4 0.7 %fusion = (bf16[384,128]{1,0:T(8,128)(2,1)}, bf16[384,128]{1,0:T(8,128)(2,1)}) fusion(bf16[768,128]{1,0:T(8,128)(2,1)S(1)} %add_convert_fusion), kind=kLoop, calls=%fused_computation.1 | loop fusion | bytes 393216 | tf_op jit(solution)/shard_map/slice | solution.py:715
  (7 shorter events, 0.1 us)
Async XLA Ops:
  4.3 10.1 %collective-permute-start = (bf16[272,256]{1,0:T(8,128)(2,1)S(1)}, bf16[272,256]{1,0:T(8,128)(2,1)S(1)}, u32[]{:S(2)}, u32[]{:S(2)}) collective-permute-start(bf16[272,256]{1,0:T(8,128)(2,1)S(1)} %get-tuple-element.81), channel_id=1, source_target_pairs={{0,6},{2,4},{4,2},{6,0},{8,14},{10,12},{12,10},{14,8},{16,22},{18,... | collective-permute-start | bytes 417800 | tf_op jit(solution)/shard_map/ppermute | solution.py:408
  8.2 8.2 %collective-permute-start.1 = (bf16[272,256]{1,0:T(8,128)(2,1)S(1)}, bf16[272,256]{1,0:T(8,128)(2,1)S(1)}, u32[]{:S(2)}, u32[]{:S(2)}) collective-permute-start(bf16[272,256]{1,0:T(8,128)(2,1)S(1)} %get-tuple-element.82), channel_id=1, source_target_pairs={{0,4},{2,6},{4,0},{6,2},{8,12},{10,14},{12,8},{14,10},{16,20},{18,... | collective-permute-start | bytes 417800 | tf_op jit(solution)/shard_map/ppermute | solution.py:408
  8.7 7.7 %collective-permute-start.2 = (bf16[272,256]{1,0:T(8,128)(2,1)S(1)}, bf16[272,256]{1,0:T(8,128)(2,1)S(1)}, u32[]{:S(2)}, u32[]{:S(2)}) collective-permute-start(bf16[272,256]{1,0:T(8,128)(2,1)S(1)} %get-tuple-element.83), channel_id=1, source_target_pairs={{0,2},{2,0},{4,6},{6,4},{8,10},{10,8},{12,14},{14,12},{16,18},{18,... | collective-permute-start | bytes 417800 | tf_op jit(solution)/shard_map/ppermute | solution.py:408
  10.5 8.8 %collective-permute-start.4 = (bf16[272,256]{1,0:T(8,128)(2,1)S(1)}, bf16[272,256]{1,0:T(8,128)(2,1)S(1)}, u32[]{:S(2)}, u32[]{:S(2)}) collective-permute-start(bf16[272,256]{1,0:T(8,128)(2,1)S(1)} %get-tuple-element.86), channel_id=1, source_target_pairs={{0,6},{2,4},{4,2},{6,0},{8,14},{10,12},{12,10},{14,8},{16,22},{18,... | collective-permute-start | bytes 417800 | tf_op jit(solution)/shard_map/ppermute | solution.py:408
  13.4 7.5 %collective-permute-start.5 = (bf16[272,256]{1,0:T(8,128)(2,1)S(1)}, bf16[272,256]{1,0:T(8,128)(2,1)S(1)}, u32[]{:S(2)}, u32[]{:S(2)}) collective-permute-start(bf16[272,256]{1,0:T(8,128)(2,1)S(1)} %get-tuple-element.87), channel_id=1, source_target_pairs={{0,4},{2,6},{4,0},{6,2},{8,12},{10,14},{12,8},{14,10},{16,20},{18,... | collective-permute-start | bytes 417800 | tf_op jit(solution)/shard_map/ppermute | solution.py:408
  14.3 6.8 %collective-permute-start.6 = (bf16[272,256]{1,0:T(8,128)(2,1)S(1)}, bf16[272,256]{1,0:T(8,128)(2,1)S(1)}, u32[]{:S(2)}, u32[]{:S(2)}) collective-permute-start(bf16[272,256]{1,0:T(8,128)(2,1)S(1)} %get-tuple-element.88), channel_id=1, source_target_pairs={{0,2},{2,0},{4,6},{6,4},{8,10},{10,8},{12,14},{14,12},{16,18},{18,... | collective-permute-start | bytes 417800 | tf_op jit(solution)/shard_map/ppermute | solution.py:408
  16.6 6.3 %collective-permute-start.3 = (bf16[272,256]{1,0:T(8,128)(2,1)S(1)}, bf16[272,256]{1,0:T(8,128)(2,1)S(1)}, u32[]{:S(2)}, u32[]{:S(2)}) collective-permute-start(bf16[272,256]{1,0:T(8,128)(2,1)S(1)} %totals.2.own), channel_id=1, source_target_pairs={{0,8},{2,10},{4,12},{6,14},{8,0},{10,2},{12,4},{14,6},{16,24},{18,... | collective-permute-start | bytes 417800 | tf_op jit(solution)/shard_map/ppermute | solution.py:682
  21.3 9.6 %collective-permute-start.7 = (bf16[272,256]{1,0:T(8,128)(2,1)S(1)}, bf16[272,256]{1,0:T(8,128)(2,1)S(1)}, u32[]{:S(2)}, u32[]{:S(2)}) collective-permute-start(bf16[272,256]{1,0:T(8,128)(2,1)S(1)} %totals.3.own), channel_id=1, source_target_pairs={{0,8},{2,10},{4,12},{6,14},{8,0},{10,2},{12,4},{14,6},{16,24},{18,... | collective-permute-start | bytes 417800 | tf_op jit(solution)/shard_map/ppermute | solution.py:682
  23.0 5.9 %collective-permute-start.12 = (bf16[144,256]{1,0:T(8,128)(2,1)S(1)}, bf16[144,256]{1,0:T(8,128)(2,1)S(1)}, u32[]{:S(2)}, u32[]{:S(2)}) collective-permute-start(bf16[144,256]{1,0:T(8,128)(2,1)S(1)} %merged.2.refs_10_), channel_id=1, source_target_pairs={{0,16},{2,18},{4,20},{6,22},{8,24},{10,26},{12,28},{14,30},{16,0},... | collective-permute-start | bytes 221192 | tf_op jit(solution)/shard_map/ppermute | solution.py:682
  29.0 12.4 %collective-permute-start.13 = (bf16[256,256]{1,0:T(8,128)(2,1)S(1)}, bf16[256,256]{1,0:T(8,128)(2,1)S(1)}, u32[]{:S(2)}, u32[]{:S(2)}) collective-permute-start(bf16[256,256]{1,0:T(8,128)(2,1)S(1)} %get-tuple-element.100), channel_id=1, source_target_pairs={{0,6},{2,4},{4,2},{6,0},{8,14},{10,12},{12,10},{14,8},{16,22},{18,... | collective-permute-start | bytes 393224 | tf_op jit(solution)/shard_map/ppermute | solution.py:408
  30.9 6.9 %collective-permute-start.8 = (bf16[144,256]{1,0:T(8,128)(2,1)S(1)}, bf16[144,256]{1,0:T(8,128)(2,1)S(1)}, u32[]{:S(2)}, u32[]{:S(2)}) collective-permute-start(bf16[144,256]{1,0:T(8,128)(2,1)S(1)} %merged.3.refs_9_), channel_id=1, source_target_pairs={{0,16},{2,18},{4,20},{6,22},{8,24},{10,26},{12,28},{14,30},{16,0},... | collective-permute-start | bytes 221192 | tf_op jit(solution)/shard_map/ppermute | solution.py:682
  33.2 10.0 %collective-permute-start.14 = (bf16[256,256]{1,0:T(8,128)(2,1)S(1)}, bf16[256,256]{1,0:T(8,128)(2,1)S(1)}, u32[]{:S(2)}, u32[]{:S(2)}) collective-permute-start(bf16[256,256]{1,0:T(8,128)(2,1)S(1)} %get-tuple-element.101), channel_id=1, source_target_pairs={{0,4},{2,6},{4,0},{6,2},{8,12},{10,14},{12,8},{14,10},{16,20},{18,... | collective-permute-start | bytes 393224 | tf_op jit(solution)/shard_map/ppermute | solution.py:408
  34.3 8.9 %collective-permute-start.15 = (bf16[256,256]{1,0:T(8,128)(2,1)S(1)}, bf16[256,256]{1,0:T(8,128)(2,1)S(1)}, u32[]{:S(2)}, u32[]{:S(2)}) collective-permute-start(bf16[256,256]{1,0:T(8,128)(2,1)S(1)} %get-tuple-element.102), channel_id=1, source_target_pairs={{0,2},{2,0},{4,6},{6,4},{8,10},{10,8},{12,14},{14,12},{16,18},{18,... | collective-permute-start | bytes 393224 | tf_op jit(solution)/shard_map/ppermute | solution.py:408
  38.3 6.2 %collective-permute-start.11 = (bf16[256,256]{1,0:T(8,128)(2,1)S(1)}, bf16[256,256]{1,0:T(8,128)(2,1)S(1)}, u32[]{:S(2)}, u32[]{:S(2)}) collective-permute-start(bf16[256,256]{1,0:T(8,128)(2,1)S(1)} %get-tuple-element.96), channel_id=1, source_target_pairs={{0,6},{2,4},{4,2},{6,0},{8,14},{10,12},{12,10},{14,8},{16,22},{18,... | collective-permute-start | bytes 393224 | tf_op jit(solution)/shard_map/ppermute | solution.py:408
  40.2 6.2 %collective-permute-start.10 = (bf16[256,256]{1,0:T(8,128)(2,1)S(1)}, bf16[256,256]{1,0:T(8,128)(2,1)S(1)}, u32[]{:S(2)}, u32[]{:S(2)}) collective-permute-start(bf16[256,256]{1,0:T(8,128)(2,1)S(1)} %get-tuple-element.95), channel_id=1, source_target_pairs={{0,2},{2,0},{4,6},{6,4},{8,10},{10,8},{12,14},{14,12},{16,18},{18,... | collective-permute-start | bytes 393224 | tf_op jit(solution)/shard_map/ppermute | solution.py:408
  41.4 5.1 %collective-permute-start.9 = (bf16[256,256]{1,0:T(8,128)(2,1)S(1)}, bf16[256,256]{1,0:T(8,128)(2,1)S(1)}, u32[]{:S(2)}, u32[]{:S(2)}) collective-permute-start(bf16[256,256]{1,0:T(8,128)(2,1)S(1)} %get-tuple-element.94), channel_id=1, source_target_pairs={{0,4},{2,6},{4,0},{6,2},{8,12},{10,14},{12,8},{14,10},{16,20},{18,... | collective-permute-start | bytes 393224 | tf_op jit(solution)/shard_map/ppermute | solution.py:408
  46.8 1.5 %collective-permute-start.16 = (bf16[768,128]{1,0:T(8,128)(2,1)S(1)}, bf16[768,128]{1,0:T(8,128)(2,1)S(1)}, u32[]{:S(2)}, u32[]{:S(2)}) collective-permute-start(bf16[768,128]{1,0:T(8,128)(2,1)S(1)} %entry_parts.5), channel_id=1, source_target_pairs={{0,1},{1,0},{2,3},{3,2},{4,5},{5,4},{6,7},{7,6},{8,9},{9,8},{10,11... | collective-permute-start | bytes 589832 | tf_op jit(solution)/shard_map/ppermute | solution.py:659

commit v11 on v8

--- a/solution.py
+++ b/solution.py
@@ -219,8 +219,8 @@
     ref[first:, :] = both.astype(BF16)
 
 
-def sent_order(parts, fixed=1):
-    return [*parts[:fixed], *parts[: fixed - 1 : -1]]
+def sent_order(parts):
+    return [parts[0], *parts[:0:-1]]
 
 
 def in_order(group, forward):
@@ -231,9 +231,9 @@
     return slice(0, state) if forward else slice(state, 2 * state)
 
 
-def totals_kernel(state, levels, where, *refs):
+def totals_kernel(state, split, where, *refs):
     group = GROUP
-    blocks, outs, sums = sent_order(refs[:group]), refs[-1 - levels : -1], refs[-1]
+    blocks, sums = sent_order(refs[:group]), refs[-1]
     for here in range(group):
 
         @pl.when(place_of(where) == here)
@@ -249,32 +249,54 @@
     factor = decay_of(blocks[0][2 * state :, :])
     for block in blocks[1:]:
         factor = factor * decay_of(block[2 * state :, :])
-    if not levels:
+    if not split:
         put_decay(sums, 2 * state, factor)
-    for level, out in enumerate(outs):
+        return
+    sent, kept = refs[-3:-1]
+    for out in (sent, kept):
         put_decay(out, state, factor)
-        for forward in (True, False):
-
-            @pl.when(bit_of(where, level) != forward)
-            def _(out=out, forward=forward):
-                out[:state, :] = sums[side_rows(state, forward), :]
-
-
-def totals(state, levels, where, blocks, after):
+    for odd in (False, True):
+
+        @pl.when(bit_of(where, 0) == odd)
+        def _(odd=odd):
+            sent[:state, :] = sums[side_rows(state, not odd), :]
+            kept[:state, :] = sums[side_rows(state, odd), :]
+
+
+def totals(state, split, where, blocks, after):
     part = blocks[0].shape[1]
-    outs = [jax.ShapeDtypeStruct((state + TAIL, part), BF16)] * levels
-    if not levels:
+    if split:
+        outs = [jax.ShapeDtypeStruct((state + TAIL, part), BF16)] * 2
+    else:
         outs = [jax.ShapeDtypeStruct(blocks[0].shape, BF16)]
     return pl.pallas_call(
-        functools.partial(totals_kernel, state, levels),
+        functools.partial(totals_kernel, state, split),
         out_shape=outs,
         in_specs=[SMEM] + whole(len(blocks)) + [ANY] * len(after),
         out_specs=whole(len(outs)),
-        scratch_shapes=[pltpu.VMEM((2 * state, part), BF16)] if levels else [],
+        scratch_shapes=[pltpu.VMEM((2 * state, part), BF16)] if split else [],
         compiler_params=params(4),
         cost_estimate=cost(8 * blocks[0].size, 10 * blocks[0].size),
         name="totals",
     )(where, *sent_order(blocks), *after)
+
+
+def joined_kernel(state, kept, received, out):
+    d = decay_of(kept[state:, :])
+    value = kept[:state, :].astype(F32) + d * received[:state, :].astype(F32)
+    out[...] = value.astype(BF16)
+
+
+def joined(state, kept, received):
+    return pl.pallas_call(
+        functools.partial(joined_kernel, state),
+        out_shape=jax.ShapeDtypeStruct((state, kept.shape[1]), BF16),
+        in_specs=whole(2),
+        out_specs=whole(1)[0],
+        compiler_params=params(4),
+        cost_estimate=cost(2 * kept.size, 4 * kept.size),
+        name="joined",
+    )(kept, received)
 
 
 def merged_kernel(state, level, last, where, own, received, *refs):
@@ -311,22 +333,20 @@
     )(where, own, received, *after)
 
 
-def put_direct(state, groups, number, received, entry):
-    for mine in range(groups):
-
-        @pl.when(number == mine)
-        def _(mine=mine):
-            for forward in (True, False):
-                rows = side_rows(state, forward)
-                others = range(mine - 1, -1, -1) if forward else range(mine + 1, groups)
-                value, factor = jnp.zeros((state, entry.shape[1]), F32), None
-                for other in others:
-                    r = received[(mine ^ other) - 1]
-                    piece = r[:state, :].astype(F32)
-                    value = piece if factor is None else value + factor * piece
-                    d = decay_of(r[state:, :])
-                    factor = d if factor is None else factor * d
-                entry[rows, :] = value
+def put_four(state, where, received, entry):
+    near, middle, outer = received
+    d = decay_of(near[state:, :])
+    is_middle = bit_of(where, 0) != bit_of(where, 1)
+    for forward in (True, False):
+        gets = bit_of(where, 0) == forward
+        from_near = jnp.where(gets, 1.0, 0.0)
+        from_far = jnp.where(bit_of(where, 1) == forward, 1.0, 0.0)
+        of_middle = jnp.where(is_middle, from_far, 0.0)
+        far = middle[...].astype(F32) * of_middle
+        far = far + outer[...].astype(F32) * (from_far - of_middle)
+        factor = jnp.where(gets, d, 1.0)
+        value = near[:state, :].astype(F32) * from_near + factor * far
+        entry[side_rows(state, forward), :] = value
 
 
 def put_rounds(state, where, received, entry):
@@ -343,12 +363,12 @@
         entry[side_rows(state, forward), :] = value
 
 
-def members_kernel(state, direct, n_received, where, *refs):
+def members_kernel(state, four, n_received, where, *refs):
     received, refs = refs[:n_received], refs[n_received:]
     group = GROUP
     blocks, outs, entry = refs[:group], refs[-1 - group : -1], refs[-1]
-    if direct:
-        put_direct(state, n_received + 1, where[0] // group, received, entry)
+    if four:
+        put_four(state, where, received, entry)
     else:
         put_rounds(state, where, received, entry)
     for here in range(group):
@@ -365,10 +385,10 @@
                         value = decays[q] * value + blocks[q ^ here][rows, :].astype(F32)
 
 
-def member_entries(state, direct, where, blocks, received, after):
+def member_entries(state, four, where, blocks, received, after):
     group, part = len(blocks), blocks[0].shape[1]
     return pl.pallas_call(
-        functools.partial(members_kernel, state, direct, len(received)),
+        functools.partial(members_kernel, state, four, len(received)),
         out_shape=[jax.ShapeDtypeStruct((2 * state, part), BF16)] * group,
         in_specs=[SMEM] + whole(group + len(received)) + [ANY] * len(after),
         out_specs=whole(group),
@@ -584,47 +604,77 @@
     )(x_scaled, dy_scaled, db_before, dc_before, *sent_order(entries), *after)
 
 
-def values_kernel(chunk, last, where, spread, b, dx_local, *refs):
-    entries, (dx, sems) = sent_order(refs[:GROUP], 2 if last else 1), refs[-2:]
-    out = refs[-3 if last else -4]
-    if not last:
-        refs[-3][...] = jnp.zeros_like(refs[-3])
+def put_values(where, spread, b, dx_local, entries, put):
     state, part = b.shape[1], entries[0].shape[1]
-    stores = []
     for k, entry in enumerate(entries):
         here = slice(k * part, (k + 1) * part)
         local = dx_local[:, pl.ds(pl.multiple_of((place_of(where) ^ k) * part, part), part)]
         far = spread[:, here].astype(F32) * dot(b[...], entry[state:, :], NN)
-        dx[k] = (local.astype(F32) + far).astype(BF16)
+        put(k, here, (local.astype(F32) + far).astype(BF16))
+
+
+def values_kernel(where, spread, b, dx_local, *refs):
+    entries, out = sent_order(refs[:GROUP]), refs[-1]
+
+    def put(k, here, value):
+        out[:, here] = value
+
+    put_values(where, spread, b, dx_local, entries, put)
+
+
+def last_values_kernel(chunks, where, spread, b, dx_local, *refs):
+    entries, before = sent_order(refs[:GROUP]), refs[GROUP : GROUP + chunks - 1]
+    out, dx, sems = refs[-3:]
+    part = entries[0].shape[1]
+    stores = []
+
+    def store(chunk, k, source):
         lanes = chunk_lanes(where, k, chunk, part, out.shape[1])
-        store = pltpu.make_async_copy(dx.at[k], out.at[:, lanes], sems.at[k])
-        store.start()
-        stores.append(store)
-    for store in stores:
-        store.wait()
-
-
-def entry_values(chunk, chunks, where, spread, b, dx_local, entries, before, after):
-    group, part = len(entries), entries[0].shape[1]
-    length, state = b.shape
-    size, last = dx_local.size, chunk == chunks - 1
-    sent = sent_order(entries, 2 if last else 1)
-    operands = [where, spread, b, dx_local, *sent, *after, *before]
-    return pl.pallas_call(
-        functools.partial(values_kernel, chunk, last),
-        out_shape=[pltpu.HBM((length, chunks * group * part), BF16)]
-        + [pltpu.VMEM((8, LANES), F32)] * (not last),
-        in_specs=[SMEM] + whole(3 + group) + [ANY] * len(after) + [HBM] * len(before),
-        out_specs=[HBM] + whole(0 if last else 1),
-        input_output_aliases={len(operands) - 1: 0} if before else {},
+        at = sems.at[chunk * GROUP + k]
+        stores.append(pltpu.make_async_copy(source, out.at[:, lanes], at))
+        stores[-1].start()
+
+    for chunk, values in enumerate(before):
+        for k in range(GROUP):
+            store(chunk, k, values.at[:, pl.ds(k * part, part)])
+
+    def put(k, here, value):
+        dx[k] = value
+        store(chunks - 1, k, dx.at[k])
+
+    put_values(where, spread, b, dx_local, entries, put)
+    for one in stores:
+        one.wait()
+
+
+def entry_values(chunk, chunks, where, spread, b, dx_local, entries, before):
+    length, part = b.shape[0], entries[0].shape[1]
+    last = chunk == chunks - 1
+    estimate = cost(2 * dx_local.size * b.shape[1], 4 * dx_local.size)
+    operands = [where, spread, b, dx_local, *sent_order(entries)]
+    if not last:
+        return pl.pallas_call(
+            values_kernel,
+            out_shape=jax.ShapeDtypeStruct((length, GROUP * part), BF16),
+            in_specs=[SMEM] + whole(3 + GROUP),
+            out_specs=whole(1)[0],
+            compiler_params=params(8),
+            cost_estimate=estimate,
+            name="entry_values",
+        )(*operands)
+    return pl.pallas_call(
+        functools.partial(last_values_kernel, chunks),
+        out_shape=pltpu.HBM((length, chunks * GROUP * part), BF16),
+        in_specs=[SMEM] + whole(3 + GROUP + len(before)),
+        out_specs=HBM,
         scratch_shapes=[
-            pltpu.VMEM((group, length, part), BF16),
-            pltpu.SemaphoreType.DMA((group,)),
+            pltpu.VMEM((GROUP, length, part), BF16),
+            pltpu.SemaphoreType.DMA((chunks * GROUP,)),
         ],
         compiler_params=params(8),
-        cost_estimate=cost(2 * size * state, 4 * size),
-        name="entry_values",
-    )(*operands)
+        cost_estimate=estimate,
+        name="last_values",
+    )(*operands, *before)
 
 
 def over_heads(part):
@@ -655,30 +705,42 @@
     def to_group(block, k):
         return lax.ppermute(block, "seq", [(s, s ^ (k * group)) for s in range(count)])
 
+    groups = count // group
+    four = groups == 4
+    received, after = [], setup[-1:]
+    for chunk in range(chunks):
+        sent, *kept = totals(state, four, where, blocks[chunk], after)
+        received.append([to_group(sent, 1)])
+        if four:
+            sent = joined(state, kept[0], received[chunk][0])
+            for other in ([(1, 2), (2, 1)], [(1, 3), (2, 0)]):
+                pairs = [(m * group + j, n * group + j) for m, n in other for j in range(group)]
+                received[chunk].append(lax.ppermute(sent, "seq", pairs))
+        else:
+            for level in range(levels - 1):
+                last = level == levels - 2
+                sent = merged(state, level, last, where, sent, received[chunk][level], [])
+                received[chunk].append(to_group(sent, 2 << level))
+        after = [sent]
     entries, inner, sums = [], [], []
     for chunk in range(chunks):
-        (own,) = totals(state, 0, where, blocks[chunk], setup[-1:] if chunk == 0 else [])
-        received = [to_group(own, 1)]
-        for level in range(levels - 1):
-            last = level == levels - 2
-            own = merged(state, level, last, where, own, received[level], [])
-            received.append(to_group(own, 2 << level))
-        inner.append(inner_terms(head_dim, chunk, setup, b, c, x, dy, sums, [own]))
+        found = member_entries(state, four, where, blocks[chunk], received[chunk], sums[:1])
+        entries.append(exchange(found))
+        inner.append(inner_terms(head_dim, chunk, setup, b, c, x, dy, sums, found[:1]))
         sums = list(inner[chunk][1:])
-        found = member_entries(state, False, where, blocks[chunk], received, sums[:1])
-        entries.append(exchange(found))
-
-    grad_values, done = [], []
+
+    values = []
     for chunk in range(chunks):
         x_scaled, dy_scaled, spread = states[chunk][:3]
         last = chunk == chunks - 1
-        sums = entry_parts(last, x_scaled, dy_scaled, *sums, entries[chunk], done)
-        outs = entry_values(
-            chunk, chunks, where, spread, b, inner[chunk][0], entries[chunk], grad_values, []
+        sums = entry_parts(last, x_scaled, dy_scaled, *sums, entries[chunk], values)
+        values.append(
+            entry_values(
+                chunk, chunks, where, spread, b, inner[chunk][0], entries[chunk], values
+            )
         )
-        grad_values, done = list(outs[:1]), list(outs[1:])
     both = over_heads(sums[0])
-    return grad_values[0], both[:length], both[length:]
+    return values[-1], both[:length], both[length:]
 
 
 def solution(mesh):

time: 49.2 us -> 54 us (1.098)
  the two profiles are of different devices: /device:TPU:0 before, /device:TPU:15 now
where the time goes in v11:
time: 54 us; the launch traced here: 53.8 us
  starting transfers between devices  29.1 us (54%)
  Pallas kernels  15.9 us (29%)
  waiting for transfers between devices  7.05 us (13%)
  between operations  0.89 us (2%)
  local copies, waits for them, and re-layouts  0.69 us (1%)
    ppermute x12, starting transfers between devices, exchange(): out[k] = lax.ppermute(parts[k], 'seq', [(s, s ^ k) for s in range(count)])  12 us
    ppermute x4, starting transfers between devices, shards(): received[chunk].append(lax.ppermute(sent, 'seq', pairs))  9.95 us
    pallas_call x2, Pallas kernels, inner_terms(): pl.pallas_call(functools.partial(inner_kernel, head_dim, chunk, len(befor...  6.93 us
    ppermute x1, starting transfers between devices, over_heads(): total = total + lax.ppermute(part, 'head', pairs).astype(F32)  6.88 us
    ppermute x2, waiting for transfers between devices, to_group(): lax.ppermute(block, 'seq', [(s, s ^ k * group) for s in range(count)])  3.33 us
    pallas_call x1, Pallas kernels, first_states(): pl.pallas_call(functools.partial(first_states_kernel, head_dim, group), o...  3.26 us
    ppermute x4, waiting for transfers between devices, shards(): received[chunk].append(lax.ppermute(sent, 'seq', pairs))  3.04 us
    pallas_call x1, Pallas kernels, next_states(): pl.pallas_call(functools.partial(next_states_kernel, head_dim, chunk), ou...  1.58 us
  transfers between devices with their start and end apart: 19, of which 3 were waited for; matrix products, arithmetic and copies ran while one was open for 0% of the time, Pallas kernels for 23%

profile of v11, /device:TPU:15, one launch (start us, length us, event | category | flops | bytes accessed | tf_op | source)
XLA Modules:
  0.0 53.8 jit_solution(3357574025992941006)
XLA Ops:
  0.6 3.3 %first_states.1 = (f32[32,384]{1,0:T(8,128)S(1)}, bf16[384,128]{1,0:T(8,128)(2,1)S(1)}, bf16[384,128]{1,0:T(8,128)(2,1)S(1)}, bf16[384,2048]{1,0:T(8,128)(2,1)S(...) custom-call(s32[1]{0:T(128)} %bitcast.where, ...), custom_call_target="tpu_custom_call" | custom-call | flops 402653184 | bytes 6291456 | tf_op jit(solution)/shard_map/first_states/pallas_call | solution.py:184
  3.9 0.3 collective-permute-start
  4.2 1.2 %collective-permute-start.1 = (bf16[272,256]{1,0:T(8,128)(2,1)S(1)}, bf16[272,256]{1,0:T(8,128)(2,1)S(1)}, u32[]{:S(2)}, u32[]{:S(2)}) collective-permute-start(bf16[272,256]{1,0:T(8,128)(2,1)S(1)} %get-tuple-element.71), channel_id=1, source_target_pairs={{0,4},{2,6},{4,0},{6,2},{8,12},{10,14},{12,8},{14,10},{16,20},{18,... | collective-permute-start | bytes 417800 | tf_op jit(solution)/shard_map/ppermute | solution.py:406
  5.4 1.2 %collective-permute-start.2 = (bf16[272,256]{1,0:T(8,128)(2,1)S(1)}, bf16[272,256]{1,0:T(8,128)(2,1)S(1)}, u32[]{:S(2)}, u32[]{:S(2)}) collective-permute-start(bf16[272,256]{1,0:T(8,128)(2,1)S(1)} %get-tuple-element.72), channel_id=1, source_target_pairs={{0,2},{2,0},{4,6},{6,4},{8,10},{10,8},{12,14},{14,12},{16,18},{18,... | collective-permute-start | bytes 417800 | tf_op jit(solution)/shard_map/ppermute | solution.py:406
  6.6 1.6 %next_states.1 = (bf16[384,1024]{1,0:T(8,128)(2,1)S(1)}, bf16[384,1024]{1,0:T(8,128)(2,1)S(1)}, bf16[384,1024]{1,0:T(8,128)(2,1)S(1)}, bf16[272,256]{1,0:T(8,128...) custom-call(s32[1]{0:T(128)} %bitcast.where, ...), custom_call_target="tpu_custom_call" | custom-call | flops 402653184 | bytes 3145728 | tf_op jit(solution)/shard_map/next_states/pallas_call | solution.py:199
  8.2 0.3 collective-permute-start.6
  8.5 1.2 %collective-permute-start.7 = (bf16[272,256]{1,0:T(8,128)(2,1)S(1)}, bf16[272,256]{1,0:T(8,128)(2,1)S(1)}, u32[]{:S(2)}, u32[]{:S(2)}) collective-permute-start(bf16[272,256]{1,0:T(8,128)(2,1)S(1)} %get-tuple-element.79), channel_id=1, source_target_pairs={{0,4},{2,6},{4,0},{6,2},{8,12},{10,14},{12,8},{14,10},{16,20},{18,... | collective-permute-start | bytes 417800 | tf_op jit(solution)/shard_map/ppermute | solution.py:406
  9.7 0.0 collective-permute-done.refs_1_.refs_6_
  9.7 1.2 %collective-permute-start.8 = (bf16[272,256]{1,0:T(8,128)(2,1)S(1)}, bf16[272,256]{1,0:T(8,128)(2,1)S(1)}, u32[]{:S(2)}, u32[]{:S(2)}) collective-permute-start(bf16[272,256]{1,0:T(8,128)(2,1)S(1)} %get-tuple-element.80), channel_id=1, source_target_pairs={{0,2},{2,0},{4,6},{6,4},{8,10},{10,8},{12,14},{14,12},{16,18},{18,... | collective-permute-start | bytes 417800 | tf_op jit(solution)/shard_map/ppermute | solution.py:406
  10.9 0.5 inner_setup.1
  11.4 0.6 %collective-permute-done.1.refs_2_.refs_5_ = bf16[272,256]{1,0:T(8,128)(2,1)S(1)} collective-permute-done((bf16[272,256]{1,0:T(8,128)(2,1)S(1)}, bf16[272,256]{1,0:T(8,128)(2,1)S(1)}, u32[]{:S(2)}, u32[]{:S(2)}) %collective-permute-start.1) | collective-permute-done | bytes 139296 | tf_op jit(solution)/shard_map/ppermute | solution.py:406
  12.0 0.0 collective-permute-done.2.refs_3_.refs_4_
  12.0 0.1 totals.2
  12.2 0.2 collective-permute-start.3
  12.4 3.3 %collective-permute-done.3.received.refs_0_ = bf16[144,256]{1,0:T(8,128)(2,1)S(1)} collective-permute-done((bf16[144,256]{1,0:T(8,128)(2,1)S(1)}, bf16[144,256]{1,0:T(8,128)(2,1)S(1)}, u32[]{:S(2)}, u32[]{:S(2)}) %collective-permute-start.3) | collective-permute-done | bytes 73760 | tf_op jit(solution)/shard_map/ppermute | solution.py:706
  15.8 4.2 %collective-permute-start.5 = (bf16[128,256]{1,0:T(8,128)(2,1)S(1)}, bf16[128,256]{1,0:T(8,128)(2,1)S(1)}, u32[]{:S(2)}, u32[]{:S(2)}) collective-permute-start(bf16[128,256]{1,0:T(8,128)(2,1)S(1)} %joined.2.refs_4_), channel_id=1, source_target_pairs={{8,24},{10,26},{12,28},{14,30},{16,0},{18,2},{20,4},{22,6},{9,25},... | collective-permute-start | bytes 196616 | tf_op jit(solution)/shard_map/ppermute | solution.py:718
  20.0 1.9 %collective-permute-start.4 = (bf16[128,256]{1,0:T(8,128)(2,1)S(1)}, bf16[128,256]{1,0:T(8,128)(2,1)S(1)}, u32[]{:S(2)}, u32[]{:S(2)}) collective-permute-start(bf16[128,256]{1,0:T(8,128)(2,1)S(1)} %joined.2.refs_4_), channel_id=1, source_target_pairs={{8,16},{10,18},{12,20},{14,22},{16,8},{18,10},{20,12},{22,14},{9,1... | collective-permute-start | bytes 196616 | tf_op jit(solution)/shard_map/ppermute | solution.py:718
  21.9 0.0 collective-permute-done.6.refs_1_.refs_6_
  21.9 0.0 collective-permute-done.7.refs_2_.refs_5_
  21.9 0.0 collective-permute-done.8.refs_3_.refs_4_
  21.9 0.2 totals.3
  22.1 0.1 collective-permute-start.9
  22.2 0.0 collective-permute-done.5.refs_2_
  22.2 3.0 %collective-permute-done.4.refs_1_ = bf16[128,256]{1,0:T(8,128)(2,1)S(1)} collective-permute-done((bf16[128,256]{1,0:T(8,128)(2,1)S(1)}, bf16[128,256]{1,0:T(8,128)(2,1)S(1)}, u32[]{:S(2)}, u32[]{:S(2)}) %collective-permute-start.4) | collective-permute-done | bytes 65568 | tf_op jit(solution)/shard_map/ppermute | solution.py:718
  25.2 0.2 member_entries.2
  25.4 2.6 %collective-permute-start.15 = (bf16[256,256]{1,0:T(8,128)(2,1)S(1)}, bf16[256,256]{1,0:T(8,128)(2,1)S(1)}, u32[]{:S(2)}, u32[]{:S(2)}) collective-permute-start(bf16[256,256]{1,0:T(8,128)(2,1)S(1)} %get-tuple-element.90), channel_id=1, source_target_pairs={{0,6},{2,4},{4,2},{6,0},{8,14},{10,12},{12,10},{14,8},{16,22},{18,... | collective-permute-start | bytes 393224 | tf_op jit(solution)/shard_map/ppermute | solution.py:406
  28.0 1.1 %collective-permute-start.16 = (bf16[256,256]{1,0:T(8,128)(2,1)S(1)}, bf16[256,256]{1,0:T(8,128)(2,1)S(1)}, u32[]{:S(2)}, u32[]{:S(2)}) collective-permute-start(bf16[256,256]{1,0:T(8,128)(2,1)S(1)} %get-tuple-element.91), channel_id=1, source_target_pairs={{0,4},{2,6},{4,0},{6,2},{8,12},{10,14},{12,8},{14,10},{16,20},{18,... | collective-permute-start | bytes 393224 | tf_op jit(solution)/shard_map/ppermute | solution.py:406
  29.2 0.0 collective-permute-start.17
  29.2 1.7 %collective-permute-start.11 = (bf16[128,256]{1,0:T(8,128)(2,1)S(1)}, bf16[128,256]{1,0:T(8,128)(2,1)S(1)}, u32[]{:S(2)}, u32[]{:S(2)}) collective-permute-start(bf16[128,256]{1,0:T(8,128)(2,1)S(1)} %joined.3), channel_id=1, source_target_pairs={{8,24},{10,26},{12,28},{14,30},{16,0},{18,2},{20,4},{22,6},{9,25},... | collective-permute-start | bytes 196616 | tf_op jit(solution)/shard_map/ppermute | solution.py:718
  30.9 2.1 %collective-permute-start.10 = (bf16[128,256]{1,0:T(8,128)(2,1)S(1)}, bf16[128,256]{1,0:T(8,128)(2,1)S(1)}, u32[]{:S(2)}, u32[]{:S(2)}) collective-permute-start(bf16[128,256]{1,0:T(8,128)(2,1)S(1)} %joined.3), channel_id=1, source_target_pairs={{8,16},{10,18},{12,20},{14,22},{16,8},{18,10},{20,12},{22,14},{9,1... | collective-permute-start | bytes 196616 | tf_op jit(solution)/shard_map/ppermute | solution.py:718
  33.0 3.5 %inner_terms.2 = (bf16[384,1024]{1,0:T(8,128)(2,1)S(1)}, f32[384,128]{1,0:T(8,128)S(1)}, f32[384,128]{1,0:T(8,128)S(1)}) custom-call(bf16[384,128]{1,0:T(8,128)(2,1)S(1)} %get-tuple-element.55.refs_0_.b, bf16[384,128]{1,0:T(8,128)(2,1)S(1)} %get-tuple-element.56.refs_1_.c, bf16[384,2048]{1,0:T(8,128)(2,1)S(1)} %get-tuple-element.57.refs_2_.x, ...), custom_call_target="tpu_custom_call" | custom-call | flops 805306368 | bytes 3145728 | tf_op jit(solution)/shard_map/inner_terms/pallas_call | solution.py:557
  36.5 0.4 member_entries.3
  36.9 1.7 %collective-permute-start.12 = (bf16[256,256]{1,0:T(8,128)(2,1)S(1)}, bf16[256,256]{1,0:T(8,128)(2,1)S(1)}, u32[]{:S(2)}, u32[]{:S(2)}) collective-permute-start(bf16[256,256]{1,0:T(8,128)(2,1)S(1)} %get-tuple-element.85), channel_id=1, source_target_pairs={{0,6},{2,4},{4,2},{6,0},{8,14},{10,12},{12,10},{14,8},{16,22},{18,... | collective-permute-start | bytes 393224 | tf_op jit(solution)/shard_map/ppermute | solution.py:406
  38.6 1.1 %collective-permute-start.13 = (bf16[256,256]{1,0:T(8,128)(2,1)S(1)}, bf16[256,256]{1,0:T(8,128)(2,1)S(1)}, u32[]{:S(2)}, u32[]{:S(2)}) collective-permute-start(bf16[256,256]{1,0:T(8,128)(2,1)S(1)} %get-tuple-element.86), channel_id=1, source_target_pairs={{0,4},{2,6},{4,0},{6,2},{8,12},{10,14},{12,8},{14,10},{16,20},{18,... | collective-permute-start | bytes 393224 | tf_op jit(solution)/shard_map/ppermute | solution.py:406
  39.7 0.0 collective-permute-done.15.refs_1_
  39.7 0.1 collective-permute-start.14
  39.8 3.5 %inner_terms.3 = (bf16[384,1024]{1,0:T(8,128)(2,1)S(1)}, f32[384,128]{1,0:T(8,128)S(1)}, f32[384,128]{1,0:T(8,128)S(1)}) custom-call(bf16[384,128]{1,0:T(8,128)(2,1)S(1)} %get-tuple-element.55.refs_0_.b, bf16[384,128]{1,0:T(8,128)(2,1)S(1)} %get-tuple-element.56.refs_1_.c, bf16[384,2048]{1,0:T(8,128)(2,1)S(1)} %get-tuple-element.57.refs_2_.x, ...), custom_call_target="tpu_custom_call" | custom-call | flops 805306368 | bytes 3145728 | tf_op jit(solution)/shard_map/inner_terms/pallas_call | solution.py:557
  43.3 0.0 collective-permute-done.17.refs_3_
  43.3 0.4 entry_values.1.refs_4_
  43.7 0.6 %entry_parts.2 = (f32[384,128]{1,0:T(8,128)S(1)}, f32[384,128]{1,0:T(8,128)S(1)}) custom-call(bf16[384,1024]{1,0:T(8,128)(2,1)S(1)} %get-tuple-element.95.x_scaled, bf16[384,1024]{1,0:T(8,128)(2,1)S(1)} %get-tuple-element.96.dy_scaled, f32[384,128]{1,0:T(8,128)S(1)} %get-tuple-element.97.db_before, f32[384,128]{1,0:T(8,128)S(1)} %get-tuple-element.98.dc_before, ...), custom_call_target="tpu_custom_call" | custom-call | flops 201326592 | bytes 1572864 | tf_op jit(solution)/shard_map/entry_parts/pallas_call | solution.py:596
  44.3 0.0 collective-permute-done.12.refs_1_
  44.3 0.0 collective-permute-done.13.refs_2_
  44.3 0.6 %entry_parts.3 = bf16[768,128]{1,0:T(8,128)(2,1)S(1)} custom-call(bf16[384,1024]{1,0:T(8,128)(2,1)S(1)} %get-tuple-element.93.x_scaled, bf16[384,1024]{1,0:T(8,128)(2,1)S(1)} %get-tuple-element.94.dy_scaled, f32[384,128]{1,0:T(8,128)S(1)} %get-tuple-element.99.db_before, f32[384,128]{1,0:T(8,128)S(1)} %get-tuple-element.100.dc_before, ...), custom_call_target="tpu_custom_call" | custom-call | flops 201326592 | bytes 1572864 | tf_op jit(solution)/shard_map/entry_parts/pallas_call | solution.py:596
  44.9 6.9 %collective-permute-start.18 = (bf16[768,128]{1,0:T(8,128)(2,1)S(1)}, bf16[768,128]{1,0:T(8,128)(2,1)S(1)}, u32[]{:S(2)}, u32[]{:S(2)}) collective-permute-start(bf16[768,128]{1,0:T(8,128)(2,1)S(1)} %entry_parts.3), channel_id=1, source_target_pairs={{0,1},{1,0},{2,3},{3,2},{4,5},{5,4},{6,7},{7,6},{8,9},{9,8},{10,11... | collective-permute-start | bytes 589832 | tf_op jit(solution)/shard_map/ppermute | solution.py:685
  51.7 1.3 %last_values.1 = bf16[384,2048]{1,0:T(8,128)(2,1)} custom-call(s32[1]{0:T(128)} %bitcast.where, bf16[384,1024]{1,0:T(8,128)(2,1)S(1)} %get-tuple-element.59.spread, bf16[384,128]{1,0:T(8,128)(2,1)S(1)} %get-tuple-element.55.refs_0_.b, bf16[384,1024]{1,0:T(8,128)(2,1)S(1)} %get-tuple-element.84.dx_local, ...), custom_call_target="tpu_custom_call" | custom-call | flops 100663296 | bytes 1572864 | tf_op jit(solution)/shard_map/last_values/pallas_call | solution.py:665
  53.0 0.0 collective-permute-done.18
  53.0 0.1 add_convert_fusion
  53.1 0.7 %fusion = (bf16[384,128]{1,0:T(8,128)(2,1)}, bf16[384,128]{1,0:T(8,128)(2,1)}) fusion(bf16[768,128]{1,0:T(8,128)(2,1)S(1)} %add_convert_fusion), kind=kLoop, calls=%fused_computation.1 | loop fusion | bytes 393216 | tf_op jit(solution)/shard_map/slice | solution.py:743
  (7 shorter events, 0.1 us)
Async XLA Ops:
  3.9 5.8 %collective-permute-start = (bf16[272,256]{1,0:T(8,128)(2,1)S(1)}, bf16[272,256]{1,0:T(8,128)(2,1)S(1)}, u32[]{:S(2)}, u32[]{:S(2)}) collective-permute-start(bf16[272,256]{1,0:T(8,128)(2,1)S(1)} %get-tuple-element.70), channel_id=1, source_target_pairs={{0,6},{2,4},{4,2},{6,0},{8,14},{10,12},{12,10},{14,8},{16,22},{18,... | collective-permute-start | bytes 417800 | tf_op jit(solution)/shard_map/ppermute | solution.py:406
  4.2 7.9 %collective-permute-start.1 = (bf16[272,256]{1,0:T(8,128)(2,1)S(1)}, bf16[272,256]{1,0:T(8,128)(2,1)S(1)}, u32[]{:S(2)}, u32[]{:S(2)}) collective-permute-start(bf16[272,256]{1,0:T(8,128)(2,1)S(1)} %get-tuple-element.71), channel_id=1, source_target_pairs={{0,4},{2,6},{4,0},{6,2},{8,12},{10,14},{12,8},{14,10},{16,20},{18,... | collective-permute-start | bytes 417800 | tf_op jit(solution)/shard_map/ppermute | solution.py:406
  5.4 6.6 %collective-permute-start.2 = (bf16[272,256]{1,0:T(8,128)(2,1)S(1)}, bf16[272,256]{1,0:T(8,128)(2,1)S(1)}, u32[]{:S(2)}, u32[]{:S(2)}) collective-permute-start(bf16[272,256]{1,0:T(8,128)(2,1)S(1)} %get-tuple-element.72), channel_id=1, source_target_pairs={{0,2},{2,0},{4,6},{6,4},{8,10},{10,8},{12,14},{14,12},{16,18},{18,... | collective-permute-start | bytes 417800 | tf_op jit(solution)/shard_map/ppermute | solution.py:406
  8.2 13.7 %collective-permute-start.6 = (bf16[272,256]{1,0:T(8,128)(2,1)S(1)}, bf16[272,256]{1,0:T(8,128)(2,1)S(1)}, u32[]{:S(2)}, u32[]{:S(2)}) collective-permute-start(bf16[272,256]{1,0:T(8,128)(2,1)S(1)} %get-tuple-element.78), channel_id=1, source_target_pairs={{0,6},{2,4},{4,2},{6,0},{8,14},{10,12},{12,10},{14,8},{16,22},{18,... | collective-permute-start | bytes 417800 | tf_op jit(solution)/shard_map/ppermute | solution.py:406
  8.5 13.4 %collective-permute-start.7 = (bf16[272,256]{1,0:T(8,128)(2,1)S(1)}, bf16[272,256]{1,0:T(8,128)(2,1)S(1)}, u32[]{:S(2)}, u32[]{:S(2)}) collective-permute-start(bf16[272,256]{1,0:T(8,128)(2,1)S(1)} %get-tuple-element.79), channel_id=1, source_target_pairs={{0,4},{2,6},{4,0},{6,2},{8,12},{10,14},{12,8},{14,10},{16,20},{18,... | collective-permute-start | bytes 417800 | tf_op jit(solution)/shard_map/ppermute | solution.py:406
  9.7 12.2 %collective-permute-start.8 = (bf16[272,256]{1,0:T(8,128)(2,1)S(1)}, bf16[272,256]{1,0:T(8,128)(2,1)S(1)}, u32[]{:S(2)}, u32[]{:S(2)}) collective-permute-start(bf16[272,256]{1,0:T(8,128)(2,1)S(1)} %get-tuple-element.80), channel_id=1, source_target_pairs={{0,2},{2,0},{4,6},{6,4},{8,10},{10,8},{12,14},{14,12},{16,18},{18,... | collective-permute-start | bytes 417800 | tf_op jit(solution)/shard_map/ppermute | solution.py:406
  12.2 3.6 %collective-permute-start.3 = (bf16[144,256]{1,0:T(8,128)(2,1)S(1)}, bf16[144,256]{1,0:T(8,128)(2,1)S(1)}, u32[]{:S(2)}, u32[]{:S(2)}) collective-permute-start(bf16[144,256]{1,0:T(8,128)(2,1)S(1)} %get-tuple-element.73), channel_id=1, source_target_pairs={{0,8},{2,10},{4,12},{6,14},{8,0},{10,2},{12,4},{14,6},{16,24},{18,... | collective-permute-start | bytes 221192 | tf_op jit(solution)/shard_map/ppermute | solution.py:706
  15.8 6.4 %collective-permute-start.5 = (bf16[128,256]{1,0:T(8,128)(2,1)S(1)}, bf16[128,256]{1,0:T(8,128)(2,1)S(1)}, u32[]{:S(2)}, u32[]{:S(2)}) collective-permute-start(bf16[128,256]{1,0:T(8,128)(2,1)S(1)} %joined.2.refs_4_), channel_id=1, source_target_pairs={{8,24},{10,26},{12,28},{14,30},{16,0},{18,2},{20,4},{22,6},{9,25},... | collective-permute-start | bytes 196616 | tf_op jit(solution)/shard_map/ppermute | solution.py:718
  20.0 5.2 %collective-permute-start.4 = (bf16[128,256]{1,0:T(8,128)(2,1)S(1)}, bf16[128,256]{1,0:T(8,128)(2,1)S(1)}, u32[]{:S(2)}, u32[]{:S(2)}) collective-permute-start(bf16[128,256]{1,0:T(8,128)(2,1)S(1)} %joined.2.refs_4_), channel_id=1, source_target_pairs={{8,16},{10,18},{12,20},{14,22},{16,8},{18,10},{20,12},{22,14},{9,1... | collective-permute-start | bytes 196616 | tf_op jit(solution)/shard_map/ppermute | solution.py:718
  22.1 7.1 %collective-permute-start.9 = (bf16[144,256]{1,0:T(8,128)(2,1)S(1)}, bf16[144,256]{1,0:T(8,128)(2,1)S(1)}, u32[]{:S(2)}, u32[]{:S(2)}) collective-permute-start(bf16[144,256]{1,0:T(8,128)(2,1)S(1)} %get-tuple-element.81), channel_id=1, source_target_pairs={{0,8},{2,10},{4,12},{6,14},{8,0},{10,2},{12,4},{14,6},{16,24},{18,... | collective-permute-start | bytes 221192 | tf_op jit(solution)/shard_map/ppermute | solution.py:706
  25.4 14.3 %collective-permute-start.15 = (bf16[256,256]{1,0:T(8,128)(2,1)S(1)}, bf16[256,256]{1,0:T(8,128)(2,1)S(1)}, u32[]{:S(2)}, u32[]{:S(2)}) collective-permute-start(bf16[256,256]{1,0:T(8,128)(2,1)S(1)} %get-tuple-element.90), channel_id=1, source_target_pairs={{0,6},{2,4},{4,2},{6,0},{8,14},{10,12},{12,10},{14,8},{16,22},{18,... | collective-permute-start | bytes 393224 | tf_op jit(solution)/shard_map/ppermute | solution.py:406
  28.0 15.2 %collective-permute-start.16 = (bf16[256,256]{1,0:T(8,128)(2,1)S(1)}, bf16[256,256]{1,0:T(8,128)(2,1)S(1)}, u32[]{:S(2)}, u32[]{:S(2)}) collective-permute-start(bf16[256,256]{1,0:T(8,128)(2,1)S(1)} %get-tuple-element.91), channel_id=1, source_target_pairs={{0,4},{2,6},{4,0},{6,2},{8,12},{10,14},{12,8},{14,10},{16,20},{18,... | collective-permute-start | bytes 393224 | tf_op jit(solution)/shard_map/ppermute | solution.py:406
  29.2 14.1 %collective-permute-start.17 = (bf16[256,256]{1,0:T(8,128)(2,1)S(1)}, bf16[256,256]{1,0:T(8,128)(2,1)S(1)}, u32[]{:S(2)}, u32[]{:S(2)}) collective-permute-start(bf16[256,256]{1,0:T(8,128)(2,1)S(1)} %get-tuple-element.92), channel_id=1, source_target_pairs={{0,2},{2,0},{4,6},{6,4},{8,10},{10,8},{12,14},{14,12},{16,18},{18,... | collective-permute-start | bytes 393224 | tf_op jit(solution)/shard_map/ppermute | solution.py:406
  29.2 7.3 %collective-permute-start.11 = (bf16[128,256]{1,0:T(8,128)(2,1)S(1)}, bf16[128,256]{1,0:T(8,128)(2,1)S(1)}, u32[]{:S(2)}, u32[]{:S(2)}) collective-permute-start(bf16[128,256]{1,0:T(8,128)(2,1)S(1)} %joined.3), channel_id=1, source_target_pairs={{8,24},{10,26},{12,28},{14,30},{16,0},{18,2},{20,4},{22,6},{9,25},... | collective-permute-start | bytes 196616 | tf_op jit(solution)/shard_map/ppermute | solution.py:718
  30.9 5.6 %collective-permute-start.10 = (bf16[128,256]{1,0:T(8,128)(2,1)S(1)}, bf16[128,256]{1,0:T(8,128)(2,1)S(1)}, u32[]{:S(2)}, u32[]{:S(2)}) collective-permute-start(bf16[128,256]{1,0:T(8,128)(2,1)S(1)} %joined.3), channel_id=1, source_target_pairs={{8,16},{10,18},{12,20},{14,22},{16,8},{18,10},{20,12},{22,14},{9,1... | collective-permute-start | bytes 196616 | tf_op jit(solution)/shard_map/ppermute | solution.py:718
  36.9 7.3 %collective-permute-start.12 = (bf16[256,256]{1,0:T(8,128)(2,1)S(1)}, bf16[256,256]{1,0:T(8,128)(2,1)S(1)}, u32[]{:S(2)}, u32[]{:S(2)}) collective-permute-start(bf16[256,256]{1,0:T(8,128)(2,1)S(1)} %get-tuple-element.85), channel_id=1, source_target_pairs={{0,6},{2,4},{4,2},{6,0},{8,14},{10,12},{12,10},{14,8},{16,22},{18,... | collective-permute-start | bytes 393224 | tf_op jit(solution)/shard_map/ppermute | solution.py:406
  38.6 5.7 %collective-permute-start.13 = (bf16[256,256]{1,0:T(8,128)(2,1)S(1)}, bf16[256,256]{1,0:T(8,128)(2,1)S(1)}, u32[]{:S(2)}, u32[]{:S(2)}) collective-permute-start(bf16[256,256]{1,0:T(8,128)(2,1)S(1)} %get-tuple-element.86), channel_id=1, source_target_pairs={{0,4},{2,6},{4,0},{6,2},{8,12},{10,14},{12,8},{14,10},{16,20},{18,... | collective-permute-start | bytes 393224 | tf_op jit(solution)/shard_map/ppermute | solution.py:406
  39.7 4.6 %collective-permute-start.14 = (bf16[256,256]{1,0:T(8,128)(2,1)S(1)}, bf16[256,256]{1,0:T(8,128)(2,1)S(1)}, u32[]{:S(2)}, u32[]{:S(2)}) collective-permute-start(bf16[256,256]{1,0:T(8,128)(2,1)S(1)} %get-tuple-element.87), channel_id=1, source_target_pairs={{0,2},{2,0},{4,6},{6,4},{8,10},{10,8},{12,14},{14,12},{16,18},{18,... | collective-permute-start | bytes 393224 | tf_op jit(solution)/shard_map/ppermute | solution.py:406
  44.9 8.1 %collective-permute-start.18 = (bf16[768,128]{1,0:T(8,128)(2,1)S(1)}, bf16[768,128]{1,0:T(8,128)(2,1)S(1)}, u32[]{:S(2)}, u32[]{:S(2)}) collective-permute-start(bf16[768,128]{1,0:T(8,128)(2,1)S(1)} %entry_parts.3), channel_id=1, source_target_pairs={{0,1},{1,0},{2,3},{3,2},{4,5},{5,4},{6,7},{7,6},{8,9},{9,8},{10,11... | collective-permute-start | bytes 589832 | tf_op jit(solution)/shard_map/ppermute | solution.py:685

commit v12 on v8

--- a/solution.py
+++ b/solution.py
@@ -118,33 +118,30 @@
     return into_end, from_start, halves
 
 
-def put_states(head_dim, chunk, where, operands, outs, ready):
+def put_states(head_dim, pieces, where, operands, outs, ready):
     into_end, from_start, halves, b, c, x, dy = operands
-    x_scaled, dy_scaled, spread, *sends = outs
-    group, state = len(sends), b.shape[1]
-    width = x.shape[1]
+    state, width = b.shape[1], x.shape[1]
     chunks = chunk_count(width)
-    part = width // (group * chunks)
+    part = width // (GROUP * chunks)
     difference = row_less_head(head_dim, part)
-    sides = [(into_end, b, x, x_scaled, 0), (from_start, c, dy, dy_scaled, state)]
-    for side, (factors, proj, cols, scaled, first) in enumerate(sides):
+    for side, (factors, proj, cols) in enumerate([(into_end, b, x), (from_start, c, dy)]):
         ready(side)
         turned = proj[...].T
-        for k in range(group):
-            here = slice(k * part, (k + 1) * part)
+        for n, (chunk, k) in enumerate(pieces):
+            x_scaled, dy_scaled, spread, send = outs[4 * n : 4 * n + 4]
             lanes = chunk_lanes(where, k, chunk, part, width)
             first_head = ((place_of(where) ^ k) * chunks + chunk) * (part // head_dim)
             hot = head_of_lane(difference, first_head)
             wide = dot(factors, hot, NN).astype(BF16)
             if side == 0:
-                spread[:, here] = wide
-                sends[k][2 * state :, :] = dot(halves, hot, NN).astype(BF16)
+                spread[...] = wide
+                send[2 * state :, :] = dot(halves, hot, NN).astype(BF16)
             piece = cols[:, lanes] * wide
-            scaled[:, here] = piece
-            sends[k][first : first + state, :] = dot(turned, piece, NN).astype(BF16)
-
-
-def first_states_kernel(head_dim, group, where, ld_in, b_in, c_in, x_in, dy_in, *refs):
+            (dy_scaled if side else x_scaled)[...] = piece
+            send[side * state : (side + 1) * state, :] = dot(turned, piece, NN).astype(BF16)
+
+
+def first_states_kernel(head_dim, pieces, where, ld_in, b_in, c_in, x_in, dy_in, *refs):
     ld, b, c, x, dy, into_end, from_start, halves = refs[:8]
     outs, sems = refs[8:-1], refs[-1]
     pairs = [(ld_in, ld), (b_in, b), (x_in, x), (c_in, c), (dy_in, dy)]
@@ -161,28 +158,34 @@
         copies[1 + 2 * side].wait()
         copies[2 + 2 * side].wait()
 
-    put_states(head_dim, 0, where, (*factors, b, c, x, dy), outs, ready)
-
-
-def next_states_kernel(head_dim, chunk, where, into_end, from_start, halves, *refs):
+    put_states(head_dim, pieces, where, (*factors, b, c, x, dy), outs, ready)
+
+
+def next_states_kernel(head_dim, pieces, where, into_end, from_start, halves, *refs):
     operands = (into_end[...], from_start[...], halves[...], *refs[:4])
-    put_states(head_dim, chunk, where, operands, refs[4:], lambda side: None)
-
-
-def states_shapes(group, length, width, state):
-    part = width // (group * chunk_count(width))
-    scaled = pltpu.VMEM((length, group * part), BF16)
-    return [scaled] * 3 + [pltpu.VMEM((2 * state + TAIL, part), BF16)] * group
-
-
-def first_states(head_dim, group, where, inputs):
+    outs = refs[-4 * len(pieces) :]
+    put_states(head_dim, pieces, where, operands, outs, lambda side: None)
+
+
+def states_shapes(n_parts, length, width, state):
+    part = width // (GROUP * chunk_count(width))
+    scaled = jax.ShapeDtypeStruct((length, part), BF16)
+    send = jax.ShapeDtypeStruct((2 * state + TAIL, part), BF16)
+    return [scaled, scaled, scaled, send] * n_parts
+
+
+def by_piece(pieces, outs):
+    return {piece: outs[4 * n : 4 * n + 4] for n, piece in enumerate(pieces)}
+
+
+def first_states(head_dim, pieces, where, inputs):
     ld, b, c, x, dy = inputs
     (length, width), state = x.shape, b.shape[1]
-    kept = [pltpu.VMEM(a.shape, a.dtype) for a in inputs]
-    kept += [pltpu.VMEM((rows, LANES), BF16) for rows in (length, length, TAIL)]
-    outs = kept + states_shapes(group, length, width, state)
-    return pl.pallas_call(
-        functools.partial(first_states_kernel, head_dim, group),
+    kept = [jax.ShapeDtypeStruct(a.shape, a.dtype) for a in inputs]
+    kept += [jax.ShapeDtypeStruct((rows, LANES), BF16) for rows in (length, length, TAIL)]
+    outs = kept + states_shapes(len(pieces), length, width, state)
+    found = pl.pallas_call(
+        functools.partial(first_states_kernel, head_dim, pieces),
         out_shape=outs,
         in_specs=[SMEM] + [HBM] * 5,
         out_specs=whole(len(outs)),
@@ -191,13 +194,14 @@
         cost_estimate=cost(2 * length * width * (state + LANES), 8 * length * width),
         name="first_states",
     )(where, *in_hbm(*inputs))
-
-
-def next_states(head_dim, group, chunk, where, factors, b, c, x, dy):
+    return found[:8], by_piece(pieces, found[8:])
+
+
+def next_states(head_dim, pieces, where, factors, b, c, x, dy):
     (length, width), state = x.shape, b.shape[1]
-    outs = states_shapes(group, length, width, state)
-    return pl.pallas_call(
-        functools.partial(next_states_kernel, head_dim, chunk),
+    outs = states_shapes(len(pieces), length, width, state)
+    found = pl.pallas_call(
+        functools.partial(next_states_kernel, head_dim, pieces),
         out_shape=outs,
         in_specs=[SMEM] + whole(7),
         out_specs=whole(len(outs)),
@@ -205,6 +209,7 @@
         cost_estimate=cost(2 * length * width * (state + LANES), 4 * length * width),
         name="next_states",
     )(where, *factors, b, c, x, dy)
+    return by_piece(pieces, found)
 
 
 def decay_of(tail):
@@ -552,15 +557,14 @@
     )(b, c, x, dy, *setup, *before, *after)
 
 
-def parts_kernel(last, x_scaled, dy_scaled, db_before, dc_before, *refs):
+def parts_kernel(last, db_before, dc_before, *refs):
+    scaled, refs = refs[: 2 * GROUP], refs[2 * GROUP :]
     entries, outs = sent_order(refs[:GROUP]), refs[-1 if last else -2 :]
     length, state = db_before.shape
-    part = entries[0].shape[1]
     db, dc = db_before[...], dc_before[...]
     for k, entry in enumerate(entries):
-        here = slice(k * part, (k + 1) * part)
-        db = db + dot(x_scaled[:, here], entry[state:, :], NT)
-        dc = dc + dot(dy_scaled[:, here], entry[:state, :], NT)
+        db = db + dot(scaled[2 * k][...], entry[state:, :], NT)
+        dc = dc + dot(scaled[2 * k + 1][...], entry[:state, :], NT)
     if last:
         outs[0][:length, :] = db.astype(BF16)
         outs[0][length:, :] = dc.astype(BF16)
@@ -569,62 +573,93 @@
         outs[1][...] = dc
 
 
-def entry_parts(last, x_scaled, dy_scaled, db_before, dc_before, entries, after):
+def entry_parts(last, scaled, db_before, dc_before, entries, after):
     length, state = db_before.shape
-    one = pltpu.VMEM((length, state), F32)
-    outs = [pltpu.VMEM((2 * length, state), BF16)] if last else [one, one]
+    one = jax.ShapeDtypeStruct((length, state), F32)
+    outs = [jax.ShapeDtypeStruct((2 * length, state), BF16)] if last else [one, one]
     return pl.pallas_call(
         functools.partial(parts_kernel, last),
         out_shape=outs,
-        in_specs=whole(4 + len(entries)) + [ANY] * len(after),
+        in_specs=whole(2 + 3 * GROUP) + [ANY] * len(after),
         out_specs=whole(len(outs)),
         compiler_params=params(8),
-        cost_estimate=cost(4 * x_scaled.size * state, 4 * x_scaled.size),
+        cost_estimate=cost(8 * scaled[0].size * state, 8 * scaled[0].size),
         name="entry_parts",
-    )(x_scaled, dy_scaled, db_before, dc_before, *sent_order(entries), *after)
-
-
-def values_kernel(chunk, last, where, spread, b, dx_local, *refs):
-    entries, (dx, sems) = sent_order(refs[:GROUP], 2 if last else 1), refs[-2:]
-    out = refs[-3 if last else -4]
-    if not last:
-        refs[-3][...] = jnp.zeros_like(refs[-3])
+    )(db_before, dc_before, *scaled, *sent_order(entries), *after)
+
+
+def put_values(where, spread, b, dx_local, entries, put):
     state, part = b.shape[1], entries[0].shape[1]
-    stores = []
     for k, entry in enumerate(entries):
         here = slice(k * part, (k + 1) * part)
         local = dx_local[:, pl.ds(pl.multiple_of((place_of(where) ^ k) * part, part), part)]
-        far = spread[:, here].astype(F32) * dot(b[...], entry[state:, :], NN)
-        dx[k] = (local.astype(F32) + far).astype(BF16)
+        far = spread[k][...].astype(F32) * dot(b[...], entry[state:, :], NN)
+        put(k, here, (local.astype(F32) + far).astype(BF16))
+
+
+def values_kernel(where, b, dx_local, *refs):
+    spread, entries, out = refs[:GROUP], sent_order(refs[GROUP : 2 * GROUP]), refs[-1]
+
+    def put(k, here, value):
+        out[:, here] = value
+
+    put_values(where, spread, b, dx_local, entries, put)
+
+
+def last_values_kernel(chunks, where, b, dx_local, *refs):
+    spread, refs = refs[:GROUP], refs[GROUP:]
+    entries, before = sent_order(refs[:GROUP], 2), refs[GROUP : GROUP + chunks - 1]
+    out, dx, sems = refs[-3:]
+    part = entries[0].shape[1]
+    stores = []
+
+    def store(chunk, k, source):
         lanes = chunk_lanes(where, k, chunk, part, out.shape[1])
-        store = pltpu.make_async_copy(dx.at[k], out.at[:, lanes], sems.at[k])
-        store.start()
-        stores.append(store)
-    for store in stores:
-        store.wait()
-
-
-def entry_values(chunk, chunks, where, spread, b, dx_local, entries, before, after):
-    group, part = len(entries), entries[0].shape[1]
-    length, state = b.shape
-    size, last = dx_local.size, chunk == chunks - 1
-    sent = sent_order(entries, 2 if last else 1)
-    operands = [where, spread, b, dx_local, *sent, *after, *before]
+        at = sems.at[chunk * GROUP + k]
+        stores.append(pltpu.make_async_copy(source, out.at[:, lanes], at))
+        stores[-1].start()
+
+    for chunk, values in enumerate(before):
+        for k in range(GROUP):
+            store(chunk, k, values.at[:, pl.ds(k * part, part)])
+
+    def put(k, here, value):
+        dx[k] = value
+        store(chunks - 1, k, dx.at[k])
+
+    put_values(where, spread, b, dx_local, entries, put)
+    for one in stores:
+        one.wait()
+
+
+def entry_values(chunk, chunks, where, spread, b, dx_local, entries, before):
+    length, part = b.shape[0], entries[0].shape[1]
+    last = chunk == chunks - 1
+    estimate = cost(2 * dx_local.size * b.shape[1], 4 * dx_local.size)
+    operands = [where, b, dx_local, *spread, *sent_order(entries, 2 if last else 1)]
+    if not last:
+        return pl.pallas_call(
+            values_kernel,
+            out_shape=jax.ShapeDtypeStruct((length, GROUP * part), BF16),
+            in_specs=[SMEM] + whole(2 + 2 * GROUP),
+            out_specs=whole(1)[0],
+            compiler_params=params(8),
+            cost_estimate=estimate,
+            name="entry_values",
+        )(*operands)
     return pl.pallas_call(
-        functools.partial(values_kernel, chunk, last),
-        out_shape=[pltpu.HBM((length, chunks * group * part), BF16)]
-        + [pltpu.VMEM((8, LANES), F32)] * (not last),
-        in_specs=[SMEM] + whole(3 + group) + [ANY] * len(after) + [HBM] * len(before),
-        out_specs=[HBM] + whole(0 if last else 1),
-        input_output_aliases={len(operands) - 1: 0} if before else {},
+        functools.partial(last_values_kernel, chunks),
+        out_shape=pltpu.HBM((length, chunks * GROUP * part), BF16),
+        in_specs=[SMEM] + whole(2 + 2 * GROUP + len(before)),
+        out_specs=HBM,
         scratch_shapes=[
-            pltpu.VMEM((group, length, part), BF16),
-            pltpu.SemaphoreType.DMA((group,)),
+            pltpu.VMEM((GROUP, length, part), BF16),
+            pltpu.SemaphoreType.DMA((chunks * GROUP,)),
         ],
         compiler_params=params(8),
-        cost_estimate=cost(2 * size * state, 4 * size),
-        name="entry_values",
-    )(*operands)
+        cost_estimate=estimate,
+        name="last_values",
+    )(*operands, *before)
 
 
 def over_heads(part):
@@ -644,13 +679,15 @@
     levels = (count // group).bit_length() - 1
     where = lax.axis_index("seq").astype(jnp.int32)[None]
     inputs = (log_decay, b_inputs, c_inputs, token_values, grad_out)
-    ld, b, c, x, dy, *rest = first_states(head_dim, group, where, inputs)
-    factors, states = rest[:3], [rest[3:]]
-    blocks = [exchange(states[0][3:])]
-    for chunk in range(1, chunks):
-        states.append(next_states(head_dim, group, chunk, where, factors, b, c, x, dy))
-        blocks.append(exchange(states[chunk][3:]))
-    setup = inner_setup(head_dim, ld, b, c, [states[-1][3]])
+    order = [(chunk, k) for chunk in range(chunks) for k in range(group - 1, -1, -1)]
+    kept, states = first_states(head_dim, order[: group - 1], where, inputs)
+    ld, b, c, x, dy, *factors = kept
+    late = order[group:] + order[group - 1 : group]
+    states.update(next_states(head_dim, late, where, factors, b, c, x, dy))
+    blocks = [
+        exchange([states[chunk, k][3] for k in range(group)]) for chunk in range(chunks)
+    ]
+    setup = inner_setup(head_dim, ld, b, c, [states[late[-1]][0]])
 
     def to_group(block, k):
         return lax.ppermute(block, "seq", [(s, s ^ (k * group)) for s in range(count)])
@@ -668,17 +705,19 @@
         found = member_entries(state, False, where, blocks[chunk], received, sums[:1])
         entries.append(exchange(found))
 
-    grad_values, done = [], []
+    values = []
     for chunk in range(chunks):
-        x_scaled, dy_scaled, spread = states[chunk][:3]
         last = chunk == chunks - 1
-        sums = entry_parts(last, x_scaled, dy_scaled, *sums, entries[chunk], done)
-        outs = entry_values(
-            chunk, chunks, where, spread, b, inner[chunk][0], entries[chunk], grad_values, []
+        ours = [states[chunk, k] for k in range(group)]
+        scaled = [one for k in range(group) for one in ours[k][:2]]
+        spread = [one[2] for one in ours]
+        sums = entry_parts(last, scaled, *sums, entries[chunk], values)
+        local = inner[chunk][0]
+        values.append(
+            entry_values(chunk, chunks, where, spread, b, local, entries[chunk], values)
         )
-        grad_values, done = list(outs[:1]), list(outs[1:])
     both = over_heads(sums[0])
-    return grad_values[0], both[:length], both[length:]
+    return values[-1], both[:length], both[length:]
 
 
 def solution(mesh):

time: 49.2 us -> 48.7 us (0.990)
  Pallas kernels: 16.6 us -> 15.8 us
  waiting for transfers between devices: 7.03 us -> 7.69 us
    pallas_call x4, Pallas kernels: 7.28 us -> 6.52 us  [the longest x1 2.91 us: first_states(): pl.pallas_call(functools.partial(first_states_kernel, head_dim, pieces),...]
    ppermute x12, waiting for transfers between devices: 6.82 us -> 7.51 us  [exchange(): out[k] = lax.ppermute(parts[k], 'seq', [(s, s ^ k) for s in range(count)])]
  transfers between devices with their start and end apart: 17 -> 17, of which waited for: 8 -> 9; matrix products, arithmetic and copies ran while one was open for 0% -> 0% of each run, Pallas kernels for 26% -> 25%
where the time goes in v12:
time: 48.7 us; the launch traced here: 48.6 us
  starting transfers between devices  23.5 us (48%)
  Pallas kernels  15.8 us (32%)
  waiting for transfers between devices  7.69 us (16%)
  between operations  0.78 us (2%)
  local copies, waits for them, and re-layouts  0.69 us (1%)
    ppermute x12, starting transfers between devices, exchange(): out[k] = lax.ppermute(parts[k], 'seq', [(s, s ^ k) for s in range(count)])  15.6 us
    ppermute x4, starting transfers between devices, to_group(): lax.ppermute(block, 'seq', [(s, s ^ k * group) for s in range(count)])  7.91 us
    ppermute x12, waiting for transfers between devices, exchange(): out[k] = lax.ppermute(parts[k], 'seq', [(s, s ^ k) for s in range(count)])  7.51 us
    pallas_call x2, Pallas kernels, inner_terms(): pl.pallas_call(functools.partial(inner_kernel, head_dim, chunk, len(befor...  7 us
    pallas_call x1, Pallas kernels, first_states(): pl.pallas_call(functools.partial(first_states_kernel, head_dim, pieces),...  2.91 us
    pallas_call x1, Pallas kernels, next_states(): pl.pallas_call(functools.partial(next_states_kernel, head_dim, pieces), o...  1.94 us
    pallas_call x1, Pallas kernels, entry_values(): pl.pallas_call(functools.partial(last_values_kernel, chunks), out_shape=p...  1.26 us
    pallas_call x2, Pallas kernels, entry_parts(): pl.pallas_call(functools.partial(parts_kernel, last), out_shape=outs, in_...  1.14 us
  transfers between devices with their start and end apart: 17, of which 9 were waited for; matrix products, arithmetic and copies ran while one was open for 0% of the time, Pallas kernels for 25%

profile of v12, /device:TPU:0, one launch (start us, length us, event | category | flops | bytes accessed | tf_op | source)
XLA Modules:
  0.0 48.6 jit_solution(6824259530701588263)
XLA Ops:
  0.6 2.9 %first_states.1 = (f32[32,384]{1,0:T(8,128)S(1)}, bf16[384,128]{1,0:T(8,128)(2,1)S(1)}, bf16[384,128]{1,0:T(8,128)(2,1)S(1)}, bf16[384,2048]{1,0:T(8,128)(2,1)S(...) custom-call(s32[1]{0:T(128)} %bitcast.where, ...), custom_call_target="tpu_custom_call" | custom-call | flops 402653184 | bytes 6291456 | tf_op jit(solution)/shard_map/first_states/pallas_call | solution.py:187
  3.5 4.0 %collective-permute-start = (bf16[272,256]{1,0:T(8,128)(2,1)S(1)}, bf16[272,256]{1,0:T(8,128)(2,1)S(1)}, u32[]{:S(2)}, u32[]{:S(2)}) collective-permute-start(bf16[272,256]{1,0:T(8,128)(2,1)S(1)} %get-tuple-element.83), channel_id=1, source_target_pairs={{0,6},{2,4},{4,2},{6,0},{8,14},{10,12},{12,10},{14,8},{16,22},{18,... | collective-permute-start | bytes 417800 | tf_op jit(solution)/shard_map/ppermute | solution.py:391
  7.5 0.5 %collective-permute-start.1 = (bf16[272,256]{1,0:T(8,128)(2,1)S(1)}, bf16[272,256]{1,0:T(8,128)(2,1)S(1)}, u32[]{:S(2)}, u32[]{:S(2)}) collective-permute-start(bf16[272,256]{1,0:T(8,128)(2,1)S(1)} %get-tuple-element.84), channel_id=1, source_target_pairs={{0,4},{2,6},{4,0},{6,2},{8,12},{10,14},{12,8},{14,10},{16,20},{18,... | collective-permute-start | bytes 417800 | tf_op jit(solution)/shard_map/ppermute | solution.py:391
  8.0 0.1 collective-permute-start.2
  8.2 1.9 %next_states.1 = (bf16[384,256]{1,0:T(8,128)(2,1)S(1)}, bf16[384,256]{1,0:T(8,128)(2,1)S(1)}, bf16[384,256]{1,0:T(8,128)(2,1)S(1)}, bf16[272,256]{1,0:T(8,128)(2...) custom-call(s32[1]{0:T(128)} %bitcast.where, ...), custom_call_target="tpu_custom_call" | custom-call | flops 402653184 | bytes 3145728 | tf_op jit(solution)/shard_map/next_states/pallas_call | solution.py:203
  10.1 2.9 %collective-permute-start.4 = (bf16[272,256]{1,0:T(8,128)(2,1)S(1)}, bf16[272,256]{1,0:T(8,128)(2,1)S(1)}, u32[]{:S(2)}, u32[]{:S(2)}) collective-permute-start(bf16[272,256]{1,0:T(8,128)(2,1)S(1)} %get-tuple-element.89), channel_id=1, source_target_pairs={{0,6},{2,4},{4,2},{6,0},{8,14},{10,12},{12,10},{14,8},{16,22},{18,... | collective-permute-start | bytes 417800 | tf_op jit(solution)/shard_map/ppermute | solution.py:391
  13.0 0.5 %collective-permute-start.5 = (bf16[272,256]{1,0:T(8,128)(2,1)S(1)}, bf16[272,256]{1,0:T(8,128)(2,1)S(1)}, u32[]{:S(2)}, u32[]{:S(2)}) collective-permute-start(bf16[272,256]{1,0:T(8,128)(2,1)S(1)} %get-tuple-element.90), channel_id=1, source_target_pairs={{0,4},{2,6},{4,0},{6,2},{8,12},{10,14},{12,8},{14,10},{16,20},{18,... | collective-permute-start | bytes 417800 | tf_op jit(solution)/shard_map/ppermute | solution.py:391
  13.5 0.0 collective-permute-done.refs_1_.refs_5_
  13.5 0.5 %collective-permute-start.6 = (bf16[272,256]{1,0:T(8,128)(2,1)S(1)}, bf16[272,256]{1,0:T(8,128)(2,1)S(1)}, u32[]{:S(2)}, u32[]{:S(2)}) collective-permute-start(bf16[272,256]{1,0:T(8,128)(2,1)S(1)} %get-tuple-element.91), channel_id=1, source_target_pairs={{0,2},{2,0},{4,6},{6,4},{8,10},{10,8},{12,14},{14,12},{16,18},{18,... | collective-permute-start | bytes 417800 | tf_op jit(solution)/shard_map/ppermute | solution.py:391
  14.0 0.5 inner_setup.1
  14.5 1.0 %collective-permute-done.1.refs_2_.refs_4_ = bf16[272,256]{1,0:T(8,128)(2,1)S(1)} collective-permute-done((bf16[272,256]{1,0:T(8,128)(2,1)S(1)}, bf16[272,256]{1,0:T(8,128)(2,1)S(1)}, u32[]{:S(2)}, u32[]{:S(2)}) %collective-permute-start.1) | collective-permute-done | bytes 139296 | tf_op jit(solution)/shard_map/ppermute | solution.py:391
  15.5 0.1 collective-permute-done.2.refs_3_
  15.6 0.1 totals.2.own
  15.7 1.8 %collective-permute-start.3 = (bf16[272,256]{1,0:T(8,128)(2,1)S(1)}, bf16[272,256]{1,0:T(8,128)(2,1)S(1)}, u32[]{:S(2)}, u32[]{:S(2)}) collective-permute-start(bf16[272,256]{1,0:T(8,128)(2,1)S(1)} %totals.2.own), channel_id=1, source_target_pairs={{0,8},{2,10},{4,12},{6,14},{8,0},{10,2},{12,4},{14,6},{16,24},{18,... | collective-permute-start | bytes 417800 | tf_op jit(solution)/shard_map/ppermute | solution.py:693
  17.5 0.9 %collective-permute-done.4.refs_1_.refs_5_ = bf16[272,256]{1,0:T(8,128)(2,1)S(1)} collective-permute-done((bf16[272,256]{1,0:T(8,128)(2,1)S(1)}, bf16[272,256]{1,0:T(8,128)(2,1)S(1)}, u32[]{:S(2)}, u32[]{:S(2)}) %collective-permute-start.4) | collective-permute-done | bytes 139296 | tf_op jit(solution)/shard_map/ppermute | solution.py:391
  18.4 1.7 %collective-permute-done.5.refs_2_.refs_4_ = bf16[272,256]{1,0:T(8,128)(2,1)S(1)} collective-permute-done((bf16[272,256]{1,0:T(8,128)(2,1)S(1)}, bf16[272,256]{1,0:T(8,128)(2,1)S(1)}, u32[]{:S(2)}, u32[]{:S(2)}) %collective-permute-start.5) | collective-permute-done | bytes 139296 | tf_op jit(solution)/shard_map/ppermute | solution.py:391
  20.1 0.3 collective-permute-done.6.refs_3_
  20.4 0.1 totals.3.own
  20.5 1.6 %collective-permute-start.7 = (bf16[272,256]{1,0:T(8,128)(2,1)S(1)}, bf16[272,256]{1,0:T(8,128)(2,1)S(1)}, u32[]{:S(2)}, u32[]{:S(2)}) collective-permute-start(bf16[272,256]{1,0:T(8,128)(2,1)S(1)} %totals.3.own), channel_id=1, source_target_pairs={{0,8},{2,10},{4,12},{6,14},{8,0},{10,2},{12,4},{14,6},{16,24},{18,... | collective-permute-start | bytes 417800 | tf_op jit(solution)/shard_map/ppermute | solution.py:693
  22.2 0.0 collective-permute-done.3.received.refs_0_
  22.2 2.6 %collective-permute-start.12 = (bf16[144,256]{1,0:T(8,128)(2,1)S(1)}, bf16[144,256]{1,0:T(8,128)(2,1)S(1)}, u32[]{:S(2)}, u32[]{:S(2)}) collective-permute-start(bf16[144,256]{1,0:T(8,128)(2,1)S(1)} %merged.2.refs_7_), channel_id=1, source_target_pairs={{0,16},{2,18},{4,20},{6,22},{8,24},{10,26},{12,28},{14,30},{16,0},... | collective-permute-start | bytes 221192 | tf_op jit(solution)/shard_map/ppermute | solution.py:693
  24.9 3.5 %inner_terms.2 = (bf16[384,1024]{1,0:T(8,128)(2,1)S(1)}, f32[384,128]{1,0:T(8,128)S(1)}, f32[384,128]{1,0:T(8,128)S(1)}) custom-call(bf16[384,128]{1,0:T(8,128)(2,1)S(1)} %get-tuple-element.66.refs_0_.b, bf16[384,128]{1,0:T(8,128)(2,1)S(1)} %get-tuple-element.67.refs_1_.c, bf16[384,2048]{1,0:T(8,128)(2,1)S(1)} %get-tuple-element.68.refs_2_.x, ...), custom_call_target="tpu_custom_call" | custom-call | flops 805306368 | bytes 3145728 | tf_op jit(solution)/shard_map/inner_terms/pallas_call | solution.py:542
  28.4 0.0 collective-permute-done.12.refs_1_
  28.4 0.2 member_entries.3
  28.6 2.0 %collective-permute-start.13 = (bf16[256,256]{1,0:T(8,128)(2,1)S(1)}, bf16[256,256]{1,0:T(8,128)(2,1)S(1)}, u32[]{:S(2)}, u32[]{:S(2)}) collective-permute-start(bf16[256,256]{1,0:T(8,128)(2,1)S(1)} %get-tuple-element.108), channel_id=1, source_target_pairs={{0,6},{2,4},{4,2},{6,0},{8,14},{10,12},{12,10},{14,8},{16,22},{18,... | collective-permute-start | bytes 393224 | tf_op jit(solution)/shard_map/ppermute | solution.py:391
  30.6 0.0 collective-permute-done.7.received.refs_0_
  30.6 1.9 %collective-permute-start.8 = (bf16[144,256]{1,0:T(8,128)(2,1)S(1)}, bf16[144,256]{1,0:T(8,128)(2,1)S(1)}, u32[]{:S(2)}, u32[]{:S(2)}) collective-permute-start(bf16[144,256]{1,0:T(8,128)(2,1)S(1)} %merged.3.refs_9_), channel_id=1, source_target_pairs={{0,16},{2,18},{4,20},{6,22},{8,24},{10,26},{12,28},{14,30},{16,0},... | collective-permute-start | bytes 221192 | tf_op jit(solution)/shard_map/ppermute | solution.py:693
  32.5 1.0 %collective-permute-start.14 = (bf16[256,256]{1,0:T(8,128)(2,1)S(1)}, bf16[256,256]{1,0:T(8,128)(2,1)S(1)}, u32[]{:S(2)}, u32[]{:S(2)}) collective-permute-start(bf16[256,256]{1,0:T(8,128)(2,1)S(1)} %get-tuple-element.109), channel_id=1, source_target_pairs={{0,4},{2,6},{4,0},{6,2},{8,12},{10,14},{12,8},{14,10},{16,20},{18,... | collective-permute-start | bytes 393224 | tf_op jit(solution)/shard_map/ppermute | solution.py:391
  33.5 0.5 collective-permute-start.15
  34.0 3.5 %inner_terms.3 = (bf16[384,1024]{1,0:T(8,128)(2,1)S(1)}, f32[384,128]{1,0:T(8,128)S(1)}, f32[384,128]{1,0:T(8,128)S(1)}) custom-call(bf16[384,128]{1,0:T(8,128)(2,1)S(1)} %get-tuple-element.66.refs_0_.b, bf16[384,128]{1,0:T(8,128)(2,1)S(1)} %get-tuple-element.67.refs_1_.c, bf16[384,2048]{1,0:T(8,128)(2,1)S(1)} %get-tuple-element.68.refs_2_.x, ...), custom_call_target="tpu_custom_call" | custom-call | flops 805306368 | bytes 3145728 | tf_op jit(solution)/shard_map/inner_terms/pallas_call | solution.py:542
  37.5 0.0 collective-permute-done.8.refs_1_
  37.5 0.2 member_entries.2
  37.7 2.1 %collective-permute-start.10 = (bf16[256,256]{1,0:T(8,128)(2,1)S(1)}, bf16[256,256]{1,0:T(8,128)(2,1)S(1)}, u32[]{:S(2)}, u32[]{:S(2)}) collective-permute-start(bf16[256,256]{1,0:T(8,128)(2,1)S(1)} %get-tuple-element.100), channel_id=1, source_target_pairs={{0,6},{2,4},{4,2},{6,0},{8,14},{10,12},{12,10},{14,8},{16,22},{18,... | collective-permute-start | bytes 393224 | tf_op jit(solution)/shard_map/ppermute | solution.py:391
  39.8 1.0 %collective-permute-start.11 = (bf16[256,256]{1,0:T(8,128)(2,1)S(1)}, bf16[256,256]{1,0:T(8,128)(2,1)S(1)}, u32[]{:S(2)}, u32[]{:S(2)}) collective-permute-start(bf16[256,256]{1,0:T(8,128)(2,1)S(1)} %get-tuple-element.101), channel_id=1, source_target_pairs={{0,4},{2,6},{4,0},{6,2},{8,12},{10,14},{12,8},{14,10},{16,20},{18,... | collective-permute-start | bytes 393224 | tf_op jit(solution)/shard_map/ppermute | solution.py:391
  40.8 0.0 collective-permute-done.13.refs_5_.refs_9_
  40.8 0.5 collective-permute-start.9
  41.2 0.0 collective-permute-done.14.refs_6_.refs_10_
  41.3 0.4 entry_values.1.refs_8_.refs_12_
  41.7 0.6 %entry_parts.2 = (f32[384,128]{1,0:T(8,128)S(1)}, f32[384,128]{1,0:T(8,128)S(1)}) custom-call(f32[384,128]{1,0:T(8,128)S(1)} %get-tuple-element.97.refs_6_.db_before, f32[384,128]{1,0:T(8,128)S(1)} %get-tuple-element.111.dc_before, bf16[384,256]{1,0:T(8,128)(2,1)S(1)} %get-tuple-element.74.refs_0_, bf16[384,256]{1,0:T(8,128)(2,1)S(1)} %get-tuple-element.112.refs_1_, ...), custom_call_target="tpu_custom_call" | custom-call | flops 100663296 | bytes 786432 | tf_op jit(solution)/shard_map/entry_parts/pallas_call | solution.py:580
  42.3 1.4 %collective-permute-done.10.refs_6_.refs_9_ = bf16[256,256]{1,0:T(8,128)(2,1)S(1)} collective-permute-done((bf16[256,256]{1,0:T(8,128)(2,1)S(1)}, bf16[256,256]{1,0:T(8,128)(2,1)S(1)}, u32[]{:S(2)}, u32[]{:S(2)}) %collective-permute-start.10) | collective-permute-done | bytes 131104 | tf_op jit(solution)/shard_map/ppermute | solution.py:391
  43.7 1.4 %collective-permute-done.11.refs_7_.refs_10_ = bf16[256,256]{1,0:T(8,128)(2,1)S(1)} collective-permute-done((bf16[256,256]{1,0:T(8,128)(2,1)S(1)}, bf16[256,256]{1,0:T(8,128)(2,1)S(1)}, u32[]{:S(2)}, u32[]{:S(2)}) %collective-permute-start.11) | collective-permute-done | bytes 131104 | tf_op jit(solution)/shard_map/ppermute | solution.py:391
  45.0 0.7 %collective-permute-done.9.refs_5_.refs_11_ = bf16[256,256]{1,0:T(8,128)(2,1)S(1)} collective-permute-done((bf16[256,256]{1,0:T(8,128)(2,1)S(1)}, bf16[256,256]{1,0:T(8,128)(2,1)S(1)}, u32[]{:S(2)}, u32[]{:S(2)}) %collective-permute-start.9) | collective-permute-done | bytes 131104 | tf_op jit(solution)/shard_map/ppermute | solution.py:391
  45.8 0.6 %entry_parts.3 = bf16[768,128]{1,0:T(8,128)(2,1)S(1)} custom-call(f32[384,128]{1,0:T(8,128)S(1)} %get-tuple-element.119.db_before, f32[384,128]{1,0:T(8,128)S(1)} %get-tuple-element.120.dc_before, bf16[384,256]{1,0:T(8,128)(2,1)S(1)} %get-tuple-element.121.refs_0_, bf16[384,256]{1,0:T(8,128)(2,1)S(1)} %get-tuple-element.122.refs_1_, ...), custom_call_target="tpu_custom_call" | custom-call | flops 100663296 | bytes 786432 | tf_op jit(solution)/shard_map/entry_parts/pallas_call | solution.py:580
  46.3 0.1 collective-permute-start.16
  46.4 1.3 %last_values.1 = bf16[384,2048]{1,0:T(8,128)(2,1)} custom-call(s32[1]{0:T(128)} %bitcast.where, bf16[384,128]{1,0:T(8,128)(2,1)S(1)} %get-tuple-element.66.refs_0_.b, bf16[384,1024]{1,0:T(8,128)(2,1)S(1)} %get-tuple-element.92.dx_local, bf16[384,256]{1,0:T(8,128)(2,1)S(1)} %get-tuple-element.93.refs_0_, bf16[384,256]{1,0:T(8,128)(2,1)S(1)} %get-tuple-element.94.refs_1_, ...), custom_call_target="tpu_custom_call" | custom-call | flops 100663296 | bytes 1572864 | tf_op jit(solution)/shard_map/last_values/pallas_call | solution.py:650
  47.7 0.2 collective-permute-done.16
  47.8 0.1 add_convert_fusion
  47.9 0.7 %fusion = (bf16[384,128]{1,0:T(8,128)(2,1)}, bf16[384,128]{1,0:T(8,128)(2,1)}) fusion(bf16[768,128]{1,0:T(8,128)(2,1)S(1)} %add_convert_fusion), kind=kLoop, calls=%fused_computation.1 | loop fusion | bytes 393216 | tf_op jit(solution)/shard_map/slice | solution.py:720
  (3 shorter events, 0.1 us)
Async XLA Ops:
  3.5 10.0 %collective-permute-start = (bf16[272,256]{1,0:T(8,128)(2,1)S(1)}, bf16[272,256]{1,0:T(8,128)(2,1)S(1)}, u32[]{:S(2)}, u32[]{:S(2)}) collective-permute-start(bf16[272,256]{1,0:T(8,128)(2,1)S(1)} %get-tuple-element.83), channel_id=1, source_target_pairs={{0,6},{2,4},{4,2},{6,0},{8,14},{10,12},{12,10},{14,8},{16,22},{18,... | collective-permute-start | bytes 417800 | tf_op jit(solution)/shard_map/ppermute | solution.py:391
  7.5 8.0 %collective-permute-start.1 = (bf16[272,256]{1,0:T(8,128)(2,1)S(1)}, bf16[272,256]{1,0:T(8,128)(2,1)S(1)}, u32[]{:S(2)}, u32[]{:S(2)}) collective-permute-start(bf16[272,256]{1,0:T(8,128)(2,1)S(1)} %get-tuple-element.84), channel_id=1, source_target_pairs={{0,4},{2,6},{4,0},{6,2},{8,12},{10,14},{12,8},{14,10},{16,20},{18,... | collective-permute-start | bytes 417800 | tf_op jit(solution)/shard_map/ppermute | solution.py:391
  8.0 7.6 %collective-permute-start.2 = (bf16[272,256]{1,0:T(8,128)(2,1)S(1)}, bf16[272,256]{1,0:T(8,128)(2,1)S(1)}, u32[]{:S(2)}, u32[]{:S(2)}) collective-permute-start(bf16[272,256]{1,0:T(8,128)(2,1)S(1)} %get-tuple-element.85), channel_id=1, source_target_pairs={{0,2},{2,0},{4,6},{6,4},{8,10},{10,8},{12,14},{14,12},{16,18},{18,... | collective-permute-start | bytes 417800 | tf_op jit(solution)/shard_map/ppermute | solution.py:391
  10.1 8.3 %collective-permute-start.4 = (bf16[272,256]{1,0:T(8,128)(2,1)S(1)}, bf16[272,256]{1,0:T(8,128)(2,1)S(1)}, u32[]{:S(2)}, u32[]{:S(2)}) collective-permute-start(bf16[272,256]{1,0:T(8,128)(2,1)S(1)} %get-tuple-element.89), channel_id=1, source_target_pairs={{0,6},{2,4},{4,2},{6,0},{8,14},{10,12},{12,10},{14,8},{16,22},{18,... | collective-permute-start | bytes 417800 | tf_op jit(solution)/shard_map/ppermute | solution.py:391
  13.0 7.1 %collective-permute-start.5 = (bf16[272,256]{1,0:T(8,128)(2,1)S(1)}, bf16[272,256]{1,0:T(8,128)(2,1)S(1)}, u32[]{:S(2)}, u32[]{:S(2)}) collective-permute-start(bf16[272,256]{1,0:T(8,128)(2,1)S(1)} %get-tuple-element.90), channel_id=1, source_target_pairs={{0,4},{2,6},{4,0},{6,2},{8,12},{10,14},{12,8},{14,10},{16,20},{18,... | collective-permute-start | bytes 417800 | tf_op jit(solution)/shard_map/ppermute | solution.py:391
  13.5 6.9 %collective-permute-start.6 = (bf16[272,256]{1,0:T(8,128)(2,1)S(1)}, bf16[272,256]{1,0:T(8,128)(2,1)S(1)}, u32[]{:S(2)}, u32[]{:S(2)}) collective-permute-start(bf16[272,256]{1,0:T(8,128)(2,1)S(1)} %get-tuple-element.91), channel_id=1, source_target_pairs={{0,2},{2,0},{4,6},{6,4},{8,10},{10,8},{12,14},{14,12},{16,18},{18,... | collective-permute-start | bytes 417800 | tf_op jit(solution)/shard_map/ppermute | solution.py:391
  15.7 6.5 %collective-permute-start.3 = (bf16[272,256]{1,0:T(8,128)(2,1)S(1)}, bf16[272,256]{1,0:T(8,128)(2,1)S(1)}, u32[]{:S(2)}, u32[]{:S(2)}) collective-permute-start(bf16[272,256]{1,0:T(8,128)(2,1)S(1)} %totals.2.own), channel_id=1, source_target_pairs={{0,8},{2,10},{4,12},{6,14},{8,0},{10,2},{12,4},{14,6},{16,24},{18,... | collective-permute-start | bytes 417800 | tf_op jit(solution)/shard_map/ppermute | solution.py:693
  20.5 10.1 %collective-permute-start.7 = (bf16[272,256]{1,0:T(8,128)(2,1)S(1)}, bf16[272,256]{1,0:T(8,128)(2,1)S(1)}, u32[]{:S(2)}, u32[]{:S(2)}) collective-permute-start(bf16[272,256]{1,0:T(8,128)(2,1)S(1)} %totals.3.own), channel_id=1, source_target_pairs={{0,8},{2,10},{4,12},{6,14},{8,0},{10,2},{12,4},{14,6},{16,24},{18,... | collective-permute-start | bytes 417800 | tf_op jit(solution)/shard_map/ppermute | solution.py:693
  22.2 6.2 %collective-permute-start.12 = (bf16[144,256]{1,0:T(8,128)(2,1)S(1)}, bf16[144,256]{1,0:T(8,128)(2,1)S(1)}, u32[]{:S(2)}, u32[]{:S(2)}) collective-permute-start(bf16[144,256]{1,0:T(8,128)(2,1)S(1)} %merged.2.refs_7_), channel_id=1, source_target_pairs={{0,16},{2,18},{4,20},{6,22},{8,24},{10,26},{12,28},{14,30},{16,0},... | collective-permute-start | bytes 221192 | tf_op jit(solution)/shard_map/ppermute | solution.py:693
  28.6 12.2 %collective-permute-start.13 = (bf16[256,256]{1,0:T(8,128)(2,1)S(1)}, bf16[256,256]{1,0:T(8,128)(2,1)S(1)}, u32[]{:S(2)}, u32[]{:S(2)}) collective-permute-start(bf16[256,256]{1,0:T(8,128)(2,1)S(1)} %get-tuple-element.108), channel_id=1, source_target_pairs={{0,6},{2,4},{4,2},{6,0},{8,14},{10,12},{12,10},{14,8},{16,22},{18,... | collective-permute-start | bytes 393224 | tf_op jit(solution)/shard_map/ppermute | solution.py:391
  30.6 6.8 %collective-permute-start.8 = (bf16[144,256]{1,0:T(8,128)(2,1)S(1)}, bf16[144,256]{1,0:T(8,128)(2,1)S(1)}, u32[]{:S(2)}, u32[]{:S(2)}) collective-permute-start(bf16[144,256]{1,0:T(8,128)(2,1)S(1)} %merged.3.refs_9_), channel_id=1, source_target_pairs={{0,16},{2,18},{4,20},{6,22},{8,24},{10,26},{12,28},{14,30},{16,0},... | collective-permute-start | bytes 221192 | tf_op jit(solution)/shard_map/ppermute | solution.py:693
  32.5 8.8 %collective-permute-start.14 = (bf16[256,256]{1,0:T(8,128)(2,1)S(1)}, bf16[256,256]{1,0:T(8,128)(2,1)S(1)}, u32[]{:S(2)}, u32[]{:S(2)}) collective-permute-start(bf16[256,256]{1,0:T(8,128)(2,1)S(1)} %get-tuple-element.109), channel_id=1, source_target_pairs={{0,4},{2,6},{4,0},{6,2},{8,12},{10,14},{12,8},{14,10},{16,20},{18,... | collective-permute-start | bytes 393224 | tf_op jit(solution)/shard_map/ppermute | solution.py:391
  33.5 7.7 %collective-permute-start.15 = (bf16[256,256]{1,0:T(8,128)(2,1)S(1)}, bf16[256,256]{1,0:T(8,128)(2,1)S(1)}, u32[]{:S(2)}, u32[]{:S(2)}) collective-permute-start(bf16[256,256]{1,0:T(8,128)(2,1)S(1)} %get-tuple-element.110), channel_id=1, source_target_pairs={{0,2},{2,0},{4,6},{6,4},{8,10},{10,8},{12,14},{14,12},{16,18},{18,... | collective-permute-start | bytes 393224 | tf_op jit(solution)/shard_map/ppermute | solution.py:391
  37.7 6.0 %collective-permute-start.10 = (bf16[256,256]{1,0:T(8,128)(2,1)S(1)}, bf16[256,256]{1,0:T(8,128)(2,1)S(1)}, u32[]{:S(2)}, u32[]{:S(2)}) collective-permute-start(bf16[256,256]{1,0:T(8,128)(2,1)S(1)} %get-tuple-element.100), channel_id=1, source_target_pairs={{0,6},{2,4},{4,2},{6,0},{8,14},{10,12},{12,10},{14,8},{16,22},{18,... | collective-permute-start | bytes 393224 | tf_op jit(solution)/shard_map/ppermute | solution.py:391
  39.8 5.3 %collective-permute-start.11 = (bf16[256,256]{1,0:T(8,128)(2,1)S(1)}, bf16[256,256]{1,0:T(8,128)(2,1)S(1)}, u32[]{:S(2)}, u32[]{:S(2)}) collective-permute-start(bf16[256,256]{1,0:T(8,128)(2,1)S(1)} %get-tuple-element.101), channel_id=1, source_target_pairs={{0,4},{2,6},{4,0},{6,2},{8,12},{10,14},{12,8},{14,10},{16,20},{18,... | collective-permute-start | bytes 393224 | tf_op jit(solution)/shard_map/ppermute | solution.py:391
  40.8 5.0 %collective-permute-start.9 = (bf16[256,256]{1,0:T(8,128)(2,1)S(1)}, bf16[256,256]{1,0:T(8,128)(2,1)S(1)}, u32[]{:S(2)}, u32[]{:S(2)}) collective-permute-start(bf16[256,256]{1,0:T(8,128)(2,1)S(1)} %get-tuple-element.99), channel_id=1, source_target_pairs={{0,2},{2,0},{4,6},{6,4},{8,10},{10,8},{12,14},{14,12},{16,18},{18,... | collective-permute-start | bytes 393224 | tf_op jit(solution)/shard_map/ppermute | solution.py:391
  46.3 1.5 %collective-permute-start.16 = (bf16[768,128]{1,0:T(8,128)(2,1)S(1)}, bf16[768,128]{1,0:T(8,128)(2,1)S(1)}, u32[]{:S(2)}, u32[]{:S(2)}) collective-permute-start(bf16[768,128]{1,0:T(8,128)(2,1)S(1)} %entry_parts.3), channel_id=1, source_target_pairs={{0,1},{1,0},{2,3},{3,2},{4,5},{5,4},{6,7},{7,6},{8,9},{9,8},{10,11... | collective-permute-start | bytes 589832 | tf_op jit(solution)/shard_map/ppermute | solution.py:670

commit v13 on v12

--- a/solution.py
+++ b/solution.py
@@ -224,8 +224,8 @@
     ref[first:, :] = both.astype(BF16)
 
 
-def sent_order(parts, fixed=1):
-    return [*parts[:fixed], *parts[: fixed - 1 : -1]]
+def sent_order(parts):
+    return [parts[0], *parts[:0:-1]]
 
 
 def in_order(group, forward):
@@ -300,11 +300,12 @@
                 value = mine + d_own * other if is_upper == forward else other + d_other * mine
                 out[slice(0, state) if last else rows, :] = value.astype(BF16)
 
-    put_decay(out, state if last else 2 * state, d_own * d_other)
+    if not last:
+        put_decay(out, 2 * state, d_own * d_other)
 
 
 def merged(state, level, last, where, own, received, after):
-    rows = (state if last else 2 * state) + TAIL
+    rows = state if last else own.shape[0]
     return pl.pallas_call(
         functools.partial(merged_kernel, state, level, last),
         out_shape=pltpu.VMEM((rows, own.shape[1]), BF16),
@@ -459,7 +460,7 @@
     setup_kernel(piece, ld, b, c, *refs[n_after:])
 
 
-def inner_kernel(head_dim, chunk, n_before, n_after, b, c, x, dy, *refs):
+def inner_kernel(head_dim, worked, n_before, n_after, b, c, x, dy, *refs):
     length, width = x.shape
     piece = head_dim
     pieces = length // piece
@@ -467,14 +468,14 @@
     n_cuts = sum(len(same) for _, same in groups)
     fars, (near, cum_terms), refs = refs[:n_cuts], refs[n_cuts : n_cuts + 2], refs[n_cuts + 2 :]
     before, refs = refs[:n_before], refs[n_before + n_after :]
-    dx_out, db_out, dc_out, x_near, dy_near, *scratch = refs
+    dx_outs, (db_out, dc_out, x_near, dy_near, *scratch) = refs[: len(worked)], refs[len(worked) :]
     lefts, rights = scratch[: len(groups)], scratch[len(groups) :]
-    part = dx_out.shape[1] // GROUP
+    part = dx_outs[0].shape[1]
     difference = row_less_head(head_dim, part, SLOT)
 
-    for m in range(GROUP):
+    for at, (chunk, m) in enumerate(worked):
         owned = m * (width // GROUP) + chunk * part
-        lanes, here = slice(owned, owned + part), slice(m * part, (m + 1) * part)
+        lanes, here = slice(owned, owned + part), slice(at * part, (at + 1) * part)
         cum = dot(cum_terms[...], head_of_lane(difference, owned // head_dim), NN)
         dx = []
         for n in range(pieces):
@@ -501,7 +502,7 @@
                 for n in range(lo, mid):
                     dx[n] = dx[n] + far[rows_of(n - lo, n - lo + 1, piece), :]
         for n in range(pieces):
-            dx_out[rows_of(n, n + 1, piece), here] = dx[n].astype(BF16)
+            dx_outs[at][rows_of(n, n + 1, piece), :] = dx[n].astype(BF16)
 
     if before:
         db_out[...] = before[0][...]
@@ -534,27 +535,26 @@
             dc_out[rows_of(mid, hi, piece), :] += dc[rows_of(g, g + 1, n_right * piece), :]
 
 
-def inner_terms(head_dim, chunk, setup, b, c, x, dy, before, after):
-    length, state = b.shape
-    columns = x.shape[1] // chunk_count(x.shape[1])
+def inner_terms(head_dim, worked, setup, b, c, x, dy, before, after):
+    (length, state), width = b.shape, x.shape[1]
+    part = width // (GROUP * chunk_count(width))
+    used = part * len(worked)
     groups = grouped_cuts(length // head_dim)
     sizes = [[len(same) * n * head_dim for n in halves] for halves, same in groups]
-    return pl.pallas_call(
-        functools.partial(inner_kernel, head_dim, chunk, len(before), len(after)),
-        out_shape=[
-            jax.ShapeDtypeStruct((length, columns), BF16),
-            jax.ShapeDtypeStruct((length, state), F32),
-            jax.ShapeDtypeStruct((length, state), F32),
-        ],
+    found = pl.pallas_call(
+        functools.partial(inner_kernel, head_dim, worked, len(before), len(after)),
+        out_shape=[jax.ShapeDtypeStruct((length, part), BF16)] * len(worked)
+        + [jax.ShapeDtypeStruct((length, state), F32)] * 2,
         in_specs=whole(4 + len(setup) + len(before)) + [ANY] * len(after),
-        out_specs=whole(3),
-        scratch_shapes=[pltpu.VMEM((length, columns), BF16)] * 2
-        + [pltpu.VMEM((left, columns), BF16) for left, _ in sizes]
-        + [pltpu.VMEM((right, columns), BF16) for _, right in sizes],
+        out_specs=whole(len(worked) + 2),
+        scratch_shapes=[pltpu.VMEM((length, used), BF16)] * 2
+        + [pltpu.VMEM((left, used), BF16) for left, _ in sizes]
+        + [pltpu.VMEM((right, used), BF16) for _, right in sizes],
         compiler_params=params(16),
         cost_estimate=cost(8 * x.size * state, 4 * x.size, 2 * x.size),
         name="inner_terms",
     )(b, c, x, dy, *setup, *before, *after)
+    return dict(zip(worked, found)), list(found[-2:])
 
 
 def parts_kernel(last, db_before, dc_before, *refs):
@@ -588,8 +588,10 @@
     )(db_before, dc_before, *scaled, *sent_order(entries), *after)
 
 
-def put_values(where, spread, b, dx_local, entries, put):
+def put_values(where, spread, b, local_parts, dx_local, entries, put):
     state, part = b.shape[1], entries[0].shape[1]
+    for m, one in enumerate(local_parts):
+        dx_local[:, m * part : (m + 1) * part] = one[...]
     for k, entry in enumerate(entries):
         here = slice(k * part, (k + 1) * part)
         local = dx_local[:, pl.ds(pl.multiple_of((place_of(where) ^ k) * part, part), part)]
@@ -597,19 +599,20 @@
         put(k, here, (local.astype(F32) + far).astype(BF16))
 
 
-def values_kernel(where, b, dx_local, *refs):
-    spread, entries, out = refs[:GROUP], sent_order(refs[GROUP : 2 * GROUP]), refs[-1]
+def values_kernel(where, b, *refs):
+    local_parts, spread = refs[:GROUP], refs[GROUP : 2 * GROUP]
+    entries, (out, dx_local) = sent_order(refs[2 * GROUP : 3 * GROUP]), refs[-2:]
 
     def put(k, here, value):
         out[:, here] = value
 
-    put_values(where, spread, b, dx_local, entries, put)
-
-
-def last_values_kernel(chunks, where, b, dx_local, *refs):
-    spread, refs = refs[:GROUP], refs[GROUP:]
-    entries, before = sent_order(refs[:GROUP], 2), refs[GROUP : GROUP + chunks - 1]
-    out, dx, sems = refs[-3:]
+    put_values(where, spread, b, local_parts, dx_local, entries, put)
+
+
+def last_values_kernel(chunks, where, b, *refs):
+    local_parts, spread, refs = refs[:GROUP], refs[GROUP : 2 * GROUP], refs[2 * GROUP :]
+    entries, before = sent_order(refs[:GROUP]), refs[GROUP : GROUP + chunks - 1]
+    out, dx, dx_local, sems = refs[-4:]
     part = entries[0].shape[1]
     stores = []
 
@@ -627,22 +630,23 @@
         dx[k] = value
         store(chunks - 1, k, dx.at[k])
 
-    put_values(where, spread, b, dx_local, entries, put)
+    put_values(where, spread, b, local_parts, dx_local, entries, put)
     for one in stores:
         one.wait()
 
 
-def entry_values(chunk, chunks, where, spread, b, dx_local, entries, before):
+def entry_values(chunk, chunks, where, spread, b, local_parts, entries, before):
     length, part = b.shape[0], entries[0].shape[1]
     last = chunk == chunks - 1
-    estimate = cost(2 * dx_local.size * b.shape[1], 4 * dx_local.size)
-    operands = [where, b, dx_local, *spread, *sent_order(entries, 2 if last else 1)]
+    estimate = cost(8 * local_parts[0].size * b.shape[1], 16 * local_parts[0].size)
+    operands = [where, b, *local_parts, *spread, *sent_order(entries)]
     if not last:
         return pl.pallas_call(
             values_kernel,
             out_shape=jax.ShapeDtypeStruct((length, GROUP * part), BF16),
-            in_specs=[SMEM] + whole(2 + 2 * GROUP),
+            in_specs=[SMEM] + whole(1 + 3 * GROUP),
             out_specs=whole(1)[0],
+            scratch_shapes=[pltpu.VMEM((length, GROUP * part), BF16)],
             compiler_params=params(8),
             cost_estimate=estimate,
             name="entry_values",
@@ -650,10 +654,11 @@
     return pl.pallas_call(
         functools.partial(last_values_kernel, chunks),
         out_shape=pltpu.HBM((length, chunks * GROUP * part), BF16),
-        in_specs=[SMEM] + whole(2 + 2 * GROUP + len(before)),
+        in_specs=[SMEM] + whole(1 + 3 * GROUP + len(before)),
         out_specs=HBM,
         scratch_shapes=[
             pltpu.VMEM((GROUP, length, part), BF16),
+            pltpu.VMEM((length, GROUP * part), BF16),
             pltpu.SemaphoreType.DMA((chunks * GROUP,)),
         ],
         compiler_params=params(8),
@@ -692,7 +697,15 @@
     def to_group(block, k):
         return lax.ppermute(block, "seq", [(s, s ^ (k * group)) for s in range(count)])
 
-    entries, inner, sums = [], [], []
+    every = [(chunk, m) for chunk in range(chunks) for m in range(group)]
+    worked = [every[:3]] + [every[chunk * group :][:2] for chunk in range(1, chunks)]
+    rest = [one for one in every if not any(one in some for some in worked)]
+    entries, inner, sums = [], {}, []
+
+    def add_inner(some, after):
+        found, sums[:] = inner_terms(head_dim, some, setup, b, c, x, dy, sums, after)
+        inner.update(found)
+
     for chunk in range(chunks):
         (own,) = totals(state, 0, where, blocks[chunk], setup[-1:] if chunk == 0 else [])
         received = [to_group(own, 1)]
@@ -700,10 +713,10 @@
             last = level == levels - 2
             own = merged(state, level, last, where, own, received[level], [])
             received.append(to_group(own, 2 << level))
-        inner.append(inner_terms(head_dim, chunk, setup, b, c, x, dy, sums, [own]))
-        sums = list(inner[chunk][1:])
+        add_inner(worked[chunk], [own])
         found = member_entries(state, False, where, blocks[chunk], received, sums[:1])
         entries.append(exchange(found))
+    add_inner(rest, found[:1])
 
     values = []
     for chunk in range(chunks):
@@ -712,7 +725,7 @@
         scaled = [one for k in range(group) for one in ours[k][:2]]
         spread = [one[2] for one in ours]
         sums = entry_parts(last, scaled, *sums, entries[chunk], values)
-        local = inner[chunk][0]
+        local = [inner[chunk, m] for m in range(group)]
         values.append(
             entry_values(chunk, chunks, where, spread, b, local, entries[chunk], values)
         )

time: 48.7 us -> 47.4 us (0.973)
  waiting for transfers between devices: 7.69 us -> 4.68 us
  Pallas kernels: 15.8 us -> 17.3 us
    ppermute x12, waiting for transfers between devices: 7.51 us -> 4.4 us  [exchange(): out[k] = lax.ppermute(parts[k], 'seq', [(s, s ^ k) for s in range(count)])]
    pallas_call x2 -> x3, Pallas kernels: 7 us -> 8.24 us  [inner_terms(): pl.pallas_call(functools.partial(inner_kernel, head_dim, worked, len(befo...]
  transfers between devices with their start and end apart: 17 -> 17, of which waited for: 9 -> 9; matrix products, arithmetic and copies ran while one was open for 0% -> 0% of each run, Pallas kernels for 25% -> 29%
where the time goes in v13:
time: 47.4 us; the launch traced here: 47.2 us
  starting transfers between devices  23.7 us (50%)
  Pallas kernels  17.3 us (36%)
  waiting for transfers between devices  4.68 us (10%)
  between operations  0.81 us (2%)
  local copies, waits for them, and re-layouts  0.69 us (1%)
    ppermute x12, starting transfers between devices, exchange(): out[k] = lax.ppermute(parts[k], 'seq', [(s, s ^ k) for s in range(count)])  15.4 us
    pallas_call x3, Pallas kernels, inner_terms(): pl.pallas_call(functools.partial(inner_kernel, head_dim, worked, len(befo...  8.24 us
    ppermute x4, starting transfers between devices, to_group(): lax.ppermute(block, 'seq', [(s, s ^ k * group) for s in range(count)])  8.23 us
    ppermute x12, waiting for transfers between devices, exchange(): out[k] = lax.ppermute(parts[k], 'seq', [(s, s ^ k) for s in range(count)])  4.4 us
    pallas_call x1, Pallas kernels, first_states(): pl.pallas_call(functools.partial(first_states_kernel, head_dim, pieces),...  2.91 us
    pallas_call x1, Pallas kernels, next_states(): pl.pallas_call(functools.partial(next_states_kernel, head_dim, pieces), o...  1.93 us
    pallas_call x1, Pallas kernels, entry_values(): pl.pallas_call(functools.partial(last_values_kernel, chunks), out_shape=p...  1.33 us
    pallas_call x2, Pallas kernels, entry_parts(): pl.pallas_call(functools.partial(parts_kernel, last), out_shape=outs, in_...  1.13 us
  transfers between devices with their start and end apart: 17, of which 9 were waited for; matrix products, arithmetic and copies ran while one was open for 0% of the time, Pallas kernels for 29%

profile of v13, /device:TPU:0, one launch (start us, length us, event | category | flops | bytes accessed | tf_op | source)
XLA Modules:
  0.0 47.2 jit_solution(10502571972625004022)
XLA Ops:
  0.6 2.9 %first_states.1 = (f32[32,384]{1,0:T(8,128)S(1)}, bf16[384,128]{1,0:T(8,128)(2,1)S(1)}, bf16[384,128]{1,0:T(8,128)(2,1)S(1)}, bf16[384,2048]{1,0:T(8,128)(2,1)S(...) custom-call(s32[1]{0:T(128)} %bitcast.where, ...), custom_call_target="tpu_custom_call" | custom-call | flops 402653184 | bytes 6291456 | tf_op jit(solution)/shard_map/first_states/pallas_call | solution.py:187
  3.6 4.0 %collective-permute-start = (bf16[272,256]{1,0:T(8,128)(2,1)S(1)}, bf16[272,256]{1,0:T(8,128)(2,1)S(1)}, u32[]{:S(2)}, u32[]{:S(2)}) collective-permute-start(bf16[272,256]{1,0:T(8,128)(2,1)S(1)} %get-tuple-element.91), channel_id=1, source_target_pairs={{0,6},{2,4},{4,2},{6,0},{8,14},{10,12},{12,10},{14,8},{16,22},{18,... | collective-permute-start | bytes 417800 | tf_op jit(solution)/shard_map/ppermute | solution.py:392
  7.5 0.5 %collective-permute-start.1 = (bf16[272,256]{1,0:T(8,128)(2,1)S(1)}, bf16[272,256]{1,0:T(8,128)(2,1)S(1)}, u32[]{:S(2)}, u32[]{:S(2)}) collective-permute-start(bf16[272,256]{1,0:T(8,128)(2,1)S(1)} %get-tuple-element.92), channel_id=1, source_target_pairs={{0,4},{2,6},{4,0},{6,2},{8,12},{10,14},{12,8},{14,10},{16,20},{18,... | collective-permute-start | bytes 417800 | tf_op jit(solution)/shard_map/ppermute | solution.py:392
  8.0 0.1 collective-permute-start.2
  8.2 1.9 %next_states.1 = (bf16[384,256]{1,0:T(8,128)(2,1)S(1)}, bf16[384,256]{1,0:T(8,128)(2,1)S(1)}, bf16[384,256]{1,0:T(8,128)(2,1)S(1)}, bf16[272,256]{1,0:T(8,128)(2...) custom-call(s32[1]{0:T(128)} %bitcast.where, ...), custom_call_target="tpu_custom_call" | custom-call | flops 402653184 | bytes 3145728 | tf_op jit(solution)/shard_map/next_states/pallas_call | solution.py:203
  10.1 2.9 %collective-permute-start.4 = (bf16[272,256]{1,0:T(8,128)(2,1)S(1)}, bf16[272,256]{1,0:T(8,128)(2,1)S(1)}, u32[]{:S(2)}, u32[]{:S(2)}) collective-permute-start(bf16[272,256]{1,0:T(8,128)(2,1)S(1)} %get-tuple-element.97), channel_id=1, source_target_pairs={{0,6},{2,4},{4,2},{6,0},{8,14},{10,12},{12,10},{14,8},{16,22},{18,... | collective-permute-start | bytes 417800 | tf_op jit(solution)/shard_map/ppermute | solution.py:392
  13.0 0.5 %collective-permute-start.5 = (bf16[272,256]{1,0:T(8,128)(2,1)S(1)}, bf16[272,256]{1,0:T(8,128)(2,1)S(1)}, u32[]{:S(2)}, u32[]{:S(2)}) collective-permute-start(bf16[272,256]{1,0:T(8,128)(2,1)S(1)} %get-tuple-element.98), channel_id=1, source_target_pairs={{0,4},{2,6},{4,0},{6,2},{8,12},{10,14},{12,8},{14,10},{16,20},{18,... | collective-permute-start | bytes 417800 | tf_op jit(solution)/shard_map/ppermute | solution.py:392
  13.5 0.0 collective-permute-done.refs_1_.refs_5_
  13.5 0.5 %collective-permute-start.6 = (bf16[272,256]{1,0:T(8,128)(2,1)S(1)}, bf16[272,256]{1,0:T(8,128)(2,1)S(1)}, u32[]{:S(2)}, u32[]{:S(2)}) collective-permute-start(bf16[272,256]{1,0:T(8,128)(2,1)S(1)} %get-tuple-element.99), channel_id=1, source_target_pairs={{0,2},{2,0},{4,6},{6,4},{8,10},{10,8},{12,14},{14,12},{16,18},{18,... | collective-permute-start | bytes 417800 | tf_op jit(solution)/shard_map/ppermute | solution.py:392
  14.0 0.5 inner_setup.1
  14.5 1.0 %collective-permute-done.1.refs_2_.refs_4_ = bf16[272,256]{1,0:T(8,128)(2,1)S(1)} collective-permute-done((bf16[272,256]{1,0:T(8,128)(2,1)S(1)}, bf16[272,256]{1,0:T(8,128)(2,1)S(1)}, u32[]{:S(2)}, u32[]{:S(2)}) %collective-permute-start.1) | collective-permute-done | bytes 139296 | tf_op jit(solution)/shard_map/ppermute | solution.py:392
  15.5 0.1 collective-permute-done.2.refs_3_
  15.6 0.1 totals.2.own
  15.7 1.8 %collective-permute-start.3 = (bf16[272,256]{1,0:T(8,128)(2,1)S(1)}, bf16[272,256]{1,0:T(8,128)(2,1)S(1)}, u32[]{:S(2)}, u32[]{:S(2)}) collective-permute-start(bf16[272,256]{1,0:T(8,128)(2,1)S(1)} %totals.2.own), channel_id=1, source_target_pairs={{0,8},{2,10},{4,12},{6,14},{8,0},{10,2},{12,4},{14,6},{16,24},{18,... | collective-permute-start | bytes 417800 | tf_op jit(solution)/shard_map/ppermute | solution.py:698
  17.5 0.9 %collective-permute-done.4.refs_1_.refs_5_ = bf16[272,256]{1,0:T(8,128)(2,1)S(1)} collective-permute-done((bf16[272,256]{1,0:T(8,128)(2,1)S(1)}, bf16[272,256]{1,0:T(8,128)(2,1)S(1)}, u32[]{:S(2)}, u32[]{:S(2)}) %collective-permute-start.4) | collective-permute-done | bytes 139296 | tf_op jit(solution)/shard_map/ppermute | solution.py:392
  18.4 1.7 %collective-permute-done.5.refs_2_.refs_4_ = bf16[272,256]{1,0:T(8,128)(2,1)S(1)} collective-permute-done((bf16[272,256]{1,0:T(8,128)(2,1)S(1)}, bf16[272,256]{1,0:T(8,128)(2,1)S(1)}, u32[]{:S(2)}, u32[]{:S(2)}) %collective-permute-start.5) | collective-permute-done | bytes 139296 | tf_op jit(solution)/shard_map/ppermute | solution.py:392
  20.1 0.3 collective-permute-done.6.refs_3_
  20.4 0.1 totals.3.own
  20.5 1.6 %collective-permute-start.7 = (bf16[272,256]{1,0:T(8,128)(2,1)S(1)}, bf16[272,256]{1,0:T(8,128)(2,1)S(1)}, u32[]{:S(2)}, u32[]{:S(2)}) collective-permute-start(bf16[272,256]{1,0:T(8,128)(2,1)S(1)} %totals.3.own), channel_id=1, source_target_pairs={{0,8},{2,10},{4,12},{6,14},{8,0},{10,2},{12,4},{14,6},{16,24},{18,... | collective-permute-start | bytes 417800 | tf_op jit(solution)/shard_map/ppermute | solution.py:698
  22.2 0.0 collective-permute-done.3.received.refs_0_
  22.2 2.6 %collective-permute-start.12 = (bf16[128,256]{1,0:T(8,128)(2,1)S(1)}, bf16[128,256]{1,0:T(8,128)(2,1)S(1)}, u32[]{:S(2)}, u32[]{:S(2)}) collective-permute-start(bf16[128,256]{1,0:T(8,128)(2,1)S(1)} %merged.2.refs_7_), channel_id=1, source_target_pairs={{0,16},{2,18},{4,20},{6,22},{8,24},{10,26},{12,28},{14,30},{16,0},... | collective-permute-start | bytes 196616 | tf_op jit(solution)/shard_map/ppermute | solution.py:698
  24.9 3.1 %inner_terms.3 = (bf16[384,256]{1,0:T(8,128)(2,1)S(1)}, bf16[384,256]{1,0:T(8,128)(2,1)S(1)}, bf16[384,256]{1,0:T(8,128)(2,1)S(1)}, f32[384,128]{1,0:T(8,128)S(1)}, f32[384,128]{1,0:T(8,128)S(1)}) custom-call(bf16[384,128]{1,0:T(8,128)(2,1)S(1)} %get-tuple-element.74.refs_0_.b, bf16[384,128]{1,0:T(8,128)(2,1)S(1)} %get-tuple-element.75.refs_1_.c, ...), custom_call_target="tpu_custom_call" | custom-call | flops 805306368 | bytes 3145728 | tf_op jit(solution)/shard_map/inner_terms/pallas_call | solution.py:544
  28.0 0.2 collective-permute-done.12.refs_1_
  28.1 0.2 member_entries.3
  28.3 1.8 %collective-permute-start.13 = (bf16[256,256]{1,0:T(8,128)(2,1)S(1)}, bf16[256,256]{1,0:T(8,128)(2,1)S(1)}, u32[]{:S(2)}, u32[]{:S(2)}) collective-permute-start(bf16[256,256]{1,0:T(8,128)(2,1)S(1)} %get-tuple-element.123), channel_id=1, source_target_pairs={{0,6},{2,4},{4,2},{6,0},{8,14},{10,12},{12,10},{14,8},{16,22},{18,... | collective-permute-start | bytes 393224 | tf_op jit(solution)/shard_map/ppermute | solution.py:392
  30.2 0.0 collective-permute-done.7.received.refs_0_
  30.2 2.2 %collective-permute-start.8 = (bf16[128,256]{1,0:T(8,128)(2,1)S(1)}, bf16[128,256]{1,0:T(8,128)(2,1)S(1)}, u32[]{:S(2)}, u32[]{:S(2)}) collective-permute-start(bf16[128,256]{1,0:T(8,128)(2,1)S(1)} %merged.3.refs_9_), channel_id=1, source_target_pairs={{0,16},{2,18},{4,20},{6,22},{8,24},{10,26},{12,28},{14,30},{16,0},... | collective-permute-start | bytes 196616 | tf_op jit(solution)/shard_map/ppermute | solution.py:698
  32.4 1.0 %collective-permute-start.14 = (bf16[256,256]{1,0:T(8,128)(2,1)S(1)}, bf16[256,256]{1,0:T(8,128)(2,1)S(1)}, u32[]{:S(2)}, u32[]{:S(2)}) collective-permute-start(bf16[256,256]{1,0:T(8,128)(2,1)S(1)} %get-tuple-element.124), channel_id=1, source_target_pairs={{0,4},{2,6},{4,0},{6,2},{8,12},{10,14},{12,8},{14,10},{16,20},{18,... | collective-permute-start | bytes 393224 | tf_op jit(solution)/shard_map/ppermute | solution.py:392
  33.4 0.5 %collective-permute-start.15 = (bf16[256,256]{1,0:T(8,128)(2,1)S(1)}, bf16[256,256]{1,0:T(8,128)(2,1)S(1)}, u32[]{:S(2)}, u32[]{:S(2)}) collective-permute-start(bf16[256,256]{1,0:T(8,128)(2,1)S(1)} %get-tuple-element.125), channel_id=1, source_target_pairs={{0,2},{2,0},{4,6},{6,4},{8,10},{10,8},{12,14},{14,12},{16,18},{18,... | collective-permute-start | bytes 393224 | tf_op jit(solution)/shard_map/ppermute | solution.py:392
  33.9 2.1 %inner_terms.4 = (bf16[384,256]{1,0:T(8,128)(2,1)S(1)}, bf16[384,256]{1,0:T(8,128)(2,1)S(1)}, f32[384,128]{1,0:T(8,128)S(1)}, f32[384,128]{1,0:T(8,128)S(1)}) custom-call(bf16[384,128]{1,0:T(8,128)(2,1)S(1)} %get-tuple-element.74.refs_0_.b, bf16[384,128]{1,0:T(8,128)(2,1)S(1)} %get-tuple-element.75.refs_1_.c, ...), custom_call_target="tpu_custom_call" | custom-call | flops 805306368 | bytes 3145728 | tf_op jit(solution)/shard_map/inner_terms/pallas_call | solution.py:544
  36.0 0.0 collective-permute-done.8.refs_1_
  36.0 0.4 member_entries.2
  36.4 2.1 %collective-permute-start.9 = (bf16[256,256]{1,0:T(8,128)(2,1)S(1)}, bf16[256,256]{1,0:T(8,128)(2,1)S(1)}, u32[]{:S(2)}, u32[]{:S(2)}) collective-permute-start(bf16[256,256]{1,0:T(8,128)(2,1)S(1)} %get-tuple-element.111), channel_id=1, source_target_pairs={{0,6},{2,4},{4,2},{6,0},{8,14},{10,12},{12,10},{14,8},{16,22},{18,... | collective-permute-start | bytes 393224 | tf_op jit(solution)/shard_map/ppermute | solution.py:392
  38.4 1.0 %collective-permute-start.10 = (bf16[256,256]{1,0:T(8,128)(2,1)S(1)}, bf16[256,256]{1,0:T(8,128)(2,1)S(1)}, u32[]{:S(2)}, u32[]{:S(2)}) collective-permute-start(bf16[256,256]{1,0:T(8,128)(2,1)S(1)} %get-tuple-element.112), channel_id=1, source_target_pairs={{0,4},{2,6},{4,0},{6,2},{8,12},{10,14},{12,8},{14,10},{16,20},{18,... | collective-permute-start | bytes 393224 | tf_op jit(solution)/shard_map/ppermute | solution.py:392
  39.4 0.0 collective-permute-done.13.refs_9_
  39.4 0.5 %collective-permute-start.11 = (bf16[256,256]{1,0:T(8,128)(2,1)S(1)}, bf16[256,256]{1,0:T(8,128)(2,1)S(1)}, u32[]{:S(2)}, u32[]{:S(2)}) collective-permute-start(bf16[256,256]{1,0:T(8,128)(2,1)S(1)} %get-tuple-element.113), channel_id=1, source_target_pairs={{0,2},{2,0},{4,6},{6,4},{8,10},{10,8},{12,14},{14,12},{16,18},{18,... | collective-permute-start | bytes 393224 | tf_op jit(solution)/shard_map/ppermute | solution.py:392
  39.9 3.1 %inner_terms.5 = (bf16[384,256]{1,0:T(8,128)(2,1)S(1)}, bf16[384,256]{1,0:T(8,128)(2,1)S(1)}, bf16[384,256]{1,0:T(8,128)(2,1)S(1)}, f32[384,128]{1,0:T(8,128)S(1)}, f32[384,128]{1,0:T(8,128)S(1)}) custom-call(bf16[384,128]{1,0:T(8,128)(2,1)S(1)} %get-tuple-element.74.refs_0_.b, bf16[384,128]{1,0:T(8,128)(2,1)S(1)} %get-tuple-element.75.refs_1_.c, ...), custom_call_target="tpu_custom_call" | custom-call | flops 805306368 | bytes 3145728 | tf_op jit(solution)/shard_map/inner_terms/pallas_call | solution.py:544
  43.0 0.0 collective-permute-done.15.refs_11_
  43.0 0.4 entry_values.1.refs_12_
  43.5 0.6 %entry_parts.2 = (f32[384,128]{1,0:T(8,128)S(1)}, f32[384,128]{1,0:T(8,128)S(1)}) custom-call(f32[384,128]{1,0:T(8,128)S(1)} %get-tuple-element.126.db_before, f32[384,128]{1,0:T(8,128)S(1)} %get-tuple-element.127.dc_before, bf16[384,256]{1,0:T(8,128)(2,1)S(1)} %get-tuple-element.82.refs_0_, bf16[384,256]{1,0:T(8,128)(2,1)S(1)} %get-tuple-element.128.refs_1_, ...), custom_call_target="tpu_custom_call" | custom-call | flops 100663296 | bytes 786432 | tf_op jit(solution)/shard_map/entry_parts/pallas_call | solution.py:580
  44.0 0.2 collective-permute-done.10.refs_10_
  44.3 0.1 collective-permute-done.11.refs_11_
  44.4 0.6 %entry_parts.3 = bf16[768,128]{1,0:T(8,128)(2,1)S(1)} custom-call(f32[384,128]{1,0:T(8,128)S(1)} %get-tuple-element.135.db_before, f32[384,128]{1,0:T(8,128)S(1)} %get-tuple-element.136.dc_before, bf16[384,256]{1,0:T(8,128)(2,1)S(1)} %get-tuple-element.137.refs_0_, bf16[384,256]{1,0:T(8,128)(2,1)S(1)} %get-tuple-element.138.refs_1_, ...), custom_call_target="tpu_custom_call" | custom-call | flops 100663296 | bytes 786432 | tf_op jit(solution)/shard_map/entry_parts/pallas_call | solution.py:580
  45.0 0.1 collective-permute-start.16
  45.1 1.3 %last_values.1 = bf16[384,2048]{1,0:T(8,128)(2,1)} custom-call(s32[1]{0:T(128)} %bitcast.where, bf16[384,128]{1,0:T(8,128)(2,1)S(1)} %get-tuple-element.74.refs_0_.b, bf16[384,256]{1,0:T(8,128)(2,1)S(1)} %get-tuple-element.100.refs_0_, bf16[384,256]{1,0:T(8,128)(2,1)S(1)} %get-tuple-element.101.refs_1_, bf16[384,256]{1,0:T(8,128)(2,1)S(1)} %get-tuple-element.105.refs_2_, ...), custom_call_target="tpu_custom_call" | custom-call | flops 100663296 | bytes 1572864 | tf_op jit(solution)/shard_map/last_values/pallas_call | solution.py:654
  46.4 0.1 collective-permute-done.16
  46.5 0.1 add_convert_fusion
  46.5 0.7 %fusion = (bf16[384,128]{1,0:T(8,128)(2,1)}, bf16[384,128]{1,0:T(8,128)(2,1)}) fusion(bf16[768,128]{1,0:T(8,128)(2,1)S(1)} %add_convert_fusion), kind=kLoop, calls=%fused_computation.1 | loop fusion | bytes 393216 | tf_op jit(solution)/shard_map/slice | solution.py:733
  (4 shorter events, 0.1 us)
Async XLA Ops:
  3.6 10.0 %collective-permute-start = (bf16[272,256]{1,0:T(8,128)(2,1)S(1)}, bf16[272,256]{1,0:T(8,128)(2,1)S(1)}, u32[]{:S(2)}, u32[]{:S(2)}) collective-permute-start(bf16[272,256]{1,0:T(8,128)(2,1)S(1)} %get-tuple-element.91), channel_id=1, source_target_pairs={{0,6},{2,4},{4,2},{6,0},{8,14},{10,12},{12,10},{14,8},{16,22},{18,... | collective-permute-start | bytes 417800 | tf_op jit(solution)/shard_map/ppermute | solution.py:392
  7.5 8.0 %collective-permute-start.1 = (bf16[272,256]{1,0:T(8,128)(2,1)S(1)}, bf16[272,256]{1,0:T(8,128)(2,1)S(1)}, u32[]{:S(2)}, u32[]{:S(2)}) collective-permute-start(bf16[272,256]{1,0:T(8,128)(2,1)S(1)} %get-tuple-element.92), channel_id=1, source_target_pairs={{0,4},{2,6},{4,0},{6,2},{8,12},{10,14},{12,8},{14,10},{16,20},{18,... | collective-permute-start | bytes 417800 | tf_op jit(solution)/shard_map/ppermute | solution.py:392
  8.0 7.6 %collective-permute-start.2 = (bf16[272,256]{1,0:T(8,128)(2,1)S(1)}, bf16[272,256]{1,0:T(8,128)(2,1)S(1)}, u32[]{:S(2)}, u32[]{:S(2)}) collective-permute-start(bf16[272,256]{1,0:T(8,128)(2,1)S(1)} %get-tuple-element.93), channel_id=1, source_target_pairs={{0,2},{2,0},{4,6},{6,4},{8,10},{10,8},{12,14},{14,12},{16,18},{18,... | collective-permute-start | bytes 417800 | tf_op jit(solution)/shard_map/ppermute | solution.py:392
  10.1 8.3 %collective-permute-start.4 = (bf16[272,256]{1,0:T(8,128)(2,1)S(1)}, bf16[272,256]{1,0:T(8,128)(2,1)S(1)}, u32[]{:S(2)}, u32[]{:S(2)}) collective-permute-start(bf16[272,256]{1,0:T(8,128)(2,1)S(1)} %get-tuple-element.97), channel_id=1, source_target_pairs={{0,6},{2,4},{4,2},{6,0},{8,14},{10,12},{12,10},{14,8},{16,22},{18,... | collective-permute-start | bytes 417800 | tf_op jit(solution)/shard_map/ppermute | solution.py:392
  13.0 7.1 %collective-permute-start.5 = (bf16[272,256]{1,0:T(8,128)(2,1)S(1)}, bf16[272,256]{1,0:T(8,128)(2,1)S(1)}, u32[]{:S(2)}, u32[]{:S(2)}) collective-permute-start(bf16[272,256]{1,0:T(8,128)(2,1)S(1)} %get-tuple-element.98), channel_id=1, source_target_pairs={{0,4},{2,6},{4,0},{6,2},{8,12},{10,14},{12,8},{14,10},{16,20},{18,... | collective-permute-start | bytes 417800 | tf_op jit(solution)/shard_map/ppermute | solution.py:392
  13.5 6.9 %collective-permute-start.6 = (bf16[272,256]{1,0:T(8,128)(2,1)S(1)}, bf16[272,256]{1,0:T(8,128)(2,1)S(1)}, u32[]{:S(2)}, u32[]{:S(2)}) collective-permute-start(bf16[272,256]{1,0:T(8,128)(2,1)S(1)} %get-tuple-element.99), channel_id=1, source_target_pairs={{0,2},{2,0},{4,6},{6,4},{8,10},{10,8},{12,14},{14,12},{16,18},{18,... | collective-permute-start | bytes 417800 | tf_op jit(solution)/shard_map/ppermute | solution.py:392
  15.7 6.5 %collective-permute-start.3 = (bf16[272,256]{1,0:T(8,128)(2,1)S(1)}, bf16[272,256]{1,0:T(8,128)(2,1)S(1)}, u32[]{:S(2)}, u32[]{:S(2)}) collective-permute-start(bf16[272,256]{1,0:T(8,128)(2,1)S(1)} %totals.2.own), channel_id=1, source_target_pairs={{0,8},{2,10},{4,12},{6,14},{8,0},{10,2},{12,4},{14,6},{16,24},{18,... | collective-permute-start | bytes 417800 | tf_op jit(solution)/shard_map/ppermute | solution.py:698
  20.5 9.6 %collective-permute-start.7 = (bf16[272,256]{1,0:T(8,128)(2,1)S(1)}, bf16[272,256]{1,0:T(8,128)(2,1)S(1)}, u32[]{:S(2)}, u32[]{:S(2)}) collective-permute-start(bf16[272,256]{1,0:T(8,128)(2,1)S(1)} %totals.3.own), channel_id=1, source_target_pairs={{0,8},{2,10},{4,12},{6,14},{8,0},{10,2},{12,4},{14,6},{16,24},{18,... | collective-permute-start | bytes 417800 | tf_op jit(solution)/shard_map/ppermute | solution.py:698
  22.2 5.9 %collective-permute-start.12 = (bf16[128,256]{1,0:T(8,128)(2,1)S(1)}, bf16[128,256]{1,0:T(8,128)(2,1)S(1)}, u32[]{:S(2)}, u32[]{:S(2)}) collective-permute-start(bf16[128,256]{1,0:T(8,128)(2,1)S(1)} %merged.2.refs_7_), channel_id=1, source_target_pairs={{0,16},{2,18},{4,20},{6,22},{8,24},{10,26},{12,28},{14,30},{16,0},... | collective-permute-start | bytes 196616 | tf_op jit(solution)/shard_map/ppermute | solution.py:698
  28.3 11.1 %collective-permute-start.13 = (bf16[256,256]{1,0:T(8,128)(2,1)S(1)}, bf16[256,256]{1,0:T(8,128)(2,1)S(1)}, u32[]{:S(2)}, u32[]{:S(2)}) collective-permute-start(bf16[256,256]{1,0:T(8,128)(2,1)S(1)} %get-tuple-element.123), channel_id=1, source_target_pairs={{0,6},{2,4},{4,2},{6,0},{8,14},{10,12},{12,10},{14,8},{16,22},{18,... | collective-permute-start | bytes 393224 | tf_op jit(solution)/shard_map/ppermute | solution.py:392
  30.2 5.8 %collective-permute-start.8 = (bf16[128,256]{1,0:T(8,128)(2,1)S(1)}, bf16[128,256]{1,0:T(8,128)(2,1)S(1)}, u32[]{:S(2)}, u32[]{:S(2)}) collective-permute-start(bf16[128,256]{1,0:T(8,128)(2,1)S(1)} %merged.3.refs_9_), channel_id=1, source_target_pairs={{0,16},{2,18},{4,20},{6,22},{8,24},{10,26},{12,28},{14,30},{16,0},... | collective-permute-start | bytes 196616 | tf_op jit(solution)/shard_map/ppermute | solution.py:698
  32.4 10.6 %collective-permute-start.14 = (bf16[256,256]{1,0:T(8,128)(2,1)S(1)}, bf16[256,256]{1,0:T(8,128)(2,1)S(1)}, u32[]{:S(2)}, u32[]{:S(2)}) collective-permute-start(bf16[256,256]{1,0:T(8,128)(2,1)S(1)} %get-tuple-element.124), channel_id=1, source_target_pairs={{0,4},{2,6},{4,0},{6,2},{8,12},{10,14},{12,8},{14,10},{16,20},{18,... | collective-permute-start | bytes 393224 | tf_op jit(solution)/shard_map/ppermute | solution.py:392
  33.4 9.6 %collective-permute-start.15 = (bf16[256,256]{1,0:T(8,128)(2,1)S(1)}, bf16[256,256]{1,0:T(8,128)(2,1)S(1)}, u32[]{:S(2)}, u32[]{:S(2)}) collective-permute-start(bf16[256,256]{1,0:T(8,128)(2,1)S(1)} %get-tuple-element.125), channel_id=1, source_target_pairs={{0,2},{2,0},{4,6},{6,4},{8,10},{10,8},{12,14},{14,12},{16,18},{18,... | collective-permute-start | bytes 393224 | tf_op jit(solution)/shard_map/ppermute | solution.py:392
  36.4 7.7 %collective-permute-start.9 = (bf16[256,256]{1,0:T(8,128)(2,1)S(1)}, bf16[256,256]{1,0:T(8,128)(2,1)S(1)}, u32[]{:S(2)}, u32[]{:S(2)}) collective-permute-start(bf16[256,256]{1,0:T(8,128)(2,1)S(1)} %get-tuple-element.111), channel_id=1, source_target_pairs={{0,6},{2,4},{4,2},{6,0},{8,14},{10,12},{12,10},{14,8},{16,22},{18,... | collective-permute-start | bytes 393224 | tf_op jit(solution)/shard_map/ppermute | solution.py:392
  38.4 5.9 %collective-permute-start.10 = (bf16[256,256]{1,0:T(8,128)(2,1)S(1)}, bf16[256,256]{1,0:T(8,128)(2,1)S(1)}, u32[]{:S(2)}, u32[]{:S(2)}) collective-permute-start(bf16[256,256]{1,0:T(8,128)(2,1)S(1)} %get-tuple-element.112), channel_id=1, source_target_pairs={{0,4},{2,6},{4,0},{6,2},{8,12},{10,14},{12,8},{14,10},{16,20},{18,... | collective-permute-start | bytes 393224 | tf_op jit(solution)/shard_map/ppermute | solution.py:392
  39.4 5.0 %collective-permute-start.11 = (bf16[256,256]{1,0:T(8,128)(2,1)S(1)}, bf16[256,256]{1,0:T(8,128)(2,1)S(1)}, u32[]{:S(2)}, u32[]{:S(2)}) collective-permute-start(bf16[256,256]{1,0:T(8,128)(2,1)S(1)} %get-tuple-element.113), channel_id=1, source_target_pairs={{0,2},{2,0},{4,6},{6,4},{8,10},{10,8},{12,14},{14,12},{16,18},{18,... | collective-permute-start | bytes 393224 | tf_op jit(solution)/shard_map/ppermute | solution.py:392
  45.0 1.5 %collective-permute-start.16 = (bf16[768,128]{1,0:T(8,128)(2,1)S(1)}, bf16[768,128]{1,0:T(8,128)(2,1)S(1)}, u32[]{:S(2)}, u32[]{:S(2)}) collective-permute-start(bf16[768,128]{1,0:T(8,128)(2,1)S(1)} %entry_parts.3), channel_id=1, source_target_pairs={{0,1},{1,0},{2,3},{3,2},{4,5},{5,4},{6,7},{7,6},{8,9},{9,8},{10,11... | collective-permute-start | bytes 589832 | tf_op jit(solution)/shard_map/ppermute | solution.py:675

commit v14 on v13

--- a/solution.py
+++ b/solution.py
@@ -535,7 +535,7 @@
             dc_out[rows_of(mid, hi, piece), :] += dc[rows_of(g, g + 1, n_right * piece), :]
 
 
-def inner_terms(head_dim, worked, setup, b, c, x, dy, before, after):
+def inner_terms(head_dim, worked, setup, b, c, x, dy, before, after, hides=True):
     (length, state), width = b.shape, x.shape[1]
     part = width // (GROUP * chunk_count(width))
     used = part * len(worked)
@@ -551,7 +551,7 @@
         + [pltpu.VMEM((left, used), BF16) for left, _ in sizes]
         + [pltpu.VMEM((right, used), BF16) for _, right in sizes],
         compiler_params=params(16),
-        cost_estimate=cost(8 * x.size * state, 4 * x.size, 2 * x.size),
+        cost_estimate=cost(8 * x.size * state, 4 * x.size, 2 * x.size) if hides else cost(1, 1),
         name="inner_terms",
     )(b, c, x, dy, *setup, *before, *after)
     return dict(zip(worked, found)), list(found[-2:])
@@ -698,22 +698,25 @@
         return lax.ppermute(block, "seq", [(s, s ^ (k * group)) for s in range(count)])
 
     every = [(chunk, m) for chunk in range(chunks) for m in range(group)]
-    worked = [every[:3]] + [every[chunk * group :][:2] for chunk in range(1, chunks)]
-    rest = [one for one in every if not any(one in some for some in worked)]
+    worked = [every[1:3]] + [every[chunk * group :][:2] for chunk in range(1, chunks)]
+    rest = [one for one in every[1:] if not any(one in some for some in worked)]
     entries, inner, sums = [], {}, []
 
-    def add_inner(some, after):
-        found, sums[:] = inner_terms(head_dim, some, setup, b, c, x, dy, sums, after)
+    def add_inner(some, after, hides=True):
+        found, sums[:] = inner_terms(head_dim, some, setup, b, c, x, dy, sums, after, hides)
         inner.update(found)
 
+    own = [totals(state, 0, where, blocks[0], setup[-1:])]
+    add_inner(every[:1], own[0], False)
+    own += [totals(state, 0, where, blocks[chunk], sums[:1]) for chunk in range(1, chunks)]
     for chunk in range(chunks):
-        (own,) = totals(state, 0, where, blocks[chunk], setup[-1:] if chunk == 0 else [])
-        received = [to_group(own, 1)]
+        (total,) = own[chunk]
+        received = [to_group(total, 1)]
         for level in range(levels - 1):
             last = level == levels - 2
-            own = merged(state, level, last, where, own, received[level], [])
-            received.append(to_group(own, 2 << level))
-        add_inner(worked[chunk], [own])
+            total = merged(state, level, last, where, total, received[level], [])
+            received.append(to_group(total, 2 << level))
+        add_inner(worked[chunk], [total])
         found = member_entries(state, False, where, blocks[chunk], received, sums[:1])
         entries.append(exchange(found))
     add_inner(rest, found[:1])

time: 47.4 us -> 47.4 us (level)
    ppermute x12, waiting for transfers between devices: 4.4 us -> 3 us  [exchange(): out[k] = lax.ppermute(parts[k], 'seq', [(s, s ^ k) for s in range(count)])]
    ppermute x4, waiting for transfers between devices: 0.18 us -> 1.19 us  [to_group(): lax.ppermute(block, 'seq', [(s, s ^ k * group) for s in range(count)])]
    ppermute x12, starting transfers between devices: 15.4 us -> 14.8 us  [exchange(): out[k] = lax.ppermute(parts[k], 'seq', [(s, s ^ k) for s in range(count)])]
    ppermute x4, starting transfers between devices: 8.23 us -> 8.86 us  [to_group(): lax.ppermute(block, 'seq', [(s, s ^ k * group) for s in range(count)])]
    pallas_call x3 -> x4, Pallas kernels: 8.24 us -> 8.6 us  [inner_terms(): pl.pallas_call(functools.partial(inner_kernel, head_dim, worked, len(befo...]
  transfers between devices with their start and end apart: 17 -> 17, of which waited for: 9 -> 8; matrix products, arithmetic and copies ran while one was open for 0% -> 0% of each run, Pallas kernels for 29% -> 30%
where the time goes in v14:
time: 47.4 us; the launch traced here: 47.2 us
  starting transfers between devices  23.7 us (50%)
  Pallas kernels  17.7 us (37%)
  waiting for transfers between devices  4.28 us (9%)
  between operations  0.82 us (2%)
  local copies, waits for them, and re-layouts  0.69 us (1%)
    ppermute x12, starting transfers between devices, exchange(): out[k] = lax.ppermute(parts[k], 'seq', [(s, s ^ k) for s in range(count)])  14.8 us
    ppermute x4, starting transfers between devices, to_group(): lax.ppermute(block, 'seq', [(s, s ^ k * group) for s in range(count)])  8.86 us
    pallas_call x4, Pallas kernels, inner_terms(): pl.pallas_call(functools.partial(inner_kernel, head_dim, worked, len(befo...  8.6 us
    ppermute x12, waiting for transfers between devices, exchange(): out[k] = lax.ppermute(parts[k], 'seq', [(s, s ^ k) for s in range(count)])  3 us
    pallas_call x1, Pallas kernels, first_states(): pl.pallas_call(functools.partial(first_states_kernel, head_dim, pieces),...  2.91 us
    pallas_call x1, Pallas kernels, next_states(): pl.pallas_call(functools.partial(next_states_kernel, head_dim, pieces), o...  1.93 us
    pallas_call x1, Pallas kernels, entry_values(): pl.pallas_call(functools.partial(last_values_kernel, chunks), out_shape=p...  1.33 us
    ppermute x4, waiting for transfers between devices, to_group(): lax.ppermute(block, 'seq', [(s, s ^ k * group) for s in range(count)])  1.19 us
  transfers between devices with their start and end apart: 17, of which 8 were waited for; matrix products, arithmetic and copies ran while one was open for 0% of the time, Pallas kernels for 30%

profile of v14, /device:TPU:0, one launch (start us, length us, event | category | flops | bytes accessed | tf_op | source)
XLA Modules:
  0.0 47.2 jit_solution(8087924113785091716)
XLA Ops:
  0.6 2.9 %first_states.1 = (f32[32,384]{1,0:T(8,128)S(1)}, bf16[384,128]{1,0:T(8,128)(2,1)S(1)}, bf16[384,128]{1,0:T(8,128)(2,1)S(1)}, bf16[384,2048]{1,0:T(8,128)(2,1)S(...) custom-call(s32[1]{0:T(128)} %bitcast.where, ...), custom_call_target="tpu_custom_call" | custom-call | flops 402653184 | bytes 6291456 | tf_op jit(solution)/shard_map/first_states/pallas_call | solution.py:187
  3.6 4.0 %collective-permute-start = (bf16[272,256]{1,0:T(8,128)(2,1)S(1)}, bf16[272,256]{1,0:T(8,128)(2,1)S(1)}, u32[]{:S(2)}, u32[]{:S(2)}) collective-permute-start(bf16[272,256]{1,0:T(8,128)(2,1)S(1)} %get-tuple-element.93), channel_id=1, source_target_pairs={{0,6},{2,4},{4,2},{6,0},{8,14},{10,12},{12,10},{14,8},{16,22},{18,... | collective-permute-start | bytes 417800 | tf_op jit(solution)/shard_map/ppermute | solution.py:392
  7.5 0.5 %collective-permute-start.1 = (bf16[272,256]{1,0:T(8,128)(2,1)S(1)}, bf16[272,256]{1,0:T(8,128)(2,1)S(1)}, u32[]{:S(2)}, u32[]{:S(2)}) collective-permute-start(bf16[272,256]{1,0:T(8,128)(2,1)S(1)} %get-tuple-element.94), channel_id=1, source_target_pairs={{0,4},{2,6},{4,0},{6,2},{8,12},{10,14},{12,8},{14,10},{16,20},{18,... | collective-permute-start | bytes 417800 | tf_op jit(solution)/shard_map/ppermute | solution.py:392
  8.0 0.1 collective-permute-start.2
  8.2 1.9 %next_states.1 = (bf16[384,256]{1,0:T(8,128)(2,1)S(1)}, bf16[384,256]{1,0:T(8,128)(2,1)S(1)}, bf16[384,256]{1,0:T(8,128)(2,1)S(1)}, bf16[272,256]{1,0:T(8,128)(2...) custom-call(s32[1]{0:T(128)} %bitcast.where, ...), custom_call_target="tpu_custom_call" | custom-call | flops 402653184 | bytes 3145728 | tf_op jit(solution)/shard_map/next_states/pallas_call | solution.py:203
  10.1 2.9 %collective-permute-start.4 = (bf16[272,256]{1,0:T(8,128)(2,1)S(1)}, bf16[272,256]{1,0:T(8,128)(2,1)S(1)}, u32[]{:S(2)}, u32[]{:S(2)}) collective-permute-start(bf16[272,256]{1,0:T(8,128)(2,1)S(1)} %get-tuple-element.101), channel_id=1, source_target_pairs={{0,6},{2,4},{4,2},{6,0},{8,14},{10,12},{12,10},{14,8},{16,22},{18,... | collective-permute-start | bytes 417800 | tf_op jit(solution)/shard_map/ppermute | solution.py:392
  13.0 0.5 %collective-permute-start.5 = (bf16[272,256]{1,0:T(8,128)(2,1)S(1)}, bf16[272,256]{1,0:T(8,128)(2,1)S(1)}, u32[]{:S(2)}, u32[]{:S(2)}) collective-permute-start(bf16[272,256]{1,0:T(8,128)(2,1)S(1)} %get-tuple-element.102), channel_id=1, source_target_pairs={{0,4},{2,6},{4,0},{6,2},{8,12},{10,14},{12,8},{14,10},{16,20},{18,... | collective-permute-start | bytes 417800 | tf_op jit(solution)/shard_map/ppermute | solution.py:392
  13.5 0.0 collective-permute-done.refs_1_.refs_5_
  13.5 0.5 %collective-permute-start.6 = (bf16[272,256]{1,0:T(8,128)(2,1)S(1)}, bf16[272,256]{1,0:T(8,128)(2,1)S(1)}, u32[]{:S(2)}, u32[]{:S(2)}) collective-permute-start(bf16[272,256]{1,0:T(8,128)(2,1)S(1)} %get-tuple-element.103), channel_id=1, source_target_pairs={{0,2},{2,0},{4,6},{6,4},{8,10},{10,8},{12,14},{14,12},{16,18},{18,... | collective-permute-start | bytes 417800 | tf_op jit(solution)/shard_map/ppermute | solution.py:392
  14.0 0.5 inner_setup.1
  14.5 1.0 %collective-permute-done.1.refs_2_.refs_4_ = bf16[272,256]{1,0:T(8,128)(2,1)S(1)} collective-permute-done((bf16[272,256]{1,0:T(8,128)(2,1)S(1)}, bf16[272,256]{1,0:T(8,128)(2,1)S(1)}, u32[]{:S(2)}, u32[]{:S(2)}) %collective-permute-start.1) | collective-permute-done | bytes 139296 | tf_op jit(solution)/shard_map/ppermute | solution.py:392
  15.5 0.1 collective-permute-done.2.refs_3_
  15.6 0.1 totals.2.refs_7_.own
  15.7 1.8 %collective-permute-start.3 = (bf16[272,256]{1,0:T(8,128)(2,1)S(1)}, bf16[272,256]{1,0:T(8,128)(2,1)S(1)}, u32[]{:S(2)}, u32[]{:S(2)}) collective-permute-start(bf16[272,256]{1,0:T(8,128)(2,1)S(1)} %totals.2.refs_7_.own), channel_id=1, source_target_pairs={{0,8},{2,10},{4,12},{6,14},{8,0},{10,2},{12,4},{14,6},{16,24},{18,... | collective-permute-start | bytes 417800 | tf_op jit(solution)/shard_map/ppermute | solution.py:698
  17.5 1.4 %inner_terms.4 = (bf16[384,256]{1,0:T(8,128)(2,1)S(1)}, f32[384,128]{1,0:T(8,128)S(1)}, f32[384,128]{1,0:T(8,128)S(1)}) custom-call(bf16[384,128]{1,0:T(8,128)(2,1)S(1)} %get-tuple-element.76.refs_0_.b, bf16[384,128]{1,0:T(8,128)(2,1)S(1)} %get-tuple-element.77.refs_1_.c, bf16[384,2048]{1,0:T(8,128)(2,1)S(1)} %get-tuple-element.78.refs_2_.x, ...), custom_call_target="tpu_custom_call" | custom-call | flops 1 | bytes 1 | tf_op jit(solution)/shard_map/inner_terms/pallas_call | solution.py:544
  18.8 0.0 collective-permute-done.4.refs_1_.refs_5_
  18.9 1.3 %collective-permute-done.5.refs_2_.refs_4_ = bf16[272,256]{1,0:T(8,128)(2,1)S(1)} collective-permute-done((bf16[272,256]{1,0:T(8,128)(2,1)S(1)}, bf16[272,256]{1,0:T(8,128)(2,1)S(1)}, u32[]{:S(2)}, u32[]{:S(2)}) %collective-permute-start.5) | collective-permute-done | bytes 139296 | tf_op jit(solution)/shard_map/ppermute | solution.py:392
  20.1 0.3 collective-permute-done.6.refs_3_
  20.4 0.1 totals.3.own
  20.5 1.6 %collective-permute-start.7 = (bf16[272,256]{1,0:T(8,128)(2,1)S(1)}, bf16[272,256]{1,0:T(8,128)(2,1)S(1)}, u32[]{:S(2)}, u32[]{:S(2)}) collective-permute-start(bf16[272,256]{1,0:T(8,128)(2,1)S(1)} %totals.3.own), channel_id=1, source_target_pairs={{0,8},{2,10},{4,12},{6,14},{8,0},{10,2},{12,4},{14,6},{16,24},{18,... | collective-permute-start | bytes 417800 | tf_op jit(solution)/shard_map/ppermute | solution.py:698
  22.2 0.0 collective-permute-done.3.received.refs_0_
  22.2 2.6 %collective-permute-start.12 = (bf16[128,256]{1,0:T(8,128)(2,1)S(1)}, bf16[128,256]{1,0:T(8,128)(2,1)S(1)}, u32[]{:S(2)}, u32[]{:S(2)}) collective-permute-start(bf16[128,256]{1,0:T(8,128)(2,1)S(1)} %merged.2.refs_9_), channel_id=1, source_target_pairs={{0,16},{2,18},{4,20},{6,22},{8,24},{10,26},{12,28},{14,30},{16,0},... | collective-permute-start | bytes 196616 | tf_op jit(solution)/shard_map/ppermute | solution.py:698
  24.9 2.1 %inner_terms.5 = (bf16[384,256]{1,0:T(8,128)(2,1)S(1)}, bf16[384,256]{1,0:T(8,128)(2,1)S(1)}, f32[384,128]{1,0:T(8,128)S(1)}, f32[384,128]{1,0:T(8,128)S(1)}) custom-call(bf16[384,128]{1,0:T(8,128)(2,1)S(1)} %get-tuple-element.76.refs_0_.b, bf16[384,128]{1,0:T(8,128)(2,1)S(1)} %get-tuple-element.77.refs_1_.c, ...), custom_call_target="tpu_custom_call" | custom-call | flops 805306368 | bytes 3145728 | tf_op jit(solution)/shard_map/inner_terms/pallas_call | solution.py:544
  27.0 1.2 %collective-permute-done.12.refs_1_ = bf16[128,256]{1,0:T(8,128)(2,1)S(1)} collective-permute-done((bf16[128,256]{1,0:T(8,128)(2,1)S(1)}, bf16[128,256]{1,0:T(8,128)(2,1)S(1)}, u32[]{:S(2)}, u32[]{:S(2)}) %collective-permute-start.12) | collective-permute-done | bytes 65568 | tf_op jit(solution)/shard_map/ppermute | solution.py:698
  28.1 0.2 member_entries.3
  28.3 1.2 %collective-permute-start.13 = (bf16[256,256]{1,0:T(8,128)(2,1)S(1)}, bf16[256,256]{1,0:T(8,128)(2,1)S(1)}, u32[]{:S(2)}, u32[]{:S(2)}) collective-permute-start(bf16[256,256]{1,0:T(8,128)(2,1)S(1)} %get-tuple-element.127), channel_id=1, source_target_pairs={{0,6},{2,4},{4,2},{6,0},{8,14},{10,12},{12,10},{14,8},{16,22},{18,... | collective-permute-start | bytes 393224 | tf_op jit(solution)/shard_map/ppermute | solution.py:392
  29.6 2.8 %collective-permute-start.8 = (bf16[128,256]{1,0:T(8,128)(2,1)S(1)}, bf16[128,256]{1,0:T(8,128)(2,1)S(1)}, u32[]{:S(2)}, u32[]{:S(2)}) collective-permute-start(bf16[128,256]{1,0:T(8,128)(2,1)S(1)} %merged.3.refs_9_), channel_id=1, source_target_pairs={{0,16},{2,18},{4,20},{6,22},{8,24},{10,26},{12,28},{14,30},{16,0},... | collective-permute-start | bytes 196616 | tf_op jit(solution)/shard_map/ppermute | solution.py:698
  32.4 1.0 %collective-permute-start.14 = (bf16[256,256]{1,0:T(8,128)(2,1)S(1)}, bf16[256,256]{1,0:T(8,128)(2,1)S(1)}, u32[]{:S(2)}, u32[]{:S(2)}) collective-permute-start(bf16[256,256]{1,0:T(8,128)(2,1)S(1)} %get-tuple-element.128), channel_id=1, source_target_pairs={{0,4},{2,6},{4,0},{6,2},{8,12},{10,14},{12,8},{14,10},{16,20},{18,... | collective-permute-start | bytes 393224 | tf_op jit(solution)/shard_map/ppermute | solution.py:392
  33.4 0.5 %collective-permute-start.15 = (bf16[256,256]{1,0:T(8,128)(2,1)S(1)}, bf16[256,256]{1,0:T(8,128)(2,1)S(1)}, u32[]{:S(2)}, u32[]{:S(2)}) collective-permute-start(bf16[256,256]{1,0:T(8,128)(2,1)S(1)} %get-tuple-element.129), channel_id=1, source_target_pairs={{0,2},{2,0},{4,6},{6,4},{8,10},{10,8},{12,14},{14,12},{16,18},{18,... | collective-permute-start | bytes 393224 | tf_op jit(solution)/shard_map/ppermute | solution.py:392
  33.9 2.1 %inner_terms.6 = (bf16[384,256]{1,0:T(8,128)(2,1)S(1)}, bf16[384,256]{1,0:T(8,128)(2,1)S(1)}, f32[384,128]{1,0:T(8,128)S(1)}, f32[384,128]{1,0:T(8,128)S(1)}) custom-call(bf16[384,128]{1,0:T(8,128)(2,1)S(1)} %get-tuple-element.76.refs_0_.b, bf16[384,128]{1,0:T(8,128)(2,1)S(1)} %get-tuple-element.77.refs_1_.c, ...), custom_call_target="tpu_custom_call" | custom-call | flops 805306368 | bytes 3145728 | tf_op jit(solution)/shard_map/inner_terms/pallas_call | solution.py:544
  36.0 0.0 collective-permute-done.8.refs_1_
  36.0 0.4 member_entries.2
  36.4 2.1 %collective-permute-start.9 = (bf16[256,256]{1,0:T(8,128)(2,1)S(1)}, bf16[256,256]{1,0:T(8,128)(2,1)S(1)}, u32[]{:S(2)}, u32[]{:S(2)}) collective-permute-start(bf16[256,256]{1,0:T(8,128)(2,1)S(1)} %get-tuple-element.115), channel_id=1, source_target_pairs={{0,6},{2,4},{4,2},{6,0},{8,14},{10,12},{12,10},{14,8},{16,22},{18,... | collective-permute-start | bytes 393224 | tf_op jit(solution)/shard_map/ppermute | solution.py:392
  38.4 1.0 %collective-permute-start.10 = (bf16[256,256]{1,0:T(8,128)(2,1)S(1)}, bf16[256,256]{1,0:T(8,128)(2,1)S(1)}, u32[]{:S(2)}, u32[]{:S(2)}) collective-permute-start(bf16[256,256]{1,0:T(8,128)(2,1)S(1)} %get-tuple-element.116), channel_id=1, source_target_pairs={{0,4},{2,6},{4,0},{6,2},{8,12},{10,14},{12,8},{14,10},{16,20},{18,... | collective-permute-start | bytes 393224 | tf_op jit(solution)/shard_map/ppermute | solution.py:392
  39.4 0.0 collective-permute-done.13.refs_9_
  39.4 0.5 %collective-permute-start.11 = (bf16[256,256]{1,0:T(8,128)(2,1)S(1)}, bf16[256,256]{1,0:T(8,128)(2,1)S(1)}, u32[]{:S(2)}, u32[]{:S(2)}) collective-permute-start(bf16[256,256]{1,0:T(8,128)(2,1)S(1)} %get-tuple-element.117), channel_id=1, source_target_pairs={{0,2},{2,0},{4,6},{6,4},{8,10},{10,8},{12,14},{14,12},{16,18},{18,... | collective-permute-start | bytes 393224 | tf_op jit(solution)/shard_map/ppermute | solution.py:392
  39.9 3.1 %inner_terms.7 = (bf16[384,256]{1,0:T(8,128)(2,1)S(1)}, bf16[384,256]{1,0:T(8,128)(2,1)S(1)}, bf16[384,256]{1,0:T(8,128)(2,1)S(1)}, f32[384,128]{1,0:T(8,128)S(1)}, f32[384,128]{1,0:T(8,128)S(1)}) custom-call(bf16[384,128]{1,0:T(8,128)(2,1)S(1)} %get-tuple-element.76.refs_0_.b, bf16[384,128]{1,0:T(8,128)(2,1)S(1)} %get-tuple-element.77.refs_1_.c, ...), custom_call_target="tpu_custom_call" | custom-call | flops 805306368 | bytes 3145728 | tf_op jit(solution)/shard_map/inner_terms/pallas_call | solution.py:544
  43.0 0.0 collective-permute-done.14.refs_10_
  43.0 0.4 entry_values.1.refs_12_
  43.5 0.6 %entry_parts.2 = (f32[384,128]{1,0:T(8,128)S(1)}, f32[384,128]{1,0:T(8,128)S(1)}) custom-call(f32[384,128]{1,0:T(8,128)S(1)} %get-tuple-element.130.db_before, f32[384,128]{1,0:T(8,128)S(1)} %get-tuple-element.131.dc_before, bf16[384,256]{1,0:T(8,128)(2,1)S(1)} %get-tuple-element.84.refs_0_, bf16[384,256]{1,0:T(8,128)(2,1)S(1)} %get-tuple-element.132.refs_1_, ...), custom_call_target="tpu_custom_call" | custom-call | flops 100663296 | bytes 786432 | tf_op jit(solution)/shard_map/entry_parts/pallas_call | solution.py:580
  44.1 0.2 collective-permute-done.10.refs_10_
  44.3 0.1 collective-permute-done.11.refs_11_
  44.4 0.6 %entry_parts.3 = bf16[768,128]{1,0:T(8,128)(2,1)S(1)} custom-call(f32[384,128]{1,0:T(8,128)S(1)} %get-tuple-element.139.db_before, f32[384,128]{1,0:T(8,128)S(1)} %get-tuple-element.140.dc_before, bf16[384,256]{1,0:T(8,128)(2,1)S(1)} %get-tuple-element.141.refs_0_, bf16[384,256]{1,0:T(8,128)(2,1)S(1)} %get-tuple-element.142.refs_1_, ...), custom_call_target="tpu_custom_call" | custom-call | flops 100663296 | bytes 786432 | tf_op jit(solution)/shard_map/entry_parts/pallas_call | solution.py:580
  45.0 0.1 collective-permute-start.16
  45.1 1.3 %last_values.1 = bf16[384,2048]{1,0:T(8,128)(2,1)} custom-call(s32[1]{0:T(128)} %bitcast.where, bf16[384,128]{1,0:T(8,128)(2,1)S(1)} %get-tuple-element.76.refs_0_.b, bf16[384,256]{1,0:T(8,128)(2,1)S(1)} %get-tuple-element.104.refs_0_, bf16[384,256]{1,0:T(8,128)(2,1)S(1)} %get-tuple-element.105.refs_1_, bf16[384,256]{1,0:T(8,128)(2,1)S(1)} %get-tuple-element.109.refs_2_, ...), custom_call_target="tpu_custom_call" | custom-call | flops 100663296 | bytes 1572864 | tf_op jit(solution)/shard_map/last_values/pallas_call | solution.py:654
  46.4 0.1 collective-permute-done.16
  46.5 0.1 add_convert_fusion
  46.5 0.7 %fusion = (bf16[384,128]{1,0:T(8,128)(2,1)}, bf16[384,128]{1,0:T(8,128)(2,1)}) fusion(bf16[768,128]{1,0:T(8,128)(2,1)S(1)} %add_convert_fusion), kind=kLoop, calls=%fused_computation.1 | loop fusion | bytes 393216 | tf_op jit(solution)/shard_map/slice | solution.py:736
  (5 shorter events, 0.1 us)
Async XLA Ops:
  3.6 10.0 %collective-permute-start = (bf16[272,256]{1,0:T(8,128)(2,1)S(1)}, bf16[272,256]{1,0:T(8,128)(2,1)S(1)}, u32[]{:S(2)}, u32[]{:S(2)}) collective-permute-start(bf16[272,256]{1,0:T(8,128)(2,1)S(1)} %get-tuple-element.93), channel_id=1, source_target_pairs={{0,6},{2,4},{4,2},{6,0},{8,14},{10,12},{12,10},{14,8},{16,22},{18,... | collective-permute-start | bytes 417800 | tf_op jit(solution)/shard_map/ppermute | solution.py:392
  7.5 8.0 %collective-permute-start.1 = (bf16[272,256]{1,0:T(8,128)(2,1)S(1)}, bf16[272,256]{1,0:T(8,128)(2,1)S(1)}, u32[]{:S(2)}, u32[]{:S(2)}) collective-permute-start(bf16[272,256]{1,0:T(8,128)(2,1)S(1)} %get-tuple-element.94), channel_id=1, source_target_pairs={{0,4},{2,6},{4,0},{6,2},{8,12},{10,14},{12,8},{14,10},{16,20},{18,... | collective-permute-start | bytes 417800 | tf_op jit(solution)/shard_map/ppermute | solution.py:392
  8.0 7.6 %collective-permute-start.2 = (bf16[272,256]{1,0:T(8,128)(2,1)S(1)}, bf16[272,256]{1,0:T(8,128)(2,1)S(1)}, u32[]{:S(2)}, u32[]{:S(2)}) collective-permute-start(bf16[272,256]{1,0:T(8,128)(2,1)S(1)} %get-tuple-element.95), channel_id=1, source_target_pairs={{0,2},{2,0},{4,6},{6,4},{8,10},{10,8},{12,14},{14,12},{16,18},{18,... | collective-permute-start | bytes 417800 | tf_op jit(solution)/shard_map/ppermute | solution.py:392
  10.1 8.8 %collective-permute-start.4 = (bf16[272,256]{1,0:T(8,128)(2,1)S(1)}, bf16[272,256]{1,0:T(8,128)(2,1)S(1)}, u32[]{:S(2)}, u32[]{:S(2)}) collective-permute-start(bf16[272,256]{1,0:T(8,128)(2,1)S(1)} %get-tuple-element.101), channel_id=1, source_target_pairs={{0,6},{2,4},{4,2},{6,0},{8,14},{10,12},{12,10},{14,8},{16,22},{18,... | collective-permute-start | bytes 417800 | tf_op jit(solution)/shard_map/ppermute | solution.py:392
  13.0 7.1 %collective-permute-start.5 = (bf16[272,256]{1,0:T(8,128)(2,1)S(1)}, bf16[272,256]{1,0:T(8,128)(2,1)S(1)}, u32[]{:S(2)}, u32[]{:S(2)}) collective-permute-start(bf16[272,256]{1,0:T(8,128)(2,1)S(1)} %get-tuple-element.102), channel_id=1, source_target_pairs={{0,4},{2,6},{4,0},{6,2},{8,12},{10,14},{12,8},{14,10},{16,20},{18,... | collective-permute-start | bytes 417800 | tf_op jit(solution)/shard_map/ppermute | solution.py:392
  13.5 6.9 %collective-permute-start.6 = (bf16[272,256]{1,0:T(8,128)(2,1)S(1)}, bf16[272,256]{1,0:T(8,128)(2,1)S(1)}, u32[]{:S(2)}, u32[]{:S(2)}) collective-permute-start(bf16[272,256]{1,0:T(8,128)(2,1)S(1)} %get-tuple-element.103), channel_id=1, source_target_pairs={{0,2},{2,0},{4,6},{6,4},{8,10},{10,8},{12,14},{14,12},{16,18},{18,... | collective-permute-start | bytes 417800 | tf_op jit(solution)/shard_map/ppermute | solution.py:392
  15.7 6.5 %collective-permute-start.3 = (bf16[272,256]{1,0:T(8,128)(2,1)S(1)}, bf16[272,256]{1,0:T(8,128)(2,1)S(1)}, u32[]{:S(2)}, u32[]{:S(2)}) collective-permute-start(bf16[272,256]{1,0:T(8,128)(2,1)S(1)} %totals.2.refs_7_.own), channel_id=1, source_target_pairs={{0,8},{2,10},{4,12},{6,14},{8,0},{10,2},{12,4},{14,6},{16,24},{18,... | collective-permute-start | bytes 417800 | tf_op jit(solution)/shard_map/ppermute | solution.py:698
  20.5 9.0 %collective-permute-start.7 = (bf16[272,256]{1,0:T(8,128)(2,1)S(1)}, bf16[272,256]{1,0:T(8,128)(2,1)S(1)}, u32[]{:S(2)}, u32[]{:S(2)}) collective-permute-start(bf16[272,256]{1,0:T(8,128)(2,1)S(1)} %totals.3.own), channel_id=1, source_target_pairs={{0,8},{2,10},{4,12},{6,14},{8,0},{10,2},{12,4},{14,6},{16,24},{18,... | collective-permute-start | bytes 417800 | tf_op jit(solution)/shard_map/ppermute | solution.py:698
  22.2 5.9 %collective-permute-start.12 = (bf16[128,256]{1,0:T(8,128)(2,1)S(1)}, bf16[128,256]{1,0:T(8,128)(2,1)S(1)}, u32[]{:S(2)}, u32[]{:S(2)}) collective-permute-start(bf16[128,256]{1,0:T(8,128)(2,1)S(1)} %merged.2.refs_9_), channel_id=1, source_target_pairs={{0,16},{2,18},{4,20},{6,22},{8,24},{10,26},{12,28},{14,30},{16,0},... | collective-permute-start | bytes 196616 | tf_op jit(solution)/shard_map/ppermute | solution.py:698
  28.3 11.1 %collective-permute-start.13 = (bf16[256,256]{1,0:T(8,128)(2,1)S(1)}, bf16[256,256]{1,0:T(8,128)(2,1)S(1)}, u32[]{:S(2)}, u32[]{:S(2)}) collective-permute-start(bf16[256,256]{1,0:T(8,128)(2,1)S(1)} %get-tuple-element.127), channel_id=1, source_target_pairs={{0,6},{2,4},{4,2},{6,0},{8,14},{10,12},{12,10},{14,8},{16,22},{18,... | collective-permute-start | bytes 393224 | tf_op jit(solution)/shard_map/ppermute | solution.py:392
  29.6 6.4 %collective-permute-start.8 = (bf16[128,256]{1,0:T(8,128)(2,1)S(1)}, bf16[128,256]{1,0:T(8,128)(2,1)S(1)}, u32[]{:S(2)}, u32[]{:S(2)}) collective-permute-start(bf16[128,256]{1,0:T(8,128)(2,1)S(1)} %merged.3.refs_9_), channel_id=1, source_target_pairs={{0,16},{2,18},{4,20},{6,22},{8,24},{10,26},{12,28},{14,30},{16,0},... | collective-permute-start | bytes 196616 | tf_op jit(solution)/shard_map/ppermute | solution.py:698
  32.4 10.6 %collective-permute-start.14 = (bf16[256,256]{1,0:T(8,128)(2,1)S(1)}, bf16[256,256]{1,0:T(8,128)(2,1)S(1)}, u32[]{:S(2)}, u32[]{:S(2)}) collective-permute-start(bf16[256,256]{1,0:T(8,128)(2,1)S(1)} %get-tuple-element.128), channel_id=1, source_target_pairs={{0,4},{2,6},{4,0},{6,2},{8,12},{10,14},{12,8},{14,10},{16,20},{18,... | collective-permute-start | bytes 393224 | tf_op jit(solution)/shard_map/ppermute | solution.py:392
  33.4 9.6 %collective-permute-start.15 = (bf16[256,256]{1,0:T(8,128)(2,1)S(1)}, bf16[256,256]{1,0:T(8,128)(2,1)S(1)}, u32[]{:S(2)}, u32[]{:S(2)}) collective-permute-start(bf16[256,256]{1,0:T(8,128)(2,1)S(1)} %get-tuple-element.129), channel_id=1, source_target_pairs={{0,2},{2,0},{4,6},{6,4},{8,10},{10,8},{12,14},{14,12},{16,18},{18,... | collective-permute-start | bytes 393224 | tf_op jit(solution)/shard_map/ppermute | solution.py:392
  36.4 7.7 %collective-permute-start.9 = (bf16[256,256]{1,0:T(8,128)(2,1)S(1)}, bf16[256,256]{1,0:T(8,128)(2,1)S(1)}, u32[]{:S(2)}, u32[]{:S(2)}) collective-permute-start(bf16[256,256]{1,0:T(8,128)(2,1)S(1)} %get-tuple-element.115), channel_id=1, source_target_pairs={{0,6},{2,4},{4,2},{6,0},{8,14},{10,12},{12,10},{14,8},{16,22},{18,... | collective-permute-start | bytes 393224 | tf_op jit(solution)/shard_map/ppermute | solution.py:392
  38.4 5.9 %collective-permute-start.10 = (bf16[256,256]{1,0:T(8,128)(2,1)S(1)}, bf16[256,256]{1,0:T(8,128)(2,1)S(1)}, u32[]{:S(2)}, u32[]{:S(2)}) collective-permute-start(bf16[256,256]{1,0:T(8,128)(2,1)S(1)} %get-tuple-element.116), channel_id=1, source_target_pairs={{0,4},{2,6},{4,0},{6,2},{8,12},{10,14},{12,8},{14,10},{16,20},{18,... | collective-permute-start | bytes 393224 | tf_op jit(solution)/shard_map/ppermute | solution.py:392
  39.4 5.0 %collective-permute-start.11 = (bf16[256,256]{1,0:T(8,128)(2,1)S(1)}, bf16[256,256]{1,0:T(8,128)(2,1)S(1)}, u32[]{:S(2)}, u32[]{:S(2)}) collective-permute-start(bf16[256,256]{1,0:T(8,128)(2,1)S(1)} %get-tuple-element.117), channel_id=1, source_target_pairs={{0,2},{2,0},{4,6},{6,4},{8,10},{10,8},{12,14},{14,12},{16,18},{18,... | collective-permute-start | bytes 393224 | tf_op jit(solution)/shard_map/ppermute | solution.py:392
  45.0 1.5 %collective-permute-start.16 = (bf16[768,128]{1,0:T(8,128)(2,1)S(1)}, bf16[768,128]{1,0:T(8,128)(2,1)S(1)}, u32[]{:S(2)}, u32[]{:S(2)}) collective-permute-start(bf16[768,128]{1,0:T(8,128)(2,1)S(1)} %entry_parts.3), channel_id=1, source_target_pairs={{0,1},{1,0},{2,3},{3,2},{4,5},{5,4},{6,7},{7,6},{8,9},{9,8},{10,11... | collective-permute-start | bytes 589832 | tf_op jit(solution)/shard_map/ppermute | solution.py:675

commit v15 on v14

--- a/solution.py
+++ b/solution.py
@@ -146,10 +146,12 @@
     outs, sems = refs[8:-1], refs[-1]
     pairs = [(ld_in, ld), (b_in, b), (x_in, x), (c_in, c), (dy_in, dy)]
     copies = [pltpu.make_async_copy(i, o, sems.at[n]) for n, (i, o) in enumerate(pairs)]
-    for copy in copies:
+    for copy in copies[:3]:
         copy.start()
     masks = masks_of(ld.shape[1])
     copies[0].wait()
+    for copy in copies[3:]:
+        copy.start()
     factors = factors_of(ld[...], *masks)
     for ref, value in zip((into_end, from_start, halves), factors):
         ref[...] = value
@@ -557,14 +559,14 @@
     return dict(zip(worked, found)), list(found[-2:])
 
 
-def parts_kernel(last, db_before, dc_before, *refs):
-    scaled, refs = refs[: 2 * GROUP], refs[2 * GROUP :]
-    entries, outs = sent_order(refs[:GROUP]), refs[-1 if last else -2 :]
+def parts_kernel(last, ks, db_before, dc_before, *refs):
+    scaled, refs = refs[: 2 * len(ks)], refs[2 * len(ks) :]
+    entries, outs = refs[: len(ks)], refs[-1 if last else -2 :]
     length, state = db_before.shape
     db, dc = db_before[...], dc_before[...]
-    for k, entry in enumerate(entries):
-        db = db + dot(scaled[2 * k][...], entry[state:, :], NT)
-        dc = dc + dot(scaled[2 * k + 1][...], entry[:state, :], NT)
+    for n, entry in enumerate(entries):
+        db = db + dot(scaled[2 * n][...], entry[state:, :], NT)
+        dc = dc + dot(scaled[2 * n + 1][...], entry[:state, :], NT)
     if last:
         outs[0][:length, :] = db.astype(BF16)
         outs[0][length:, :] = dc.astype(BF16)
@@ -573,19 +575,20 @@
         outs[1][...] = dc
 
 
-def entry_parts(last, scaled, db_before, dc_before, entries, after):
+def entry_parts(last, ks, scaled, db_before, dc_before, entries, after):
     length, state = db_before.shape
     one = jax.ShapeDtypeStruct((length, state), F32)
     outs = [jax.ShapeDtypeStruct((2 * length, state), BF16)] if last else [one, one]
+    operands = [one for k in ks for one in scaled[k]] + [entries[k] for k in ks]
     return pl.pallas_call(
-        functools.partial(parts_kernel, last),
+        functools.partial(parts_kernel, last, ks),
         out_shape=outs,
-        in_specs=whole(2 + 3 * GROUP) + [ANY] * len(after),
+        in_specs=whole(2 + len(operands)) + [ANY] * len(after),
         out_specs=whole(len(outs)),
         compiler_params=params(8),
-        cost_estimate=cost(8 * scaled[0].size * state, 8 * scaled[0].size),
+        cost_estimate=cost(2 * len(operands) * scaled[0][0].size * state, scaled[0][0].size),
         name="entry_parts",
-    )(db_before, dc_before, *scaled, *sent_order(entries), *after)
+    )(db_before, dc_before, *operands, *after)
 
 
 def put_values(where, spread, b, local_parts, dx_local, entries, put):
@@ -667,18 +670,36 @@
     )(*operands, *before)
 
 
+def sum_kernel(*refs):
+    parts, (db, dc) = refs[:-2], refs[-2:]
+    length = db.shape[0]
+    for out, rows in ((db, slice(0, length)), (dc, slice(length, 2 * length))):
+        total = parts[0][rows, :].astype(F32)
+        for part in parts[1:]:
+            total = total + part[rows, :].astype(F32)
+        out[...] = total.astype(BF16)
+
+
 def over_heads(part):
-    count = lax.axis_size("head")
-    total = part.astype(F32)
+    count, (rows, state) = lax.axis_size("head"), part.shape
+    parts = [part]
     for shift in range(1, count):
         pairs = [(s, (s + shift) % count) for s in range(count)]
-        total = total + lax.ppermute(part, "head", pairs).astype(F32)
-    return total.astype(BF16)
+        parts.append(lax.ppermute(part, "head", pairs))
+    return pl.pallas_call(
+        sum_kernel,
+        out_shape=[jax.ShapeDtypeStruct((rows // 2, state), BF16)] * 2,
+        in_specs=whole(count),
+        out_specs=whole(2),
+        compiler_params=params(4),
+        cost_estimate=cost(count * part.size, 2 * count * part.size),
+        name="sum_over_heads",
+    )(*parts)
 
 
 def shards(token_values, b_inputs, c_inputs, log_decay, grad_out):
     head_dim = token_values.shape[1] // log_decay.shape[0]
-    length, state = b_inputs.shape
+    state = b_inputs.shape[1]
     count, group = lax.axis_size("seq"), GROUP
     chunks = chunk_count(token_values.shape[1])
     levels = (count // group).bit_length() - 1
@@ -698,7 +719,7 @@
         return lax.ppermute(block, "seq", [(s, s ^ (k * group)) for s in range(count)])
 
     every = [(chunk, m) for chunk in range(chunks) for m in range(group)]
-    worked = [every[1:3]] + [every[chunk * group :][:2] for chunk in range(1, chunks)]
+    worked = [every[1:4]] + [every[chunk * group :][:2] for chunk in range(1, chunks)]
     rest = [one for one in every[1:] if not any(one in some for some in worked)]
     entries, inner, sums = [], {}, []
 
@@ -719,21 +740,24 @@
         add_inner(worked[chunk], [total])
         found = member_entries(state, False, where, blocks[chunk], received, sums[:1])
         entries.append(exchange(found))
-    add_inner(rest, found[:1])
+    if rest:
+        add_inner(rest, found[:1])
 
     values = []
     for chunk in range(chunks):
         last = chunk == chunks - 1
         ours = [states[chunk, k] for k in range(group)]
-        scaled = [one for k in range(group) for one in ours[k][:2]]
+        scaled = [one[:2] for one in ours]
         spread = [one[2] for one in ours]
-        sums = entry_parts(last, scaled, *sums, entries[chunk], values)
+        if last:
+            sums = entry_parts(False, (0, 3), scaled, *sums, entries[chunk], values)
+        ks = (2, 1) if last else (0, 3, 2, 1)
+        sums = entry_parts(last, ks, scaled, *sums, entries[chunk], [])
         local = [inner[chunk, m] for m in range(group)]
         values.append(
             entry_values(chunk, chunks, where, spread, b, local, entries[chunk], values)
         )
-    both = over_heads(sums[0])
-    return values[-1], both[:length], both[length:]
+    return (values[-1], *over_heads(sums[0]))
 
 
 def solution(mesh):

time: 47.4 us -> 47.7 us (level)
  Pallas kernels: 17.7 us -> 19.1 us
  local copies, waits for them, and re-layouts: 0.69 us -> 0 us
    ppermute x4, waiting for transfers between devices: 1.19 us -> 0.19 us  [to_group(): lax.ppermute(block, 'seq', [(s, s ^ k * group) for s in range(count)])]
    pallas_call x2 -> x4, Pallas kernels: 1.14 us -> 1.99 us  [the longest x3 1.29 us: entry_parts(): pl.pallas_call(functools.partial(parts_kernel, last, ks), out_shape=outs,...]
    slice x1 -> x0, local copies, waits for them, and re-layouts: 0.69 us -> none  [shards(): return (values[-1], both[:length], both[length:])]
    ppermute x12, starting transfers between devices: 14.8 us -> 15.4 us  [exchange(): out[k] = lax.ppermute(parts[k], 'seq', [(s, s ^ k) for s in range(count)])]
    ppermute x12, waiting for transfers between devices: 3 us -> 3.62 us  [exchange(): out[k] = lax.ppermute(parts[k], 'seq', [(s, s ^ k) for s in range(count)])]
    ppermute x4, starting transfers between devices: 8.86 us -> 8.24 us  [to_group(): lax.ppermute(block, 'seq', [(s, s ^ k * group) for s in range(count)])]
    pallas_call x1, Pallas kernels: 2.91 us -> 3.48 us  [first_states(): pl.pallas_call(functools.partial(first_states_kernel, head_dim, pieces),...]
  transfers between devices with their start and end apart: 17 -> 17, of which waited for: 8 -> 9; matrix products, arithmetic and copies ran while one was open for 0% -> 0% of each run, Pallas kernels for 30% -> 31%
where the time goes in v15:
time: 47.7 us; the launch traced here: 47.6 us
  starting transfers between devices  23.7 us (50%)
  Pallas kernels  19.1 us (40%)
  waiting for transfers between devices  3.9 us (8%)
  between operations  0.82 us (2%)
    ppermute x12, starting transfers between devices, exchange(): out[k] = lax.ppermute(parts[k], 'seq', [(s, s ^ k) for s in range(count)])  15.4 us
    pallas_call x4, Pallas kernels, inner_terms(): pl.pallas_call(functools.partial(inner_kernel, head_dim, worked, len(befo...  8.6 us
    ppermute x4, starting transfers between devices, to_group(): lax.ppermute(block, 'seq', [(s, s ^ k * group) for s in range(count)])  8.24 us
    ppermute x12, waiting for transfers between devices, exchange(): out[k] = lax.ppermute(parts[k], 'seq', [(s, s ^ k) for s in range(count)])  3.62 us
    pallas_call x1, Pallas kernels, first_states(): pl.pallas_call(functools.partial(first_states_kernel, head_dim, pieces),...  3.48 us
    pallas_call x1, Pallas kernels, next_states(): pl.pallas_call(functools.partial(next_states_kernel, head_dim, pieces), o...  1.93 us
    pallas_call x1, Pallas kernels, entry_values(): pl.pallas_call(functools.partial(last_values_kernel, chunks), out_shape=p...  1.33 us
    pallas_call x3, Pallas kernels, entry_parts(): pl.pallas_call(functools.partial(parts_kernel, last, ks), out_shape=outs,...  1.29 us
  transfers between devices with their start and end apart: 17, of which 9 were waited for; matrix products, arithmetic and copies ran while one was open for 0% of the time, Pallas kernels for 31%

profile of v15, /device:TPU:0, one launch (start us, length us, event | category | flops | bytes accessed | tf_op | source)
XLA Modules:
  0.0 47.6 jit_solution(9613859770684821042)
XLA Ops:
  0.6 3.5 %first_states.1 = (f32[32,384]{1,0:T(8,128)S(1)}, bf16[384,128]{1,0:T(8,128)(2,1)S(1)}, bf16[384,128]{1,0:T(8,128)(2,1)S(1)}, bf16[384,2048]{1,0:T(8,128)(2,1)S(...) custom-call(s32[1]{0:T(128)} %bitcast.where, ...), custom_call_target="tpu_custom_call" | custom-call | flops 402653184 | bytes 6291456 | tf_op jit(solution)/shard_map/first_states/pallas_call | solution.py:189
  4.1 4.0 %collective-permute-start = (bf16[272,256]{1,0:T(8,128)(2,1)S(1)}, bf16[272,256]{1,0:T(8,128)(2,1)S(1)}, u32[]{:S(2)}, u32[]{:S(2)}) collective-permute-start(bf16[272,256]{1,0:T(8,128)(2,1)S(1)} %get-tuple-element.97), channel_id=1, source_target_pairs={{0,6},{2,4},{4,2},{6,0},{8,14},{10,12},{12,10},{14,8},{16,22},{18,... | collective-permute-start | bytes 417800 | tf_op jit(solution)/shard_map/ppermute | solution.py:394
  8.1 0.5 %collective-permute-start.1 = (bf16[272,256]{1,0:T(8,128)(2,1)S(1)}, bf16[272,256]{1,0:T(8,128)(2,1)S(1)}, u32[]{:S(2)}, u32[]{:S(2)}) collective-permute-start(bf16[272,256]{1,0:T(8,128)(2,1)S(1)} %get-tuple-element.98), channel_id=1, source_target_pairs={{0,4},{2,6},{4,0},{6,2},{8,12},{10,14},{12,8},{14,10},{16,20},{18,... | collective-permute-start | bytes 417800 | tf_op jit(solution)/shard_map/ppermute | solution.py:394
  8.6 0.1 collective-permute-start.2
  8.7 1.9 %next_states.1 = (bf16[384,256]{1,0:T(8,128)(2,1)S(1)}, bf16[384,256]{1,0:T(8,128)(2,1)S(1)}, bf16[384,256]{1,0:T(8,128)(2,1)S(1)}, bf16[272,256]{1,0:T(8,128)(2...) custom-call(s32[1]{0:T(128)} %bitcast.where, ...), custom_call_target="tpu_custom_call" | custom-call | flops 402653184 | bytes 3145728 | tf_op jit(solution)/shard_map/next_states/pallas_call | solution.py:205
  10.7 2.9 %collective-permute-start.4 = (bf16[272,256]{1,0:T(8,128)(2,1)S(1)}, bf16[272,256]{1,0:T(8,128)(2,1)S(1)}, u32[]{:S(2)}, u32[]{:S(2)}) collective-permute-start(bf16[272,256]{1,0:T(8,128)(2,1)S(1)} %get-tuple-element.105), channel_id=1, source_target_pairs={{0,6},{2,4},{4,2},{6,0},{8,14},{10,12},{12,10},{14,8},{16,22},{18,... | collective-permute-start | bytes 417800 | tf_op jit(solution)/shard_map/ppermute | solution.py:394
  13.6 0.5 %collective-permute-start.5 = (bf16[272,256]{1,0:T(8,128)(2,1)S(1)}, bf16[272,256]{1,0:T(8,128)(2,1)S(1)}, u32[]{:S(2)}, u32[]{:S(2)}) collective-permute-start(bf16[272,256]{1,0:T(8,128)(2,1)S(1)} %get-tuple-element.106), channel_id=1, source_target_pairs={{0,4},{2,6},{4,0},{6,2},{8,12},{10,14},{12,8},{14,10},{16,20},{18,... | collective-permute-start | bytes 417800 | tf_op jit(solution)/shard_map/ppermute | solution.py:394
  14.1 0.0 collective-permute-done.refs_1_.refs_5_
  14.1 0.5 %collective-permute-start.6 = (bf16[272,256]{1,0:T(8,128)(2,1)S(1)}, bf16[272,256]{1,0:T(8,128)(2,1)S(1)}, u32[]{:S(2)}, u32[]{:S(2)}) collective-permute-start(bf16[272,256]{1,0:T(8,128)(2,1)S(1)} %get-tuple-element.107), channel_id=1, source_target_pairs={{0,2},{2,0},{4,6},{6,4},{8,10},{10,8},{12,14},{14,12},{16,18},{18,... | collective-permute-start | bytes 417800 | tf_op jit(solution)/shard_map/ppermute | solution.py:394
  14.6 0.5 inner_setup.1
  15.1 1.0 %collective-permute-done.1.refs_2_.refs_4_ = bf16[272,256]{1,0:T(8,128)(2,1)S(1)} collective-permute-done((bf16[272,256]{1,0:T(8,128)(2,1)S(1)}, bf16[272,256]{1,0:T(8,128)(2,1)S(1)}, u32[]{:S(2)}, u32[]{:S(2)}) %collective-permute-start.1) | collective-permute-done | bytes 139296 | tf_op jit(solution)/shard_map/ppermute | solution.py:394
  16.1 0.1 collective-permute-done.2.refs_3_
  16.2 0.1 totals.2.refs_7_.own
  16.3 1.8 %collective-permute-start.3 = (bf16[272,256]{1,0:T(8,128)(2,1)S(1)}, bf16[272,256]{1,0:T(8,128)(2,1)S(1)}, u32[]{:S(2)}, u32[]{:S(2)}) collective-permute-start(bf16[272,256]{1,0:T(8,128)(2,1)S(1)} %totals.2.refs_7_.own), channel_id=1, source_target_pairs={{0,8},{2,10},{4,12},{6,14},{8,0},{10,2},{12,4},{14,6},{16,24},{18,... | collective-permute-start | bytes 417800 | tf_op jit(solution)/shard_map/ppermute | solution.py:719
  18.1 1.4 %inner_terms.4 = (bf16[384,256]{1,0:T(8,128)(2,1)S(1)}, f32[384,128]{1,0:T(8,128)S(1)}, f32[384,128]{1,0:T(8,128)S(1)}) custom-call(bf16[384,128]{1,0:T(8,128)(2,1)S(1)} %get-tuple-element.80.refs_0_.b, bf16[384,128]{1,0:T(8,128)(2,1)S(1)} %get-tuple-element.81.refs_1_.c, bf16[384,2048]{1,0:T(8,128)(2,1)S(1)} %get-tuple-element.82.refs_2_.x, ...), custom_call_target="tpu_custom_call" | custom-call | flops 1 | bytes 1 | tf_op jit(solution)/shard_map/inner_terms/pallas_call | solution.py:546
  19.4 0.0 collective-permute-done.4.refs_1_.refs_5_
  19.4 1.3 %collective-permute-done.5.refs_2_.refs_4_ = bf16[272,256]{1,0:T(8,128)(2,1)S(1)} collective-permute-done((bf16[272,256]{1,0:T(8,128)(2,1)S(1)}, bf16[272,256]{1,0:T(8,128)(2,1)S(1)}, u32[]{:S(2)}, u32[]{:S(2)}) %collective-permute-start.5) | collective-permute-done | bytes 139296 | tf_op jit(solution)/shard_map/ppermute | solution.py:394
  20.7 0.3 collective-permute-done.6.refs_3_
  21.0 0.1 totals.3.own
  21.1 1.6 %collective-permute-start.7 = (bf16[272,256]{1,0:T(8,128)(2,1)S(1)}, bf16[272,256]{1,0:T(8,128)(2,1)S(1)}, u32[]{:S(2)}, u32[]{:S(2)}) collective-permute-start(bf16[272,256]{1,0:T(8,128)(2,1)S(1)} %totals.3.own), channel_id=1, source_target_pairs={{0,8},{2,10},{4,12},{6,14},{8,0},{10,2},{12,4},{14,6},{16,24},{18,... | collective-permute-start | bytes 417800 | tf_op jit(solution)/shard_map/ppermute | solution.py:719
  22.7 0.0 collective-permute-done.3.received.refs_0_
  22.8 2.6 %collective-permute-start.12 = (bf16[128,256]{1,0:T(8,128)(2,1)S(1)}, bf16[128,256]{1,0:T(8,128)(2,1)S(1)}, u32[]{:S(2)}, u32[]{:S(2)}) collective-permute-start(bf16[128,256]{1,0:T(8,128)(2,1)S(1)} %merged.2.refs_9_), channel_id=1, source_target_pairs={{0,16},{2,18},{4,20},{6,22},{8,24},{10,26},{12,28},{14,30},{16,0},... | collective-permute-start | bytes 196616 | tf_op jit(solution)/shard_map/ppermute | solution.py:719
  25.4 3.1 %inner_terms.5 = (bf16[384,256]{1,0:T(8,128)(2,1)S(1)}, bf16[384,256]{1,0:T(8,128)(2,1)S(1)}, bf16[384,256]{1,0:T(8,128)(2,1)S(1)}, f32[384,128]{1,0:T(8,128)S(1)}, f32[384,128]{1,0:T(8,128)S(1)}) custom-call(bf16[384,128]{1,0:T(8,128)(2,1)S(1)} %get-tuple-element.80.refs_0_.b, bf16[384,128]{1,0:T(8,128)(2,1)S(1)} %get-tuple-element.81.refs_1_.c, ...), custom_call_target="tpu_custom_call" | custom-call | flops 805306368 | bytes 3145728 | tf_op jit(solution)/shard_map/inner_terms/pallas_call | solution.py:546
  28.5 0.2 collective-permute-done.12.refs_1_
  28.7 0.2 member_entries.3
  28.9 1.8 %collective-permute-start.13 = (bf16[256,256]{1,0:T(8,128)(2,1)S(1)}, bf16[256,256]{1,0:T(8,128)(2,1)S(1)}, u32[]{:S(2)}, u32[]{:S(2)}) collective-permute-start(bf16[256,256]{1,0:T(8,128)(2,1)S(1)} %get-tuple-element.131), channel_id=1, source_target_pairs={{0,6},{2,4},{4,2},{6,0},{8,14},{10,12},{12,10},{14,8},{16,22},{18,... | collective-permute-start | bytes 393224 | tf_op jit(solution)/shard_map/ppermute | solution.py:394
  30.7 0.0 collective-permute-done.7.received.refs_0_
  30.8 2.2 %collective-permute-start.8 = (bf16[128,256]{1,0:T(8,128)(2,1)S(1)}, bf16[128,256]{1,0:T(8,128)(2,1)S(1)}, u32[]{:S(2)}, u32[]{:S(2)}) collective-permute-start(bf16[128,256]{1,0:T(8,128)(2,1)S(1)} %merged.3.refs_9_), channel_id=1, source_target_pairs={{0,16},{2,18},{4,20},{6,22},{8,24},{10,26},{12,28},{14,30},{16,0},... | collective-permute-start | bytes 196616 | tf_op jit(solution)/shard_map/ppermute | solution.py:719
  33.0 1.0 %collective-permute-start.14 = (bf16[256,256]{1,0:T(8,128)(2,1)S(1)}, bf16[256,256]{1,0:T(8,128)(2,1)S(1)}, u32[]{:S(2)}, u32[]{:S(2)}) collective-permute-start(bf16[256,256]{1,0:T(8,128)(2,1)S(1)} %get-tuple-element.132), channel_id=1, source_target_pairs={{0,4},{2,6},{4,0},{6,2},{8,12},{10,14},{12,8},{14,10},{16,20},{18,... | collective-permute-start | bytes 393224 | tf_op jit(solution)/shard_map/ppermute | solution.py:394
  34.0 0.5 %collective-permute-start.15 = (bf16[256,256]{1,0:T(8,128)(2,1)S(1)}, bf16[256,256]{1,0:T(8,128)(2,1)S(1)}, u32[]{:S(2)}, u32[]{:S(2)}) collective-permute-start(bf16[256,256]{1,0:T(8,128)(2,1)S(1)} %get-tuple-element.133), channel_id=1, source_target_pairs={{0,2},{2,0},{4,6},{6,4},{8,10},{10,8},{12,14},{14,12},{16,18},{18,... | collective-permute-start | bytes 393224 | tf_op jit(solution)/shard_map/ppermute | solution.py:394
  34.5 2.1 %inner_terms.6 = (bf16[384,256]{1,0:T(8,128)(2,1)S(1)}, bf16[384,256]{1,0:T(8,128)(2,1)S(1)}, f32[384,128]{1,0:T(8,128)S(1)}, f32[384,128]{1,0:T(8,128)S(1)}) custom-call(bf16[384,128]{1,0:T(8,128)(2,1)S(1)} %get-tuple-element.80.refs_0_.b, bf16[384,128]{1,0:T(8,128)(2,1)S(1)} %get-tuple-element.81.refs_1_.c, ...), custom_call_target="tpu_custom_call" | custom-call | flops 805306368 | bytes 3145728 | tf_op jit(solution)/shard_map/inner_terms/pallas_call | solution.py:546
  36.6 0.4 member_entries.2
  36.9 2.1 %collective-permute-start.9 = (bf16[256,256]{1,0:T(8,128)(2,1)S(1)}, bf16[256,256]{1,0:T(8,128)(2,1)S(1)}, u32[]{:S(2)}, u32[]{:S(2)}) collective-permute-start(bf16[256,256]{1,0:T(8,128)(2,1)S(1)} %get-tuple-element.119), channel_id=1, source_target_pairs={{0,6},{2,4},{4,2},{6,0},{8,14},{10,12},{12,10},{14,8},{16,22},{18,... | collective-permute-start | bytes 393224 | tf_op jit(solution)/shard_map/ppermute | solution.py:394
  39.0 1.0 %collective-permute-start.10 = (bf16[256,256]{1,0:T(8,128)(2,1)S(1)}, bf16[256,256]{1,0:T(8,128)(2,1)S(1)}, u32[]{:S(2)}, u32[]{:S(2)}) collective-permute-start(bf16[256,256]{1,0:T(8,128)(2,1)S(1)} %get-tuple-element.120), channel_id=1, source_target_pairs={{0,4},{2,6},{4,0},{6,2},{8,12},{10,14},{12,8},{14,10},{16,20},{18,... | collective-permute-start | bytes 393224 | tf_op jit(solution)/shard_map/ppermute | solution.py:394
  40.0 0.5 %collective-permute-start.11 = (bf16[256,256]{1,0:T(8,128)(2,1)S(1)}, bf16[256,256]{1,0:T(8,128)(2,1)S(1)}, u32[]{:S(2)}, u32[]{:S(2)}) collective-permute-start(bf16[256,256]{1,0:T(8,128)(2,1)S(1)} %get-tuple-element.121), channel_id=1, source_target_pairs={{0,2},{2,0},{4,6},{6,4},{8,10},{10,8},{12,14},{14,12},{16,18},{18,... | collective-permute-start | bytes 393224 | tf_op jit(solution)/shard_map/ppermute | solution.py:394
  40.5 2.1 %inner_terms.7 = (bf16[384,256]{1,0:T(8,128)(2,1)S(1)}, bf16[384,256]{1,0:T(8,128)(2,1)S(1)}, f32[384,128]{1,0:T(8,128)S(1)}, f32[384,128]{1,0:T(8,128)S(1)}) custom-call(bf16[384,128]{1,0:T(8,128)(2,1)S(1)} %get-tuple-element.80.refs_0_.b, bf16[384,128]{1,0:T(8,128)(2,1)S(1)} %get-tuple-element.81.refs_1_.c, ...), custom_call_target="tpu_custom_call" | custom-call | flops 805306368 | bytes 3145728 | tf_op jit(solution)/shard_map/inner_terms/pallas_call | solution.py:546
  42.6 0.0 collective-permute-done.14.refs_10_
  42.6 0.4 entry_values.1.refs_12_.refs_6_
  43.0 0.6 %entry_parts.3 = (f32[384,128]{1,0:T(8,128)S(1)}, f32[384,128]{1,0:T(8,128)S(1)}) custom-call(f32[384,128]{1,0:T(8,128)S(1)} %get-tuple-element.134.db_before, f32[384,128]{1,0:T(8,128)S(1)} %get-tuple-element.135.dc_before, bf16[384,256]{1,0:T(8,128)(2,1)S(1)} %get-tuple-element.88.refs_0_, bf16[384,256]{1,0:T(8,128)(2,1)S(1)} %get-tuple-element.136.refs_1_, ...), custom_call_target="tpu_custom_call" | custom-call | flops 301989888 | bytes 98304 | tf_op jit(solution)/shard_map/entry_parts/pallas_call | solution.py:583
  43.6 0.1 collective-permute-done.9.refs_9_.refs_5_
  43.7 0.4 entry_parts.4
  44.1 0.8 %collective-permute-done.10.refs_10_.refs_4_ = bf16[256,256]{1,0:T(8,128)(2,1)S(1)} collective-permute-done((bf16[256,256]{1,0:T(8,128)(2,1)S(1)}, bf16[256,256]{1,0:T(8,128)(2,1)S(1)}, u32[]{:S(2)}, u32[]{:S(2)}) %collective-permute-start.10) | collective-permute-done | bytes 131104 | tf_op jit(solution)/shard_map/ppermute | solution.py:394
  44.9 0.1 collective-permute-done.11.refs_11_.refs_5_
  45.0 0.4 entry_parts.5.refs_0_
  45.4 0.1 collective-permute-start.16
  45.4 1.3 %last_values.1 = bf16[384,2048]{1,0:T(8,128)(2,1)} custom-call(s32[1]{0:T(128)} %bitcast.where, bf16[384,128]{1,0:T(8,128)(2,1)S(1)} %get-tuple-element.80.refs_0_.b, bf16[384,256]{1,0:T(8,128)(2,1)S(1)} %get-tuple-element.108.refs_0_, bf16[384,256]{1,0:T(8,128)(2,1)S(1)} %get-tuple-element.109.refs_1_, bf16[384,256]{1,0:T(8,128)(2,1)S(1)} %get-tuple-element.113.refs_2_, ...), custom_call_target="tpu_custom_call" | custom-call | flops 100663296 | bytes 1572864 | tf_op jit(solution)/shard_map/last_values/pallas_call | solution.py:657
  46.8 0.1 collective-permute-done.16.refs_1_
  46.9 0.7 %sum_over_heads.1 = (bf16[384,128]{1,0:T(8,128)(2,1)}, bf16[384,128]{1,0:T(8,128)(2,1)}) custom-call(bf16[768,128]{1,0:T(8,128)(2,1)S(1)} %entry_parts.5.refs_0_, bf16[768,128]{1,0:T(8,128)(2,1)S(1)} %collective-permute-done.16.refs_1_), custom_call_target="tpu_custom_call" | custom-call | flops 196608 | bytes 393216 | tf_op jit(solution)/shard_map/sum_over_heads/pallas_call | solution.py:689
  (5 shorter events, 0.1 us)
Async XLA Ops:
  4.1 10.0 %collective-permute-start = (bf16[272,256]{1,0:T(8,128)(2,1)S(1)}, bf16[272,256]{1,0:T(8,128)(2,1)S(1)}, u32[]{:S(2)}, u32[]{:S(2)}) collective-permute-start(bf16[272,256]{1,0:T(8,128)(2,1)S(1)} %get-tuple-element.97), channel_id=1, source_target_pairs={{0,6},{2,4},{4,2},{6,0},{8,14},{10,12},{12,10},{14,8},{16,22},{18,... | collective-permute-start | bytes 417800 | tf_op jit(solution)/shard_map/ppermute | solution.py:394
  8.1 8.0 %collective-permute-start.1 = (bf16[272,256]{1,0:T(8,128)(2,1)S(1)}, bf16[272,256]{1,0:T(8,128)(2,1)S(1)}, u32[]{:S(2)}, u32[]{:S(2)}) collective-permute-start(bf16[272,256]{1,0:T(8,128)(2,1)S(1)} %get-tuple-element.98), channel_id=1, source_target_pairs={{0,4},{2,6},{4,0},{6,2},{8,12},{10,14},{12,8},{14,10},{16,20},{18,... | collective-permute-start | bytes 417800 | tf_op jit(solution)/shard_map/ppermute | solution.py:394
  8.6 7.6 %collective-permute-start.2 = (bf16[272,256]{1,0:T(8,128)(2,1)S(1)}, bf16[272,256]{1,0:T(8,128)(2,1)S(1)}, u32[]{:S(2)}, u32[]{:S(2)}) collective-permute-start(bf16[272,256]{1,0:T(8,128)(2,1)S(1)} %get-tuple-element.99), channel_id=1, source_target_pairs={{0,2},{2,0},{4,6},{6,4},{8,10},{10,8},{12,14},{14,12},{16,18},{18,... | collective-permute-start | bytes 417800 | tf_op jit(solution)/shard_map/ppermute | solution.py:394
  10.7 8.8 %collective-permute-start.4 = (bf16[272,256]{1,0:T(8,128)(2,1)S(1)}, bf16[272,256]{1,0:T(8,128)(2,1)S(1)}, u32[]{:S(2)}, u32[]{:S(2)}) collective-permute-start(bf16[272,256]{1,0:T(8,128)(2,1)S(1)} %get-tuple-element.105), channel_id=1, source_target_pairs={{0,6},{2,4},{4,2},{6,0},{8,14},{10,12},{12,10},{14,8},{16,22},{18,... | collective-permute-start | bytes 417800 | tf_op jit(solution)/shard_map/ppermute | solution.py:394
  13.6 7.1 %collective-permute-start.5 = (bf16[272,256]{1,0:T(8,128)(2,1)S(1)}, bf16[272,256]{1,0:T(8,128)(2,1)S(1)}, u32[]{:S(2)}, u32[]{:S(2)}) collective-permute-start(bf16[272,256]{1,0:T(8,128)(2,1)S(1)} %get-tuple-element.106), channel_id=1, source_target_pairs={{0,4},{2,6},{4,0},{6,2},{8,12},{10,14},{12,8},{14,10},{16,20},{18,... | collective-permute-start | bytes 417800 | tf_op jit(solution)/shard_map/ppermute | solution.py:394
  14.1 6.9 %collective-permute-start.6 = (bf16[272,256]{1,0:T(8,128)(2,1)S(1)}, bf16[272,256]{1,0:T(8,128)(2,1)S(1)}, u32[]{:S(2)}, u32[]{:S(2)}) collective-permute-start(bf16[272,256]{1,0:T(8,128)(2,1)S(1)} %get-tuple-element.107), channel_id=1, source_target_pairs={{0,2},{2,0},{4,6},{6,4},{8,10},{10,8},{12,14},{14,12},{16,18},{18,... | collective-permute-start | bytes 417800 | tf_op jit(solution)/shard_map/ppermute | solution.py:394
  16.3 6.5 %collective-permute-start.3 = (bf16[272,256]{1,0:T(8,128)(2,1)S(1)}, bf16[272,256]{1,0:T(8,128)(2,1)S(1)}, u32[]{:S(2)}, u32[]{:S(2)}) collective-permute-start(bf16[272,256]{1,0:T(8,128)(2,1)S(1)} %totals.2.refs_7_.own), channel_id=1, source_target_pairs={{0,8},{2,10},{4,12},{6,14},{8,0},{10,2},{12,4},{14,6},{16,24},{18,... | collective-permute-start | bytes 417800 | tf_op jit(solution)/shard_map/ppermute | solution.py:719
  21.1 9.6 %collective-permute-start.7 = (bf16[272,256]{1,0:T(8,128)(2,1)S(1)}, bf16[272,256]{1,0:T(8,128)(2,1)S(1)}, u32[]{:S(2)}, u32[]{:S(2)}) collective-permute-start(bf16[272,256]{1,0:T(8,128)(2,1)S(1)} %totals.3.own), channel_id=1, source_target_pairs={{0,8},{2,10},{4,12},{6,14},{8,0},{10,2},{12,4},{14,6},{16,24},{18,... | collective-permute-start | bytes 417800 | tf_op jit(solution)/shard_map/ppermute | solution.py:719
  22.8 5.9 %collective-permute-start.12 = (bf16[128,256]{1,0:T(8,128)(2,1)S(1)}, bf16[128,256]{1,0:T(8,128)(2,1)S(1)}, u32[]{:S(2)}, u32[]{:S(2)}) collective-permute-start(bf16[128,256]{1,0:T(8,128)(2,1)S(1)} %merged.2.refs_9_), channel_id=1, source_target_pairs={{0,16},{2,18},{4,20},{6,22},{8,24},{10,26},{12,28},{14,30},{16,0},... | collective-permute-start | bytes 196616 | tf_op jit(solution)/shard_map/ppermute | solution.py:719
  28.9 11.1 %collective-permute-start.13 = (bf16[256,256]{1,0:T(8,128)(2,1)S(1)}, bf16[256,256]{1,0:T(8,128)(2,1)S(1)}, u32[]{:S(2)}, u32[]{:S(2)}) collective-permute-start(bf16[256,256]{1,0:T(8,128)(2,1)S(1)} %get-tuple-element.131), channel_id=1, source_target_pairs={{0,6},{2,4},{4,2},{6,0},{8,14},{10,12},{12,10},{14,8},{16,22},{18,... | collective-permute-start | bytes 393224 | tf_op jit(solution)/shard_map/ppermute | solution.py:394
  30.8 5.8 %collective-permute-start.8 = (bf16[128,256]{1,0:T(8,128)(2,1)S(1)}, bf16[128,256]{1,0:T(8,128)(2,1)S(1)}, u32[]{:S(2)}, u32[]{:S(2)}) collective-permute-start(bf16[128,256]{1,0:T(8,128)(2,1)S(1)} %merged.3.refs_9_), channel_id=1, source_target_pairs={{0,16},{2,18},{4,20},{6,22},{8,24},{10,26},{12,28},{14,30},{16,0},... | collective-permute-start | bytes 196616 | tf_op jit(solution)/shard_map/ppermute | solution.py:719
  33.0 9.6 %collective-permute-start.14 = (bf16[256,256]{1,0:T(8,128)(2,1)S(1)}, bf16[256,256]{1,0:T(8,128)(2,1)S(1)}, u32[]{:S(2)}, u32[]{:S(2)}) collective-permute-start(bf16[256,256]{1,0:T(8,128)(2,1)S(1)} %get-tuple-element.132), channel_id=1, source_target_pairs={{0,4},{2,6},{4,0},{6,2},{8,12},{10,14},{12,8},{14,10},{16,20},{18,... | collective-permute-start | bytes 393224 | tf_op jit(solution)/shard_map/ppermute | solution.py:394
  34.0 8.6 %collective-permute-start.15 = (bf16[256,256]{1,0:T(8,128)(2,1)S(1)}, bf16[256,256]{1,0:T(8,128)(2,1)S(1)}, u32[]{:S(2)}, u32[]{:S(2)}) collective-permute-start(bf16[256,256]{1,0:T(8,128)(2,1)S(1)} %get-tuple-element.133), channel_id=1, source_target_pairs={{0,2},{2,0},{4,6},{6,4},{8,10},{10,8},{12,14},{14,12},{16,18},{18,... | collective-permute-start | bytes 393224 | tf_op jit(solution)/shard_map/ppermute | solution.py:394
  36.9 6.8 %collective-permute-start.9 = (bf16[256,256]{1,0:T(8,128)(2,1)S(1)}, bf16[256,256]{1,0:T(8,128)(2,1)S(1)}, u32[]{:S(2)}, u32[]{:S(2)}) collective-permute-start(bf16[256,256]{1,0:T(8,128)(2,1)S(1)} %get-tuple-element.119), channel_id=1, source_target_pairs={{0,6},{2,4},{4,2},{6,0},{8,14},{10,12},{12,10},{14,8},{16,22},{18,... | collective-permute-start | bytes 393224 | tf_op jit(solution)/shard_map/ppermute | solution.py:394
  39.0 5.9 %collective-permute-start.10 = (bf16[256,256]{1,0:T(8,128)(2,1)S(1)}, bf16[256,256]{1,0:T(8,128)(2,1)S(1)}, u32[]{:S(2)}, u32[]{:S(2)}) collective-permute-start(bf16[256,256]{1,0:T(8,128)(2,1)S(1)} %get-tuple-element.120), channel_id=1, source_target_pairs={{0,4},{2,6},{4,0},{6,2},{8,12},{10,14},{12,8},{14,10},{16,20},{18,... | collective-permute-start | bytes 393224 | tf_op jit(solution)/shard_map/ppermute | solution.py:394
  40.0 5.0 %collective-permute-start.11 = (bf16[256,256]{1,0:T(8,128)(2,1)S(1)}, bf16[256,256]{1,0:T(8,128)(2,1)S(1)}, u32[]{:S(2)}, u32[]{:S(2)}) collective-permute-start(bf16[256,256]{1,0:T(8,128)(2,1)S(1)} %get-tuple-element.121), channel_id=1, source_target_pairs={{0,2},{2,0},{4,6},{6,4},{8,10},{10,8},{12,14},{14,12},{16,18},{18,... | collective-permute-start | bytes 393224 | tf_op jit(solution)/shard_map/ppermute | solution.py:394
  45.4 1.5 %collective-permute-start.16 = (bf16[768,128]{1,0:T(8,128)(2,1)S(1)}, bf16[768,128]{1,0:T(8,128)(2,1)S(1)}, u32[]{:S(2)}, u32[]{:S(2)}) collective-permute-start(bf16[768,128]{1,0:T(8,128)(2,1)S(1)} %entry_parts.5.refs_0_), channel_id=1, source_target_pairs={{0,1},{1,0},{2,3},{3,2},{4,5},{5,4},{6,7},{7,6},{8,9},{9,8},{10,11... | collective-permute-start | bytes 589832 | tf_op jit(solution)/shard_map/ppermute | solution.py:688

commit v16 on v15

--- a/solution.py
+++ b/solution.py
@@ -118,55 +118,87 @@
     return into_end, from_start, halves
 
 
-def put_states(head_dim, pieces, where, operands, outs, ready):
-    into_end, from_start, halves, b, c, x, dy = operands
-    state, width = b.shape[1], x.shape[1]
-    chunks = chunk_count(width)
-    part = width // (GROUP * chunks)
+def put_states(head_dim, chunks, pieces, where, operands, outs, ready):
+    into_end, from_start, halves, b, c, xs, dys = operands
+    state, part = b.shape[1], xs[0].shape[1] // GROUP
     difference = row_less_head(head_dim, part)
-    for side, (factors, proj, cols) in enumerate([(into_end, b, x), (from_start, c, dy)]):
-        ready(side)
-        turned = proj[...].T
+    for side, (factors, proj, cols) in enumerate([(into_end, b, xs), (from_start, c, dys)]):
+        turned = None
         for n, (chunk, k) in enumerate(pieces):
+            if n == 0 or chunk != pieces[n - 1][0]:
+                ready(side, chunk)
+            if turned is None:
+                turned = proj[...].T
             x_scaled, dy_scaled, spread, send = outs[4 * n : 4 * n + 4]
-            lanes = chunk_lanes(where, k, chunk, part, width)
-            first_head = ((place_of(where) ^ k) * chunks + chunk) * (part // head_dim)
+            member = place_of(where) ^ k
+            first_head = (member * chunks + chunk) * (part // head_dim)
             hot = head_of_lane(difference, first_head)
             wide = dot(factors, hot, NN).astype(BF16)
             if side == 0:
                 spread[...] = wide
                 send[2 * state :, :] = dot(halves, hot, NN).astype(BF16)
-            piece = cols[:, lanes] * wide
+            lanes = pl.ds(pl.multiple_of(member * part, part), part)
+            piece = cols[chunk][:, lanes] * wide
             (dy_scaled if side else x_scaled)[...] = piece
             send[side * state : (side + 1) * state, :] = dot(turned, piece, NN).astype(BF16)
 
 
-def first_states_kernel(head_dim, pieces, where, ld_in, b_in, c_in, x_in, dy_in, *refs):
+def load_chunk(chunk, chunks, source, target, sems, first):
+    part = target.shape[1] // GROUP
+    copies = []
+    for m in range(GROUP):
+        lanes = pl.ds((m * chunks + chunk) * part, part)
+        at = target.at[:, pl.ds(m * part, part)]
+        copies.append(pltpu.make_async_copy(source.at[:, lanes], at, sems.at[first + m]))
+        copies[-1].start()
+    return copies
+
+
+def first_states_kernel(head_dim, chunks, pieces, where, ld_in, b_in, c_in, x_in, dy_in, *refs):
     ld, b, c, x, dy, into_end, from_start, halves = refs[:8]
     outs, sems = refs[8:-1], refs[-1]
-    pairs = [(ld_in, ld), (b_in, b), (x_in, x), (c_in, c), (dy_in, dy)]
-    copies = [pltpu.make_async_copy(i, o, sems.at[n]) for n, (i, o) in enumerate(pairs)]
-    for copy in copies[:3]:
+
+    def load(n, source, target):
+        copy = pltpu.make_async_copy(source, target, sems.at[n])
         copy.start()
+        return copy
+
+    first = load(0, ld_in, ld)
+    copies = [
+        [load(1, b_in, b), *load_chunk(0, chunks, x_in, x, sems, 3)],
+        [load(2, c_in, c), *load_chunk(0, chunks, dy_in, dy, sems, 3 + GROUP)],
+    ]
     masks = masks_of(ld.shape[1])
-    copies[0].wait()
-    for copy in copies[3:]:
-        copy.start()
+    first.wait()
     factors = factors_of(ld[...], *masks)
     for ref, value in zip((into_end, from_start, halves), factors):
         ref[...] = value
 
-    def ready(side):
-        copies[1 + 2 * side].wait()
-        copies[2 + 2 * side].wait()
-
-    put_states(head_dim, pieces, where, (*factors, b, c, x, dy), outs, ready)
-
-
-def next_states_kernel(head_dim, pieces, where, into_end, from_start, halves, *refs):
-    operands = (into_end[...], from_start[...], halves[...], *refs[:4])
-    outs = refs[-4 * len(pieces) :]
-    put_states(head_dim, pieces, where, operands, outs, lambda side: None)
+    def ready(side, chunk):
+        for copy in copies[side]:
+            copy.wait()
+
+    operands = (*factors, b, c, {0: x}, {0: dy})
+    put_states(head_dim, chunks, pieces, where, operands, outs, ready)
+
+
+def next_states_kernel(head_dim, chunks, pieces, where, into_end, from_start, halves, *refs):
+    b, c, x, dy, x_in, dy_in = refs[:6]
+    outs, sems = refs[6:-1], refs[-1]
+    kept, outs = outs[: 2 * (chunks - 1)], outs[2 * (chunks - 1) :]
+    xs, dys, copies = {0: x}, {0: dy}, {}
+    for chunk in range(1, chunks):
+        xs[chunk], dys[chunk] = kept[2 * chunk - 2 : 2 * chunk]
+        at = 2 * GROUP * (chunk - 1)
+        copies[0, chunk] = load_chunk(chunk, chunks, x_in, xs[chunk], sems, at)
+        copies[1, chunk] = load_chunk(chunk, chunks, dy_in, dys[chunk], sems, at + GROUP)
+
+    def ready(side, chunk):
+        for copy in copies.get((side, chunk), []):
+            copy.wait()
+
+    operands = (into_end[...], from_start[...], halves[...], b, c, xs, dys)
+    put_states(head_dim, chunks, pieces, where, operands, outs, ready)
 
 
 def states_shapes(n_parts, length, width, state):
@@ -183,15 +215,17 @@
 def first_states(head_dim, pieces, where, inputs):
     ld, b, c, x, dy = inputs
     (length, width), state = x.shape, b.shape[1]
-    kept = [jax.ShapeDtypeStruct(a.shape, a.dtype) for a in inputs]
+    chunks = chunk_count(width)
+    columns = jax.ShapeDtypeStruct((length, width // chunks), BF16)
+    kept = [jax.ShapeDtypeStruct(a.shape, a.dtype) for a in (ld, b, c)] + [columns] * 2
     kept += [jax.ShapeDtypeStruct((rows, LANES), BF16) for rows in (length, length, TAIL)]
     outs = kept + states_shapes(len(pieces), length, width, state)
     found = pl.pallas_call(
-        functools.partial(first_states_kernel, head_dim, pieces),
+        functools.partial(first_states_kernel, head_dim, chunks, pieces),
         out_shape=outs,
         in_specs=[SMEM] + [HBM] * 5,
         out_specs=whole(len(outs)),
-        scratch_shapes=[pltpu.SemaphoreType.DMA((5,))],
+        scratch_shapes=[pltpu.SemaphoreType.DMA((3 + 2 * GROUP,))],
         compiler_params=params(8),
         cost_estimate=cost(2 * length * width * (state + LANES), 8 * length * width),
         name="first_states",
@@ -199,19 +233,23 @@
     return found[:8], by_piece(pieces, found[8:])
 
 
-def next_states(head_dim, pieces, where, factors, b, c, x, dy):
+def next_states(head_dim, pieces, where, factors, b, c, x_0, dy_0, x, dy):
     (length, width), state = x.shape, b.shape[1]
-    outs = states_shapes(len(pieces), length, width, state)
+    chunks = chunk_count(width)
+    n_kept = 2 * (chunks - 1)
+    outs = [jax.ShapeDtypeStruct(x_0.shape, BF16)] * n_kept
+    outs += states_shapes(len(pieces), length, width, state)
     found = pl.pallas_call(
-        functools.partial(next_states_kernel, head_dim, pieces),
+        functools.partial(next_states_kernel, head_dim, chunks, pieces),
         out_shape=outs,
-        in_specs=[SMEM] + whole(7),
+        in_specs=[SMEM] + whole(7) + [HBM] * 2,
         out_specs=whole(len(outs)),
+        scratch_shapes=[pltpu.SemaphoreType.DMA((max(n_kept, 1) * GROUP,))],
         compiler_params=params(8),
         cost_estimate=cost(2 * length * width * (state + LANES), 4 * length * width),
         name="next_states",
-    )(where, *factors, b, c, x, dy)
-    return by_piece(pieces, found)
+    )(where, *factors, b, c, x_0, dy_0, *in_hbm(x, dy))
+    return found[:n_kept], by_piece(pieces, found[n_kept:])
 
 
 def decay_of(tail):
@@ -462,8 +500,9 @@
     setup_kernel(piece, ld, b, c, *refs[n_after:])
 
 
-def inner_kernel(head_dim, worked, n_before, n_after, b, c, x, dy, *refs):
-    length, width = x.shape
+def inner_kernel(head_dim, worked, chunks, n_before, n_after, b, c, *refs):
+    xs, dys, refs = refs[:chunks], refs[chunks : 2 * chunks], refs[2 * chunks :]
+    length, width = xs[0].shape
     piece = head_dim
     pieces = length // piece
     groups = grouped_cuts(pieces)
@@ -476,9 +515,9 @@
     difference = row_less_head(head_dim, part, SLOT)
 
     for at, (chunk, m) in enumerate(worked):
-        owned = m * (width // GROUP) + chunk * part
-        lanes, here = slice(owned, owned + part), slice(at * part, (at + 1) * part)
-        cum = dot(cum_terms[...], head_of_lane(difference, owned // head_dim), NN)
+        x, dy, first_head = xs[chunk], dys[chunk], (m * chunks + chunk) * (part // head_dim)
+        lanes, here = slice(m * part, (m + 1) * part), slice(at * part, (at + 1) * part)
+        cum = dot(cum_terms[...], head_of_lane(difference, first_head), NN)
         dx = []
         for n in range(pieces):
             rows = rows_of(n, n + 1, piece)
@@ -537,25 +576,25 @@
             dc_out[rows_of(mid, hi, piece), :] += dc[rows_of(g, g + 1, n_right * piece), :]
 
 
-def inner_terms(head_dim, worked, setup, b, c, x, dy, before, after, hides=True):
-    (length, state), width = b.shape, x.shape[1]
-    part = width // (GROUP * chunk_count(width))
+def inner_terms(head_dim, worked, setup, b, c, xs, dys, before, after, hides=True):
+    (length, state), columns, chunks = b.shape, xs[0].size, len(xs)
+    part = xs[0].shape[1] // GROUP
     used = part * len(worked)
     groups = grouped_cuts(length // head_dim)
     sizes = [[len(same) * n * head_dim for n in halves] for halves, same in groups]
     found = pl.pallas_call(
-        functools.partial(inner_kernel, head_dim, worked, len(before), len(after)),
+        functools.partial(inner_kernel, head_dim, worked, chunks, len(before), len(after)),
         out_shape=[jax.ShapeDtypeStruct((length, part), BF16)] * len(worked)
         + [jax.ShapeDtypeStruct((length, state), F32)] * 2,
-        in_specs=whole(4 + len(setup) + len(before)) + [ANY] * len(after),
+        in_specs=whole(2 + 2 * chunks + len(setup) + len(before)) + [ANY] * len(after),
         out_specs=whole(len(worked) + 2),
         scratch_shapes=[pltpu.VMEM((length, used), BF16)] * 2
         + [pltpu.VMEM((left, used), BF16) for left, _ in sizes]
         + [pltpu.VMEM((right, used), BF16) for _, right in sizes],
         compiler_params=params(16),
-        cost_estimate=cost(8 * x.size * state, 4 * x.size, 2 * x.size) if hides else cost(1, 1),
+        cost_estimate=cost(16 * columns * state, 8 * columns, 4 * columns) if hides else cost(1, 1),
         name="inner_terms",
-    )(b, c, x, dy, *setup, *before, *after)
+    )(b, c, *xs, *dys, *setup, *before, *after)
     return dict(zip(worked, found)), list(found[-2:])
 
 
@@ -707,9 +746,12 @@
     inputs = (log_decay, b_inputs, c_inputs, token_values, grad_out)
     order = [(chunk, k) for chunk in range(chunks) for k in range(group - 1, -1, -1)]
     kept, states = first_states(head_dim, order[: group - 1], where, inputs)
-    ld, b, c, x, dy, *factors = kept
-    late = order[group:] + order[group - 1 : group]
-    states.update(next_states(head_dim, late, where, factors, b, c, x, dy))
+    ld, b, c, x_0, dy_0, *factors = kept
+    late = order[group - 1 :]
+    columns = (x_0, dy_0, token_values, grad_out)
+    more, found = next_states(head_dim, late, where, factors, b, c, *columns)
+    states.update(found)
+    xs, dys = [x_0, *more[::2]], [dy_0, *more[1::2]]
     blocks = [
         exchange([states[chunk, k][3] for k in range(group)]) for chunk in range(chunks)
     ]
@@ -724,7 +766,7 @@
     entries, inner, sums = [], {}, []
 
     def add_inner(some, after, hides=True):
-        found, sums[:] = inner_terms(head_dim, some, setup, b, c, x, dy, sums, after, hides)
+        found, sums[:] = inner_terms(head_dim, some, setup, b, c, xs, dys, sums, after, hides)
         inner.update(found)
 
     own = [totals(state, 0, where, blocks[0], setup[-1:])]

time: 47.7 us -> 47.2 us (0.990)
  waiting for transfers between devices: 3.9 us -> 2.46 us
  Pallas kernels: 19.1 us -> 19.9 us
    ppermute x12, waiting for transfers between devices: 3.62 us -> 2.35 us  [exchange(): out[k] = lax.ppermute(parts[k], 'seq', [(s, s ^ k) for s in range(count)])]
    pallas_call x6, Pallas kernels: 14 us -> 14.8 us  [the longest x4 8.61 us: inner_terms(): pl.pallas_call(functools.partial(inner_kernel, head_dim, worked, chunks,...]
  transfers between devices with their start and end apart: 17 -> 17, of which waited for: 9 -> 5; matrix products, arithmetic and copies ran while one was open for 0% -> 0% of each run, Pallas kernels for 31% -> 34%
where the time goes in v16:
time: 47.2 us; the launch traced here: 47 us
  starting transfers between devices  23.8 us (50%)
  Pallas kernels  19.9 us (42%)
  waiting for transfers between devices  2.46 us (5%)
  between operations  0.84 us (2%)
    ppermute x12, starting transfers between devices, exchange(): out[k] = lax.ppermute(parts[k], 'seq', [(s, s ^ k) for s in range(count)])  15.2 us
    pallas_call x4, Pallas kernels, inner_terms(): pl.pallas_call(functools.partial(inner_kernel, head_dim, worked, chunks,...  8.61 us
    ppermute x4, starting transfers between devices, to_group(): lax.ppermute(block, 'seq', [(s, s ^ k * group) for s in range(count)])  8.55 us
    pallas_call x1, Pallas kernels, next_states(): pl.pallas_call(functools.partial(next_states_kernel, head_dim, chunks, pi...  3.5 us
    pallas_call x1, Pallas kernels, first_states(): pl.pallas_call(functools.partial(first_states_kernel, head_dim, chunks, p...  2.73 us
    ppermute x12, waiting for transfers between devices, exchange(): out[k] = lax.ppermute(parts[k], 'seq', [(s, s ^ k) for s in range(count)])  2.35 us
    pallas_call x1, Pallas kernels, entry_values(): pl.pallas_call(functools.partial(last_values_kernel, chunks), out_shape=p...  1.33 us
    pallas_call x3, Pallas kernels, entry_parts(): pl.pallas_call(functools.partial(parts_kernel, last, ks), out_shape=outs,...  1.29 us
  transfers between devices with their start and end apart: 17, of which 5 were waited for; matrix products, arithmetic and copies ran while one was open for 0% of the time, Pallas kernels for 34%

profile of v16, /device:TPU:0, one launch (start us, length us, event | category | flops | bytes accessed | tf_op | source)
XLA Modules:
  0.0 47.0 jit_solution(7981322358902998101)
XLA Ops:
  0.6 2.7 %first_states.1 = (f32[32,384]{1,0:T(8,128)S(1)}, bf16[384,128]{1,0:T(8,128)(2,1)S(1)}, bf16[384,128]{1,0:T(8,128)(2,1)S(1)}, bf16[384,1024]{1,0:T(8,128)(2,1)S(...) custom-call(s32[1]{0:T(128)} %bitcast.where, ...), custom_call_target="tpu_custom_call" | custom-call | flops 402653184 | bytes 6291456 | tf_op jit(solution)/shard_map/first_states/pallas_call | solution.py:223
  3.4 4.0 %collective-permute-start = (bf16[272,256]{1,0:T(8,128)(2,1)S(1)}, bf16[272,256]{1,0:T(8,128)(2,1)S(1)}, u32[]{:S(2)}, u32[]{:S(2)}) collective-permute-start(bf16[272,256]{1,0:T(8,128)(2,1)S(1)} %get-tuple-element.101), channel_id=1, source_target_pairs={{0,6},{2,4},{4,2},{6,0},{8,14},{10,12},{12,10},{14,8},{16,22},{18,... | collective-permute-start | bytes 417800 | tf_op jit(solution)/shard_map/ppermute | solution.py:432
  7.3 0.5 %collective-permute-start.1 = (bf16[272,256]{1,0:T(8,128)(2,1)S(1)}, bf16[272,256]{1,0:T(8,128)(2,1)S(1)}, u32[]{:S(2)}, u32[]{:S(2)}) collective-permute-start(bf16[272,256]{1,0:T(8,128)(2,1)S(1)} %get-tuple-element.102), channel_id=1, source_target_pairs={{0,4},{2,6},{4,0},{6,2},{8,12},{10,14},{12,8},{14,10},{16,20},{18,... | collective-permute-start | bytes 417800 | tf_op jit(solution)/shard_map/ppermute | solution.py:432
  7.8 0.1 collective-permute-start.2
  8.0 3.5 %next_states.1 = (bf16[384,1024]{1,0:T(8,128)(2,1)S(1)}, bf16[384,1024]{1,0:T(8,128)(2,1)S(1)}, bf16[384,256]{1,0:T(8,128)(2,1)S(1)}, bf16[384,256]{1,0:T(8,128)...) custom-call(s32[1]{0:T(128)} %bitcast.where, ...), custom_call_target="tpu_custom_call" | custom-call | flops 402653184 | bytes 3145728 | tf_op jit(solution)/shard_map/next_states/pallas_call | solution.py:242
  11.5 2.9 %collective-permute-start.4 = (bf16[272,256]{1,0:T(8,128)(2,1)S(1)}, bf16[272,256]{1,0:T(8,128)(2,1)S(1)}, u32[]{:S(2)}, u32[]{:S(2)}) collective-permute-start(bf16[272,256]{1,0:T(8,128)(2,1)S(1)} %get-tuple-element.109), channel_id=1, source_target_pairs={{0,6},{2,4},{4,2},{6,0},{8,14},{10,12},{12,10},{14,8},{16,22},{18,... | collective-permute-start | bytes 417800 | tf_op jit(solution)/shard_map/ppermute | solution.py:432
  14.4 0.5 %collective-permute-start.5 = (bf16[272,256]{1,0:T(8,128)(2,1)S(1)}, bf16[272,256]{1,0:T(8,128)(2,1)S(1)}, u32[]{:S(2)}, u32[]{:S(2)}) collective-permute-start(bf16[272,256]{1,0:T(8,128)(2,1)S(1)} %get-tuple-element.110), channel_id=1, source_target_pairs={{0,4},{2,6},{4,0},{6,2},{8,12},{10,14},{12,8},{14,10},{16,20},{18,... | collective-permute-start | bytes 417800 | tf_op jit(solution)/shard_map/ppermute | solution.py:432
  14.9 0.0 collective-permute-done.refs_1_.refs_5_
  14.9 0.1 collective-permute-start.6
  15.1 0.5 inner_setup.1
  15.5 0.0 collective-permute-done.1.refs_2_.refs_4_
  15.5 0.0 collective-permute-done.2.refs_3_
  15.5 0.1 totals.2.refs_11_.own
  15.7 2.0 %collective-permute-start.3 = (bf16[272,256]{1,0:T(8,128)(2,1)S(1)}, bf16[272,256]{1,0:T(8,128)(2,1)S(1)}, u32[]{:S(2)}, u32[]{:S(2)}) collective-permute-start(bf16[272,256]{1,0:T(8,128)(2,1)S(1)} %totals.2.refs_11_.own), channel_id=1, source_target_pairs={{0,8},{2,10},{4,12},{6,14},{8,0},{10,2},{12,4},{14,6},{16,24},{18,... | collective-permute-start | bytes 417800 | tf_op jit(solution)/shard_map/ppermute | solution.py:761
  17.7 1.4 %inner_terms.4 = (bf16[384,256]{1,0:T(8,128)(2,1)S(1)}, f32[384,128]{1,0:T(8,128)S(1)}, f32[384,128]{1,0:T(8,128)S(1)}) custom-call(bf16[384,128]{1,0:T(8,128)(2,1)S(1)} %get-tuple-element.82.refs_0_.b, bf16[384,128]{1,0:T(8,128)(2,1)S(1)} %get-tuple-element.83.refs_1_.c, bf16[384,1024]{1,0:T(8,128)(2,1)S(1)} %get-tuple-element.84.refs_2_.refs_0_, ...), custom_call_target="tpu_custom_call" | custom-call | flops 1 | bytes 1 | tf_op jit(solution)/shard_map/inner_terms/pallas_call | solution.py:585
  19.1 0.0 collective-permute-done.4.refs_1_.refs_5_
  19.1 1.2 %collective-permute-done.5.refs_2_.refs_4_ = bf16[272,256]{1,0:T(8,128)(2,1)S(1)} collective-permute-done((bf16[272,256]{1,0:T(8,128)(2,1)S(1)}, bf16[272,256]{1,0:T(8,128)(2,1)S(1)}, u32[]{:S(2)}, u32[]{:S(2)}) %collective-permute-start.5) | collective-permute-done | bytes 139296 | tf_op jit(solution)/shard_map/ppermute | solution.py:432
  20.3 0.2 collective-permute-done.6.refs_3_
  20.5 0.1 totals.3.own
  20.6 1.6 %collective-permute-start.7 = (bf16[272,256]{1,0:T(8,128)(2,1)S(1)}, bf16[272,256]{1,0:T(8,128)(2,1)S(1)}, u32[]{:S(2)}, u32[]{:S(2)}) collective-permute-start(bf16[272,256]{1,0:T(8,128)(2,1)S(1)} %totals.3.own), channel_id=1, source_target_pairs={{0,8},{2,10},{4,12},{6,14},{8,0},{10,2},{12,4},{14,6},{16,24},{18,... | collective-permute-start | bytes 417800 | tf_op jit(solution)/shard_map/ppermute | solution.py:761
  22.2 0.0 collective-permute-done.3.received.refs_0_
  22.3 2.6 %collective-permute-start.12 = (bf16[128,256]{1,0:T(8,128)(2,1)S(1)}, bf16[128,256]{1,0:T(8,128)(2,1)S(1)}, u32[]{:S(2)}, u32[]{:S(2)}) collective-permute-start(bf16[128,256]{1,0:T(8,128)(2,1)S(1)} %merged.2.refs_13_), channel_id=1, source_target_pairs={{0,16},{2,18},{4,20},{6,22},{8,24},{10,26},{12,28},{14,30},{16,0},... | collective-permute-start | bytes 196616 | tf_op jit(solution)/shard_map/ppermute | solution.py:761
  24.9 3.1 %inner_terms.5 = (bf16[384,256]{1,0:T(8,128)(2,1)S(1)}, bf16[384,256]{1,0:T(8,128)(2,1)S(1)}, bf16[384,256]{1,0:T(8,128)(2,1)S(1)}, f32[384,128]{1,0:T(8,128)S(1)}, f32[384,128]{1,0:T(8,128)S(1)}) custom-call(bf16[384,128]{1,0:T(8,128)(2,1)S(1)} %get-tuple-element.82.refs_0_.b, bf16[384,128]{1,0:T(8,128)(2,1)S(1)} %get-tuple-element.83.refs_1_.c, ...), custom_call_target="tpu_custom_call" | custom-call | flops 805306368 | bytes 3145728 | tf_op jit(solution)/shard_map/inner_terms/pallas_call | solution.py:585
  28.0 0.0 collective-permute-done.12.refs_1_
  28.0 0.2 member_entries.3
  28.2 1.7 %collective-permute-start.13 = (bf16[256,256]{1,0:T(8,128)(2,1)S(1)}, bf16[256,256]{1,0:T(8,128)(2,1)S(1)}, u32[]{:S(2)}, u32[]{:S(2)}) collective-permute-start(bf16[256,256]{1,0:T(8,128)(2,1)S(1)} %get-tuple-element.135), channel_id=1, source_target_pairs={{0,6},{2,4},{4,2},{6,0},{8,14},{10,12},{12,10},{14,8},{16,22},{18,... | collective-permute-start | bytes 393224 | tf_op jit(solution)/shard_map/ppermute | solution.py:432
  29.9 0.0 collective-permute-done.7.received.refs_0_
  30.0 2.2 %collective-permute-start.8 = (bf16[128,256]{1,0:T(8,128)(2,1)S(1)}, bf16[128,256]{1,0:T(8,128)(2,1)S(1)}, u32[]{:S(2)}, u32[]{:S(2)}) collective-permute-start(bf16[128,256]{1,0:T(8,128)(2,1)S(1)} %merged.3.refs_13_), channel_id=1, source_target_pairs={{0,16},{2,18},{4,20},{6,22},{8,24},{10,26},{12,28},{14,30},{16,0},... | collective-permute-start | bytes 196616 | tf_op jit(solution)/shard_map/ppermute | solution.py:761
  32.2 1.2 %collective-permute-start.14 = (bf16[256,256]{1,0:T(8,128)(2,1)S(1)}, bf16[256,256]{1,0:T(8,128)(2,1)S(1)}, u32[]{:S(2)}, u32[]{:S(2)}) collective-permute-start(bf16[256,256]{1,0:T(8,128)(2,1)S(1)} %get-tuple-element.136), channel_id=1, source_target_pairs={{0,4},{2,6},{4,0},{6,2},{8,12},{10,14},{12,8},{14,10},{16,20},{18,... | collective-permute-start | bytes 393224 | tf_op jit(solution)/shard_map/ppermute | solution.py:432
  33.5 0.5 %collective-permute-start.15 = (bf16[256,256]{1,0:T(8,128)(2,1)S(1)}, bf16[256,256]{1,0:T(8,128)(2,1)S(1)}, u32[]{:S(2)}, u32[]{:S(2)}) collective-permute-start(bf16[256,256]{1,0:T(8,128)(2,1)S(1)} %get-tuple-element.137), channel_id=1, source_target_pairs={{0,2},{2,0},{4,6},{6,4},{8,10},{10,8},{12,14},{14,12},{16,18},{18,... | collective-permute-start | bytes 393224 | tf_op jit(solution)/shard_map/ppermute | solution.py:432
  34.0 2.1 %inner_terms.6 = (bf16[384,256]{1,0:T(8,128)(2,1)S(1)}, bf16[384,256]{1,0:T(8,128)(2,1)S(1)}, f32[384,128]{1,0:T(8,128)S(1)}, f32[384,128]{1,0:T(8,128)S(1)}) custom-call(bf16[384,128]{1,0:T(8,128)(2,1)S(1)} %get-tuple-element.82.refs_0_.b, bf16[384,128]{1,0:T(8,128)(2,1)S(1)} %get-tuple-element.83.refs_1_.c, ...), custom_call_target="tpu_custom_call" | custom-call | flops 805306368 | bytes 3145728 | tf_op jit(solution)/shard_map/inner_terms/pallas_call | solution.py:585
  36.0 0.0 collective-permute-done.8.refs_1_
  36.1 0.4 member_entries.2
  36.4 1.8 %collective-permute-start.9 = (bf16[256,256]{1,0:T(8,128)(2,1)S(1)}, bf16[256,256]{1,0:T(8,128)(2,1)S(1)}, u32[]{:S(2)}, u32[]{:S(2)}) collective-permute-start(bf16[256,256]{1,0:T(8,128)(2,1)S(1)} %get-tuple-element.123), channel_id=1, source_target_pairs={{0,6},{2,4},{4,2},{6,0},{8,14},{10,12},{12,10},{14,8},{16,22},{18,... | collective-permute-start | bytes 393224 | tf_op jit(solution)/shard_map/ppermute | solution.py:432
  38.3 1.2 %collective-permute-start.10 = (bf16[256,256]{1,0:T(8,128)(2,1)S(1)}, bf16[256,256]{1,0:T(8,128)(2,1)S(1)}, u32[]{:S(2)}, u32[]{:S(2)}) collective-permute-start(bf16[256,256]{1,0:T(8,128)(2,1)S(1)} %get-tuple-element.124), channel_id=1, source_target_pairs={{0,4},{2,6},{4,0},{6,2},{8,12},{10,14},{12,8},{14,10},{16,20},{18,... | collective-permute-start | bytes 393224 | tf_op jit(solution)/shard_map/ppermute | solution.py:432
  39.5 0.5 %collective-permute-start.11 = (bf16[256,256]{1,0:T(8,128)(2,1)S(1)}, bf16[256,256]{1,0:T(8,128)(2,1)S(1)}, u32[]{:S(2)}, u32[]{:S(2)}) collective-permute-start(bf16[256,256]{1,0:T(8,128)(2,1)S(1)} %get-tuple-element.125), channel_id=1, source_target_pairs={{0,2},{2,0},{4,6},{6,4},{8,10},{10,8},{12,14},{14,12},{16,18},{18,... | collective-permute-start | bytes 393224 | tf_op jit(solution)/shard_map/ppermute | solution.py:432
  40.0 2.1 %inner_terms.7 = (bf16[384,256]{1,0:T(8,128)(2,1)S(1)}, bf16[384,256]{1,0:T(8,128)(2,1)S(1)}, f32[384,128]{1,0:T(8,128)S(1)}, f32[384,128]{1,0:T(8,128)S(1)}) custom-call(bf16[384,128]{1,0:T(8,128)(2,1)S(1)} %get-tuple-element.82.refs_0_.b, bf16[384,128]{1,0:T(8,128)(2,1)S(1)} %get-tuple-element.83.refs_1_.c, ...), custom_call_target="tpu_custom_call" | custom-call | flops 805306368 | bytes 3145728 | tf_op jit(solution)/shard_map/inner_terms/pallas_call | solution.py:585
  42.1 0.0 collective-permute-done.15.refs_11_
  42.1 0.4 entry_values.1.refs_12_.refs_6_
  42.5 0.6 %entry_parts.3 = (f32[384,128]{1,0:T(8,128)S(1)}, f32[384,128]{1,0:T(8,128)S(1)}) custom-call(f32[384,128]{1,0:T(8,128)S(1)} %get-tuple-element.138.db_before, f32[384,128]{1,0:T(8,128)S(1)} %get-tuple-element.139.dc_before, bf16[384,256]{1,0:T(8,128)(2,1)S(1)} %get-tuple-element.140.refs_0_, bf16[384,256]{1,0:T(8,128)(2,1)S(1)} %get-tuple-element.141.refs_1_, ...), custom_call_target="tpu_custom_call" | custom-call | flops 301989888 | bytes 98304 | tf_op jit(solution)/shard_map/entry_parts/pallas_call | solution.py:622
  43.1 0.4 entry_parts.4
  43.5 0.6 %collective-permute-done.10.refs_10_.refs_4_ = bf16[256,256]{1,0:T(8,128)(2,1)S(1)} collective-permute-done((bf16[256,256]{1,0:T(8,128)(2,1)S(1)}, bf16[256,256]{1,0:T(8,128)(2,1)S(1)}, u32[]{:S(2)}, u32[]{:S(2)}) %collective-permute-start.10) | collective-permute-done | bytes 131104 | tf_op jit(solution)/shard_map/ppermute | solution.py:432
  44.1 0.4 collective-permute-done.11.refs_11_.refs_5_
  44.5 0.4 entry_parts.5.refs_0_
  44.8 0.1 collective-permute-start.16
  44.9 1.3 %last_values.1 = bf16[384,2048]{1,0:T(8,128)(2,1)} custom-call(s32[1]{0:T(128)} %bitcast.where, bf16[384,128]{1,0:T(8,128)(2,1)S(1)} %get-tuple-element.82.refs_0_.b, bf16[384,256]{1,0:T(8,128)(2,1)S(1)} %get-tuple-element.112.refs_0_, bf16[384,256]{1,0:T(8,128)(2,1)S(1)} %get-tuple-element.113.refs_1_, bf16[384,256]{1,0:T(8,128)(2,1)S(1)} %get-tuple-element.117.refs_2_, ...), custom_call_target="tpu_custom_call" | custom-call | flops 100663296 | bytes 1572864 | tf_op jit(solution)/shard_map/last_values/pallas_call | solution.py:696
  46.2 0.1 collective-permute-done.16.refs_1_
  46.3 0.7 %sum_over_heads.1 = (bf16[384,128]{1,0:T(8,128)(2,1)}, bf16[384,128]{1,0:T(8,128)(2,1)}) custom-call(bf16[768,128]{1,0:T(8,128)(2,1)S(1)} %entry_parts.5.refs_0_, bf16[768,128]{1,0:T(8,128)(2,1)S(1)} %collective-permute-done.16.refs_1_), custom_call_target="tpu_custom_call" | custom-call | flops 196608 | bytes 393216 | tf_op jit(solution)/shard_map/sum_over_heads/pallas_call | solution.py:728
  (5 shorter events, 0.1 us)
Async XLA Ops:
  3.4 11.5 %collective-permute-start = (bf16[272,256]{1,0:T(8,128)(2,1)S(1)}, bf16[272,256]{1,0:T(8,128)(2,1)S(1)}, u32[]{:S(2)}, u32[]{:S(2)}) collective-permute-start(bf16[272,256]{1,0:T(8,128)(2,1)S(1)} %get-tuple-element.101), channel_id=1, source_target_pairs={{0,6},{2,4},{4,2},{6,0},{8,14},{10,12},{12,10},{14,8},{16,22},{18,... | collective-permute-start | bytes 417800 | tf_op jit(solution)/shard_map/ppermute | solution.py:432
  7.3 8.2 %collective-permute-start.1 = (bf16[272,256]{1,0:T(8,128)(2,1)S(1)}, bf16[272,256]{1,0:T(8,128)(2,1)S(1)}, u32[]{:S(2)}, u32[]{:S(2)}) collective-permute-start(bf16[272,256]{1,0:T(8,128)(2,1)S(1)} %get-tuple-element.102), channel_id=1, source_target_pairs={{0,4},{2,6},{4,0},{6,2},{8,12},{10,14},{12,8},{14,10},{16,20},{18,... | collective-permute-start | bytes 417800 | tf_op jit(solution)/shard_map/ppermute | solution.py:432
  7.8 7.7 %collective-permute-start.2 = (bf16[272,256]{1,0:T(8,128)(2,1)S(1)}, bf16[272,256]{1,0:T(8,128)(2,1)S(1)}, u32[]{:S(2)}, u32[]{:S(2)}) collective-permute-start(bf16[272,256]{1,0:T(8,128)(2,1)S(1)} %get-tuple-element.103), channel_id=1, source_target_pairs={{0,2},{2,0},{4,6},{6,4},{8,10},{10,8},{12,14},{14,12},{16,18},{18,... | collective-permute-start | bytes 417800 | tf_op jit(solution)/shard_map/ppermute | solution.py:432
  11.5 7.6 %collective-permute-start.4 = (bf16[272,256]{1,0:T(8,128)(2,1)S(1)}, bf16[272,256]{1,0:T(8,128)(2,1)S(1)}, u32[]{:S(2)}, u32[]{:S(2)}) collective-permute-start(bf16[272,256]{1,0:T(8,128)(2,1)S(1)} %get-tuple-element.109), channel_id=1, source_target_pairs={{0,6},{2,4},{4,2},{6,0},{8,14},{10,12},{12,10},{14,8},{16,22},{18,... | collective-permute-start | bytes 417800 | tf_op jit(solution)/shard_map/ppermute | solution.py:432
  14.4 5.9 %collective-permute-start.5 = (bf16[272,256]{1,0:T(8,128)(2,1)S(1)}, bf16[272,256]{1,0:T(8,128)(2,1)S(1)}, u32[]{:S(2)}, u32[]{:S(2)}) collective-permute-start(bf16[272,256]{1,0:T(8,128)(2,1)S(1)} %get-tuple-element.110), channel_id=1, source_target_pairs={{0,4},{2,6},{4,0},{6,2},{8,12},{10,14},{12,8},{14,10},{16,20},{18,... | collective-permute-start | bytes 417800 | tf_op jit(solution)/shard_map/ppermute | solution.py:432
  14.9 5.6 %collective-permute-start.6 = (bf16[272,256]{1,0:T(8,128)(2,1)S(1)}, bf16[272,256]{1,0:T(8,128)(2,1)S(1)}, u32[]{:S(2)}, u32[]{:S(2)}) collective-permute-start(bf16[272,256]{1,0:T(8,128)(2,1)S(1)} %get-tuple-element.111), channel_id=1, source_target_pairs={{0,2},{2,0},{4,6},{6,4},{8,10},{10,8},{12,14},{14,12},{16,18},{18,... | collective-permute-start | bytes 417800 | tf_op jit(solution)/shard_map/ppermute | solution.py:432
  15.7 6.6 %collective-permute-start.3 = (bf16[272,256]{1,0:T(8,128)(2,1)S(1)}, bf16[272,256]{1,0:T(8,128)(2,1)S(1)}, u32[]{:S(2)}, u32[]{:S(2)}) collective-permute-start(bf16[272,256]{1,0:T(8,128)(2,1)S(1)} %totals.2.refs_11_.own), channel_id=1, source_target_pairs={{0,8},{2,10},{4,12},{6,14},{8,0},{10,2},{12,4},{14,6},{16,24},{18,... | collective-permute-start | bytes 417800 | tf_op jit(solution)/shard_map/ppermute | solution.py:761
  20.6 9.3 %collective-permute-start.7 = (bf16[272,256]{1,0:T(8,128)(2,1)S(1)}, bf16[272,256]{1,0:T(8,128)(2,1)S(1)}, u32[]{:S(2)}, u32[]{:S(2)}) collective-permute-start(bf16[272,256]{1,0:T(8,128)(2,1)S(1)} %totals.3.own), channel_id=1, source_target_pairs={{0,8},{2,10},{4,12},{6,14},{8,0},{10,2},{12,4},{14,6},{16,24},{18,... | collective-permute-start | bytes 417800 | tf_op jit(solution)/shard_map/ppermute | solution.py:761
  22.3 5.7 %collective-permute-start.12 = (bf16[128,256]{1,0:T(8,128)(2,1)S(1)}, bf16[128,256]{1,0:T(8,128)(2,1)S(1)}, u32[]{:S(2)}, u32[]{:S(2)}) collective-permute-start(bf16[128,256]{1,0:T(8,128)(2,1)S(1)} %merged.2.refs_13_), channel_id=1, source_target_pairs={{0,16},{2,18},{4,20},{6,22},{8,24},{10,26},{12,28},{14,30},{16,0},... | collective-permute-start | bytes 196616 | tf_op jit(solution)/shard_map/ppermute | solution.py:761
  28.2 11.3 %collective-permute-start.13 = (bf16[256,256]{1,0:T(8,128)(2,1)S(1)}, bf16[256,256]{1,0:T(8,128)(2,1)S(1)}, u32[]{:S(2)}, u32[]{:S(2)}) collective-permute-start(bf16[256,256]{1,0:T(8,128)(2,1)S(1)} %get-tuple-element.135), channel_id=1, source_target_pairs={{0,6},{2,4},{4,2},{6,0},{8,14},{10,12},{12,10},{14,8},{16,22},{18,... | collective-permute-start | bytes 393224 | tf_op jit(solution)/shard_map/ppermute | solution.py:432
  30.0 6.0 %collective-permute-start.8 = (bf16[128,256]{1,0:T(8,128)(2,1)S(1)}, bf16[128,256]{1,0:T(8,128)(2,1)S(1)}, u32[]{:S(2)}, u32[]{:S(2)}) collective-permute-start(bf16[128,256]{1,0:T(8,128)(2,1)S(1)} %merged.3.refs_13_), channel_id=1, source_target_pairs={{0,16},{2,18},{4,20},{6,22},{8,24},{10,26},{12,28},{14,30},{16,0},... | collective-permute-start | bytes 196616 | tf_op jit(solution)/shard_map/ppermute | solution.py:761
  32.2 9.8 %collective-permute-start.14 = (bf16[256,256]{1,0:T(8,128)(2,1)S(1)}, bf16[256,256]{1,0:T(8,128)(2,1)S(1)}, u32[]{:S(2)}, u32[]{:S(2)}) collective-permute-start(bf16[256,256]{1,0:T(8,128)(2,1)S(1)} %get-tuple-element.136), channel_id=1, source_target_pairs={{0,4},{2,6},{4,0},{6,2},{8,12},{10,14},{12,8},{14,10},{16,20},{18,... | collective-permute-start | bytes 393224 | tf_op jit(solution)/shard_map/ppermute | solution.py:432
  33.5 8.6 %collective-permute-start.15 = (bf16[256,256]{1,0:T(8,128)(2,1)S(1)}, bf16[256,256]{1,0:T(8,128)(2,1)S(1)}, u32[]{:S(2)}, u32[]{:S(2)}) collective-permute-start(bf16[256,256]{1,0:T(8,128)(2,1)S(1)} %get-tuple-element.137), channel_id=1, source_target_pairs={{0,2},{2,0},{4,6},{6,4},{8,10},{10,8},{12,14},{14,12},{16,18},{18,... | collective-permute-start | bytes 393224 | tf_op jit(solution)/shard_map/ppermute | solution.py:432
  36.4 6.7 %collective-permute-start.9 = (bf16[256,256]{1,0:T(8,128)(2,1)S(1)}, bf16[256,256]{1,0:T(8,128)(2,1)S(1)}, u32[]{:S(2)}, u32[]{:S(2)}) collective-permute-start(bf16[256,256]{1,0:T(8,128)(2,1)S(1)} %get-tuple-element.123), channel_id=1, source_target_pairs={{0,6},{2,4},{4,2},{6,0},{8,14},{10,12},{12,10},{14,8},{16,22},{18,... | collective-permute-start | bytes 393224 | tf_op jit(solution)/shard_map/ppermute | solution.py:432
  38.3 5.8 %collective-permute-start.10 = (bf16[256,256]{1,0:T(8,128)(2,1)S(1)}, bf16[256,256]{1,0:T(8,128)(2,1)S(1)}, u32[]{:S(2)}, u32[]{:S(2)}) collective-permute-start(bf16[256,256]{1,0:T(8,128)(2,1)S(1)} %get-tuple-element.124), channel_id=1, source_target_pairs={{0,4},{2,6},{4,0},{6,2},{8,12},{10,14},{12,8},{14,10},{16,20},{18,... | collective-permute-start | bytes 393224 | tf_op jit(solution)/shard_map/ppermute | solution.py:432
  39.5 5.0 %collective-permute-start.11 = (bf16[256,256]{1,0:T(8,128)(2,1)S(1)}, bf16[256,256]{1,0:T(8,128)(2,1)S(1)}, u32[]{:S(2)}, u32[]{:S(2)}) collective-permute-start(bf16[256,256]{1,0:T(8,128)(2,1)S(1)} %get-tuple-element.125), channel_id=1, source_target_pairs={{0,2},{2,0},{4,6},{6,4},{8,10},{10,8},{12,14},{14,12},{16,18},{18,... | collective-permute-start | bytes 393224 | tf_op jit(solution)/shard_map/ppermute | solution.py:432
  44.8 1.5 %collective-permute-start.16 = (bf16[768,128]{1,0:T(8,128)(2,1)S(1)}, bf16[768,128]{1,0:T(8,128)(2,1)S(1)}, u32[]{:S(2)}, u32[]{:S(2)}) collective-permute-start(bf16[768,128]{1,0:T(8,128)(2,1)S(1)} %entry_parts.5.refs_0_), channel_id=1, source_target_pairs={{0,1},{1,0},{2,3},{3,2},{4,5},{5,4},{6,7},{7,6},{8,9},{9,8},{10,11... | collective-permute-start | bytes 589832 | tf_op jit(solution)/shard_map/ppermute | solution.py:727

commit v17 on v16

--- a/solution.py
+++ b/solution.py
@@ -96,8 +96,8 @@
     return 2 if (width // GROUP) % (2 * LANES) == 0 else 1
 
 
-def chunk_lanes(where, k, chunk, part, width):
-    start = (place_of(where) ^ k) * (width // GROUP) + chunk * part
+def chunk_lanes(where, k, chunk, part):
+    start = (chunk * GROUP + (place_of(where) ^ k)) * part
     return pl.ds(pl.multiple_of(start, part), part)
 
 
@@ -131,7 +131,7 @@
                 turned = proj[...].T
             x_scaled, dy_scaled, spread, send = outs[4 * n : 4 * n + 4]
             member = place_of(where) ^ k
-            first_head = (member * chunks + chunk) * (part // head_dim)
+            first_head = (chunk * GROUP + member) * (part // head_dim)
             hot = head_of_lane(difference, first_head)
             wide = dot(factors, hot, NN).astype(BF16)
             if side == 0:
@@ -143,15 +143,11 @@
             send[side * state : (side + 1) * state, :] = dot(turned, piece, NN).astype(BF16)
 
 
-def load_chunk(chunk, chunks, source, target, sems, first):
-    part = target.shape[1] // GROUP
-    copies = []
-    for m in range(GROUP):
-        lanes = pl.ds((m * chunks + chunk) * part, part)
-        at = target.at[:, pl.ds(m * part, part)]
-        copies.append(pltpu.make_async_copy(source.at[:, lanes], at, sems.at[first + m]))
-        copies[-1].start()
-    return copies
+def load_chunk(chunk, source, target, sem):
+    width = target.shape[1]
+    copy = pltpu.make_async_copy(source.at[:, pl.ds(chunk * width, width)], target, sem)
+    copy.start()
+    return copy
 
 
 def first_states_kernel(head_dim, chunks, pieces, where, ld_in, b_in, c_in, x_in, dy_in, *refs):
@@ -165,8 +161,8 @@
 
     first = load(0, ld_in, ld)
     copies = [
-        [load(1, b_in, b), *load_chunk(0, chunks, x_in, x, sems, 3)],
-        [load(2, c_in, c), *load_chunk(0, chunks, dy_in, dy, sems, 3 + GROUP)],
+        [load(1, b_in, b), load_chunk(0, x_in, x, sems.at[3])],
+        [load(2, c_in, c), load_chunk(0, dy_in, dy, sems.at[4])],
     ]
     masks = masks_of(ld.shape[1])
     first.wait()
@@ -189,13 +185,12 @@
     xs, dys, copies = {0: x}, {0: dy}, {}
     for chunk in range(1, chunks):
         xs[chunk], dys[chunk] = kept[2 * chunk - 2 : 2 * chunk]
-        at = 2 * GROUP * (chunk - 1)
-        copies[0, chunk] = load_chunk(chunk, chunks, x_in, xs[chunk], sems, at)
-        copies[1, chunk] = load_chunk(chunk, chunks, dy_in, dys[chunk], sems, at + GROUP)
+        copies[0, chunk] = load_chunk(chunk, x_in, xs[chunk], sems.at[2 * chunk - 2])
+        copies[1, chunk] = load_chunk(chunk, dy_in, dys[chunk], sems.at[2 * chunk - 1])
 
     def ready(side, chunk):
-        for copy in copies.get((side, chunk), []):
-            copy.wait()
+        if (side, chunk) in copies:
+            copies[side, chunk].wait()
 
     operands = (into_end[...], from_start[...], halves[...], b, c, xs, dys)
     put_states(head_dim, chunks, pieces, where, operands, outs, ready)
@@ -225,7 +220,7 @@
         out_shape=outs,
         in_specs=[SMEM] + [HBM] * 5,
         out_specs=whole(len(outs)),
-        scratch_shapes=[pltpu.SemaphoreType.DMA((3 + 2 * GROUP,))],
+        scratch_shapes=[pltpu.SemaphoreType.DMA((5,))],
         compiler_params=params(8),
         cost_estimate=cost(2 * length * width * (state + LANES), 8 * length * width),
         name="first_states",
@@ -244,7 +239,7 @@
         out_shape=outs,
         in_specs=[SMEM] + whole(7) + [HBM] * 2,
         out_specs=whole(len(outs)),
-        scratch_shapes=[pltpu.SemaphoreType.DMA((max(n_kept, 1) * GROUP,))],
+        scratch_shapes=[pltpu.SemaphoreType.DMA((max(n_kept, 1),))],
         compiler_params=params(8),
         cost_estimate=cost(2 * length * width * (state + LANES), 4 * length * width),
         name="next_states",
@@ -515,7 +510,7 @@
     difference = row_less_head(head_dim, part, SLOT)
 
     for at, (chunk, m) in enumerate(worked):
-        x, dy, first_head = xs[chunk], dys[chunk], (m * chunks + chunk) * (part // head_dim)
+        x, dy, first_head = xs[chunk], dys[chunk], (chunk * GROUP + m) * (part // head_dim)
         lanes, here = slice(m * part, (m + 1) * part), slice(at * part, (at + 1) * part)
         cum = dot(cum_terms[...], head_of_lane(difference, first_head), NN)
         dx = []
@@ -659,7 +654,7 @@
     stores = []
 
     def store(chunk, k, source):
-        lanes = chunk_lanes(where, k, chunk, part, out.shape[1])
+        lanes = chunk_lanes(where, k, chunk, part)
         at = sems.at[chunk * GROUP + k]
         stores.append(pltpu.make_async_copy(source, out.at[:, lanes], at))
         stores[-1].start()

time: 47.2 us -> 46.9 us (level)
  no operation moved by 1% of the time
where the time goes in v17:
time: 46.9 us; the launch traced here: 46.7 us
  starting transfers between devices  23.8 us (51%)
  Pallas kernels  19.6 us (42%)
  waiting for transfers between devices  2.51 us (5%)
  between operations  0.84 us (2%)
    ppermute x12, starting transfers between devices, exchange(): out[k] = lax.ppermute(parts[k], 'seq', [(s, s ^ k) for s in range(count)])  15.2 us
    pallas_call x4, Pallas kernels, inner_terms(): pl.pallas_call(functools.partial(inner_kernel, head_dim, worked, chunks,...  8.61 us
    ppermute x4, starting transfers between devices, to_group(): lax.ppermute(block, 'seq', [(s, s ^ k * group) for s in range(count)])  8.54 us
    pallas_call x1, Pallas kernels, next_states(): pl.pallas_call(functools.partial(next_states_kernel, head_dim, chunks, pi...  3.23 us
    pallas_call x1, Pallas kernels, first_states(): pl.pallas_call(functools.partial(first_states_kernel, head_dim, chunks, p...  2.67 us
    ppermute x12, waiting for transfers between devices, exchange(): out[k] = lax.ppermute(parts[k], 'seq', [(s, s ^ k) for s in range(count)])  2.4 us
    pallas_call x1, Pallas kernels, entry_values(): pl.pallas_call(functools.partial(last_values_kernel, chunks), out_shape=p...  1.33 us
    pallas_call x3, Pallas kernels, entry_parts(): pl.pallas_call(functools.partial(parts_kernel, last, ks), out_shape=outs,...  1.29 us
  transfers between devices with their start and end apart: 17, of which 5 were waited for; matrix products, arithmetic and copies ran while one was open for 0% of the time, Pallas kernels for 34%

profile of v17, /device:TPU:0, one launch (start us, length us, event | category | flops | bytes accessed | tf_op | source)
XLA Modules:
  0.0 46.7 jit_solution(5403835922403263716)
XLA Ops:
  0.6 2.7 %first_states.1 = (f32[32,384]{1,0:T(8,128)S(1)}, bf16[384,128]{1,0:T(8,128)(2,1)S(1)}, bf16[384,128]{1,0:T(8,128)(2,1)S(1)}, bf16[384,1024]{1,0:T(8,128)(2,1)S(...) custom-call(s32[1]{0:T(128)} %bitcast.where, ...), custom_call_target="tpu_custom_call" | custom-call | flops 402653184 | bytes 6291456 | tf_op jit(solution)/shard_map/first_states/pallas_call | solution.py:218
  3.3 4.0 %collective-permute-start = (bf16[272,256]{1,0:T(8,128)(2,1)S(1)}, bf16[272,256]{1,0:T(8,128)(2,1)S(1)}, u32[]{:S(2)}, u32[]{:S(2)}) collective-permute-start(bf16[272,256]{1,0:T(8,128)(2,1)S(1)} %get-tuple-element.101), channel_id=1, source_target_pairs={{0,6},{2,4},{4,2},{6,0},{8,14},{10,12},{12,10},{14,8},{16,22},{18,... | collective-permute-start | bytes 417800 | tf_op jit(solution)/shard_map/ppermute | solution.py:427
  7.3 0.5 %collective-permute-start.1 = (bf16[272,256]{1,0:T(8,128)(2,1)S(1)}, bf16[272,256]{1,0:T(8,128)(2,1)S(1)}, u32[]{:S(2)}, u32[]{:S(2)}) collective-permute-start(bf16[272,256]{1,0:T(8,128)(2,1)S(1)} %get-tuple-element.102), channel_id=1, source_target_pairs={{0,4},{2,6},{4,0},{6,2},{8,12},{10,14},{12,8},{14,10},{16,20},{18,... | collective-permute-start | bytes 417800 | tf_op jit(solution)/shard_map/ppermute | solution.py:427
  7.8 0.1 collective-permute-start.2
  7.9 3.2 %next_states.1 = (bf16[384,1024]{1,0:T(8,128)(2,1)S(1)}, bf16[384,1024]{1,0:T(8,128)(2,1)S(1)}, bf16[384,256]{1,0:T(8,128)(2,1)S(1)}, bf16[384,256]{1,0:T(8,128)...) custom-call(s32[1]{0:T(128)} %bitcast.where, ...), custom_call_target="tpu_custom_call" | custom-call | flops 402653184 | bytes 3145728 | tf_op jit(solution)/shard_map/next_states/pallas_call | solution.py:237
  11.1 2.9 %collective-permute-start.4 = (bf16[272,256]{1,0:T(8,128)(2,1)S(1)}, bf16[272,256]{1,0:T(8,128)(2,1)S(1)}, u32[]{:S(2)}, u32[]{:S(2)}) collective-permute-start(bf16[272,256]{1,0:T(8,128)(2,1)S(1)} %get-tuple-element.109), channel_id=1, source_target_pairs={{0,6},{2,4},{4,2},{6,0},{8,14},{10,12},{12,10},{14,8},{16,22},{18,... | collective-permute-start | bytes 417800 | tf_op jit(solution)/shard_map/ppermute | solution.py:427
  14.1 0.5 %collective-permute-start.5 = (bf16[272,256]{1,0:T(8,128)(2,1)S(1)}, bf16[272,256]{1,0:T(8,128)(2,1)S(1)}, u32[]{:S(2)}, u32[]{:S(2)}) collective-permute-start(bf16[272,256]{1,0:T(8,128)(2,1)S(1)} %get-tuple-element.110), channel_id=1, source_target_pairs={{0,4},{2,6},{4,0},{6,2},{8,12},{10,14},{12,8},{14,10},{16,20},{18,... | collective-permute-start | bytes 417800 | tf_op jit(solution)/shard_map/ppermute | solution.py:427
  14.6 0.0 collective-permute-done.refs_1_.refs_5_
  14.6 0.1 collective-permute-start.6
  14.7 0.5 inner_setup.1
  15.2 0.0 collective-permute-done.1.refs_2_.refs_4_
  15.2 0.0 collective-permute-done.2.refs_3_
  15.2 0.1 totals.2.refs_11_.own
  15.3 2.0 %collective-permute-start.3 = (bf16[272,256]{1,0:T(8,128)(2,1)S(1)}, bf16[272,256]{1,0:T(8,128)(2,1)S(1)}, u32[]{:S(2)}, u32[]{:S(2)}) collective-permute-start(bf16[272,256]{1,0:T(8,128)(2,1)S(1)} %totals.2.refs_11_.own), channel_id=1, source_target_pairs={{0,8},{2,10},{4,12},{6,14},{8,0},{10,2},{12,4},{14,6},{16,24},{18,... | collective-permute-start | bytes 417800 | tf_op jit(solution)/shard_map/ppermute | solution.py:756
  17.4 1.4 %inner_terms.4 = (bf16[384,256]{1,0:T(8,128)(2,1)S(1)}, f32[384,128]{1,0:T(8,128)S(1)}, f32[384,128]{1,0:T(8,128)S(1)}) custom-call(bf16[384,128]{1,0:T(8,128)(2,1)S(1)} %get-tuple-element.82.refs_0_.b, bf16[384,128]{1,0:T(8,128)(2,1)S(1)} %get-tuple-element.83.refs_1_.c, bf16[384,1024]{1,0:T(8,128)(2,1)S(1)} %get-tuple-element.84.refs_2_.refs_0_, ...), custom_call_target="tpu_custom_call" | custom-call | flops 1 | bytes 1 | tf_op jit(solution)/shard_map/inner_terms/pallas_call | solution.py:580
  18.7 0.0 collective-permute-done.4.refs_1_.refs_5_
  18.7 1.2 %collective-permute-done.5.refs_2_.refs_4_ = bf16[272,256]{1,0:T(8,128)(2,1)S(1)} collective-permute-done((bf16[272,256]{1,0:T(8,128)(2,1)S(1)}, bf16[272,256]{1,0:T(8,128)(2,1)S(1)}, u32[]{:S(2)}, u32[]{:S(2)}) %collective-permute-start.5) | collective-permute-done | bytes 139296 | tf_op jit(solution)/shard_map/ppermute | solution.py:427
  20.0 0.2 collective-permute-done.6.refs_3_
  20.1 0.1 totals.3.own
  20.3 1.6 %collective-permute-start.7 = (bf16[272,256]{1,0:T(8,128)(2,1)S(1)}, bf16[272,256]{1,0:T(8,128)(2,1)S(1)}, u32[]{:S(2)}, u32[]{:S(2)}) collective-permute-start(bf16[272,256]{1,0:T(8,128)(2,1)S(1)} %totals.3.own), channel_id=1, source_target_pairs={{0,8},{2,10},{4,12},{6,14},{8,0},{10,2},{12,4},{14,6},{16,24},{18,... | collective-permute-start | bytes 417800 | tf_op jit(solution)/shard_map/ppermute | solution.py:756
  21.9 0.0 collective-permute-done.3.received.refs_0_
  22.0 2.7 %collective-permute-start.12 = (bf16[128,256]{1,0:T(8,128)(2,1)S(1)}, bf16[128,256]{1,0:T(8,128)(2,1)S(1)}, u32[]{:S(2)}, u32[]{:S(2)}) collective-permute-start(bf16[128,256]{1,0:T(8,128)(2,1)S(1)} %merged.2.refs_13_), channel_id=1, source_target_pairs={{0,16},{2,18},{4,20},{6,22},{8,24},{10,26},{12,28},{14,30},{16,0},... | collective-permute-start | bytes 196616 | tf_op jit(solution)/shard_map/ppermute | solution.py:756
  24.6 3.1 %inner_terms.5 = (bf16[384,256]{1,0:T(8,128)(2,1)S(1)}, bf16[384,256]{1,0:T(8,128)(2,1)S(1)}, bf16[384,256]{1,0:T(8,128)(2,1)S(1)}, f32[384,128]{1,0:T(8,128)S(1)}, f32[384,128]{1,0:T(8,128)S(1)}) custom-call(bf16[384,128]{1,0:T(8,128)(2,1)S(1)} %get-tuple-element.82.refs_0_.b, bf16[384,128]{1,0:T(8,128)(2,1)S(1)} %get-tuple-element.83.refs_1_.c, ...), custom_call_target="tpu_custom_call" | custom-call | flops 805306368 | bytes 3145728 | tf_op jit(solution)/shard_map/inner_terms/pallas_call | solution.py:580
  27.7 0.0 collective-permute-done.12.refs_1_
  27.7 0.2 member_entries.3
  27.9 1.7 %collective-permute-start.13 = (bf16[256,256]{1,0:T(8,128)(2,1)S(1)}, bf16[256,256]{1,0:T(8,128)(2,1)S(1)}, u32[]{:S(2)}, u32[]{:S(2)}) collective-permute-start(bf16[256,256]{1,0:T(8,128)(2,1)S(1)} %get-tuple-element.135), channel_id=1, source_target_pairs={{0,6},{2,4},{4,2},{6,0},{8,14},{10,12},{12,10},{14,8},{16,22},{18,... | collective-permute-start | bytes 393224 | tf_op jit(solution)/shard_map/ppermute | solution.py:427
  29.6 0.0 collective-permute-done.7.received.refs_0_
  29.7 2.2 %collective-permute-start.8 = (bf16[128,256]{1,0:T(8,128)(2,1)S(1)}, bf16[128,256]{1,0:T(8,128)(2,1)S(1)}, u32[]{:S(2)}, u32[]{:S(2)}) collective-permute-start(bf16[128,256]{1,0:T(8,128)(2,1)S(1)} %merged.3.refs_13_), channel_id=1, source_target_pairs={{0,16},{2,18},{4,20},{6,22},{8,24},{10,26},{12,28},{14,30},{16,0},... | collective-permute-start | bytes 196616 | tf_op jit(solution)/shard_map/ppermute | solution.py:756
  31.9 1.3 %collective-permute-start.14 = (bf16[256,256]{1,0:T(8,128)(2,1)S(1)}, bf16[256,256]{1,0:T(8,128)(2,1)S(1)}, u32[]{:S(2)}, u32[]{:S(2)}) collective-permute-start(bf16[256,256]{1,0:T(8,128)(2,1)S(1)} %get-tuple-element.136), channel_id=1, source_target_pairs={{0,4},{2,6},{4,0},{6,2},{8,12},{10,14},{12,8},{14,10},{16,20},{18,... | collective-permute-start | bytes 393224 | tf_op jit(solution)/shard_map/ppermute | solution.py:427
  33.2 0.5 collective-permute-start.15
  33.6 2.1 %inner_terms.6 = (bf16[384,256]{1,0:T(8,128)(2,1)S(1)}, bf16[384,256]{1,0:T(8,128)(2,1)S(1)}, f32[384,128]{1,0:T(8,128)S(1)}, f32[384,128]{1,0:T(8,128)S(1)}) custom-call(bf16[384,128]{1,0:T(8,128)(2,1)S(1)} %get-tuple-element.82.refs_0_.b, bf16[384,128]{1,0:T(8,128)(2,1)S(1)} %get-tuple-element.83.refs_1_.c, ...), custom_call_target="tpu_custom_call" | custom-call | flops 805306368 | bytes 3145728 | tf_op jit(solution)/shard_map/inner_terms/pallas_call | solution.py:580
  35.7 0.4 member_entries.2
  36.1 1.8 %collective-permute-start.9 = (bf16[256,256]{1,0:T(8,128)(2,1)S(1)}, bf16[256,256]{1,0:T(8,128)(2,1)S(1)}, u32[]{:S(2)}, u32[]{:S(2)}) collective-permute-start(bf16[256,256]{1,0:T(8,128)(2,1)S(1)} %get-tuple-element.123), channel_id=1, source_target_pairs={{0,6},{2,4},{4,2},{6,0},{8,14},{10,12},{12,10},{14,8},{16,22},{18,... | collective-permute-start | bytes 393224 | tf_op jit(solution)/shard_map/ppermute | solution.py:427
  37.9 1.3 %collective-permute-start.10 = (bf16[256,256]{1,0:T(8,128)(2,1)S(1)}, bf16[256,256]{1,0:T(8,128)(2,1)S(1)}, u32[]{:S(2)}, u32[]{:S(2)}) collective-permute-start(bf16[256,256]{1,0:T(8,128)(2,1)S(1)} %get-tuple-element.124), channel_id=1, source_target_pairs={{0,4},{2,6},{4,0},{6,2},{8,12},{10,14},{12,8},{14,10},{16,20},{18,... | collective-permute-start | bytes 393224 | tf_op jit(solution)/shard_map/ppermute | solution.py:427
  39.2 0.0 collective-permute-done.13.refs_9_
  39.2 0.5 %collective-permute-start.11 = (bf16[256,256]{1,0:T(8,128)(2,1)S(1)}, bf16[256,256]{1,0:T(8,128)(2,1)S(1)}, u32[]{:S(2)}, u32[]{:S(2)}) collective-permute-start(bf16[256,256]{1,0:T(8,128)(2,1)S(1)} %get-tuple-element.125), channel_id=1, source_target_pairs={{0,2},{2,0},{4,6},{6,4},{8,10},{10,8},{12,14},{14,12},{16,18},{18,... | collective-permute-start | bytes 393224 | tf_op jit(solution)/shard_map/ppermute | solution.py:427
  39.7 2.1 %inner_terms.7 = (bf16[384,256]{1,0:T(8,128)(2,1)S(1)}, bf16[384,256]{1,0:T(8,128)(2,1)S(1)}, f32[384,128]{1,0:T(8,128)S(1)}, f32[384,128]{1,0:T(8,128)S(1)}) custom-call(bf16[384,128]{1,0:T(8,128)(2,1)S(1)} %get-tuple-element.82.refs_0_.b, bf16[384,128]{1,0:T(8,128)(2,1)S(1)} %get-tuple-element.83.refs_1_.c, ...), custom_call_target="tpu_custom_call" | custom-call | flops 805306368 | bytes 3145728 | tf_op jit(solution)/shard_map/inner_terms/pallas_call | solution.py:580
  41.8 0.0 collective-permute-done.15.refs_11_
  41.8 0.4 entry_values.1.refs_12_.refs_6_
  42.2 0.6 %entry_parts.3 = (f32[384,128]{1,0:T(8,128)S(1)}, f32[384,128]{1,0:T(8,128)S(1)}) custom-call(f32[384,128]{1,0:T(8,128)S(1)} %get-tuple-element.138.db_before, f32[384,128]{1,0:T(8,128)S(1)} %get-tuple-element.139.dc_before, bf16[384,256]{1,0:T(8,128)(2,1)S(1)} %get-tuple-element.140.refs_0_, bf16[384,256]{1,0:T(8,128)(2,1)S(1)} %get-tuple-element.141.refs_1_, ...), custom_call_target="tpu_custom_call" | custom-call | flops 301989888 | bytes 98304 | tf_op jit(solution)/shard_map/entry_parts/pallas_call | solution.py:617
  42.8 0.4 entry_parts.4
  43.2 0.6 %collective-permute-done.10.refs_10_.refs_4_ = bf16[256,256]{1,0:T(8,128)(2,1)S(1)} collective-permute-done((bf16[256,256]{1,0:T(8,128)(2,1)S(1)}, bf16[256,256]{1,0:T(8,128)(2,1)S(1)}, u32[]{:S(2)}, u32[]{:S(2)}) %collective-permute-start.10) | collective-permute-done | bytes 131104 | tf_op jit(solution)/shard_map/ppermute | solution.py:427
  43.8 0.4 collective-permute-done.11.refs_11_.refs_5_
  44.2 0.4 entry_parts.5.refs_0_
  44.5 0.1 collective-permute-start.16
  44.6 1.3 %last_values.1 = bf16[384,2048]{1,0:T(8,128)(2,1)} custom-call(s32[1]{0:T(128)} %bitcast.where, bf16[384,128]{1,0:T(8,128)(2,1)S(1)} %get-tuple-element.82.refs_0_.b, bf16[384,256]{1,0:T(8,128)(2,1)S(1)} %get-tuple-element.112.refs_0_, bf16[384,256]{1,0:T(8,128)(2,1)S(1)} %get-tuple-element.113.refs_1_, bf16[384,256]{1,0:T(8,128)(2,1)S(1)} %get-tuple-element.117.refs_2_, ...), custom_call_target="tpu_custom_call" | custom-call | flops 100663296 | bytes 1572864 | tf_op jit(solution)/shard_map/last_values/pallas_call | solution.py:691
  45.9 0.1 collective-permute-done.16.refs_1_
  46.0 0.7 %sum_over_heads.1 = (bf16[384,128]{1,0:T(8,128)(2,1)}, bf16[384,128]{1,0:T(8,128)(2,1)}) custom-call(bf16[768,128]{1,0:T(8,128)(2,1)S(1)} %entry_parts.5.refs_0_, bf16[768,128]{1,0:T(8,128)(2,1)S(1)} %collective-permute-done.16.refs_1_), custom_call_target="tpu_custom_call" | custom-call | flops 196608 | bytes 393216 | tf_op jit(solution)/shard_map/sum_over_heads/pallas_call | solution.py:723
  (5 shorter events, 0.1 us)
Async XLA Ops:
  3.3 11.3 %collective-permute-start = (bf16[272,256]{1,0:T(8,128)(2,1)S(1)}, bf16[272,256]{1,0:T(8,128)(2,1)S(1)}, u32[]{:S(2)}, u32[]{:S(2)}) collective-permute-start(bf16[272,256]{1,0:T(8,128)(2,1)S(1)} %get-tuple-element.101), channel_id=1, source_target_pairs={{0,6},{2,4},{4,2},{6,0},{8,14},{10,12},{12,10},{14,8},{16,22},{18,... | collective-permute-start | bytes 417800 | tf_op jit(solution)/shard_map/ppermute | solution.py:427
  7.3 7.9 %collective-permute-start.1 = (bf16[272,256]{1,0:T(8,128)(2,1)S(1)}, bf16[272,256]{1,0:T(8,128)(2,1)S(1)}, u32[]{:S(2)}, u32[]{:S(2)}) collective-permute-start(bf16[272,256]{1,0:T(8,128)(2,1)S(1)} %get-tuple-element.102), channel_id=1, source_target_pairs={{0,4},{2,6},{4,0},{6,2},{8,12},{10,14},{12,8},{14,10},{16,20},{18,... | collective-permute-start | bytes 417800 | tf_op jit(solution)/shard_map/ppermute | solution.py:427
  7.8 7.4 %collective-permute-start.2 = (bf16[272,256]{1,0:T(8,128)(2,1)S(1)}, bf16[272,256]{1,0:T(8,128)(2,1)S(1)}, u32[]{:S(2)}, u32[]{:S(2)}) collective-permute-start(bf16[272,256]{1,0:T(8,128)(2,1)S(1)} %get-tuple-element.103), channel_id=1, source_target_pairs={{0,2},{2,0},{4,6},{6,4},{8,10},{10,8},{12,14},{14,12},{16,18},{18,... | collective-permute-start | bytes 417800 | tf_op jit(solution)/shard_map/ppermute | solution.py:427
  11.1 7.6 %collective-permute-start.4 = (bf16[272,256]{1,0:T(8,128)(2,1)S(1)}, bf16[272,256]{1,0:T(8,128)(2,1)S(1)}, u32[]{:S(2)}, u32[]{:S(2)}) collective-permute-start(bf16[272,256]{1,0:T(8,128)(2,1)S(1)} %get-tuple-element.109), channel_id=1, source_target_pairs={{0,6},{2,4},{4,2},{6,0},{8,14},{10,12},{12,10},{14,8},{16,22},{18,... | collective-permute-start | bytes 417800 | tf_op jit(solution)/shard_map/ppermute | solution.py:427
  14.1 5.9 %collective-permute-start.5 = (bf16[272,256]{1,0:T(8,128)(2,1)S(1)}, bf16[272,256]{1,0:T(8,128)(2,1)S(1)}, u32[]{:S(2)}, u32[]{:S(2)}) collective-permute-start(bf16[272,256]{1,0:T(8,128)(2,1)S(1)} %get-tuple-element.110), channel_id=1, source_target_pairs={{0,4},{2,6},{4,0},{6,2},{8,12},{10,14},{12,8},{14,10},{16,20},{18,... | collective-permute-start | bytes 417800 | tf_op jit(solution)/shard_map/ppermute | solution.py:427
  14.6 5.6 %collective-permute-start.6 = (bf16[272,256]{1,0:T(8,128)(2,1)S(1)}, bf16[272,256]{1,0:T(8,128)(2,1)S(1)}, u32[]{:S(2)}, u32[]{:S(2)}) collective-permute-start(bf16[272,256]{1,0:T(8,128)(2,1)S(1)} %get-tuple-element.111), channel_id=1, source_target_pairs={{0,2},{2,0},{4,6},{6,4},{8,10},{10,8},{12,14},{14,12},{16,18},{18,... | collective-permute-start | bytes 417800 | tf_op jit(solution)/shard_map/ppermute | solution.py:427
  15.3 6.6 %collective-permute-start.3 = (bf16[272,256]{1,0:T(8,128)(2,1)S(1)}, bf16[272,256]{1,0:T(8,128)(2,1)S(1)}, u32[]{:S(2)}, u32[]{:S(2)}) collective-permute-start(bf16[272,256]{1,0:T(8,128)(2,1)S(1)} %totals.2.refs_11_.own), channel_id=1, source_target_pairs={{0,8},{2,10},{4,12},{6,14},{8,0},{10,2},{12,4},{14,6},{16,24},{18,... | collective-permute-start | bytes 417800 | tf_op jit(solution)/shard_map/ppermute | solution.py:756
  20.3 9.3 %collective-permute-start.7 = (bf16[272,256]{1,0:T(8,128)(2,1)S(1)}, bf16[272,256]{1,0:T(8,128)(2,1)S(1)}, u32[]{:S(2)}, u32[]{:S(2)}) collective-permute-start(bf16[272,256]{1,0:T(8,128)(2,1)S(1)} %totals.3.own), channel_id=1, source_target_pairs={{0,8},{2,10},{4,12},{6,14},{8,0},{10,2},{12,4},{14,6},{16,24},{18,... | collective-permute-start | bytes 417800 | tf_op jit(solution)/shard_map/ppermute | solution.py:756
  22.0 5.7 %collective-permute-start.12 = (bf16[128,256]{1,0:T(8,128)(2,1)S(1)}, bf16[128,256]{1,0:T(8,128)(2,1)S(1)}, u32[]{:S(2)}, u32[]{:S(2)}) collective-permute-start(bf16[128,256]{1,0:T(8,128)(2,1)S(1)} %merged.2.refs_13_), channel_id=1, source_target_pairs={{0,16},{2,18},{4,20},{6,22},{8,24},{10,26},{12,28},{14,30},{16,0},... | collective-permute-start | bytes 196616 | tf_op jit(solution)/shard_map/ppermute | solution.py:756
  27.9 11.3 %collective-permute-start.13 = (bf16[256,256]{1,0:T(8,128)(2,1)S(1)}, bf16[256,256]{1,0:T(8,128)(2,1)S(1)}, u32[]{:S(2)}, u32[]{:S(2)}) collective-permute-start(bf16[256,256]{1,0:T(8,128)(2,1)S(1)} %get-tuple-element.135), channel_id=1, source_target_pairs={{0,6},{2,4},{4,2},{6,0},{8,14},{10,12},{12,10},{14,8},{16,22},{18,... | collective-permute-start | bytes 393224 | tf_op jit(solution)/shard_map/ppermute | solution.py:427
  29.7 6.0 %collective-permute-start.8 = (bf16[128,256]{1,0:T(8,128)(2,1)S(1)}, bf16[128,256]{1,0:T(8,128)(2,1)S(1)}, u32[]{:S(2)}, u32[]{:S(2)}) collective-permute-start(bf16[128,256]{1,0:T(8,128)(2,1)S(1)} %merged.3.refs_13_), channel_id=1, source_target_pairs={{0,16},{2,18},{4,20},{6,22},{8,24},{10,26},{12,28},{14,30},{16,0},... | collective-permute-start | bytes 196616 | tf_op jit(solution)/shard_map/ppermute | solution.py:756
  31.9 9.8 %collective-permute-start.14 = (bf16[256,256]{1,0:T(8,128)(2,1)S(1)}, bf16[256,256]{1,0:T(8,128)(2,1)S(1)}, u32[]{:S(2)}, u32[]{:S(2)}) collective-permute-start(bf16[256,256]{1,0:T(8,128)(2,1)S(1)} %get-tuple-element.136), channel_id=1, source_target_pairs={{0,4},{2,6},{4,0},{6,2},{8,12},{10,14},{12,8},{14,10},{16,20},{18,... | collective-permute-start | bytes 393224 | tf_op jit(solution)/shard_map/ppermute | solution.py:427
  33.2 8.6 %collective-permute-start.15 = (bf16[256,256]{1,0:T(8,128)(2,1)S(1)}, bf16[256,256]{1,0:T(8,128)(2,1)S(1)}, u32[]{:S(2)}, u32[]{:S(2)}) collective-permute-start(bf16[256,256]{1,0:T(8,128)(2,1)S(1)} %get-tuple-element.137), channel_id=1, source_target_pairs={{0,2},{2,0},{4,6},{6,4},{8,10},{10,8},{12,14},{14,12},{16,18},{18,... | collective-permute-start | bytes 393224 | tf_op jit(solution)/shard_map/ppermute | solution.py:427
  36.1 6.7 %collective-permute-start.9 = (bf16[256,256]{1,0:T(8,128)(2,1)S(1)}, bf16[256,256]{1,0:T(8,128)(2,1)S(1)}, u32[]{:S(2)}, u32[]{:S(2)}) collective-permute-start(bf16[256,256]{1,0:T(8,128)(2,1)S(1)} %get-tuple-element.123), channel_id=1, source_target_pairs={{0,6},{2,4},{4,2},{6,0},{8,14},{10,12},{12,10},{14,8},{16,22},{18,... | collective-permute-start | bytes 393224 | tf_op jit(solution)/shard_map/ppermute | solution.py:427
  37.9 5.9 %collective-permute-start.10 = (bf16[256,256]{1,0:T(8,128)(2,1)S(1)}, bf16[256,256]{1,0:T(8,128)(2,1)S(1)}, u32[]{:S(2)}, u32[]{:S(2)}) collective-permute-start(bf16[256,256]{1,0:T(8,128)(2,1)S(1)} %get-tuple-element.124), channel_id=1, source_target_pairs={{0,4},{2,6},{4,0},{6,2},{8,12},{10,14},{12,8},{14,10},{16,20},{18,... | collective-permute-start | bytes 393224 | tf_op jit(solution)/shard_map/ppermute | solution.py:427
  39.2 5.0 %collective-permute-start.11 = (bf16[256,256]{1,0:T(8,128)(2,1)S(1)}, bf16[256,256]{1,0:T(8,128)(2,1)S(1)}, u32[]{:S(2)}, u32[]{:S(2)}) collective-permute-start(bf16[256,256]{1,0:T(8,128)(2,1)S(1)} %get-tuple-element.125), channel_id=1, source_target_pairs={{0,2},{2,0},{4,6},{6,4},{8,10},{10,8},{12,14},{14,12},{16,18},{18,... | collective-permute-start | bytes 393224 | tf_op jit(solution)/shard_map/ppermute | solution.py:427
  44.5 1.5 %collective-permute-start.16 = (bf16[768,128]{1,0:T(8,128)(2,1)S(1)}, bf16[768,128]{1,0:T(8,128)(2,1)S(1)}, u32[]{:S(2)}, u32[]{:S(2)}) collective-permute-start(bf16[768,128]{1,0:T(8,128)(2,1)S(1)} %entry_parts.5.refs_0_), channel_id=1, source_target_pairs={{0,1},{1,0},{2,3},{3,2},{4,5},{5,4},{6,7},{7,6},{8,9},{9,8},{10,11... | collective-permute-start | bytes 589832 | tf_op jit(solution)/shard_map/ppermute | solution.py:722

commit v18 on v17

--- a/solution.py
+++ b/solution.py
@@ -118,7 +118,7 @@
     return into_end, from_start, halves
 
 
-def put_states(head_dim, chunks, pieces, where, operands, outs, ready):
+def put_states(head_dim, pieces, where, operands, outs, ready):
     into_end, from_start, halves, b, c, xs, dys = operands
     state, part = b.shape[1], xs[0].shape[1] // GROUP
     difference = row_less_head(head_dim, part)
@@ -150,7 +150,7 @@
     return copy
 
 
-def first_states_kernel(head_dim, chunks, pieces, where, ld_in, b_in, c_in, x_in, dy_in, *refs):
+def first_states_kernel(head_dim, pieces, where, ld_in, b_in, c_in, x_in, dy_in, *refs):
     ld, b, c, x, dy, into_end, from_start, halves = refs[:8]
     outs, sems = refs[8:-1], refs[-1]
 
@@ -175,12 +175,12 @@
             copy.wait()
 
     operands = (*factors, b, c, {0: x}, {0: dy})
-    put_states(head_dim, chunks, pieces, where, operands, outs, ready)
-
-
-def next_states_kernel(head_dim, chunks, pieces, where, into_end, from_start, halves, *refs):
-    b, c, x, dy, x_in, dy_in = refs[:6]
-    outs, sems = refs[6:-1], refs[-1]
+    put_states(head_dim, pieces, where, operands, outs, ready)
+
+
+def next_states_kernel(head_dim, chunks, pieces, n_setup, where, into_end, from_start, halves, *refs):
+    ld, b, c, x, dy, x_in, dy_in = refs[:7]
+    setup, outs, sems = refs[7 : 7 + n_setup], refs[7 + n_setup : -1], refs[-1]
     kept, outs = outs[: 2 * (chunks - 1)], outs[2 * (chunks - 1) :]
     xs, dys, copies = {0: x}, {0: dy}, {}
     for chunk in range(1, chunks):
@@ -192,8 +192,10 @@
         if (side, chunk) in copies:
             copies[side, chunk].wait()
 
+    put_setup(head_dim, ld, b, c, *setup)
     operands = (into_end[...], from_start[...], halves[...], b, c, xs, dys)
-    put_states(head_dim, chunks, pieces, where, operands, outs, ready)
+    put_states(head_dim, pieces[:1], where, operands, outs[:4], ready)
+    put_states(head_dim, pieces[1:], where, operands, outs[4:], ready)
 
 
 def states_shapes(n_parts, length, width, state):
@@ -216,7 +218,7 @@
     kept += [jax.ShapeDtypeStruct((rows, LANES), BF16) for rows in (length, length, TAIL)]
     outs = kept + states_shapes(len(pieces), length, width, state)
     found = pl.pallas_call(
-        functools.partial(first_states_kernel, head_dim, chunks, pieces),
+        functools.partial(first_states_kernel, head_dim, pieces),
         out_shape=outs,
         in_specs=[SMEM] + [HBM] * 5,
         out_specs=whole(len(outs)),
@@ -228,23 +230,25 @@
     return found[:8], by_piece(pieces, found[8:])
 
 
-def next_states(head_dim, pieces, where, factors, b, c, x_0, dy_0, x, dy):
+def next_states(head_dim, pieces, where, factors, ld, b, c, x_0, dy_0, x, dy):
     (length, width), state = x.shape, b.shape[1]
     chunks = chunk_count(width)
     n_kept = 2 * (chunks - 1)
-    outs = [jax.ShapeDtypeStruct(x_0.shape, BF16)] * n_kept
+    setup = setup_shapes(head_dim, length)
+    outs = setup + [jax.ShapeDtypeStruct(x_0.shape, BF16)] * n_kept
     outs += states_shapes(len(pieces), length, width, state)
     found = pl.pallas_call(
-        functools.partial(next_states_kernel, head_dim, chunks, pieces),
+        functools.partial(next_states_kernel, head_dim, chunks, pieces, len(setup)),
         out_shape=outs,
-        in_specs=[SMEM] + whole(7) + [HBM] * 2,
+        in_specs=[SMEM] + whole(8) + [HBM] * 2,
         out_specs=whole(len(outs)),
         scratch_shapes=[pltpu.SemaphoreType.DMA((max(n_kept, 1),))],
         compiler_params=params(8),
         cost_estimate=cost(2 * length * width * (state + LANES), 4 * length * width),
         name="next_states",
-    )(where, *factors, b, c, x_0, dy_0, *in_hbm(x, dy))
-    return found[:n_kept], by_piece(pieces, found[n_kept:])
+    )(where, *factors, ld, b, c, x_0, dy_0, *in_hbm(x, dy))
+    setup, found = found[: len(setup)], found[len(setup) :]
+    return setup, found[:n_kept], by_piece(pieces, found[n_kept:])
 
 
 def decay_of(tail):
@@ -450,7 +454,7 @@
     return slice(first * piece, end * piece)
 
 
-def setup_kernel(piece, ld, b, c, *refs):
+def put_setup(piece, ld, b, c, *refs):
     near, cum_terms = refs[-2:]
     heads, length = ld.shape
     rows, other = iota((length, length), 0), iota((length, length), 1)
@@ -472,27 +476,11 @@
         far[...] = dot(b[left, :], c[right, :], NT).astype(BF16)
 
 
-def inner_setup(piece, ld, b, c, after):
-    length = b.shape[0]
+def setup_shapes(piece, length):
     cuts = [cut for _, same in grouped_cuts(length // piece) for cut in same]
-    outs = [
-        jax.ShapeDtypeStruct(((mid - lo) * piece, (hi - mid) * piece), BF16) for lo, mid, hi in cuts
-    ]
-    outs.append(jax.ShapeDtypeStruct((length, piece), BF16))
-    outs.append(jax.ShapeDtypeStruct((length, LANES), BF16))
-    return pl.pallas_call(
-        functools.partial(setup_kernel_after, piece, len(after)),
-        out_shape=outs,
-        in_specs=whole(3) + [ANY] * len(after),
-        out_specs=whole(len(outs)),
-        compiler_params=params(4),
-        cost_estimate=cost(8 * b.size * length, 8 * b.size),
-        name="inner_setup",
-    )(ld, b, c, *after)
-
-
-def setup_kernel_after(piece, n_after, ld, b, c, *refs):
-    setup_kernel(piece, ld, b, c, *refs[n_after:])
+    sizes = [((mid - lo) * piece, (hi - mid) * piece) for lo, mid, hi in cuts]
+    sizes += [(length, piece), (length, LANES)]
+    return [jax.ShapeDtypeStruct(size, BF16) for size in sizes]
 
 
 def inner_kernel(head_dim, worked, chunks, n_before, n_after, b, c, *refs):
@@ -744,13 +732,12 @@
     ld, b, c, x_0, dy_0, *factors = kept
     late = order[group - 1 :]
     columns = (x_0, dy_0, token_values, grad_out)
-    more, found = next_states(head_dim, late, where, factors, b, c, *columns)
+    setup, more, found = next_states(head_dim, late, where, factors, ld, b, c, *columns)
     states.update(found)
     xs, dys = [x_0, *more[::2]], [dy_0, *more[1::2]]
     blocks = [
         exchange([states[chunk, k][3] for k in range(group)]) for chunk in range(chunks)
     ]
-    setup = inner_setup(head_dim, ld, b, c, [states[late[-1]][0]])
 
     def to_group(block, k):
         return lax.ppermute(block, "seq", [(s, s ^ (k * group)) for s in range(count)])

time: 46.9 us -> 47.2 us (level)
    pallas_call x2 -> x1, Pallas kernels: 3.12 us -> 2.67 us  [first_states(): pl.pallas_call(functools.partial(first_states_kernel, head_dim, pieces),...]
where the time goes in v18:
time: 47.2 us; the launch traced here: 47 us
  starting transfers between devices  23.8 us (50%)
  Pallas kernels  19.5 us (41%)
  waiting for transfers between devices  2.93 us (6%)
  between operations  0.82 us (2%)
    ppermute x12, starting transfers between devices, exchange(): out[k] = lax.ppermute(parts[k], 'seq', [(s, s ^ k) for s in range(count)])  15.2 us
    pallas_call x4, Pallas kernels, inner_terms(): pl.pallas_call(functools.partial(inner_kernel, head_dim, worked, chunks,...  8.61 us
    ppermute x4, starting transfers between devices, to_group(): lax.ppermute(block, 'seq', [(s, s ^ k * group) for s in range(count)])  8.46 us
    pallas_call x1, Pallas kernels, next_states(): pl.pallas_call(functools.partial(next_states_kernel, head_dim, chunks, pi...  3.58 us
    ppermute x12, waiting for transfers between devices, exchange(): out[k] = lax.ppermute(parts[k], 'seq', [(s, s ^ k) for s in range(count)])  2.83 us
    pallas_call x1, Pallas kernels, first_states(): pl.pallas_call(functools.partial(first_states_kernel, head_dim, pieces),...  2.67 us
    pallas_call x1, Pallas kernels, entry_values(): pl.pallas_call(functools.partial(last_values_kernel, chunks), out_shape=p...  1.33 us
    pallas_call x3, Pallas kernels, entry_parts(): pl.pallas_call(functools.partial(parts_kernel, last, ks), out_shape=outs,...  1.31 us
  transfers between devices with their start and end apart: 17, of which 5 were waited for; matrix products, arithmetic and copies ran while one was open for 0% of the time, Pallas kernels for 34%

profile of v18, /device:TPU:0, one launch (start us, length us, event | category | flops | bytes accessed | tf_op | source)
XLA Modules:
  0.0 47.0 jit_solution(5008803727251875636)
XLA Ops:
  0.6 2.7 %first_states.1 = (f32[32,384]{1,0:T(8,128)S(1)}, bf16[384,128]{1,0:T(8,128)(2,1)S(1)}, bf16[384,128]{1,0:T(8,128)(2,1)S(1)}, bf16[384,1024]{1,0:T(8,128)(2,1)S(...) custom-call(s32[1]{0:T(128)} %bitcast.where, ...), custom_call_target="tpu_custom_call" | custom-call | flops 402653184 | bytes 6291456 | tf_op jit(solution)/shard_map/first_states/pallas_call | solution.py:220
  3.3 4.0 %collective-permute-start = (bf16[272,256]{1,0:T(8,128)(2,1)S(1)}, bf16[272,256]{1,0:T(8,128)(2,1)S(1)}, u32[]{:S(2)}, u32[]{:S(2)}) collective-permute-start(bf16[272,256]{1,0:T(8,128)(2,1)S(1)} %get-tuple-element.100), channel_id=1, source_target_pairs={{0,6},{2,4},{4,2},{6,0},{8,14},{10,12},{12,10},{14,8},{16,22},{18,... | collective-permute-start | bytes 417800 | tf_op jit(solution)/shard_map/ppermute | solution.py:431
  7.3 0.5 %collective-permute-start.1 = (bf16[272,256]{1,0:T(8,128)(2,1)S(1)}, bf16[272,256]{1,0:T(8,128)(2,1)S(1)}, u32[]{:S(2)}, u32[]{:S(2)}) collective-permute-start(bf16[272,256]{1,0:T(8,128)(2,1)S(1)} %get-tuple-element.101), channel_id=1, source_target_pairs={{0,4},{2,6},{4,0},{6,2},{8,12},{10,14},{12,8},{14,10},{16,20},{18,... | collective-permute-start | bytes 417800 | tf_op jit(solution)/shard_map/ppermute | solution.py:431
  7.8 0.1 collective-permute-start.2
  7.9 3.6 %next_states.1 = (bf16[192,192]{1,0:T(8,128)(2,1)S(1)}, bf16[64,128]{1,0:T(8,128)(2,1)S(1)}, bf16[64,128]{1,0:T(8,128)(2,1)S(1)}, bf16[64,64]{1,0:T(8,128)(2,1)S...) custom-call(s32[1]{0:T(128)} %bitcast.where, ...), custom_call_target="tpu_custom_call" | custom-call | flops 402653184 | bytes 3145728 | tf_op jit(solution)/shard_map/next_states/pallas_call | solution.py:240
  11.5 2.9 %collective-permute-start.4 = (bf16[272,256]{1,0:T(8,128)(2,1)S(1)}, bf16[272,256]{1,0:T(8,128)(2,1)S(1)}, u32[]{:S(2)}, u32[]{:S(2)}) collective-permute-start(bf16[272,256]{1,0:T(8,128)(2,1)S(1)} %get-tuple-element.108), channel_id=1, source_target_pairs={{0,6},{2,4},{4,2},{6,0},{8,14},{10,12},{12,10},{14,8},{16,22},{18,... | collective-permute-start | bytes 417800 | tf_op jit(solution)/shard_map/ppermute | solution.py:431
  14.4 0.5 %collective-permute-start.5 = (bf16[272,256]{1,0:T(8,128)(2,1)S(1)}, bf16[272,256]{1,0:T(8,128)(2,1)S(1)}, u32[]{:S(2)}, u32[]{:S(2)}) collective-permute-start(bf16[272,256]{1,0:T(8,128)(2,1)S(1)} %get-tuple-element.109), channel_id=1, source_target_pairs={{0,4},{2,6},{4,0},{6,2},{8,12},{10,14},{12,8},{14,10},{16,20},{18,... | collective-permute-start | bytes 417800 | tf_op jit(solution)/shard_map/ppermute | solution.py:431
  14.9 0.0 collective-permute-done.refs_1_.refs_5_
  14.9 0.1 collective-permute-start.6
  15.1 0.0 collective-permute-done.1.refs_2_.refs_4_
  15.1 0.0 collective-permute-done.2.refs_3_
  15.1 0.1 totals.2.refs_11_.own
  15.2 2.0 %collective-permute-start.3 = (bf16[272,256]{1,0:T(8,128)(2,1)S(1)}, bf16[272,256]{1,0:T(8,128)(2,1)S(1)}, u32[]{:S(2)}, u32[]{:S(2)}) collective-permute-start(bf16[272,256]{1,0:T(8,128)(2,1)S(1)} %totals.2.refs_11_.own), channel_id=1, source_target_pairs={{0,8},{2,10},{4,12},{6,14},{8,0},{10,2},{12,4},{14,6},{16,24},{18,... | collective-permute-start | bytes 417800 | tf_op jit(solution)/shard_map/ppermute | solution.py:743
  17.2 1.4 %inner_terms.4 = (bf16[384,256]{1,0:T(8,128)(2,1)S(1)}, f32[384,128]{1,0:T(8,128)S(1)}, f32[384,128]{1,0:T(8,128)S(1)}) custom-call(bf16[384,128]{1,0:T(8,128)(2,1)S(1)} %get-tuple-element.82.refs_1_.b, bf16[384,128]{1,0:T(8,128)(2,1)S(1)} %get-tuple-element.83.refs_2_.c, bf16[384,1024]{1,0:T(8,128)(2,1)S(1)} %get-tuple-element.84.refs_3_.refs_0_, ...), custom_call_target="tpu_custom_call" | custom-call | flops 1 | bytes 1 | tf_op jit(solution)/shard_map/inner_terms/pallas_call | solution.py:568
  18.6 0.0 collective-permute-done.4.refs_1_.refs_5_
  18.6 1.7 %collective-permute-done.5.refs_2_.refs_4_ = bf16[272,256]{1,0:T(8,128)(2,1)S(1)} collective-permute-done((bf16[272,256]{1,0:T(8,128)(2,1)S(1)}, bf16[272,256]{1,0:T(8,128)(2,1)S(1)}, u32[]{:S(2)}, u32[]{:S(2)}) %collective-permute-start.5) | collective-permute-done | bytes 139296 | tf_op jit(solution)/shard_map/ppermute | solution.py:431
  20.3 0.2 collective-permute-done.6.refs_3_
  20.5 0.1 totals.3.own
  20.6 1.6 %collective-permute-start.7 = (bf16[272,256]{1,0:T(8,128)(2,1)S(1)}, bf16[272,256]{1,0:T(8,128)(2,1)S(1)}, u32[]{:S(2)}, u32[]{:S(2)}) collective-permute-start(bf16[272,256]{1,0:T(8,128)(2,1)S(1)} %totals.3.own), channel_id=1, source_target_pairs={{0,8},{2,10},{4,12},{6,14},{8,0},{10,2},{12,4},{14,6},{16,24},{18,... | collective-permute-start | bytes 417800 | tf_op jit(solution)/shard_map/ppermute | solution.py:743
  22.3 2.6 %collective-permute-start.12 = (bf16[128,256]{1,0:T(8,128)(2,1)S(1)}, bf16[128,256]{1,0:T(8,128)(2,1)S(1)}, u32[]{:S(2)}, u32[]{:S(2)}) collective-permute-start(bf16[128,256]{1,0:T(8,128)(2,1)S(1)} %merged.2.refs_13_), channel_id=1, source_target_pairs={{0,16},{2,18},{4,20},{6,22},{8,24},{10,26},{12,28},{14,30},{16,0},... | collective-permute-start | bytes 196616 | tf_op jit(solution)/shard_map/ppermute | solution.py:743
  24.9 3.1 %inner_terms.5 = (bf16[384,256]{1,0:T(8,128)(2,1)S(1)}, bf16[384,256]{1,0:T(8,128)(2,1)S(1)}, bf16[384,256]{1,0:T(8,128)(2,1)S(1)}, f32[384,128]{1,0:T(8,128)S(1)}, f32[384,128]{1,0:T(8,128)S(1)}) custom-call(bf16[384,128]{1,0:T(8,128)(2,1)S(1)} %get-tuple-element.82.refs_1_.b, bf16[384,128]{1,0:T(8,128)(2,1)S(1)} %get-tuple-element.83.refs_2_.c, ...), custom_call_target="tpu_custom_call" | custom-call | flops 805306368 | bytes 3145728 | tf_op jit(solution)/shard_map/inner_terms/pallas_call | solution.py:568
  28.0 0.0 collective-permute-done.12.refs_1_
  28.0 0.2 member_entries.3
  28.2 1.7 %collective-permute-start.13 = (bf16[256,256]{1,0:T(8,128)(2,1)S(1)}, bf16[256,256]{1,0:T(8,128)(2,1)S(1)}, u32[]{:S(2)}, u32[]{:S(2)}) collective-permute-start(bf16[256,256]{1,0:T(8,128)(2,1)S(1)} %get-tuple-element.134), channel_id=1, source_target_pairs={{0,6},{2,4},{4,2},{6,0},{8,14},{10,12},{12,10},{14,8},{16,22},{18,... | collective-permute-start | bytes 393224 | tf_op jit(solution)/shard_map/ppermute | solution.py:431
  30.0 0.0 collective-permute-done.7.received.refs_0_
  30.0 2.1 %collective-permute-start.8 = (bf16[128,256]{1,0:T(8,128)(2,1)S(1)}, bf16[128,256]{1,0:T(8,128)(2,1)S(1)}, u32[]{:S(2)}, u32[]{:S(2)}) collective-permute-start(bf16[128,256]{1,0:T(8,128)(2,1)S(1)} %merged.3.refs_13_), channel_id=1, source_target_pairs={{0,16},{2,18},{4,20},{6,22},{8,24},{10,26},{12,28},{14,30},{16,0},... | collective-permute-start | bytes 196616 | tf_op jit(solution)/shard_map/ppermute | solution.py:743
  32.2 1.3 %collective-permute-start.14 = (bf16[256,256]{1,0:T(8,128)(2,1)S(1)}, bf16[256,256]{1,0:T(8,128)(2,1)S(1)}, u32[]{:S(2)}, u32[]{:S(2)}) collective-permute-start(bf16[256,256]{1,0:T(8,128)(2,1)S(1)} %get-tuple-element.135), channel_id=1, source_target_pairs={{0,4},{2,6},{4,0},{6,2},{8,12},{10,14},{12,8},{14,10},{16,20},{18,... | collective-permute-start | bytes 393224 | tf_op jit(solution)/shard_map/ppermute | solution.py:431
  33.5 0.5 %collective-permute-start.15 = (bf16[256,256]{1,0:T(8,128)(2,1)S(1)}, bf16[256,256]{1,0:T(8,128)(2,1)S(1)}, u32[]{:S(2)}, u32[]{:S(2)}) collective-permute-start(bf16[256,256]{1,0:T(8,128)(2,1)S(1)} %get-tuple-element.136), channel_id=1, source_target_pairs={{0,2},{2,0},{4,6},{6,4},{8,10},{10,8},{12,14},{14,12},{16,18},{18,... | collective-permute-start | bytes 393224 | tf_op jit(solution)/shard_map/ppermute | solution.py:431
  34.0 2.1 %inner_terms.6 = (bf16[384,256]{1,0:T(8,128)(2,1)S(1)}, bf16[384,256]{1,0:T(8,128)(2,1)S(1)}, f32[384,128]{1,0:T(8,128)S(1)}, f32[384,128]{1,0:T(8,128)S(1)}) custom-call(bf16[384,128]{1,0:T(8,128)(2,1)S(1)} %get-tuple-element.82.refs_1_.b, bf16[384,128]{1,0:T(8,128)(2,1)S(1)} %get-tuple-element.83.refs_2_.c, ...), custom_call_target="tpu_custom_call" | custom-call | flops 805306368 | bytes 3145728 | tf_op jit(solution)/shard_map/inner_terms/pallas_call | solution.py:568
  36.0 0.0 collective-permute-done.8.refs_1_
  36.1 0.4 member_entries.2
  36.4 1.8 %collective-permute-start.9 = (bf16[256,256]{1,0:T(8,128)(2,1)S(1)}, bf16[256,256]{1,0:T(8,128)(2,1)S(1)}, u32[]{:S(2)}, u32[]{:S(2)}) collective-permute-start(bf16[256,256]{1,0:T(8,128)(2,1)S(1)} %get-tuple-element.122), channel_id=1, source_target_pairs={{0,6},{2,4},{4,2},{6,0},{8,14},{10,12},{12,10},{14,8},{16,22},{18,... | collective-permute-start | bytes 393224 | tf_op jit(solution)/shard_map/ppermute | solution.py:431
  38.2 1.3 %collective-permute-start.10 = (bf16[256,256]{1,0:T(8,128)(2,1)S(1)}, bf16[256,256]{1,0:T(8,128)(2,1)S(1)}, u32[]{:S(2)}, u32[]{:S(2)}) collective-permute-start(bf16[256,256]{1,0:T(8,128)(2,1)S(1)} %get-tuple-element.123), channel_id=1, source_target_pairs={{0,4},{2,6},{4,0},{6,2},{8,12},{10,14},{12,8},{14,10},{16,20},{18,... | collective-permute-start | bytes 393224 | tf_op jit(solution)/shard_map/ppermute | solution.py:431
  39.5 0.0 collective-permute-done.13.refs_9_
  39.5 0.5 %collective-permute-start.11 = (bf16[256,256]{1,0:T(8,128)(2,1)S(1)}, bf16[256,256]{1,0:T(8,128)(2,1)S(1)}, u32[]{:S(2)}, u32[]{:S(2)}) collective-permute-start(bf16[256,256]{1,0:T(8,128)(2,1)S(1)} %get-tuple-element.124), channel_id=1, source_target_pairs={{0,2},{2,0},{4,6},{6,4},{8,10},{10,8},{12,14},{14,12},{16,18},{18,... | collective-permute-start | bytes 393224 | tf_op jit(solution)/shard_map/ppermute | solution.py:431
  40.0 2.1 %inner_terms.7 = (bf16[384,256]{1,0:T(8,128)(2,1)S(1)}, bf16[384,256]{1,0:T(8,128)(2,1)S(1)}, f32[384,128]{1,0:T(8,128)S(1)}, f32[384,128]{1,0:T(8,128)S(1)}) custom-call(bf16[384,128]{1,0:T(8,128)(2,1)S(1)} %get-tuple-element.82.refs_1_.b, bf16[384,128]{1,0:T(8,128)(2,1)S(1)} %get-tuple-element.83.refs_2_.c, ...), custom_call_target="tpu_custom_call" | custom-call | flops 805306368 | bytes 3145728 | tf_op jit(solution)/shard_map/inner_terms/pallas_call | solution.py:568
  42.1 0.0 collective-permute-done.14.refs_10_
  42.1 0.4 entry_values.1.refs_12_.refs_6_
  42.5 0.6 %entry_parts.3 = (f32[384,128]{1,0:T(8,128)S(1)}, f32[384,128]{1,0:T(8,128)S(1)}) custom-call(f32[384,128]{1,0:T(8,128)S(1)} %get-tuple-element.137.db_before, f32[384,128]{1,0:T(8,128)S(1)} %get-tuple-element.138.dc_before, bf16[384,256]{1,0:T(8,128)(2,1)S(1)} %get-tuple-element.139.refs_0_, bf16[384,256]{1,0:T(8,128)(2,1)S(1)} %get-tuple-element.140.refs_1_, ...), custom_call_target="tpu_custom_call" | custom-call | flops 301989888 | bytes 98304 | tf_op jit(solution)/shard_map/entry_parts/pallas_call | solution.py:605
  43.1 0.0 collective-permute-done.9.refs_9_.refs_5_
  43.1 0.4 entry_parts.4
  43.5 0.6 %collective-permute-done.10.refs_10_.refs_4_ = bf16[256,256]{1,0:T(8,128)(2,1)S(1)} collective-permute-done((bf16[256,256]{1,0:T(8,128)(2,1)S(1)}, bf16[256,256]{1,0:T(8,128)(2,1)S(1)}, u32[]{:S(2)}, u32[]{:S(2)}) %collective-permute-start.10) | collective-permute-done | bytes 131104 | tf_op jit(solution)/shard_map/ppermute | solution.py:431
  44.1 0.4 collective-permute-done.11.refs_11_.refs_5_
  44.5 0.4 entry_parts.5.refs_0_
  44.8 0.1 collective-permute-start.16
  44.9 1.3 %last_values.1 = bf16[384,2048]{1,0:T(8,128)(2,1)} custom-call(s32[1]{0:T(128)} %bitcast.where, bf16[384,128]{1,0:T(8,128)(2,1)S(1)} %get-tuple-element.82.refs_1_.b, bf16[384,256]{1,0:T(8,128)(2,1)S(1)} %get-tuple-element.111.refs_0_, bf16[384,256]{1,0:T(8,128)(2,1)S(1)} %get-tuple-element.112.refs_1_, bf16[384,256]{1,0:T(8,128)(2,1)S(1)} %get-tuple-element.116.refs_2_, ...), custom_call_target="tpu_custom_call" | custom-call | flops 100663296 | bytes 1572864 | tf_op jit(solution)/shard_map/last_values/pallas_call | solution.py:679
  46.2 0.1 collective-permute-done.16.refs_1_
  46.3 0.7 %sum_over_heads.1 = (bf16[384,128]{1,0:T(8,128)(2,1)}, bf16[384,128]{1,0:T(8,128)(2,1)}) custom-call(bf16[768,128]{1,0:T(8,128)(2,1)S(1)} %entry_parts.5.refs_0_, bf16[768,128]{1,0:T(8,128)(2,1)S(1)} %collective-permute-done.16.refs_1_), custom_call_target="tpu_custom_call" | custom-call | flops 196608 | bytes 393216 | tf_op jit(solution)/shard_map/sum_over_heads/pallas_call | solution.py:711
  (4 shorter events, 0.1 us)
Async XLA Ops:
  3.3 11.6 %collective-permute-start = (bf16[272,256]{1,0:T(8,128)(2,1)S(1)}, bf16[272,256]{1,0:T(8,128)(2,1)S(1)}, u32[]{:S(2)}, u32[]{:S(2)}) collective-permute-start(bf16[272,256]{1,0:T(8,128)(2,1)S(1)} %get-tuple-element.100), channel_id=1, source_target_pairs={{0,6},{2,4},{4,2},{6,0},{8,14},{10,12},{12,10},{14,8},{16,22},{18,... | collective-permute-start | bytes 417800 | tf_op jit(solution)/shard_map/ppermute | solution.py:431
  7.3 7.8 %collective-permute-start.1 = (bf16[272,256]{1,0:T(8,128)(2,1)S(1)}, bf16[272,256]{1,0:T(8,128)(2,1)S(1)}, u32[]{:S(2)}, u32[]{:S(2)}) collective-permute-start(bf16[272,256]{1,0:T(8,128)(2,1)S(1)} %get-tuple-element.101), channel_id=1, source_target_pairs={{0,4},{2,6},{4,0},{6,2},{8,12},{10,14},{12,8},{14,10},{16,20},{18,... | collective-permute-start | bytes 417800 | tf_op jit(solution)/shard_map/ppermute | solution.py:431
  7.8 7.3 %collective-permute-start.2 = (bf16[272,256]{1,0:T(8,128)(2,1)S(1)}, bf16[272,256]{1,0:T(8,128)(2,1)S(1)}, u32[]{:S(2)}, u32[]{:S(2)}) collective-permute-start(bf16[272,256]{1,0:T(8,128)(2,1)S(1)} %get-tuple-element.102), channel_id=1, source_target_pairs={{0,2},{2,0},{4,6},{6,4},{8,10},{10,8},{12,14},{14,12},{16,18},{18,... | collective-permute-start | bytes 417800 | tf_op jit(solution)/shard_map/ppermute | solution.py:431
  11.5 7.1 %collective-permute-start.4 = (bf16[272,256]{1,0:T(8,128)(2,1)S(1)}, bf16[272,256]{1,0:T(8,128)(2,1)S(1)}, u32[]{:S(2)}, u32[]{:S(2)}) collective-permute-start(bf16[272,256]{1,0:T(8,128)(2,1)S(1)} %get-tuple-element.108), channel_id=1, source_target_pairs={{0,6},{2,4},{4,2},{6,0},{8,14},{10,12},{12,10},{14,8},{16,22},{18,... | collective-permute-start | bytes 417800 | tf_op jit(solution)/shard_map/ppermute | solution.py:431
  14.4 5.9 %collective-permute-start.5 = (bf16[272,256]{1,0:T(8,128)(2,1)S(1)}, bf16[272,256]{1,0:T(8,128)(2,1)S(1)}, u32[]{:S(2)}, u32[]{:S(2)}) collective-permute-start(bf16[272,256]{1,0:T(8,128)(2,1)S(1)} %get-tuple-element.109), channel_id=1, source_target_pairs={{0,4},{2,6},{4,0},{6,2},{8,12},{10,14},{12,8},{14,10},{16,20},{18,... | collective-permute-start | bytes 417800 | tf_op jit(solution)/shard_map/ppermute | solution.py:431
  14.9 5.6 %collective-permute-start.6 = (bf16[272,256]{1,0:T(8,128)(2,1)S(1)}, bf16[272,256]{1,0:T(8,128)(2,1)S(1)}, u32[]{:S(2)}, u32[]{:S(2)}) collective-permute-start(bf16[272,256]{1,0:T(8,128)(2,1)S(1)} %get-tuple-element.110), channel_id=1, source_target_pairs={{0,2},{2,0},{4,6},{6,4},{8,10},{10,8},{12,14},{14,12},{16,18},{18,... | collective-permute-start | bytes 417800 | tf_op jit(solution)/shard_map/ppermute | solution.py:431
  15.2 7.1 %collective-permute-start.3 = (bf16[272,256]{1,0:T(8,128)(2,1)S(1)}, bf16[272,256]{1,0:T(8,128)(2,1)S(1)}, u32[]{:S(2)}, u32[]{:S(2)}) collective-permute-start(bf16[272,256]{1,0:T(8,128)(2,1)S(1)} %totals.2.refs_11_.own), channel_id=1, source_target_pairs={{0,8},{2,10},{4,12},{6,14},{8,0},{10,2},{12,4},{14,6},{16,24},{18,... | collective-permute-start | bytes 417800 | tf_op jit(solution)/shard_map/ppermute | solution.py:743
  20.6 9.4 %collective-permute-start.7 = (bf16[272,256]{1,0:T(8,128)(2,1)S(1)}, bf16[272,256]{1,0:T(8,128)(2,1)S(1)}, u32[]{:S(2)}, u32[]{:S(2)}) collective-permute-start(bf16[272,256]{1,0:T(8,128)(2,1)S(1)} %totals.3.own), channel_id=1, source_target_pairs={{0,8},{2,10},{4,12},{6,14},{8,0},{10,2},{12,4},{14,6},{16,24},{18,... | collective-permute-start | bytes 417800 | tf_op jit(solution)/shard_map/ppermute | solution.py:743
  22.3 5.7 %collective-permute-start.12 = (bf16[128,256]{1,0:T(8,128)(2,1)S(1)}, bf16[128,256]{1,0:T(8,128)(2,1)S(1)}, u32[]{:S(2)}, u32[]{:S(2)}) collective-permute-start(bf16[128,256]{1,0:T(8,128)(2,1)S(1)} %merged.2.refs_13_), channel_id=1, source_target_pairs={{0,16},{2,18},{4,20},{6,22},{8,24},{10,26},{12,28},{14,30},{16,0},... | collective-permute-start | bytes 196616 | tf_op jit(solution)/shard_map/ppermute | solution.py:743
  28.2 11.3 %collective-permute-start.13 = (bf16[256,256]{1,0:T(8,128)(2,1)S(1)}, bf16[256,256]{1,0:T(8,128)(2,1)S(1)}, u32[]{:S(2)}, u32[]{:S(2)}) collective-permute-start(bf16[256,256]{1,0:T(8,128)(2,1)S(1)} %get-tuple-element.134), channel_id=1, source_target_pairs={{0,6},{2,4},{4,2},{6,0},{8,14},{10,12},{12,10},{14,8},{16,22},{18,... | collective-permute-start | bytes 393224 | tf_op jit(solution)/shard_map/ppermute | solution.py:431
  30.0 6.0 %collective-permute-start.8 = (bf16[128,256]{1,0:T(8,128)(2,1)S(1)}, bf16[128,256]{1,0:T(8,128)(2,1)S(1)}, u32[]{:S(2)}, u32[]{:S(2)}) collective-permute-start(bf16[128,256]{1,0:T(8,128)(2,1)S(1)} %merged.3.refs_13_), channel_id=1, source_target_pairs={{0,16},{2,18},{4,20},{6,22},{8,24},{10,26},{12,28},{14,30},{16,0},... | collective-permute-start | bytes 196616 | tf_op jit(solution)/shard_map/ppermute | solution.py:743
  32.2 9.9 %collective-permute-start.14 = (bf16[256,256]{1,0:T(8,128)(2,1)S(1)}, bf16[256,256]{1,0:T(8,128)(2,1)S(1)}, u32[]{:S(2)}, u32[]{:S(2)}) collective-permute-start(bf16[256,256]{1,0:T(8,128)(2,1)S(1)} %get-tuple-element.135), channel_id=1, source_target_pairs={{0,4},{2,6},{4,0},{6,2},{8,12},{10,14},{12,8},{14,10},{16,20},{18,... | collective-permute-start | bytes 393224 | tf_op jit(solution)/shard_map/ppermute | solution.py:431
  33.5 8.6 %collective-permute-start.15 = (bf16[256,256]{1,0:T(8,128)(2,1)S(1)}, bf16[256,256]{1,0:T(8,128)(2,1)S(1)}, u32[]{:S(2)}, u32[]{:S(2)}) collective-permute-start(bf16[256,256]{1,0:T(8,128)(2,1)S(1)} %get-tuple-element.136), channel_id=1, source_target_pairs={{0,2},{2,0},{4,6},{6,4},{8,10},{10,8},{12,14},{14,12},{16,18},{18,... | collective-permute-start | bytes 393224 | tf_op jit(solution)/shard_map/ppermute | solution.py:431
  36.4 6.7 %collective-permute-start.9 = (bf16[256,256]{1,0:T(8,128)(2,1)S(1)}, bf16[256,256]{1,0:T(8,128)(2,1)S(1)}, u32[]{:S(2)}, u32[]{:S(2)}) collective-permute-start(bf16[256,256]{1,0:T(8,128)(2,1)S(1)} %get-tuple-element.122), channel_id=1, source_target_pairs={{0,6},{2,4},{4,2},{6,0},{8,14},{10,12},{12,10},{14,8},{16,22},{18,... | collective-permute-start | bytes 393224 | tf_op jit(solution)/shard_map/ppermute | solution.py:431
  38.2 5.9 %collective-permute-start.10 = (bf16[256,256]{1,0:T(8,128)(2,1)S(1)}, bf16[256,256]{1,0:T(8,128)(2,1)S(1)}, u32[]{:S(2)}, u32[]{:S(2)}) collective-permute-start(bf16[256,256]{1,0:T(8,128)(2,1)S(1)} %get-tuple-element.123), channel_id=1, source_target_pairs={{0,4},{2,6},{4,0},{6,2},{8,12},{10,14},{12,8},{14,10},{16,20},{18,... | collective-permute-start | bytes 393224 | tf_op jit(solution)/shard_map/ppermute | solution.py:431
  39.5 5.0 %collective-permute-start.11 = (bf16[256,256]{1,0:T(8,128)(2,1)S(1)}, bf16[256,256]{1,0:T(8,128)(2,1)S(1)}, u32[]{:S(2)}, u32[]{:S(2)}) collective-permute-start(bf16[256,256]{1,0:T(8,128)(2,1)S(1)} %get-tuple-element.124), channel_id=1, source_target_pairs={{0,2},{2,0},{4,6},{6,4},{8,10},{10,8},{12,14},{14,12},{16,18},{18,... | collective-permute-start | bytes 393224 | tf_op jit(solution)/shard_map/ppermute | solution.py:431
  44.8 1.5 %collective-permute-start.16 = (bf16[768,128]{1,0:T(8,128)(2,1)S(1)}, bf16[768,128]{1,0:T(8,128)(2,1)S(1)}, u32[]{:S(2)}, u32[]{:S(2)}) collective-permute-start(bf16[768,128]{1,0:T(8,128)(2,1)S(1)} %entry_parts.5.refs_0_), channel_id=1, source_target_pairs={{0,1},{1,0},{2,3},{3,2},{4,5},{5,4},{6,7},{7,6},{8,9},{9,8},{10,11... | collective-permute-start | bytes 589832 | tf_op jit(solution)/shard_map/ppermute | solution.py:710

commit v19 on v17

--- a/solution.py
+++ b/solution.py
@@ -630,18 +630,18 @@
     for m, one in enumerate(local_parts):
         dx_local[:, m * part : (m + 1) * part] = one[...]
     for k, entry in enumerate(entries):
-        here = slice(k * part, (k + 1) * part)
-        local = dx_local[:, pl.ds(pl.multiple_of((place_of(where) ^ k) * part, part), part)]
+        lanes = pl.ds(pl.multiple_of((place_of(where) ^ k) * part, part), part)
+        local = dx_local[:, lanes]
         far = spread[k][...].astype(F32) * dot(b[...], entry[state:, :], NN)
-        put(k, here, (local.astype(F32) + far).astype(BF16))
+        put(k, lanes, (local.astype(F32) + far).astype(BF16))
 
 
 def values_kernel(where, b, *refs):
     local_parts, spread = refs[:GROUP], refs[GROUP : 2 * GROUP]
     entries, (out, dx_local) = sent_order(refs[2 * GROUP : 3 * GROUP]), refs[-2:]
 
-    def put(k, here, value):
-        out[:, here] = value
+    def put(k, lanes, value):
+        out[:, lanes] = value
 
     put_values(where, spread, b, local_parts, dx_local, entries, put)
 
@@ -653,19 +653,16 @@
     part = entries[0].shape[1]
     stores = []
 
-    def store(chunk, k, source):
-        lanes = chunk_lanes(where, k, chunk, part)
-        at = sems.at[chunk * GROUP + k]
-        stores.append(pltpu.make_async_copy(source, out.at[:, lanes], at))
+    def store(n, source, target):
+        stores.append(pltpu.make_async_copy(source, target, sems.at[n]))
         stores[-1].start()
 
     for chunk, values in enumerate(before):
-        for k in range(GROUP):
-            store(chunk, k, values.at[:, pl.ds(k * part, part)])
-
-    def put(k, here, value):
+        store(GROUP + chunk, values, out.at[:, pl.ds(chunk * GROUP * part, GROUP * part)])
+
+    def put(k, lanes, value):
         dx[k] = value
-        store(chunks - 1, k, dx.at[k])
+        store(k, dx.at[k], out.at[:, chunk_lanes(where, k, chunks - 1, part)])
 
     put_values(where, spread, b, local_parts, dx_local, entries, put)
     for one in stores:
@@ -696,7 +693,7 @@
         scratch_shapes=[
             pltpu.VMEM((GROUP, length, part), BF16),
             pltpu.VMEM((length, GROUP * part), BF16),
-            pltpu.SemaphoreType.DMA((chunks * GROUP,)),
+            pltpu.SemaphoreType.DMA((GROUP + chunks - 1,)),
         ],
         compiler_params=params(8),
         cost_estimate=estimate,

time: 46.9 us -> 46.9 us (level)
  no operation moved by 1% of the time
where the time goes in v19:
time: 46.9 us; the launch traced here: 46.7 us
  starting transfers between devices  23.8 us (51%)
  Pallas kernels  19.6 us (42%)
  waiting for transfers between devices  2.5 us (5%)
  between operations  0.85 us (2%)
    ppermute x12, starting transfers between devices, exchange(): out[k] = lax.ppermute(parts[k], 'seq', [(s, s ^ k) for s in range(count)])  15.2 us
    pallas_call x4, Pallas kernels, inner_terms(): pl.pallas_call(functools.partial(inner_kernel, head_dim, worked, chunks,...  8.61 us
    ppermute x4, starting transfers between devices, to_group(): lax.ppermute(block, 'seq', [(s, s ^ k * group) for s in range(count)])  8.54 us
    pallas_call x1, Pallas kernels, next_states(): pl.pallas_call(functools.partial(next_states_kernel, head_dim, chunks, pi...  3.23 us
    pallas_call x1, Pallas kernels, first_states(): pl.pallas_call(functools.partial(first_states_kernel, head_dim, chunks, p...  2.67 us
    ppermute x12, waiting for transfers between devices, exchange(): out[k] = lax.ppermute(parts[k], 'seq', [(s, s ^ k) for s in range(count)])  2.36 us
    pallas_call x3, Pallas kernels, entry_parts(): pl.pallas_call(functools.partial(parts_kernel, last, ks), out_shape=outs,...  1.3 us
    pallas_call x1, Pallas kernels, entry_values(): pl.pallas_call(functools.partial(last_values_kernel, chunks), out_shape=p...  1.29 us
  transfers between devices with their start and end apart: 17, of which 5 were waited for; matrix products, arithmetic and copies ran while one was open for 0% of the time, Pallas kernels for 34%

profile of v19, /device:TPU:0, one launch (start us, length us, event | category | flops | bytes accessed | tf_op | source)
XLA Modules:
  0.0 46.7 jit_solution(10809705378342393047)
XLA Ops:
  0.6 2.7 %first_states.1 = (f32[32,384]{1,0:T(8,128)S(1)}, bf16[384,128]{1,0:T(8,128)(2,1)S(1)}, bf16[384,128]{1,0:T(8,128)(2,1)S(1)}, bf16[384,1024]{1,0:T(8,128)(2,1)S(...) custom-call(s32[1]{0:T(128)} %bitcast.where, ...), custom_call_target="tpu_custom_call" | custom-call | flops 402653184 | bytes 6291456 | tf_op jit(solution)/shard_map/first_states/pallas_call | solution.py:218
  3.3 4.0 %collective-permute-start = (bf16[272,256]{1,0:T(8,128)(2,1)S(1)}, bf16[272,256]{1,0:T(8,128)(2,1)S(1)}, u32[]{:S(2)}, u32[]{:S(2)}) collective-permute-start(bf16[272,256]{1,0:T(8,128)(2,1)S(1)} %get-tuple-element.101), channel_id=1, source_target_pairs={{0,6},{2,4},{4,2},{6,0},{8,14},{10,12},{12,10},{14,8},{16,22},{18,... | collective-permute-start | bytes 417800 | tf_op jit(solution)/shard_map/ppermute | solution.py:427
  7.3 0.5 %collective-permute-start.1 = (bf16[272,256]{1,0:T(8,128)(2,1)S(1)}, bf16[272,256]{1,0:T(8,128)(2,1)S(1)}, u32[]{:S(2)}, u32[]{:S(2)}) collective-permute-start(bf16[272,256]{1,0:T(8,128)(2,1)S(1)} %get-tuple-element.102), channel_id=1, source_target_pairs={{0,4},{2,6},{4,0},{6,2},{8,12},{10,14},{12,8},{14,10},{16,20},{18,... | collective-permute-start | bytes 417800 | tf_op jit(solution)/shard_map/ppermute | solution.py:427
  7.8 0.1 collective-permute-start.2
  7.9 3.2 %next_states.1 = (bf16[384,1024]{1,0:T(8,128)(2,1)S(1)}, bf16[384,1024]{1,0:T(8,128)(2,1)S(1)}, bf16[384,256]{1,0:T(8,128)(2,1)S(1)}, bf16[384,256]{1,0:T(8,128)...) custom-call(s32[1]{0:T(128)} %bitcast.where, ...), custom_call_target="tpu_custom_call" | custom-call | flops 402653184 | bytes 3145728 | tf_op jit(solution)/shard_map/next_states/pallas_call | solution.py:237
  11.1 2.9 %collective-permute-start.4 = (bf16[272,256]{1,0:T(8,128)(2,1)S(1)}, bf16[272,256]{1,0:T(8,128)(2,1)S(1)}, u32[]{:S(2)}, u32[]{:S(2)}) collective-permute-start(bf16[272,256]{1,0:T(8,128)(2,1)S(1)} %get-tuple-element.109), channel_id=1, source_target_pairs={{0,6},{2,4},{4,2},{6,0},{8,14},{10,12},{12,10},{14,8},{16,22},{18,... | collective-permute-start | bytes 417800 | tf_op jit(solution)/shard_map/ppermute | solution.py:427
  14.1 0.5 %collective-permute-start.5 = (bf16[272,256]{1,0:T(8,128)(2,1)S(1)}, bf16[272,256]{1,0:T(8,128)(2,1)S(1)}, u32[]{:S(2)}, u32[]{:S(2)}) collective-permute-start(bf16[272,256]{1,0:T(8,128)(2,1)S(1)} %get-tuple-element.110), channel_id=1, source_target_pairs={{0,4},{2,6},{4,0},{6,2},{8,12},{10,14},{12,8},{14,10},{16,20},{18,... | collective-permute-start | bytes 417800 | tf_op jit(solution)/shard_map/ppermute | solution.py:427
  14.6 0.0 collective-permute-done.refs_1_.refs_5_
  14.6 0.1 collective-permute-start.6
  14.7 0.5 inner_setup.1
  15.2 0.0 collective-permute-done.1.refs_2_.refs_4_
  15.2 0.0 collective-permute-done.2.refs_3_
  15.2 0.1 totals.2.refs_11_.own
  15.3 2.0 %collective-permute-start.3 = (bf16[272,256]{1,0:T(8,128)(2,1)S(1)}, bf16[272,256]{1,0:T(8,128)(2,1)S(1)}, u32[]{:S(2)}, u32[]{:S(2)}) collective-permute-start(bf16[272,256]{1,0:T(8,128)(2,1)S(1)} %totals.2.refs_11_.own), channel_id=1, source_target_pairs={{0,8},{2,10},{4,12},{6,14},{8,0},{10,2},{12,4},{14,6},{16,24},{18,... | collective-permute-start | bytes 417800 | tf_op jit(solution)/shard_map/ppermute | solution.py:753
  17.4 1.4 %inner_terms.4 = (bf16[384,256]{1,0:T(8,128)(2,1)S(1)}, f32[384,128]{1,0:T(8,128)S(1)}, f32[384,128]{1,0:T(8,128)S(1)}) custom-call(bf16[384,128]{1,0:T(8,128)(2,1)S(1)} %get-tuple-element.82.refs_0_.b, bf16[384,128]{1,0:T(8,128)(2,1)S(1)} %get-tuple-element.83.refs_1_.c, bf16[384,1024]{1,0:T(8,128)(2,1)S(1)} %get-tuple-element.84.refs_2_.refs_0_, ...), custom_call_target="tpu_custom_call" | custom-call | flops 1 | bytes 1 | tf_op jit(solution)/shard_map/inner_terms/pallas_call | solution.py:580
  18.7 0.0 collective-permute-done.4.refs_1_.refs_5_
  18.7 1.2 %collective-permute-done.5.refs_2_.refs_4_ = bf16[272,256]{1,0:T(8,128)(2,1)S(1)} collective-permute-done((bf16[272,256]{1,0:T(8,128)(2,1)S(1)}, bf16[272,256]{1,0:T(8,128)(2,1)S(1)}, u32[]{:S(2)}, u32[]{:S(2)}) %collective-permute-start.5) | collective-permute-done | bytes 139296 | tf_op jit(solution)/shard_map/ppermute | solution.py:427
  20.0 0.2 collective-permute-done.6.refs_3_
  20.1 0.1 totals.3.own
  20.3 1.6 %collective-permute-start.7 = (bf16[272,256]{1,0:T(8,128)(2,1)S(1)}, bf16[272,256]{1,0:T(8,128)(2,1)S(1)}, u32[]{:S(2)}, u32[]{:S(2)}) collective-permute-start(bf16[272,256]{1,0:T(8,128)(2,1)S(1)} %totals.3.own), channel_id=1, source_target_pairs={{0,8},{2,10},{4,12},{6,14},{8,0},{10,2},{12,4},{14,6},{16,24},{18,... | collective-permute-start | bytes 417800 | tf_op jit(solution)/shard_map/ppermute | solution.py:753
  21.9 0.0 collective-permute-done.3.received.refs_0_
  22.0 2.7 %collective-permute-start.12 = (bf16[128,256]{1,0:T(8,128)(2,1)S(1)}, bf16[128,256]{1,0:T(8,128)(2,1)S(1)}, u32[]{:S(2)}, u32[]{:S(2)}) collective-permute-start(bf16[128,256]{1,0:T(8,128)(2,1)S(1)} %merged.2.refs_13_), channel_id=1, source_target_pairs={{0,16},{2,18},{4,20},{6,22},{8,24},{10,26},{12,28},{14,30},{16,0},... | collective-permute-start | bytes 196616 | tf_op jit(solution)/shard_map/ppermute | solution.py:753
  24.6 3.1 %inner_terms.5 = (bf16[384,256]{1,0:T(8,128)(2,1)S(1)}, bf16[384,256]{1,0:T(8,128)(2,1)S(1)}, bf16[384,256]{1,0:T(8,128)(2,1)S(1)}, f32[384,128]{1,0:T(8,128)S(1)}, f32[384,128]{1,0:T(8,128)S(1)}) custom-call(bf16[384,128]{1,0:T(8,128)(2,1)S(1)} %get-tuple-element.82.refs_0_.b, bf16[384,128]{1,0:T(8,128)(2,1)S(1)} %get-tuple-element.83.refs_1_.c, ...), custom_call_target="tpu_custom_call" | custom-call | flops 805306368 | bytes 3145728 | tf_op jit(solution)/shard_map/inner_terms/pallas_call | solution.py:580
  27.7 0.0 collective-permute-done.12.refs_1_
  27.7 0.2 member_entries.3
  27.9 1.7 %collective-permute-start.13 = (bf16[256,256]{1,0:T(8,128)(2,1)S(1)}, bf16[256,256]{1,0:T(8,128)(2,1)S(1)}, u32[]{:S(2)}, u32[]{:S(2)}) collective-permute-start(bf16[256,256]{1,0:T(8,128)(2,1)S(1)} %get-tuple-element.135), channel_id=1, source_target_pairs={{0,6},{2,4},{4,2},{6,0},{8,14},{10,12},{12,10},{14,8},{16,22},{18,... | collective-permute-start | bytes 393224 | tf_op jit(solution)/shard_map/ppermute | solution.py:427
  29.6 0.0 collective-permute-done.7.received.refs_0_
  29.7 2.2 %collective-permute-start.8 = (bf16[128,256]{1,0:T(8,128)(2,1)S(1)}, bf16[128,256]{1,0:T(8,128)(2,1)S(1)}, u32[]{:S(2)}, u32[]{:S(2)}) collective-permute-start(bf16[128,256]{1,0:T(8,128)(2,1)S(1)} %merged.3.refs_13_), channel_id=1, source_target_pairs={{0,16},{2,18},{4,20},{6,22},{8,24},{10,26},{12,28},{14,30},{16,0},... | collective-permute-start | bytes 196616 | tf_op jit(solution)/shard_map/ppermute | solution.py:753
  31.9 1.3 %collective-permute-start.14 = (bf16[256,256]{1,0:T(8,128)(2,1)S(1)}, bf16[256,256]{1,0:T(8,128)(2,1)S(1)}, u32[]{:S(2)}, u32[]{:S(2)}) collective-permute-start(bf16[256,256]{1,0:T(8,128)(2,1)S(1)} %get-tuple-element.136), channel_id=1, source_target_pairs={{0,4},{2,6},{4,0},{6,2},{8,12},{10,14},{12,8},{14,10},{16,20},{18,... | collective-permute-start | bytes 393224 | tf_op jit(solution)/shard_map/ppermute | solution.py:427
  33.2 0.5 collective-permute-start.15
  33.6 2.1 %inner_terms.6 = (bf16[384,256]{1,0:T(8,128)(2,1)S(1)}, bf16[384,256]{1,0:T(8,128)(2,1)S(1)}, f32[384,128]{1,0:T(8,128)S(1)}, f32[384,128]{1,0:T(8,128)S(1)}) custom-call(bf16[384,128]{1,0:T(8,128)(2,1)S(1)} %get-tuple-element.82.refs_0_.b, bf16[384,128]{1,0:T(8,128)(2,1)S(1)} %get-tuple-element.83.refs_1_.c, ...), custom_call_target="tpu_custom_call" | custom-call | flops 805306368 | bytes 3145728 | tf_op jit(solution)/shard_map/inner_terms/pallas_call | solution.py:580
  35.7 0.0 collective-permute-done.8.refs_1_
  35.7 0.4 member_entries.2
  36.1 1.8 %collective-permute-start.9 = (bf16[256,256]{1,0:T(8,128)(2,1)S(1)}, bf16[256,256]{1,0:T(8,128)(2,1)S(1)}, u32[]{:S(2)}, u32[]{:S(2)}) collective-permute-start(bf16[256,256]{1,0:T(8,128)(2,1)S(1)} %get-tuple-element.123), channel_id=1, source_target_pairs={{0,6},{2,4},{4,2},{6,0},{8,14},{10,12},{12,10},{14,8},{16,22},{18,... | collective-permute-start | bytes 393224 | tf_op jit(solution)/shard_map/ppermute | solution.py:427
  37.9 1.3 %collective-permute-start.10 = (bf16[256,256]{1,0:T(8,128)(2,1)S(1)}, bf16[256,256]{1,0:T(8,128)(2,1)S(1)}, u32[]{:S(2)}, u32[]{:S(2)}) collective-permute-start(bf16[256,256]{1,0:T(8,128)(2,1)S(1)} %get-tuple-element.124), channel_id=1, source_target_pairs={{0,4},{2,6},{4,0},{6,2},{8,12},{10,14},{12,8},{14,10},{16,20},{18,... | collective-permute-start | bytes 393224 | tf_op jit(solution)/shard_map/ppermute | solution.py:427
  39.2 0.5 %collective-permute-start.11 = (bf16[256,256]{1,0:T(8,128)(2,1)S(1)}, bf16[256,256]{1,0:T(8,128)(2,1)S(1)}, u32[]{:S(2)}, u32[]{:S(2)}) collective-permute-start(bf16[256,256]{1,0:T(8,128)(2,1)S(1)} %get-tuple-element.125), channel_id=1, source_target_pairs={{0,2},{2,0},{4,6},{6,4},{8,10},{10,8},{12,14},{14,12},{16,18},{18,... | collective-permute-start | bytes 393224 | tf_op jit(solution)/shard_map/ppermute | solution.py:427
  39.7 2.1 %inner_terms.7 = (bf16[384,256]{1,0:T(8,128)(2,1)S(1)}, bf16[384,256]{1,0:T(8,128)(2,1)S(1)}, f32[384,128]{1,0:T(8,128)S(1)}, f32[384,128]{1,0:T(8,128)S(1)}) custom-call(bf16[384,128]{1,0:T(8,128)(2,1)S(1)} %get-tuple-element.82.refs_0_.b, bf16[384,128]{1,0:T(8,128)(2,1)S(1)} %get-tuple-element.83.refs_1_.c, ...), custom_call_target="tpu_custom_call" | custom-call | flops 805306368 | bytes 3145728 | tf_op jit(solution)/shard_map/inner_terms/pallas_call | solution.py:580
  41.8 0.5 %entry_values.1.refs_12_.refs_6_ = bf16[384,1024]{1,0:T(8,128)(2,1)S(1)} custom-call(s32[1]{0:T(128)} %bitcast.where, bf16[384,128]{1,0:T(8,128)(2,1)S(1)} %get-tuple-element.82.refs_0_.b, bf16[384,256]{1,0:T(8,128)(2,1)S(1)} %get-tuple-element.126.refs_0_, bf16[384,256]{1,0:T(8,128)(2,1)S(1)} %get-tuple-element.127.refs_1_, ...), custom_call_target="tpu_custom_call" | custom-call | flops 100663296 | bytes 1572864 | tf_op jit(solution)/shard_map/entry_values/pallas_call | solution.py:678
  42.3 0.6 %entry_parts.3 = (f32[384,128]{1,0:T(8,128)S(1)}, f32[384,128]{1,0:T(8,128)S(1)}) custom-call(f32[384,128]{1,0:T(8,128)S(1)} %get-tuple-element.138.db_before, f32[384,128]{1,0:T(8,128)S(1)} %get-tuple-element.139.dc_before, bf16[384,256]{1,0:T(8,128)(2,1)S(1)} %get-tuple-element.140.refs_0_, bf16[384,256]{1,0:T(8,128)(2,1)S(1)} %get-tuple-element.141.refs_1_, ...), custom_call_target="tpu_custom_call" | custom-call | flops 301989888 | bytes 98304 | tf_op jit(solution)/shard_map/entry_parts/pallas_call | solution.py:617
  42.8 0.0 collective-permute-done.9.refs_9_.refs_5_
  42.8 0.4 entry_parts.4
  43.2 0.6 %collective-permute-done.10.refs_10_.refs_4_ = bf16[256,256]{1,0:T(8,128)(2,1)S(1)} collective-permute-done((bf16[256,256]{1,0:T(8,128)(2,1)S(1)}, bf16[256,256]{1,0:T(8,128)(2,1)S(1)}, u32[]{:S(2)}, u32[]{:S(2)}) %collective-permute-start.10) | collective-permute-done | bytes 131104 | tf_op jit(solution)/shard_map/ppermute | solution.py:427
  43.8 0.4 collective-permute-done.11.refs_11_.refs_5_
  44.2 0.4 entry_parts.5.refs_0_
  44.5 0.1 collective-permute-start.16
  44.6 1.3 %last_values.1 = bf16[384,2048]{1,0:T(8,128)(2,1)} custom-call(s32[1]{0:T(128)} %bitcast.where, bf16[384,128]{1,0:T(8,128)(2,1)S(1)} %get-tuple-element.82.refs_0_.b, bf16[384,256]{1,0:T(8,128)(2,1)S(1)} %get-tuple-element.112.refs_0_, bf16[384,256]{1,0:T(8,128)(2,1)S(1)} %get-tuple-element.113.refs_1_, bf16[384,256]{1,0:T(8,128)(2,1)S(1)} %get-tuple-element.117.refs_2_, ...), custom_call_target="tpu_custom_call" | custom-call | flops 100663296 | bytes 1572864 | tf_op jit(solution)/shard_map/last_values/pallas_call | solution.py:688
  45.9 0.1 collective-permute-done.16.refs_1_
  46.0 0.7 %sum_over_heads.1 = (bf16[384,128]{1,0:T(8,128)(2,1)}, bf16[384,128]{1,0:T(8,128)(2,1)}) custom-call(bf16[768,128]{1,0:T(8,128)(2,1)S(1)} %entry_parts.5.refs_0_, bf16[768,128]{1,0:T(8,128)(2,1)S(1)} %collective-permute-done.16.refs_1_), custom_call_target="tpu_custom_call" | custom-call | flops 196608 | bytes 393216 | tf_op jit(solution)/shard_map/sum_over_heads/pallas_call | solution.py:720
  (5 shorter events, 0.1 us)
Async XLA Ops:
  3.3 11.3 %collective-permute-start = (bf16[272,256]{1,0:T(8,128)(2,1)S(1)}, bf16[272,256]{1,0:T(8,128)(2,1)S(1)}, u32[]{:S(2)}, u32[]{:S(2)}) collective-permute-start(bf16[272,256]{1,0:T(8,128)(2,1)S(1)} %get-tuple-element.101), channel_id=1, source_target_pairs={{0,6},{2,4},{4,2},{6,0},{8,14},{10,12},{12,10},{14,8},{16,22},{18,... | collective-permute-start | bytes 417800 | tf_op jit(solution)/shard_map/ppermute | solution.py:427
  7.3 7.9 %collective-permute-start.1 = (bf16[272,256]{1,0:T(8,128)(2,1)S(1)}, bf16[272,256]{1,0:T(8,128)(2,1)S(1)}, u32[]{:S(2)}, u32[]{:S(2)}) collective-permute-start(bf16[272,256]{1,0:T(8,128)(2,1)S(1)} %get-tuple-element.102), channel_id=1, source_target_pairs={{0,4},{2,6},{4,0},{6,2},{8,12},{10,14},{12,8},{14,10},{16,20},{18,... | collective-permute-start | bytes 417800 | tf_op jit(solution)/shard_map/ppermute | solution.py:427
  7.8 7.4 %collective-permute-start.2 = (bf16[272,256]{1,0:T(8,128)(2,1)S(1)}, bf16[272,256]{1,0:T(8,128)(2,1)S(1)}, u32[]{:S(2)}, u32[]{:S(2)}) collective-permute-start(bf16[272,256]{1,0:T(8,128)(2,1)S(1)} %get-tuple-element.103), channel_id=1, source_target_pairs={{0,2},{2,0},{4,6},{6,4},{8,10},{10,8},{12,14},{14,12},{16,18},{18,... | collective-permute-start | bytes 417800 | tf_op jit(solution)/shard_map/ppermute | solution.py:427
  11.1 7.6 %collective-permute-start.4 = (bf16[272,256]{1,0:T(8,128)(2,1)S(1)}, bf16[272,256]{1,0:T(8,128)(2,1)S(1)}, u32[]{:S(2)}, u32[]{:S(2)}) collective-permute-start(bf16[272,256]{1,0:T(8,128)(2,1)S(1)} %get-tuple-element.109), channel_id=1, source_target_pairs={{0,6},{2,4},{4,2},{6,0},{8,14},{10,12},{12,10},{14,8},{16,22},{18,... | collective-permute-start | bytes 417800 | tf_op jit(solution)/shard_map/ppermute | solution.py:427
  14.1 5.9 %collective-permute-start.5 = (bf16[272,256]{1,0:T(8,128)(2,1)S(1)}, bf16[272,256]{1,0:T(8,128)(2,1)S(1)}, u32[]{:S(2)}, u32[]{:S(2)}) collective-permute-start(bf16[272,256]{1,0:T(8,128)(2,1)S(1)} %get-tuple-element.110), channel_id=1, source_target_pairs={{0,4},{2,6},{4,0},{6,2},{8,12},{10,14},{12,8},{14,10},{16,20},{18,... | collective-permute-start | bytes 417800 | tf_op jit(solution)/shard_map/ppermute | solution.py:427
  14.6 5.6 %collective-permute-start.6 = (bf16[272,256]{1,0:T(8,128)(2,1)S(1)}, bf16[272,256]{1,0:T(8,128)(2,1)S(1)}, u32[]{:S(2)}, u32[]{:S(2)}) collective-permute-start(bf16[272,256]{1,0:T(8,128)(2,1)S(1)} %get-tuple-element.111), channel_id=1, source_target_pairs={{0,2},{2,0},{4,6},{6,4},{8,10},{10,8},{12,14},{14,12},{16,18},{18,... | collective-permute-start | bytes 417800 | tf_op jit(solution)/shard_map/ppermute | solution.py:427
  15.3 6.6 %collective-permute-start.3 = (bf16[272,256]{1,0:T(8,128)(2,1)S(1)}, bf16[272,256]{1,0:T(8,128)(2,1)S(1)}, u32[]{:S(2)}, u32[]{:S(2)}) collective-permute-start(bf16[272,256]{1,0:T(8,128)(2,1)S(1)} %totals.2.refs_11_.own), channel_id=1, source_target_pairs={{0,8},{2,10},{4,12},{6,14},{8,0},{10,2},{12,4},{14,6},{16,24},{18,... | collective-permute-start | bytes 417800 | tf_op jit(solution)/shard_map/ppermute | solution.py:753
  20.3 9.3 %collective-permute-start.7 = (bf16[272,256]{1,0:T(8,128)(2,1)S(1)}, bf16[272,256]{1,0:T(8,128)(2,1)S(1)}, u32[]{:S(2)}, u32[]{:S(2)}) collective-permute-start(bf16[272,256]{1,0:T(8,128)(2,1)S(1)} %totals.3.own), channel_id=1, source_target_pairs={{0,8},{2,10},{4,12},{6,14},{8,0},{10,2},{12,4},{14,6},{16,24},{18,... | collective-permute-start | bytes 417800 | tf_op jit(solution)/shard_map/ppermute | solution.py:753
  22.0 5.7 %collective-permute-start.12 = (bf16[128,256]{1,0:T(8,128)(2,1)S(1)}, bf16[128,256]{1,0:T(8,128)(2,1)S(1)}, u32[]{:S(2)}, u32[]{:S(2)}) collective-permute-start(bf16[128,256]{1,0:T(8,128)(2,1)S(1)} %merged.2.refs_13_), channel_id=1, source_target_pairs={{0,16},{2,18},{4,20},{6,22},{8,24},{10,26},{12,28},{14,30},{16,0},... | collective-permute-start | bytes 196616 | tf_op jit(solution)/shard_map/ppermute | solution.py:753
  27.9 11.3 %collective-permute-start.13 = (bf16[256,256]{1,0:T(8,128)(2,1)S(1)}, bf16[256,256]{1,0:T(8,128)(2,1)S(1)}, u32[]{:S(2)}, u32[]{:S(2)}) collective-permute-start(bf16[256,256]{1,0:T(8,128)(2,1)S(1)} %get-tuple-element.135), channel_id=1, source_target_pairs={{0,6},{2,4},{4,2},{6,0},{8,14},{10,12},{12,10},{14,8},{16,22},{18,... | collective-permute-start | bytes 393224 | tf_op jit(solution)/shard_map/ppermute | solution.py:427
  29.7 6.0 %collective-permute-start.8 = (bf16[128,256]{1,0:T(8,128)(2,1)S(1)}, bf16[128,256]{1,0:T(8,128)(2,1)S(1)}, u32[]{:S(2)}, u32[]{:S(2)}) collective-permute-start(bf16[128,256]{1,0:T(8,128)(2,1)S(1)} %merged.3.refs_13_), channel_id=1, source_target_pairs={{0,16},{2,18},{4,20},{6,22},{8,24},{10,26},{12,28},{14,30},{16,0},... | collective-permute-start | bytes 196616 | tf_op jit(solution)/shard_map/ppermute | solution.py:753
  31.9 9.8 %collective-permute-start.14 = (bf16[256,256]{1,0:T(8,128)(2,1)S(1)}, bf16[256,256]{1,0:T(8,128)(2,1)S(1)}, u32[]{:S(2)}, u32[]{:S(2)}) collective-permute-start(bf16[256,256]{1,0:T(8,128)(2,1)S(1)} %get-tuple-element.136), channel_id=1, source_target_pairs={{0,4},{2,6},{4,0},{6,2},{8,12},{10,14},{12,8},{14,10},{16,20},{18,... | collective-permute-start | bytes 393224 | tf_op jit(solution)/shard_map/ppermute | solution.py:427
  33.2 8.6 %collective-permute-start.15 = (bf16[256,256]{1,0:T(8,128)(2,1)S(1)}, bf16[256,256]{1,0:T(8,128)(2,1)S(1)}, u32[]{:S(2)}, u32[]{:S(2)}) collective-permute-start(bf16[256,256]{1,0:T(8,128)(2,1)S(1)} %get-tuple-element.137), channel_id=1, source_target_pairs={{0,2},{2,0},{4,6},{6,4},{8,10},{10,8},{12,14},{14,12},{16,18},{18,... | collective-permute-start | bytes 393224 | tf_op jit(solution)/shard_map/ppermute | solution.py:427
  36.1 6.7 %collective-permute-start.9 = (bf16[256,256]{1,0:T(8,128)(2,1)S(1)}, bf16[256,256]{1,0:T(8,128)(2,1)S(1)}, u32[]{:S(2)}, u32[]{:S(2)}) collective-permute-start(bf16[256,256]{1,0:T(8,128)(2,1)S(1)} %get-tuple-element.123), channel_id=1, source_target_pairs={{0,6},{2,4},{4,2},{6,0},{8,14},{10,12},{12,10},{14,8},{16,22},{18,... | collective-permute-start | bytes 393224 | tf_op jit(solution)/shard_map/ppermute | solution.py:427
  37.9 5.9 %collective-permute-start.10 = (bf16[256,256]{1,0:T(8,128)(2,1)S(1)}, bf16[256,256]{1,0:T(8,128)(2,1)S(1)}, u32[]{:S(2)}, u32[]{:S(2)}) collective-permute-start(bf16[256,256]{1,0:T(8,128)(2,1)S(1)} %get-tuple-element.124), channel_id=1, source_target_pairs={{0,4},{2,6},{4,0},{6,2},{8,12},{10,14},{12,8},{14,10},{16,20},{18,... | collective-permute-start | bytes 393224 | tf_op jit(solution)/shard_map/ppermute | solution.py:427
  39.2 5.0 %collective-permute-start.11 = (bf16[256,256]{1,0:T(8,128)(2,1)S(1)}, bf16[256,256]{1,0:T(8,128)(2,1)S(1)}, u32[]{:S(2)}, u32[]{:S(2)}) collective-permute-start(bf16[256,256]{1,0:T(8,128)(2,1)S(1)} %get-tuple-element.125), channel_id=1, source_target_pairs={{0,2},{2,0},{4,6},{6,4},{8,10},{10,8},{12,14},{14,12},{16,18},{18,... | collective-permute-start | bytes 393224 | tf_op jit(solution)/shard_map/ppermute | solution.py:427
  44.5 1.5 %collective-permute-start.16 = (bf16[768,128]{1,0:T(8,128)(2,1)S(1)}, bf16[768,128]{1,0:T(8,128)(2,1)S(1)}, u32[]{:S(2)}, u32[]{:S(2)}) collective-permute-start(bf16[768,128]{1,0:T(8,128)(2,1)S(1)} %entry_parts.5.refs_0_), channel_id=1, source_target_pairs={{0,1},{1,0},{2,3},{3,2},{4,5},{5,4},{6,7},{7,6},{8,9},{9,8},{10,11... | collective-permute-start | bytes 589832 | tf_op jit(solution)/shard_map/ppermute | solution.py:719

commit v20 on v19

--- a/solution.py
+++ b/solution.py
@@ -753,7 +753,7 @@
         return lax.ppermute(block, "seq", [(s, s ^ (k * group)) for s in range(count)])
 
     every = [(chunk, m) for chunk in range(chunks) for m in range(group)]
-    worked = [every[1:4]] + [every[chunk * group :][:2] for chunk in range(1, chunks)]
+    worked = [every[1:4]] + [every[chunk * group :][:1] for chunk in range(1, chunks)]
     rest = [one for one in every[1:] if not any(one in some for some in worked)]
     entries, inner, sums = [], {}, []
 

time: 46.9 us -> 46.5 us (level)
  waiting for transfers between devices: 2.5 us -> 1.82 us
    ppermute x12, waiting for transfers between devices: 2.36 us -> 1.68 us  [exchange(): out[k] = lax.ppermute(parts[k], 'seq', [(s, s ^ k) for s in range(count)])]
  transfers between devices with their start and end apart: 17 -> 17, of which waited for: 5 -> 4; matrix products, arithmetic and copies ran while one was open for 0% -> 0% of each run, Pallas kernels for 34% -> 35%
where the time goes in v20:
time: 46.5 us; the launch traced here: 46.3 us
  starting transfers between devices  23.8 us (51%)
  Pallas kernels  19.9 us (43%)
  waiting for transfers between devices  1.82 us (4%)
  between operations  0.85 us (2%)
    ppermute x12, starting transfers between devices, exchange(): out[k] = lax.ppermute(parts[k], 'seq', [(s, s ^ k) for s in range(count)])  15.2 us
    pallas_call x4, Pallas kernels, inner_terms(): pl.pallas_call(functools.partial(inner_kernel, head_dim, worked, chunks,...  8.89 us
    ppermute x4, starting transfers between devices, to_group(): lax.ppermute(block, 'seq', [(s, s ^ k * group) for s in range(count)])  8.53 us
    pallas_call x1, Pallas kernels, next_states(): pl.pallas_call(functools.partial(next_states_kernel, head_dim, chunks, pi...  3.23 us
    pallas_call x1, Pallas kernels, first_states(): pl.pallas_call(functools.partial(first_states_kernel, head_dim, chunks, p...  2.67 us
    ppermute x12, waiting for transfers between devices, exchange(): out[k] = lax.ppermute(parts[k], 'seq', [(s, s ^ k) for s in range(count)])  1.68 us
    pallas_call x3, Pallas kernels, entry_parts(): pl.pallas_call(functools.partial(parts_kernel, last, ks), out_shape=outs,...  1.3 us
    pallas_call x1, Pallas kernels, entry_values(): pl.pallas_call(functools.partial(last_values_kernel, chunks), out_shape=p...  1.29 us
  transfers between devices with their start and end apart: 17, of which 4 were waited for; matrix products, arithmetic and copies ran while one was open for 0% of the time, Pallas kernels for 35%

profile of v20, /device:TPU:0, one launch (start us, length us, event | category | flops | bytes accessed | tf_op | source)
XLA Modules:
  0.0 46.3 jit_solution(3498840249538127366)
XLA Ops:
  0.6 2.7 %first_states.1 = (f32[32,384]{1,0:T(8,128)S(1)}, bf16[384,128]{1,0:T(8,128)(2,1)S(1)}, bf16[384,128]{1,0:T(8,128)(2,1)S(1)}, bf16[384,1024]{1,0:T(8,128)(2,1)S(...) custom-call(s32[1]{0:T(128)} %bitcast.where, ...), custom_call_target="tpu_custom_call" | custom-call | flops 402653184 | bytes 6291456 | tf_op jit(solution)/shard_map/first_states/pallas_call | solution.py:218
  3.3 4.0 %collective-permute-start = (bf16[272,256]{1,0:T(8,128)(2,1)S(1)}, bf16[272,256]{1,0:T(8,128)(2,1)S(1)}, u32[]{:S(2)}, u32[]{:S(2)}) collective-permute-start(bf16[272,256]{1,0:T(8,128)(2,1)S(1)} %get-tuple-element.101), channel_id=1, source_target_pairs={{0,6},{2,4},{4,2},{6,0},{8,14},{10,12},{12,10},{14,8},{16,22},{18,... | collective-permute-start | bytes 417800 | tf_op jit(solution)/shard_map/ppermute | solution.py:427
  7.3 0.5 %collective-permute-start.1 = (bf16[272,256]{1,0:T(8,128)(2,1)S(1)}, bf16[272,256]{1,0:T(8,128)(2,1)S(1)}, u32[]{:S(2)}, u32[]{:S(2)}) collective-permute-start(bf16[272,256]{1,0:T(8,128)(2,1)S(1)} %get-tuple-element.102), channel_id=1, source_target_pairs={{0,4},{2,6},{4,0},{6,2},{8,12},{10,14},{12,8},{14,10},{16,20},{18,... | collective-permute-start | bytes 417800 | tf_op jit(solution)/shard_map/ppermute | solution.py:427
  7.8 0.1 collective-permute-start.2
  7.9 3.2 %next_states.1 = (bf16[384,1024]{1,0:T(8,128)(2,1)S(1)}, bf16[384,1024]{1,0:T(8,128)(2,1)S(1)}, bf16[384,256]{1,0:T(8,128)(2,1)S(1)}, bf16[384,256]{1,0:T(8,128)...) custom-call(s32[1]{0:T(128)} %bitcast.where, ...), custom_call_target="tpu_custom_call" | custom-call | flops 402653184 | bytes 3145728 | tf_op jit(solution)/shard_map/next_states/pallas_call | solution.py:237
  11.1 2.9 %collective-permute-start.4 = (bf16[272,256]{1,0:T(8,128)(2,1)S(1)}, bf16[272,256]{1,0:T(8,128)(2,1)S(1)}, u32[]{:S(2)}, u32[]{:S(2)}) collective-permute-start(bf16[272,256]{1,0:T(8,128)(2,1)S(1)} %get-tuple-element.109), channel_id=1, source_target_pairs={{0,6},{2,4},{4,2},{6,0},{8,14},{10,12},{12,10},{14,8},{16,22},{18,... | collective-permute-start | bytes 417800 | tf_op jit(solution)/shard_map/ppermute | solution.py:427
  14.1 0.5 %collective-permute-start.5 = (bf16[272,256]{1,0:T(8,128)(2,1)S(1)}, bf16[272,256]{1,0:T(8,128)(2,1)S(1)}, u32[]{:S(2)}, u32[]{:S(2)}) collective-permute-start(bf16[272,256]{1,0:T(8,128)(2,1)S(1)} %get-tuple-element.110), channel_id=1, source_target_pairs={{0,4},{2,6},{4,0},{6,2},{8,12},{10,14},{12,8},{14,10},{16,20},{18,... | collective-permute-start | bytes 417800 | tf_op jit(solution)/shard_map/ppermute | solution.py:427
  14.6 0.0 collective-permute-done.refs_1_.refs_5_
  14.6 0.1 collective-permute-start.6
  14.7 0.5 inner_setup.1
  15.2 0.0 collective-permute-done.1.refs_2_.refs_4_
  15.2 0.0 collective-permute-done.2.refs_3_
  15.2 0.1 totals.2.refs_11_.own
  15.3 2.0 %collective-permute-start.3 = (bf16[272,256]{1,0:T(8,128)(2,1)S(1)}, bf16[272,256]{1,0:T(8,128)(2,1)S(1)}, u32[]{:S(2)}, u32[]{:S(2)}) collective-permute-start(bf16[272,256]{1,0:T(8,128)(2,1)S(1)} %totals.2.refs_11_.own), channel_id=1, source_target_pairs={{0,8},{2,10},{4,12},{6,14},{8,0},{10,2},{12,4},{14,6},{16,24},{18,... | collective-permute-start | bytes 417800 | tf_op jit(solution)/shard_map/ppermute | solution.py:753
  17.4 1.4 %inner_terms.4 = (bf16[384,256]{1,0:T(8,128)(2,1)S(1)}, f32[384,128]{1,0:T(8,128)S(1)}, f32[384,128]{1,0:T(8,128)S(1)}) custom-call(bf16[384,128]{1,0:T(8,128)(2,1)S(1)} %get-tuple-element.82.refs_0_.b, bf16[384,128]{1,0:T(8,128)(2,1)S(1)} %get-tuple-element.83.refs_1_.c, bf16[384,1024]{1,0:T(8,128)(2,1)S(1)} %get-tuple-element.84.refs_2_.refs_0_, ...), custom_call_target="tpu_custom_call" | custom-call | flops 1 | bytes 1 | tf_op jit(solution)/shard_map/inner_terms/pallas_call | solution.py:580
  18.7 0.0 collective-permute-done.4.refs_1_.refs_5_
  18.7 1.2 %collective-permute-done.5.refs_2_.refs_4_ = bf16[272,256]{1,0:T(8,128)(2,1)S(1)} collective-permute-done((bf16[272,256]{1,0:T(8,128)(2,1)S(1)}, bf16[272,256]{1,0:T(8,128)(2,1)S(1)}, u32[]{:S(2)}, u32[]{:S(2)}) %collective-permute-start.5) | collective-permute-done | bytes 139296 | tf_op jit(solution)/shard_map/ppermute | solution.py:427
  20.0 0.2 collective-permute-done.6.refs_3_
  20.1 0.1 totals.3.own
  20.3 1.6 %collective-permute-start.7 = (bf16[272,256]{1,0:T(8,128)(2,1)S(1)}, bf16[272,256]{1,0:T(8,128)(2,1)S(1)}, u32[]{:S(2)}, u32[]{:S(2)}) collective-permute-start(bf16[272,256]{1,0:T(8,128)(2,1)S(1)} %totals.3.own), channel_id=1, source_target_pairs={{0,8},{2,10},{4,12},{6,14},{8,0},{10,2},{12,4},{14,6},{16,24},{18,... | collective-permute-start | bytes 417800 | tf_op jit(solution)/shard_map/ppermute | solution.py:753
  21.9 0.0 collective-permute-done.3.received.refs_0_
  22.0 2.7 %collective-permute-start.12 = (bf16[128,256]{1,0:T(8,128)(2,1)S(1)}, bf16[128,256]{1,0:T(8,128)(2,1)S(1)}, u32[]{:S(2)}, u32[]{:S(2)}) collective-permute-start(bf16[128,256]{1,0:T(8,128)(2,1)S(1)} %merged.2.refs_13_), channel_id=1, source_target_pairs={{0,16},{2,18},{4,20},{6,22},{8,24},{10,26},{12,28},{14,30},{16,0},... | collective-permute-start | bytes 196616 | tf_op jit(solution)/shard_map/ppermute | solution.py:753
  24.6 3.1 %inner_terms.5 = (bf16[384,256]{1,0:T(8,128)(2,1)S(1)}, bf16[384,256]{1,0:T(8,128)(2,1)S(1)}, bf16[384,256]{1,0:T(8,128)(2,1)S(1)}, f32[384,128]{1,0:T(8,128)S(1)}, f32[384,128]{1,0:T(8,128)S(1)}) custom-call(bf16[384,128]{1,0:T(8,128)(2,1)S(1)} %get-tuple-element.82.refs_0_.b, bf16[384,128]{1,0:T(8,128)(2,1)S(1)} %get-tuple-element.83.refs_1_.c, ...), custom_call_target="tpu_custom_call" | custom-call | flops 805306368 | bytes 3145728 | tf_op jit(solution)/shard_map/inner_terms/pallas_call | solution.py:580
  27.7 0.0 collective-permute-done.12.refs_1_
  27.7 0.2 member_entries.3
  27.9 1.7 %collective-permute-start.13 = (bf16[256,256]{1,0:T(8,128)(2,1)S(1)}, bf16[256,256]{1,0:T(8,128)(2,1)S(1)}, u32[]{:S(2)}, u32[]{:S(2)}) collective-permute-start(bf16[256,256]{1,0:T(8,128)(2,1)S(1)} %get-tuple-element.135), channel_id=1, source_target_pairs={{0,6},{2,4},{4,2},{6,0},{8,14},{10,12},{12,10},{14,8},{16,22},{18,... | collective-permute-start | bytes 393224 | tf_op jit(solution)/shard_map/ppermute | solution.py:427
  29.7 2.2 %collective-permute-start.8 = (bf16[128,256]{1,0:T(8,128)(2,1)S(1)}, bf16[128,256]{1,0:T(8,128)(2,1)S(1)}, u32[]{:S(2)}, u32[]{:S(2)}) collective-permute-start(bf16[128,256]{1,0:T(8,128)(2,1)S(1)} %merged.3.refs_13_), channel_id=1, source_target_pairs={{0,16},{2,18},{4,20},{6,22},{8,24},{10,26},{12,28},{14,30},{16,0},... | collective-permute-start | bytes 196616 | tf_op jit(solution)/shard_map/ppermute | solution.py:753
  31.9 1.3 %collective-permute-start.14 = (bf16[256,256]{1,0:T(8,128)(2,1)S(1)}, bf16[256,256]{1,0:T(8,128)(2,1)S(1)}, u32[]{:S(2)}, u32[]{:S(2)}) collective-permute-start(bf16[256,256]{1,0:T(8,128)(2,1)S(1)} %get-tuple-element.136), channel_id=1, source_target_pairs={{0,4},{2,6},{4,0},{6,2},{8,12},{10,14},{12,8},{14,10},{16,20},{18,... | collective-permute-start | bytes 393224 | tf_op jit(solution)/shard_map/ppermute | solution.py:427
  33.2 0.5 %collective-permute-start.15 = (bf16[256,256]{1,0:T(8,128)(2,1)S(1)}, bf16[256,256]{1,0:T(8,128)(2,1)S(1)}, u32[]{:S(2)}, u32[]{:S(2)}) collective-permute-start(bf16[256,256]{1,0:T(8,128)(2,1)S(1)} %get-tuple-element.137), channel_id=1, source_target_pairs={{0,2},{2,0},{4,6},{6,4},{8,10},{10,8},{12,14},{14,12},{16,18},{18,... | collective-permute-start | bytes 393224 | tf_op jit(solution)/shard_map/ppermute | solution.py:427
  33.6 1.4 %inner_terms.6 = (bf16[384,256]{1,0:T(8,128)(2,1)S(1)}, f32[384,128]{1,0:T(8,128)S(1)}, f32[384,128]{1,0:T(8,128)S(1)}) custom-call(bf16[384,128]{1,0:T(8,128)(2,1)S(1)} %get-tuple-element.82.refs_0_.b, bf16[384,128]{1,0:T(8,128)(2,1)S(1)} %get-tuple-element.83.refs_1_.c, bf16[384,1024]{1,0:T(8,128)(2,1)S(1)} %get-tuple-element.84.refs_2_.refs_0_, ...), custom_call_target="tpu_custom_call" | custom-call | flops 805306368 | bytes 3145728 | tf_op jit(solution)/shard_map/inner_terms/pallas_call | solution.py:580
  35.0 0.4 member_entries.2
  35.4 1.9 %collective-permute-start.9 = (bf16[256,256]{1,0:T(8,128)(2,1)S(1)}, bf16[256,256]{1,0:T(8,128)(2,1)S(1)}, u32[]{:S(2)}, u32[]{:S(2)}) collective-permute-start(bf16[256,256]{1,0:T(8,128)(2,1)S(1)} %get-tuple-element.123), channel_id=1, source_target_pairs={{0,6},{2,4},{4,2},{6,0},{8,14},{10,12},{12,10},{14,8},{16,22},{18,... | collective-permute-start | bytes 393224 | tf_op jit(solution)/shard_map/ppermute | solution.py:427
  37.3 1.2 %collective-permute-start.10 = (bf16[256,256]{1,0:T(8,128)(2,1)S(1)}, bf16[256,256]{1,0:T(8,128)(2,1)S(1)}, u32[]{:S(2)}, u32[]{:S(2)}) collective-permute-start(bf16[256,256]{1,0:T(8,128)(2,1)S(1)} %get-tuple-element.124), channel_id=1, source_target_pairs={{0,4},{2,6},{4,0},{6,2},{8,12},{10,14},{12,8},{14,10},{16,20},{18,... | collective-permute-start | bytes 393224 | tf_op jit(solution)/shard_map/ppermute | solution.py:427
  38.5 0.0 collective-permute-done.13.refs_9_
  38.5 0.5 %collective-permute-start.11 = (bf16[256,256]{1,0:T(8,128)(2,1)S(1)}, bf16[256,256]{1,0:T(8,128)(2,1)S(1)}, u32[]{:S(2)}, u32[]{:S(2)}) collective-permute-start(bf16[256,256]{1,0:T(8,128)(2,1)S(1)} %get-tuple-element.125), channel_id=1, source_target_pairs={{0,2},{2,0},{4,6},{6,4},{8,10},{10,8},{12,14},{14,12},{16,18},{18,... | collective-permute-start | bytes 393224 | tf_op jit(solution)/shard_map/ppermute | solution.py:427
  38.9 3.1 %inner_terms.7 = (bf16[384,256]{1,0:T(8,128)(2,1)S(1)}, bf16[384,256]{1,0:T(8,128)(2,1)S(1)}, bf16[384,256]{1,0:T(8,128)(2,1)S(1)}, f32[384,128]{1,0:T(8,128)S(1)}, f32[384,128]{1,0:T(8,128)S(1)}) custom-call(bf16[384,128]{1,0:T(8,128)(2,1)S(1)} %get-tuple-element.82.refs_0_.b, bf16[384,128]{1,0:T(8,128)(2,1)S(1)} %get-tuple-element.83.refs_1_.c, ...), custom_call_target="tpu_custom_call" | custom-call | flops 805306368 | bytes 3145728 | tf_op jit(solution)/shard_map/inner_terms/pallas_call | solution.py:580
  42.0 0.0 collective-permute-done.14.refs_10_
  42.0 0.0 collective-permute-done.15.refs_11_
  42.0 0.5 %entry_values.1.refs_12_.refs_6_ = bf16[384,1024]{1,0:T(8,128)(2,1)S(1)} custom-call(s32[1]{0:T(128)} %bitcast.where, bf16[384,128]{1,0:T(8,128)(2,1)S(1)} %get-tuple-element.82.refs_0_.b, bf16[384,256]{1,0:T(8,128)(2,1)S(1)} %get-tuple-element.126.refs_0_, bf16[384,256]{1,0:T(8,128)(2,1)S(1)} %get-tuple-element.127.refs_1_, ...), custom_call_target="tpu_custom_call" | custom-call | flops 100663296 | bytes 1572864 | tf_op jit(solution)/shard_map/entry_values/pallas_call | solution.py:678
  42.5 0.6 %entry_parts.3 = (f32[384,128]{1,0:T(8,128)S(1)}, f32[384,128]{1,0:T(8,128)S(1)}) custom-call(f32[384,128]{1,0:T(8,128)S(1)} %get-tuple-element.138.db_before, f32[384,128]{1,0:T(8,128)S(1)} %get-tuple-element.139.dc_before, bf16[384,256]{1,0:T(8,128)(2,1)S(1)} %get-tuple-element.140.refs_0_, bf16[384,256]{1,0:T(8,128)(2,1)S(1)} %get-tuple-element.141.refs_1_, ...), custom_call_target="tpu_custom_call" | custom-call | flops 301989888 | bytes 98304 | tf_op jit(solution)/shard_map/entry_parts/pallas_call | solution.py:617
  43.1 0.0 collective-permute-done.9.refs_9_.refs_5_
  43.1 0.4 entry_parts.4
  43.5 0.3 collective-permute-done.11.refs_11_.refs_5_
  43.8 0.4 entry_parts.5.refs_0_
  44.1 0.1 collective-permute-start.16
  44.2 1.3 %last_values.1 = bf16[384,2048]{1,0:T(8,128)(2,1)} custom-call(s32[1]{0:T(128)} %bitcast.where, bf16[384,128]{1,0:T(8,128)(2,1)S(1)} %get-tuple-element.82.refs_0_.b, bf16[384,256]{1,0:T(8,128)(2,1)S(1)} %get-tuple-element.112.refs_0_, bf16[384,256]{1,0:T(8,128)(2,1)S(1)} %get-tuple-element.116.refs_1_, bf16[384,256]{1,0:T(8,128)(2,1)S(1)} %get-tuple-element.117.refs_2_, ...), custom_call_target="tpu_custom_call" | custom-call | flops 100663296 | bytes 1572864 | tf_op jit(solution)/shard_map/last_values/pallas_call | solution.py:688
  45.5 0.1 collective-permute-done.16.refs_1_
  45.6 0.7 %sum_over_heads.1 = (bf16[384,128]{1,0:T(8,128)(2,1)}, bf16[384,128]{1,0:T(8,128)(2,1)}) custom-call(bf16[768,128]{1,0:T(8,128)(2,1)S(1)} %entry_parts.5.refs_0_, bf16[768,128]{1,0:T(8,128)(2,1)S(1)} %collective-permute-done.16.refs_1_), custom_call_target="tpu_custom_call" | custom-call | flops 196608 | bytes 393216 | tf_op jit(solution)/shard_map/sum_over_heads/pallas_call | solution.py:720
  (5 shorter events, 0.1 us)
Async XLA Ops:
  3.3 11.3 %collective-permute-start = (bf16[272,256]{1,0:T(8,128)(2,1)S(1)}, bf16[272,256]{1,0:T(8,128)(2,1)S(1)}, u32[]{:S(2)}, u32[]{:S(2)}) collective-permute-start(bf16[272,256]{1,0:T(8,128)(2,1)S(1)} %get-tuple-element.101), channel_id=1, source_target_pairs={{0,6},{2,4},{4,2},{6,0},{8,14},{10,12},{12,10},{14,8},{16,22},{18,... | collective-permute-start | bytes 417800 | tf_op jit(solution)/shard_map/ppermute | solution.py:427
  7.3 7.9 %collective-permute-start.1 = (bf16[272,256]{1,0:T(8,128)(2,1)S(1)}, bf16[272,256]{1,0:T(8,128)(2,1)S(1)}, u32[]{:S(2)}, u32[]{:S(2)}) collective-permute-start(bf16[272,256]{1,0:T(8,128)(2,1)S(1)} %get-tuple-element.102), channel_id=1, source_target_pairs={{0,4},{2,6},{4,0},{6,2},{8,12},{10,14},{12,8},{14,10},{16,20},{18,... | collective-permute-start | bytes 417800 | tf_op jit(solution)/shard_map/ppermute | solution.py:427
  7.8 7.4 %collective-permute-start.2 = (bf16[272,256]{1,0:T(8,128)(2,1)S(1)}, bf16[272,256]{1,0:T(8,128)(2,1)S(1)}, u32[]{:S(2)}, u32[]{:S(2)}) collective-permute-start(bf16[272,256]{1,0:T(8,128)(2,1)S(1)} %get-tuple-element.103), channel_id=1, source_target_pairs={{0,2},{2,0},{4,6},{6,4},{8,10},{10,8},{12,14},{14,12},{16,18},{18,... | collective-permute-start | bytes 417800 | tf_op jit(solution)/shard_map/ppermute | solution.py:427
  11.1 7.6 %collective-permute-start.4 = (bf16[272,256]{1,0:T(8,128)(2,1)S(1)}, bf16[272,256]{1,0:T(8,128)(2,1)S(1)}, u32[]{:S(2)}, u32[]{:S(2)}) collective-permute-start(bf16[272,256]{1,0:T(8,128)(2,1)S(1)} %get-tuple-element.109), channel_id=1, source_target_pairs={{0,6},{2,4},{4,2},{6,0},{8,14},{10,12},{12,10},{14,8},{16,22},{18,... | collective-permute-start | bytes 417800 | tf_op jit(solution)/shard_map/ppermute | solution.py:427
  14.1 5.9 %collective-permute-start.5 = (bf16[272,256]{1,0:T(8,128)(2,1)S(1)}, bf16[272,256]{1,0:T(8,128)(2,1)S(1)}, u32[]{:S(2)}, u32[]{:S(2)}) collective-permute-start(bf16[272,256]{1,0:T(8,128)(2,1)S(1)} %get-tuple-element.110), channel_id=1, source_target_pairs={{0,4},{2,6},{4,0},{6,2},{8,12},{10,14},{12,8},{14,10},{16,20},{18,... | collective-permute-start | bytes 417800 | tf_op jit(solution)/shard_map/ppermute | solution.py:427
  14.6 5.6 %collective-permute-start.6 = (bf16[272,256]{1,0:T(8,128)(2,1)S(1)}, bf16[272,256]{1,0:T(8,128)(2,1)S(1)}, u32[]{:S(2)}, u32[]{:S(2)}) collective-permute-start(bf16[272,256]{1,0:T(8,128)(2,1)S(1)} %get-tuple-element.111), channel_id=1, source_target_pairs={{0,2},{2,0},{4,6},{6,4},{8,10},{10,8},{12,14},{14,12},{16,18},{18,... | collective-permute-start | bytes 417800 | tf_op jit(solution)/shard_map/ppermute | solution.py:427
  15.3 6.6 %collective-permute-start.3 = (bf16[272,256]{1,0:T(8,128)(2,1)S(1)}, bf16[272,256]{1,0:T(8,128)(2,1)S(1)}, u32[]{:S(2)}, u32[]{:S(2)}) collective-permute-start(bf16[272,256]{1,0:T(8,128)(2,1)S(1)} %totals.2.refs_11_.own), channel_id=1, source_target_pairs={{0,8},{2,10},{4,12},{6,14},{8,0},{10,2},{12,4},{14,6},{16,24},{18,... | collective-permute-start | bytes 417800 | tf_op jit(solution)/shard_map/ppermute | solution.py:753
  20.3 9.4 %collective-permute-start.7 = (bf16[272,256]{1,0:T(8,128)(2,1)S(1)}, bf16[272,256]{1,0:T(8,128)(2,1)S(1)}, u32[]{:S(2)}, u32[]{:S(2)}) collective-permute-start(bf16[272,256]{1,0:T(8,128)(2,1)S(1)} %totals.3.own), channel_id=1, source_target_pairs={{0,8},{2,10},{4,12},{6,14},{8,0},{10,2},{12,4},{14,6},{16,24},{18,... | collective-permute-start | bytes 417800 | tf_op jit(solution)/shard_map/ppermute | solution.py:753
  22.0 5.7 %collective-permute-start.12 = (bf16[128,256]{1,0:T(8,128)(2,1)S(1)}, bf16[128,256]{1,0:T(8,128)(2,1)S(1)}, u32[]{:S(2)}, u32[]{:S(2)}) collective-permute-start(bf16[128,256]{1,0:T(8,128)(2,1)S(1)} %merged.2.refs_13_), channel_id=1, source_target_pairs={{0,16},{2,18},{4,20},{6,22},{8,24},{10,26},{12,28},{14,30},{16,0},... | collective-permute-start | bytes 196616 | tf_op jit(solution)/shard_map/ppermute | solution.py:753
  27.9 10.6 %collective-permute-start.13 = (bf16[256,256]{1,0:T(8,128)(2,1)S(1)}, bf16[256,256]{1,0:T(8,128)(2,1)S(1)}, u32[]{:S(2)}, u32[]{:S(2)}) collective-permute-start(bf16[256,256]{1,0:T(8,128)(2,1)S(1)} %get-tuple-element.135), channel_id=1, source_target_pairs={{0,6},{2,4},{4,2},{6,0},{8,14},{10,12},{12,10},{14,8},{16,22},{18,... | collective-permute-start | bytes 393224 | tf_op jit(solution)/shard_map/ppermute | solution.py:427
  29.7 5.3 %collective-permute-start.8 = (bf16[128,256]{1,0:T(8,128)(2,1)S(1)}, bf16[128,256]{1,0:T(8,128)(2,1)S(1)}, u32[]{:S(2)}, u32[]{:S(2)}) collective-permute-start(bf16[128,256]{1,0:T(8,128)(2,1)S(1)} %merged.3.refs_13_), channel_id=1, source_target_pairs={{0,16},{2,18},{4,20},{6,22},{8,24},{10,26},{12,28},{14,30},{16,0},... | collective-permute-start | bytes 196616 | tf_op jit(solution)/shard_map/ppermute | solution.py:753
  31.9 10.1 %collective-permute-start.14 = (bf16[256,256]{1,0:T(8,128)(2,1)S(1)}, bf16[256,256]{1,0:T(8,128)(2,1)S(1)}, u32[]{:S(2)}, u32[]{:S(2)}) collective-permute-start(bf16[256,256]{1,0:T(8,128)(2,1)S(1)} %get-tuple-element.136), channel_id=1, source_target_pairs={{0,4},{2,6},{4,0},{6,2},{8,12},{10,14},{12,8},{14,10},{16,20},{18,... | collective-permute-start | bytes 393224 | tf_op jit(solution)/shard_map/ppermute | solution.py:427
  33.2 8.9 %collective-permute-start.15 = (bf16[256,256]{1,0:T(8,128)(2,1)S(1)}, bf16[256,256]{1,0:T(8,128)(2,1)S(1)}, u32[]{:S(2)}, u32[]{:S(2)}) collective-permute-start(bf16[256,256]{1,0:T(8,128)(2,1)S(1)} %get-tuple-element.137), channel_id=1, source_target_pairs={{0,2},{2,0},{4,6},{6,4},{8,10},{10,8},{12,14},{14,12},{16,18},{18,... | collective-permute-start | bytes 393224 | tf_op jit(solution)/shard_map/ppermute | solution.py:427
  35.4 7.7 %collective-permute-start.9 = (bf16[256,256]{1,0:T(8,128)(2,1)S(1)}, bf16[256,256]{1,0:T(8,128)(2,1)S(1)}, u32[]{:S(2)}, u32[]{:S(2)}) collective-permute-start(bf16[256,256]{1,0:T(8,128)(2,1)S(1)} %get-tuple-element.123), channel_id=1, source_target_pairs={{0,6},{2,4},{4,2},{6,0},{8,14},{10,12},{12,10},{14,8},{16,22},{18,... | collective-permute-start | bytes 393224 | tf_op jit(solution)/shard_map/ppermute | solution.py:427
  37.3 6.2 %collective-permute-start.10 = (bf16[256,256]{1,0:T(8,128)(2,1)S(1)}, bf16[256,256]{1,0:T(8,128)(2,1)S(1)}, u32[]{:S(2)}, u32[]{:S(2)}) collective-permute-start(bf16[256,256]{1,0:T(8,128)(2,1)S(1)} %get-tuple-element.124), channel_id=1, source_target_pairs={{0,4},{2,6},{4,0},{6,2},{8,12},{10,14},{12,8},{14,10},{16,20},{18,... | collective-permute-start | bytes 393224 | tf_op jit(solution)/shard_map/ppermute | solution.py:427
  38.5 5.3 %collective-permute-start.11 = (bf16[256,256]{1,0:T(8,128)(2,1)S(1)}, bf16[256,256]{1,0:T(8,128)(2,1)S(1)}, u32[]{:S(2)}, u32[]{:S(2)}) collective-permute-start(bf16[256,256]{1,0:T(8,128)(2,1)S(1)} %get-tuple-element.125), channel_id=1, source_target_pairs={{0,2},{2,0},{4,6},{6,4},{8,10},{10,8},{12,14},{14,12},{16,18},{18,... | collective-permute-start | bytes 393224 | tf_op jit(solution)/shard_map/ppermute | solution.py:427
  44.1 1.5 %collective-permute-start.16 = (bf16[768,128]{1,0:T(8,128)(2,1)S(1)}, bf16[768,128]{1,0:T(8,128)(2,1)S(1)}, u32[]{:S(2)}, u32[]{:S(2)}) collective-permute-start(bf16[768,128]{1,0:T(8,128)(2,1)S(1)} %entry_parts.5.refs_0_), channel_id=1, source_target_pairs={{0,1},{1,0},{2,3},{3,2},{4,5},{5,4},{6,7},{7,6},{8,9},{9,8},{10,11... | collective-permute-start | bytes 589832 | tf_op jit(solution)/shard_map/ppermute | solution.py:719

commit v21 on v20

--- a/solution.py
+++ b/solution.py
@@ -753,8 +753,9 @@
         return lax.ppermute(block, "seq", [(s, s ^ (k * group)) for s in range(count)])
 
     every = [(chunk, m) for chunk in range(chunks) for m in range(group)]
-    worked = [every[1:4]] + [every[chunk * group :][:1] for chunk in range(1, chunks)]
-    rest = [one for one in every[1:] if not any(one in some for some in worked)]
+    early, rest = every[:2], every[2:]
+    worked = [rest[:3]] + [[one for one in rest[3:] if one[0] == n][:1] for n in range(1, chunks)]
+    rest = [one for one in rest if not any(one in some for some in worked)]
     entries, inner, sums = [], {}, []
 
     def add_inner(some, after, hides=True):
@@ -762,7 +763,7 @@
         inner.update(found)
 
     own = [totals(state, 0, where, blocks[0], setup[-1:])]
-    add_inner(every[:1], own[0], False)
+    add_inner(early, own[0], False)
     own += [totals(state, 0, where, blocks[chunk], sums[:1]) for chunk in range(1, chunks)]
     for chunk in range(chunks):
         (total,) = own[chunk]

time: 46.5 us -> 46.5 us (level)
  transfers between devices with their start and end apart: 17 -> 17, of which waited for: 4 -> 5; matrix products, arithmetic and copies ran while one was open for 0% -> 0% of each run, Pallas kernels for 35% -> 34%
where the time goes in v21:
time: 46.5 us; the launch traced here: 46.3 us
  starting transfers between devices  23.8 us (51%)
  Pallas kernels  19.6 us (42%)
  waiting for transfers between devices  2.07 us (4%)
  between operations  0.85 us (2%)
    ppermute x12, starting transfers between devices, exchange(): out[k] = lax.ppermute(parts[k], 'seq', [(s, s ^ k) for s in range(count)])  15.2 us
    pallas_call x4, Pallas kernels, inner_terms(): pl.pallas_call(functools.partial(inner_kernel, head_dim, worked, chunks,...  8.6 us
    ppermute x4, starting transfers between devices, to_group(): lax.ppermute(block, 'seq', [(s, s ^ k * group) for s in range(count)])  8.55 us
    pallas_call x1, Pallas kernels, next_states(): pl.pallas_call(functools.partial(next_states_kernel, head_dim, chunks, pi...  3.23 us
    pallas_call x1, Pallas kernels, first_states(): pl.pallas_call(functools.partial(first_states_kernel, head_dim, chunks, p...  2.67 us
    ppermute x12, waiting for transfers between devices, exchange(): out[k] = lax.ppermute(parts[k], 'seq', [(s, s ^ k) for s in range(count)])  1.92 us
    pallas_call x3, Pallas kernels, entry_parts(): pl.pallas_call(functools.partial(parts_kernel, last, ks), out_shape=outs,...  1.32 us
    pallas_call x1, Pallas kernels, entry_values(): pl.pallas_call(functools.partial(last_values_kernel, chunks), out_shape=p...  1.29 us
  transfers between devices with their start and end apart: 17, of which 5 were waited for; matrix products, arithmetic and copies ran while one was open for 0% of the time, Pallas kernels for 34%

profile of v21, /device:TPU:0, one launch (start us, length us, event | category | flops | bytes accessed | tf_op | source)
XLA Modules:
  0.0 46.3 jit_solution(7471822230766203297)
XLA Ops:
  0.6 2.7 %first_states.1 = (f32[32,384]{1,0:T(8,128)S(1)}, bf16[384,128]{1,0:T(8,128)(2,1)S(1)}, bf16[384,128]{1,0:T(8,128)(2,1)S(1)}, bf16[384,1024]{1,0:T(8,128)(2,1)S(...) custom-call(s32[1]{0:T(128)} %bitcast.where, ...), custom_call_target="tpu_custom_call" | custom-call | flops 402653184 | bytes 6291456 | tf_op jit(solution)/shard_map/first_states/pallas_call | solution.py:218
  3.3 4.0 %collective-permute-start = (bf16[272,256]{1,0:T(8,128)(2,1)S(1)}, bf16[272,256]{1,0:T(8,128)(2,1)S(1)}, u32[]{:S(2)}, u32[]{:S(2)}) collective-permute-start(bf16[272,256]{1,0:T(8,128)(2,1)S(1)} %get-tuple-element.101), channel_id=1, source_target_pairs={{0,6},{2,4},{4,2},{6,0},{8,14},{10,12},{12,10},{14,8},{16,22},{18,... | collective-permute-start | bytes 417800 | tf_op jit(solution)/shard_map/ppermute | solution.py:427
  7.3 0.5 %collective-permute-start.1 = (bf16[272,256]{1,0:T(8,128)(2,1)S(1)}, bf16[272,256]{1,0:T(8,128)(2,1)S(1)}, u32[]{:S(2)}, u32[]{:S(2)}) collective-permute-start(bf16[272,256]{1,0:T(8,128)(2,1)S(1)} %get-tuple-element.102), channel_id=1, source_target_pairs={{0,4},{2,6},{4,0},{6,2},{8,12},{10,14},{12,8},{14,10},{16,20},{18,... | collective-permute-start | bytes 417800 | tf_op jit(solution)/shard_map/ppermute | solution.py:427
  7.8 0.1 collective-permute-start.2
  7.9 3.2 %next_states.1 = (bf16[384,1024]{1,0:T(8,128)(2,1)S(1)}, bf16[384,1024]{1,0:T(8,128)(2,1)S(1)}, bf16[384,256]{1,0:T(8,128)(2,1)S(1)}, bf16[384,256]{1,0:T(8,128)...) custom-call(s32[1]{0:T(128)} %bitcast.where, ...), custom_call_target="tpu_custom_call" | custom-call | flops 402653184 | bytes 3145728 | tf_op jit(solution)/shard_map/next_states/pallas_call | solution.py:237
  11.2 2.9 %collective-permute-start.4 = (bf16[272,256]{1,0:T(8,128)(2,1)S(1)}, bf16[272,256]{1,0:T(8,128)(2,1)S(1)}, u32[]{:S(2)}, u32[]{:S(2)}) collective-permute-start(bf16[272,256]{1,0:T(8,128)(2,1)S(1)} %get-tuple-element.110), channel_id=1, source_target_pairs={{0,6},{2,4},{4,2},{6,0},{8,14},{10,12},{12,10},{14,8},{16,22},{18,... | collective-permute-start | bytes 417800 | tf_op jit(solution)/shard_map/ppermute | solution.py:427
  14.1 0.5 %collective-permute-start.5 = (bf16[272,256]{1,0:T(8,128)(2,1)S(1)}, bf16[272,256]{1,0:T(8,128)(2,1)S(1)}, u32[]{:S(2)}, u32[]{:S(2)}) collective-permute-start(bf16[272,256]{1,0:T(8,128)(2,1)S(1)} %get-tuple-element.111), channel_id=1, source_target_pairs={{0,4},{2,6},{4,0},{6,2},{8,12},{10,14},{12,8},{14,10},{16,20},{18,... | collective-permute-start | bytes 417800 | tf_op jit(solution)/shard_map/ppermute | solution.py:427
  14.6 0.0 collective-permute-done.refs_1_.refs_5_
  14.6 0.1 collective-permute-start.6
  14.7 0.5 inner_setup.1
  15.2 0.0 collective-permute-done.1.refs_2_.refs_4_
  15.2 0.0 collective-permute-done.2.refs_3_
  15.2 0.1 totals.2.refs_11_.own
  15.3 2.0 %collective-permute-start.3 = (bf16[272,256]{1,0:T(8,128)(2,1)S(1)}, bf16[272,256]{1,0:T(8,128)(2,1)S(1)}, u32[]{:S(2)}, u32[]{:S(2)}) collective-permute-start(bf16[272,256]{1,0:T(8,128)(2,1)S(1)} %totals.2.refs_11_.own), channel_id=1, source_target_pairs={{0,8},{2,10},{4,12},{6,14},{8,0},{10,2},{12,4},{14,6},{16,24},{18,... | collective-permute-start | bytes 417800 | tf_op jit(solution)/shard_map/ppermute | solution.py:753
  17.4 2.1 %inner_terms.4 = (bf16[384,256]{1,0:T(8,128)(2,1)S(1)}, bf16[384,256]{1,0:T(8,128)(2,1)S(1)}, f32[384,128]{1,0:T(8,128)S(1)}, f32[384,128]{1,0:T(8,128)S(1)}) custom-call(bf16[384,128]{1,0:T(8,128)(2,1)S(1)} %get-tuple-element.82.refs_0_.b, bf16[384,128]{1,0:T(8,128)(2,1)S(1)} %get-tuple-element.83.refs_1_.c, ...), custom_call_target="tpu_custom_call" | custom-call | flops 1 | bytes 1 | tf_op jit(solution)/shard_map/inner_terms/pallas_call | solution.py:580
  19.5 0.0 collective-permute-done.4.refs_1_.refs_5_
  19.5 0.5 %collective-permute-done.5.refs_2_.refs_4_ = bf16[272,256]{1,0:T(8,128)(2,1)S(1)} collective-permute-done((bf16[272,256]{1,0:T(8,128)(2,1)S(1)}, bf16[272,256]{1,0:T(8,128)(2,1)S(1)}, u32[]{:S(2)}, u32[]{:S(2)}) %collective-permute-start.5) | collective-permute-done | bytes 139296 | tf_op jit(solution)/shard_map/ppermute | solution.py:427
  20.0 0.2 collective-permute-done.6.refs_3_
  20.2 0.1 totals.3.own
  20.3 1.6 %collective-permute-start.7 = (bf16[272,256]{1,0:T(8,128)(2,1)S(1)}, bf16[272,256]{1,0:T(8,128)(2,1)S(1)}, u32[]{:S(2)}, u32[]{:S(2)}) collective-permute-start(bf16[272,256]{1,0:T(8,128)(2,1)S(1)} %totals.3.own), channel_id=1, source_target_pairs={{0,8},{2,10},{4,12},{6,14},{8,0},{10,2},{12,4},{14,6},{16,24},{18,... | collective-permute-start | bytes 417800 | tf_op jit(solution)/shard_map/ppermute | solution.py:753
  21.9 0.0 collective-permute-done.3.received.refs_0_
  22.0 2.6 %collective-permute-start.12 = (bf16[128,256]{1,0:T(8,128)(2,1)S(1)}, bf16[128,256]{1,0:T(8,128)(2,1)S(1)}, u32[]{:S(2)}, u32[]{:S(2)}) collective-permute-start(bf16[128,256]{1,0:T(8,128)(2,1)S(1)} %merged.2.refs_13_), channel_id=1, source_target_pairs={{0,16},{2,18},{4,20},{6,22},{8,24},{10,26},{12,28},{14,30},{16,0},... | collective-permute-start | bytes 196616 | tf_op jit(solution)/shard_map/ppermute | solution.py:753
  24.6 3.1 %inner_terms.5 = (bf16[384,256]{1,0:T(8,128)(2,1)S(1)}, bf16[384,256]{1,0:T(8,128)(2,1)S(1)}, bf16[384,256]{1,0:T(8,128)(2,1)S(1)}, f32[384,128]{1,0:T(8,128)S(1)}, f32[384,128]{1,0:T(8,128)S(1)}) custom-call(bf16[384,128]{1,0:T(8,128)(2,1)S(1)} %get-tuple-element.82.refs_0_.b, bf16[384,128]{1,0:T(8,128)(2,1)S(1)} %get-tuple-element.83.refs_1_.c, ...), custom_call_target="tpu_custom_call" | custom-call | flops 805306368 | bytes 3145728 | tf_op jit(solution)/shard_map/inner_terms/pallas_call | solution.py:580
  27.7 0.2 member_entries.3
  27.9 1.7 %collective-permute-start.13 = (bf16[256,256]{1,0:T(8,128)(2,1)S(1)}, bf16[256,256]{1,0:T(8,128)(2,1)S(1)}, u32[]{:S(2)}, u32[]{:S(2)}) collective-permute-start(bf16[256,256]{1,0:T(8,128)(2,1)S(1)} %get-tuple-element.135), channel_id=1, source_target_pairs={{0,6},{2,4},{4,2},{6,0},{8,14},{10,12},{12,10},{14,8},{16,22},{18,... | collective-permute-start | bytes 393224 | tf_op jit(solution)/shard_map/ppermute | solution.py:427
  29.6 0.0 collective-permute-done.7.received.refs_0_
  29.7 2.2 %collective-permute-start.8 = (bf16[128,256]{1,0:T(8,128)(2,1)S(1)}, bf16[128,256]{1,0:T(8,128)(2,1)S(1)}, u32[]{:S(2)}, u32[]{:S(2)}) collective-permute-start(bf16[128,256]{1,0:T(8,128)(2,1)S(1)} %merged.3.refs_13_), channel_id=1, source_target_pairs={{0,16},{2,18},{4,20},{6,22},{8,24},{10,26},{12,28},{14,30},{16,0},... | collective-permute-start | bytes 196616 | tf_op jit(solution)/shard_map/ppermute | solution.py:753
  31.9 1.3 %collective-permute-start.14 = (bf16[256,256]{1,0:T(8,128)(2,1)S(1)}, bf16[256,256]{1,0:T(8,128)(2,1)S(1)}, u32[]{:S(2)}, u32[]{:S(2)}) collective-permute-start(bf16[256,256]{1,0:T(8,128)(2,1)S(1)} %get-tuple-element.136), channel_id=1, source_target_pairs={{0,4},{2,6},{4,0},{6,2},{8,12},{10,14},{12,8},{14,10},{16,20},{18,... | collective-permute-start | bytes 393224 | tf_op jit(solution)/shard_map/ppermute | solution.py:427
  33.2 0.5 collective-permute-start.15
  33.6 1.4 %inner_terms.6 = (bf16[384,256]{1,0:T(8,128)(2,1)S(1)}, f32[384,128]{1,0:T(8,128)S(1)}, f32[384,128]{1,0:T(8,128)S(1)}) custom-call(bf16[384,128]{1,0:T(8,128)(2,1)S(1)} %get-tuple-element.82.refs_0_.b, bf16[384,128]{1,0:T(8,128)(2,1)S(1)} %get-tuple-element.83.refs_1_.c, bf16[384,1024]{1,0:T(8,128)(2,1)S(1)} %get-tuple-element.84.refs_2_.refs_0_, ...), custom_call_target="tpu_custom_call" | custom-call | flops 805306368 | bytes 3145728 | tf_op jit(solution)/shard_map/inner_terms/pallas_call | solution.py:580
  35.0 0.0 collective-permute-done.8.refs_1_
  35.0 0.4 member_entries.2
  35.4 1.9 %collective-permute-start.9 = (bf16[256,256]{1,0:T(8,128)(2,1)S(1)}, bf16[256,256]{1,0:T(8,128)(2,1)S(1)}, u32[]{:S(2)}, u32[]{:S(2)}) collective-permute-start(bf16[256,256]{1,0:T(8,128)(2,1)S(1)} %get-tuple-element.123), channel_id=1, source_target_pairs={{0,6},{2,4},{4,2},{6,0},{8,14},{10,12},{12,10},{14,8},{16,22},{18,... | collective-permute-start | bytes 393224 | tf_op jit(solution)/shard_map/ppermute | solution.py:427
  37.3 1.2 %collective-permute-start.10 = (bf16[256,256]{1,0:T(8,128)(2,1)S(1)}, bf16[256,256]{1,0:T(8,128)(2,1)S(1)}, u32[]{:S(2)}, u32[]{:S(2)}) collective-permute-start(bf16[256,256]{1,0:T(8,128)(2,1)S(1)} %get-tuple-element.124), channel_id=1, source_target_pairs={{0,4},{2,6},{4,0},{6,2},{8,12},{10,14},{12,8},{14,10},{16,20},{18,... | collective-permute-start | bytes 393224 | tf_op jit(solution)/shard_map/ppermute | solution.py:427
  38.5 0.0 collective-permute-done.13.refs_9_
  38.5 0.5 %collective-permute-start.11 = (bf16[256,256]{1,0:T(8,128)(2,1)S(1)}, bf16[256,256]{1,0:T(8,128)(2,1)S(1)}, u32[]{:S(2)}, u32[]{:S(2)}) collective-permute-start(bf16[256,256]{1,0:T(8,128)(2,1)S(1)} %get-tuple-element.125), channel_id=1, source_target_pairs={{0,2},{2,0},{4,6},{6,4},{8,10},{10,8},{12,14},{14,12},{16,18},{18,... | collective-permute-start | bytes 393224 | tf_op jit(solution)/shard_map/ppermute | solution.py:427
  38.9 2.1 %inner_terms.7 = (bf16[384,256]{1,0:T(8,128)(2,1)S(1)}, bf16[384,256]{1,0:T(8,128)(2,1)S(1)}, f32[384,128]{1,0:T(8,128)S(1)}, f32[384,128]{1,0:T(8,128)S(1)}) custom-call(bf16[384,128]{1,0:T(8,128)(2,1)S(1)} %get-tuple-element.82.refs_0_.b, bf16[384,128]{1,0:T(8,128)(2,1)S(1)} %get-tuple-element.83.refs_1_.c, ...), custom_call_target="tpu_custom_call" | custom-call | flops 805306368 | bytes 3145728 | tf_op jit(solution)/shard_map/inner_terms/pallas_call | solution.py:580
  41.0 0.0 collective-permute-done.15.refs_11_
  41.0 0.5 %entry_values.1.refs_12_.refs_6_ = bf16[384,1024]{1,0:T(8,128)(2,1)S(1)} custom-call(s32[1]{0:T(128)} %bitcast.where, bf16[384,128]{1,0:T(8,128)(2,1)S(1)} %get-tuple-element.82.refs_0_.b, bf16[384,256]{1,0:T(8,128)(2,1)S(1)} %get-tuple-element.126.refs_0_, bf16[384,256]{1,0:T(8,128)(2,1)S(1)} %get-tuple-element.127.refs_1_, ...), custom_call_target="tpu_custom_call" | custom-call | flops 100663296 | bytes 1572864 | tf_op jit(solution)/shard_map/entry_values/pallas_call | solution.py:678
  41.5 0.6 %entry_parts.3 = (f32[384,128]{1,0:T(8,128)S(1)}, f32[384,128]{1,0:T(8,128)S(1)}) custom-call(f32[384,128]{1,0:T(8,128)S(1)} %get-tuple-element.138.db_before, f32[384,128]{1,0:T(8,128)S(1)} %get-tuple-element.139.dc_before, bf16[384,256]{1,0:T(8,128)(2,1)S(1)} %get-tuple-element.140.refs_0_, bf16[384,256]{1,0:T(8,128)(2,1)S(1)} %get-tuple-element.141.refs_1_, ...), custom_call_target="tpu_custom_call" | custom-call | flops 301989888 | bytes 98304 | tf_op jit(solution)/shard_map/entry_parts/pallas_call | solution.py:617
  42.1 0.4 entry_parts.4
  42.5 0.6 %collective-permute-done.10.refs_10_.refs_4_ = bf16[256,256]{1,0:T(8,128)(2,1)S(1)} collective-permute-done((bf16[256,256]{1,0:T(8,128)(2,1)S(1)}, bf16[256,256]{1,0:T(8,128)(2,1)S(1)}, u32[]{:S(2)}, u32[]{:S(2)}) %collective-permute-start.10) | collective-permute-done | bytes 131104 | tf_op jit(solution)/shard_map/ppermute | solution.py:427
  43.1 0.7 %collective-permute-done.11.refs_11_.refs_5_ = bf16[256,256]{1,0:T(8,128)(2,1)S(1)} collective-permute-done((bf16[256,256]{1,0:T(8,128)(2,1)S(1)}, bf16[256,256]{1,0:T(8,128)(2,1)S(1)}, u32[]{:S(2)}, u32[]{:S(2)}) %collective-permute-start.11) | collective-permute-done | bytes 131104 | tf_op jit(solution)/shard_map/ppermute | solution.py:427
  43.8 0.4 entry_parts.5.refs_0_
  44.1 0.1 collective-permute-start.16
  44.2 1.3 %last_values.1 = bf16[384,2048]{1,0:T(8,128)(2,1)} custom-call(s32[1]{0:T(128)} %bitcast.where, bf16[384,128]{1,0:T(8,128)(2,1)S(1)} %get-tuple-element.82.refs_0_.b, bf16[384,256]{1,0:T(8,128)(2,1)S(1)} %get-tuple-element.106.refs_0_, bf16[384,256]{1,0:T(8,128)(2,1)S(1)} %get-tuple-element.113.refs_1_, bf16[384,256]{1,0:T(8,128)(2,1)S(1)} %get-tuple-element.117.refs_2_, ...), custom_call_target="tpu_custom_call" | custom-call | flops 100663296 | bytes 1572864 | tf_op jit(solution)/shard_map/last_values/pallas_call | solution.py:688
  45.5 0.1 collective-permute-done.16.refs_1_
  45.6 0.7 %sum_over_heads.1 = (bf16[384,128]{1,0:T(8,128)(2,1)}, bf16[384,128]{1,0:T(8,128)(2,1)}) custom-call(bf16[768,128]{1,0:T(8,128)(2,1)S(1)} %entry_parts.5.refs_0_, bf16[768,128]{1,0:T(8,128)(2,1)S(1)} %collective-permute-done.16.refs_1_), custom_call_target="tpu_custom_call" | custom-call | flops 196608 | bytes 393216 | tf_op jit(solution)/shard_map/sum_over_heads/pallas_call | solution.py:720
  (5 shorter events, 0.1 us)
Async XLA Ops:
  3.3 11.3 %collective-permute-start = (bf16[272,256]{1,0:T(8,128)(2,1)S(1)}, bf16[272,256]{1,0:T(8,128)(2,1)S(1)}, u32[]{:S(2)}, u32[]{:S(2)}) collective-permute-start(bf16[272,256]{1,0:T(8,128)(2,1)S(1)} %get-tuple-element.101), channel_id=1, source_target_pairs={{0,6},{2,4},{4,2},{6,0},{8,14},{10,12},{12,10},{14,8},{16,22},{18,... | collective-permute-start | bytes 417800 | tf_op jit(solution)/shard_map/ppermute | solution.py:427
  7.3 7.9 %collective-permute-start.1 = (bf16[272,256]{1,0:T(8,128)(2,1)S(1)}, bf16[272,256]{1,0:T(8,128)(2,1)S(1)}, u32[]{:S(2)}, u32[]{:S(2)}) collective-permute-start(bf16[272,256]{1,0:T(8,128)(2,1)S(1)} %get-tuple-element.102), channel_id=1, source_target_pairs={{0,4},{2,6},{4,0},{6,2},{8,12},{10,14},{12,8},{14,10},{16,20},{18,... | collective-permute-start | bytes 417800 | tf_op jit(solution)/shard_map/ppermute | solution.py:427
  7.8 7.4 %collective-permute-start.2 = (bf16[272,256]{1,0:T(8,128)(2,1)S(1)}, bf16[272,256]{1,0:T(8,128)(2,1)S(1)}, u32[]{:S(2)}, u32[]{:S(2)}) collective-permute-start(bf16[272,256]{1,0:T(8,128)(2,1)S(1)} %get-tuple-element.103), channel_id=1, source_target_pairs={{0,2},{2,0},{4,6},{6,4},{8,10},{10,8},{12,14},{14,12},{16,18},{18,... | collective-permute-start | bytes 417800 | tf_op jit(solution)/shard_map/ppermute | solution.py:427
  11.2 8.3 %collective-permute-start.4 = (bf16[272,256]{1,0:T(8,128)(2,1)S(1)}, bf16[272,256]{1,0:T(8,128)(2,1)S(1)}, u32[]{:S(2)}, u32[]{:S(2)}) collective-permute-start(bf16[272,256]{1,0:T(8,128)(2,1)S(1)} %get-tuple-element.110), channel_id=1, source_target_pairs={{0,6},{2,4},{4,2},{6,0},{8,14},{10,12},{12,10},{14,8},{16,22},{18,... | collective-permute-start | bytes 417800 | tf_op jit(solution)/shard_map/ppermute | solution.py:427
  14.1 5.9 %collective-permute-start.5 = (bf16[272,256]{1,0:T(8,128)(2,1)S(1)}, bf16[272,256]{1,0:T(8,128)(2,1)S(1)}, u32[]{:S(2)}, u32[]{:S(2)}) collective-permute-start(bf16[272,256]{1,0:T(8,128)(2,1)S(1)} %get-tuple-element.111), channel_id=1, source_target_pairs={{0,4},{2,6},{4,0},{6,2},{8,12},{10,14},{12,8},{14,10},{16,20},{18,... | collective-permute-start | bytes 417800 | tf_op jit(solution)/shard_map/ppermute | solution.py:427
  14.6 5.6 %collective-permute-start.6 = (bf16[272,256]{1,0:T(8,128)(2,1)S(1)}, bf16[272,256]{1,0:T(8,128)(2,1)S(1)}, u32[]{:S(2)}, u32[]{:S(2)}) collective-permute-start(bf16[272,256]{1,0:T(8,128)(2,1)S(1)} %get-tuple-element.112), channel_id=1, source_target_pairs={{0,2},{2,0},{4,6},{6,4},{8,10},{10,8},{12,14},{14,12},{16,18},{18,... | collective-permute-start | bytes 417800 | tf_op jit(solution)/shard_map/ppermute | solution.py:427
  15.3 6.6 %collective-permute-start.3 = (bf16[272,256]{1,0:T(8,128)(2,1)S(1)}, bf16[272,256]{1,0:T(8,128)(2,1)S(1)}, u32[]{:S(2)}, u32[]{:S(2)}) collective-permute-start(bf16[272,256]{1,0:T(8,128)(2,1)S(1)} %totals.2.refs_11_.own), channel_id=1, source_target_pairs={{0,8},{2,10},{4,12},{6,14},{8,0},{10,2},{12,4},{14,6},{16,24},{18,... | collective-permute-start | bytes 417800 | tf_op jit(solution)/shard_map/ppermute | solution.py:753
  20.3 9.3 %collective-permute-start.7 = (bf16[272,256]{1,0:T(8,128)(2,1)S(1)}, bf16[272,256]{1,0:T(8,128)(2,1)S(1)}, u32[]{:S(2)}, u32[]{:S(2)}) collective-permute-start(bf16[272,256]{1,0:T(8,128)(2,1)S(1)} %totals.3.own), channel_id=1, source_target_pairs={{0,8},{2,10},{4,12},{6,14},{8,0},{10,2},{12,4},{14,6},{16,24},{18,... | collective-permute-start | bytes 417800 | tf_op jit(solution)/shard_map/ppermute | solution.py:753
  22.0 5.7 %collective-permute-start.12 = (bf16[128,256]{1,0:T(8,128)(2,1)S(1)}, bf16[128,256]{1,0:T(8,128)(2,1)S(1)}, u32[]{:S(2)}, u32[]{:S(2)}) collective-permute-start(bf16[128,256]{1,0:T(8,128)(2,1)S(1)} %merged.2.refs_13_), channel_id=1, source_target_pairs={{0,16},{2,18},{4,20},{6,22},{8,24},{10,26},{12,28},{14,30},{16,0},... | collective-permute-start | bytes 196616 | tf_op jit(solution)/shard_map/ppermute | solution.py:753
  27.9 10.6 %collective-permute-start.13 = (bf16[256,256]{1,0:T(8,128)(2,1)S(1)}, bf16[256,256]{1,0:T(8,128)(2,1)S(1)}, u32[]{:S(2)}, u32[]{:S(2)}) collective-permute-start(bf16[256,256]{1,0:T(8,128)(2,1)S(1)} %get-tuple-element.135), channel_id=1, source_target_pairs={{0,6},{2,4},{4,2},{6,0},{8,14},{10,12},{12,10},{14,8},{16,22},{18,... | collective-permute-start | bytes 393224 | tf_op jit(solution)/shard_map/ppermute | solution.py:427
  29.7 5.3 %collective-permute-start.8 = (bf16[128,256]{1,0:T(8,128)(2,1)S(1)}, bf16[128,256]{1,0:T(8,128)(2,1)S(1)}, u32[]{:S(2)}, u32[]{:S(2)}) collective-permute-start(bf16[128,256]{1,0:T(8,128)(2,1)S(1)} %merged.3.refs_13_), channel_id=1, source_target_pairs={{0,16},{2,18},{4,20},{6,22},{8,24},{10,26},{12,28},{14,30},{16,0},... | collective-permute-start | bytes 196616 | tf_op jit(solution)/shard_map/ppermute | solution.py:753
  31.9 9.1 %collective-permute-start.14 = (bf16[256,256]{1,0:T(8,128)(2,1)S(1)}, bf16[256,256]{1,0:T(8,128)(2,1)S(1)}, u32[]{:S(2)}, u32[]{:S(2)}) collective-permute-start(bf16[256,256]{1,0:T(8,128)(2,1)S(1)} %get-tuple-element.136), channel_id=1, source_target_pairs={{0,4},{2,6},{4,0},{6,2},{8,12},{10,14},{12,8},{14,10},{16,20},{18,... | collective-permute-start | bytes 393224 | tf_op jit(solution)/shard_map/ppermute | solution.py:427
  33.2 7.9 %collective-permute-start.15 = (bf16[256,256]{1,0:T(8,128)(2,1)S(1)}, bf16[256,256]{1,0:T(8,128)(2,1)S(1)}, u32[]{:S(2)}, u32[]{:S(2)}) collective-permute-start(bf16[256,256]{1,0:T(8,128)(2,1)S(1)} %get-tuple-element.137), channel_id=1, source_target_pairs={{0,2},{2,0},{4,6},{6,4},{8,10},{10,8},{12,14},{14,12},{16,18},{18,... | collective-permute-start | bytes 393224 | tf_op jit(solution)/shard_map/ppermute | solution.py:427
  35.4 6.8 %collective-permute-start.9 = (bf16[256,256]{1,0:T(8,128)(2,1)S(1)}, bf16[256,256]{1,0:T(8,128)(2,1)S(1)}, u32[]{:S(2)}, u32[]{:S(2)}) collective-permute-start(bf16[256,256]{1,0:T(8,128)(2,1)S(1)} %get-tuple-element.123), channel_id=1, source_target_pairs={{0,6},{2,4},{4,2},{6,0},{8,14},{10,12},{12,10},{14,8},{16,22},{18,... | collective-permute-start | bytes 393224 | tf_op jit(solution)/shard_map/ppermute | solution.py:427
  37.3 5.8 %collective-permute-start.10 = (bf16[256,256]{1,0:T(8,128)(2,1)S(1)}, bf16[256,256]{1,0:T(8,128)(2,1)S(1)}, u32[]{:S(2)}, u32[]{:S(2)}) collective-permute-start(bf16[256,256]{1,0:T(8,128)(2,1)S(1)} %get-tuple-element.124), channel_id=1, source_target_pairs={{0,4},{2,6},{4,0},{6,2},{8,12},{10,14},{12,8},{14,10},{16,20},{18,... | collective-permute-start | bytes 393224 | tf_op jit(solution)/shard_map/ppermute | solution.py:427
  38.5 5.3 %collective-permute-start.11 = (bf16[256,256]{1,0:T(8,128)(2,1)S(1)}, bf16[256,256]{1,0:T(8,128)(2,1)S(1)}, u32[]{:S(2)}, u32[]{:S(2)}) collective-permute-start(bf16[256,256]{1,0:T(8,128)(2,1)S(1)} %get-tuple-element.125), channel_id=1, source_target_pairs={{0,2},{2,0},{4,6},{6,4},{8,10},{10,8},{12,14},{14,12},{16,18},{18,... | collective-permute-start | bytes 393224 | tf_op jit(solution)/shard_map/ppermute | solution.py:427
  44.1 1.5 %collective-permute-start.16 = (bf16[768,128]{1,0:T(8,128)(2,1)S(1)}, bf16[768,128]{1,0:T(8,128)(2,1)S(1)}, u32[]{:S(2)}, u32[]{:S(2)}) collective-permute-start(bf16[768,128]{1,0:T(8,128)(2,1)S(1)} %entry_parts.5.refs_0_), channel_id=1, source_target_pairs={{0,1},{1,0},{2,3},{3,2},{4,5},{5,4},{6,7},{7,6},{8,9},{9,8},{10,11... | collective-permute-start | bytes 589832 | tf_op jit(solution)/shard_map/ppermute | solution.py:719

commit v22 on v21

--- a/solution.py
+++ b/solution.py
@@ -754,7 +754,7 @@
 
     every = [(chunk, m) for chunk in range(chunks) for m in range(group)]
     early, rest = every[:2], every[2:]
-    worked = [rest[:3]] + [[one for one in rest[3:] if one[0] == n][:1] for n in range(1, chunks)]
+    worked = [rest[:3]] + [[]] * (chunks - 1)
     rest = [one for one in rest if not any(one in some for some in worked)]
     entries, inner, sums = [], {}, []
 
@@ -772,7 +772,8 @@
             last = level == levels - 2
             total = merged(state, level, last, where, total, received[level], [])
             received.append(to_group(total, 2 << level))
-        add_inner(worked[chunk], [total])
+        if worked[chunk]:
+            add_inner(worked[chunk], [total])
         found = member_entries(state, False, where, blocks[chunk], received, sums[:1])
         entries.append(exchange(found))
     if rest:

time: 46.5 us -> 46.5 us (level)
    ppermute x4, waiting for transfers between devices: 0.01 us -> 1.28 us  [to_group(): lax.ppermute(block, 'seq', [(s, s ^ k * group) for s in range(count)])]
    ppermute x12, waiting for transfers between devices: 1.92 us -> 1.05 us  [exchange(): out[k] = lax.ppermute(parts[k], 'seq', [(s, s ^ k) for s in range(count)])]
    pallas_call x4 -> x3, Pallas kernels: 8.6 us -> 8.24 us  [inner_terms(): pl.pallas_call(functools.partial(inner_kernel, head_dim, worked, chunks,...]
where the time goes in v22:
time: 46.5 us; the launch traced here: 46.3 us
  starting transfers between devices  23.8 us (51%)
  Pallas kernels  19.3 us (42%)
  waiting for transfers between devices  2.47 us (5%)
  between operations  0.84 us (2%)
    ppermute x12, starting transfers between devices, exchange(): out[k] = lax.ppermute(parts[k], 'seq', [(s, s ^ k) for s in range(count)])  15.2 us
    ppermute x4, starting transfers between devices, to_group(): lax.ppermute(block, 'seq', [(s, s ^ k * group) for s in range(count)])  8.54 us
    pallas_call x3, Pallas kernels, inner_terms(): pl.pallas_call(functools.partial(inner_kernel, head_dim, worked, chunks,...  8.24 us
    pallas_call x1, Pallas kernels, next_states(): pl.pallas_call(functools.partial(next_states_kernel, head_dim, chunks, pi...  3.23 us
    pallas_call x1, Pallas kernels, first_states(): pl.pallas_call(functools.partial(first_states_kernel, head_dim, chunks, p...  2.67 us
    pallas_call x3, Pallas kernels, entry_parts(): pl.pallas_call(functools.partial(parts_kernel, last, ks), out_shape=outs,...  1.31 us
    pallas_call x1, Pallas kernels, entry_values(): pl.pallas_call(functools.partial(last_values_kernel, chunks), out_shape=p...  1.29 us
    ppermute x4, waiting for transfers between devices, to_group(): lax.ppermute(block, 'seq', [(s, s ^ k * group) for s in range(count)])  1.28 us
  transfers between devices with their start and end apart: 17, of which 5 were waited for; matrix products, arithmetic and copies ran while one was open for 0% of the time, Pallas kernels for 34%

profile of v22, /device:TPU:0, one launch (start us, length us, event | category | flops | bytes accessed | tf_op | source)
XLA Modules:
  0.0 46.3 jit_solution(13453134547814301616)
XLA Ops:
  0.6 2.7 %first_states.1 = (f32[32,384]{1,0:T(8,128)S(1)}, bf16[384,128]{1,0:T(8,128)(2,1)S(1)}, bf16[384,128]{1,0:T(8,128)(2,1)S(1)}, bf16[384,1024]{1,0:T(8,128)(2,1)S(...) custom-call(s32[1]{0:T(128)} %bitcast.where, ...), custom_call_target="tpu_custom_call" | custom-call | flops 402653184 | bytes 6291456 | tf_op jit(solution)/shard_map/first_states/pallas_call | solution.py:218
  3.3 4.0 %collective-permute-start = (bf16[272,256]{1,0:T(8,128)(2,1)S(1)}, bf16[272,256]{1,0:T(8,128)(2,1)S(1)}, u32[]{:S(2)}, u32[]{:S(2)}) collective-permute-start(bf16[272,256]{1,0:T(8,128)(2,1)S(1)} %get-tuple-element.99), channel_id=1, source_target_pairs={{0,6},{2,4},{4,2},{6,0},{8,14},{10,12},{12,10},{14,8},{16,22},{18,... | collective-permute-start | bytes 417800 | tf_op jit(solution)/shard_map/ppermute | solution.py:427
  7.3 0.5 %collective-permute-start.1 = (bf16[272,256]{1,0:T(8,128)(2,1)S(1)}, bf16[272,256]{1,0:T(8,128)(2,1)S(1)}, u32[]{:S(2)}, u32[]{:S(2)}) collective-permute-start(bf16[272,256]{1,0:T(8,128)(2,1)S(1)} %get-tuple-element.100), channel_id=1, source_target_pairs={{0,4},{2,6},{4,0},{6,2},{8,12},{10,14},{12,8},{14,10},{16,20},{18,... | collective-permute-start | bytes 417800 | tf_op jit(solution)/shard_map/ppermute | solution.py:427
  7.8 0.1 collective-permute-start.2
  7.9 3.2 %next_states.1 = (bf16[384,1024]{1,0:T(8,128)(2,1)S(1)}, bf16[384,1024]{1,0:T(8,128)(2,1)S(1)}, bf16[384,256]{1,0:T(8,128)(2,1)S(1)}, bf16[384,256]{1,0:T(8,128)...) custom-call(s32[1]{0:T(128)} %bitcast.where, ...), custom_call_target="tpu_custom_call" | custom-call | flops 402653184 | bytes 3145728 | tf_op jit(solution)/shard_map/next_states/pallas_call | solution.py:237
  11.1 2.9 %collective-permute-start.4 = (bf16[272,256]{1,0:T(8,128)(2,1)S(1)}, bf16[272,256]{1,0:T(8,128)(2,1)S(1)}, u32[]{:S(2)}, u32[]{:S(2)}) collective-permute-start(bf16[272,256]{1,0:T(8,128)(2,1)S(1)} %get-tuple-element.108), channel_id=1, source_target_pairs={{0,6},{2,4},{4,2},{6,0},{8,14},{10,12},{12,10},{14,8},{16,22},{18,... | collective-permute-start | bytes 417800 | tf_op jit(solution)/shard_map/ppermute | solution.py:427
  14.1 0.5 %collective-permute-start.5 = (bf16[272,256]{1,0:T(8,128)(2,1)S(1)}, bf16[272,256]{1,0:T(8,128)(2,1)S(1)}, u32[]{:S(2)}, u32[]{:S(2)}) collective-permute-start(bf16[272,256]{1,0:T(8,128)(2,1)S(1)} %get-tuple-element.109), channel_id=1, source_target_pairs={{0,4},{2,6},{4,0},{6,2},{8,12},{10,14},{12,8},{14,10},{16,20},{18,... | collective-permute-start | bytes 417800 | tf_op jit(solution)/shard_map/ppermute | solution.py:427
  14.6 0.0 collective-permute-done.refs_1_.refs_5_
  14.6 0.1 collective-permute-start.6
  14.7 0.5 inner_setup.1
  15.2 0.0 collective-permute-done.1.refs_2_.refs_4_
  15.2 0.0 collective-permute-done.2.refs_3_
  15.2 0.1 totals.2.refs_11_.own
  15.3 2.0 %collective-permute-start.3 = (bf16[272,256]{1,0:T(8,128)(2,1)S(1)}, bf16[272,256]{1,0:T(8,128)(2,1)S(1)}, u32[]{:S(2)}, u32[]{:S(2)}) collective-permute-start(bf16[272,256]{1,0:T(8,128)(2,1)S(1)} %totals.2.refs_11_.own), channel_id=1, source_target_pairs={{0,8},{2,10},{4,12},{6,14},{8,0},{10,2},{12,4},{14,6},{16,24},{18,... | collective-permute-start | bytes 417800 | tf_op jit(solution)/shard_map/ppermute | solution.py:753
  17.4 2.1 %inner_terms.3 = (bf16[384,256]{1,0:T(8,128)(2,1)S(1)}, bf16[384,256]{1,0:T(8,128)(2,1)S(1)}, f32[384,128]{1,0:T(8,128)S(1)}, f32[384,128]{1,0:T(8,128)S(1)}) custom-call(bf16[384,128]{1,0:T(8,128)(2,1)S(1)} %get-tuple-element.80.refs_0_.b, bf16[384,128]{1,0:T(8,128)(2,1)S(1)} %get-tuple-element.81.refs_1_.c, ...), custom_call_target="tpu_custom_call" | custom-call | flops 1 | bytes 1 | tf_op jit(solution)/shard_map/inner_terms/pallas_call | solution.py:580
  19.5 0.0 collective-permute-done.4.refs_1_.refs_5_
  19.5 0.5 %collective-permute-done.5.refs_2_.refs_4_ = bf16[272,256]{1,0:T(8,128)(2,1)S(1)} collective-permute-done((bf16[272,256]{1,0:T(8,128)(2,1)S(1)}, bf16[272,256]{1,0:T(8,128)(2,1)S(1)}, u32[]{:S(2)}, u32[]{:S(2)}) %collective-permute-start.5) | collective-permute-done | bytes 139296 | tf_op jit(solution)/shard_map/ppermute | solution.py:427
  20.0 0.2 collective-permute-done.6.refs_3_
  20.2 0.1 totals.3.own
  20.3 1.6 %collective-permute-start.7 = (bf16[272,256]{1,0:T(8,128)(2,1)S(1)}, bf16[272,256]{1,0:T(8,128)(2,1)S(1)}, u32[]{:S(2)}, u32[]{:S(2)}) collective-permute-start(bf16[272,256]{1,0:T(8,128)(2,1)S(1)} %totals.3.own), channel_id=1, source_target_pairs={{0,8},{2,10},{4,12},{6,14},{8,0},{10,2},{12,4},{14,6},{16,24},{18,... | collective-permute-start | bytes 417800 | tf_op jit(solution)/shard_map/ppermute | solution.py:753
  21.9 0.0 collective-permute-done.3.received.refs_0_
  22.0 2.6 %collective-permute-start.12 = (bf16[128,256]{1,0:T(8,128)(2,1)S(1)}, bf16[128,256]{1,0:T(8,128)(2,1)S(1)}, u32[]{:S(2)}, u32[]{:S(2)}) collective-permute-start(bf16[128,256]{1,0:T(8,128)(2,1)S(1)} %merged.2.refs_13_), channel_id=1, source_target_pairs={{0,16},{2,18},{4,20},{6,22},{8,24},{10,26},{12,28},{14,30},{16,0},... | collective-permute-start | bytes 196616 | tf_op jit(solution)/shard_map/ppermute | solution.py:753
  24.6 3.1 %inner_terms.4 = (bf16[384,256]{1,0:T(8,128)(2,1)S(1)}, bf16[384,256]{1,0:T(8,128)(2,1)S(1)}, bf16[384,256]{1,0:T(8,128)(2,1)S(1)}, f32[384,128]{1,0:T(8,128)S(1)}, f32[384,128]{1,0:T(8,128)S(1)}) custom-call(bf16[384,128]{1,0:T(8,128)(2,1)S(1)} %get-tuple-element.80.refs_0_.b, bf16[384,128]{1,0:T(8,128)(2,1)S(1)} %get-tuple-element.81.refs_1_.c, ...), custom_call_target="tpu_custom_call" | custom-call | flops 805306368 | bytes 3145728 | tf_op jit(solution)/shard_map/inner_terms/pallas_call | solution.py:580
  27.7 0.0 collective-permute-done.12.refs_1_
  27.7 0.2 member_entries.3
  27.9 1.7 %collective-permute-start.13 = (bf16[256,256]{1,0:T(8,128)(2,1)S(1)}, bf16[256,256]{1,0:T(8,128)(2,1)S(1)}, u32[]{:S(2)}, u32[]{:S(2)}) collective-permute-start(bf16[256,256]{1,0:T(8,128)(2,1)S(1)} %get-tuple-element.131), channel_id=1, source_target_pairs={{0,6},{2,4},{4,2},{6,0},{8,14},{10,12},{12,10},{14,8},{16,22},{18,... | collective-permute-start | bytes 393224 | tf_op jit(solution)/shard_map/ppermute | solution.py:427
  29.6 0.0 collective-permute-done.7.received.refs_0_
  29.7 2.2 %collective-permute-start.8 = (bf16[128,256]{1,0:T(8,128)(2,1)S(1)}, bf16[128,256]{1,0:T(8,128)(2,1)S(1)}, u32[]{:S(2)}, u32[]{:S(2)}) collective-permute-start(bf16[128,256]{1,0:T(8,128)(2,1)S(1)} %merged.3), channel_id=1, source_target_pairs={{0,16},{2,18},{4,20},{6,22},{8,24},{10,26},{12,28},{14,30},{16,0},... | collective-permute-start | bytes 196616 | tf_op jit(solution)/shard_map/ppermute | solution.py:753
  31.9 1.3 %collective-permute-start.14 = (bf16[256,256]{1,0:T(8,128)(2,1)S(1)}, bf16[256,256]{1,0:T(8,128)(2,1)S(1)}, u32[]{:S(2)}, u32[]{:S(2)}) collective-permute-start(bf16[256,256]{1,0:T(8,128)(2,1)S(1)} %get-tuple-element.132), channel_id=1, source_target_pairs={{0,4},{2,6},{4,0},{6,2},{8,12},{10,14},{12,8},{14,10},{16,20},{18,... | collective-permute-start | bytes 393224 | tf_op jit(solution)/shard_map/ppermute | solution.py:427
  33.2 0.5 collective-permute-start.15
  33.6 1.3 %collective-permute-done.8.refs_1_ = bf16[128,256]{1,0:T(8,128)(2,1)S(1)} collective-permute-done((bf16[128,256]{1,0:T(8,128)(2,1)S(1)}, bf16[128,256]{1,0:T(8,128)(2,1)S(1)}, u32[]{:S(2)}, u32[]{:S(2)}) %collective-permute-start.8) | collective-permute-done | bytes 65568 | tf_op jit(solution)/shard_map/ppermute | solution.py:753
  34.9 0.4 member_entries.2
  35.3 2.0 %collective-permute-start.9 = (bf16[256,256]{1,0:T(8,128)(2,1)S(1)}, bf16[256,256]{1,0:T(8,128)(2,1)S(1)}, u32[]{:S(2)}, u32[]{:S(2)}) collective-permute-start(bf16[256,256]{1,0:T(8,128)(2,1)S(1)} %get-tuple-element.119), channel_id=1, source_target_pairs={{0,6},{2,4},{4,2},{6,0},{8,14},{10,12},{12,10},{14,8},{16,22},{18,... | collective-permute-start | bytes 393224 | tf_op jit(solution)/shard_map/ppermute | solution.py:427
  37.3 0.7 %collective-permute-start.10 = (bf16[256,256]{1,0:T(8,128)(2,1)S(1)}, bf16[256,256]{1,0:T(8,128)(2,1)S(1)}, u32[]{:S(2)}, u32[]{:S(2)}) collective-permute-start(bf16[256,256]{1,0:T(8,128)(2,1)S(1)} %get-tuple-element.120), channel_id=1, source_target_pairs={{0,4},{2,6},{4,0},{6,2},{8,12},{10,14},{12,8},{14,10},{16,20},{18,... | collective-permute-start | bytes 393224 | tf_op jit(solution)/shard_map/ppermute | solution.py:427
  38.0 0.8 %collective-permute-start.11 = (bf16[256,256]{1,0:T(8,128)(2,1)S(1)}, bf16[256,256]{1,0:T(8,128)(2,1)S(1)}, u32[]{:S(2)}, u32[]{:S(2)}) collective-permute-start(bf16[256,256]{1,0:T(8,128)(2,1)S(1)} %get-tuple-element.121), channel_id=1, source_target_pairs={{0,2},{2,0},{4,6},{6,4},{8,10},{10,8},{12,14},{14,12},{16,18},{18,... | collective-permute-start | bytes 393224 | tf_op jit(solution)/shard_map/ppermute | solution.py:427
  38.8 3.1 %inner_terms.5 = (bf16[384,256]{1,0:T(8,128)(2,1)S(1)}, bf16[384,256]{1,0:T(8,128)(2,1)S(1)}, bf16[384,256]{1,0:T(8,128)(2,1)S(1)}, f32[384,128]{1,0:T(8,128)S(1)}, f32[384,128]{1,0:T(8,128)S(1)}) custom-call(bf16[384,128]{1,0:T(8,128)(2,1)S(1)} %get-tuple-element.80.refs_0_.b, bf16[384,128]{1,0:T(8,128)(2,1)S(1)} %get-tuple-element.81.refs_1_.c, ...), custom_call_target="tpu_custom_call" | custom-call | flops 805306368 | bytes 3145728 | tf_op jit(solution)/shard_map/inner_terms/pallas_call | solution.py:580
  41.9 0.0 collective-permute-done.15.refs_11_
  41.9 0.5 %entry_values.1.refs_12_.refs_6_ = bf16[384,1024]{1,0:T(8,128)(2,1)S(1)} custom-call(s32[1]{0:T(128)} %bitcast.where, bf16[384,128]{1,0:T(8,128)(2,1)S(1)} %get-tuple-element.80.refs_0_.b, bf16[384,256]{1,0:T(8,128)(2,1)S(1)} %get-tuple-element.122.refs_0_, bf16[384,256]{1,0:T(8,128)(2,1)S(1)} %get-tuple-element.123.refs_1_, ...), custom_call_target="tpu_custom_call" | custom-call | flops 100663296 | bytes 1572864 | tf_op jit(solution)/shard_map/entry_values/pallas_call | solution.py:678
  42.4 0.6 %entry_parts.3 = (f32[384,128]{1,0:T(8,128)S(1)}, f32[384,128]{1,0:T(8,128)S(1)}) custom-call(f32[384,128]{1,0:T(8,128)S(1)} %get-tuple-element.134.db_before, f32[384,128]{1,0:T(8,128)S(1)} %get-tuple-element.135.dc_before, bf16[384,256]{1,0:T(8,128)(2,1)S(1)} %get-tuple-element.136.refs_0_, bf16[384,256]{1,0:T(8,128)(2,1)S(1)} %get-tuple-element.137.refs_1_, ...), custom_call_target="tpu_custom_call" | custom-call | flops 301989888 | bytes 98304 | tf_op jit(solution)/shard_map/entry_parts/pallas_call | solution.py:617
  43.0 0.0 collective-permute-done.9.refs_9_.refs_5_
  43.0 0.4 entry_parts.4
  43.4 0.0 collective-permute-done.10.refs_10_.refs_4_
  43.4 0.3 collective-permute-done.11.refs_11_.refs_5_
  43.8 0.4 entry_parts.5.refs_0_
  44.1 0.1 collective-permute-start.16
  44.2 1.3 %last_values.1 = bf16[384,2048]{1,0:T(8,128)(2,1)} custom-call(s32[1]{0:T(128)} %bitcast.where, bf16[384,128]{1,0:T(8,128)(2,1)S(1)} %get-tuple-element.80.refs_0_.b, bf16[384,256]{1,0:T(8,128)(2,1)S(1)} %get-tuple-element.104.refs_0_, bf16[384,256]{1,0:T(8,128)(2,1)S(1)} %get-tuple-element.112.refs_1_, bf16[384,256]{1,0:T(8,128)(2,1)S(1)} %get-tuple-element.113.refs_2_, ...), custom_call_target="tpu_custom_call" | custom-call | flops 100663296 | bytes 1572864 | tf_op jit(solution)/shard_map/last_values/pallas_call | solution.py:688
  45.5 0.1 collective-permute-done.16.refs_1_
  45.6 0.7 %sum_over_heads.1 = (bf16[384,128]{1,0:T(8,128)(2,1)}, bf16[384,128]{1,0:T(8,128)(2,1)}) custom-call(bf16[768,128]{1,0:T(8,128)(2,1)S(1)} %entry_parts.5.refs_0_, bf16[768,128]{1,0:T(8,128)(2,1)S(1)} %collective-permute-done.16.refs_1_), custom_call_target="tpu_custom_call" | custom-call | flops 196608 | bytes 393216 | tf_op jit(solution)/shard_map/sum_over_heads/pallas_call | solution.py:720
  (4 shorter events, 0.1 us)
Async XLA Ops:
  3.3 11.3 %collective-permute-start = (bf16[272,256]{1,0:T(8,128)(2,1)S(1)}, bf16[272,256]{1,0:T(8,128)(2,1)S(1)}, u32[]{:S(2)}, u32[]{:S(2)}) collective-permute-start(bf16[272,256]{1,0:T(8,128)(2,1)S(1)} %get-tuple-element.99), channel_id=1, source_target_pairs={{0,6},{2,4},{4,2},{6,0},{8,14},{10,12},{12,10},{14,8},{16,22},{18,... | collective-permute-start | bytes 417800 | tf_op jit(solution)/shard_map/ppermute | solution.py:427
  7.3 7.9 %collective-permute-start.1 = (bf16[272,256]{1,0:T(8,128)(2,1)S(1)}, bf16[272,256]{1,0:T(8,128)(2,1)S(1)}, u32[]{:S(2)}, u32[]{:S(2)}) collective-permute-start(bf16[272,256]{1,0:T(8,128)(2,1)S(1)} %get-tuple-element.100), channel_id=1, source_target_pairs={{0,4},{2,6},{4,0},{6,2},{8,12},{10,14},{12,8},{14,10},{16,20},{18,... | collective-permute-start | bytes 417800 | tf_op jit(solution)/shard_map/ppermute | solution.py:427
  7.8 7.4 %collective-permute-start.2 = (bf16[272,256]{1,0:T(8,128)(2,1)S(1)}, bf16[272,256]{1,0:T(8,128)(2,1)S(1)}, u32[]{:S(2)}, u32[]{:S(2)}) collective-permute-start(bf16[272,256]{1,0:T(8,128)(2,1)S(1)} %get-tuple-element.101), channel_id=1, source_target_pairs={{0,2},{2,0},{4,6},{6,4},{8,10},{10,8},{12,14},{14,12},{16,18},{18,... | collective-permute-start | bytes 417800 | tf_op jit(solution)/shard_map/ppermute | solution.py:427
  11.1 8.3 %collective-permute-start.4 = (bf16[272,256]{1,0:T(8,128)(2,1)S(1)}, bf16[272,256]{1,0:T(8,128)(2,1)S(1)}, u32[]{:S(2)}, u32[]{:S(2)}) collective-permute-start(bf16[272,256]{1,0:T(8,128)(2,1)S(1)} %get-tuple-element.108), channel_id=1, source_target_pairs={{0,6},{2,4},{4,2},{6,0},{8,14},{10,12},{12,10},{14,8},{16,22},{18,... | collective-permute-start | bytes 417800 | tf_op jit(solution)/shard_map/ppermute | solution.py:427
  14.1 5.9 %collective-permute-start.5 = (bf16[272,256]{1,0:T(8,128)(2,1)S(1)}, bf16[272,256]{1,0:T(8,128)(2,1)S(1)}, u32[]{:S(2)}, u32[]{:S(2)}) collective-permute-start(bf16[272,256]{1,0:T(8,128)(2,1)S(1)} %get-tuple-element.109), channel_id=1, source_target_pairs={{0,4},{2,6},{4,0},{6,2},{8,12},{10,14},{12,8},{14,10},{16,20},{18,... | collective-permute-start | bytes 417800 | tf_op jit(solution)/shard_map/ppermute | solution.py:427
  14.6 5.6 %collective-permute-start.6 = (bf16[272,256]{1,0:T(8,128)(2,1)S(1)}, bf16[272,256]{1,0:T(8,128)(2,1)S(1)}, u32[]{:S(2)}, u32[]{:S(2)}) collective-permute-start(bf16[272,256]{1,0:T(8,128)(2,1)S(1)} %get-tuple-element.110), channel_id=1, source_target_pairs={{0,2},{2,0},{4,6},{6,4},{8,10},{10,8},{12,14},{14,12},{16,18},{18,... | collective-permute-start | bytes 417800 | tf_op jit(solution)/shard_map/ppermute | solution.py:427
  15.3 6.6 %collective-permute-start.3 = (bf16[272,256]{1,0:T(8,128)(2,1)S(1)}, bf16[272,256]{1,0:T(8,128)(2,1)S(1)}, u32[]{:S(2)}, u32[]{:S(2)}) collective-permute-start(bf16[272,256]{1,0:T(8,128)(2,1)S(1)} %totals.2.refs_11_.own), channel_id=1, source_target_pairs={{0,8},{2,10},{4,12},{6,14},{8,0},{10,2},{12,4},{14,6},{16,24},{18,... | collective-permute-start | bytes 417800 | tf_op jit(solution)/shard_map/ppermute | solution.py:753
  20.3 9.3 %collective-permute-start.7 = (bf16[272,256]{1,0:T(8,128)(2,1)S(1)}, bf16[272,256]{1,0:T(8,128)(2,1)S(1)}, u32[]{:S(2)}, u32[]{:S(2)}) collective-permute-start(bf16[272,256]{1,0:T(8,128)(2,1)S(1)} %totals.3.own), channel_id=1, source_target_pairs={{0,8},{2,10},{4,12},{6,14},{8,0},{10,2},{12,4},{14,6},{16,24},{18,... | collective-permute-start | bytes 417800 | tf_op jit(solution)/shard_map/ppermute | solution.py:753
  22.0 5.7 %collective-permute-start.12 = (bf16[128,256]{1,0:T(8,128)(2,1)S(1)}, bf16[128,256]{1,0:T(8,128)(2,1)S(1)}, u32[]{:S(2)}, u32[]{:S(2)}) collective-permute-start(bf16[128,256]{1,0:T(8,128)(2,1)S(1)} %merged.2.refs_13_), channel_id=1, source_target_pairs={{0,16},{2,18},{4,20},{6,22},{8,24},{10,26},{12,28},{14,30},{16,0},... | collective-permute-start | bytes 196616 | tf_op jit(solution)/shard_map/ppermute | solution.py:753
  27.9 10.1 %collective-permute-start.13 = (bf16[256,256]{1,0:T(8,128)(2,1)S(1)}, bf16[256,256]{1,0:T(8,128)(2,1)S(1)}, u32[]{:S(2)}, u32[]{:S(2)}) collective-permute-start(bf16[256,256]{1,0:T(8,128)(2,1)S(1)} %get-tuple-element.131), channel_id=1, source_target_pairs={{0,6},{2,4},{4,2},{6,0},{8,14},{10,12},{12,10},{14,8},{16,22},{18,... | collective-permute-start | bytes 393224 | tf_op jit(solution)/shard_map/ppermute | solution.py:427
  29.7 5.2 %collective-permute-start.8 = (bf16[128,256]{1,0:T(8,128)(2,1)S(1)}, bf16[128,256]{1,0:T(8,128)(2,1)S(1)}, u32[]{:S(2)}, u32[]{:S(2)}) collective-permute-start(bf16[128,256]{1,0:T(8,128)(2,1)S(1)} %merged.3), channel_id=1, source_target_pairs={{0,16},{2,18},{4,20},{6,22},{8,24},{10,26},{12,28},{14,30},{16,0},... | collective-permute-start | bytes 196616 | tf_op jit(solution)/shard_map/ppermute | solution.py:753
  31.9 10.0 %collective-permute-start.14 = (bf16[256,256]{1,0:T(8,128)(2,1)S(1)}, bf16[256,256]{1,0:T(8,128)(2,1)S(1)}, u32[]{:S(2)}, u32[]{:S(2)}) collective-permute-start(bf16[256,256]{1,0:T(8,128)(2,1)S(1)} %get-tuple-element.132), channel_id=1, source_target_pairs={{0,4},{2,6},{4,0},{6,2},{8,12},{10,14},{12,8},{14,10},{16,20},{18,... | collective-permute-start | bytes 393224 | tf_op jit(solution)/shard_map/ppermute | solution.py:427
  33.2 8.8 %collective-permute-start.15 = (bf16[256,256]{1,0:T(8,128)(2,1)S(1)}, bf16[256,256]{1,0:T(8,128)(2,1)S(1)}, u32[]{:S(2)}, u32[]{:S(2)}) collective-permute-start(bf16[256,256]{1,0:T(8,128)(2,1)S(1)} %get-tuple-element.133), channel_id=1, source_target_pairs={{0,2},{2,0},{4,6},{6,4},{8,10},{10,8},{12,14},{14,12},{16,18},{18,... | collective-permute-start | bytes 393224 | tf_op jit(solution)/shard_map/ppermute | solution.py:427
  35.3 7.7 %collective-permute-start.9 = (bf16[256,256]{1,0:T(8,128)(2,1)S(1)}, bf16[256,256]{1,0:T(8,128)(2,1)S(1)}, u32[]{:S(2)}, u32[]{:S(2)}) collective-permute-start(bf16[256,256]{1,0:T(8,128)(2,1)S(1)} %get-tuple-element.119), channel_id=1, source_target_pairs={{0,6},{2,4},{4,2},{6,0},{8,14},{10,12},{12,10},{14,8},{16,22},{18,... | collective-permute-start | bytes 393224 | tf_op jit(solution)/shard_map/ppermute | solution.py:427
  37.3 6.1 %collective-permute-start.10 = (bf16[256,256]{1,0:T(8,128)(2,1)S(1)}, bf16[256,256]{1,0:T(8,128)(2,1)S(1)}, u32[]{:S(2)}, u32[]{:S(2)}) collective-permute-start(bf16[256,256]{1,0:T(8,128)(2,1)S(1)} %get-tuple-element.120), channel_id=1, source_target_pairs={{0,4},{2,6},{4,0},{6,2},{8,12},{10,14},{12,8},{14,10},{16,20},{18,... | collective-permute-start | bytes 393224 | tf_op jit(solution)/shard_map/ppermute | solution.py:427
  38.0 5.7 %collective-permute-start.11 = (bf16[256,256]{1,0:T(8,128)(2,1)S(1)}, bf16[256,256]{1,0:T(8,128)(2,1)S(1)}, u32[]{:S(2)}, u32[]{:S(2)}) collective-permute-start(bf16[256,256]{1,0:T(8,128)(2,1)S(1)} %get-tuple-element.121), channel_id=1, source_target_pairs={{0,2},{2,0},{4,6},{6,4},{8,10},{10,8},{12,14},{14,12},{16,18},{18,... | collective-permute-start | bytes 393224 | tf_op jit(solution)/shard_map/ppermute | solution.py:427
  44.1 1.5 %collective-permute-start.16 = (bf16[768,128]{1,0:T(8,128)(2,1)S(1)}, bf16[768,128]{1,0:T(8,128)(2,1)S(1)}, u32[]{:S(2)}, u32[]{:S(2)}) collective-permute-start(bf16[768,128]{1,0:T(8,128)(2,1)S(1)} %entry_parts.5.refs_0_), channel_id=1, source_target_pairs={{0,1},{1,0},{2,3},{3,2},{4,5},{5,4},{6,7},{7,6},{8,9},{9,8},{10,11... | collective-permute-start | bytes 589832 | tf_op jit(solution)/shard_map/ppermute | solution.py:719
